TPU v7x, 32 devices: a whole 2x2x4 slice. The times are simulated.
32 devices in a mesh: row: 4 (over z), col: 8 (over y, x, core).
Axes of the slice: x: 2, y: 2, z: 4, core: 2. Of those that a mesh axis runs over, the one named last changes fastest.
Arguments:
- image_embeds: float32 [8192, 512], P(('row', 'col')), may hold values from -60 to 60
- text_embeds: float32 [8192, 512], P(('col', 'row')), may hold values from -60 to 60
- logit_scale: float32 [], replicated, may hold values from 1 to 4
Outputs:
- grad_image: float32 [8192, 512], P(('row', 'col'))
- grad_text: float32 [8192, 512], P(('col', 'row'))
- grad_scale: float32 [], replicated
All inputs are finite; a program needn't handle non-finite values.
Results may differ from a plain program's by a relative error of at most 0.0023.
The roundings to bfloat16 on the way count: a program that leaves them out, or rounds other values in their place, can miss the bound.
Values may be sent and summed in bfloat16 or wider, within the bound.
No kernel may reach another device: no remote copies, remote signals or barrier semaphores. Data moves between devices by JAX's collectives and lax.ppermute only.
A program may use at most 128 MiB of HBM per device.

v0:
```python
import jax
import jax.numpy as jnp
from jax import lax
from jax.sharding import PartitionSpec as P


def on_device(image_embeds, text_embeds, logit_scale):
    image_half = image_embeds.astype(jnp.bfloat16)
    text_half = text_embeds.astype(jnp.bfloat16)
    images = lax.all_gather(image_half, "col", axis=0, tiled=True)
    text_cols = lax.all_gather(text_half, "row", axis=0, tiled=True)
    rows_tile = images.shape[0]
    cols_tile = text_cols.shape[0]
    row_start = lax.axis_index("row") * rows_tile
    col_start = lax.axis_index("col") * cols_tile
    similar = lax.dot_general(
        images, text_cols, (((1,), (1,)), ((), ())), preferred_element_type=jnp.float32
    )
    logits = logit_scale * similar
    row_max = lax.pmax(jnp.max(logits, axis=1), "col")
    col_max = lax.pmax(jnp.max(logits, axis=0), "row")
    row_sum = lax.psum(jnp.sum(jnp.exp(logits - row_max[:, None]), axis=1), "col")
    col_sum = lax.psum(jnp.sum(jnp.exp(logits - col_max[None, :]), axis=0), "row")
    row_lse = row_max + jnp.log(row_sum)
    col_lse = col_max + jnp.log(col_sum)
    row_ids = row_start + jnp.arange(rows_tile, dtype=jnp.int32)
    col_ids = col_start + jnp.arange(cols_tile, dtype=jnp.int32)
    matched = (row_ids[:, None] == col_ids[None, :]).astype(jnp.float32)
    logit_grad = (
        0.5 * jnp.exp(logits - row_lse[:, None])
        + 0.5 * jnp.exp(logits - col_lse[None, :])
        - matched
    )
    partial_scale = jnp.sum(logit_grad * similar)
    grad_half = logit_grad.astype(jnp.bfloat16)
    picked = grad_half
    grad_image = lax.psum_scatter(
        logit_scale * jnp.dot(picked, text_cols, preferred_element_type=jnp.float32),
        "col",
        scatter_dimension=0,
        tiled=True,
    )
    picked = grad_half
    grad_text = lax.psum_scatter(
        logit_scale
        * lax.dot_general(
            picked, images, (((0,), (0,)), ((), ())), preferred_element_type=jnp.float32
        ),
        "row",
        scatter_dimension=0,
        tiled=True,
    )
    grad_scale = lax.psum(partial_scale, ("row", "col"))
    return (grad_image, grad_text, grad_scale)


def solution(mesh):
    placed = (P(("row", "col"), None), P(("col", "row"), None), P())
    return jax.shard_map(
        on_device,
        mesh=mesh,
        in_specs=placed,
        out_specs=(P(("row", "col"), None), P(("col", "row"), None), P()),
        check_vma=False,
    )
```

profile of v0, /device:TPU:0, one launch (start us, length us, event | category | flops | bytes accessed | tf_op | source)
XLA Modules:
  0.0 252.6 jit_solution(5975073493388908202)
XLA Ops:
  7.2 0.0 all-gather.5.cloned.1.call-start
  7.2 1.8 convert_element_type.13
  9.0 0.0 all-gather.5.cloned.1.call-update
  9.0 0.0 all-gather.3.cloned.1.call-start
  9.1 1.8 convert_element_type.12
  10.8 0.0 all-gather.3.cloned.1.call-update
  10.9 0.0 reduce-scatter.5.cloned.1.call-start
  11.6 29.2 %all-gather.5.cloned.1.call-done = bf16[1024,512]{1,0:T(8,128)(2,1)} async-done(((bf16[256,512]{1,0:T(8,128)(2,1)}), bf16[1024,512]{1,0:T(8,128)(2,1)}) %all-gather.5.cloned.1.call-update) | async-done | bytes 1048592 | tf_op jit(solution)/shard_map/all_gather | solution.py:11
  40.8 29.9 %all-gather.3.cloned.1.call-done = bf16[2048,512]{1,0:T(8,128)(2,1)} async-done(((bf16[256,512]{1,0:T(8,128)(2,1)}), bf16[2048,512]{1,0:T(8,128)(2,1)}) %all-gather.3.cloned.1.call-update) | async-done | bytes 2097168 | tf_op jit(solution)/shard_map/all_gather | solution.py:10
  70.7 7.5 %multiply_reduce_fusion.2 = (f32[2048]{0:T(1024)S(1)}, f32[2048,1024]{1,0:T(8,128)}) fusion(f32[]{:T(128)S(6)} %copy.6, bf16[2048,512]{1,0:T(8,128)(2,1)} %all-gather.3.cloned.1.call-done, bf16[1024,512]{1,0:T(8,128)(2,1)} %all-gather.5.cloned.1.call-done), kind=kOutput, calls=%fused_computation.5 | convolution fusion | flops 2151675904 | bytes 11542532 | tf_op jit(solution)/shard_map/dot_general | solution.py:16
  78.2 13.3 %pmax.14 = f32[2048]{0:T(1024)S(1)} all-reduce(f32[2048]{0:T(1024)S(1)} %get-tuple-element.7), channel_id=1, replica_groups=mesh['row'=4,'col'=8] {'col'}, use_global_device_ids=true, to_apply=%region_1.0 | all-reduce | flops 2048 | bytes 16384 | tf_op jit(solution)/shard_map/pmax | solution.py:20
  91.5 4.5 %exponential_reduce_fusion.1 = (f32[2048]{0:T(1024)S(1)}, f32[1024]{0:T(1024)S(1)}) fusion(f32[2048,1024]{1,0:T(8,128)} %get-tuple-element.8, f32[2048]{0:T(1024)S(1)} %pmax.14, f32[]{:T(128)S(6)} %copy.6), kind=kLoop, calls=%fused_computation.3 | loop fusion | flops 8385536 | bytes 8409092 | tf_op jit(solution)/shard_map/reduce_sum | solution.py:22
  96.0 12.0 %psum.21 = f32[2048]{0:T(1024)S(1)} all-reduce(f32[2048]{0:T(1024)S(1)} %get-tuple-element.3), channel_id=1, replica_groups=mesh['row'=4,'col'=8] {'col'}, use_global_device_ids=true, to_apply=%region_3.0 | all-reduce | flops 2048 | bytes 16384 | tf_op jit(solution)/shard_map/psum | solution.py:22
  108.0 11.7 %pmax.15 = f32[1024]{0:T(1024)S(1)} all-reduce(f32[1024]{0:T(1024)S(1)} %get-tuple-element.4), channel_id=1, replica_groups=mesh['row'=4,'col'=8] {'row'}, use_global_device_ids=true, to_apply=%region_5.0 | all-reduce | flops 1024 | bytes 8192 | tf_op jit(solution)/shard_map/pmax | solution.py:21
  119.7 4.8 %exponential_reduce_fusion = f32[1024]{0:T(1024)S(1)} fusion(f32[2048,1024]{1,0:T(8,128)} %get-tuple-element.8, f32[1024]{0:T(1024)S(1)} %pmax.15, f32[]{:T(128)S(6)} %copy.6), kind=kLoop, calls=%fused_computation.2 | loop fusion | flops 6290432 | bytes 8396804 | tf_op jit(solution)/shard_map/reduce_sum | solution.py:23
  124.5 0.0 copy-start.1
  124.5 8.5 %psum.22 = f32[1024]{0:T(1024)S(1)} all-reduce(f32[1024]{0:T(1024)S(1)} %exponential_reduce_fusion), channel_id=1, replica_groups=mesh['row'=4,'col'=8] {'row'}, use_global_device_ids=true, to_apply=%region_7.0 | all-reduce | flops 1024 | bytes 8192 | tf_op jit(solution)/shard_map/psum | solution.py:23
  133.1 8.6 %multiply_reduce_fusion = (f32[]{:T(128)}, bf16[2048,1024]{1,0:T(8,128)(2,1)S(1)}) fusion(f32[2048,1024]{1,0:T(8,128)} %get-tuple-element.8, s32[1024]{0:T(1024)S(1)} %iota_add_fusion.1, f32[1024]{0:T(1024)S(1)} %log_add_fusion.1, f32[2048]{0:T(1024)S(1)} %log_add_fusion, f32[]{:T(128)S(6)} %copy.6, s32[2048]{0:T(1024)S(1)} %iota_add_fusion), kind=kLoop, calls=%fused_computation | loop fusion | flops 23068672 | bytes 12607496 | tf_op jit(solution)/shard_map/reduce_sum | solution.py:34
  141.7 0.0 copy-start
  141.7 0.0 copy-start.2
  141.7 1.9 copy-done
  143.6 0.0 copy-done.1
  143.6 3.8 %convolution_multiply_fusion.1 = f32[1024,512]{1,0:T(8,128)} fusion(bf16[2048,1024]{1,0:T(8,128)(2,1)S(1)} %get-tuple-element.6, bf16[2048,512]{1,0:T(8,128)(2,1)S(1)} %copy-done.1, f32[]{:T(128)S(6)} %copy.6), kind=kOutput, calls=%fused_computation.8 | convolution fusion | flops 2148007936 | bytes 8388612 | tf_op jit(solution)/shard_map/dot_general | solution.py:46
  147.4 0.0 reduce-scatter.5.cloned.1.call-update
  147.4 0.0 reduce-scatter.3.cloned.1.call-start
  147.4 0.0 copy-done.2
  147.5 6.5 %convolution_multiply_fusion = f32[2048,512]{1,0:T(8,128)} fusion(bf16[2048,1024]{1,0:T(8,128)(2,1)} %copy-done, bf16[1024,512]{1,0:T(8,128)(2,1)S(1)} %copy-done.2, f32[]{:T(128)S(6)} %copy.6), kind=kOutput, calls=%fused_computation.7 | convolution fusion | flops 2148532224 | bytes 9437188 | tf_op jit(solution)/shard_map/dot_general | solution.py:38
  153.9 0.0 reduce-scatter.3.cloned.1.call-update
  154.0 43.4 %psum.23 = f32[]{:T(128)} all-reduce(f32[]{:T(128)} %get-tuple-element.5), channel_id=1, replica_groups=mesh['row'=4,'col'=8] {'row','col'}, use_global_device_ids=true, to_apply=%region_11.0 | all-reduce | flops 1 | bytes 8 | tf_op jit(solution)/shard_map/psum | solution.py:53
  197.4 0.0 reduce-scatter.5.cloned.1.call-done
  197.4 48.6 %reduce-scatter.3.cloned.1.call-done = f32[256,512]{1,0:T(8,128)} async-done(((f32[2048,512]{1,0:T(8,128)}), f32[256,512]{1,0:T(8,128)}) %reduce-scatter.3.cloned.1.call-update) | async-done | bytes 524304 | tf_op jit(solution)/shard_map/reduce_scatter | solution.py:37
  (4 shorter events, 0.0 us)
Async XLA Ops:
  7.2 33.6 %all-gather.5.cloned.1.call-start = ((), (), s32[]{:S(2)}) async-start(), calls=%async_computation.3 | async-start | bytes 1310720 | tf_op jit(solution)/shard_map/all_gather | solution.py:11
  9.0 61.7 %all-gather.3.cloned.1.call-start = ((), (), s32[]{:S(2)}) async-start(), calls=%async_computation.2 | async-start | bytes 2359296 | tf_op jit(solution)/shard_map/all_gather | solution.py:10
  10.9 186.5 %reduce-scatter.5.cloned.1.call-start = ((), (), s32[]{:S(2)}) async-start(), calls=%async_computation.5 | async-start | bytes 2621440 | tf_op jit(solution)/shard_map/reduce_scatter | solution.py:44
  124.5 19.1 %copy-start.1 = (bf16[2048,512]{1,0:T(8,128)(2,1)S(1)}, bf16[2048,512]{1,0:T(8,128)(2,1)}, u32[]{:S(2)}) copy-start(bf16[2048,512]{1,0:T(8,128)(2,1)} %all-gather.3.cloned.1.call-done) | copy-start | bytes 6291460
  141.7 1.9 copy-start
  141.7 5.8 %copy-start.2 = (bf16[1024,512]{1,0:T(8,128)(2,1)S(1)}, bf16[1024,512]{1,0:T(8,128)(2,1)}, u32[]{:S(2)}) copy-start(bf16[1024,512]{1,0:T(8,128)(2,1)} %all-gather.5.cloned.1.call-done) | copy-start | bytes 3145732
  147.4 98.6 %reduce-scatter.3.cloned.1.call-start = ((), (), s32[]{:S(2)}) async-start(), calls=%async_computation.4 | async-start | bytes 4718592 | tf_op jit(solution)/shard_map/reduce_scatter | solution.py:37
Sparse Core Ops, SparseCore 0:
  10.1 30.6 all-gather.4
  43.3 27.3 all-gather.2
  147.5 43.7 reduce-scatter.4
  195.4 50.5 reduce-scatter.2
where the time goes:
time: 253 us
  waiting for transfers between devices  108 us (43%)
  blocking collectives  89 us (35%)
  other arithmetic  21.5 us (8%)
  matrix products  17.7 us (7%)
  between operations  14.5 us (6%)
    reduce_scatter x1, waiting for transfers between devices, on_device(): lax.psum_scatter(logit_scale * jnp.dot(picked, text_cols, preferred_eleme...  48.6 us
    psum x1, blocking collectives, on_device(): grad_scale = lax.psum(partial_scale, ('row', 'col'))  43.4 us
    all_gather x1, waiting for transfers between devices, on_device(): images = lax.all_gather(image_half, 'col', axis=0, tiled=True)  29.9 us
    all_gather x1, waiting for transfers between devices, on_device(): text_cols = lax.all_gather(text_half, 'row', axis=0, tiled=True)  29.2 us
    pmax x1, blocking collectives, on_device(): row_max = lax.pmax(jnp.max(logits, axis=1), 'col')  13.3 us
    psum x1, blocking collectives, on_device(): lax.psum(jnp.sum(jnp.exp(logits - row_max[:, None]), axis=1), 'col')  12 us
    pmax x1, blocking collectives, on_device(): col_max = lax.pmax(jnp.max(logits, axis=0), 'row')  11.7 us
    reduce_sum x1, other arithmetic, on_device(): partial_scale = jnp.sum(logit_grad * similar)  8.63 us
  transfers between devices with their start and end apart: 4, of which 3 were waited for; matrix products, arithmetic and copies ran while one was open for 3% of the time, Pallas kernels for 0%

commit v1 on v0

v1 whole, which is shorter than its diff:
```python
import functools
import math

import jax
import jax.numpy as jnp
from jax import lax
from jax.experimental import pallas as pl
from jax.experimental.pallas import tpu as pltpu
from jax.sharding import PartitionSpec as P

LOG2E = 1.4426950408889634
LN2 = 0.6931471805599453
LANES = 128
VMEM = pltpu.VMEM
SMEM = pltpu.SMEM


def swap(x, axis, n, q):
    return lax.ppermute(x, axis, [(i, i ^ q) for i in range(n)])


def gather_hops(own, axis, n):
    half = own.shape[0] // 2
    blocks = {0: [own]}

    def top(pieces):
        return pieces[0][:half] if len(pieces) == 1 else pieces[0]

    def bottom(pieces):
        return pieces[0][half:] if len(pieces) == 1 else pieces[1]

    for q in sorted(range(1, n), key=lambda q: (bin(q).count("1"), q)):
        if q & 1:
            blocks[q] = [swap(p, axis, n, 1) for p in blocks[q ^ 1]]
        elif q & (q - 1) == 0:
            blocks[q] = [swap(own, axis, n, q)]
        else:
            high = 1 << (q.bit_length() - 1)
            low = q & -q
            blocks[q] = [
                swap(top(blocks[q ^ high]), axis, n, high),
                swap(bottom(blocks[q ^ low]), axis, n, low),
            ]
    return [blocks[q] for q in range(n)]


def nt_dot(a, b):
    return lax.dot_general(a, b, (((1,), (1,)), ((), ())), preferred_element_type=jnp.float32)


def stats_kernel(counts, block, coef_ref, *refs):
    n_image, n_text = counts
    pieces = refs[: n_image + n_text]
    row_ref, col_ref, images_out, texts_out = refs[n_image + n_text : n_image + n_text + 4]
    images, texts, tile, col_max, col_sum, sems, out_sems = refs[n_image + n_text + 4 :]
    copies = []
    for where, held in ((pieces[:n_image], images), (pieces[n_image:], texts)):
        at = 0
        for piece in where:
            rows = piece.shape[0]
            copies.append(
                pltpu.make_async_copy(piece, held.at[pl.ds(at, rows)], sems.at[len(copies)])
            )
            at += rows
    for copy in copies:
        copy.start()
    for copy in copies:
        copy.wait()
    keep = [
        pltpu.make_async_copy(images, images_out, out_sems.at[0]),
        pltpu.make_async_copy(texts, texts_out, out_sems.at[1]),
    ]
    for copy in keep:
        copy.start()

    coef = coef_ref[0, 0]
    cols, rows = tile.shape
    col_max[...] = jnp.full(col_max.shape, -jnp.inf, jnp.float32)

    def products(k, carry):
        at = pl.multiple_of(k * block, block)
        image = images[pl.ds(at, block), :]
        row_max = None
        for t in range(cols // block):
            part = pl.ds(t * block, block)
            x = nt_dot(texts[part, :], image) * coef
            tile[part, pl.ds(at, block)] = x
            top = jnp.max(x, axis=0, keepdims=True)
            row_max = top if row_max is None else jnp.maximum(row_max, top)
            held = col_max[part, :]
            for lane in range(0, block, LANES):
                held = jnp.maximum(held, x[:, lane : lane + LANES])
            col_max[part, :] = held
        row_ref[0:1, pl.ds(at, block)] = row_max
        return carry

    lax.fori_loop(0, rows // block, products, 0)

    def exponentials(i, acc):
        part = pl.ds(pl.multiple_of(i * 8, 8), 8)
        top = jnp.max(col_max[part, :], axis=1, keepdims=True)
        col_max[part, :] = jnp.broadcast_to(top, (8, LANES))
        x = tile[part, :]
        acc = acc + jnp.exp2(x - row_ref[0:1, :])
        e = jnp.exp2(x - top)
        total = e[:, :LANES]
        for lane in range(LANES, rows, LANES):
            total = total + e[:, lane : lane + LANES]
        col_sum[part, :] = total
        return acc

    acc = lax.fori_loop(0, cols // 8, exponentials, jnp.zeros((8, rows), jnp.float32), unroll=2)
    row_ref[1:2, :] = jnp.sum(acc, axis=0, keepdims=True)
    for t in range(cols // block):
        part = pl.ds(t * block, block)
        col_ref[0:1, part] = col_max[part, :].T[0:1, :]
        col_ref[1:2, part] = jnp.sum(col_sum[part, :].T, axis=0, keepdims=True)
    for copy in keep:
        copy.wait()


def stats(coef, image_pieces, text_pieces, block):
    rows = sum(p.shape[0] for p in image_pieces)
    cols = sum(p.shape[0] for p in text_pieces)
    width = image_pieces[0].shape[1]
    counts = (len(image_pieces), len(text_pieces))
    anywhere = pl.BlockSpec(memory_space=pl.ANY)
    return pl.pallas_call(
        functools.partial(stats_kernel, counts, block),
        out_shape=(
            jax.ShapeDtypeStruct((2, rows), jnp.float32),
            jax.ShapeDtypeStruct((2, cols), jnp.float32),
            jax.ShapeDtypeStruct((rows, width), jnp.bfloat16),
            jax.ShapeDtypeStruct((cols, width), jnp.bfloat16),
        ),
        in_specs=[pl.BlockSpec(memory_space=SMEM)] + [anywhere] * sum(counts),
        out_specs=(
            pl.BlockSpec(memory_space=VMEM),
            pl.BlockSpec(memory_space=VMEM),
            anywhere,
            anywhere,
        ),
        scratch_shapes=[
            VMEM((rows, width), jnp.bfloat16),
            VMEM((cols, width), jnp.bfloat16),
            VMEM((cols, rows), jnp.float32),
            VMEM((cols, LANES), jnp.float32),
            VMEM((cols, LANES), jnp.float32),
            pltpu.SemaphoreType.DMA((sum(counts),)),
            pltpu.SemaphoreType.DMA((2,)),
        ],
        compiler_params=pltpu.CompilerParams(vmem_limit_bytes=48 * 2**20),
        cost_estimate=pl.CostEstimate(
            flops=2 * rows * cols * width,
            bytes_accessed=4 * (rows + cols) * width,
            transcendentals=2 * rows * cols,
        ),
        name="stats",
    )(coef, *image_pieces, *text_pieces)


def lse_kernel(counts, block, *refs):
    outs = refs[sum(counts) :]
    for held, out in zip((refs[: counts[0]], refs[counts[0] : sum(counts)]), outs):
        n = len(held)
        for k in range(n):
            there = [pl.ds((k ^ q) * block, block) for q in range(n)]
            top = functools.reduce(
                jnp.maximum, [held[q][0:1, there[q]] for q in range(n)]
            )
            total = sum(
                held[q][1:2, there[q]] * jnp.exp2(held[q][0:1, there[q]] - top) for q in range(n)
            )
            out[0:1, pl.ds(k * block, block)] = top + jnp.log(total) * LOG2E


def lse(row_parts, col_parts, block):
    counts = (len(row_parts), len(col_parts))
    return pl.pallas_call(
        functools.partial(lse_kernel, counts, block),
        out_shape=(
            jax.ShapeDtypeStruct((1, row_parts[0].shape[1]), jnp.float32),
            jax.ShapeDtypeStruct((1, col_parts[0].shape[1]), jnp.float32),
        ),
        in_specs=[pl.BlockSpec(memory_space=VMEM)] * sum(counts),
        out_specs=(pl.BlockSpec(memory_space=VMEM),) * 2,
        name="lse",
    )(*row_parts, *col_parts)


def text_kernel(
    block, scale_ref, coef_ref, same_ref, images, text, row_lse, col_lse, grad_ref, out_ref, sum_ref
):
    coef = coef_ref[0, 0]
    rows = images.shape[0]
    size = text.shape[0]
    col_lse_down = jnp.broadcast_to(col_lse[...], (LANES, size)).T
    step = 32
    lane_ids = lax.broadcasted_iota(jnp.int32, (step, LANES), 1)
    row_ids = lax.broadcasted_iota(jnp.int32, (step, LANES), 0)

    def one(k, acc):
        at = pl.multiple_of(k * block, block)
        inner = nt_dot(text[...], images[pl.ds(at, block), :])
        same = same_ref[0, k]
        for r in range(0, size, step):
            for lane in range(0, block, LANES):
                v = inner[r : r + step, lane : lane + LANES]
                x = v * coef
                e = jnp.exp2(x - row_lse[0:1, pl.ds(at + lane, LANES)]) + jnp.exp2(
                    x - col_lse_down[r : r + step, :]
                )
                g = 0.5 * e
                if lane <= r < lane + LANES:
                    g = g - jnp.where(row_ids + (r - lane) == lane_ids, same, 0.0)
                acc = acc + g * v
                grad_ref[r : r + step, pl.ds(at + lane, LANES)] = g.astype(jnp.bfloat16)
        return acc

    acc = lax.fori_loop(0, rows // block, one, jnp.zeros((step, LANES), jnp.float32), unroll=2)
    sum_ref[...] = functools.reduce(jnp.add, [acc[i : i + 8] for i in range(0, step, 8)])
    out_ref[...] = scale_ref[0, 0] * jnp.dot(
        grad_ref[...], images[...], preferred_element_type=jnp.float32
    )


def text_grads(scale, coef, same, images, texts, row_lse, col_lse, t, block):
    rows, width = images.shape
    vmem = pl.BlockSpec(memory_space=VMEM)
    smem = pl.BlockSpec(memory_space=SMEM)
    return pl.pallas_call(
        functools.partial(text_kernel, block),
        grid=(1,),
        out_shape=(
            jax.ShapeDtypeStruct((block, rows), jnp.bfloat16),
            jax.ShapeDtypeStruct((block, width), jnp.float32),
            jax.ShapeDtypeStruct((8, LANES), jnp.float32),
        ),
        in_specs=[
            smem,
            smem,
            smem,
            vmem,
            pl.BlockSpec((block, width), lambda i: (t, 0)),
            vmem,
            pl.BlockSpec((1, block), lambda i: (0, t)),
        ],
        out_specs=(vmem, vmem, vmem),
        compiler_params=pltpu.CompilerParams(vmem_limit_bytes=32 * 2**20),
        cost_estimate=pl.CostEstimate(
            flops=4 * rows * block * width,
            bytes_accessed=2 * rows * (block + width) + 6 * block * width,
            transcendentals=2 * rows * block,
        ),
        name=f"text_grads_{t}",
    )(scale, coef, same, images, texts, row_lse, col_lse)


def image_kernel(n_text, block, scale_ref, *refs):
    grads, texts, out_ref = refs[:n_text], refs[n_text], refs[n_text + 1]
    total = None
    for t in range(n_text):
        part = lax.dot_general(
            grads[t][...],
            texts[pl.ds(t * block, block), :],
            (((0,), (0,)), ((), ())),
            preferred_element_type=jnp.float32,
        )
        total = part if total is None else total + part
    out_ref[0] = scale_ref[0, 0] * total


def image_grads(scale, grads, texts, odd, block):
    n_text = len(grads)
    rows = grads[0].shape[1]
    width = texts.shape[1]
    n = rows // block // 2
    return pl.pallas_call(
        functools.partial(image_kernel, n_text, block),
        grid=(n,),
        out_shape=jax.ShapeDtypeStruct((n, block, width), jnp.float32),
        in_specs=[pl.BlockSpec(memory_space=SMEM)]
        + [pl.BlockSpec((block, block), lambda j: (0, 2 * j + odd))] * n_text
        + [pl.BlockSpec(memory_space=VMEM)],
        out_specs=pl.BlockSpec((1, block, width), lambda j: (j, 0, 0)),
        compiler_params=pltpu.CompilerParams(vmem_limit_bytes=32 * 2**20),
        cost_estimate=pl.CostEstimate(
            flops=2 * n * block * n_text * block * width,
            bytes_accessed=2 * n * block * n_text * block + 4 * n * block * width,
            transcendentals=0,
        ),
        name=f"image_grads_{odd}",
    )(scale, *grads, texts)


def halve(blocks, axis, n, bits):
    for bit in bits:
        far = sorted(q for q in blocks if q & bit)
        sent = swap(jnp.stack([blocks[q] for q in far]), axis, n, bit)
        blocks = {q ^ bit: blocks[q ^ bit] + sent[i] for i, q in enumerate(far)}
    return blocks[0]


def scatter_images(scale, grads, texts, axis, n, block):
    far = image_grads(scale, grads, texts, 1, block)
    sent = swap(far, axis, n, 1)
    near = image_grads(scale, grads, texts, 0, block)
    half = block // 2
    bits = [1 << b for b in range(1, n.bit_length() - 1)]
    parts = []
    for piece, order in ((slice(0, half), bits), (slice(half, block), bits[::-1])):
        blocks = {2 * j: near[j, piece] + sent[j, piece] for j in range(n // 2)}
        parts.append(halve(blocks, axis, n, order))
    return jnp.concatenate(parts, axis=0)


def line_scatter(parts, axis):
    ends = [(0, 1), (3, 2)]
    middle = [(1, 2), (2, 1)]
    outward = [(1, 0), (2, 3)]
    first = lax.ppermute(parts[3], axis, ends)
    second = lax.ppermute(parts[2], axis, ends)
    second_middle = lax.ppermute(parts[2] + first, axis, middle)
    third = lax.ppermute(parts[1], axis, ends)
    third_middle = lax.ppermute(parts[3] + second, axis, middle)
    third_out = lax.ppermute(parts[1] + second_middle, axis, outward)
    return parts[0] + (third + third_middle + third_out)


def on_device(n_row, n_col, image_embeds, text_embeds, logit_scale):
    block = image_embeds.shape[0]
    r, c = lax.axis_index("row"), lax.axis_index("col")
    scale = logit_scale.reshape(1, 1)
    coef = scale * LOG2E
    image_half = image_embeds.astype(jnp.bfloat16)
    text_half = text_embeds.astype(jnp.bfloat16)
    text_blocks = [text_half] + [swap(text_half, "row", n_row, q) for q in range(1, n_row)]
    image_blocks = gather_hops(image_half, "col", n_col)
    image_pieces = [p for pieces in image_blocks for p in pieces]

    row_own, col_own, images, texts = stats(coef, image_pieces, text_blocks, block)
    row_parts = [row_own] + [swap(row_own, "col", n_col, q) for q in range(1, n_col)]
    col_parts = [col_own] + [swap(col_own, "row", n_row, q) for q in range(1, n_row)]
    row_lse, col_lse = lse(row_parts, col_parts, block)

    image_ids = r * n_col + (c ^ jnp.arange(n_col, dtype=jnp.int32))
    grads, parts, sums = {}, {}, []
    order = [3, 2, 1, 0] if n_row == 4 else list(range(n_row))[::-1]
    for t in order:
        same = (image_ids == c * n_row + (r ^ t)).astype(jnp.float32).reshape(1, n_col)
        grads[t], parts[t], partial = text_grads(
            scale, coef, same, images, texts, row_lse, col_lse, t, block
        )
        sums.append(partial)
    if n_row == 4:
        grad_text = line_scatter(parts, "row")
    else:
        grad_text = halve(parts, "row", n_row, [1 << b for b in range(n_row.bit_length() - 1)])

    total = functools.reduce(jnp.add, sums)
    for axis, n in (("col", n_col), ("row", n_row)):
        for b in range(n.bit_length() - 1):
            total = total + swap(total, axis, n, 1 << b)
    grad_scale = jnp.sum(total)

    grad_image = scatter_images(
        scale, [grads[t] for t in range(n_row)], texts, "col", n_col, block
    )
    return grad_image, grad_text, grad_scale


def solution(mesh):
    images = P(("row", "col"), None)
    texts = P(("col", "row"), None)
    return jax.shard_map(
        functools.partial(on_device, mesh.shape["row"], mesh.shape["col"]),
        mesh=mesh,
        in_specs=(images, texts, P()),
        out_specs=(images, texts, P()),
        check_vma=False,
    )
```

time: 253 us -> 145 us (0.57)
  blocking collectives: 89 us -> 0 us
  waiting for transfers between devices: 108 us -> 52.2 us
  starting transfers between devices: 0.16 us -> 42 us
  Pallas kernels: 0 us -> 31.2 us
  matrix products: 17.7 us -> 0 us
  other arithmetic: 21.5 us -> 5.46 us
  between operations: 14.5 us -> 1.72 us
  local copies, waits for them, and re-layouts: 1.93 us -> 12 us
    psum x3 -> x0, blocking collectives: 64 us -> none  [the longest x1 43.4 us: on_device(): grad_scale = lax.psum(partial_scale, ('row', 'col'))]
    all_gather x2 -> x0, waiting for transfers between devices: 59.1 us -> none  [the longest x1 29.9 us: on_device(): images = lax.all_gather(image_half, 'col', axis=0, tiled=True)]
    ppermute x0 -> x38, waiting for transfers between devices: none -> 52.2 us  [the longest x32 36.7 us: swap(): return lax.ppermute(x, axis, [(i, i ^ q) for i in range(n)])]
    reduce_scatter x2 -> x0, waiting for transfers between devices: 48.6 us -> none  [the longest x1 48.6 us: on_device(): lax.psum_scatter(logit_scale * jnp.dot(picked, text_cols, preferred_eleme...]
    ppermute x0 -> x38, starting transfers between devices: none -> 42 us  [the longest x32 32 us: swap(): return lax.ppermute(x, axis, [(i, i ^ q) for i in range(n)])]
    pallas_call x0 -> x8, Pallas kernels: none -> 31.2 us  [the longest x4 13.1 us: text_grads(): pl.pallas_call(functools.partial(text_kernel, block), grid=(1,), out_shap...]
    pmax x2 -> x0, blocking collectives: 25 us -> none  [the longest x1 13.3 us: on_device(): row_max = lax.pmax(jnp.max(logits, axis=1), 'col')]
    dot_general x3 -> x0, matrix products: 17.7 us -> none  [the longest x1 7.47 us: on_device(): lax.dot_general(images, text_cols, (((1,), (1,)), ((), ())), preferred_el...]
  transfers between devices with their start and end apart: 4 -> 38, of which waited for: 3 -> 14; matrix products, arithmetic and copies ran while one was open for 3% -> 2% of each run, Pallas kernels for 0% -> 2%
where the time goes in v1:
time: 145 us
  waiting for transfers between devices  52.2 us (36%)
  starting transfers between devices  42 us (29%)
  Pallas kernels  31.2 us (22%)
  local copies, waits for them, and re-layouts  12 us (8%)
  other arithmetic  5.46 us (4%)
  between operations  1.72 us (1%)
    ppermute x32, waiting for transfers between devices, swap(): return lax.ppermute(x, axis, [(i, i ^ q) for i in range(n)])  36.7 us
    ppermute x32, starting transfers between devices, swap(): return lax.ppermute(x, axis, [(i, i ^ q) for i in range(n)])  32 us
    pallas_call x4, Pallas kernels, text_grads(): pl.pallas_call(functools.partial(text_kernel, block), grid=(1,), out_shap...  13.1 us
    pallas_call x1, Pallas kernels, stats(): pl.pallas_call(functools.partial(stats_kernel, counts, block), out_shape=...  12 us
    unnamed x54, local copies, waits for them, and re-layouts  12 us
    ppermute x1, waiting for transfers between devices, line_scatter(): first = lax.ppermute(parts[3], axis, ends)  6.66 us
    ppermute x1, waiting for transfers between devices, line_scatter(): third_out = lax.ppermute(parts[1] + second_middle, axis, outward)  5 us
    pallas_call x2, Pallas kernels, image_grads(): pl.pallas_call(functools.partial(image_kernel, n_text, block), grid=(n,),...  4.48 us
  transfers between devices with their start and end apart: 38, of which 14 were waited for; matrix products, arithmetic and copies ran while one was open for 2% of the time, Pallas kernels for 2%

profile of v1, /device:TPU:0, one launch (start us, length us, event | category | flops | bytes accessed | tf_op | source)
XLA Modules:
  0.0 144.6 jit_solution(15218099303674692342)
XLA Ops:
  1.7 3.0 %collective-permute-start.3 = (bf16[256,512]{1,0:T(8,128)(2,1)S(1)}, bf16[256,512]{1,0:T(8,128)(2,1)S(1)}, u32[]{:S(2)}, u32[]{:S(2)}) collective-permute-start(bf16[256,512]{1,0:T(8,128)(2,1)S(1)} %convert_element_type.47.refs_0_), channel_id=1, source_target_pairs={{0,4},{1,5},{2,6},{3,7},{4,0},{5,1},{6,2},{7,3},{8,12},{9,13},{10,... | collective-permute-start | bytes 786440 | tf_op jit(solution)/shard_map/ppermute | solution.py:19
  4.7 1.5 %collective-permute-start.1 = (bf16[256,512]{1,0:T(8,128)(2,1)S(1)}, bf16[256,512]{1,0:T(8,128)(2,1)S(1)}, u32[]{:S(2)}, u32[]{:S(2)}) collective-permute-start(bf16[256,512]{1,0:T(8,128)(2,1)S(1)} %convert_element_type.47.refs_0_), channel_id=1, source_target_pairs={{0,2},{1,3},{2,0},{3,1},{4,6},{5,7},{6,4},{7,5},{8,10},{9,11},{10,... | collective-permute-start | bytes 786440 | tf_op jit(solution)/shard_map/ppermute | solution.py:19
  7.3 3.7 %collective-permute-start.11 = (bf16[256,512]{1,0:T(8,128)(2,1)S(1)}, bf16[256,512]{1,0:T(8,128)(2,1)S(1)}, u32[]{:S(2)}, u32[]{:S(2)}) collective-permute-start(bf16[256,512]{1,0:T(8,128)(2,1)S(1)} %convert_element_type.48.refs_10_), channel_id=1, source_target_pairs={{0,24},{8,16},{16,8},{24,0},{1,25},{9,17},{17,9},{25,1},{2,26},{10... | collective-permute-start | bytes 786440 | tf_op jit(solution)/shard_map/ppermute | solution.py:19
  12.5 1.5 %collective-permute-start.6 = (bf16[128,512]{1,0:T(8,128)(2,1)S(1)}, bf16[128,512]{1,0:T(8,128)(2,1)S(1)}, u32[]{:S(2)}, u32[]{:S(2)}) collective-permute-start(bf16[128,512]{1,0:T(8,128)(2,1)S(1)} %slice.89), channel_id=1, source_target_pairs={{0,2},{1,3},{2,0},{3,1},{4,6},{5,7},{6,4},{7,5},{8,10},{9,11},{10,... | collective-permute-start | bytes 393224 | tf_op jit(solution)/shard_map/ppermute | solution.py:19
  14.0 4.5 %collective-permute-done.11.refs_13_ = bf16[256,512]{1,0:T(8,128)(2,1)S(1)} collective-permute-done((bf16[256,512]{1,0:T(8,128)(2,1)S(1)}, bf16[256,512]{1,0:T(8,128)(2,1)S(1)}, u32[]{:S(2)}, u32[]{:S(2)}) %collective-permute-start.11) | collective-permute-done | bytes 262176 | tf_op jit(solution)/shard_map/ppermute | solution.py:19
  19.0 13.7 %collective-permute-done.10.refs_12_ = bf16[256,512]{1,0:T(8,128)(2,1)S(1)} collective-permute-done((bf16[256,512]{1,0:T(8,128)(2,1)S(1)}, bf16[256,512]{1,0:T(8,128)(2,1)S(1)}, u32[]{:S(2)}, u32[]{:S(2)}) %collective-permute-start.10) | collective-permute-done | bytes 262176 | tf_op jit(solution)/shard_map/ppermute | solution.py:19
  42.3 12.0 %stats.1 = (f32[2,2048]{1,0:T(2,128)S(1)}, f32[2,1024]{1,0:T(2,128)S(1)}, bf16[2048,512]{1,0:T(8,128)(2,1)}, bf16[1024,512]{1,0:T(8,128)(2,1)S(1)}) custom-call(f32[1,1]{1,0:T(1,128)S(6)} %mul.12.coef_ref, bf16[256,512]{1,0:T(8,128)(2,1)S(1)} %convert_element_type.47.refs_0_, bf16[256,512]{1,0:T(8,128)(2,1)S(1)} %collective-permute-done.refs_1_, ...), custom_call_target="tpu_custom_call" | custom-call | flops 2147483648 | bytes 6291456 | tf_op jit(solution)/shard_map/stats/pallas_call | solution.py:128
  54.4 2.5 %collective-permute-start.21 = (f32[2,1024]{1,0:T(2,128)S(1)}, f32[2,1024]{1,0:T(2,128)S(1)}, u32[]{:S(2)}, u32[]{:S(2)}) collective-permute-start(f32[2,1024]{1,0:T(2,128)S(1)} %get-tuple-element.24.refs_8_), channel_id=1, source_target_pairs={{0,24},{8,16},{16,8},{24,0},{1,25},{9,17},{17,9},{25,1},{2,26},{10... | collective-permute-start | bytes 24584 | tf_op jit(solution)/shard_map/ppermute | solution.py:19
  57.0 1.9 %collective-permute-start.19 = (f32[2,1024]{1,0:T(2,128)S(1)}, f32[2,1024]{1,0:T(2,128)S(1)}, u32[]{:S(2)}, u32[]{:S(2)}) collective-permute-start(f32[2,1024]{1,0:T(2,128)S(1)} %get-tuple-element.24.refs_8_), channel_id=1, source_target_pairs={{0,8},{8,0},{16,24},{24,16},{1,9},{9,1},{17,25},{25,17},{2,10},{10... | collective-permute-start | bytes 24584 | tf_op jit(solution)/shard_map/ppermute | solution.py:19
  58.9 1.8 %collective-permute-start.17 = (f32[2,2048]{1,0:T(2,128)S(1)}, f32[2,2048]{1,0:T(2,128)S(1)}, u32[]{:S(2)}, u32[]{:S(2)}) collective-permute-start(f32[2,2048]{1,0:T(2,128)S(1)} %get-tuple-element.23.refs_0_), channel_id=1, source_target_pairs={{0,6},{1,7},{2,4},{3,5},{4,2},{5,3},{6,0},{7,1},{8,14},{9,15},{10,... | collective-permute-start | bytes 49160 | tf_op jit(solution)/shard_map/ppermute | solution.py:19
  61.8 1.5 %collective-permute-start.15 = (f32[2,2048]{1,0:T(2,128)S(1)}, f32[2,2048]{1,0:T(2,128)S(1)}, u32[]{:S(2)}, u32[]{:S(2)}) collective-permute-start(f32[2,2048]{1,0:T(2,128)S(1)} %get-tuple-element.23.refs_0_), channel_id=1, source_target_pairs={{0,4},{1,5},{2,6},{3,7},{4,0},{5,1},{6,2},{7,3},{8,12},{9,13},{10,... | collective-permute-start | bytes 49160 | tf_op jit(solution)/shard_map/ppermute | solution.py:19
  68.4 1.5 %lse.1 = (f32[1,2048]{1,0:T(1,128)}, f32[1,1024]{1,0:T(1,128)}) custom-call(f32[2,2048]{1,0:T(2,128)} %copy-done, f32[2,2048]{1,0:T(2,128)} %copy-done.23, f32[2,2048]{1,0:T(2,128)} %copy-done.22, f32[2,2048]{1,0:T(2,128)} %copy-done.21, f32[2,2048]{1,0:T(2,128)} %copy-done.20, f32[2,2048]{1,0:T(2,128)} %copy-done.19, f32[2,2048]{1,0:T(2,128)} %copy-done.18, ...), custom_call_target="tpu_custom_call" | custom-call | tf_op jit(solution)/shard_map/lse/pallas_call | solution.py:179
  71.3 1.6 %copy-done.16 = bf16[2048,512]{1,0:T(8,128)(2,1)S(1)} copy-done((bf16[2048,512]{1,0:T(8,128)(2,1)S(1)}, bf16[2048,512]{1,0:T(8,128)(2,1)}, u32[]{:S(2)}) %copy-start.16) | copy-done | bytes 2097176
  72.9 3.3 %text_grads_3.1 = (bf16[256,2048]{1,0:T(8,128)(2,1)S(1)}, f32[256,512]{1,0:T(8,128)S(1)}, f32[8,128]{1,0:T(8,128)S(1)}) custom-call(f32[1,1]{1,0:T(1,128)} %bitcast.9.scale_ref, f32[1,1]{1,0:T(1,128)S(6)} %mul.12.coef_ref, f32[1,8]{1,0:T(1,128)S(1)} %get-tuple-element.39.same_ref, bf16[2048,512]{1,0:T(8,128)(2,1)S(1)} %copy-done.16, ...), custom_call_target="tpu_custom_call" | custom-call | flops 1073741824 | bytes 3932160 | tf_op jit(solution)/shard_map/text_grads_3/pallas_call | solution.py:231
  76.2 3.3 %text_grads_2.1 = (bf16[256,2048]{1,0:T(8,128)(2,1)S(1)}, f32[256,512]{1,0:T(8,128)S(1)}, f32[8,128]{1,0:T(8,128)S(1)}) custom-call(f32[1,1]{1,0:T(1,128)} %bitcast.8.scale_ref, f32[1,1]{1,0:T(1,128)S(6)} %mul.12.coef_ref, f32[1,8]{1,0:T(1,128)S(1)} %get-tuple-element.48.same_ref, bf16[2048,512]{1,0:T(8,128)(2,1)S(1)} %copy-done.16, ...), custom_call_target="tpu_custom_call" | custom-call | flops 1073741824 | bytes 3932160 | tf_op jit(solution)/shard_map/text_grads_2/pallas_call | solution.py:231
  79.5 3.3 %text_grads_1.1 = (bf16[256,2048]{1,0:T(8,128)(2,1)S(1)}, f32[256,512]{1,0:T(8,128)S(1)}, f32[8,128]{1,0:T(8,128)S(1)}) custom-call(f32[1,1]{1,0:T(1,128)} %bitcast.7.scale_ref, f32[1,1]{1,0:T(1,128)S(6)} %mul.12.coef_ref, f32[1,8]{1,0:T(1,128)S(1)} %get-tuple-element.49.same_ref, bf16[2048,512]{1,0:T(8,128)(2,1)S(1)} %copy-done.16, ...), custom_call_target="tpu_custom_call" | custom-call | flops 1073741824 | bytes 3932160 | tf_op jit(solution)/shard_map/text_grads_1/pallas_call | solution.py:231
  82.8 3.3 %text_grads_0.1 = (bf16[256,2048]{1,0:T(8,128)(2,1)S(1)}, f32[256,512]{1,0:T(8,128)S(1)}, f32[8,128]{1,0:T(8,128)S(1)}) custom-call(f32[1,1]{1,0:T(1,128)} %bitcast.6.scale_ref, f32[1,1]{1,0:T(1,128)S(6)} %mul.12.coef_ref, f32[1,8]{1,0:T(1,128)S(1)} %get-tuple-element.50.same_ref, bf16[2048,512]{1,0:T(8,128)(2,1)S(1)} %copy-done.16, ...), custom_call_target="tpu_custom_call" | custom-call | flops 1073741824 | bytes 3932160 | tf_op jit(solution)/shard_map/text_grads_0/pallas_call | solution.py:231
  86.1 2.2 %image_grads_1.1 = f32[4,256,512]{2,1,0:T(8,128)S(1)} custom-call(f32[1,1]{1,0:T(1,128)} %bitcast.11.scale_ref, bf16[256,2048]{1,0:T(8,128)(2,1)S(1)} %get-tuple-element.27.refs_0_, bf16[256,2048]{1,0:T(8,128)(2,1)S(1)} %get-tuple-element.28.refs_1_, bf16[256,2048]{1,0:T(8,128)(2,1)S(1)} %get-tuple-element.29.refs_2_, ...), custom_call_target="tpu_custom_call" | custom-call | flops 1073741824 | bytes 4194304 | tf_op jit(solution)/shard_map/image_grads_1/pallas_call | solution.py:278
  88.4 2.0 %collective-permute-start.30 = (f32[256,512]{1,0:T(8,128)S(1)}, f32[256,512]{1,0:T(8,128)S(1)}, u32[]{:S(2)}, u32[]{:S(2)}) collective-permute-start(f32[256,512]{1,0:T(8,128)S(1)} %get-tuple-element.33), channel_id=1, source_target_pairs={{0,8},{24,16},{1,9},{25,17},{2,10},{26,18},{3,11},{27,19},{4,12},{... | collective-permute-start | bytes 1572872 | tf_op jit(solution)/shard_map/ppermute | solution.py:321
  90.5 2.2 %image_grads_0.1 = f32[4,256,512]{2,1,0:T(8,128)S(1)} custom-call(f32[1,1]{1,0:T(1,128)} %bitcast.10.scale_ref, bf16[256,2048]{1,0:T(8,128)(2,1)S(1)} %get-tuple-element.27.refs_0_, bf16[256,2048]{1,0:T(8,128)(2,1)S(1)} %get-tuple-element.28.refs_1_, bf16[256,2048]{1,0:T(8,128)(2,1)S(1)} %get-tuple-element.29.refs_2_, ...), custom_call_target="tpu_custom_call" | custom-call | flops 1073741824 | bytes 4194304 | tf_op jit(solution)/shard_map/image_grads_0/pallas_call | solution.py:278
  92.9 1.4 collective-permute-start.23
  94.2 1.8 %collective-permute-start.28 = (f32[256,512]{1,0:T(8,128)S(1)}, f32[256,512]{1,0:T(8,128)S(1)}, u32[]{:S(2)}, u32[]{:S(2)}) collective-permute-start(f32[256,512]{1,0:T(8,128)S(1)} %get-tuple-element.34), channel_id=1, source_target_pairs={{0,8},{24,16},{1,9},{25,17},{2,10},{26,18},{3,11},{27,19},{4,12},{... | collective-permute-start | bytes 1572872 | tf_op jit(solution)/shard_map/ppermute | solution.py:322
  96.0 6.7 %collective-permute-done.30 = f32[256,512]{1,0:T(8,128)S(1)} collective-permute-done((f32[256,512]{1,0:T(8,128)S(1)}, f32[256,512]{1,0:T(8,128)S(1)}, u32[]{:S(2)}, u32[]{:S(2)}) %collective-permute-start.30) | collective-permute-done | bytes 524320 | tf_op jit(solution)/shard_map/ppermute | solution.py:321
  103.4 3.5 %collective-permute-done.23 = f32[2,128,512]{2,1,0:T(8,128)S(1)} collective-permute-done((f32[2,128,512]{2,1,0:T(8,128)S(1)}, f32[2,128,512]{2,1,0:T(8,128)S(1)}, u32[]{:S(2)}, u32[]{:S(2)}) %collective-permute-start.23) | collective-permute-done | bytes 524320 | tf_op jit(solution)/shard_map/ppermute | solution.py:19
  110.2 2.4 %collective-permute-done.34 = f32[8,128]{1,0:T(8,128)S(1)} collective-permute-done((f32[8,128]{1,0:T(8,128)S(1)}, f32[8,128]{1,0:T(8,128)S(1)}, u32[]{:S(2)}, u32[]{:S(2)}) %collective-permute-start.34) | collective-permute-done | bytes 4128 | tf_op jit(solution)/shard_map/ppermute | solution.py:19
  112.6 1.5 %collective-permute-start.35 = (f32[8,128]{1,0:T(8,128)S(1)}, f32[8,128]{1,0:T(8,128)S(1)}, u32[]{:S(2)}, u32[]{:S(2)}) collective-permute-start(f32[8,128]{1,0:T(8,128)S(1)} %add.171), channel_id=1, source_target_pairs={{0,4},{1,5},{2,6},{3,7},{4,0},{5,1},{6,2},{7,3},{8,12},{9,13},{10,... | collective-permute-start | bytes 12296 | tf_op jit(solution)/shard_map/ppermute | solution.py:19
  114.1 6.5 %collective-permute-done.35 = f32[8,128]{1,0:T(8,128)S(1)} collective-permute-done((f32[8,128]{1,0:T(8,128)S(1)}, f32[8,128]{1,0:T(8,128)S(1)}, u32[]{:S(2)}, u32[]{:S(2)}) %collective-permute-start.35) | collective-permute-done | bytes 4128 | tf_op jit(solution)/shard_map/ppermute | solution.py:19
  121.8 2.3 %collective-permute-done.36 = f32[8,128]{1,0:T(8,128)S(1)} collective-permute-done((f32[8,128]{1,0:T(8,128)S(1)}, f32[8,128]{1,0:T(8,128)S(1)}, u32[]{:S(2)}, u32[]{:S(2)}) %collective-permute-start.36) | collective-permute-done | bytes 4128 | tf_op jit(solution)/shard_map/ppermute | solution.py:19
  126.0 3.6 %collective-permute-start.27 = (f32[256,512]{1,0:T(8,128)S(1)}, f32[256,512]{1,0:T(8,128)S(1)}, u32[]{:S(2)}, u32[]{:S(2)}) collective-permute-start(f32[256,512]{1,0:T(8,128)S(1)} %get-tuple-element.32), channel_id=1, source_target_pairs={{0,8},{24,16},{1,9},{25,17},{2,10},{26,18},{3,11},{27,19},{4,12},{... | collective-permute-start | bytes 1572872 | tf_op jit(solution)/shard_map/ppermute | solution.py:324
  132.5 1.3 collective-permute-start.26
  133.9 3.8 %collective-permute-done.27 = f32[256,512]{1,0:T(8,128)S(1)} collective-permute-done((f32[256,512]{1,0:T(8,128)S(1)}, f32[256,512]{1,0:T(8,128)S(1)}, u32[]{:S(2)}, u32[]{:S(2)}) %collective-permute-start.27) | collective-permute-done | bytes 524320 | tf_op jit(solution)/shard_map/ppermute | solution.py:324
  137.7 5.0 %collective-permute-done.32 = f32[256,512]{1,0:T(8,128)S(1)} collective-permute-done((f32[256,512]{1,0:T(8,128)S(1)}, f32[256,512]{1,0:T(8,128)S(1)}, u32[]{:S(2)}, u32[]{:S(2)}) %collective-permute-start.32) | collective-permute-done | bytes 524320 | tf_op jit(solution)/shard_map/ppermute | solution.py:326
  (129 shorter events, 32.8 us)
Async XLA Ops:
  1.7 10.1 %collective-permute-start.3 = (bf16[256,512]{1,0:T(8,128)(2,1)S(1)}, bf16[256,512]{1,0:T(8,128)(2,1)S(1)}, u32[]{:S(2)}, u32[]{:S(2)}) collective-permute-start(bf16[256,512]{1,0:T(8,128)(2,1)S(1)} %convert_element_type.47.refs_0_), channel_id=1, source_target_pairs={{0,4},{1,5},{2,6},{3,7},{4,0},{5,1},{6,2},{7,3},{8,12},{9,13},{10,... | collective-permute-start | bytes 786440 | tf_op jit(solution)/shard_map/ppermute | solution.py:19
  4.7 7.8 %collective-permute-start.1 = (bf16[256,512]{1,0:T(8,128)(2,1)S(1)}, bf16[256,512]{1,0:T(8,128)(2,1)S(1)}, u32[]{:S(2)}, u32[]{:S(2)}) collective-permute-start(bf16[256,512]{1,0:T(8,128)(2,1)S(1)} %convert_element_type.47.refs_0_), channel_id=1, source_target_pairs={{0,2},{1,3},{2,0},{3,1},{4,6},{5,7},{6,4},{7,5},{8,10},{9,11},{10,... | collective-permute-start | bytes 786440 | tf_op jit(solution)/shard_map/ppermute | solution.py:19
  7.3 11.2 %collective-permute-start.11 = (bf16[256,512]{1,0:T(8,128)(2,1)S(1)}, bf16[256,512]{1,0:T(8,128)(2,1)S(1)}, u32[]{:S(2)}, u32[]{:S(2)}) collective-permute-start(bf16[256,512]{1,0:T(8,128)(2,1)S(1)} %convert_element_type.48.refs_10_), channel_id=1, source_target_pairs={{0,24},{8,16},{16,8},{24,0},{1,25},{9,17},{17,9},{25,1},{2,26},{10... | collective-permute-start | bytes 786440 | tf_op jit(solution)/shard_map/ppermute | solution.py:19
  11.0 21.7 %collective-permute-start.10 = (bf16[256,512]{1,0:T(8,128)(2,1)S(1)}, bf16[256,512]{1,0:T(8,128)(2,1)S(1)}, u32[]{:S(2)}, u32[]{:S(2)}) collective-permute-start(bf16[256,512]{1,0:T(8,128)(2,1)S(1)} %convert_element_type.48.refs_10_), channel_id=1, source_target_pairs={{0,16},{8,24},{16,0},{24,8},{1,17},{9,25},{17,1},{25,9},{2,18},{10... | collective-permute-start | bytes 786440 | tf_op jit(solution)/shard_map/ppermute | solution.py:19
  11.0 21.8 %collective-permute-start.9 = (bf16[256,512]{1,0:T(8,128)(2,1)S(1)}, bf16[256,512]{1,0:T(8,128)(2,1)S(1)}, u32[]{:S(2)}, u32[]{:S(2)}) collective-permute-start(bf16[256,512]{1,0:T(8,128)(2,1)S(1)} %convert_element_type.48.refs_10_), channel_id=1, source_target_pairs={{0,8},{8,0},{16,24},{24,16},{1,9},{9,1},{17,25},{25,17},{2,10},{10... | collective-permute-start | bytes 786440 | tf_op jit(solution)/shard_map/ppermute | solution.py:19
  11.8 24.0 %collective-permute-start = (bf16[256,512]{1,0:T(8,128)(2,1)S(1)}, bf16[256,512]{1,0:T(8,128)(2,1)S(1)}, u32[]{:S(2)}, u32[]{:S(2)}) collective-permute-start(bf16[256,512]{1,0:T(8,128)(2,1)S(1)} %convert_element_type.47.refs_0_), channel_id=1, source_target_pairs={{0,1},{1,0},{2,3},{3,2},{4,5},{5,4},{6,7},{7,6},{8,9},{9,8},{10,11... | collective-permute-start | bytes 786440 | tf_op jit(solution)/shard_map/ppermute | solution.py:19
  12.5 20.7 %collective-permute-start.6 = (bf16[128,512]{1,0:T(8,128)(2,1)S(1)}, bf16[128,512]{1,0:T(8,128)(2,1)S(1)}, u32[]{:S(2)}, u32[]{:S(2)}) collective-permute-start(bf16[128,512]{1,0:T(8,128)(2,1)S(1)} %slice.89), channel_id=1, source_target_pairs={{0,2},{1,3},{2,0},{3,1},{4,6},{5,7},{6,4},{7,5},{8,10},{9,11},{10,... | collective-permute-start | bytes 393224 | tf_op jit(solution)/shard_map/ppermute | solution.py:19
  18.5 15.5 %collective-permute-start.5 = (bf16[128,512]{1,0:T(8,128)(2,1)S(1)}, bf16[128,512]{1,0:T(8,128)(2,1)S(1)}, u32[]{:S(2)}, u32[]{:S(2)}) collective-permute-start(bf16[128,512]{1,0:T(8,128)(2,1)S(1)} %slice.88), channel_id=1, source_target_pairs={{0,4},{1,5},{2,6},{3,7},{4,0},{5,1},{6,2},{7,3},{8,12},{9,13},{10,... | collective-permute-start | bytes 393224 | tf_op jit(solution)/shard_map/ppermute | solution.py:19
  32.7 3.7 %collective-permute-start.4 = (bf16[256,512]{1,0:T(8,128)(2,1)S(1)}, bf16[256,512]{1,0:T(8,128)(2,1)S(1)}, u32[]{:S(2)}, u32[]{:S(2)}) collective-permute-start(bf16[256,512]{1,0:T(8,128)(2,1)S(1)} %collective-permute-done.3.refs_4_), channel_id=1, source_target_pairs={{0,1},{1,0},{2,3},{3,2},{4,5},{5,4},{6,7},{7,6},{8,9},{9,8},{10,11... | collective-permute-start | bytes 786440 | tf_op jit(solution)/shard_map/ppermute | solution.py:19
  32.7 4.3 %collective-permute-start.2 = (bf16[256,512]{1,0:T(8,128)(2,1)S(1)}, bf16[256,512]{1,0:T(8,128)(2,1)S(1)}, u32[]{:S(2)}, u32[]{:S(2)}) collective-permute-start(bf16[256,512]{1,0:T(8,128)(2,1)S(1)} %collective-permute-done.1.refs_2_), channel_id=1, source_target_pairs={{0,1},{1,0},{2,3},{3,2},{4,5},{5,4},{6,7},{7,6},{8,9},{9,8},{10,11... | collective-permute-start | bytes 786440 | tf_op jit(solution)/shard_map/ppermute | solution.py:19
  54.4 6.2 %collective-permute-start.21 = (f32[2,1024]{1,0:T(2,128)S(1)}, f32[2,1024]{1,0:T(2,128)S(1)}, u32[]{:S(2)}, u32[]{:S(2)}) collective-permute-start(f32[2,1024]{1,0:T(2,128)S(1)} %get-tuple-element.24.refs_8_), channel_id=1, source_target_pairs={{0,24},{8,16},{16,8},{24,0},{1,25},{9,17},{17,9},{25,1},{2,26},{10... | collective-permute-start | bytes 24584 | tf_op jit(solution)/shard_map/ppermute | solution.py:19
  57.0 4.9 %collective-permute-start.20 = (f32[2,1024]{1,0:T(2,128)S(1)}, f32[2,1024]{1,0:T(2,128)S(1)}, u32[]{:S(2)}, u32[]{:S(2)}) collective-permute-start(f32[2,1024]{1,0:T(2,128)S(1)} %get-tuple-element.24.refs_8_), channel_id=1, source_target_pairs={{0,16},{8,24},{16,0},{24,8},{1,17},{9,25},{17,1},{25,9},{2,18},{10... | collective-permute-start | bytes 24584 | tf_op jit(solution)/shard_map/ppermute | solution.py:19
  57.0 6.4 %collective-permute-start.19 = (f32[2,1024]{1,0:T(2,128)S(1)}, f32[2,1024]{1,0:T(2,128)S(1)}, u32[]{:S(2)}, u32[]{:S(2)}) collective-permute-start(f32[2,1024]{1,0:T(2,128)S(1)} %get-tuple-element.24.refs_8_), channel_id=1, source_target_pairs={{0,8},{8,0},{16,24},{24,16},{1,9},{9,1},{17,25},{25,17},{2,10},{10... | collective-permute-start | bytes 24584 | tf_op jit(solution)/shard_map/ppermute | solution.py:19
  58.9 4.5 %collective-permute-start.18 = (f32[2,2048]{1,0:T(2,128)S(1)}, f32[2,2048]{1,0:T(2,128)S(1)}, u32[]{:S(2)}, u32[]{:S(2)}) collective-permute-start(f32[2,2048]{1,0:T(2,128)S(1)} %get-tuple-element.23.refs_0_), channel_id=1, source_target_pairs={{0,7},{1,6},{2,5},{3,4},{4,3},{5,2},{6,1},{7,0},{8,15},{9,14},{10,... | collective-permute-start | bytes 49160 | tf_op jit(solution)/shard_map/ppermute | solution.py:19
  58.9 5.4 %collective-permute-start.17 = (f32[2,2048]{1,0:T(2,128)S(1)}, f32[2,2048]{1,0:T(2,128)S(1)}, u32[]{:S(2)}, u32[]{:S(2)}) collective-permute-start(f32[2,2048]{1,0:T(2,128)S(1)} %get-tuple-element.23.refs_0_), channel_id=1, source_target_pairs={{0,6},{1,7},{2,4},{3,5},{4,2},{5,3},{6,0},{7,1},{8,14},{9,15},{10,... | collective-permute-start | bytes 49160 | tf_op jit(solution)/shard_map/ppermute | solution.py:19
  60.6 4.6 %collective-permute-start.16 = (f32[2,2048]{1,0:T(2,128)S(1)}, f32[2,2048]{1,0:T(2,128)S(1)}, u32[]{:S(2)}, u32[]{:S(2)}) collective-permute-start(f32[2,2048]{1,0:T(2,128)S(1)} %get-tuple-element.23.refs_0_), channel_id=1, source_target_pairs={{0,5},{1,4},{2,7},{3,6},{4,1},{5,0},{6,3},{7,2},{8,13},{9,12},{10,... | collective-permute-start | bytes 49160 | tf_op jit(solution)/shard_map/ppermute | solution.py:19
  61.8 3.7 %collective-permute-start.15 = (f32[2,2048]{1,0:T(2,128)S(1)}, f32[2,2048]{1,0:T(2,128)S(1)}, u32[]{:S(2)}, u32[]{:S(2)}) collective-permute-start(f32[2,2048]{1,0:T(2,128)S(1)} %get-tuple-element.23.refs_0_), channel_id=1, source_target_pairs={{0,4},{1,5},{2,6},{3,7},{4,0},{5,1},{6,2},{7,3},{8,12},{9,13},{10,... | collective-permute-start | bytes 49160 | tf_op jit(solution)/shard_map/ppermute | solution.py:19
  63.4 3.8 %collective-permute-start.13 = (f32[2,2048]{1,0:T(2,128)S(1)}, f32[2,2048]{1,0:T(2,128)S(1)}, u32[]{:S(2)}, u32[]{:S(2)}) collective-permute-start(f32[2,2048]{1,0:T(2,128)S(1)} %get-tuple-element.23.refs_0_), channel_id=1, source_target_pairs={{0,2},{1,3},{2,0},{3,1},{4,6},{5,7},{6,4},{7,5},{8,10},{9,11},{10,... | collective-permute-start | bytes 49160 | tf_op jit(solution)/shard_map/ppermute | solution.py:19
  88.3 4.4 %collective-permute-start.22 = (f32[4,256,512]{2,1,0:T(8,128)S(1)}, f32[4,256,512]{2,1,0:T(8,128)S(1)}, u32[]{:S(2)}, u32[]{:S(2)}) collective-permute-start(f32[4,256,512]{2,1,0:T(8,128)S(1)} %image_grads_1.1), channel_id=1, source_target_pairs={{0,1},{1,0},{2,3},{3,2},{4,5},{5,4},{6,7},{7,6},{8,9},{9,8},{10,11... | collective-permute-start | bytes 6291464 | tf_op jit(solution)/shard_map/ppermute | solution.py:19
  88.4 14.2 %collective-permute-start.30 = (f32[256,512]{1,0:T(8,128)S(1)}, f32[256,512]{1,0:T(8,128)S(1)}, u32[]{:S(2)}, u32[]{:S(2)}) collective-permute-start(f32[256,512]{1,0:T(8,128)S(1)} %get-tuple-element.33), channel_id=1, source_target_pairs={{0,8},{24,16},{1,9},{25,17},{2,10},{26,18},{3,11},{27,19},{4,12},{... | collective-permute-start | bytes 1572872 | tf_op jit(solution)/shard_map/ppermute | solution.py:321
  92.9 14.1 %collective-permute-start.23 = (f32[2,128,512]{2,1,0:T(8,128)S(1)}, f32[2,128,512]{2,1,0:T(8,128)S(1)}, u32[]{:S(2)}, u32[]{:S(2)}) collective-permute-start(f32[2,128,512]{2,1,0:T(8,128)S(1)} %pad_maximum_fusion), channel_id=1, source_target_pairs={{0,2},{1,3},{2,0},{3,1},{4,6},{5,7},{6,4},{7,5},{8,10},{9,11},{10,... | collective-permute-start | bytes 1572872 | tf_op jit(solution)/shard_map/ppermute | solution.py:19
  94.2 31.8 %collective-permute-start.28 = (f32[256,512]{1,0:T(8,128)S(1)}, f32[256,512]{1,0:T(8,128)S(1)}, u32[]{:S(2)}, u32[]{:S(2)}) collective-permute-start(f32[256,512]{1,0:T(8,128)S(1)} %get-tuple-element.34), channel_id=1, source_target_pairs={{0,8},{24,16},{1,9},{25,17},{2,10},{26,18},{3,11},{27,19},{4,12},{... | collective-permute-start | bytes 1572872 | tf_op jit(solution)/shard_map/ppermute | solution.py:322
  102.7 26.9 %collective-permute-start.31 = (f32[256,512]{1,0:T(8,128)S(1)}, f32[256,512]{1,0:T(8,128)S(1)}, u32[]{:S(2)}, u32[]{:S(2)}) collective-permute-start(f32[256,512]{1,0:T(8,128)S(1)} %add.163), channel_id=1, source_target_pairs={{8,16},{16,8},{9,17},{17,9},{10,18},{18,10},{11,19},{19,11},{12,20... | collective-permute-start | bytes 1572872 | tf_op jit(solution)/shard_map/ppermute | solution.py:323
  107.2 25.2 %collective-permute-start.25 = (f32[2,128,512]{2,1,0:T(8,128)S(1)}, f32[2,128,512]{2,1,0:T(8,128)S(1)}, u32[]{:S(2)}, u32[]{:S(2)}) collective-permute-start(f32[2,128,512]{2,1,0:T(8,128)S(1)} %pad_maximum_fusion.1), channel_id=1, source_target_pairs={{0,4},{1,5},{2,6},{3,7},{4,0},{5,1},{6,2},{7,3},{8,12},{9,13},{10,... | collective-permute-start | bytes 1572872 | tf_op jit(solution)/shard_map/ppermute | solution.py:19
  108.9 3.6 %collective-permute-start.34 = (f32[8,128]{1,0:T(8,128)S(1)}, f32[8,128]{1,0:T(8,128)S(1)}, u32[]{:S(2)}, u32[]{:S(2)}) collective-permute-start(f32[8,128]{1,0:T(8,128)S(1)} %add.170), channel_id=1, source_target_pairs={{0,2},{1,3},{2,0},{3,1},{4,6},{5,7},{6,4},{7,5},{8,10},{9,11},{10,... | collective-permute-start | bytes 12296 | tf_op jit(solution)/shard_map/ppermute | solution.py:19
  112.6 8.0 %collective-permute-start.35 = (f32[8,128]{1,0:T(8,128)S(1)}, f32[8,128]{1,0:T(8,128)S(1)}, u32[]{:S(2)}, u32[]{:S(2)}) collective-permute-start(f32[8,128]{1,0:T(8,128)S(1)} %add.171), channel_id=1, source_target_pairs={{0,4},{1,5},{2,6},{3,7},{4,0},{5,1},{6,2},{7,3},{8,12},{9,13},{10,... | collective-permute-start | bytes 12296 | tf_op jit(solution)/shard_map/ppermute | solution.py:19
  124.2 6.3 %collective-permute-start.37 = (f32[8,128]{1,0:T(8,128)S(1)}, f32[8,128]{1,0:T(8,128)S(1)}, u32[]{:S(2)}, u32[]{:S(2)}) collective-permute-start(f32[8,128]{1,0:T(8,128)S(1)} %add.173), channel_id=1, source_target_pairs={{0,16},{8,24},{16,0},{24,8},{1,17},{9,25},{17,1},{25,9},{2,18},{10... | collective-permute-start | bytes 12296 | tf_op jit(solution)/shard_map/ppermute | solution.py:19
  125.5 6.9 %collective-permute-start.24 = (f32[1,128,512]{2,1,0:T(8,128)S(1)}, f32[1,128,512]{2,1,0:T(8,128)S(1)}, u32[]{:S(2)}, u32[]{:S(2)}) collective-permute-start(f32[1,128,512]{2,1,0:T(8,128)S(1)} %get-tuple-element.43), channel_id=1, source_target_pairs={{0,4},{1,5},{2,6},{3,7},{4,0},{5,1},{6,2},{7,3},{8,12},{9,13},{10,... | collective-permute-start | bytes 786440 | tf_op jit(solution)/shard_map/ppermute | solution.py:19
  126.0 11.7 %collective-permute-start.27 = (f32[256,512]{1,0:T(8,128)S(1)}, f32[256,512]{1,0:T(8,128)S(1)}, u32[]{:S(2)}, u32[]{:S(2)}) collective-permute-start(f32[256,512]{1,0:T(8,128)S(1)} %get-tuple-element.32), channel_id=1, source_target_pairs={{0,8},{24,16},{1,9},{25,17},{2,10},{26,18},{3,11},{27,19},{4,12},{... | collective-permute-start | bytes 1572872 | tf_op jit(solution)/shard_map/ppermute | solution.py:324
  129.6 8.0 %collective-permute-start.29 = (f32[256,512]{1,0:T(8,128)S(1)}, f32[256,512]{1,0:T(8,128)S(1)}, u32[]{:S(2)}, u32[]{:S(2)}) collective-permute-start(f32[256,512]{1,0:T(8,128)S(1)} %add.161), channel_id=1, source_target_pairs={{8,16},{16,8},{9,17},{17,9},{10,18},{18,10},{11,19},{19,11},{12,20... | collective-permute-start | bytes 1572872 | tf_op jit(solution)/shard_map/ppermute | solution.py:325
  130.4 12.2 %collective-permute-start.32 = (f32[256,512]{1,0:T(8,128)S(1)}, f32[256,512]{1,0:T(8,128)S(1)}, u32[]{:S(2)}, u32[]{:S(2)}) collective-permute-start(f32[256,512]{1,0:T(8,128)S(1)} %add.164), channel_id=1, source_target_pairs={{8,0},{16,24},{9,1},{17,25},{10,2},{18,26},{11,3},{19,27},{12,4},{... | collective-permute-start | bytes 1572872 | tf_op jit(solution)/shard_map/ppermute | solution.py:326
  132.5 11.1 %collective-permute-start.26 = (f32[1,128,512]{2,1,0:T(8,128)S(1)}, f32[1,128,512]{2,1,0:T(8,128)S(1)}, u32[]{:S(2)}, u32[]{:S(2)}) collective-permute-start(f32[1,128,512]{2,1,0:T(8,128)S(1)} %get-tuple-element.42), channel_id=1, source_target_pairs={{0,2},{1,3},{2,0},{3,1},{4,6},{5,7},{6,4},{7,5},{8,10},{9,11},{10,... | collective-permute-start | bytes 786440 | tf_op jit(solution)/shard_map/ppermute | solution.py:19
  (33 other events, 90.3 us)

commit v2 on v0

v2 whole, which is shorter than its diff:
```python
import functools
import math

import jax
import jax.numpy as jnp
from jax import lax
from jax.experimental import pallas as pl
from jax.experimental.pallas import tpu as pltpu
from jax.sharding import PartitionSpec as P

LOG2E = 1.4426950408889634
LN2 = 0.6931471805599453
LANES = 128
VMEM = pltpu.VMEM
SMEM = pltpu.SMEM
FLOPS = 20


def swap(x, axis, n, q):
    return lax.ppermute(x, axis, [(i, i ^ q) for i in range(n)])


def gather_both(image, text, n_col, n_row):
    rounds = [1 << b for b in range(1, n_col.bit_length() - 1)][::-1]
    if n_row == 4 and n_col == 8:
        four = swap(image, "col", n_col, 4)
        two = swap(image, "col", n_col, 2)
        one = swap(text, "row", n_row, 1)
        middle = [(1, 2), (2, 1)]
        outward = [(1, 0), (2, 3)]
        mid_three = lax.ppermute(text, "row", middle)
        four, two, one, mid_three = lax.optimization_barrier((four, two, one, mid_three))
        six = swap(four, "col", n_col, 2)
        mid_two = lax.ppermute(one, "row", middle)
        end_two = lax.ppermute(mid_three, "row", outward)
        six, mid_two, end_two = lax.optimization_barrier((six, mid_two, end_two))
        even = jnp.concatenate([image, two, four, six], axis=0)
        odd = swap(even, "col", n_col, 1)
        end_three = lax.ppermute(mid_two, "row", outward)
        return even, odd, [text, one, mid_two + end_two, mid_three + end_three]
    blocks = {0: image}
    for bit in rounds:
        for q in sorted(blocks):
            blocks[q | bit] = swap(blocks[q], "col", n_col, bit)
    even = jnp.concatenate([blocks[q] for q in range(0, n_col, 2)], axis=0)
    texts = [text] + [swap(text, "row", n_row, q) for q in range(1, n_row)]
    return even, swap(even, "col", n_col, 1), texts


def cast_kernel(a_ref, b_ref, a_out, b_out):
    a_out[...] = a_ref[...].astype(jnp.bfloat16)
    b_out[...] = b_ref[...].astype(jnp.bfloat16)


def cast_both(a, b):
    vmem = pl.BlockSpec(memory_space=VMEM)
    return pl.pallas_call(
        cast_kernel,
        out_shape=tuple(jax.ShapeDtypeStruct(x.shape, jnp.bfloat16) for x in (a, b)),
        in_specs=[vmem] * 2,
        out_specs=(vmem,) * 2,
        name="cast_both",
    )(a, b)


def nt_dot(a, b):
    return lax.dot_general(a, b, (((1,), (1,)), ((), ())), preferred_element_type=jnp.float32)


def stats_kernel(n_text, first, block, coef_ref, place_ref, *refs):
    halves, texts = refs[:2], refs[2 : 2 + n_text]
    before = refs[2 + n_text : -6]
    row_ref, col_ref, tile, row_max, col_max, col_sum = refs[-6:]
    coef = coef_ref[0, 0]
    r_place, c_place = place_ref[0, 0], place_ref[0, 1]
    cols, rows = tile.shape
    half = rows // 2
    col_max[...] = jnp.full(col_max.shape, -jnp.inf, jnp.float32)

    for odd in range(2):

        def products(j, carry):
            image = halves[odd][pl.ds(pl.multiple_of(j * block, block), block), :]
            at = pl.multiple_of(j * block + odd * half, block)
            top = None
            for t in range(n_text):
                part = pl.ds(t * block, block)
                x = nt_dot(texts[t][...], image) * coef
                tile[part, pl.ds(at, block)] = x
                top_t = jnp.max(x, axis=0, keepdims=True)
                top = top_t if top is None else jnp.maximum(top, top_t)
                held = col_max[part, :]
                for lane in range(0, block, LANES):
                    held = jnp.maximum(held, x[:, lane : lane + LANES])
                col_max[part, :] = held
            row_max[0:1, pl.ds(at, block)] = top
            return carry

        lax.fori_loop(0, half // block, products, 0, unroll=2)

    col_max[...] = jnp.broadcast_to(
        jnp.max(col_max[...], axis=1, keepdims=True), col_max.shape
    )

    def exponentials(i, acc):
        part = pl.ds(pl.multiple_of(i * 8, 8), 8)
        top = col_max[part, :]
        total = None
        out = []
        for lane in range(0, rows, LANES):
            x = tile[part, lane : lane + LANES]
            out.append(acc[lane // LANES] + jnp.exp2(x - row_max[0:1, lane : lane + LANES]))
            e = jnp.exp2(x - top)
            total = e if total is None else total + e
        col_sum[part, :] = total
        return tuple(out)

    acc = lax.fori_loop(
        0,
        cols // 8,
        exponentials,
        tuple(jnp.zeros((8, LANES), jnp.float32) for _ in range(rows // LANES)),
        unroll=2,
    )
    n_col, n_row = row_ref.shape[1], col_ref.shape[1]
    row_ids = lax.broadcasted_iota(jnp.int32, (n_col, block), 0)
    top, total = jnp.zeros((n_col, block), jnp.float32), jnp.zeros((n_col, block), jnp.float32)
    for q in range(n_col):
        at = (q // 2) * block + (q % 2) * half
        sums = [
            jnp.sum(acc[(at + lane) // LANES], axis=0, keepdims=True)
            for lane in range(0, block, LANES)
        ]
        here = row_ids == (c_place ^ q)
        top = jnp.where(here, row_max[0:1, at : at + block], top)
        total = jnp.where(here, jnp.concatenate(sums, axis=1), total)
    if before:
        old_top, old_total = before[0][0], before[0][1]
        new_top = jnp.maximum(top, old_top)
        total = total * jnp.exp2(top - new_top) + old_total * jnp.exp2(old_top - new_top)
        top = new_top
    row_ref[0], row_ref[1] = top, total
    row_ids = lax.broadcasted_iota(jnp.int32, (n_row, block), 0)
    if before:
        top, total = before[1][0], before[1][1]
    else:
        top = total = jnp.zeros((n_row, block), jnp.float32)
    for t in range(n_text):
        part = pl.ds(t * block, block)
        here = row_ids == (r_place ^ (first + t))
        top = jnp.where(here, col_max[part, :].T[0:1, :], top)
        total = jnp.where(here, jnp.sum(col_sum[part, :].T, axis=0, keepdims=True), total)
    col_ref[0], col_ref[1] = top, total


def stats(coef, place, even, odd, texts, before, first, n_row):
    rows = 2 * even.shape[0]
    block, width = texts[0].shape
    cols = block * len(texts)
    vmem = pl.BlockSpec(memory_space=VMEM)
    smem = pl.BlockSpec(memory_space=SMEM)
    return pl.pallas_call(
        functools.partial(stats_kernel, len(texts), first, block),
        out_shape=(
            jax.ShapeDtypeStruct((2, rows // block, block), jnp.float32),
            jax.ShapeDtypeStruct((2, n_row, block), jnp.float32),
        ),
        in_specs=[smem, smem] + [vmem] * (2 + len(texts) + len(before)),
        out_specs=(vmem, vmem),
        scratch_shapes=[
            VMEM((cols, rows), jnp.float32),
            VMEM((8, rows), jnp.float32),
            VMEM((cols, LANES), jnp.float32),
            VMEM((cols, LANES), jnp.float32),
        ],
        compiler_params=pltpu.CompilerParams(vmem_limit_bytes=4 * rows * cols + 8 * 2**20),
        cost_estimate=pl.CostEstimate(
            flops=2 * rows * cols * width,
            bytes_accessed=2 * (rows + cols) * width,
            transcendentals=2 * rows * cols,
        ),
        name=f"stats_{first}",
    )(coef, place, even, odd, *texts, *before)


def merged(a, b):
    top = jnp.maximum(a[0], b[0])
    return jnp.stack([top, a[1] * jnp.exp2(a[0] - top) + b[1] * jnp.exp2(b[0] - top)])


def exchanged_lse(pairs, axis, n):
    for b in range(n.bit_length() - 1):
        pairs = merged(pairs, swap(pairs, axis, n, 1 << b))
    return pairs[0] + jnp.log(pairs[1]) * LOG2E


def text_block(text, t, halves, row_lse, col_lse, place_ref, scale_ref, coef_ref, grad_ref, out_ref, acc):
    coef = coef_ref[0, 0]
    r_place, c_place = place_ref[0, 0], place_ref[0, 1]
    half, width = halves[0].shape
    n_col, n_row = row_lse.shape[0], col_lse.shape[0]
    size = text.shape[0]
    block = size
    col_lse_down = jnp.broadcast_to(col_lse[pl.ds(r_place ^ t, 1), :], (LANES, size)).T
    text_id = c_place * n_row + (r_place ^ t)
    step = acc.shape[0]
    lane_ids = lax.broadcasted_iota(jnp.int32, (step, LANES), 1)
    row_ids = lax.broadcasted_iota(jnp.int32, (step, LANES), 0)

    for which, images in enumerate(halves):

        def one(j, acc):
            inner = nt_dot(text[...], images[pl.ds(pl.multiple_of(j * block, block), block), :])
            at = pl.multiple_of(j * block + which * half, block)
            column = c_place ^ (2 * j + which)
            same = jnp.where(r_place * n_col + column == text_id, 1.0, 0.0)
            lse = row_lse[pl.ds(column, 1), :]
            for r in range(0, size, step):
                for lane in range(0, block, LANES):
                    v = inner[r : r + step, lane : lane + LANES]
                    x = v * coef
                    e = jnp.exp2(x - lse[:, lane : lane + LANES]) + jnp.exp2(
                        x - col_lse_down[r : r + step, :]
                    )
                    g = 0.5 * e
                    if lane <= r < lane + LANES:
                        g = g - jnp.where(row_ids + (r - lane) == lane_ids, same, 0.0)
                    acc = acc + g * v
                    grad_ref[r : r + step, pl.ds(at + lane, LANES)] = g.astype(jnp.bfloat16)
            return acc

        acc = lax.fori_loop(0, half // block, one, acc, unroll=2)
    out_ref[...] = scale_ref[0, 0] * (
        jnp.dot(grad_ref[:, :half], halves[0][...], preferred_element_type=jnp.float32)
        + jnp.dot(grad_ref[:, half:], halves[1][...], preferred_element_type=jnp.float32)
    )
    return acc


def image_block(grads, texts, at, block, scale):
    total = None
    for grad, text in zip(grads, texts):
        part = lax.dot_general(
            grad[:, pl.ds(at, block)],
            text[...],
            (((0,), (0,)), ((), ())),
            preferred_element_type=jnp.float32,
        )
        total = part if total is None else total + part
    return scale * total


def text_kernel(order, n_done, block, scale_ref, coef_ref, place_ref, *refs):
    even, odd, row_lse, col_lse = refs[:4]
    n = len(order)
    texts = refs[4 : 4 + n]
    done_grads, done_texts = refs[4 + n : 4 + n + n_done], refs[4 + n + n_done : 4 + n + 2 * n_done]
    rest = refs[4 + n + 2 * n_done :]
    grads, outs, sum_ref = rest[:n], rest[n : 2 * n], rest[2 * n]
    acc = jnp.zeros((32, LANES), jnp.float32)
    for i, t in enumerate(order):
        acc = text_block(
            texts[i], t, (even, odd), row_lse, col_lse, place_ref, scale_ref, coef_ref, grads[i], outs[i], acc
        )
    sum_ref[...] = functools.reduce(jnp.add, [acc[i : i + 8] for i in range(0, 32, 8)])
    if n_done:
        far_ref = rest[2 * n + 1]
        half = even.shape[0]

        def one(j, carry):
            at = pl.multiple_of(j * block + half, block)
            far_ref[j] = image_block(
                [*done_grads, *grads], [*done_texts, *texts], at, block, scale_ref[0, 0]
            )
            return carry

        lax.fori_loop(0, half // block, one, 0)


def text_grads(scale, coef, place, even, odd, row_lse, col_lse, texts, order, done):
    half, width = even.shape
    block = texts[0].shape[0]
    n = len(order)
    vmem = pl.BlockSpec(memory_space=VMEM)
    smem = pl.BlockSpec(memory_space=SMEM)
    out_shape = (
        [jax.ShapeDtypeStruct((block, 2 * half), jnp.bfloat16)] * n
        + [jax.ShapeDtypeStruct((block, width), jnp.float32)] * n
        + [jax.ShapeDtypeStruct((8, LANES), jnp.float32)]
    )
    if done:
        out_shape.append(jax.ShapeDtypeStruct((half // block, block, width), jnp.float32))
    operands = [even, odd, row_lse, col_lse, *[texts[t] for t in order]]
    operands += [done[t] for t in done] + [texts[t] for t in done]
    outs = pl.pallas_call(
        functools.partial(text_kernel, tuple(order), len(done), block),
        out_shape=tuple(out_shape),
        in_specs=[smem] * 3 + [vmem] * len(operands),
        out_specs=(vmem,) * len(out_shape),
        compiler_params=pltpu.CompilerParams(vmem_limit_bytes=12 * 2**20),
        cost_estimate=pl.CostEstimate(
            flops=FLOPS * 4 * n * block * 2 * half * width, bytes_accessed=0, transcendentals=0
        ),
        name=f"text_grads_{n}",
    )(scale, coef, place, *operands)
    grads = {t: outs[i] for i, t in enumerate(order)}
    parts = {t: outs[n + i] for i, t in enumerate(order)}
    return grads, parts, outs[2 * n], outs[-1] if done else None


def image_kernel(n_text, block, scale_ref, *refs):
    grads, texts, out_ref = refs[:n_text], refs[n_text : 2 * n_text], refs[-1]

    def one(j, carry):
        out_ref[j] = image_block(
            grads, texts, pl.multiple_of(j * block, block), block, scale_ref[0, 0]
        )
        return carry

    lax.fori_loop(0, out_ref.shape[0], one, 0)


def image_grads(scale, grads, texts, after):
    n_text = len(grads)
    rows = grads[0].shape[1]
    block, width = texts[0].shape
    n = rows // block // 2
    vmem = pl.BlockSpec(memory_space=VMEM)
    return pl.pallas_call(
        functools.partial(image_kernel, n_text, block),
        out_shape=jax.ShapeDtypeStruct((n, block, width), jnp.float32),
        in_specs=[pl.BlockSpec(memory_space=SMEM)]
        + [vmem] * (2 * n_text)
        + [pl.BlockSpec(memory_space=pl.ANY)] * len(after),
        out_specs=vmem,
        compiler_params=pltpu.CompilerParams(vmem_limit_bytes=12 * 2**20),
        cost_estimate=pl.CostEstimate(
            flops=FLOPS * 2 * n * block * n_text * block * width, bytes_accessed=0, transcendentals=0
        ),
        name="image_grads",
    )(scale, *grads, *texts, *after)


def halve(blocks, axis, n, bits):
    for bit in bits:
        far = sorted(q for q in blocks if q & bit)
        sent = swap(jnp.stack([blocks[q] for q in far]), axis, n, bit)
        blocks = {q ^ bit: blocks[q ^ bit] + sent[i] for i, q in enumerate(far)}
    return blocks[0]


def scatter_images(near, far, axis, n):
    sent = swap(far, axis, n, 1)
    total = near[0] + sent[0]
    for j in range(1, n // 2):
        total = total + swap(near[j] + sent[j], axis, n, 2 * j)
    return total


def on_device(n_row, n_col, image_embeds, text_embeds, logit_scale):
    block = image_embeds.shape[0]
    r, c = lax.axis_index("row"), lax.axis_index("col")
    place = jnp.stack([r, c]).reshape(1, 2)
    scale = logit_scale.reshape(1, 1)
    coef = scale * LOG2E
    image_half, text_half = cast_both(image_embeds, text_embeds)
    even, odd, texts = gather_both(image_half, text_half, n_col, n_row)
    row_pairs, col_pairs = stats(coef, place, even, odd, texts, (), 0, n_row)
    row_lse = exchanged_lse(row_pairs, "col", n_col)
    col_lse = exchanged_lse(col_pairs, "row", n_row)

    held = (scale, coef, place, even, odd, row_lse, col_lse, texts)
    last = n_row - 1
    grads, parts, sum_first, _ = text_grads(*held, [last], {})
    received = swap(parts[last], "row", n_row, 1)
    more, more_parts, sum_rest, far = text_grads(*held, list(range(last))[::-1], grads)
    grads |= more
    parts |= more_parts
    sums = {last ^ 1: parts[last ^ 1] + received}
    near = image_grads(
        scale, [grads[t] for t in range(n_row)], texts, [sums[last ^ 1]]
    )
    for q in range(1, last, 2):
        sums[q ^ 1] = parts[q ^ 1] + swap(parts[q], "row", n_row, 1)
    grad_text = halve(sums, "row", n_row, [1 << b for b in range(1, n_row.bit_length() - 1)])
    grad_image = scatter_images(near, far, "col", n_col)
    total = lax.all_gather(sum_first + sum_rest, ("row", "col"))
    return grad_image, grad_text, jnp.sum(total)


def solution(mesh):
    images = P(("row", "col"), None)
    texts = P(("col", "row"), None)
    return jax.shard_map(
        functools.partial(on_device, mesh.shape["row"], mesh.shape["col"]),
        mesh=mesh,
        in_specs=(images, texts, P()),
        out_specs=(images, texts, P()),
        check_vma=False,
    )
```

time: 253 us -> 142 us (0.56)
  waiting for transfers between devices: 108 us -> 30.1 us
  blocking collectives: 89 us -> 53.5 us
  Pallas kernels: 0 us -> 25.2 us
  starting transfers between devices: 0.16 us -> 22 us
  matrix products: 17.7 us -> 0 us
  other arithmetic: 21.5 us -> 8.17 us
  between operations: 14.5 us -> 1.52 us
    psum x3 -> x0, blocking collectives: 64 us -> none  [the longest x1 43.4 us: on_device(): grad_scale = lax.psum(partial_scale, ('row', 'col'))]
    all_gather x2 -> x0, waiting for transfers between devices: 59.1 us -> none  [the longest x1 29.9 us: on_device(): images = lax.all_gather(image_half, 'col', axis=0, tiled=True)]
    all_gather x0 -> x1, blocking collectives: none -> 53.5 us  [on_device(): total = lax.all_gather(sum_first + sum_rest, ('row', 'col'))]
    reduce_scatter x2 -> x0, waiting for transfers between devices: 48.6 us -> none  [the longest x1 48.6 us: on_device(): lax.psum_scatter(logit_scale * jnp.dot(picked, text_cols, preferred_eleme...]
    ppermute x0 -> x21, waiting for transfers between devices: none -> 30.1 us  [the longest x17 17.7 us: swap(): return lax.ppermute(x, axis, [(i, i ^ q) for i in range(n)])]
    pallas_call x0 -> x5, Pallas kernels: none -> 25.2 us  [the longest x2 14.1 us: text_grads(): pl.pallas_call(functools.partial(text_kernel, tuple(order), len(done), bl...]
    pmax x2 -> x0, blocking collectives: 25 us -> none  [the longest x1 13.3 us: on_device(): row_max = lax.pmax(jnp.max(logits, axis=1), 'col')]
    ppermute x0 -> x21, starting transfers between devices: none -> 22 us  [the longest x17 18.1 us: swap(): return lax.ppermute(x, axis, [(i, i ^ q) for i in range(n)])]
  transfers between devices with their start and end apart: 4 -> 21, of which waited for: 3 -> 9; matrix products, arithmetic and copies ran while one was open for 3% -> 5% of each run, Pallas kernels for 0% -> 9%
where the time goes in v2:
time: 142 us
  blocking collectives  53.5 us (38%)
  waiting for transfers between devices  30.1 us (21%)
  Pallas kernels  25.2 us (18%)
  starting transfers between devices  22 us (15%)
  other arithmetic  8.17 us (6%)
  between operations  1.52 us (1%)
    all_gather x1, blocking collectives, on_device(): total = lax.all_gather(sum_first + sum_rest, ('row', 'col'))  53.5 us
    ppermute x17, starting transfers between devices, swap(): return lax.ppermute(x, axis, [(i, i ^ q) for i in range(n)])  18.1 us
    ppermute x17, waiting for transfers between devices, swap(): return lax.ppermute(x, axis, [(i, i ^ q) for i in range(n)])  17.7 us
    pallas_call x2, Pallas kernels, text_grads(): pl.pallas_call(functools.partial(text_kernel, tuple(order), len(done), bl...  14.1 us
    ppermute x1, waiting for transfers between devices, gather_both(): end_three = lax.ppermute(mid_two, 'row', outward)  10.2 us
    pallas_call x1, Pallas kernels, stats(): pl.pallas_call(functools.partial(stats_kernel, len(texts), first, block),...  7.15 us
    add x2, other arithmetic, scatter_images(): total = total + swap(near[j] + sent[j], axis, n, 2 * j)  4.06 us
  transfers between devices with their start and end apart: 21, of which 9 were waited for; matrix products, arithmetic and copies ran while one was open for 5% of the time, Pallas kernels for 9%

profile of v2, /device:TPU:0, one launch (start us, length us, event | category | flops | bytes accessed | tf_op | source)
XLA Modules:
  0.0 141.9 jit_solution(3806908225379474053)
XLA Ops:
  0.6 2.0 %cast_both.1 = (bf16[256,512]{1,0:T(8,128)(2,1)}, bf16[256,512]{1,0:T(8,128)(2,1)}) custom-call(f32[256,512]{1,0:T(8,128)} %a_ref.1, f32[256,512]{1,0:T(8,128)} %b_ref.1), custom_call_target="tpu_custom_call" | custom-call | tf_op jit(solution)/shard_map/cast_both/pallas_call | solution.py:57
  2.6 2.9 %collective-permute-start.1 = (bf16[256,512]{1,0:T(8,128)(2,1)}, bf16[256,512]{1,0:T(8,128)(2,1)S(1)}, u32[]{:S(2)}, u32[]{:S(2)}) collective-permute-start(bf16[256,512]{1,0:T(8,128)(2,1)} %get-tuple-element.25), channel_id=1, source_target_pairs={{0,2},{1,3},{2,0},{3,1},{4,6},{5,7},{6,4},{7,5},{8,10},{9,11},{10,... | collective-permute-start | bytes 786440 | tf_op jit(solution)/shard_map/ppermute | solution.py:20
  5.6 1.5 %collective-permute-start = (bf16[256,512]{1,0:T(8,128)(2,1)}, bf16[256,512]{1,0:T(8,128)(2,1)S(1)}, u32[]{:S(2)}, u32[]{:S(2)}) collective-permute-start(bf16[256,512]{1,0:T(8,128)(2,1)} %get-tuple-element.25), channel_id=1, source_target_pairs={{0,4},{1,5},{2,6},{3,7},{4,0},{5,1},{6,2},{7,3},{8,12},{9,13},{10,... | collective-permute-start | bytes 786440 | tf_op jit(solution)/shard_map/ppermute | solution.py:20
  7.8 4.4 %collective-permute-start.2 = (bf16[256,512]{1,0:T(8,128)(2,1)}, bf16[256,512]{1,0:T(8,128)(2,1)S(1)}, u32[]{:S(2)}, u32[]{:S(2)}) collective-permute-start(bf16[256,512]{1,0:T(8,128)(2,1)} %get-tuple-element.26.refs_2_.refs_6_.refs_4_), channel_id=1, source_target_pairs={{0,8},{8,0},{16,24},{24,16},{1,9},{9,1},{17,25},{25,17},{2,10},{10... | collective-permute-start | bytes 786440 | tf_op jit(solution)/shard_map/ppermute | solution.py:20
  12.2 1.3 collective-permute-done
  13.6 4.3 %collective-permute-done.2.refs_3_.refs_5_ = bf16[256,512]{1,0:T(8,128)(2,1)S(1)} collective-permute-done((bf16[256,512]{1,0:T(8,128)(2,1)}, bf16[256,512]{1,0:T(8,128)(2,1)S(1)}, u32[]{:S(2)}, u32[]{:S(2)}) %collective-permute-start.2) | collective-permute-done | bytes 262176 | tf_op jit(solution)/shard_map/ppermute | solution.py:20
  18.4 1.3 collective-permute-start.6
  19.7 0.7 collective-permute-start.5
  20.4 1.0 constant_dynamic-update-slice_fusion.3
  21.4 3.0 %collective-permute-done.4 = bf16[256,512]{1,0:T(8,128)(2,1)S(1)} collective-permute-done((bf16[256,512]{1,0:T(8,128)(2,1)S(1)}, bf16[256,512]{1,0:T(8,128)(2,1)S(1)}, u32[]{:S(2)}, u32[]{:S(2)}) %collective-permute-start.4) | collective-permute-done | bytes 262176 | tf_op jit(solution)/shard_map/ppermute | solution.py:20
  24.5 2.2 %collective-permute-done.6 = bf16[256,512]{1,0:T(8,128)(2,1)S(1)} collective-permute-done((bf16[256,512]{1,0:T(8,128)(2,1)S(1)}, bf16[256,512]{1,0:T(8,128)(2,1)S(1)}, u32[]{:S(2)}, u32[]{:S(2)}) %collective-permute-start.6) | collective-permute-done | bytes 262176 | tf_op jit(solution)/shard_map/ppermute | solution.py:35
  26.8 1.3 collective-permute-start.8
  28.9 10.2 %collective-permute-done.8 = bf16[256,512]{1,0:T(8,128)(2,1)} collective-permute-done((bf16[256,512]{1,0:T(8,128)(2,1)S(1)}, bf16[256,512]{1,0:T(8,128)(2,1)}, u32[]{:S(2)}, u32[]{:S(2)}) %collective-permute-start.8) | collective-permute-done | bytes 262176 | tf_op jit(solution)/shard_map/ppermute | solution.py:39
  39.1 1.0 add.83.refs_5_.refs_4_.refs_8_.refs_7_
  40.1 7.2 %stats_0.1 = (f32[2,8,256]{2,1,0:T(8,128)S(1)}, f32[2,4,256]{2,1,0:T(4,128)S(1)}) custom-call(f32[1,1]{1,0:T(1,128)S(6)} %mul.65.coef_ref, s32[1,2]{1,0:T(1,128)S(1)} %add_bitcast_fusion.place_ref, bf16[1024,512]{1,0:T(8,128)(2,1)S(1)} %constant_dynamic-update-slice_fusion.refs_0_, bf16[1024,512]{1,0:T(8,128)(2,1)S(1)} %collective-permute-done.7.refs_1_, ...), custom_call_target="tpu_custom_call" | custom-call | flops 2147483648 | bytes 3145728 | tf_op jit(solution)/shard_map/stats_0/pallas_call | solution.py:162
  47.4 3.6 %collective-permute-done.12 = f32[2,4,256]{2,1,0:T(4,128)S(1)} collective-permute-done((f32[2,4,256]{2,1,0:T(4,128)S(1)}, f32[2,4,256]{2,1,0:T(4,128)S(1)}, u32[]{:S(2)}, u32[]{:S(2)}) %collective-permute-start.12) | collective-permute-done | bytes 8224 | tf_op jit(solution)/shard_map/ppermute | solution.py:20
  51.1 1.6 %collective-permute-start.10 = (f32[2,8,256]{2,1,0:T(8,128)S(1)}, f32[2,8,256]{2,1,0:T(8,128)S(1)}, u32[]{:S(2)}, u32[]{:S(2)}) collective-permute-start(f32[2,8,256]{2,1,0:T(8,128)S(1)} %pad_maximum_fusion), channel_id=1, source_target_pairs={{0,2},{1,3},{2,0},{3,1},{4,6},{5,7},{6,4},{7,5},{8,10},{9,11},{10,... | collective-permute-start | bytes 49160 | tf_op jit(solution)/shard_map/ppermute | solution.py:20
  52.6 2.2 %collective-permute-done.10 = f32[2,8,256]{2,1,0:T(8,128)S(1)} collective-permute-done((f32[2,8,256]{2,1,0:T(8,128)S(1)}, f32[2,8,256]{2,1,0:T(8,128)S(1)}, u32[]{:S(2)}, u32[]{:S(2)}) %collective-permute-start.10) | collective-permute-done | bytes 16416 | tf_op jit(solution)/shard_map/ppermute | solution.py:20
  55.5 1.7 %collective-permute-done.13 = f32[2,4,256]{2,1,0:T(4,128)S(1)} collective-permute-done((f32[2,4,256]{2,1,0:T(4,128)S(1)}, f32[2,4,256]{2,1,0:T(4,128)S(1)}, u32[]{:S(2)}, u32[]{:S(2)}) %collective-permute-start.13) | collective-permute-done | bytes 8224 | tf_op jit(solution)/shard_map/ppermute | solution.py:20
  57.2 1.5 %collective-permute-done.11 = f32[2,8,256]{2,1,0:T(8,128)S(1)} collective-permute-done((f32[2,8,256]{2,1,0:T(8,128)S(1)}, f32[2,8,256]{2,1,0:T(8,128)S(1)}, u32[]{:S(2)}, u32[]{:S(2)}) %collective-permute-start.11) | collective-permute-done | bytes 16416 | tf_op jit(solution)/shard_map/ppermute | solution.py:20
  58.7 3.3 %text_grads_1.1 = (bf16[256,2048]{1,0:T(8,128)(2,1)S(1)}, f32[256,512]{1,0:T(8,128)S(1)}, f32[8,128]{1,0:T(8,128)S(1)}) custom-call(f32[1,1]{1,0:T(1,128)} %bitcast.190.scale_ref, f32[1,1]{1,0:T(1,128)S(6)} %mul.65.coef_ref, s32[1,2]{1,0:T(1,128)S(1)} %add_bitcast_fusion.place_ref, bf16[1024,512]{1,0:T(8,128)(2,1)S(1)} %constant_dynamic-update-slice_fusion.refs_0_, ...), custom_call_target="tpu_custom_call" | custom-call | flops 21474836480 | tf_op jit(solution)/shard_map/text_grads_1/pallas_call | solution.py:295
  62.1 10.8 %text_grads_3.1 = (bf16[256,2048]{1,0:T(8,128)(2,1)S(1)}, bf16[256,2048]{1,0:T(8,128)(2,1)S(1)}, bf16[256,2048]{1,0:T(8,128)(2,1)S(1)}, f32[256,512]{1,0:T(8,128...) custom-call(f32[1,1]{1,0:T(1,128)} %bitcast.191.scale_ref, ...), custom_call_target="tpu_custom_call" | custom-call | flops 64424509440 | tf_op jit(solution)/shard_map/text_grads_3/pallas_call | solution.py:295
  72.9 2.0 %collective-permute-start.19 = (f32[256,512]{1,0:T(8,128)}, f32[256,512]{1,0:T(8,128)}, u32[]{:S(2)}, u32[]{:S(2)}) collective-permute-start(f32[256,512]{1,0:T(8,128)} %get-tuple-element.44), channel_id=1, source_target_pairs={{0,8},{8,0},{16,24},{24,16},{1,9},{9,1},{17,25},{25,17},{2,10},{10... | collective-permute-start | bytes 1572872 | tf_op jit(solution)/shard_map/ppermute | solution.py:20
  75.0 0.8 collective-permute-start.20
  75.8 2.0 %image_grads.1 = f32[4,256,512]{2,1,0:T(8,128)S(1)} custom-call(f32[1,1]{1,0:T(1,128)} %bitcast.192.scale_ref, bf16[256,2048]{1,0:T(8,128)(2,1)S(1)} %get-tuple-element.37.refs_0_, bf16[256,2048]{1,0:T(8,128)(2,1)S(1)} %get-tuple-element.38.refs_1_, bf16[256,2048]{1,0:T(8,128)(2,1)S(1)} %get-tuple-element.39.refs_2_, ...), custom_call_target="tpu_custom_call" | custom-call | flops 21474836480 | tf_op jit(solution)/shard_map/image_grads/pallas_call | solution.py:329
  77.7 1.5 %fusion.2 = (f32[256,512]{1,0:T(8,128)}, f32[256,512]{1,0:T(8,128)}, f32[256,512]{1,0:T(8,128)}) fusion(f32[4,256,512]{2,1,0:T(8,128)S(1)} %collective-permute-done.15, f32[4,256,512]{2,1,0:T(8,128)S(1)} %image_grads.1), kind=kLoop, calls=%fused_computation.5 | loop fusion | flops 393216 | bytes 4718592 | tf_op jit(solution)/shard_map/add | solution.py:356
  79.5 0.9 collective-permute-start.16
  80.4 1.1 collective-permute-start.18
  81.5 1.5 %collective-permute-start.17 = (f32[256,512]{1,0:T(8,128)}, f32[256,512]{1,0:T(8,128)}, u32[]{:S(2)}, u32[]{:S(2)}) collective-permute-start(f32[256,512]{1,0:T(8,128)} %get-tuple-element.53), channel_id=1, source_target_pairs={{0,4},{1,5},{2,6},{3,7},{4,0},{5,1},{6,2},{7,3},{8,12},{9,13},{10,... | collective-permute-start | bytes 1572872 | tf_op jit(solution)/shard_map/ppermute | solution.py:20
  83.0 53.5 %all-gather = f32[256,128]{1,0:T(8,128)S(1)} all-gather(f32[8,128]{1,0:T(8,128)S(1)} %add.108), channel_id=2, replica_groups=mesh['row'=4,'col'=8] {'row','col'}, dimensions={0}, use_global_device_ids=true | all-gather | bytes 135168 | tf_op jit(solution)/shard_map/all_gather | solution.py:387
  137.2 2.1 %bitcast_add_fusion = f32[256,512]{1,0:T(8,128)} fusion(f32[1,256,512]{2,1,0:T(8,128)} %collective-permute-done.20, f32[256,512]{1,0:T(8,128)S(1)} %get-tuple-element.43, f32[256,512]{1,0:T(8,128)} %collective-permute-done.19), kind=kLoop, calls=%fused_computation.11 | loop fusion | flops 262144 | bytes 2097152 | tf_op jit(solution)/shard_map/add | solution.py:348
  139.3 2.6 %fusion.6 = f32[256,512]{1,0:T(8,128)} fusion(f32[256,512]{1,0:T(8,128)} %collective-permute-done.18, f32[256,512]{1,0:T(8,128)} %collective-permute-done.17, f32[256,512]{1,0:T(8,128)} %collective-permute-done.16, f32[4,256,512]{2,1,0:T(8,128)} %copy-done.3, f32[4,256,512]{2,1,0:T(8,128)S(1)} %image_grads.1), kind=kLoop, calls=%fused_computation.10 | loop fusion | flops 524288 | bytes 3145728 | tf_op jit(solution)/shard_map/add | solution.py:356
  (45 shorter events, 3.5 us)
Async XLA Ops:
  2.6 37.5 %copy-start = (bf16[256,512]{1,0:T(8,128)(2,1)S(1)}, bf16[256,512]{1,0:T(8,128)(2,1)}, u32[]{:S(2)}) copy-start(bf16[256,512]{1,0:T(8,128)(2,1)} %get-tuple-element.26.refs_2_.refs_6_.refs_4_) | copy-start | bytes 786436
  2.6 9.6 %collective-permute-start.1 = (bf16[256,512]{1,0:T(8,128)(2,1)}, bf16[256,512]{1,0:T(8,128)(2,1)S(1)}, u32[]{:S(2)}, u32[]{:S(2)}) collective-permute-start(bf16[256,512]{1,0:T(8,128)(2,1)} %get-tuple-element.25), channel_id=1, source_target_pairs={{0,2},{1,3},{2,0},{3,1},{4,6},{5,7},{6,4},{7,5},{8,10},{9,11},{10,... | collective-permute-start | bytes 786440 | tf_op jit(solution)/shard_map/ppermute | solution.py:20
  5.6 8.0 %collective-permute-start = (bf16[256,512]{1,0:T(8,128)(2,1)}, bf16[256,512]{1,0:T(8,128)(2,1)S(1)}, u32[]{:S(2)}, u32[]{:S(2)}) collective-permute-start(bf16[256,512]{1,0:T(8,128)(2,1)} %get-tuple-element.25), channel_id=1, source_target_pairs={{0,4},{1,5},{2,6},{3,7},{4,0},{5,1},{6,2},{7,3},{8,12},{9,13},{10,... | collective-permute-start | bytes 786440 | tf_op jit(solution)/shard_map/ppermute | solution.py:20
  7.1 6.5 %collective-permute-start.3 = (bf16[256,512]{1,0:T(8,128)(2,1)}, bf16[256,512]{1,0:T(8,128)(2,1)S(1)}, u32[]{:S(2)}, u32[]{:S(2)}) collective-permute-start(bf16[256,512]{1,0:T(8,128)(2,1)} %get-tuple-element.26.refs_2_.refs_6_.refs_4_), channel_id=1, source_target_pairs={{8,16},{16,8},{9,17},{17,9},{10,18},{18,10},{11,19},{19,11},{12,20... | collective-permute-start | bytes 786440 | tf_op jit(solution)/shard_map/ppermute | solution.py:31
  7.8 10.1 %collective-permute-start.2 = (bf16[256,512]{1,0:T(8,128)(2,1)}, bf16[256,512]{1,0:T(8,128)(2,1)S(1)}, u32[]{:S(2)}, u32[]{:S(2)}) collective-permute-start(bf16[256,512]{1,0:T(8,128)(2,1)} %get-tuple-element.26.refs_2_.refs_6_.refs_4_), channel_id=1, source_target_pairs={{0,8},{8,0},{16,24},{24,16},{1,9},{9,1},{17,25},{25,17},{2,10},{10... | collective-permute-start | bytes 786440 | tf_op jit(solution)/shard_map/ppermute | solution.py:20
  17.9 29.4 %copy-start.1 = (bf16[256,512]{1,0:T(8,128)(2,1)}, bf16[256,512]{1,0:T(8,128)(2,1)S(1)}, u32[]{:S(2)}) copy-start(bf16[256,512]{1,0:T(8,128)(2,1)S(1)} %collective-permute-done.2.refs_3_.refs_5_) | copy-start | bytes 786436
  17.9 6.6 %collective-permute-start.4 = (bf16[256,512]{1,0:T(8,128)(2,1)S(1)}, bf16[256,512]{1,0:T(8,128)(2,1)S(1)}, u32[]{:S(2)}, u32[]{:S(2)}) collective-permute-start(bf16[256,512]{1,0:T(8,128)(2,1)S(1)} %collective-permute-done), channel_id=1, source_target_pairs={{0,2},{1,3},{2,0},{3,1},{4,6},{5,7},{6,4},{7,5},{8,10},{9,11},{10,... | collective-permute-start | bytes 786440 | tf_op jit(solution)/shard_map/ppermute | solution.py:20
  18.4 8.3 %collective-permute-start.6 = (bf16[256,512]{1,0:T(8,128)(2,1)S(1)}, bf16[256,512]{1,0:T(8,128)(2,1)S(1)}, u32[]{:S(2)}, u32[]{:S(2)}) collective-permute-start(bf16[256,512]{1,0:T(8,128)(2,1)S(1)} %collective-permute-done.3), channel_id=1, source_target_pairs={{8,0},{16,24},{9,1},{17,25},{10,2},{18,26},{11,3},{19,27},{12,4},{... | collective-permute-start | bytes 786440 | tf_op jit(solution)/shard_map/ppermute | solution.py:35
  19.7 7.0 %collective-permute-start.5 = (bf16[256,512]{1,0:T(8,128)(2,1)S(1)}, bf16[256,512]{1,0:T(8,128)(2,1)S(1)}, u32[]{:S(2)}, u32[]{:S(2)}) collective-permute-start(bf16[256,512]{1,0:T(8,128)(2,1)S(1)} %collective-permute-done.2.refs_3_.refs_5_), channel_id=1, source_target_pairs={{8,16},{16,8},{9,17},{17,9},{10,18},{18,10},{11,19},{19,11},{12,20... | collective-permute-start | bytes 786440 | tf_op jit(solution)/shard_map/ppermute | solution.py:34
  26.7 13.4 %collective-permute-start.7 = (bf16[1024,512]{1,0:T(8,128)(2,1)S(1)}, bf16[1024,512]{1,0:T(8,128)(2,1)S(1)}, u32[]{:S(2)}, u32[]{:S(2)}) collective-permute-start(bf16[1024,512]{1,0:T(8,128)(2,1)S(1)} %constant_dynamic-update-slice_fusion.refs_0_), channel_id=1, source_target_pairs={{0,1},{1,0},{2,3},{3,2},{4,5},{5,4},{6,7},{7,6},{8,9},{9,8},{10,11... | collective-permute-start | bytes 3145736 | tf_op jit(solution)/shard_map/ppermute | solution.py:20
  26.8 12.3 %collective-permute-start.8 = (bf16[256,512]{1,0:T(8,128)(2,1)S(1)}, bf16[256,512]{1,0:T(8,128)(2,1)}, u32[]{:S(2)}, u32[]{:S(2)}) collective-permute-start(bf16[256,512]{1,0:T(8,128)(2,1)S(1)} %collective-permute-done.5), channel_id=1, source_target_pairs={{8,0},{16,24},{9,1},{17,25},{10,2},{18,26},{11,3},{19,27},{12,4},{... | collective-permute-start | bytes 786440 | tf_op jit(solution)/shard_map/ppermute | solution.py:39
  47.3 3.7 %collective-permute-start.12 = (f32[2,4,256]{2,1,0:T(4,128)S(1)}, f32[2,4,256]{2,1,0:T(4,128)S(1)}, u32[]{:S(2)}, u32[]{:S(2)}) collective-permute-start(f32[2,4,256]{2,1,0:T(4,128)S(1)} %get-tuple-element.35), channel_id=1, source_target_pairs={{0,8},{8,0},{16,24},{24,16},{1,9},{9,1},{17,25},{25,17},{2,10},{10... | collective-permute-start | bytes 24584 | tf_op jit(solution)/shard_map/ppermute | solution.py:20
  47.4 3.7 %collective-permute-start.9 = (f32[2,8,256]{2,1,0:T(8,128)S(1)}, f32[2,8,256]{2,1,0:T(8,128)S(1)}, u32[]{:S(2)}, u32[]{:S(2)}) collective-permute-start(f32[2,8,256]{2,1,0:T(8,128)S(1)} %get-tuple-element.34), channel_id=1, source_target_pairs={{0,1},{1,0},{2,3},{3,2},{4,5},{5,4},{6,7},{7,6},{8,9},{9,8},{10,11... | collective-permute-start | bytes 49160 | tf_op jit(solution)/shard_map/ppermute | solution.py:20
  51.1 3.8 %collective-permute-start.10 = (f32[2,8,256]{2,1,0:T(8,128)S(1)}, f32[2,8,256]{2,1,0:T(8,128)S(1)}, u32[]{:S(2)}, u32[]{:S(2)}) collective-permute-start(f32[2,8,256]{2,1,0:T(8,128)S(1)} %pad_maximum_fusion), channel_id=1, source_target_pairs={{0,2},{1,3},{2,0},{3,1},{4,6},{5,7},{6,4},{7,5},{8,10},{9,11},{10,... | collective-permute-start | bytes 49160 | tf_op jit(solution)/shard_map/ppermute | solution.py:20
  52.6 4.5 %collective-permute-start.13 = (f32[2,4,256]{2,1,0:T(4,128)S(1)}, f32[2,4,256]{2,1,0:T(4,128)S(1)}, u32[]{:S(2)}, u32[]{:S(2)}) collective-permute-start(f32[2,4,256]{2,1,0:T(4,128)S(1)} %pad_maximum_fusion.2), channel_id=1, source_target_pairs={{0,16},{8,24},{16,0},{24,8},{1,17},{9,25},{17,1},{25,9},{2,18},{10... | collective-permute-start | bytes 24584 | tf_op jit(solution)/shard_map/ppermute | solution.py:20
  54.9 3.8 %collective-permute-start.11 = (f32[2,8,256]{2,1,0:T(8,128)S(1)}, f32[2,8,256]{2,1,0:T(8,128)S(1)}, u32[]{:S(2)}, u32[]{:S(2)}) collective-permute-start(f32[2,8,256]{2,1,0:T(8,128)S(1)} %pad_maximum_fusion.1), channel_id=1, source_target_pairs={{0,4},{1,5},{2,6},{3,7},{4,0},{5,1},{6,2},{7,3},{8,12},{9,13},{10,... | collective-permute-start | bytes 49160 | tf_op jit(solution)/shard_map/ppermute | solution.py:20
  58.7 3.4 %copy-start.2 = (bf16[256,512]{1,0:T(8,128)(2,1)S(1)}, bf16[256,512]{1,0:T(8,128)(2,1)}, u32[]{:S(2)}) copy-start(bf16[256,512]{1,0:T(8,128)(2,1)} %copy-done.1) | copy-start | bytes 786436
  62.0 12.9 %collective-permute-start.14 = (f32[256,512]{1,0:T(8,128)S(1)}, f32[256,512]{1,0:T(8,128)S(1)}, u32[]{:S(2)}, u32[]{:S(2)}) collective-permute-start(f32[256,512]{1,0:T(8,128)S(1)} %get-tuple-element.41), channel_id=1, source_target_pairs={{0,8},{8,0},{16,24},{24,16},{1,9},{9,1},{17,25},{25,17},{2,10},{10... | collective-permute-start | bytes 1572872 | tf_op jit(solution)/shard_map/ppermute | solution.py:20
  72.9 4.8 %collective-permute-start.15 = (f32[4,256,512]{2,1,0:T(8,128)S(1)}, f32[4,256,512]{2,1,0:T(8,128)S(1)}, u32[]{:S(2)}, u32[]{:S(2)}) collective-permute-start(f32[4,256,512]{2,1,0:T(8,128)S(1)} %get-tuple-element.42), channel_id=1, source_target_pairs={{0,1},{1,0},{2,3},{3,2},{4,5},{5,4},{6,7},{7,6},{8,9},{9,8},{10,11... | collective-permute-start | bytes 6291464 | tf_op jit(solution)/shard_map/ppermute | solution.py:20
  72.9 64.2 %collective-permute-start.19 = (f32[256,512]{1,0:T(8,128)}, f32[256,512]{1,0:T(8,128)}, u32[]{:S(2)}, u32[]{:S(2)}) collective-permute-start(f32[256,512]{1,0:T(8,128)} %get-tuple-element.44), channel_id=1, source_target_pairs={{0,8},{8,0},{16,24},{24,16},{1,9},{9,1},{17,25},{25,17},{2,10},{10... | collective-permute-start | bytes 1572872 | tf_op jit(solution)/shard_map/ppermute | solution.py:20
  75.0 62.2 %collective-permute-start.20 = (f32[1,256,512]{2,1,0:T(8,128)S(1)}, f32[1,256,512]{2,1,0:T(8,128)}, u32[]{:S(2)}, u32[]{:S(2)}) collective-permute-start(f32[1,256,512]{2,1,0:T(8,128)S(1)} %bitcast.193), channel_id=1, source_target_pairs={{0,16},{8,24},{16,0},{24,8},{1,17},{9,25},{17,1},{25,9},{2,18},{10... | collective-permute-start | bytes 1572872 | tf_op jit(solution)/shard_map/ppermute | solution.py:20
  77.7 1.8 %copy-start.3 = (f32[4,256,512]{2,1,0:T(8,128)}, f32[4,256,512]{2,1,0:T(8,128)S(1)}, u32[]{:S(2)}) copy-start(f32[4,256,512]{2,1,0:T(8,128)S(1)} %collective-permute-done.15) | copy-start | bytes 6291460
  79.5 59.8 %collective-permute-start.16 = (f32[256,512]{1,0:T(8,128)}, f32[256,512]{1,0:T(8,128)}, u32[]{:S(2)}, u32[]{:S(2)}) collective-permute-start(f32[256,512]{1,0:T(8,128)} %get-tuple-element.51), channel_id=1, source_target_pairs={{0,2},{1,3},{2,0},{3,1},{4,6},{5,7},{6,4},{7,5},{8,10},{9,11},{10,... | collective-permute-start | bytes 1572872 | tf_op jit(solution)/shard_map/ppermute | solution.py:20
  80.4 58.9 %collective-permute-start.18 = (f32[256,512]{1,0:T(8,128)}, f32[256,512]{1,0:T(8,128)}, u32[]{:S(2)}, u32[]{:S(2)}) collective-permute-start(f32[256,512]{1,0:T(8,128)} %get-tuple-element.52), channel_id=1, source_target_pairs={{0,6},{1,7},{2,4},{3,5},{4,2},{5,3},{6,0},{7,1},{8,14},{9,15},{10,... | collective-permute-start | bytes 1572872 | tf_op jit(solution)/shard_map/ppermute | solution.py:20
  81.5 57.8 %collective-permute-start.17 = (f32[256,512]{1,0:T(8,128)}, f32[256,512]{1,0:T(8,128)}, u32[]{:S(2)}, u32[]{:S(2)}) collective-permute-start(f32[256,512]{1,0:T(8,128)} %get-tuple-element.53), channel_id=1, source_target_pairs={{0,4},{1,5},{2,6},{3,7},{4,0},{5,1},{6,2},{7,3},{8,12},{9,13},{10,... | collective-permute-start | bytes 1572872 | tf_op jit(solution)/shard_map/ppermute | solution.py:20

commit v3 on v2

v3 whole, which is shorter than its diff:
```python
import functools
import math

import jax
import jax.numpy as jnp
from jax import lax
from jax.experimental import pallas as pl
from jax.experimental.pallas import tpu as pltpu
from jax.sharding import PartitionSpec as P

LOG2E = 1.4426950408889634
LN2 = 0.6931471805599453
LANES = 128
VMEM = pltpu.VMEM
SMEM = pltpu.SMEM
FLOPS = 20


def swap(x, axis, n, q):
    return lax.ppermute(x, axis, [(i, i ^ q) for i in range(n)])


def gather_both(image, text, n_col, n_row):
    images = [swap(image, "col", n_col, q) for q in range(2, n_col, 2)]
    texts = [swap(text, "row", n_row, q) for q in range(1, n_row)]
    odd = [swap(image, "col", n_col, 1)]
    texts, images = lax.optimization_barrier((texts, images))
    odd += [swap(i, "col", n_col, 1) for i in images]
    return [image, *images], odd, [text, *texts]


def cast_kernel(a_ref, b_ref, a_out, b_out):
    a_out[...] = a_ref[...].astype(jnp.bfloat16)
    b_out[...] = b_ref[...].astype(jnp.bfloat16)


def cast_both(a, b):
    vmem = pl.BlockSpec(memory_space=VMEM)
    return pl.pallas_call(
        cast_kernel,
        out_shape=tuple(jax.ShapeDtypeStruct(x.shape, jnp.bfloat16) for x in (a, b)),
        in_specs=[vmem] * 2,
        out_specs=(vmem,) * 2,
        name="cast_both",
    )(a, b)


def nt_dot(a, b):
    return lax.dot_general(a, b, (((1,), (1,)), ((), ())), preferred_element_type=jnp.float32)


def stats_kernel(n_text, n_image, odd, block, coef_ref, place_ref, *refs):
    pieces, refs = refs[:n_image], refs[n_image:]
    texts = refs[:n_text]
    before = refs[n_text:-9]
    row_ref, col_ref, images, tile, row_max, col_max, col_sum, col_dot, row_diag = refs[-9:]
    coef = coef_ref[0, 0]
    r_place, c_place = place_ref[0, 0], place_ref[0, 1]
    cols, rows = tile.shape
    col_max[...] = jnp.full(col_max.shape, -jnp.inf, jnp.float32)
    row_diag[...] = jnp.zeros(row_diag.shape, jnp.float32)
    n_col, n_row = row_ref.shape[1], col_ref.shape[1]
    for j, piece in enumerate(pieces):
        images[j * block : (j + 1) * block, :] = piece[...]

    def products(j, carry):
        at = pl.multiple_of(j * block, block)
        image = images[pl.ds(at, block), :]
        image_id = r_place * n_col + (c_place ^ (2 * j + odd))
        top = None
        for t in range(n_text):
            part = pl.ds(t * block, block)
            x = nt_dot(texts[t][...], image) * coef
            tile[part, pl.ds(at, block)] = x
            top_t = jnp.max(x, axis=0, keepdims=True)
            top = top_t if top is None else jnp.maximum(top, top_t)
            held = col_max[part, :]
            for lane in range(0, block, LANES):
                held = jnp.maximum(held, x[:, lane : lane + LANES])
            col_max[part, :] = held
        row_max[0:1, pl.ds(at, block)] = top
        for t in range(n_text):

            @pl.when(image_id == c_place * n_row + (r_place ^ t))
            def _():
                x = tile[pl.ds(t * block, block), pl.ds(at, block)]
                down = lax.broadcasted_iota(jnp.int32, x.shape, 0)
                across = lax.broadcasted_iota(jnp.int32, x.shape, 1)
                row_diag[0:1, pl.ds(at, block)] = jnp.sum(
                    jnp.where(down == across, x, 0.0), axis=0, keepdims=True
                )

        return carry

    lax.fori_loop(0, rows // block, products, 0, unroll=2)

    col_max[...] = jnp.broadcast_to(
        jnp.max(col_max[...], axis=1, keepdims=True), col_max.shape
    )

    lanes = range(0, rows, LANES)

    def exponentials(i, acc):
        part = pl.ds(pl.multiple_of(i * 8, 8), 8)
        top = col_max[part, :]
        total = dot = None
        sums, dots = [], []
        for n, lane in enumerate(lanes):
            x = tile[part, lane : lane + LANES]
            e = jnp.exp2(x - row_max[0:1, lane : lane + LANES])
            sums.append(acc[0][n] + e)
            dots.append(acc[1][n] + e * x)
            e = jnp.exp2(x - top)
            total = e if total is None else total + e
            dot = e * x if dot is None else dot + e * x
        col_sum[part, :] = total
        col_dot[part, :] = dot
        return tuple(sums), tuple(dots)

    zeros = tuple(jnp.zeros((8, LANES), jnp.float32) for _ in lanes)
    acc = lax.fori_loop(0, cols // 8, exponentials, (zeros, zeros), unroll=4)

    row_ids = lax.broadcasted_iota(jnp.int32, (n_col, block), 0)
    if before:
        placed = [before[0][i] for i in range(4)]
    else:
        placed = [jnp.zeros((n_col, block), jnp.float32)] * 4
    for j in range(rows // block):
        at = j * block
        here = row_ids == (c_place ^ (2 * j + odd))
        new = [row_max[0:1, at : at + block]]
        for which in acc:
            new.append(
                jnp.concatenate(
                    [
                        jnp.sum(which[(at + lane) // LANES], axis=0, keepdims=True)
                        for lane in range(0, block, LANES)
                    ],
                    axis=1,
                )
            )
        new.append(row_diag[0:1, at : at + block])
        placed = [jnp.where(here, n, p) for n, p in zip(new, placed)]
    for i in range(4):
        row_ref[i] = placed[i]
    row_ids = lax.broadcasted_iota(jnp.int32, (n_row, block), 0)
    placed = [jnp.zeros((n_row, block), jnp.float32)] * 3
    for t in range(n_text):
        part = pl.ds(t * block, block)
        here = row_ids == (r_place ^ t)
        new = [col_max[part, :].T[0:1, :]]
        for which in (col_sum, col_dot):
            new.append(jnp.sum(which[part, :].T, axis=0, keepdims=True))
        placed = [jnp.where(here, n, p) for n, p in zip(new, placed)]
    if before:
        placed = merged(placed, [before[1][i] for i in range(3)])
    for i in range(3):
        col_ref[i] = placed[i]


def merged(a, b):
    top = jnp.maximum(a[0], b[0])
    wa, wb = jnp.exp2(a[0] - top), jnp.exp2(b[0] - top)
    out = [top] + [a[i] * wa + b[i] * wb for i in (1, 2)]
    return out + [a[i] + b[i] for i in range(3, len(a))]


def stats(coef, place, images, texts, before, n_col):
    block, width = texts[0].shape
    rows, cols = block * len(images), block * len(texts)
    vmem = pl.BlockSpec(memory_space=VMEM)
    smem = pl.BlockSpec(memory_space=SMEM)
    return pl.pallas_call(
        functools.partial(stats_kernel, len(texts), len(images), 1 if before else 0, block),
        out_shape=(
            jax.ShapeDtypeStruct((4, n_col, block), jnp.float32),
            jax.ShapeDtypeStruct((3, len(texts), block), jnp.float32),
            jax.ShapeDtypeStruct((rows, width), jnp.bfloat16),
        ),
        in_specs=[smem, smem] + [vmem] * (len(images) + len(texts) + len(before)),
        out_specs=(vmem,) * 3,
        scratch_shapes=[
            VMEM((cols, rows), jnp.float32),
            VMEM((8, rows), jnp.float32),
            VMEM((cols, LANES), jnp.float32),
            VMEM((cols, LANES), jnp.float32),
            VMEM((cols, LANES), jnp.float32),
            VMEM((8, rows), jnp.float32),
        ],
        compiler_params=pltpu.CompilerParams(vmem_limit_bytes=4 * rows * cols + 8 * 2**20),
        cost_estimate=pl.CostEstimate(
            flops=FLOPS * 2 * rows * cols * width, bytes_accessed=0, transcendentals=0
        ),
        name="stats_odd" if before else "stats_even",
    )(coef, place, *images, *texts, *before)


def exchanged(parts, axis, n):
    parts = [parts[i] for i in range(parts.shape[0])]
    for b in range(n.bit_length() - 1):
        parts = merged(parts, swap(jnp.stack(parts), axis, n, 1 << b))
    mean = 0.5 * parts[2] / parts[1]
    return parts[0] + jnp.log(parts[1]) * LOG2E, mean - parts[3] if len(parts) > 3 else mean


def put_extra(out, extra_ref):
    n, width = extra_ref.shape
    rows = min(n, 8)
    out[...] = jnp.zeros(out.shape, out.dtype)
    out[:rows, :width] = sum(extra_ref[i : i + rows, :] for i in range(0, n, rows))


def text_block(text, t, halves, row_lse, col_lse, place_ref, scale_ref, coef_ref, extra, grad_ref, out_ref):
    coef = coef_ref[0, 0]
    r_place, c_place = place_ref[0, 0], place_ref[0, 1]
    half, width = halves[0].shape
    n_col, n_row = row_lse.shape[0], col_lse.shape[0]
    size = text.shape[0]
    block = size
    col_lse_down = jnp.broadcast_to(col_lse[pl.ds(r_place ^ t, 1), :], (LANES, size)).T
    text_id = c_place * n_row + (r_place ^ t)
    step = 32
    lane_ids = lax.broadcasted_iota(jnp.int32, (step, LANES), 1)
    row_ids = lax.broadcasted_iota(jnp.int32, (step, LANES), 0)

    for which, images in enumerate(halves):

        def one(j, carry):
            inner = nt_dot(text[...], images[pl.ds(pl.multiple_of(j * block, block), block), :])
            at = pl.multiple_of(j * block + which * half, block)
            column = c_place ^ (2 * j + which)
            same = jnp.where(r_place * n_col + column == text_id, 1.0, 0.0)
            lse = row_lse[pl.ds(column, 1), :]
            for r in range(0, size, step):
                for lane in range(0, block, LANES):
                    x = inner[r : r + step, lane : lane + LANES] * coef
                    e = jnp.exp2(x - lse[:, lane : lane + LANES]) + jnp.exp2(
                        x - col_lse_down[r : r + step, :]
                    )
                    g = 0.5 * e
                    if lane <= r < lane + LANES:
                        g = g - jnp.where(row_ids + (r - lane) == lane_ids, same, 0.0)
                    grad_ref[r : r + step, pl.ds(at + lane, LANES)] = g.astype(jnp.bfloat16)
            return carry

        lax.fori_loop(0, half // block, one, 0, unroll=2)
    out_ref[:size, :] = scale_ref[0, 0] * (
        jnp.dot(grad_ref[:, :half], halves[0][...], preferred_element_type=jnp.float32)
        + jnp.dot(grad_ref[:, half:], halves[1][...], preferred_element_type=jnp.float32)
    )
    put_extra(out_ref.at[size:, :], extra)


def image_block(grads, texts, at, block, scale):
    total = None
    for grad, text in zip(grads, texts):
        part = lax.dot_general(
            grad[:, pl.ds(at, block)],
            text[...],
            (((0,), (0,)), ((), ())),
            preferred_element_type=jnp.float32,
        )
        total = part if total is None else total + part
    return scale * total


def text_kernel(order, n_done, block, scale_ref, coef_ref, place_ref, *refs):
    even, odd, row_lse, col_lse, row_extra, col_extra = refs[:6]
    n = len(order)
    texts, rest = refs[6 : 6 + n], refs[6 + n :]
    done_grads, done_texts, rest = rest[:n_done], rest[n_done : 2 * n_done], rest[2 * n_done :]
    grads, outs = rest[:n], rest[n : 2 * n]
    for i, t in enumerate(order):
        text_block(
            texts[i], t, (even, odd), row_lse, col_lse, place_ref, scale_ref, coef_ref, row_extra, grads[i], outs[i]
        )
    if n_done:
        far_ref = rest[2 * n]
        half = even.shape[0]

        def one(j, carry):
            far_ref[j, :block, :] = image_block(
                [*done_grads, *grads],
                [*done_texts, *texts],
                pl.multiple_of(j * block + half, block),
                block,
                scale_ref[0, 0],
            )
            put_extra(far_ref.at[j, block:, :], col_extra)
            return carry

        lax.fori_loop(0, half // block, one, 0)


def text_grads(scale, coef, place, even, odd, row_lse, col_lse, row_extra, col_extra, texts, order, done):
    half, width = even.shape
    block = texts[0].shape[0]
    n = len(order)
    vmem = pl.BlockSpec(memory_space=VMEM)
    smem = pl.BlockSpec(memory_space=SMEM)
    out_shape = (
        [jax.ShapeDtypeStruct((block, 2 * half), jnp.bfloat16)] * n
        + [jax.ShapeDtypeStruct((block + 8, width), jnp.float32)] * n
    )
    if done:
        out_shape.append(jax.ShapeDtypeStruct((half // block, block + 8, width), jnp.float32))
    operands = [even, odd, row_lse, col_lse, row_extra, col_extra, *[texts[t] for t in order]]
    operands += [done[t] for t in done] + [texts[t] for t in done]
    outs = pl.pallas_call(
        functools.partial(text_kernel, tuple(order), len(done), block),
        out_shape=tuple(out_shape),
        in_specs=[smem] * 3 + [vmem] * len(operands),
        out_specs=(vmem,) * len(out_shape),
        compiler_params=pltpu.CompilerParams(vmem_limit_bytes=12 * 2**20),
        cost_estimate=pl.CostEstimate(
            flops=FLOPS * 4 * n * block * 2 * half * width, bytes_accessed=0, transcendentals=0
        ),
        name=f"text_grads_{n}",
    )(scale, coef, place, *operands)
    grads = {t: outs[i] for i, t in enumerate(order)}
    parts = {t: outs[n + i] for i, t in enumerate(order)}
    return grads, parts, outs[-1]


def image_kernel(n_text, block, scale_ref, extra, *refs):
    grads, texts, out_ref = refs[:n_text], refs[n_text : 2 * n_text], refs[-1]

    def one(j, carry):
        put_extra(out_ref.at[j, block:, :], extra)
        out_ref[j, :block, :] = image_block(
            grads, texts, pl.multiple_of(j * block, block), block, scale_ref[0, 0]
        )
        return carry

    lax.fori_loop(0, out_ref.shape[0], one, 0)


def image_grads(scale, extra, grads, texts, after):
    n_text = len(grads)
    rows = grads[0].shape[1]
    block, width = texts[0].shape
    n = rows // block // 2
    vmem = pl.BlockSpec(memory_space=VMEM)
    return pl.pallas_call(
        functools.partial(image_kernel, n_text, block),
        out_shape=jax.ShapeDtypeStruct((n, block + 8, width), jnp.float32),
        in_specs=[pl.BlockSpec(memory_space=SMEM)]
        + [vmem] * (2 * n_text + 1)
        + [pl.BlockSpec(memory_space=pl.ANY)] * len(after),
        out_specs=vmem,
        compiler_params=pltpu.CompilerParams(vmem_limit_bytes=12 * 2**20),
        cost_estimate=pl.CostEstimate(
            flops=FLOPS * 2 * n * block * n_text * block * width, bytes_accessed=0, transcendentals=0
        ),
        name="image_grads",
    )(scale, extra, *grads, *texts, *after)


def halve(blocks, axis, n, bits):
    for bit in bits:
        far = sorted(q for q in blocks if q & bit)
        sent = swap(jnp.stack([blocks[q] for q in far]), axis, n, bit)
        blocks = {q ^ bit: blocks[q ^ bit] + sent[i] for i, q in enumerate(far)}
    return blocks[0]


def scatter_images(near, far, axis, n):
    sent = swap(far, axis, n, 1)
    total = near[0] + sent[0]
    for j in range(1, n // 2):
        total = total + swap(near[j] + sent[j], axis, n, 2 * j)
    return total


def on_device(n_row, n_col, image_embeds, text_embeds, logit_scale):
    block = image_embeds.shape[0]
    r, c = lax.axis_index("row"), lax.axis_index("col")
    place = jnp.stack([r, c]).reshape(1, 2)
    scale = logit_scale.reshape(1, 1)
    coef = scale * LOG2E
    image_half, text_half = cast_both(image_embeds, text_embeds)
    even, odd, texts = gather_both(image_half, text_half, n_col, n_row)
    row_parts, col_parts, even = stats(coef, place, even, texts, (), n_col)
    row_parts, col_parts, odd = stats(coef, place, odd, texts, (row_parts, col_parts), n_col)
    row_lse, row_extra = exchanged(row_parts, "col", n_col)
    col_lse, col_extra = exchanged(col_parts, "row", n_row)

    held = (scale, coef, place, even, odd, row_lse, col_lse, row_extra, col_extra, texts)
    last = n_row - 1
    grads, parts, _ = text_grads(*held, [last], {})
    received = swap(parts[last], "row", n_row, 1)
    more, more_parts, far = text_grads(*held, list(range(last))[::-1], grads)
    grads |= more
    parts |= more_parts
    sums = {last ^ 1: parts[last ^ 1] + received}
    near = image_grads(
        scale, col_extra, [grads[t] for t in range(n_row)], texts, [sums[last ^ 1]]
    )
    for q in range(1, last, 2):
        sums[q ^ 1] = parts[q ^ 1] + swap(parts[q], "row", n_row, 1)
    text_sum = halve(sums, "row", n_row, [1 << b for b in range(1, n_row.bit_length() - 1)])
    image_sum = scatter_images(near, far, "col", n_col)
    grad_scale = (jnp.sum(text_sum[block:]) + jnp.sum(image_sum[block:])) / coef[0, 0]
    return image_sum[:block], text_sum[:block], grad_scale


def solution(mesh):
    images = P(("row", "col"), None)
    texts = P(("col", "row"), None)
    return jax.shard_map(
        functools.partial(on_device, mesh.shape["row"], mesh.shape["col"]),
        mesh=mesh,
        in_specs=(images, texts, P()),
        out_specs=(images, texts, P()),
        check_vma=False,
    )
```

time: 142 us -> 111 us (0.78)
  blocking collectives: 53.5 us -> 0 us
  waiting for transfers between devices: 30.1 us -> 50 us
  other arithmetic: 8.17 us -> 2.46 us
  between operations: 1.52 us -> 3.97 us
  local copies, waits for them, and re-layouts: 1.37 us -> 3.56 us
  Pallas kernels: 25.2 us -> 27.3 us
  starting transfers between devices: 22 us -> 23.8 us
    all_gather x1 -> x0, blocking collectives: 53.5 us -> none  [on_device(): total = lax.all_gather(sum_first + sum_rest, ('row', 'col'))]
    ppermute x17 -> x22, waiting for transfers between devices: 17.7 us -> 50 us  [swap(): return lax.ppermute(x, axis, [(i, i ^ q) for i in range(n)])]
    ppermute x4 -> x0, waiting for transfers between devices: 12.4 us -> none  [the longest x1 10.2 us: gather_both(): end_three = lax.ppermute(mid_two, 'row', outward)]
    ppermute x17 -> x22, starting transfers between devices: 18.1 us -> 23.8 us  [swap(): return lax.ppermute(x, axis, [(i, i ^ q) for i in range(n)])]
    ppermute x4 -> x0, starting transfers between devices: 3.91 us -> none  [the longest x1 1.29 us: gather_both(): end_three = lax.ppermute(mid_two, 'row', outward)]
    add x2, other arithmetic: 4.06 us -> 0.66 us  [scatter_images(): total = total + swap(near[j] + sent[j], axis, n, 2 * j)]
    pallas_call x1 -> x2, Pallas kernels: 7.15 us -> 10 us  [stats(): pl.pallas_call(functools.partial(stats_kernel, len(texts), len(images), 1...]
    add x1, other arithmetic: 2.14 us -> 0.17 us  [halve(): blocks = {q ^ bit: blocks[q ^ bit] + sent[i] for i, q in enumerate(far)}]
  transfers between devices with their start and end apart: 21 -> 22, of which waited for: 9 -> 13; matrix products, arithmetic and copies ran while one was open for 5% -> 2% of each run, Pallas kernels for 9% -> 15%
where the time goes in v3:
time: 111 us
  waiting for transfers between devices  50 us (45%)
  Pallas kernels  27.3 us (25%)
  starting transfers between devices  23.8 us (21%)
  between operations  3.97 us (4%)
  local copies, waits for them, and re-layouts  3.56 us (3%)
  other arithmetic  2.46 us (2%)
    ppermute x22, waiting for transfers between devices, swap(): return lax.ppermute(x, axis, [(i, i ^ q) for i in range(n)])  50 us
    ppermute x22, starting transfers between devices, swap(): return lax.ppermute(x, axis, [(i, i ^ q) for i in range(n)])  23.8 us
    pallas_call x2, Pallas kernels, text_grads(): pl.pallas_call(functools.partial(text_kernel, tuple(order), len(done), bl...  13.3 us
    pallas_call x2, Pallas kernels, stats(): pl.pallas_call(functools.partial(stats_kernel, len(texts), len(images), 1...  10 us
  transfers between devices with their start and end apart: 22, of which 13 were waited for; matrix products, arithmetic and copies ran while one was open for 2% of the time, Pallas kernels for 15%

profile of v3, /device:TPU:0, one launch (start us, length us, event | category | flops | bytes accessed | tf_op | source)
XLA Modules:
  0.0 111.1 jit_solution(6438920975472985934)
XLA Ops:
  0.6 2.0 %cast_both.1 = (bf16[256,512]{1,0:T(8,128)(2,1)}, bf16[256,512]{1,0:T(8,128)(2,1)}) custom-call(f32[256,512]{1,0:T(8,128)} %a_ref.1, f32[256,512]{1,0:T(8,128)} %b_ref.1), custom_call_target="tpu_custom_call" | custom-call | tf_op jit(solution)/shard_map/cast_both/pallas_call | solution.py:39
  2.6 3.9 %collective-permute-start.6 = (bf16[256,512]{1,0:T(8,128)(2,1)}, bf16[256,512]{1,0:T(8,128)(2,1)S(1)}, u32[]{:S(2)}, u32[]{:S(2)}) collective-permute-start(bf16[256,512]{1,0:T(8,128)(2,1)} %get-tuple-element.26.refs_0_), channel_id=1, source_target_pairs={{0,6},{1,7},{2,4},{3,5},{4,2},{5,3},{6,0},{7,1},{8,14},{9,15},{10,... | collective-permute-start | bytes 786440 | tf_op jit(solution)/shard_map/ppermute | solution.py:20
  7.1 4.1 %collective-permute-start.3 = (bf16[256,512]{1,0:T(8,128)(2,1)}, bf16[256,512]{1,0:T(8,128)(2,1)S(1)}, u32[]{:S(2)}, u32[]{:S(2)}) collective-permute-start(bf16[256,512]{1,0:T(8,128)(2,1)} %get-tuple-element.27.refs_4_.refs_8_), channel_id=1, source_target_pairs={{0,24},{8,16},{16,8},{24,0},{1,25},{9,17},{17,9},{25,1},{2,26},{10... | collective-permute-start | bytes 786440 | tf_op jit(solution)/shard_map/ppermute | solution.py:20
  11.2 2.7 %collective-permute-done.6.refs_3_ = bf16[256,512]{1,0:T(8,128)(2,1)S(1)} collective-permute-done((bf16[256,512]{1,0:T(8,128)(2,1)}, bf16[256,512]{1,0:T(8,128)(2,1)S(1)}, u32[]{:S(2)}, u32[]{:S(2)}) %collective-permute-start.6) | collective-permute-done | bytes 262176 | tf_op jit(solution)/shard_map/ppermute | solution.py:20
  13.9 2.1 %collective-permute-start.1 = (bf16[256,512]{1,0:T(8,128)(2,1)}, bf16[256,512]{1,0:T(8,128)(2,1)S(1)}, u32[]{:S(2)}, u32[]{:S(2)}) collective-permute-start(bf16[256,512]{1,0:T(8,128)(2,1)} %get-tuple-element.27.refs_4_.refs_8_), channel_id=1, source_target_pairs={{0,8},{8,0},{16,24},{24,16},{1,9},{9,1},{17,25},{25,17},{2,10},{10... | collective-permute-start | bytes 786440 | tf_op jit(solution)/shard_map/ppermute | solution.py:20
  16.7 1.9 %collective-permute-done.5.refs_2_ = bf16[256,512]{1,0:T(8,128)(2,1)S(1)} collective-permute-done((bf16[256,512]{1,0:T(8,128)(2,1)}, bf16[256,512]{1,0:T(8,128)(2,1)S(1)}, u32[]{:S(2)}, u32[]{:S(2)}) %collective-permute-start.5) | collective-permute-done | bytes 262176 | tf_op jit(solution)/shard_map/ppermute | solution.py:20
  19.0 13.9 %collective-permute-done.2.refs_6_ = bf16[256,512]{1,0:T(8,128)(2,1)S(1)} collective-permute-done((bf16[256,512]{1,0:T(8,128)(2,1)}, bf16[256,512]{1,0:T(8,128)(2,1)S(1)}, u32[]{:S(2)}, u32[]{:S(2)}) %collective-permute-start.2) | collective-permute-done | bytes 262176 | tf_op jit(solution)/shard_map/ppermute | solution.py:20
  33.4 0.9 copy-done
  34.3 0.9 copy-done.2
  35.3 5.0 %stats_even.1 = (f32[4,8,256]{2,1,0:T(8,128)S(1)}, f32[3,4,256]{2,1,0:T(4,128)S(1)}, bf16[1024,512]{1,0:T(8,128)(2,1)S(1)}) custom-call(f32[1,1]{1,0:T(1,128)} %mul.127.coef_ref, s32[1,2]{1,0:T(1,128)S(1)} %add_bitcast_fusion.place_ref, bf16[256,512]{1,0:T(8,128)(2,1)S(1)} %copy-done.2, bf16[256,512]{1,0:T(8,128)(2,1)S(1)} %collective-permute-done.4.refs_1_, ...), custom_call_target="tpu_custom_call" | custom-call | flops 21474836480 | tf_op jit(solution)/shard_map/stats_even/pallas_call | solution.py:173
  40.3 5.0 %stats_odd.1 = (f32[4,8,256]{2,1,0:T(8,128)S(1)}, f32[3,4,256]{2,1,0:T(4,128)S(1)}, bf16[1024,512]{1,0:T(8,128)(2,1)S(1)}) custom-call(f32[1,1]{1,0:T(1,128)} %mul.127.coef_ref, s32[1,2]{1,0:T(1,128)S(1)} %add_bitcast_fusion.place_ref, bf16[256,512]{1,0:T(8,128)(2,1)S(1)} %collective-permute-done.refs_0_, ...), custom_call_target="tpu_custom_call" | custom-call | flops 21474836480 | tf_op jit(solution)/shard_map/stats_odd/pallas_call | solution.py:173
  46.0 3.1 %collective-permute-done.10 = f32[3,4,256]{2,1,0:T(4,128)S(1)} collective-permute-done((f32[3,4,256]{2,1,0:T(4,128)S(1)}, f32[3,4,256]{2,1,0:T(4,128)S(1)}, u32[]{:S(2)}, u32[]{:S(2)}) %collective-permute-start.10) | collective-permute-done | bytes 12320 | tf_op jit(solution)/shard_map/ppermute | solution.py:20
  49.2 1.0 collective-permute-start.11
  50.2 1.6 %collective-permute-start.13 = (f32[4,8,256]{2,1,0:T(8,128)S(1)}, f32[4,8,256]{2,1,0:T(8,128)S(1)}, u32[]{:S(2)}, u32[]{:S(2)}) collective-permute-start(f32[4,8,256]{2,1,0:T(8,128)S(1)} %pad_maximum_fusion), channel_id=1, source_target_pairs={{0,2},{1,3},{2,0},{3,1},{4,6},{5,7},{6,4},{7,5},{8,10},{9,11},{10,... | collective-permute-start | bytes 98312 | tf_op jit(solution)/shard_map/ppermute | solution.py:20
  51.8 2.0 %collective-permute-done.11 = f32[3,4,256]{2,1,0:T(4,128)S(1)} collective-permute-done((f32[3,4,256]{2,1,0:T(4,128)S(1)}, f32[3,4,256]{2,1,0:T(4,128)S(1)}, u32[]{:S(2)}, u32[]{:S(2)}) %collective-permute-start.11) | collective-permute-done | bytes 12320 | tf_op jit(solution)/shard_map/ppermute | solution.py:20
  54.2 1.6 %collective-permute-start.14 = (f32[4,8,256]{2,1,0:T(8,128)S(1)}, f32[4,8,256]{2,1,0:T(8,128)S(1)}, u32[]{:S(2)}, u32[]{:S(2)}) collective-permute-start(f32[4,8,256]{2,1,0:T(8,128)S(1)} %pad_maximum_fusion.1), channel_id=1, source_target_pairs={{0,4},{1,5},{2,6},{3,7},{4,0},{5,1},{6,2},{7,3},{8,12},{9,13},{10,... | collective-permute-start | bytes 98312 | tf_op jit(solution)/shard_map/ppermute | solution.py:20
  55.8 2.4 %collective-permute-done.14 = f32[4,8,256]{2,1,0:T(8,128)S(1)} collective-permute-done((f32[4,8,256]{2,1,0:T(8,128)S(1)}, f32[4,8,256]{2,1,0:T(8,128)S(1)}, u32[]{:S(2)}, u32[]{:S(2)}) %collective-permute-start.14) | collective-permute-done | bytes 32800 | tf_op jit(solution)/shard_map/ppermute | solution.py:20
  58.3 3.2 %text_grads_1.1 = (bf16[256,2048]{1,0:T(8,128)(2,1)S(1)}, f32[264,512]{1,0:T(8,128)S(1)}) custom-call(f32[1,1]{1,0:T(1,128)} %bitcast.261.scale_ref, f32[1,1]{1,0:T(1,128)} %mul.127.coef_ref, s32[1,2]{1,0:T(1,128)S(1)} %add_bitcast_fusion.place_ref, bf16[1024,512]{1,0:T(8,128)(2,1)S(1)} %get-tuple-element.37.refs_0_, ...), custom_call_target="tpu_custom_call" | custom-call | flops 21474836480 | tf_op jit(solution)/shard_map/text_grads_1/pallas_call | solution.py:309
  61.5 2.1 %collective-permute-start.15 = (f32[264,512]{1,0:T(8,128)S(1)}, f32[264,512]{1,0:T(8,128)S(1)}, u32[]{:S(2)}, u32[]{:S(2)}) collective-permute-start(f32[264,512]{1,0:T(8,128)S(1)} %get-tuple-element.45), channel_id=1, source_target_pairs={{0,8},{8,0},{16,24},{24,16},{1,9},{9,1},{17,25},{25,17},{2,10},{10... | collective-permute-start | bytes 1622024 | tf_op jit(solution)/shard_map/ppermute | solution.py:20
  63.5 10.1 %text_grads_3.1 = (bf16[256,2048]{1,0:T(8,128)(2,1)S(1)}, bf16[256,2048]{1,0:T(8,128)(2,1)S(1)}, bf16[256,2048]{1,0:T(8,128)(2,1)S(1)}, f32[264,512]{1,0:T(8,128...) custom-call(f32[1,1]{1,0:T(1,128)} %bitcast.262.scale_ref, ...), custom_call_target="tpu_custom_call" | custom-call | flops 64424509440 | tf_op jit(solution)/shard_map/text_grads_3/pallas_call | solution.py:309
  74.0 2.0 %collective-permute-start.21 = (f32[1,264,512]{2,1,0:T(8,128)S(1)}, f32[1,264,512]{2,1,0:T(8,128)S(1)}, u32[]{:S(2)}, u32[]{:S(2)}) collective-permute-start(f32[1,264,512]{2,1,0:T(8,128)S(1)} %bitcast.264), channel_id=1, source_target_pairs={{0,16},{8,24},{16,0},{24,8},{1,17},{9,25},{17,1},{25,9},{2,18},{10... | collective-permute-start | bytes 1622024 | tf_op jit(solution)/shard_map/ppermute | solution.py:20
  76.0 1.9 %image_grads.1 = f32[4,264,512]{2,1,0:T(8,128)S(1)} custom-call(f32[1,1]{1,0:T(1,128)} %bitcast.263.scale_ref, f32[4,256]{1,0:T(4,128)S(1)} %get-tuple-element.49.refs_5_.extra, bf16[256,2048]{1,0:T(8,128)(2,1)S(1)} %get-tuple-element.41.refs_0_, bf16[256,2048]{1,0:T(8,128)(2,1)S(1)} %get-tuple-element.42.refs_1_, ...), custom_call_target="tpu_custom_call" | custom-call | flops 21474836480 | tf_op jit(solution)/shard_map/image_grads/pallas_call | solution.py:344
  78.4 1.6 %collective-permute-start.17 = (f32[264,512]{1,0:T(8,128)S(1)}, f32[264,512]{1,0:T(8,128)S(1)}, u32[]{:S(2)}, u32[]{:S(2)}) collective-permute-start(f32[264,512]{1,0:T(8,128)S(1)} %get-tuple-element.55), channel_id=1, source_target_pairs={{0,2},{1,3},{2,0},{3,1},{4,6},{5,7},{6,4},{7,5},{8,10},{9,11},{10,... | collective-permute-start | bytes 1622024 | tf_op jit(solution)/shard_map/ppermute | solution.py:20
  79.9 1.5 %collective-permute-start.19 = (f32[264,512]{1,0:T(8,128)S(1)}, f32[264,512]{1,0:T(8,128)S(1)}, u32[]{:S(2)}, u32[]{:S(2)}) collective-permute-start(f32[264,512]{1,0:T(8,128)S(1)} %get-tuple-element.56), channel_id=1, source_target_pairs={{0,6},{1,7},{2,4},{3,5},{4,2},{5,3},{6,0},{7,1},{8,14},{9,15},{10,... | collective-permute-start | bytes 1622024 | tf_op jit(solution)/shard_map/ppermute | solution.py:20
  81.9 17.2 %collective-permute-done.20 = f32[264,512]{1,0:T(8,128)S(1)} collective-permute-done((f32[264,512]{1,0:T(8,128)S(1)}, f32[264,512]{1,0:T(8,128)S(1)}, u32[]{:S(2)}, u32[]{:S(2)}) %collective-permute-start.20) | collective-permute-done | bytes 540704 | tf_op jit(solution)/shard_map/ppermute | solution.py:20
  99.1 2.1 %collective-permute-done.21 = f32[1,264,512]{2,1,0:T(8,128)S(1)} collective-permute-done((f32[1,264,512]{2,1,0:T(8,128)S(1)}, f32[1,264,512]{2,1,0:T(8,128)S(1)}, u32[]{:S(2)}, u32[]{:S(2)}) %collective-permute-start.21) | collective-permute-done | bytes 540704 | tf_op jit(solution)/shard_map/ppermute | solution.py:20
  101.3 0.8 slice.182
  102.1 0.6 slice_reduce_fusion.1
  102.7 2.7 %collective-permute-done.19 = f32[264,512]{1,0:T(8,128)S(1)} collective-permute-done((f32[264,512]{1,0:T(8,128)S(1)}, f32[264,512]{1,0:T(8,128)S(1)}, u32[]{:S(2)}, u32[]{:S(2)}) %collective-permute-start.19) | collective-permute-done | bytes 540704 | tf_op jit(solution)/shard_map/ppermute | solution.py:20
  105.4 1.4 %collective-permute-done.18 = f32[264,512]{1,0:T(8,128)S(1)} collective-permute-done((f32[264,512]{1,0:T(8,128)S(1)}, f32[264,512]{1,0:T(8,128)S(1)}, u32[]{:S(2)}, u32[]{:S(2)}) %collective-permute-start.18) | collective-permute-done | bytes 540704 | tf_op jit(solution)/shard_map/ppermute | solution.py:20
  107.1 0.7 slice_reduce_fusion
  107.8 0.8 slice.181
  (45 shorter events, 4.3 us)
Async XLA Ops:
  2.6 11.3 %collective-permute-start.6 = (bf16[256,512]{1,0:T(8,128)(2,1)}, bf16[256,512]{1,0:T(8,128)(2,1)S(1)}, u32[]{:S(2)}, u32[]{:S(2)}) collective-permute-start(bf16[256,512]{1,0:T(8,128)(2,1)} %get-tuple-element.26.refs_0_), channel_id=1, source_target_pairs={{0,6},{1,7},{2,4},{3,5},{4,2},{5,3},{6,0},{7,1},{8,14},{9,15},{10,... | collective-permute-start | bytes 786440 | tf_op jit(solution)/shard_map/ppermute | solution.py:20
  6.5 12.1 %collective-permute-start.5 = (bf16[256,512]{1,0:T(8,128)(2,1)}, bf16[256,512]{1,0:T(8,128)(2,1)S(1)}, u32[]{:S(2)}, u32[]{:S(2)}) collective-permute-start(bf16[256,512]{1,0:T(8,128)(2,1)} %get-tuple-element.26.refs_0_), channel_id=1, source_target_pairs={{0,4},{1,5},{2,6},{3,7},{4,0},{5,1},{6,2},{7,3},{8,12},{9,13},{10,... | collective-permute-start | bytes 786440 | tf_op jit(solution)/shard_map/ppermute | solution.py:20
  7.0 11.9 %collective-permute-start.4 = (bf16[256,512]{1,0:T(8,128)(2,1)}, bf16[256,512]{1,0:T(8,128)(2,1)S(1)}, u32[]{:S(2)}, u32[]{:S(2)}) collective-permute-start(bf16[256,512]{1,0:T(8,128)(2,1)} %get-tuple-element.26.refs_0_), channel_id=1, source_target_pairs={{0,2},{1,3},{2,0},{3,1},{4,6},{5,7},{6,4},{7,5},{8,10},{9,11},{10,... | collective-permute-start | bytes 786440 | tf_op jit(solution)/shard_map/ppermute | solution.py:20
  7.1 11.9 %collective-permute-start.3 = (bf16[256,512]{1,0:T(8,128)(2,1)}, bf16[256,512]{1,0:T(8,128)(2,1)S(1)}, u32[]{:S(2)}, u32[]{:S(2)}) collective-permute-start(bf16[256,512]{1,0:T(8,128)(2,1)} %get-tuple-element.27.refs_4_.refs_8_), channel_id=1, source_target_pairs={{0,24},{8,16},{16,8},{24,0},{1,25},{9,17},{17,9},{25,1},{2,26},{10... | collective-permute-start | bytes 786440 | tf_op jit(solution)/shard_map/ppermute | solution.py:20
  11.2 21.7 %collective-permute-start.2 = (bf16[256,512]{1,0:T(8,128)(2,1)}, bf16[256,512]{1,0:T(8,128)(2,1)S(1)}, u32[]{:S(2)}, u32[]{:S(2)}) collective-permute-start(bf16[256,512]{1,0:T(8,128)(2,1)} %get-tuple-element.27.refs_4_.refs_8_), channel_id=1, source_target_pairs={{0,16},{8,24},{16,0},{24,8},{1,17},{9,25},{17,1},{25,9},{2,18},{10... | collective-permute-start | bytes 786440 | tf_op jit(solution)/shard_map/ppermute | solution.py:20
  13.9 18.9 %collective-permute-start.1 = (bf16[256,512]{1,0:T(8,128)(2,1)}, bf16[256,512]{1,0:T(8,128)(2,1)S(1)}, u32[]{:S(2)}, u32[]{:S(2)}) collective-permute-start(bf16[256,512]{1,0:T(8,128)(2,1)} %get-tuple-element.27.refs_4_.refs_8_), channel_id=1, source_target_pairs={{0,8},{8,0},{16,24},{24,16},{1,9},{9,1},{17,25},{25,17},{2,10},{10... | collective-permute-start | bytes 786440 | tf_op jit(solution)/shard_map/ppermute | solution.py:20
  18.7 21.6 %collective-permute-start = (bf16[256,512]{1,0:T(8,128)(2,1)}, bf16[256,512]{1,0:T(8,128)(2,1)S(1)}, u32[]{:S(2)}, u32[]{:S(2)}) collective-permute-start(bf16[256,512]{1,0:T(8,128)(2,1)} %get-tuple-element.26.refs_0_), channel_id=1, source_target_pairs={{0,1},{1,0},{2,3},{3,2},{4,5},{5,4},{6,7},{7,6},{8,9},{9,8},{10,11... | collective-permute-start | bytes 786440 | tf_op jit(solution)/shard_map/ppermute | solution.py:20
  32.9 7.4 %collective-permute-start.7 = (bf16[256,512]{1,0:T(8,128)(2,1)S(1)}, bf16[256,512]{1,0:T(8,128)(2,1)S(1)}, u32[]{:S(2)}, u32[]{:S(2)}) collective-permute-start(bf16[256,512]{1,0:T(8,128)(2,1)S(1)} %collective-permute-done.4.refs_1_), channel_id=1, source_target_pairs={{0,1},{1,0},{2,3},{3,2},{4,5},{5,4},{6,7},{7,6},{8,9},{9,8},{10,11... | collective-permute-start | bytes 786440 | tf_op jit(solution)/shard_map/ppermute | solution.py:20
  32.9 7.4 %collective-permute-start.8 = (bf16[256,512]{1,0:T(8,128)(2,1)S(1)}, bf16[256,512]{1,0:T(8,128)(2,1)S(1)}, u32[]{:S(2)}, u32[]{:S(2)}) collective-permute-start(bf16[256,512]{1,0:T(8,128)(2,1)S(1)} %collective-permute-done.5.refs_2_), channel_id=1, source_target_pairs={{0,1},{1,0},{2,3},{3,2},{4,5},{5,4},{6,7},{7,6},{8,9},{9,8},{10,11... | collective-permute-start | bytes 786440 | tf_op jit(solution)/shard_map/ppermute | solution.py:20
  33.4 6.9 %collective-permute-start.9 = (bf16[256,512]{1,0:T(8,128)(2,1)S(1)}, bf16[256,512]{1,0:T(8,128)(2,1)S(1)}, u32[]{:S(2)}, u32[]{:S(2)}) collective-permute-start(bf16[256,512]{1,0:T(8,128)(2,1)S(1)} %collective-permute-done.6.refs_3_), channel_id=1, source_target_pairs={{0,1},{1,0},{2,3},{3,2},{4,5},{5,4},{6,7},{7,6},{8,9},{9,8},{10,11... | collective-permute-start | bytes 786440 | tf_op jit(solution)/shard_map/ppermute | solution.py:20
  33.4 0.9 copy-start
  34.3 0.9 copy-start.2
  35.3 5.0 %copy-start.1 = (bf16[256,512]{1,0:T(8,128)(2,1)S(1)}, bf16[256,512]{1,0:T(8,128)(2,1)}, u32[]{:S(2)}) copy-start(bf16[256,512]{1,0:T(8,128)(2,1)} %get-tuple-element.27.refs_4_.refs_8_) | copy-start | bytes 786436
  45.4 3.8 %collective-permute-start.10 = (f32[3,4,256]{2,1,0:T(4,128)S(1)}, f32[3,4,256]{2,1,0:T(4,128)S(1)}, u32[]{:S(2)}, u32[]{:S(2)}) collective-permute-start(f32[3,4,256]{2,1,0:T(4,128)S(1)} %get-tuple-element.36), channel_id=1, source_target_pairs={{0,8},{8,0},{16,24},{24,16},{1,9},{9,1},{17,25},{25,17},{2,10},{10... | collective-permute-start | bytes 36872 | tf_op jit(solution)/shard_map/ppermute | solution.py:20
  45.4 4.7 %collective-permute-start.12 = (f32[4,8,256]{2,1,0:T(8,128)S(1)}, f32[4,8,256]{2,1,0:T(8,128)S(1)}, u32[]{:S(2)}, u32[]{:S(2)}) collective-permute-start(f32[4,8,256]{2,1,0:T(8,128)S(1)} %get-tuple-element.39), channel_id=1, source_target_pairs={{0,1},{1,0},{2,3},{3,2},{4,5},{5,4},{6,7},{7,6},{8,9},{9,8},{10,11... | collective-permute-start | bytes 98312 | tf_op jit(solution)/shard_map/ppermute | solution.py:20
  49.2 4.7 %collective-permute-start.11 = (f32[3,4,256]{2,1,0:T(4,128)S(1)}, f32[3,4,256]{2,1,0:T(4,128)S(1)}, u32[]{:S(2)}, u32[]{:S(2)}) collective-permute-start(f32[3,4,256]{2,1,0:T(4,128)S(1)} %pad_maximum_fusion.2), channel_id=1, source_target_pairs={{0,16},{8,24},{16,0},{24,8},{1,17},{9,25},{17,1},{25,9},{2,18},{10... | collective-permute-start | bytes 36872 | tf_op jit(solution)/shard_map/ppermute | solution.py:20
  50.2 4.0 %collective-permute-start.13 = (f32[4,8,256]{2,1,0:T(8,128)S(1)}, f32[4,8,256]{2,1,0:T(8,128)S(1)}, u32[]{:S(2)}, u32[]{:S(2)}) collective-permute-start(f32[4,8,256]{2,1,0:T(8,128)S(1)} %pad_maximum_fusion), channel_id=1, source_target_pairs={{0,2},{1,3},{2,0},{3,1},{4,6},{5,7},{6,4},{7,5},{8,10},{9,11},{10,... | collective-permute-start | bytes 98312 | tf_op jit(solution)/shard_map/ppermute | solution.py:20
  54.2 4.0 %collective-permute-start.14 = (f32[4,8,256]{2,1,0:T(8,128)S(1)}, f32[4,8,256]{2,1,0:T(8,128)S(1)}, u32[]{:S(2)}, u32[]{:S(2)}) collective-permute-start(f32[4,8,256]{2,1,0:T(8,128)S(1)} %pad_maximum_fusion.1), channel_id=1, source_target_pairs={{0,4},{1,5},{2,6},{3,7},{4,0},{5,1},{6,2},{7,3},{8,12},{9,13},{10,... | collective-permute-start | bytes 98312 | tf_op jit(solution)/shard_map/ppermute | solution.py:20
  61.5 12.4 %collective-permute-start.15 = (f32[264,512]{1,0:T(8,128)S(1)}, f32[264,512]{1,0:T(8,128)S(1)}, u32[]{:S(2)}, u32[]{:S(2)}) collective-permute-start(f32[264,512]{1,0:T(8,128)S(1)} %get-tuple-element.45), channel_id=1, source_target_pairs={{0,8},{8,0},{16,24},{24,16},{1,9},{9,1},{17,25},{25,17},{2,10},{10... | collective-permute-start | bytes 1622024 | tf_op jit(solution)/shard_map/ppermute | solution.py:20
  73.7 4.3 %collective-permute-start.16 = (f32[4,264,512]{2,1,0:T(8,128)S(1)}, f32[4,264,512]{2,1,0:T(8,128)S(1)}, u32[]{:S(2)}, u32[]{:S(2)}) collective-permute-start(f32[4,264,512]{2,1,0:T(8,128)S(1)} %get-tuple-element.46), channel_id=1, source_target_pairs={{0,1},{1,0},{2,3},{3,2},{4,5},{5,4},{6,7},{7,6},{8,9},{9,8},{10,11... | collective-permute-start | bytes 6488072 | tf_op jit(solution)/shard_map/ppermute | solution.py:20
  73.8 25.3 %collective-permute-start.20 = (f32[264,512]{1,0:T(8,128)S(1)}, f32[264,512]{1,0:T(8,128)S(1)}, u32[]{:S(2)}, u32[]{:S(2)}) collective-permute-start(f32[264,512]{1,0:T(8,128)S(1)} %get-tuple-element.48), channel_id=1, source_target_pairs={{0,8},{8,0},{16,24},{24,16},{1,9},{9,1},{17,25},{25,17},{2,10},{10... | collective-permute-start | bytes 1622024 | tf_op jit(solution)/shard_map/ppermute | solution.py:20
  74.0 27.2 %collective-permute-start.21 = (f32[1,264,512]{2,1,0:T(8,128)S(1)}, f32[1,264,512]{2,1,0:T(8,128)S(1)}, u32[]{:S(2)}, u32[]{:S(2)}) collective-permute-start(f32[1,264,512]{2,1,0:T(8,128)S(1)} %bitcast.264), channel_id=1, source_target_pairs={{0,16},{8,24},{16,0},{24,8},{1,17},{9,25},{17,1},{25,9},{2,18},{10... | collective-permute-start | bytes 1622024 | tf_op jit(solution)/shard_map/ppermute | solution.py:20
  78.4 24.4 %collective-permute-start.17 = (f32[264,512]{1,0:T(8,128)S(1)}, f32[264,512]{1,0:T(8,128)S(1)}, u32[]{:S(2)}, u32[]{:S(2)}) collective-permute-start(f32[264,512]{1,0:T(8,128)S(1)} %get-tuple-element.55), channel_id=1, source_target_pairs={{0,2},{1,3},{2,0},{3,1},{4,6},{5,7},{6,4},{7,5},{8,10},{9,11},{10,... | collective-permute-start | bytes 1622024 | tf_op jit(solution)/shard_map/ppermute | solution.py:20
  79.9 25.5 %collective-permute-start.19 = (f32[264,512]{1,0:T(8,128)S(1)}, f32[264,512]{1,0:T(8,128)S(1)}, u32[]{:S(2)}, u32[]{:S(2)}) collective-permute-start(f32[264,512]{1,0:T(8,128)S(1)} %get-tuple-element.56), channel_id=1, source_target_pairs={{0,6},{1,7},{2,4},{3,5},{4,2},{5,3},{6,0},{7,1},{8,14},{9,15},{10,... | collective-permute-start | bytes 1622024 | tf_op jit(solution)/shard_map/ppermute | solution.py:20
  81.4 25.3 %collective-permute-start.18 = (f32[264,512]{1,0:T(8,128)S(1)}, f32[264,512]{1,0:T(8,128)S(1)}, u32[]{:S(2)}, u32[]{:S(2)}) collective-permute-start(f32[264,512]{1,0:T(8,128)S(1)} %get-tuple-element.57), channel_id=1, source_target_pairs={{0,4},{1,5},{2,6},{3,7},{4,0},{5,1},{6,2},{7,3},{8,12},{9,13},{10,... | collective-permute-start | bytes 1622024 | tf_op jit(solution)/shard_map/ppermute | solution.py:20

commit v4 on v3

--- a/solution.py
+++ b/solution.py
@@ -27,22 +27,6 @@
     texts, images = lax.optimization_barrier((texts, images))
     odd += [swap(i, "col", n_col, 1) for i in images]
     return [image, *images], odd, [text, *texts]
-
-
-def cast_kernel(a_ref, b_ref, a_out, b_out):
-    a_out[...] = a_ref[...].astype(jnp.bfloat16)
-    b_out[...] = b_ref[...].astype(jnp.bfloat16)
-
-
-def cast_both(a, b):
-    vmem = pl.BlockSpec(memory_space=VMEM)
-    return pl.pallas_call(
-        cast_kernel,
-        out_shape=tuple(jax.ShapeDtypeStruct(x.shape, jnp.bfloat16) for x in (a, b)),
-        in_specs=[vmem] * 2,
-        out_specs=(vmem,) * 2,
-        name="cast_both",
-    )(a, b)
 
 
 def nt_dot(a, b):
@@ -92,7 +76,7 @@
 
         return carry
 
-    lax.fori_loop(0, rows // block, products, 0, unroll=2)
+    lax.fori_loop(0, rows // block, products, 0, unroll=4)
 
     col_max[...] = jnp.broadcast_to(
         jnp.max(col_max[...], axis=1, keepdims=True), col_max.shape
@@ -195,12 +179,25 @@
     )(coef, place, *images, *texts, *before)
 
 
-def exchanged(parts, axis, n):
-    parts = [parts[i] for i in range(parts.shape[0])]
-    for b in range(n.bit_length() - 1):
-        parts = merged(parts, swap(jnp.stack(parts), axis, n, 1 << b))
+def by_pairs(blocks, add):
+    while len(blocks) > 1:
+        blocks = [add(blocks[i], blocks[i + 1]) for i in range(0, len(blocks), 2)]
+    return blocks[0]
+
+
+def lse_and_mean(parts):
     mean = 0.5 * parts[2] / parts[1]
     return parts[0] + jnp.log(parts[1]) * LOG2E, mean - parts[3] if len(parts) > 3 else mean
+
+
+def exchanged(row_parts, col_parts, n_col, n_row):
+    rows = [swap(row_parts, "col", n_col, q) for q in range(2, n_col, 2)]
+    cols = [swap(col_parts, "row", n_row, q) for q in range(1, n_row)]
+    rows, cols = lax.optimization_barrier((rows, cols))
+    cols = by_pairs([list(x) for x in (col_parts, *cols)], merged)
+    rows = by_pairs([list(x) for x in (row_parts, *rows)], merged)
+    rows = merged(rows, list(swap(jnp.stack(rows), "col", n_col, 1)))
+    return *lse_and_mean(rows), *lse_and_mean(cols)
 
 
 def put_extra(out, extra_ref):
@@ -243,7 +240,7 @@
                     grad_ref[r : r + step, pl.ds(at + lane, LANES)] = g.astype(jnp.bfloat16)
             return carry
 
-        lax.fori_loop(0, half // block, one, 0, unroll=2)
+        lax.fori_loop(0, half // block, one, 0, unroll=4)
     out_ref[:size, :] = scale_ref[0, 0] * (
         jnp.dot(grad_ref[:, :half], halves[0][...], preferred_element_type=jnp.float32)
         + jnp.dot(grad_ref[:, half:], halves[1][...], preferred_element_type=jnp.float32)
@@ -366,10 +363,8 @@
 
 def scatter_images(near, far, axis, n):
     sent = swap(far, axis, n, 1)
-    total = near[0] + sent[0]
-    for j in range(1, n // 2):
-        total = total + swap(near[j] + sent[j], axis, n, 2 * j)
-    return total
+    sums = [near[j] + sent[j] for j in range(n // 2)]
+    return by_pairs([sums[0]] + [swap(sums[j], axis, n, 2 * j) for j in range(1, n // 2)], jnp.add)
 
 
 def on_device(n_row, n_col, image_embeds, text_embeds, logit_scale):
@@ -378,12 +373,11 @@
     place = jnp.stack([r, c]).reshape(1, 2)
     scale = logit_scale.reshape(1, 1)
     coef = scale * LOG2E
-    image_half, text_half = cast_both(image_embeds, text_embeds)
+    image_half, text_half = image_embeds.astype(jnp.bfloat16), text_embeds.astype(jnp.bfloat16)
     even, odd, texts = gather_both(image_half, text_half, n_col, n_row)
     row_parts, col_parts, even = stats(coef, place, even, texts, (), n_col)
     row_parts, col_parts, odd = stats(coef, place, odd, texts, (row_parts, col_parts), n_col)
-    row_lse, row_extra = exchanged(row_parts, "col", n_col)
-    col_lse, col_extra = exchanged(col_parts, "row", n_row)
+    row_lse, row_extra, col_lse, col_extra = exchanged(row_parts, col_parts, n_col, n_row)
 
     held = (scale, coef, place, even, odd, row_lse, col_lse, row_extra, col_extra, texts)
     last = n_row - 1

time: 111 us -> 108 us (0.973)
  Pallas kernels: 27.3 us -> 20.6 us
  waiting for transfers between devices: 50 us -> 53.5 us
  other arithmetic: 2.46 us -> 4.54 us
  local copies, waits for them, and re-layouts: 3.56 us -> 1.66 us
    pallas_call x2, Pallas kernels: 13.3 us -> 8.63 us  [text_grads(): pl.pallas_call(functools.partial(text_kernel, tuple(order), len(done), bl...]
    ppermute x22 -> x24, waiting for transfers between devices: 50 us -> 53.5 us  [swap(): return lax.ppermute(x, axis, [(i, i ^ q) for i in range(n)])]
    convert_element_type x0 -> x2, other arithmetic: none -> 2.15 us  [the longest x1 1.07 us: on_device(): image_embeds.astype(jnp.bfloat16)]
    pallas_call x1 -> x0, Pallas kernels: 2.02 us -> none  [cast_both(): pl.pallas_call(cast_kernel, out_shape=tuple((jax.ShapeDtypeStruct(x.shape...]
    unnamed x6 -> x0, local copies, waits for them, and re-layouts: 1.9 us -> none
    ppermute x22 -> x24, starting transfers between devices: 23.8 us -> 24 us  [swap(): return lax.ppermute(x, axis, [(i, i ^ q) for i in range(n)])]
  transfers between devices with their start and end apart: 22 -> 24, of which waited for: 13 -> 14; matrix products, arithmetic and copies ran while one was open for 2% -> 3% of each run, Pallas kernels for 15% -> 12%
where the time goes in v4:
time: 108 us
  waiting for transfers between devices  53.5 us (50%)
  starting transfers between devices  24 us (22%)
  Pallas kernels  20.6 us (19%)
  other arithmetic  4.54 us (4%)
  between operations  3.84 us (4%)
  local copies, waits for them, and re-layouts  1.66 us (2%)
    ppermute x24, waiting for transfers between devices, swap(): return lax.ppermute(x, axis, [(i, i ^ q) for i in range(n)])  53.5 us
    ppermute x24, starting transfers between devices, swap(): return lax.ppermute(x, axis, [(i, i ^ q) for i in range(n)])  24 us
    pallas_call x2, Pallas kernels, stats(): pl.pallas_call(functools.partial(stats_kernel, len(texts), len(images), 1...  10 us
    pallas_call x2, Pallas kernels, text_grads(): pl.pallas_call(functools.partial(text_kernel, tuple(order), len(done), bl...  8.63 us
  transfers between devices with their start and end apart: 24, of which 14 were waited for; matrix products, arithmetic and copies ran while one was open for 3% of the time, Pallas kernels for 12%

profile of v4, /device:TPU:0, one launch (start us, length us, event | category | flops | bytes accessed | tf_op | source)
XLA Modules:
  0.0 108.2 jit_solution(2027115616103600948)
XLA Ops:
  0.6 1.1 convert_element_type.6.refs_0_
  1.7 4.0 %collective-permute-start.6 = (bf16[256,512]{1,0:T(8,128)(2,1)S(1)}, bf16[256,512]{1,0:T(8,128)(2,1)S(1)}, u32[]{:S(2)}, u32[]{:S(2)}) collective-permute-start(bf16[256,512]{1,0:T(8,128)(2,1)S(1)} %convert_element_type.6.refs_0_), channel_id=1, source_target_pairs={{0,6},{1,7},{2,4},{3,5},{4,2},{5,3},{6,0},{7,1},{8,14},{9,15},{10,... | collective-permute-start | bytes 786440 | tf_op jit(solution)/shard_map/ppermute | solution.py:20
  6.3 1.1 convert_element_type.7.refs_4_.refs_8_
  7.4 4.1 %collective-permute-start.3 = (bf16[256,512]{1,0:T(8,128)(2,1)S(1)}, bf16[256,512]{1,0:T(8,128)(2,1)S(1)}, u32[]{:S(2)}, u32[]{:S(2)}) collective-permute-start(bf16[256,512]{1,0:T(8,128)(2,1)S(1)} %convert_element_type.7.refs_4_.refs_8_), channel_id=1, source_target_pairs={{0,24},{8,16},{16,8},{24,0},{1,25},{9,17},{17,9},{25,1},{2,26},{10... | collective-permute-start | bytes 786440 | tf_op jit(solution)/shard_map/ppermute | solution.py:20
  11.5 1.4 %collective-permute-done.6.refs_3_ = bf16[256,512]{1,0:T(8,128)(2,1)S(1)} collective-permute-done((bf16[256,512]{1,0:T(8,128)(2,1)S(1)}, bf16[256,512]{1,0:T(8,128)(2,1)S(1)}, u32[]{:S(2)}, u32[]{:S(2)}) %collective-permute-start.6) | collective-permute-done | bytes 262176 | tf_op jit(solution)/shard_map/ppermute | solution.py:20
  12.8 2.1 %collective-permute-start.1 = (bf16[256,512]{1,0:T(8,128)(2,1)S(1)}, bf16[256,512]{1,0:T(8,128)(2,1)S(1)}, u32[]{:S(2)}, u32[]{:S(2)}) collective-permute-start(bf16[256,512]{1,0:T(8,128)(2,1)S(1)} %convert_element_type.7.refs_4_.refs_8_), channel_id=1, source_target_pairs={{0,8},{8,0},{16,24},{24,16},{1,9},{9,1},{17,25},{25,17},{2,10},{10... | collective-permute-start | bytes 786440 | tf_op jit(solution)/shard_map/ppermute | solution.py:20
  15.7 1.9 %collective-permute-done.5.refs_2_ = bf16[256,512]{1,0:T(8,128)(2,1)S(1)} collective-permute-done((bf16[256,512]{1,0:T(8,128)(2,1)S(1)}, bf16[256,512]{1,0:T(8,128)(2,1)S(1)}, u32[]{:S(2)}, u32[]{:S(2)}) %collective-permute-start.5) | collective-permute-done | bytes 262176 | tf_op jit(solution)/shard_map/ppermute | solution.py:20
  17.9 0.8 collective-permute-done.3.refs_7_.refs_6_.refs_10_
  18.7 14.2 %collective-permute-done.2.refs_6_ = bf16[256,512]{1,0:T(8,128)(2,1)S(1)} collective-permute-done((bf16[256,512]{1,0:T(8,128)(2,1)S(1)}, bf16[256,512]{1,0:T(8,128)(2,1)S(1)}, u32[]{:S(2)}, u32[]{:S(2)}) %collective-permute-start.2) | collective-permute-done | bytes 262176 | tf_op jit(solution)/shard_map/ppermute | solution.py:20
  33.4 4.9 %stats_even.1 = (f32[4,8,256]{2,1,0:T(8,128)S(1)}, f32[3,4,256]{2,1,0:T(4,128)S(1)}, bf16[1024,512]{1,0:T(8,128)(2,1)S(1)}) custom-call(f32[1,1]{1,0:T(1,128)} %mul.147.coef_ref, s32[1,2]{1,0:T(1,128)S(1)} %add_bitcast_fusion.place_ref, bf16[256,512]{1,0:T(8,128)(2,1)S(1)} %convert_element_type.6.refs_0_, ...), custom_call_target="tpu_custom_call" | custom-call | flops 21474836480 | tf_op jit(solution)/shard_map/stats_even/pallas_call | solution.py:157
  38.4 5.1 %stats_odd.1 = (f32[4,8,256]{2,1,0:T(8,128)S(1)}, f32[3,4,256]{2,1,0:T(4,128)S(1)}, bf16[1024,512]{1,0:T(8,128)(2,1)S(1)}) custom-call(f32[1,1]{1,0:T(1,128)} %mul.147.coef_ref, s32[1,2]{1,0:T(1,128)S(1)} %add_bitcast_fusion.place_ref, bf16[256,512]{1,0:T(8,128)(2,1)S(1)} %collective-permute-done.refs_0_, ...), custom_call_target="tpu_custom_call" | custom-call | flops 21474836480 | tf_op jit(solution)/shard_map/stats_odd/pallas_call | solution.py:157
  43.5 2.4 %collective-permute-start.12 = (f32[4,8,256]{2,1,0:T(8,128)S(1)}, f32[4,8,256]{2,1,0:T(8,128)S(1)}, u32[]{:S(2)}, u32[]{:S(2)}) collective-permute-start(f32[4,8,256]{2,1,0:T(8,128)S(1)} %get-tuple-element.39), channel_id=1, source_target_pairs={{0,6},{1,7},{2,4},{3,5},{4,2},{5,3},{6,0},{7,1},{8,14},{9,15},{10,... | collective-permute-start | bytes 98312 | tf_op jit(solution)/shard_map/ppermute | solution.py:20
  46.5 0.6 collective-permute-start.10
  47.1 2.4 %collective-permute-start.15 = (f32[3,4,256]{2,1,0:T(4,128)S(1)}, f32[3,4,256]{2,1,0:T(4,128)S(1)}, u32[]{:S(2)}, u32[]{:S(2)}) collective-permute-start(f32[3,4,256]{2,1,0:T(4,128)S(1)} %get-tuple-element.38), channel_id=1, source_target_pairs={{0,24},{8,16},{16,8},{24,0},{1,25},{9,17},{17,9},{25,1},{2,26},{10... | collective-permute-start | bytes 36872 | tf_op jit(solution)/shard_map/ppermute | solution.py:20
  49.5 3.1 %collective-permute-done.15 = f32[3,4,256]{2,1,0:T(4,128)S(1)} collective-permute-done((f32[3,4,256]{2,1,0:T(4,128)S(1)}, f32[3,4,256]{2,1,0:T(4,128)S(1)}, u32[]{:S(2)}, u32[]{:S(2)}) %collective-permute-start.15) | collective-permute-done | bytes 12320 | tf_op jit(solution)/shard_map/ppermute | solution.py:20
  52.6 1.5 %collective-permute-done.14 = f32[3,4,256]{2,1,0:T(4,128)S(1)} collective-permute-done((f32[3,4,256]{2,1,0:T(4,128)S(1)}, f32[3,4,256]{2,1,0:T(4,128)S(1)}, u32[]{:S(2)}, u32[]{:S(2)}) %collective-permute-start.14) | collective-permute-done | bytes 12320 | tf_op jit(solution)/shard_map/ppermute | solution.py:20
  54.1 2.2 %collective-permute-done.13 = f32[3,4,256]{2,1,0:T(4,128)S(1)} collective-permute-done((f32[3,4,256]{2,1,0:T(4,128)S(1)}, f32[3,4,256]{2,1,0:T(4,128)S(1)}, u32[]{:S(2)}, u32[]{:S(2)}) %collective-permute-start.13) | collective-permute-done | bytes 12320 | tf_op jit(solution)/shard_map/ppermute | solution.py:20
  56.5 1.1 %collective-permute-done.16 = f32[4,8,256]{2,1,0:T(8,128)S(1)} collective-permute-done((f32[4,8,256]{2,1,0:T(8,128)S(1)}, f32[4,8,256]{2,1,0:T(8,128)S(1)}, u32[]{:S(2)}, u32[]{:S(2)}) %collective-permute-start.16) | collective-permute-done | bytes 32800 | tf_op jit(solution)/shard_map/ppermute | solution.py:20
  57.7 2.1 %text_grads_1.1 = (bf16[256,2048]{1,0:T(8,128)(2,1)S(1)}, f32[264,512]{1,0:T(8,128)S(1)}) custom-call(f32[1,1]{1,0:T(1,128)} %bitcast.324.scale_ref, f32[1,1]{1,0:T(1,128)} %mul.147.coef_ref, s32[1,2]{1,0:T(1,128)S(1)} %add_bitcast_fusion.place_ref, bf16[1024,512]{1,0:T(8,128)(2,1)S(1)} %get-tuple-element.43.refs_0_, ...), custom_call_target="tpu_custom_call" | custom-call | flops 21474836480 | tf_op jit(solution)/shard_map/text_grads_1/pallas_call | solution.py:306
  59.9 6.6 %text_grads_3.1 = (bf16[256,2048]{1,0:T(8,128)(2,1)S(1)}, bf16[256,2048]{1,0:T(8,128)(2,1)S(1)}, bf16[256,2048]{1,0:T(8,128)(2,1)S(1)}, f32[264,512]{1,0:T(8,128...) custom-call(f32[1,1]{1,0:T(1,128)} %bitcast.325.scale_ref, ...), custom_call_target="tpu_custom_call" | custom-call | flops 64424509440 | tf_op jit(solution)/shard_map/text_grads_3/pallas_call | solution.py:306
  66.7 1.9 %collective-permute-start.22 = (f32[264,512]{1,0:T(8,128)S(1)}, f32[264,512]{1,0:T(8,128)S(1)}, u32[]{:S(2)}, u32[]{:S(2)}) collective-permute-start(f32[264,512]{1,0:T(8,128)S(1)} %get-tuple-element.56), channel_id=1, source_target_pairs={{0,8},{8,0},{16,24},{24,16},{1,9},{9,1},{17,25},{25,17},{2,10},{10... | collective-permute-start | bytes 1622024 | tf_op jit(solution)/shard_map/ppermute | solution.py:20
  68.6 6.4 %collective-permute-done.17 = f32[264,512]{1,0:T(8,128)S(1)} collective-permute-done((f32[264,512]{1,0:T(8,128)S(1)}, f32[264,512]{1,0:T(8,128)S(1)}, u32[]{:S(2)}, u32[]{:S(2)}) %collective-permute-start.17) | collective-permute-done | bytes 540704 | tf_op jit(solution)/shard_map/ppermute | solution.py:20
  75.1 0.9 collective-permute-start.23
  76.0 1.9 %image_grads.1 = f32[4,264,512]{2,1,0:T(8,128)S(1)} custom-call(f32[1,1]{1,0:T(1,128)} %bitcast.326.scale_ref, f32[4,256]{1,0:T(4,128)S(1)} %fusion.44.refs_5_.extra, bf16[256,2048]{1,0:T(8,128)(2,1)S(1)} %get-tuple-element.49.refs_0_, bf16[256,2048]{1,0:T(8,128)(2,1)S(1)} %get-tuple-element.50.refs_1_, bf16[256,2048]{1,0:T(8,128)(2,1)S(1)} %get-tuple-element.51.refs_2_, ...), custom_call_target="tpu_custom_call" | custom-call | flops 21474836480 | tf_op jit(solution)/shard_map/image_grads/pallas_call | solution.py:341
  78.3 2.6 %collective-permute-start.21 = (f32[264,512]{1,0:T(8,128)S(1)}, f32[264,512]{1,0:T(8,128)S(1)}, u32[]{:S(2)}, u32[]{:S(2)}) collective-permute-start(f32[264,512]{1,0:T(8,128)S(1)} %get-tuple-element.59), channel_id=1, source_target_pairs={{0,6},{1,7},{2,4},{3,5},{4,2},{5,3},{6,0},{7,1},{8,14},{9,15},{10,... | collective-permute-start | bytes 1622024 | tf_op jit(solution)/shard_map/ppermute | solution.py:20
  81.9 13.2 %collective-permute-done.22 = f32[264,512]{1,0:T(8,128)S(1)} collective-permute-done((f32[264,512]{1,0:T(8,128)S(1)}, f32[264,512]{1,0:T(8,128)S(1)}, u32[]{:S(2)}, u32[]{:S(2)}) %collective-permute-start.22) | collective-permute-done | bytes 540704 | tf_op jit(solution)/shard_map/ppermute | solution.py:20
  95.1 5.4 %collective-permute-done.23 = f32[1,264,512]{2,1,0:T(8,128)S(1)} collective-permute-done((f32[1,264,512]{2,1,0:T(8,128)S(1)}, f32[1,264,512]{2,1,0:T(8,128)S(1)}, u32[]{:S(2)}, u32[]{:S(2)}) %collective-permute-start.23) | collective-permute-done | bytes 540704 | tf_op jit(solution)/shard_map/ppermute | solution.py:20
  100.6 0.8 slice.57
  101.4 0.6 slice_reduce_fusion.1
  102.0 1.9 %collective-permute-done.20 = f32[264,512]{1,0:T(8,128)S(1)} collective-permute-done((f32[264,512]{1,0:T(8,128)S(1)}, f32[264,512]{1,0:T(8,128)S(1)}, u32[]{:S(2)}, u32[]{:S(2)}) %collective-permute-start.20) | collective-permute-done | bytes 540704 | tf_op jit(solution)/shard_map/ppermute | solution.py:20
  104.4 0.6 slice_reduce_fusion
  105.0 0.8 slice.56
  (39 shorter events, 4.6 us)
Async XLA Ops:
  1.7 11.1 %collective-permute-start.6 = (bf16[256,512]{1,0:T(8,128)(2,1)S(1)}, bf16[256,512]{1,0:T(8,128)(2,1)S(1)}, u32[]{:S(2)}, u32[]{:S(2)}) collective-permute-start(bf16[256,512]{1,0:T(8,128)(2,1)S(1)} %convert_element_type.6.refs_0_), channel_id=1, source_target_pairs={{0,6},{1,7},{2,4},{3,5},{4,2},{5,3},{6,0},{7,1},{8,14},{9,15},{10,... | collective-permute-start | bytes 786440 | tf_op jit(solution)/shard_map/ppermute | solution.py:20
  5.7 11.9 %collective-permute-start.5 = (bf16[256,512]{1,0:T(8,128)(2,1)S(1)}, bf16[256,512]{1,0:T(8,128)(2,1)S(1)}, u32[]{:S(2)}, u32[]{:S(2)}) collective-permute-start(bf16[256,512]{1,0:T(8,128)(2,1)S(1)} %convert_element_type.6.refs_0_), channel_id=1, source_target_pairs={{0,4},{1,5},{2,6},{3,7},{4,0},{5,1},{6,2},{7,3},{8,12},{9,13},{10,... | collective-permute-start | bytes 786440 | tf_op jit(solution)/shard_map/ppermute | solution.py:20
  6.2 11.7 %collective-permute-start.4 = (bf16[256,512]{1,0:T(8,128)(2,1)S(1)}, bf16[256,512]{1,0:T(8,128)(2,1)S(1)}, u32[]{:S(2)}, u32[]{:S(2)}) collective-permute-start(bf16[256,512]{1,0:T(8,128)(2,1)S(1)} %convert_element_type.6.refs_0_), channel_id=1, source_target_pairs={{0,2},{1,3},{2,0},{3,1},{4,6},{5,7},{6,4},{7,5},{8,10},{9,11},{10,... | collective-permute-start | bytes 786440 | tf_op jit(solution)/shard_map/ppermute | solution.py:20
  7.4 11.3 %collective-permute-start.3 = (bf16[256,512]{1,0:T(8,128)(2,1)S(1)}, bf16[256,512]{1,0:T(8,128)(2,1)S(1)}, u32[]{:S(2)}, u32[]{:S(2)}) collective-permute-start(bf16[256,512]{1,0:T(8,128)(2,1)S(1)} %convert_element_type.7.refs_4_.refs_8_), channel_id=1, source_target_pairs={{0,24},{8,16},{16,8},{24,0},{1,25},{9,17},{17,9},{25,1},{2,26},{10... | collective-permute-start | bytes 786440 | tf_op jit(solution)/shard_map/ppermute | solution.py:20
  11.5 21.5 %collective-permute-start.2 = (bf16[256,512]{1,0:T(8,128)(2,1)S(1)}, bf16[256,512]{1,0:T(8,128)(2,1)S(1)}, u32[]{:S(2)}, u32[]{:S(2)}) collective-permute-start(bf16[256,512]{1,0:T(8,128)(2,1)S(1)} %convert_element_type.7.refs_4_.refs_8_), channel_id=1, source_target_pairs={{0,16},{8,24},{16,0},{24,8},{1,17},{9,25},{17,1},{25,9},{2,18},{10... | collective-permute-start | bytes 786440 | tf_op jit(solution)/shard_map/ppermute | solution.py:20
  12.8 20.1 %collective-permute-start.1 = (bf16[256,512]{1,0:T(8,128)(2,1)S(1)}, bf16[256,512]{1,0:T(8,128)(2,1)S(1)}, u32[]{:S(2)}, u32[]{:S(2)}) collective-permute-start(bf16[256,512]{1,0:T(8,128)(2,1)S(1)} %convert_element_type.7.refs_4_.refs_8_), channel_id=1, source_target_pairs={{0,8},{8,0},{16,24},{24,16},{1,9},{9,1},{17,25},{25,17},{2,10},{10... | collective-permute-start | bytes 786440 | tf_op jit(solution)/shard_map/ppermute | solution.py:20
  17.6 20.8 %collective-permute-start = (bf16[256,512]{1,0:T(8,128)(2,1)S(1)}, bf16[256,512]{1,0:T(8,128)(2,1)S(1)}, u32[]{:S(2)}, u32[]{:S(2)}) collective-permute-start(bf16[256,512]{1,0:T(8,128)(2,1)S(1)} %convert_element_type.6.refs_0_), channel_id=1, source_target_pairs={{0,1},{1,0},{2,3},{3,2},{4,5},{5,4},{6,7},{7,6},{8,9},{9,8},{10,11... | collective-permute-start | bytes 786440 | tf_op jit(solution)/shard_map/ppermute | solution.py:20
  32.9 5.5 %collective-permute-start.7 = (bf16[256,512]{1,0:T(8,128)(2,1)S(1)}, bf16[256,512]{1,0:T(8,128)(2,1)S(1)}, u32[]{:S(2)}, u32[]{:S(2)}) collective-permute-start(bf16[256,512]{1,0:T(8,128)(2,1)S(1)} %collective-permute-done.4.refs_1_), channel_id=1, source_target_pairs={{0,1},{1,0},{2,3},{3,2},{4,5},{5,4},{6,7},{7,6},{8,9},{9,8},{10,11... | collective-permute-start | bytes 786440 | tf_op jit(solution)/shard_map/ppermute | solution.py:20
  32.9 5.5 %collective-permute-start.8 = (bf16[256,512]{1,0:T(8,128)(2,1)S(1)}, bf16[256,512]{1,0:T(8,128)(2,1)S(1)}, u32[]{:S(2)}, u32[]{:S(2)}) collective-permute-start(bf16[256,512]{1,0:T(8,128)(2,1)S(1)} %collective-permute-done.5.refs_2_), channel_id=1, source_target_pairs={{0,1},{1,0},{2,3},{3,2},{4,5},{5,4},{6,7},{7,6},{8,9},{9,8},{10,11... | collective-permute-start | bytes 786440 | tf_op jit(solution)/shard_map/ppermute | solution.py:20
  33.4 5.0 %collective-permute-start.9 = (bf16[256,512]{1,0:T(8,128)(2,1)S(1)}, bf16[256,512]{1,0:T(8,128)(2,1)S(1)}, u32[]{:S(2)}, u32[]{:S(2)}) collective-permute-start(bf16[256,512]{1,0:T(8,128)(2,1)S(1)} %collective-permute-done.6.refs_3_), channel_id=1, source_target_pairs={{0,1},{1,0},{2,3},{3,2},{4,5},{5,4},{6,7},{7,6},{8,9},{9,8},{10,11... | collective-permute-start | bytes 786440 | tf_op jit(solution)/shard_map/ppermute | solution.py:20
  43.5 12.8 %collective-permute-start.12 = (f32[4,8,256]{2,1,0:T(8,128)S(1)}, f32[4,8,256]{2,1,0:T(8,128)S(1)}, u32[]{:S(2)}, u32[]{:S(2)}) collective-permute-start(f32[4,8,256]{2,1,0:T(8,128)S(1)} %get-tuple-element.39), channel_id=1, source_target_pairs={{0,6},{1,7},{2,4},{3,5},{4,2},{5,3},{6,0},{7,1},{8,14},{9,15},{10,... | collective-permute-start | bytes 98312 | tf_op jit(solution)/shard_map/ppermute | solution.py:20
  46.0 10.4 %collective-permute-start.11 = (f32[4,8,256]{2,1,0:T(8,128)S(1)}, f32[4,8,256]{2,1,0:T(8,128)S(1)}, u32[]{:S(2)}, u32[]{:S(2)}) collective-permute-start(f32[4,8,256]{2,1,0:T(8,128)S(1)} %get-tuple-element.39), channel_id=1, source_target_pairs={{0,4},{1,5},{2,6},{3,7},{4,0},{5,1},{6,2},{7,3},{8,12},{9,13},{10,... | collective-permute-start | bytes 98312 | tf_op jit(solution)/shard_map/ppermute | solution.py:20
  46.5 9.9 %collective-permute-start.10 = (f32[4,8,256]{2,1,0:T(8,128)S(1)}, f32[4,8,256]{2,1,0:T(8,128)S(1)}, u32[]{:S(2)}, u32[]{:S(2)}) collective-permute-start(f32[4,8,256]{2,1,0:T(8,128)S(1)} %get-tuple-element.39), channel_id=1, source_target_pairs={{0,2},{1,3},{2,0},{3,1},{4,6},{5,7},{6,4},{7,5},{8,10},{9,11},{10,... | collective-permute-start | bytes 98312 | tf_op jit(solution)/shard_map/ppermute | solution.py:20
  47.1 5.5 %collective-permute-start.15 = (f32[3,4,256]{2,1,0:T(4,128)S(1)}, f32[3,4,256]{2,1,0:T(4,128)S(1)}, u32[]{:S(2)}, u32[]{:S(2)}) collective-permute-start(f32[3,4,256]{2,1,0:T(4,128)S(1)} %get-tuple-element.38), channel_id=1, source_target_pairs={{0,24},{8,16},{16,8},{24,0},{1,25},{9,17},{17,9},{25,1},{2,26},{10... | collective-permute-start | bytes 36872 | tf_op jit(solution)/shard_map/ppermute | solution.py:20
  49.5 4.6 %collective-permute-start.14 = (f32[3,4,256]{2,1,0:T(4,128)S(1)}, f32[3,4,256]{2,1,0:T(4,128)S(1)}, u32[]{:S(2)}, u32[]{:S(2)}) collective-permute-start(f32[3,4,256]{2,1,0:T(4,128)S(1)} %get-tuple-element.38), channel_id=1, source_target_pairs={{0,16},{8,24},{16,0},{24,8},{1,17},{9,25},{17,1},{25,9},{2,18},{10... | collective-permute-start | bytes 36872 | tf_op jit(solution)/shard_map/ppermute | solution.py:20
  52.6 3.7 %collective-permute-start.13 = (f32[3,4,256]{2,1,0:T(4,128)S(1)}, f32[3,4,256]{2,1,0:T(4,128)S(1)}, u32[]{:S(2)}, u32[]{:S(2)}) collective-permute-start(f32[3,4,256]{2,1,0:T(4,128)S(1)} %get-tuple-element.38), channel_id=1, source_target_pairs={{0,8},{8,0},{16,24},{24,16},{1,9},{9,1},{17,25},{25,17},{2,10},{10... | collective-permute-start | bytes 36872 | tf_op jit(solution)/shard_map/ppermute | solution.py:20
  56.4 1.3 %collective-permute-start.16 = (f32[4,8,256]{2,1,0:T(8,128)S(1)}, f32[4,8,256]{2,1,0:T(8,128)S(1)}, u32[]{:S(2)}, u32[]{:S(2)}) collective-permute-start(f32[4,8,256]{2,1,0:T(8,128)S(1)} %pad_maximum_fusion), channel_id=1, source_target_pairs={{0,1},{1,0},{2,3},{3,2},{4,5},{5,4},{6,7},{7,6},{8,9},{9,8},{10,11... | collective-permute-start | bytes 98312 | tf_op jit(solution)/shard_map/ppermute | solution.py:20
  59.8 15.2 %collective-permute-start.17 = (f32[264,512]{1,0:T(8,128)S(1)}, f32[264,512]{1,0:T(8,128)S(1)}, u32[]{:S(2)}, u32[]{:S(2)}) collective-permute-start(f32[264,512]{1,0:T(8,128)S(1)} %get-tuple-element.53), channel_id=1, source_target_pairs={{0,8},{8,0},{16,24},{24,16},{1,9},{9,1},{17,25},{25,17},{2,10},{10... | collective-permute-start | bytes 1622024 | tf_op jit(solution)/shard_map/ppermute | solution.py:20
  66.5 11.5 %collective-permute-start.18 = (f32[4,264,512]{2,1,0:T(8,128)S(1)}, f32[4,264,512]{2,1,0:T(8,128)S(1)}, u32[]{:S(2)}, u32[]{:S(2)}) collective-permute-start(f32[4,264,512]{2,1,0:T(8,128)S(1)} %get-tuple-element.54), channel_id=1, source_target_pairs={{0,1},{1,0},{2,3},{3,2},{4,5},{5,4},{6,7},{7,6},{8,9},{9,8},{10,11... | collective-permute-start | bytes 6488072 | tf_op jit(solution)/shard_map/ppermute | solution.py:20
  66.7 28.4 %collective-permute-start.22 = (f32[264,512]{1,0:T(8,128)S(1)}, f32[264,512]{1,0:T(8,128)S(1)}, u32[]{:S(2)}, u32[]{:S(2)}) collective-permute-start(f32[264,512]{1,0:T(8,128)S(1)} %get-tuple-element.56), channel_id=1, source_target_pairs={{0,8},{8,0},{16,24},{24,16},{1,9},{9,1},{17,25},{25,17},{2,10},{10... | collective-permute-start | bytes 1622024 | tf_op jit(solution)/shard_map/ppermute | solution.py:20
  75.1 25.3 %collective-permute-start.23 = (f32[1,264,512]{2,1,0:T(8,128)S(1)}, f32[1,264,512]{2,1,0:T(8,128)S(1)}, u32[]{:S(2)}, u32[]{:S(2)}) collective-permute-start(f32[1,264,512]{2,1,0:T(8,128)S(1)} %bitcast.327), channel_id=1, source_target_pairs={{0,16},{8,24},{16,0},{24,8},{1,17},{9,25},{17,1},{25,9},{2,18},{10... | collective-permute-start | bytes 1622024 | tf_op jit(solution)/shard_map/ppermute | solution.py:20
  78.3 23.7 %collective-permute-start.21 = (f32[264,512]{1,0:T(8,128)S(1)}, f32[264,512]{1,0:T(8,128)S(1)}, u32[]{:S(2)}, u32[]{:S(2)}) collective-permute-start(f32[264,512]{1,0:T(8,128)S(1)} %get-tuple-element.59), channel_id=1, source_target_pairs={{0,6},{1,7},{2,4},{3,5},{4,2},{5,3},{6,0},{7,1},{8,14},{9,15},{10,... | collective-permute-start | bytes 1622024 | tf_op jit(solution)/shard_map/ppermute | solution.py:20
  80.9 23.0 %collective-permute-start.20 = (f32[264,512]{1,0:T(8,128)S(1)}, f32[264,512]{1,0:T(8,128)S(1)}, u32[]{:S(2)}, u32[]{:S(2)}) collective-permute-start(f32[264,512]{1,0:T(8,128)S(1)} %get-tuple-element.60), channel_id=1, source_target_pairs={{0,4},{1,5},{2,6},{3,7},{4,0},{5,1},{6,2},{7,3},{8,12},{9,13},{10,... | collective-permute-start | bytes 1622024 | tf_op jit(solution)/shard_map/ppermute | solution.py:20
  81.4 22.7 %collective-permute-start.19 = (f32[264,512]{1,0:T(8,128)S(1)}, f32[264,512]{1,0:T(8,128)S(1)}, u32[]{:S(2)}, u32[]{:S(2)}) collective-permute-start(f32[264,512]{1,0:T(8,128)S(1)} %get-tuple-element.61), channel_id=1, source_target_pairs={{0,2},{1,3},{2,0},{3,1},{4,6},{5,7},{6,4},{7,5},{8,10},{9,11},{10,... | collective-permute-start | bytes 1622024 | tf_op jit(solution)/shard_map/ppermute | solution.py:20

commit v5 on v4

--- a/solution.py
+++ b/solution.py
@@ -192,22 +192,168 @@
 
 def exchanged(row_parts, col_parts, n_col, n_row):
     rows = [swap(row_parts, "col", n_col, q) for q in range(2, n_col, 2)]
-    cols = [swap(col_parts, "row", n_row, q) for q in range(1, n_row)]
+    cols = swap(col_parts, "row", n_row, 1)
     rows, cols = lax.optimization_barrier((rows, cols))
-    cols = by_pairs([list(x) for x in (col_parts, *cols)], merged)
     rows = by_pairs([list(x) for x in (row_parts, *rows)], merged)
+    cols = merged(list(col_parts), list(cols))
+    for b in range(1, n_row.bit_length() - 1):
+        cols = merged(cols, list(swap(jnp.stack(cols), "row", n_row, 1 << b)))
     rows = merged(rows, list(swap(jnp.stack(rows), "col", n_col, 1)))
     return *lse_and_mean(rows), *lse_and_mean(cols)
 
 
+LEVELS = 32000
+LOW = 128
+BIAS = 125
+EXTRA = 8
+MORE = 32
+
+
 def put_extra(out, extra_ref):
     n, width = extra_ref.shape
-    rows = min(n, 8)
+    rows = min(n, EXTRA)
     out[...] = jnp.zeros(out.shape, out.dtype)
     out[:rows, :width] = sum(extra_ref[i : i + rows, :] for i in range(0, n, rows))
 
 
-def text_block(text, t, halves, row_lse, col_lse, place_ref, scale_ref, coef_ref, extra, grad_ref, out_ref):
+def power(k):
+    return jnp.exp2(k).astype(jnp.bfloat16).astype(jnp.float32)
+
+
+def encode(out, value, extra):
+    size, width = value.shape
+    top = jnp.maximum(jnp.max(jnp.abs(value), axis=1, keepdims=True), 1e-30)
+    k = jnp.ceil(jnp.log2(top))
+    whole = jnp.floor(jnp.abs(value) * (power(-k) * (LEVELS - 1)) + 0.5)
+    high = jnp.floor(whole * (1 / LOW))
+    code = (1.0 + (whole - LOW * high) * (1 / LOW)) * jnp.exp2(high - BIAS)
+    out[:size, :] = jnp.where(value < 0, -code, code).astype(jnp.bfloat16)
+    half = width // 2
+    first = extra[:, :half].astype(jnp.bfloat16)
+    rest = extra[:, :half] - first.astype(jnp.float32)
+    second = rest.astype(jnp.bfloat16)
+    third = (rest - second.astype(jnp.float32)).astype(jnp.bfloat16)
+    zeros = jnp.zeros((EXTRA, half), jnp.bfloat16)
+    out[size : size + 2 * EXTRA, :half] = jnp.concatenate([first, second], axis=0)
+    out[size : size + 2 * EXTRA, half:] = jnp.concatenate([third, zeros], axis=0)
+    powers = jnp.broadcast_to(power(k), (size, LANES)).T
+    out[size + 2 * EXTRA :, :] = jnp.zeros((MORE - 2 * EXTRA, width), jnp.bfloat16)
+    out[size + 2 * EXTRA :, :size] = powers[: MORE - 2 * EXTRA, :].astype(jnp.bfloat16)
+
+
+def decode_powers(code, size):
+    powers = code[size + 2 * EXTRA :, :size].astype(jnp.float32)
+    return jnp.broadcast_to(powers[0:1, :], (LANES, size)).T * (1 / (LEVELS - 1))
+
+
+def decode(code, powers):
+    lanes = []
+    for lane in range(0, code.shape[1], LANES):
+        c = code[:, lane : lane + LANES].astype(jnp.float32)
+        a = jnp.abs(c)
+        high = jnp.floor(jnp.log2(a))
+        whole = LOW * (high + (BIAS - 1) + a * jnp.exp2(-high))
+        lanes.append(jnp.where(c < 0, -whole, whole) * powers)
+    return jnp.concatenate(lanes, axis=1)
+
+
+def decode_extra(code, size):
+    half = code.shape[1] // 2
+    left = code[size : size + 2 * EXTRA, :half].astype(jnp.float32)
+    right = code[size : size + 2 * EXTRA, half:].astype(jnp.float32)
+    return left[:EXTRA] + left[EXTRA:] + right[:EXTRA]
+
+
+def pack_text_kernel(n, base, *refs):
+    codes, out, total = refs[:n], refs[n], refs[n + 1]
+    size = base.shape[0] - EXTRA
+    total[...] = base[:size, :]
+    extra = base[size:, :]
+    half = base.shape[1] // 2
+    more = extra[:, :half]
+    for code in codes:
+        total[...] += decode(code[:size, :], decode_powers(code, size))
+        more = more + decode_extra(code, size)
+    encode(out, total[...], more)
+
+
+def pack_text(base, codes):
+    size, width = base.shape[0] - EXTRA, base.shape[1]
+    vmem = pl.BlockSpec(memory_space=VMEM)
+    return pl.pallas_call(
+        functools.partial(pack_text_kernel, len(codes)),
+        out_shape=jax.ShapeDtypeStruct((size + MORE, width), jnp.bfloat16),
+        in_specs=[vmem] * (1 + len(codes)),
+        out_specs=vmem,
+        scratch_shapes=[VMEM((size, width), jnp.float32)],
+        name="pack_text",
+    )(base, *codes)
+
+
+def pack_images_kernel(near, far, own, *outs):
+    size = near.shape[1] - EXTRA
+    own[...] = near[0] + far[0]
+    for j, out in enumerate(outs, 1):
+        total = near[j] + far[j]
+        encode(out, total[:size], total[size:])
+
+
+def pack_images(near, far):
+    n, rows, width = near.shape
+    vmem = pl.BlockSpec(memory_space=VMEM)
+    code = jax.ShapeDtypeStruct((rows - EXTRA + MORE, width), jnp.bfloat16)
+    own, *codes = pl.pallas_call(
+        pack_images_kernel,
+        out_shape=(jax.ShapeDtypeStruct((rows, width), jnp.float32),) + (code,) * (n - 1),
+        in_specs=[vmem] * 2,
+        out_specs=(vmem,) * n,
+        name="pack_images",
+    )(near, far)
+    return own, codes
+
+
+def total_kernel(n, in_order, steps, base, *refs):
+    codes, before, out, extra, powers = refs[:n], refs[n:-3], *refs[-3:]
+    i = pl.program_id(0)
+    size, width = base.shape[0] - EXTRA, base.shape[1]
+    combine = functools.partial(functools.reduce, jnp.add) if in_order else by_pairs_added
+
+    @pl.when(i == 0)
+    def _():
+        for c, code in enumerate(codes):
+            powers[c] = decode_powers(code, size)
+        more = combine([base[size:, : width // 2]] + [decode_extra(code, size) for code in codes])
+        extra[...] = sum([b[...] for b in before], more)
+
+    part = pl.ds(pl.multiple_of(i * (size // steps), size // steps), size // steps)
+    out[...] = combine(
+        [base[part, :]] + [decode(code[part, :], powers[c, part, :]) for c, code in enumerate(codes)]
+    )
+
+
+def by_pairs_added(blocks):
+    return by_pairs(blocks, jnp.add)
+
+
+def total_of(base, codes, in_order, before, name):
+    size, width = base.shape[0] - EXTRA, base.shape[1]
+    vmem = pl.BlockSpec(memory_space=VMEM)
+    steps = 4
+    return pl.pallas_call(
+        functools.partial(total_kernel, len(codes), in_order, steps),
+        grid=(steps,),
+        out_shape=(
+            jax.ShapeDtypeStruct((size, width), jnp.float32),
+            jax.ShapeDtypeStruct((EXTRA, width // 2), jnp.float32),
+        ),
+        in_specs=[vmem] * (1 + len(codes) + len(before)),
+        out_specs=(pl.BlockSpec((size // steps, width), lambda i: (i, 0)), vmem),
+        scratch_shapes=[VMEM((len(codes), size, LANES), jnp.float32)],
+        name=name,
+    )(base, *codes, *before)
+
+
+def text_block(text, t, halves, row_lse, col_lse, place_ref, scale_ref, coef_ref, extra, grad_ref, out_ref, total):
     coef = coef_ref[0, 0]
     r_place, c_place = place_ref[0, 0], place_ref[0, 1]
     half, width = halves[0].shape
@@ -241,11 +387,15 @@
             return carry
 
         lax.fori_loop(0, half // block, one, 0, unroll=4)
-    out_ref[:size, :] = scale_ref[0, 0] * (
+    total[:size, :] = scale_ref[0, 0] * (
         jnp.dot(grad_ref[:, :half], halves[0][...], preferred_element_type=jnp.float32)
         + jnp.dot(grad_ref[:, half:], halves[1][...], preferred_element_type=jnp.float32)
     )
-    put_extra(out_ref.at[size:, :], extra)
+    put_extra(total.at[size:, :], extra)
+    if t & 1:
+        encode(out_ref, total[:size, :], total[size:, :])
+    else:
+        out_ref[...] = total[...]
 
 
 def image_block(grads, texts, at, block, scale):
@@ -269,7 +419,7 @@
     grads, outs = rest[:n], rest[n : 2 * n]
     for i, t in enumerate(order):
         text_block(
-            texts[i], t, (even, odd), row_lse, col_lse, place_ref, scale_ref, coef_ref, row_extra, grads[i], outs[i]
+            texts[i], t, (even, odd), row_lse, col_lse, place_ref, scale_ref, coef_ref, row_extra, grads[i], outs[i], rest[-1]
         )
     if n_done:
         far_ref = rest[2 * n]
@@ -297,10 +447,15 @@
     smem = pl.BlockSpec(memory_space=SMEM)
     out_shape = (
         [jax.ShapeDtypeStruct((block, 2 * half), jnp.bfloat16)] * n
-        + [jax.ShapeDtypeStruct((block + 8, width), jnp.float32)] * n
+        + [
+            jax.ShapeDtypeStruct((block + MORE, width), jnp.bfloat16)
+            if t & 1
+            else jax.ShapeDtypeStruct((block + EXTRA, width), jnp.float32)
+            for t in order
+        ]
     )
     if done:
-        out_shape.append(jax.ShapeDtypeStruct((half // block, block + 8, width), jnp.float32))
+        out_shape.append(jax.ShapeDtypeStruct((half // block, block + EXTRA, width), jnp.float32))
     operands = [even, odd, row_lse, col_lse, row_extra, col_extra, *[texts[t] for t in order]]
     operands += [done[t] for t in done] + [texts[t] for t in done]
     outs = pl.pallas_call(
@@ -308,6 +463,7 @@
         out_shape=tuple(out_shape),
         in_specs=[smem] * 3 + [vmem] * len(operands),
         out_specs=(vmem,) * len(out_shape),
+        scratch_shapes=[VMEM((block + EXTRA, width), jnp.float32)],
         compiler_params=pltpu.CompilerParams(vmem_limit_bytes=12 * 2**20),
         cost_estimate=pl.CostEstimate(
             flops=FLOPS * 4 * n * block * 2 * half * width, bytes_accessed=0, transcendentals=0
@@ -340,7 +496,7 @@
     vmem = pl.BlockSpec(memory_space=VMEM)
     return pl.pallas_call(
         functools.partial(image_kernel, n_text, block),
-        out_shape=jax.ShapeDtypeStruct((n, block + 8, width), jnp.float32),
+        out_shape=jax.ShapeDtypeStruct((n, block + EXTRA, width), jnp.float32),
         in_specs=[pl.BlockSpec(memory_space=SMEM)]
         + [vmem] * (2 * n_text + 1)
         + [pl.BlockSpec(memory_space=pl.ANY)] * len(after),
@@ -351,20 +507,6 @@
         ),
         name="image_grads",
     )(scale, extra, *grads, *texts, *after)
-
-
-def halve(blocks, axis, n, bits):
-    for bit in bits:
-        far = sorted(q for q in blocks if q & bit)
-        sent = swap(jnp.stack([blocks[q] for q in far]), axis, n, bit)
-        blocks = {q ^ bit: blocks[q ^ bit] + sent[i] for i, q in enumerate(far)}
-    return blocks[0]
-
-
-def scatter_images(near, far, axis, n):
-    sent = swap(far, axis, n, 1)
-    sums = [near[j] + sent[j] for j in range(n // 2)]
-    return by_pairs([sums[0]] + [swap(sums[j], axis, n, 2 * j) for j in range(1, n // 2)], jnp.add)
 
 
 def on_device(n_row, n_col, image_embeds, text_embeds, logit_scale):
@@ -386,16 +528,23 @@
     more, more_parts, far = text_grads(*held, list(range(last))[::-1], grads)
     grads |= more
     parts |= more_parts
-    sums = {last ^ 1: parts[last ^ 1] + received}
-    near = image_grads(
-        scale, col_extra, [grads[t] for t in range(n_row)], texts, [sums[last ^ 1]]
-    )
+    codes = {q: [] for q in range(0, n_row, 2)}
+    codes[last ^ 1].append(received)
+    after = [pack_text(parts[last ^ 1], codes[last ^ 1])] if n_row > 2 else [received]
+    near = image_grads(scale, col_extra, [grads[t] for t in range(n_row)], texts, after)
     for q in range(1, last, 2):
-        sums[q ^ 1] = parts[q ^ 1] + swap(parts[q], "row", n_row, 1)
-    text_sum = halve(sums, "row", n_row, [1 << b for b in range(1, n_row.bit_length() - 1)])
-    image_sum = scatter_images(near, far, "col", n_col)
-    grad_scale = (jnp.sum(text_sum[block:]) + jnp.sum(image_sum[block:])) / coef[0, 0]
-    return image_sum[:block], text_sum[:block], grad_scale
+        codes[q ^ 1].append(swap(parts[q], "row", n_row, 1))
+    for b in range(1, n_row.bit_length() - 1):
+        for q in [q for q in codes if q & (1 << b)]:
+            code = after[0] if (b, q) == (1, last ^ 1) else pack_text(parts[q], codes[q])
+            codes[q ^ (1 << b)].append(swap(code, "row", n_row, 1 << b))
+            del codes[q]
+    grad_text, text_extra = total_of(parts[0], codes[0], True, [], "grad_text")
+
+    own, others = pack_images(near, swap(far, "col", n_col, 1))
+    others = [swap(code, "col", n_col, 2 * j) for j, code in enumerate(others, 1)]
+    grad_image, extra = total_of(own, others, False, [text_extra], "grad_image")
+    return grad_image, grad_text, jnp.sum(extra) / coef[0, 0]
 
 
 def solution(mesh):

time: 108 us -> 114 us (1.056)
  waiting for transfers between devices: 53.5 us -> 36.2 us
  Pallas kernels: 20.6 us -> 34.9 us
  local copies, waits for them, and re-layouts: 1.66 us -> 13.4 us
  starting transfers between devices: 24 us -> 22.4 us
    ppermute x24 -> x23, waiting for transfers between devices: 53.5 us -> 36.2 us  [swap(): return lax.ppermute(x, axis, [(i, i ^ q) for i in range(n)])]
    pallas_call x0 -> x4, Pallas kernels: none -> 13.6 us  [the longest x2 6.53 us: total_of(): pl.pallas_call(functools.partial(total_kernel, len(codes), in_order, step...]
    unnamed x0 -> x32, local copies, waits for them, and re-layouts: none -> 13.4 us
    slice x2 -> x0, local copies, waits for them, and re-layouts: 1.66 us -> none  [on_device(): return (image_sum[:block], text_sum[:block], grad_scale)]
    ppermute x24 -> x23, starting transfers between devices: 24 us -> 22.4 us  [swap(): return lax.ppermute(x, axis, [(i, i ^ q) for i in range(n)])]
  transfers between devices with their start and end apart: 24 -> 23, of which waited for: 14 -> 9; matrix products, arithmetic and copies ran while one was open for 3% -> 1% of each run, Pallas kernels for 12% -> 21%
where the time goes in v5:
time: 114 us
  waiting for transfers between devices  36.2 us (32%)
  Pallas kernels  34.9 us (31%)
  starting transfers between devices  22.4 us (20%)
  local copies, waits for them, and re-layouts  13.4 us (12%)
  other arithmetic  3.73 us (3%)
  between operations  3.25 us (3%)
    ppermute x23, waiting for transfers between devices, swap(): return lax.ppermute(x, axis, [(i, i ^ q) for i in range(n)])  36.2 us
    ppermute x23, starting transfers between devices, swap(): return lax.ppermute(x, axis, [(i, i ^ q) for i in range(n)])  22.4 us
    unnamed x32, local copies, waits for them, and re-layouts  13.4 us
    pallas_call x2, Pallas kernels, stats(): pl.pallas_call(functools.partial(stats_kernel, len(texts), len(images), 1...  10 us
    pallas_call x2, Pallas kernels, text_grads(): pl.pallas_call(functools.partial(text_kernel, tuple(order), len(done), bl...  9.29 us
    pallas_call x2, Pallas kernels, total_of(): pl.pallas_call(functools.partial(total_kernel, len(codes), in_order, step...  6.53 us
    pallas_call x1, Pallas kernels, pack_images(): pl.pallas_call(pack_images_kernel, out_shape=(jax.ShapeDtypeStruct((rows,...  4.49 us
    pallas_call x1, Pallas kernels, pack_text(): pl.pallas_call(functools.partial(pack_text_kernel, len(codes)), out_shape...  2.56 us
  transfers between devices with their start and end apart: 23, of which 9 were waited for; matrix products, arithmetic and copies ran while one was open for 1% of the time, Pallas kernels for 21%

profile of v5, /device:TPU:0, one launch (start us, length us, event | category | flops | bytes accessed | tf_op | source)
XLA Modules:
  0.0 113.8 jit_solution(10642769414942031904)
XLA Ops:
  0.6 1.1 convert_element_type.6.refs_0_
  1.7 4.0 %collective-permute-start.6 = (bf16[256,512]{1,0:T(8,128)(2,1)S(1)}, bf16[256,512]{1,0:T(8,128)(2,1)S(1)}, u32[]{:S(2)}, u32[]{:S(2)}) collective-permute-start(bf16[256,512]{1,0:T(8,128)(2,1)S(1)} %convert_element_type.6.refs_0_), channel_id=1, source_target_pairs={{0,6},{1,7},{2,4},{3,5},{4,2},{5,3},{6,0},{7,1},{8,14},{9,15},{10,... | collective-permute-start | bytes 786440 | tf_op jit(solution)/shard_map/ppermute | solution.py:20
  6.3 1.1 convert_element_type.7.refs_4_.refs_8_
  7.4 4.1 %collective-permute-start.3 = (bf16[256,512]{1,0:T(8,128)(2,1)S(1)}, bf16[256,512]{1,0:T(8,128)(2,1)S(1)}, u32[]{:S(2)}, u32[]{:S(2)}) collective-permute-start(bf16[256,512]{1,0:T(8,128)(2,1)S(1)} %convert_element_type.7.refs_4_.refs_8_), channel_id=1, source_target_pairs={{0,24},{8,16},{16,8},{24,0},{1,25},{9,17},{17,9},{25,1},{2,26},{10... | collective-permute-start | bytes 786440 | tf_op jit(solution)/shard_map/ppermute | solution.py:20
  11.5 1.4 %collective-permute-done.6.refs_3_ = bf16[256,512]{1,0:T(8,128)(2,1)S(1)} collective-permute-done((bf16[256,512]{1,0:T(8,128)(2,1)S(1)}, bf16[256,512]{1,0:T(8,128)(2,1)S(1)}, u32[]{:S(2)}, u32[]{:S(2)}) %collective-permute-start.6) | collective-permute-done | bytes 262176 | tf_op jit(solution)/shard_map/ppermute | solution.py:20
  12.8 2.1 %collective-permute-start.1 = (bf16[256,512]{1,0:T(8,128)(2,1)S(1)}, bf16[256,512]{1,0:T(8,128)(2,1)S(1)}, u32[]{:S(2)}, u32[]{:S(2)}) collective-permute-start(bf16[256,512]{1,0:T(8,128)(2,1)S(1)} %convert_element_type.7.refs_4_.refs_8_), channel_id=1, source_target_pairs={{0,8},{8,0},{16,24},{24,16},{1,9},{9,1},{17,25},{25,17},{2,10},{10... | collective-permute-start | bytes 786440 | tf_op jit(solution)/shard_map/ppermute | solution.py:20
  15.7 1.9 %collective-permute-done.5.refs_2_ = bf16[256,512]{1,0:T(8,128)(2,1)S(1)} collective-permute-done((bf16[256,512]{1,0:T(8,128)(2,1)S(1)}, bf16[256,512]{1,0:T(8,128)(2,1)S(1)}, u32[]{:S(2)}, u32[]{:S(2)}) %collective-permute-start.5) | collective-permute-done | bytes 262176 | tf_op jit(solution)/shard_map/ppermute | solution.py:20
  18.7 14.2 %collective-permute-done.2.refs_6_ = bf16[256,512]{1,0:T(8,128)(2,1)S(1)} collective-permute-done((bf16[256,512]{1,0:T(8,128)(2,1)S(1)}, bf16[256,512]{1,0:T(8,128)(2,1)S(1)}, u32[]{:S(2)}, u32[]{:S(2)}) %collective-permute-start.2) | collective-permute-done | bytes 262176 | tf_op jit(solution)/shard_map/ppermute | solution.py:20
  33.4 4.9 %stats_even.1 = (f32[4,8,256]{2,1,0:T(8,128)S(1)}, f32[3,4,256]{2,1,0:T(4,128)S(1)}, bf16[1024,512]{1,0:T(8,128)(2,1)S(1)}) custom-call(f32[1,1]{1,0:T(1,128)} %mul.147.coef_ref, s32[1,2]{1,0:T(1,128)S(1)} %add_bitcast_fusion.place_ref, bf16[256,512]{1,0:T(8,128)(2,1)S(1)} %convert_element_type.6.refs_0_, ...), custom_call_target="tpu_custom_call" | custom-call | flops 21474836480 | tf_op jit(solution)/shard_map/stats_even/pallas_call | solution.py:157
  38.4 5.1 %stats_odd.1 = (f32[4,8,256]{2,1,0:T(8,128)S(1)}, f32[3,4,256]{2,1,0:T(4,128)S(1)}, bf16[1024,512]{1,0:T(8,128)(2,1)S(1)}) custom-call(f32[1,1]{1,0:T(1,128)} %mul.147.coef_ref, s32[1,2]{1,0:T(1,128)S(1)} %add_bitcast_fusion.place_ref, bf16[256,512]{1,0:T(8,128)(2,1)S(1)} %collective-permute-done.refs_0_, ...), custom_call_target="tpu_custom_call" | custom-call | flops 21474836480 | tf_op jit(solution)/shard_map/stats_odd/pallas_call | solution.py:157
  43.5 2.4 %collective-permute-start.12 = (f32[4,8,256]{2,1,0:T(8,128)S(1)}, f32[4,8,256]{2,1,0:T(8,128)S(1)}, u32[]{:S(2)}, u32[]{:S(2)}) collective-permute-start(f32[4,8,256]{2,1,0:T(8,128)S(1)} %get-tuple-element.45), channel_id=1, source_target_pairs={{0,6},{1,7},{2,4},{3,5},{4,2},{5,3},{6,0},{7,1},{8,14},{9,15},{10,... | collective-permute-start | bytes 98312 | tf_op jit(solution)/shard_map/ppermute | solution.py:20
  47.1 3.7 %collective-permute-done.13 = f32[3,4,256]{2,1,0:T(4,128)S(1)} collective-permute-done((f32[3,4,256]{2,1,0:T(4,128)S(1)}, f32[3,4,256]{2,1,0:T(4,128)S(1)}, u32[]{:S(2)}, u32[]{:S(2)}) %collective-permute-start.13) | collective-permute-done | bytes 12320 | tf_op jit(solution)/shard_map/ppermute | solution.py:20
  51.9 3.7 %collective-permute-done.14 = f32[3,4,256]{2,1,0:T(4,128)S(1)} collective-permute-done((f32[3,4,256]{2,1,0:T(4,128)S(1)}, f32[3,4,256]{2,1,0:T(4,128)S(1)}, u32[]{:S(2)}, u32[]{:S(2)}) %collective-permute-start.14) | collective-permute-done | bytes 12320 | tf_op jit(solution)/shard_map/ppermute | solution.py:20
  55.7 2.4 %text_grads_1.1 = (bf16[256,2048]{1,0:T(8,128)(2,1)S(1)}, bf16[288,512]{1,0:T(8,128)(2,1)S(1)}) custom-call(f32[1,1]{1,0:T(1,128)} %bitcast.277.scale_ref, f32[1,1]{1,0:T(1,128)} %mul.147.coef_ref, s32[1,2]{1,0:T(1,128)S(1)} %add_bitcast_fusion.place_ref, bf16[1024,512]{1,0:T(8,128)(2,1)S(1)} %get-tuple-element.47.refs_0_, ...), custom_call_target="tpu_custom_call" | custom-call | flops 21474836480 | tf_op jit(solution)/shard_map/text_grads_1/pallas_call | solution.py:461
  58.2 6.9 %text_grads_3.1 = (bf16[256,2048]{1,0:T(8,128)(2,1)S(1)}, bf16[256,2048]{1,0:T(8,128)(2,1)S(1)}, bf16[256,2048]{1,0:T(8,128)(2,1)S(1)}, f32[264,512]{1,0:T(8,128...) custom-call(f32[1,1]{1,0:T(1,128)} %bitcast.278.scale_ref, ...), custom_call_target="tpu_custom_call" | custom-call | flops 64424509440 | tf_op jit(solution)/shard_map/text_grads_3/pallas_call | solution.py:461
  67.7 1.0 copy-done.8
  69.7 2.0 %collective-permute-start.21 = (bf16[288,512]{1,0:T(8,128)(2,1)S(1)}, bf16[288,512]{1,0:T(8,128)(2,1)}, u32[]{:S(2)}, u32[]{:S(2)}) collective-permute-start(bf16[288,512]{1,0:T(8,128)(2,1)S(1)} %get-tuple-element.64), channel_id=1, source_target_pairs={{0,8},{8,0},{16,24},{24,16},{1,9},{9,1},{17,25},{25,17},{2,10},{10... | collective-permute-start | bytes 884744 | tf_op jit(solution)/shard_map/ppermute | solution.py:20
  72.4 2.6 %pack_text.1.refs_8_ = bf16[288,512]{1,0:T(8,128)(2,1)} custom-call(f32[264,512]{1,0:T(8,128)} %copy-done.2, bf16[288,512]{1,0:T(8,128)(2,1)} %copy-done.15), custom_call_target="tpu_custom_call" | custom-call | tf_op jit(solution)/shard_map/pack_text/pallas_call | solution.py:283
  76.9 1.2 %copy-done.5 = bf16[256,2048]{1,0:T(8,128)(2,1)S(1)} copy-done((bf16[256,2048]{1,0:T(8,128)(2,1)S(1)}, bf16[256,2048]{1,0:T(8,128)(2,1)}, u32[]{:S(2)}) %copy-start.5) | copy-done | bytes 1048600
  78.2 1.2 %copy-done.7 = bf16[256,2048]{1,0:T(8,128)(2,1)S(1)} copy-done((bf16[256,2048]{1,0:T(8,128)(2,1)S(1)}, bf16[256,2048]{1,0:T(8,128)(2,1)}, u32[]{:S(2)}) %copy-start.7) | copy-done | bytes 1048600
  79.4 1.2 %copy-done.9 = bf16[256,2048]{1,0:T(8,128)(2,1)S(1)} copy-done((bf16[256,2048]{1,0:T(8,128)(2,1)S(1)}, bf16[256,2048]{1,0:T(8,128)(2,1)}, u32[]{:S(2)}) %copy-start.9) | copy-done | bytes 1048600
  80.6 1.2 %copy-done.11 = bf16[256,2048]{1,0:T(8,128)(2,1)S(1)} copy-done((bf16[256,2048]{1,0:T(8,128)(2,1)S(1)}, bf16[256,2048]{1,0:T(8,128)(2,1)}, u32[]{:S(2)}) %copy-start.11) | copy-done | bytes 1048600
  81.8 1.9 %image_grads.1.near = f32[4,264,512]{2,1,0:T(8,128)S(1)} custom-call(f32[1,1]{1,0:T(1,128)} %bitcast.279.scale_ref, f32[4,256]{1,0:T(4,128)S(1)} %fusion.34.refs_5_.extra, bf16[256,2048]{1,0:T(8,128)(2,1)S(1)} %copy-done.11, bf16[256,2048]{1,0:T(8,128)(2,1)S(1)} %copy-done.9, bf16[256,2048]{1,0:T(8,128)(2,1)S(1)} %copy-done.7, ...), custom_call_target="tpu_custom_call" | custom-call | flops 21474836480 | tf_op jit(solution)/shard_map/image_grads/pallas_call | solution.py:497
  83.8 1.4 %copy-done = f32[4,264,512]{2,1,0:T(8,128)} copy-done((f32[4,264,512]{2,1,0:T(8,128)}, f32[4,264,512]{2,1,0:T(8,128)S(1)}, u32[]{:S(2)}) %copy-start) | copy-done | bytes 2162712
  85.2 4.5 %pack_images.1 = (f32[264,512]{1,0:T(8,128)}, bf16[288,512]{1,0:T(8,128)(2,1)}, bf16[288,512]{1,0:T(8,128)(2,1)}, bf16[288,512]{1,0:T(8,128)(2,1)}) custom-call(f32[4,264,512]{2,1,0:T(8,128)} %copy-done, f32[4,264,512]{2,1,0:T(8,128)} %collective-permute-done.17.far), custom_call_target="tpu_custom_call" | custom-call | tf_op jit(solution)/shard_map/pack_images/pallas_call | solution.py:305
  89.7 1.5 %collective-permute-start.18 = (bf16[288,512]{1,0:T(8,128)(2,1)}, bf16[288,512]{1,0:T(8,128)(2,1)S(1)}, u32[]{:S(2)}, u32[]{:S(2)}) collective-permute-start(bf16[288,512]{1,0:T(8,128)(2,1)} %get-tuple-element.60), channel_id=1, source_target_pairs={{0,2},{1,3},{2,0},{3,1},{4,6},{5,7},{6,4},{7,5},{8,10},{9,11},{10,... | collective-permute-start | bytes 884744 | tf_op jit(solution)/shard_map/ppermute | solution.py:20
  91.1 1.6 %collective-permute-start.19 = (bf16[288,512]{1,0:T(8,128)(2,1)}, bf16[288,512]{1,0:T(8,128)(2,1)S(1)}, u32[]{:S(2)}, u32[]{:S(2)}) collective-permute-start(bf16[288,512]{1,0:T(8,128)(2,1)} %get-tuple-element.61), channel_id=1, source_target_pairs={{0,4},{1,5},{2,6},{3,7},{4,0},{5,1},{6,2},{7,3},{8,12},{9,13},{10,... | collective-permute-start | bytes 884744 | tf_op jit(solution)/shard_map/ppermute | solution.py:20
  93.2 3.1 %grad_text.1 = (f32[256,512]{1,0:T(8,128)}, f32[8,256]{1,0:T(8,128)}) custom-call(f32[264,512]{1,0:T(8,128)} %copy-done.1, bf16[288,512]{1,0:T(8,128)(2,1)} %collective-permute-done.21.refs_0_, bf16[288,512]{1,0:T(8,128)(2,1)} %collective-permute-done.22.refs_1_), custom_call_target="tpu_custom_call" | custom-call | tf_op jit(solution)/shard_map/grad_text/pallas_call | solution.py:342
  96.3 3.4 %collective-permute-done.18.refs_0_ = bf16[288,512]{1,0:T(8,128)(2,1)S(1)} collective-permute-done((bf16[288,512]{1,0:T(8,128)(2,1)}, bf16[288,512]{1,0:T(8,128)(2,1)S(1)}, u32[]{:S(2)}, u32[]{:S(2)}) %collective-permute-start.18) | collective-permute-done | bytes 294944 | tf_op jit(solution)/shard_map/ppermute | solution.py:20
  99.7 6.8 %collective-permute-done.19.refs_1_ = bf16[288,512]{1,0:T(8,128)(2,1)S(1)} collective-permute-done((bf16[288,512]{1,0:T(8,128)(2,1)}, bf16[288,512]{1,0:T(8,128)(2,1)S(1)}, u32[]{:S(2)}, u32[]{:S(2)}) %collective-permute-start.19) | collective-permute-done | bytes 294944 | tf_op jit(solution)/shard_map/ppermute | solution.py:20
  107.3 3.4 %grad_image.1 = (f32[256,512]{1,0:T(8,128)}, f32[8,256]{1,0:T(8,128)}) custom-call(f32[264,512]{1,0:T(8,128)} %get-tuple-element.59.base, bf16[288,512]{1,0:T(8,128)(2,1)} %copy-done.12, bf16[288,512]{1,0:T(8,128)(2,1)} %copy-done.13, bf16[288,512]{1,0:T(8,128)(2,1)} %copy-done.14, f32[8,256]{1,0:T(8,128)} %get-tuple-element.65.refs_3_), custom_call_target="tpu_custom_call" | custom-call | tf_op jit(solution)/shard_map/grad_image/pallas_call | solution.py:342
  110.7 1.3 %reduce_sum.9 = f32[]{:T(128)} reduce(f32[8,256]{1,0:T(8,128)} %get-tuple-element.68, f32[]{:T(128)} %constant.5.clone.1), dimensions={0,1}, to_apply=%region_0.0 | reduce | flops 2047 | bytes 8200 | tf_op jit(solution)/shard_map/reduce_sum | solution.py:547
  (69 shorter events, 12.3 us)
Async XLA Ops:
  1.7 11.1 %collective-permute-start.6 = (bf16[256,512]{1,0:T(8,128)(2,1)S(1)}, bf16[256,512]{1,0:T(8,128)(2,1)S(1)}, u32[]{:S(2)}, u32[]{:S(2)}) collective-permute-start(bf16[256,512]{1,0:T(8,128)(2,1)S(1)} %convert_element_type.6.refs_0_), channel_id=1, source_target_pairs={{0,6},{1,7},{2,4},{3,5},{4,2},{5,3},{6,0},{7,1},{8,14},{9,15},{10,... | collective-permute-start | bytes 786440 | tf_op jit(solution)/shard_map/ppermute | solution.py:20
  5.7 11.9 %collective-permute-start.5 = (bf16[256,512]{1,0:T(8,128)(2,1)S(1)}, bf16[256,512]{1,0:T(8,128)(2,1)S(1)}, u32[]{:S(2)}, u32[]{:S(2)}) collective-permute-start(bf16[256,512]{1,0:T(8,128)(2,1)S(1)} %convert_element_type.6.refs_0_), channel_id=1, source_target_pairs={{0,4},{1,5},{2,6},{3,7},{4,0},{5,1},{6,2},{7,3},{8,12},{9,13},{10,... | collective-permute-start | bytes 786440 | tf_op jit(solution)/shard_map/ppermute | solution.py:20
  6.2 11.7 %collective-permute-start.4 = (bf16[256,512]{1,0:T(8,128)(2,1)S(1)}, bf16[256,512]{1,0:T(8,128)(2,1)S(1)}, u32[]{:S(2)}, u32[]{:S(2)}) collective-permute-start(bf16[256,512]{1,0:T(8,128)(2,1)S(1)} %convert_element_type.6.refs_0_), channel_id=1, source_target_pairs={{0,2},{1,3},{2,0},{3,1},{4,6},{5,7},{6,4},{7,5},{8,10},{9,11},{10,... | collective-permute-start | bytes 786440 | tf_op jit(solution)/shard_map/ppermute | solution.py:20
  7.4 11.3 %collective-permute-start.3 = (bf16[256,512]{1,0:T(8,128)(2,1)S(1)}, bf16[256,512]{1,0:T(8,128)(2,1)S(1)}, u32[]{:S(2)}, u32[]{:S(2)}) collective-permute-start(bf16[256,512]{1,0:T(8,128)(2,1)S(1)} %convert_element_type.7.refs_4_.refs_8_), channel_id=1, source_target_pairs={{0,24},{8,16},{16,8},{24,0},{1,25},{9,17},{17,9},{25,1},{2,26},{10... | collective-permute-start | bytes 786440 | tf_op jit(solution)/shard_map/ppermute | solution.py:20
  11.5 21.5 %collective-permute-start.2 = (bf16[256,512]{1,0:T(8,128)(2,1)S(1)}, bf16[256,512]{1,0:T(8,128)(2,1)S(1)}, u32[]{:S(2)}, u32[]{:S(2)}) collective-permute-start(bf16[256,512]{1,0:T(8,128)(2,1)S(1)} %convert_element_type.7.refs_4_.refs_8_), channel_id=1, source_target_pairs={{0,16},{8,24},{16,0},{24,8},{1,17},{9,25},{17,1},{25,9},{2,18},{10... | collective-permute-start | bytes 786440 | tf_op jit(solution)/shard_map/ppermute | solution.py:20
  12.8 20.1 %collective-permute-start.1 = (bf16[256,512]{1,0:T(8,128)(2,1)S(1)}, bf16[256,512]{1,0:T(8,128)(2,1)S(1)}, u32[]{:S(2)}, u32[]{:S(2)}) collective-permute-start(bf16[256,512]{1,0:T(8,128)(2,1)S(1)} %convert_element_type.7.refs_4_.refs_8_), channel_id=1, source_target_pairs={{0,8},{8,0},{16,24},{24,16},{1,9},{9,1},{17,25},{25,17},{2,10},{10... | collective-permute-start | bytes 786440 | tf_op jit(solution)/shard_map/ppermute | solution.py:20
  17.6 20.8 %collective-permute-start = (bf16[256,512]{1,0:T(8,128)(2,1)S(1)}, bf16[256,512]{1,0:T(8,128)(2,1)S(1)}, u32[]{:S(2)}, u32[]{:S(2)}) collective-permute-start(bf16[256,512]{1,0:T(8,128)(2,1)S(1)} %convert_element_type.6.refs_0_), channel_id=1, source_target_pairs={{0,1},{1,0},{2,3},{3,2},{4,5},{5,4},{6,7},{7,6},{8,9},{9,8},{10,11... | collective-permute-start | bytes 786440 | tf_op jit(solution)/shard_map/ppermute | solution.py:20
  32.9 5.4 %collective-permute-start.7 = (bf16[256,512]{1,0:T(8,128)(2,1)S(1)}, bf16[256,512]{1,0:T(8,128)(2,1)S(1)}, u32[]{:S(2)}, u32[]{:S(2)}) collective-permute-start(bf16[256,512]{1,0:T(8,128)(2,1)S(1)} %collective-permute-done.4.refs_1_), channel_id=1, source_target_pairs={{0,1},{1,0},{2,3},{3,2},{4,5},{5,4},{6,7},{7,6},{8,9},{9,8},{10,11... | collective-permute-start | bytes 786440 | tf_op jit(solution)/shard_map/ppermute | solution.py:20
  32.9 5.5 %collective-permute-start.8 = (bf16[256,512]{1,0:T(8,128)(2,1)S(1)}, bf16[256,512]{1,0:T(8,128)(2,1)S(1)}, u32[]{:S(2)}, u32[]{:S(2)}) collective-permute-start(bf16[256,512]{1,0:T(8,128)(2,1)S(1)} %collective-permute-done.5.refs_2_), channel_id=1, source_target_pairs={{0,1},{1,0},{2,3},{3,2},{4,5},{5,4},{6,7},{7,6},{8,9},{9,8},{10,11... | collective-permute-start | bytes 786440 | tf_op jit(solution)/shard_map/ppermute | solution.py:20
  33.4 5.0 %collective-permute-start.9 = (bf16[256,512]{1,0:T(8,128)(2,1)S(1)}, bf16[256,512]{1,0:T(8,128)(2,1)S(1)}, u32[]{:S(2)}, u32[]{:S(2)}) collective-permute-start(bf16[256,512]{1,0:T(8,128)(2,1)S(1)} %collective-permute-done.6.refs_3_), channel_id=1, source_target_pairs={{0,1},{1,0},{2,3},{3,2},{4,5},{5,4},{6,7},{7,6},{8,9},{9,8},{10,11... | collective-permute-start | bytes 786440 | tf_op jit(solution)/shard_map/ppermute | solution.py:20
  43.5 7.3 %collective-permute-start.12 = (f32[4,8,256]{2,1,0:T(8,128)S(1)}, f32[4,8,256]{2,1,0:T(8,128)S(1)}, u32[]{:S(2)}, u32[]{:S(2)}) collective-permute-start(f32[4,8,256]{2,1,0:T(8,128)S(1)} %get-tuple-element.45), channel_id=1, source_target_pairs={{0,6},{1,7},{2,4},{3,5},{4,2},{5,3},{6,0},{7,1},{8,14},{9,15},{10,... | collective-permute-start | bytes 98312 | tf_op jit(solution)/shard_map/ppermute | solution.py:20
  46.0 4.8 %collective-permute-start.11 = (f32[4,8,256]{2,1,0:T(8,128)S(1)}, f32[4,8,256]{2,1,0:T(8,128)S(1)}, u32[]{:S(2)}, u32[]{:S(2)}) collective-permute-start(f32[4,8,256]{2,1,0:T(8,128)S(1)} %get-tuple-element.45), channel_id=1, source_target_pairs={{0,4},{1,5},{2,6},{3,7},{4,0},{5,1},{6,2},{7,3},{8,12},{9,13},{10,... | collective-permute-start | bytes 98312 | tf_op jit(solution)/shard_map/ppermute | solution.py:20
  46.5 4.3 %collective-permute-start.10 = (f32[4,8,256]{2,1,0:T(8,128)S(1)}, f32[4,8,256]{2,1,0:T(8,128)S(1)}, u32[]{:S(2)}, u32[]{:S(2)}) collective-permute-start(f32[4,8,256]{2,1,0:T(8,128)S(1)} %get-tuple-element.45), channel_id=1, source_target_pairs={{0,2},{1,3},{2,0},{3,1},{4,6},{5,7},{6,4},{7,5},{8,10},{9,11},{10,... | collective-permute-start | bytes 98312 | tf_op jit(solution)/shard_map/ppermute | solution.py:20
  47.1 3.7 %collective-permute-start.13 = (f32[3,4,256]{2,1,0:T(4,128)S(1)}, f32[3,4,256]{2,1,0:T(4,128)S(1)}, u32[]{:S(2)}, u32[]{:S(2)}) collective-permute-start(f32[3,4,256]{2,1,0:T(4,128)S(1)} %get-tuple-element.44), channel_id=1, source_target_pairs={{0,8},{8,0},{16,24},{24,16},{1,9},{9,1},{17,25},{25,17},{2,10},{10... | collective-permute-start | bytes 36872 | tf_op jit(solution)/shard_map/ppermute | solution.py:20
  50.9 4.7 %collective-permute-start.14 = (f32[3,4,256]{2,1,0:T(4,128)S(1)}, f32[3,4,256]{2,1,0:T(4,128)S(1)}, u32[]{:S(2)}, u32[]{:S(2)}) collective-permute-start(f32[3,4,256]{2,1,0:T(4,128)S(1)} %pad_maximum_fusion.1), channel_id=1, source_target_pairs={{0,16},{8,24},{16,0},{24,8},{1,17},{9,25},{17,1},{25,9},{2,18},{10... | collective-permute-start | bytes 36872 | tf_op jit(solution)/shard_map/ppermute | solution.py:20
  51.9 3.7 %collective-permute-start.15 = (f32[4,8,256]{2,1,0:T(8,128)S(1)}, f32[4,8,256]{2,1,0:T(8,128)S(1)}, u32[]{:S(2)}, u32[]{:S(2)}) collective-permute-start(f32[4,8,256]{2,1,0:T(8,128)S(1)} %pad_maximum_fusion), channel_id=1, source_target_pairs={{0,1},{1,0},{2,3},{3,2},{4,5},{5,4},{6,7},{7,6},{8,9},{9,8},{10,11... | collective-permute-start | bytes 98312 | tf_op jit(solution)/shard_map/ppermute | solution.py:20
  58.1 7.0 %copy-start.4 = (bf16[256,2048]{1,0:T(8,128)(2,1)}, bf16[256,2048]{1,0:T(8,128)(2,1)S(1)}, u32[]{:S(2)}) copy-start(bf16[256,2048]{1,0:T(8,128)(2,1)S(1)} %get-tuple-element.52.refs_9_.refs_3_) | copy-start | bytes 3145732
  58.1 13.6 %collective-permute-start.16 = (bf16[288,512]{1,0:T(8,128)(2,1)S(1)}, bf16[288,512]{1,0:T(8,128)(2,1)S(1)}, u32[]{:S(2)}, u32[]{:S(2)}) collective-permute-start(bf16[288,512]{1,0:T(8,128)(2,1)S(1)} %get-tuple-element.57), channel_id=1, source_target_pairs={{0,8},{8,0},{16,24},{24,16},{1,9},{9,1},{17,25},{25,17},{2,10},{10... | collective-permute-start | bytes 884744 | tf_op jit(solution)/shard_map/ppermute | solution.py:20
  67.7 1.0 copy-start.8
  69.7 15.5 %collective-permute-start.17 = (f32[4,264,512]{2,1,0:T(8,128)S(1)}, f32[4,264,512]{2,1,0:T(8,128)}, u32[]{:S(2)}, u32[]{:S(2)}) collective-permute-start(f32[4,264,512]{2,1,0:T(8,128)S(1)} %get-tuple-element.58), channel_id=1, source_target_pairs={{0,1},{1,0},{2,3},{3,2},{4,5},{5,4},{6,7},{7,6},{8,9},{9,8},{10,11... | collective-permute-start | bytes 6488072 | tf_op jit(solution)/shard_map/ppermute | solution.py:20
  69.7 23.4 %collective-permute-start.21 = (bf16[288,512]{1,0:T(8,128)(2,1)S(1)}, bf16[288,512]{1,0:T(8,128)(2,1)}, u32[]{:S(2)}, u32[]{:S(2)}) collective-permute-start(bf16[288,512]{1,0:T(8,128)(2,1)S(1)} %get-tuple-element.64), channel_id=1, source_target_pairs={{0,8},{8,0},{16,24},{24,16},{1,9},{9,1},{17,25},{25,17},{2,10},{10... | collective-permute-start | bytes 884744 | tf_op jit(solution)/shard_map/ppermute | solution.py:20
  75.0 18.2 %collective-permute-start.22 = (bf16[288,512]{1,0:T(8,128)(2,1)}, bf16[288,512]{1,0:T(8,128)(2,1)}, u32[]{:S(2)}, u32[]{:S(2)}) collective-permute-start(bf16[288,512]{1,0:T(8,128)(2,1)} %pack_text.1.refs_8_), channel_id=1, source_target_pairs={{0,16},{8,24},{16,0},{24,8},{1,17},{9,25},{17,1},{25,9},{2,18},{10... | collective-permute-start | bytes 884744 | tf_op jit(solution)/shard_map/ppermute | solution.py:20
  75.9 1.0 copy-start.3
  76.9 1.2 %copy-start.5 = (bf16[256,2048]{1,0:T(8,128)(2,1)S(1)}, bf16[256,2048]{1,0:T(8,128)(2,1)}, u32[]{:S(2)}) copy-start(bf16[256,2048]{1,0:T(8,128)(2,1)} %copy-done.4) | copy-start | bytes 3145732
  78.2 1.2 %copy-start.7 = (bf16[256,2048]{1,0:T(8,128)(2,1)S(1)}, bf16[256,2048]{1,0:T(8,128)(2,1)}, u32[]{:S(2)}) copy-start(bf16[256,2048]{1,0:T(8,128)(2,1)} %copy-done.6) | copy-start | bytes 3145732
  79.4 1.2 %copy-start.9 = (bf16[256,2048]{1,0:T(8,128)(2,1)S(1)}, bf16[256,2048]{1,0:T(8,128)(2,1)}, u32[]{:S(2)}) copy-start(bf16[256,2048]{1,0:T(8,128)(2,1)} %copy-done.8) | copy-start | bytes 3145732
  80.6 1.2 %copy-start.11 = (bf16[256,2048]{1,0:T(8,128)(2,1)S(1)}, bf16[256,2048]{1,0:T(8,128)(2,1)}, u32[]{:S(2)}) copy-start(bf16[256,2048]{1,0:T(8,128)(2,1)} %copy-done.10) | copy-start | bytes 3145732
  83.8 1.4 %copy-start = (f32[4,264,512]{2,1,0:T(8,128)}, f32[4,264,512]{2,1,0:T(8,128)S(1)}, u32[]{:S(2)}) copy-start(f32[4,264,512]{2,1,0:T(8,128)S(1)} %image_grads.1.near) | copy-start | bytes 6488068
  89.7 10.1 %collective-permute-start.18 = (bf16[288,512]{1,0:T(8,128)(2,1)}, bf16[288,512]{1,0:T(8,128)(2,1)S(1)}, u32[]{:S(2)}, u32[]{:S(2)}) collective-permute-start(bf16[288,512]{1,0:T(8,128)(2,1)} %get-tuple-element.60), channel_id=1, source_target_pairs={{0,2},{1,3},{2,0},{3,1},{4,6},{5,7},{6,4},{7,5},{8,10},{9,11},{10,... | collective-permute-start | bytes 884744 | tf_op jit(solution)/shard_map/ppermute | solution.py:20
  91.1 15.4 %collective-permute-start.19 = (bf16[288,512]{1,0:T(8,128)(2,1)}, bf16[288,512]{1,0:T(8,128)(2,1)S(1)}, u32[]{:S(2)}, u32[]{:S(2)}) collective-permute-start(bf16[288,512]{1,0:T(8,128)(2,1)} %get-tuple-element.61), channel_id=1, source_target_pairs={{0,4},{1,5},{2,6},{3,7},{4,0},{5,1},{6,2},{7,3},{8,12},{9,13},{10,... | collective-permute-start | bytes 884744 | tf_op jit(solution)/shard_map/ppermute | solution.py:20
  92.8 13.7 %collective-permute-start.20 = (bf16[288,512]{1,0:T(8,128)(2,1)}, bf16[288,512]{1,0:T(8,128)(2,1)S(1)}, u32[]{:S(2)}, u32[]{:S(2)}) collective-permute-start(bf16[288,512]{1,0:T(8,128)(2,1)} %get-tuple-element.62), channel_id=1, source_target_pairs={{0,6},{1,7},{2,4},{3,5},{4,2},{5,3},{6,0},{7,1},{8,14},{9,15},{10,... | collective-permute-start | bytes 884744 | tf_op jit(solution)/shard_map/ppermute | solution.py:20
  99.7 6.8 %copy-start.12 = (bf16[288,512]{1,0:T(8,128)(2,1)}, bf16[288,512]{1,0:T(8,128)(2,1)S(1)}, u32[]{:S(2)}) copy-start(bf16[288,512]{1,0:T(8,128)(2,1)S(1)} %collective-permute-done.18.refs_0_) | copy-start | bytes 884740
  (7 other events, 5.8 us)

commit v6 on v5

--- a/solution.py
+++ b/solution.py
@@ -207,6 +207,7 @@
 BIAS = 125
 EXTRA = 8
 MORE = 32
+STEP = 32
 
 
 def put_extra(out, extra_ref):
@@ -220,14 +221,17 @@
     return jnp.exp2(k).astype(jnp.bfloat16).astype(jnp.float32)
 
 
-def encode(out, value, extra):
-    size, width = value.shape
-    top = jnp.maximum(jnp.max(jnp.abs(value), axis=1, keepdims=True), 1e-30)
-    k = jnp.ceil(jnp.log2(top))
-    whole = jnp.floor(jnp.abs(value) * (power(-k) * (LEVELS - 1)) + 0.5)
-    high = jnp.floor(whole * (1 / LOW))
-    code = (1.0 + (whole - LOW * high) * (1 / LOW)) * jnp.exp2(high - BIAS)
-    out[:size, :] = jnp.where(value < 0, -code, code).astype(jnp.bfloat16)
+def encode(out, powers, size, slab, extra):
+    width = out.shape[1]
+    for r in range(0, size, STEP):
+        value = slab(r)
+        top = jnp.maximum(jnp.max(jnp.abs(value), axis=1, keepdims=True), 1e-30)
+        k = jnp.ceil(jnp.log(top) * LOG2E)
+        powers[r : r + STEP, :] = jnp.broadcast_to(power(k), (STEP, LANES))
+        whole = jnp.floor(jnp.abs(value) * (power(-k) * (LEVELS - 1)) + 0.5) * (1 / LOW)
+        high = jnp.floor(whole)
+        code = (1.0 + (whole - high)) * jnp.exp2(high - BIAS)
+        out[r : r + STEP, :] = jnp.where(value < 0, -code, code).astype(jnp.bfloat16)
     half = width // 2
     first = extra[:, :half].astype(jnp.bfloat16)
     rest = extra[:, :half] - first.astype(jnp.float32)
@@ -236,24 +240,23 @@
     zeros = jnp.zeros((EXTRA, half), jnp.bfloat16)
     out[size : size + 2 * EXTRA, :half] = jnp.concatenate([first, second], axis=0)
     out[size : size + 2 * EXTRA, half:] = jnp.concatenate([third, zeros], axis=0)
-    powers = jnp.broadcast_to(power(k), (size, LANES)).T
     out[size + 2 * EXTRA :, :] = jnp.zeros((MORE - 2 * EXTRA, width), jnp.bfloat16)
-    out[size + 2 * EXTRA :, :size] = powers[: MORE - 2 * EXTRA, :].astype(jnp.bfloat16)
+    out[size + 2 * EXTRA :, :size] = powers[...].T[: MORE - 2 * EXTRA, :].astype(jnp.bfloat16)
 
 
 def decode_powers(code, size):
     powers = code[size + 2 * EXTRA :, :size].astype(jnp.float32)
-    return jnp.broadcast_to(powers[0:1, :], (LANES, size)).T * (1 / (LEVELS - 1))
-
-
-def decode(code, powers):
+    return jnp.broadcast_to(powers[0:1, :], (LANES, size)).T * (LOW / (LEVELS - 1))
+
+
+def decode(code, powers, r):
     lanes = []
     for lane in range(0, code.shape[1], LANES):
-        c = code[:, lane : lane + LANES].astype(jnp.float32)
+        c = code[r : r + STEP, lane : lane + LANES].astype(jnp.float32)
         a = jnp.abs(c)
-        high = jnp.floor(jnp.log2(a))
-        whole = LOW * (high + (BIAS - 1) + a * jnp.exp2(-high))
-        lanes.append(jnp.where(c < 0, -whole, whole) * powers)
+        high = jnp.floor(jnp.log(a) * LOG2E)
+        whole = (high + (BIAS - 1)) + a * jnp.exp2(-high)
+        lanes.append(jnp.where(c < 0, -whole, whole) * powers[r : r + STEP, :])
     return jnp.concatenate(lanes, axis=1)
 
 
@@ -265,16 +268,20 @@
 
 
 def pack_text_kernel(n, base, *refs):
-    codes, out, total = refs[:n], refs[n], refs[n + 1]
-    size = base.shape[0] - EXTRA
-    total[...] = base[:size, :]
-    extra = base[size:, :]
-    half = base.shape[1] // 2
-    more = extra[:, :half]
-    for code in codes:
-        total[...] += decode(code[:size, :], decode_powers(code, size))
+    codes, out, powers, received = refs[:n], *refs[n:]
+    size, half = base.shape[0] - EXTRA, base.shape[1] // 2
+    more = base[size:, :half]
+    for c, code in enumerate(codes):
+        received[c] = decode_powers(code, size)
         more = more + decode_extra(code, size)
-    encode(out, total[...], more)
+
+    def slab(r):
+        value = base[r : r + STEP, :]
+        for c, code in enumerate(codes):
+            value = value + decode(code, received.at[c], r)
+        return value
+
+    encode(out, powers, size, slab, more)
 
 
 def pack_text(base, codes):
@@ -285,75 +292,96 @@
         out_shape=jax.ShapeDtypeStruct((size + MORE, width), jnp.bfloat16),
         in_specs=[vmem] * (1 + len(codes)),
         out_specs=vmem,
-        scratch_shapes=[VMEM((size, width), jnp.float32)],
+        scratch_shapes=[VMEM((size, LANES), jnp.float32), VMEM((len(codes), size, LANES), jnp.float32)],
+        compiler_params=pltpu.CompilerParams(vmem_limit_bytes=6 * 2**20),
         name="pack_text",
     )(base, *codes)
 
 
-def pack_images_kernel(near, far, own, *outs):
+def pack_images_kernel(near, far, own, *refs):
+    outs, powers = refs[:-1], refs[-1]
     size = near.shape[1] - EXTRA
     own[...] = near[0] + far[0]
     for j, out in enumerate(outs, 1):
-        total = near[j] + far[j]
-        encode(out, total[:size], total[size:])
+        encode(
+            out,
+            powers.at[j - 1],
+            size,
+            lambda r, j=j: near[j, r : r + STEP, :] + far[j, r : r + STEP, :],
+            near[j, size:, :] + far[j, size:, :],
+        )
 
 
 def pack_images(near, far):
     n, rows, width = near.shape
+    size = rows - EXTRA
     vmem = pl.BlockSpec(memory_space=VMEM)
-    code = jax.ShapeDtypeStruct((rows - EXTRA + MORE, width), jnp.bfloat16)
+    code = jax.ShapeDtypeStruct((size + MORE, width), jnp.bfloat16)
     own, *codes = pl.pallas_call(
         pack_images_kernel,
         out_shape=(jax.ShapeDtypeStruct((rows, width), jnp.float32),) + (code,) * (n - 1),
         in_specs=[vmem] * 2,
         out_specs=(vmem,) * n,
+        scratch_shapes=[VMEM((n - 1, size, LANES), jnp.float32)],
+        compiler_params=pltpu.CompilerParams(vmem_limit_bytes=6 * 2**20),
         name="pack_images",
     )(near, far)
     return own, codes
 
 
-def total_kernel(n, in_order, steps, base, *refs):
-    codes, before, out, extra, powers = refs[:n], refs[n:-3], *refs[-3:]
-    i = pl.program_id(0)
+def total_kernel(n, in_order, coef_ref, base, *refs):
+    codes, before = refs[:n], refs[n:-6]
+    out, extra, scalar, value, powers, sems = refs[-6:]
     size, width = base.shape[0] - EXTRA, base.shape[1]
     combine = functools.partial(functools.reduce, jnp.add) if in_order else by_pairs_added
-
-    @pl.when(i == 0)
-    def _():
-        for c, code in enumerate(codes):
-            powers[c] = decode_powers(code, size)
-        more = combine([base[size:, : width // 2]] + [decode_extra(code, size) for code in codes])
-        extra[...] = sum([b[...] for b in before], more)
-
-    part = pl.ds(pl.multiple_of(i * (size // steps), size // steps), size // steps)
-    out[...] = combine(
-        [base[part, :]] + [decode(code[part, :], powers[c, part, :]) for c, code in enumerate(codes)]
-    )
+    for c, code in enumerate(codes):
+        powers[c] = decode_powers(code, size)
+    copies = []
+    steps = sems.shape[0]
+    for i in range(steps):
+        part = pl.ds(i * (size // steps), size // steps)
+        for r in range(i * (size // steps), (i + 1) * (size // steps), STEP):
+            value[r : r + STEP, :] = combine(
+                [base[r : r + STEP, :]] + [decode(code, powers.at[c], r) for c, code in enumerate(codes)]
+            )
+        copies.append(pltpu.make_async_copy(value.at[part], out.at[part], sems.at[i]))
+        copies[-1].start()
+    more = combine([base[size:, : width // 2]] + [decode_extra(code, size) for code in codes])
+    more = sum([b[...] for b in before], more)
+    extra[...] = more
+    scalar[0, 0] = jnp.sum(more) / coef_ref[0, 0]
+    for copy in copies:
+        copy.wait()
 
 
 def by_pairs_added(blocks):
     return by_pairs(blocks, jnp.add)
 
 
-def total_of(base, codes, in_order, before, name):
+def total_of(coef, base, codes, in_order, before, name):
     size, width = base.shape[0] - EXTRA, base.shape[1]
     vmem = pl.BlockSpec(memory_space=VMEM)
-    steps = 4
+    smem = pl.BlockSpec(memory_space=SMEM)
     return pl.pallas_call(
-        functools.partial(total_kernel, len(codes), in_order, steps),
-        grid=(steps,),
+        functools.partial(total_kernel, len(codes), in_order),
         out_shape=(
             jax.ShapeDtypeStruct((size, width), jnp.float32),
             jax.ShapeDtypeStruct((EXTRA, width // 2), jnp.float32),
+            jax.ShapeDtypeStruct((1, 1), jnp.float32),
         ),
-        in_specs=[vmem] * (1 + len(codes) + len(before)),
-        out_specs=(pl.BlockSpec((size // steps, width), lambda i: (i, 0)), vmem),
-        scratch_shapes=[VMEM((len(codes), size, LANES), jnp.float32)],
+        in_specs=[smem] + [vmem] * (1 + len(codes) + len(before)),
+        out_specs=(pl.BlockSpec(memory_space=pl.ANY), vmem, smem),
+        scratch_shapes=[
+            VMEM((size, width), jnp.float32),
+            VMEM((len(codes), size, LANES), jnp.float32),
+            pltpu.SemaphoreType.DMA((4,)),
+        ],
+        compiler_params=pltpu.CompilerParams(vmem_limit_bytes=8 * 2**20),
         name=name,
-    )(base, *codes, *before)
-
-
-def text_block(text, t, halves, row_lse, col_lse, place_ref, scale_ref, coef_ref, extra, grad_ref, out_ref, total):
+    )(coef, base, *codes, *before)
+
+
+def text_block(text, t, halves, row_lse, col_lse, place_ref, scale_ref, coef_ref, extra, grad_ref, out_ref, total, powers):
     coef = coef_ref[0, 0]
     r_place, c_place = place_ref[0, 0], place_ref[0, 1]
     half, width = halves[0].shape
@@ -393,7 +421,7 @@
     )
     put_extra(total.at[size:, :], extra)
     if t & 1:
-        encode(out_ref, total[:size, :], total[size:, :])
+        encode(out_ref, powers, size, lambda r: total[r : r + STEP, :], total[size:, :])
     else:
         out_ref[...] = total[...]
 
@@ -419,7 +447,7 @@
     grads, outs = rest[:n], rest[n : 2 * n]
     for i, t in enumerate(order):
         text_block(
-            texts[i], t, (even, odd), row_lse, col_lse, place_ref, scale_ref, coef_ref, row_extra, grads[i], outs[i], rest[-1]
+            texts[i], t, (even, odd), row_lse, col_lse, place_ref, scale_ref, coef_ref, row_extra, grads[i], outs[i], *rest[-2:]
         )
     if n_done:
         far_ref = rest[2 * n]
@@ -463,7 +491,10 @@
         out_shape=tuple(out_shape),
         in_specs=[smem] * 3 + [vmem] * len(operands),
         out_specs=(vmem,) * len(out_shape),
-        scratch_shapes=[VMEM((block + EXTRA, width), jnp.float32)],
+        scratch_shapes=[
+            VMEM((block + EXTRA, width), jnp.float32),
+            VMEM((block, LANES), jnp.float32),
+        ],
         compiler_params=pltpu.CompilerParams(vmem_limit_bytes=12 * 2**20),
         cost_estimate=pl.CostEstimate(
             flops=FLOPS * 4 * n * block * 2 * half * width, bytes_accessed=0, transcendentals=0
@@ -539,12 +570,12 @@
             code = after[0] if (b, q) == (1, last ^ 1) else pack_text(parts[q], codes[q])
             codes[q ^ (1 << b)].append(swap(code, "row", n_row, 1 << b))
             del codes[q]
-    grad_text, text_extra = total_of(parts[0], codes[0], True, [], "grad_text")
+    grad_text, text_extra, _ = total_of(coef, parts[0], codes[0], True, [], "grad_text")
 
     own, others = pack_images(near, swap(far, "col", n_col, 1))
     others = [swap(code, "col", n_col, 2 * j) for j, code in enumerate(others, 1)]
-    grad_image, extra = total_of(own, others, False, [text_extra], "grad_image")
-    return grad_image, grad_text, jnp.sum(extra) / coef[0, 0]
+    grad_image, _, grad_scale = total_of(coef, own, others, False, [text_extra], "grad_image")
+    return grad_image, grad_text, grad_scale.reshape(())
 
 
 def solution(mesh):

time: 114 us -> 91.5 us (0.80)
  local copies, waits for them, and re-layouts: 13.4 us -> 0 us
  Pallas kernels: 34.9 us -> 27.4 us
  between operations: 3.25 us -> 1.62 us
  other arithmetic: 3.73 us -> 2.43 us
    unnamed x32 -> x0, local copies, waits for them, and re-layouts: 13.4 us -> none
    pallas_call x1, Pallas kernels: 4.49 us -> 1.13 us  [pack_images(): pl.pallas_call(pack_images_kernel, out_shape=(jax.ShapeDtypeStruct((rows,...]
    pallas_call x2, Pallas kernels: 6.53 us -> 4.1 us  [total_of(): pl.pallas_call(functools.partial(total_kernel, len(codes), in_order), out...]
    pallas_call x1, Pallas kernels: 2.56 us -> 0.7 us  [pack_text(): pl.pallas_call(functools.partial(pack_text_kernel, len(codes)), out_shape...]
    reduce_sum x1 -> x0, other arithmetic: 1.3 us -> none  [on_device(): return (grad_image, grad_text, jnp.sum(extra) / coef[0, 0])]
  transfers between devices with their start and end apart: 23 -> 23, of which waited for: 9 -> 10; matrix products, arithmetic and copies ran while one was open for 1% -> 1% of each run, Pallas kernels for 21% -> 19%
where the time goes in v6:
time: 91.5 us; the launch traced here: 91.3 us
  waiting for transfers between devices  37.2 us (41%)
  Pallas kernels  27.4 us (30%)
  starting transfers between devices  22.6 us (25%)
  other arithmetic  2.43 us (3%)
  between operations  1.62 us (2%)
    ppermute x23, waiting for transfers between devices, swap(): return lax.ppermute(x, axis, [(i, i ^ q) for i in range(n)])  37.2 us
    ppermute x23, starting transfers between devices, swap(): return lax.ppermute(x, axis, [(i, i ^ q) for i in range(n)])  22.6 us
    pallas_call x2, Pallas kernels, stats(): pl.pallas_call(functools.partial(stats_kernel, len(texts), len(images), 1...  10 us
    pallas_call x2, Pallas kernels, text_grads(): pl.pallas_call(functools.partial(text_kernel, tuple(order), len(done), bl...  9.47 us
    pallas_call x2, Pallas kernels, total_of(): pl.pallas_call(functools.partial(total_kernel, len(codes), in_order), out...  4.1 us
    pallas_call x1, Pallas kernels, image_grads(): pl.pallas_call(functools.partial(image_kernel, n_text, block), out_shape=...  1.95 us
  transfers between devices with their start and end apart: 23, of which 10 were waited for; matrix products, arithmetic and copies ran while one was open for 1% of the time, Pallas kernels for 19%

profile of v6, /device:TPU:0, one launch (start us, length us, event | category | flops | bytes accessed | tf_op | source)
XLA Modules:
  0.0 91.3 jit_solution(8877879392710769309)
XLA Ops:
  0.6 1.1 %convert_element_type.6.refs_0_ = bf16[256,512]{1,0:T(8,128)(2,1)S(1)} convert(f32[256,512]{1,0:T(8,128)} %param.3) | non-fusion elementwise | flops 131072 | bytes 786432 | tf_op jit(solution)/shard_map/convert_element_type | solution.py:549
  1.7 4.0 %collective-permute-start.6 = (bf16[256,512]{1,0:T(8,128)(2,1)S(1)}, bf16[256,512]{1,0:T(8,128)(2,1)S(1)}, u32[]{:S(2)}, u32[]{:S(2)}) collective-permute-start(bf16[256,512]{1,0:T(8,128)(2,1)S(1)} %convert_element_type.6.refs_0_), channel_id=1, source_target_pairs={{0,6},{1,7},{2,4},{3,5},{4,2},{5,3},{6,0},{7,1},{8,14},{9,15},{10,... | collective-permute-start | bytes 786440 | tf_op jit(solution)/shard_map/ppermute | solution.py:20
  6.3 1.1 %convert_element_type.7.refs_4_.refs_8_ = bf16[256,512]{1,0:T(8,128)(2,1)S(1)} convert(f32[256,512]{1,0:T(8,128)} %param.4) | non-fusion elementwise | flops 131072 | bytes 786432 | tf_op jit(solution)/shard_map/convert_element_type | solution.py:549
  7.4 4.1 %collective-permute-start.3 = (bf16[256,512]{1,0:T(8,128)(2,1)S(1)}, bf16[256,512]{1,0:T(8,128)(2,1)S(1)}, u32[]{:S(2)}, u32[]{:S(2)}) collective-permute-start(bf16[256,512]{1,0:T(8,128)(2,1)S(1)} %convert_element_type.7.refs_4_.refs_8_), channel_id=1, source_target_pairs={{0,24},{8,16},{16,8},{24,0},{1,25},{9,17},{17,9},{25,1},{2,26},{10... | collective-permute-start | bytes 786440 | tf_op jit(solution)/shard_map/ppermute | solution.py:20
  11.5 1.4 %collective-permute-done.6.refs_3_ = bf16[256,512]{1,0:T(8,128)(2,1)S(1)} collective-permute-done((bf16[256,512]{1,0:T(8,128)(2,1)S(1)}, bf16[256,512]{1,0:T(8,128)(2,1)S(1)}, u32[]{:S(2)}, u32[]{:S(2)}) %collective-permute-start.6) | collective-permute-done | bytes 262176 | tf_op jit(solution)/shard_map/ppermute | solution.py:20
  12.8 2.1 %collective-permute-start.1 = (bf16[256,512]{1,0:T(8,128)(2,1)S(1)}, bf16[256,512]{1,0:T(8,128)(2,1)S(1)}, u32[]{:S(2)}, u32[]{:S(2)}) collective-permute-start(bf16[256,512]{1,0:T(8,128)(2,1)S(1)} %convert_element_type.7.refs_4_.refs_8_), channel_id=1, source_target_pairs={{0,8},{8,0},{16,24},{24,16},{1,9},{9,1},{17,25},{25,17},{2,10},{10... | collective-permute-start | bytes 786440 | tf_op jit(solution)/shard_map/ppermute | solution.py:20
  15.7 1.9 %collective-permute-done.5.refs_2_ = bf16[256,512]{1,0:T(8,128)(2,1)S(1)} collective-permute-done((bf16[256,512]{1,0:T(8,128)(2,1)S(1)}, bf16[256,512]{1,0:T(8,128)(2,1)S(1)}, u32[]{:S(2)}, u32[]{:S(2)}) %collective-permute-start.5) | collective-permute-done | bytes 262176 | tf_op jit(solution)/shard_map/ppermute | solution.py:20
  17.9 0.8 collective-permute-done.3.refs_7_.refs_6_.refs_10_
  18.7 14.2 %collective-permute-done.2.refs_6_ = bf16[256,512]{1,0:T(8,128)(2,1)S(1)} collective-permute-done((bf16[256,512]{1,0:T(8,128)(2,1)S(1)}, bf16[256,512]{1,0:T(8,128)(2,1)S(1)}, u32[]{:S(2)}, u32[]{:S(2)}) %collective-permute-start.2) | collective-permute-done | bytes 262176 | tf_op jit(solution)/shard_map/ppermute | solution.py:20
  32.9 0.5 collective-permute-start.8
  33.4 4.9 %stats_even.1 = (f32[4,8,256]{2,1,0:T(8,128)S(1)}, f32[3,4,256]{2,1,0:T(4,128)S(1)}, bf16[1024,512]{1,0:T(8,128)(2,1)S(1)}) custom-call(f32[1,1]{1,0:T(1,128)S(6)} %mul.147.coef_ref, s32[1,2]{1,0:T(1,128)S(1)} %add_bitcast_fusion.place_ref, bf16[256,512]{1,0:T(8,128)(2,1)S(1)} %convert_element_type.6.refs_0_, ...), custom_call_target="tpu_custom_call" | custom-call | flops 21474836480 | tf_op jit(solution)/shard_map/stats_even/pallas_call | solution.py:157
  38.4 5.1 %stats_odd.1 = (f32[4,8,256]{2,1,0:T(8,128)S(1)}, f32[3,4,256]{2,1,0:T(4,128)S(1)}, bf16[1024,512]{1,0:T(8,128)(2,1)S(1)}) custom-call(f32[1,1]{1,0:T(1,128)S(6)} %mul.147.coef_ref, s32[1,2]{1,0:T(1,128)S(1)} %add_bitcast_fusion.place_ref, bf16[256,512]{1,0:T(8,128)(2,1)S(1)} %collective-permute-done.refs_0_, ...), custom_call_target="tpu_custom_call" | custom-call | flops 21474836480 | tf_op jit(solution)/shard_map/stats_odd/pallas_call | solution.py:157
  43.5 2.4 %collective-permute-start.12 = (f32[4,8,256]{2,1,0:T(8,128)S(1)}, f32[4,8,256]{2,1,0:T(8,128)S(1)}, u32[]{:S(2)}, u32[]{:S(2)}) collective-permute-start(f32[4,8,256]{2,1,0:T(8,128)S(1)} %get-tuple-element.45), channel_id=1, source_target_pairs={{0,6},{1,7},{2,4},{3,5},{4,2},{5,3},{6,0},{7,1},{8,14},{9,15},{10,... | collective-permute-start | bytes 98312 | tf_op jit(solution)/shard_map/ppermute | solution.py:20
  45.9 0.5 collective-permute-start.11
  46.4 0.6 collective-permute-start.10
  47.1 3.7 %collective-permute-done.13 = f32[3,4,256]{2,1,0:T(4,128)S(1)} collective-permute-done((f32[3,4,256]{2,1,0:T(4,128)S(1)}, f32[3,4,256]{2,1,0:T(4,128)S(1)}, u32[]{:S(2)}, u32[]{:S(2)}) %collective-permute-start.13) | collective-permute-done | bytes 12320 | tf_op jit(solution)/shard_map/ppermute | solution.py:20
  50.9 1.0 %collective-permute-start.14 = (f32[3,4,256]{2,1,0:T(4,128)S(1)}, f32[3,4,256]{2,1,0:T(4,128)S(1)}, u32[]{:S(2)}, u32[]{:S(2)}) collective-permute-start(f32[3,4,256]{2,1,0:T(4,128)S(1)} %pad_maximum_fusion.1), channel_id=1, source_target_pairs={{0,16},{8,24},{16,0},{24,8},{1,17},{9,25},{17,1},{25,9},{2,18},{10... | collective-permute-start | bytes 36872 | tf_op jit(solution)/shard_map/ppermute | solution.py:20
  51.9 3.7 %collective-permute-done.14 = f32[3,4,256]{2,1,0:T(4,128)S(1)} collective-permute-done((f32[3,4,256]{2,1,0:T(4,128)S(1)}, f32[3,4,256]{2,1,0:T(4,128)S(1)}, u32[]{:S(2)}, u32[]{:S(2)}) %collective-permute-start.14) | collective-permute-done | bytes 12320 | tf_op jit(solution)/shard_map/ppermute | solution.py:20
  55.7 2.4 %text_grads_1.1 = (bf16[256,2048]{1,0:T(8,128)(2,1)S(1)}, bf16[288,512]{1,0:T(8,128)(2,1)S(1)}) custom-call(f32[1,1]{1,0:T(1,128)} %bitcast.277.scale_ref, f32[1,1]{1,0:T(1,128)S(6)} %mul.147.coef_ref, s32[1,2]{1,0:T(1,128)S(1)} %add_bitcast_fusion.place_ref, bf16[1024,512]{1,0:T(8,128)(2,1)S(1)} %get-tuple-element.47.refs_0_, ...), custom_call_target="tpu_custom_call" | custom-call | flops 21474836480 | tf_op jit(solution)/shard_map/text_grads_1/pallas_call | solution.py:489
  58.2 7.0 %text_grads_3.1 = (bf16[256,2048]{1,0:T(8,128)(2,1)S(1)}, bf16[256,2048]{1,0:T(8,128)(2,1)S(1)}, bf16[256,2048]{1,0:T(8,128)(2,1)S(1)}, f32[264,512]{1,0:T(8,128...) custom-call(f32[1,1]{1,0:T(1,128)} %bitcast.278.scale_ref, ...), custom_call_target="tpu_custom_call" | custom-call | flops 64424509440 | tf_op jit(solution)/shard_map/text_grads_3/pallas_call | solution.py:489
  65.4 2.1 %collective-permute-start.21 = (bf16[288,512]{1,0:T(8,128)(2,1)S(1)}, bf16[288,512]{1,0:T(8,128)(2,1)S(1)}, u32[]{:S(2)}, u32[]{:S(2)}) collective-permute-start(bf16[288,512]{1,0:T(8,128)(2,1)S(1)} %get-tuple-element.64), channel_id=1, source_target_pairs={{0,8},{8,0},{16,24},{24,16},{1,9},{9,1},{17,25},{25,17},{2,10},{10... | collective-permute-start | bytes 884744 | tf_op jit(solution)/shard_map/ppermute | solution.py:20
  67.4 0.7 pack_text.1.refs_8_
  68.1 1.0 %collective-permute-start.22 = (bf16[288,512]{1,0:T(8,128)(2,1)S(1)}, bf16[288,512]{1,0:T(8,128)(2,1)S(1)}, u32[]{:S(2)}, u32[]{:S(2)}) collective-permute-start(bf16[288,512]{1,0:T(8,128)(2,1)S(1)} %pack_text.1.refs_8_), channel_id=1, source_target_pairs={{0,16},{8,24},{16,0},{24,8},{1,17},{9,25},{17,1},{25,9},{2,18},{10... | collective-permute-start | bytes 884744 | tf_op jit(solution)/shard_map/ppermute | solution.py:20
  69.2 2.0 %image_grads.1.near = f32[4,264,512]{2,1,0:T(8,128)S(1)} custom-call(f32[1,1]{1,0:T(1,128)} %bitcast.279.scale_ref, f32[4,256]{1,0:T(4,128)S(1)} %fusion.34.refs_5_.extra, bf16[256,2048]{1,0:T(8,128)(2,1)S(1)} %get-tuple-element.53.refs_0_, bf16[256,2048]{1,0:T(8,128)(2,1)S(1)} %get-tuple-element.54.refs_1_, ...), custom_call_target="tpu_custom_call" | custom-call | flops 21474836480 | tf_op jit(solution)/shard_map/image_grads/pallas_call | solution.py:528
  71.1 1.1 %pack_images.1 = (f32[264,512]{1,0:T(8,128)S(1)}, bf16[288,512]{1,0:T(8,128)(2,1)S(1)}, bf16[288,512]{1,0:T(8,128)(2,1)S(1)}, bf16[288,512]{1,0:T(8,128)(2,1)S(1)}) custom-call(f32[4,264,512]{2,1,0:T(8,128)S(1)} %image_grads.1.near, f32[4,264,512]{2,1,0:T(8,128)S(1)} %collective-permute-done.17.far), custom_call_target="tpu_custom_call" | custom-call | tf_op jit(solution)/shard_map/pack_images/pallas_call | solution.py:320
  72.3 1.5 %collective-permute-start.18 = (bf16[288,512]{1,0:T(8,128)(2,1)S(1)}, bf16[288,512]{1,0:T(8,128)(2,1)S(1)}, u32[]{:S(2)}, u32[]{:S(2)}) collective-permute-start(bf16[288,512]{1,0:T(8,128)(2,1)S(1)} %get-tuple-element.60), channel_id=1, source_target_pairs={{0,2},{1,3},{2,0},{3,1},{4,6},{5,7},{6,4},{7,5},{8,10},{9,11},{10,... | collective-permute-start | bytes 884744 | tf_op jit(solution)/shard_map/ppermute | solution.py:20
  73.7 1.6 %collective-permute-start.19 = (bf16[288,512]{1,0:T(8,128)(2,1)S(1)}, bf16[288,512]{1,0:T(8,128)(2,1)S(1)}, u32[]{:S(2)}, u32[]{:S(2)}) collective-permute-start(bf16[288,512]{1,0:T(8,128)(2,1)S(1)} %get-tuple-element.61), channel_id=1, source_target_pairs={{0,4},{1,5},{2,6},{3,7},{4,0},{5,1},{6,2},{7,3},{8,12},{9,13},{10,... | collective-permute-start | bytes 884744 | tf_op jit(solution)/shard_map/ppermute | solution.py:20
  75.8 4.5 %collective-permute-done.21.refs_0_ = bf16[288,512]{1,0:T(8,128)(2,1)S(1)} collective-permute-done((bf16[288,512]{1,0:T(8,128)(2,1)S(1)}, bf16[288,512]{1,0:T(8,128)(2,1)S(1)}, u32[]{:S(2)}, u32[]{:S(2)}) %collective-permute-start.21) | collective-permute-done | bytes 294944 | tf_op jit(solution)/shard_map/ppermute | solution.py:20
  80.3 4.2 %collective-permute-done.22.refs_1_ = bf16[288,512]{1,0:T(8,128)(2,1)S(1)} collective-permute-done((bf16[288,512]{1,0:T(8,128)(2,1)S(1)}, bf16[288,512]{1,0:T(8,128)(2,1)S(1)}, u32[]{:S(2)}, u32[]{:S(2)}) %collective-permute-start.22) | collective-permute-done | bytes 294944 | tf_op jit(solution)/shard_map/ppermute | solution.py:20
  84.5 1.8 %grad_text.1 = (f32[256,512]{1,0:T(8,128)}, f32[8,256]{1,0:T(8,128)S(1)}, f32[1,1]{1,0:T(1,128)}) custom-call(f32[1,1]{1,0:T(1,128)S(6)} %mul.147.coef_ref, f32[264,512]{1,0:T(8,128)S(1)} %get-tuple-element.63.base, bf16[288,512]{1,0:T(8,128)(2,1)S(1)} %collective-permute-done.21.refs_0_, bf16[288,512]{1,0:T(8,128)(2,1)S(1)} %collective-permute-done.22.refs_1_), custom_call_target="tpu_custom_call" | custom-call | tf_op jit(solution)/shard_map/grad_text/pallas_call | solution.py:365
  86.4 2.5 %collective-permute-done.19.refs_1_ = bf16[288,512]{1,0:T(8,128)(2,1)S(1)} collective-permute-done((bf16[288,512]{1,0:T(8,128)(2,1)S(1)}, bf16[288,512]{1,0:T(8,128)(2,1)S(1)}, u32[]{:S(2)}, u32[]{:S(2)}) %collective-permute-start.19) | collective-permute-done | bytes 294944 | tf_op jit(solution)/shard_map/ppermute | solution.py:20
  88.9 2.3 %grad_image.1 = (f32[256,512]{1,0:T(8,128)}, f32[8,256]{1,0:T(8,128)}, f32[1,1]{1,0:T(1,128)}) custom-call(f32[1,1]{1,0:T(1,128)S(6)} %mul.147.coef_ref, f32[264,512]{1,0:T(8,128)S(1)} %get-tuple-element.59.base, bf16[288,512]{1,0:T(8,128)(2,1)S(1)} %collective-permute-done.18.refs_0_, bf16[288,512]{1,0:T(8,128)(2,1)S(1)} %collective-permute-done.19.refs_1_, ...), custom_call_target="tpu_custom_call" | custom-call | tf_op jit(solution)/shard_map/grad_image/pallas_call | solution.py:365
  (36 shorter events, 1.9 us)
Async XLA Ops:
  1.7 11.1 %collective-permute-start.6 = (bf16[256,512]{1,0:T(8,128)(2,1)S(1)}, bf16[256,512]{1,0:T(8,128)(2,1)S(1)}, u32[]{:S(2)}, u32[]{:S(2)}) collective-permute-start(bf16[256,512]{1,0:T(8,128)(2,1)S(1)} %convert_element_type.6.refs_0_), channel_id=1, source_target_pairs={{0,6},{1,7},{2,4},{3,5},{4,2},{5,3},{6,0},{7,1},{8,14},{9,15},{10,... | collective-permute-start | bytes 786440 | tf_op jit(solution)/shard_map/ppermute | solution.py:20
  5.7 11.9 %collective-permute-start.5 = (bf16[256,512]{1,0:T(8,128)(2,1)S(1)}, bf16[256,512]{1,0:T(8,128)(2,1)S(1)}, u32[]{:S(2)}, u32[]{:S(2)}) collective-permute-start(bf16[256,512]{1,0:T(8,128)(2,1)S(1)} %convert_element_type.6.refs_0_), channel_id=1, source_target_pairs={{0,4},{1,5},{2,6},{3,7},{4,0},{5,1},{6,2},{7,3},{8,12},{9,13},{10,... | collective-permute-start | bytes 786440 | tf_op jit(solution)/shard_map/ppermute | solution.py:20
  6.2 11.7 %collective-permute-start.4 = (bf16[256,512]{1,0:T(8,128)(2,1)S(1)}, bf16[256,512]{1,0:T(8,128)(2,1)S(1)}, u32[]{:S(2)}, u32[]{:S(2)}) collective-permute-start(bf16[256,512]{1,0:T(8,128)(2,1)S(1)} %convert_element_type.6.refs_0_), channel_id=1, source_target_pairs={{0,2},{1,3},{2,0},{3,1},{4,6},{5,7},{6,4},{7,5},{8,10},{9,11},{10,... | collective-permute-start | bytes 786440 | tf_op jit(solution)/shard_map/ppermute | solution.py:20
  7.4 11.3 %collective-permute-start.3 = (bf16[256,512]{1,0:T(8,128)(2,1)S(1)}, bf16[256,512]{1,0:T(8,128)(2,1)S(1)}, u32[]{:S(2)}, u32[]{:S(2)}) collective-permute-start(bf16[256,512]{1,0:T(8,128)(2,1)S(1)} %convert_element_type.7.refs_4_.refs_8_), channel_id=1, source_target_pairs={{0,24},{8,16},{16,8},{24,0},{1,25},{9,17},{17,9},{25,1},{2,26},{10... | collective-permute-start | bytes 786440 | tf_op jit(solution)/shard_map/ppermute | solution.py:20
  11.5 21.5 %collective-permute-start.2 = (bf16[256,512]{1,0:T(8,128)(2,1)S(1)}, bf16[256,512]{1,0:T(8,128)(2,1)S(1)}, u32[]{:S(2)}, u32[]{:S(2)}) collective-permute-start(bf16[256,512]{1,0:T(8,128)(2,1)S(1)} %convert_element_type.7.refs_4_.refs_8_), channel_id=1, source_target_pairs={{0,16},{8,24},{16,0},{24,8},{1,17},{9,25},{17,1},{25,9},{2,18},{10... | collective-permute-start | bytes 786440 | tf_op jit(solution)/shard_map/ppermute | solution.py:20
  12.8 20.1 %collective-permute-start.1 = (bf16[256,512]{1,0:T(8,128)(2,1)S(1)}, bf16[256,512]{1,0:T(8,128)(2,1)S(1)}, u32[]{:S(2)}, u32[]{:S(2)}) collective-permute-start(bf16[256,512]{1,0:T(8,128)(2,1)S(1)} %convert_element_type.7.refs_4_.refs_8_), channel_id=1, source_target_pairs={{0,8},{8,0},{16,24},{24,16},{1,9},{9,1},{17,25},{25,17},{2,10},{10... | collective-permute-start | bytes 786440 | tf_op jit(solution)/shard_map/ppermute | solution.py:20
  17.6 20.8 %collective-permute-start = (bf16[256,512]{1,0:T(8,128)(2,1)S(1)}, bf16[256,512]{1,0:T(8,128)(2,1)S(1)}, u32[]{:S(2)}, u32[]{:S(2)}) collective-permute-start(bf16[256,512]{1,0:T(8,128)(2,1)S(1)} %convert_element_type.6.refs_0_), channel_id=1, source_target_pairs={{0,1},{1,0},{2,3},{3,2},{4,5},{5,4},{6,7},{7,6},{8,9},{9,8},{10,11... | collective-permute-start | bytes 786440 | tf_op jit(solution)/shard_map/ppermute | solution.py:20
  32.9 5.5 %collective-permute-start.7 = (bf16[256,512]{1,0:T(8,128)(2,1)S(1)}, bf16[256,512]{1,0:T(8,128)(2,1)S(1)}, u32[]{:S(2)}, u32[]{:S(2)}) collective-permute-start(bf16[256,512]{1,0:T(8,128)(2,1)S(1)} %collective-permute-done.4.refs_1_), channel_id=1, source_target_pairs={{0,1},{1,0},{2,3},{3,2},{4,5},{5,4},{6,7},{7,6},{8,9},{9,8},{10,11... | collective-permute-start | bytes 786440 | tf_op jit(solution)/shard_map/ppermute | solution.py:20
  32.9 5.5 %collective-permute-start.8 = (bf16[256,512]{1,0:T(8,128)(2,1)S(1)}, bf16[256,512]{1,0:T(8,128)(2,1)S(1)}, u32[]{:S(2)}, u32[]{:S(2)}) collective-permute-start(bf16[256,512]{1,0:T(8,128)(2,1)S(1)} %collective-permute-done.5.refs_2_), channel_id=1, source_target_pairs={{0,1},{1,0},{2,3},{3,2},{4,5},{5,4},{6,7},{7,6},{8,9},{9,8},{10,11... | collective-permute-start | bytes 786440 | tf_op jit(solution)/shard_map/ppermute | solution.py:20
  33.4 5.0 %collective-permute-start.9 = (bf16[256,512]{1,0:T(8,128)(2,1)S(1)}, bf16[256,512]{1,0:T(8,128)(2,1)S(1)}, u32[]{:S(2)}, u32[]{:S(2)}) collective-permute-start(bf16[256,512]{1,0:T(8,128)(2,1)S(1)} %collective-permute-done.6.refs_3_), channel_id=1, source_target_pairs={{0,1},{1,0},{2,3},{3,2},{4,5},{5,4},{6,7},{7,6},{8,9},{9,8},{10,11... | collective-permute-start | bytes 786440 | tf_op jit(solution)/shard_map/ppermute | solution.py:20
  43.5 7.3 %collective-permute-start.12 = (f32[4,8,256]{2,1,0:T(8,128)S(1)}, f32[4,8,256]{2,1,0:T(8,128)S(1)}, u32[]{:S(2)}, u32[]{:S(2)}) collective-permute-start(f32[4,8,256]{2,1,0:T(8,128)S(1)} %get-tuple-element.45), channel_id=1, source_target_pairs={{0,6},{1,7},{2,4},{3,5},{4,2},{5,3},{6,0},{7,1},{8,14},{9,15},{10,... | collective-permute-start | bytes 98312 | tf_op jit(solution)/shard_map/ppermute | solution.py:20
  45.9 4.8 %collective-permute-start.11 = (f32[4,8,256]{2,1,0:T(8,128)S(1)}, f32[4,8,256]{2,1,0:T(8,128)S(1)}, u32[]{:S(2)}, u32[]{:S(2)}) collective-permute-start(f32[4,8,256]{2,1,0:T(8,128)S(1)} %get-tuple-element.45), channel_id=1, source_target_pairs={{0,4},{1,5},{2,6},{3,7},{4,0},{5,1},{6,2},{7,3},{8,12},{9,13},{10,... | collective-permute-start | bytes 98312 | tf_op jit(solution)/shard_map/ppermute | solution.py:20
  46.4 4.3 %collective-permute-start.10 = (f32[4,8,256]{2,1,0:T(8,128)S(1)}, f32[4,8,256]{2,1,0:T(8,128)S(1)}, u32[]{:S(2)}, u32[]{:S(2)}) collective-permute-start(f32[4,8,256]{2,1,0:T(8,128)S(1)} %get-tuple-element.45), channel_id=1, source_target_pairs={{0,2},{1,3},{2,0},{3,1},{4,6},{5,7},{6,4},{7,5},{8,10},{9,11},{10,... | collective-permute-start | bytes 98312 | tf_op jit(solution)/shard_map/ppermute | solution.py:20
  47.1 3.7 %collective-permute-start.13 = (f32[3,4,256]{2,1,0:T(4,128)S(1)}, f32[3,4,256]{2,1,0:T(4,128)S(1)}, u32[]{:S(2)}, u32[]{:S(2)}) collective-permute-start(f32[3,4,256]{2,1,0:T(4,128)S(1)} %get-tuple-element.44), channel_id=1, source_target_pairs={{0,8},{8,0},{16,24},{24,16},{1,9},{9,1},{17,25},{25,17},{2,10},{10... | collective-permute-start | bytes 36872 | tf_op jit(solution)/shard_map/ppermute | solution.py:20
  50.9 4.7 %collective-permute-start.14 = (f32[3,4,256]{2,1,0:T(4,128)S(1)}, f32[3,4,256]{2,1,0:T(4,128)S(1)}, u32[]{:S(2)}, u32[]{:S(2)}) collective-permute-start(f32[3,4,256]{2,1,0:T(4,128)S(1)} %pad_maximum_fusion.1), channel_id=1, source_target_pairs={{0,16},{8,24},{16,0},{24,8},{1,17},{9,25},{17,1},{25,9},{2,18},{10... | collective-permute-start | bytes 36872 | tf_op jit(solution)/shard_map/ppermute | solution.py:20
  51.9 3.7 %collective-permute-start.15 = (f32[4,8,256]{2,1,0:T(8,128)S(1)}, f32[4,8,256]{2,1,0:T(8,128)S(1)}, u32[]{:S(2)}, u32[]{:S(2)}) collective-permute-start(f32[4,8,256]{2,1,0:T(8,128)S(1)} %pad_maximum_fusion), channel_id=1, source_target_pairs={{0,1},{1,0},{2,3},{3,2},{4,5},{5,4},{6,7},{7,6},{8,9},{9,8},{10,11... | collective-permute-start | bytes 98312 | tf_op jit(solution)/shard_map/ppermute | solution.py:20
  58.1 9.3 %collective-permute-start.16 = (bf16[288,512]{1,0:T(8,128)(2,1)S(1)}, bf16[288,512]{1,0:T(8,128)(2,1)S(1)}, u32[]{:S(2)}, u32[]{:S(2)}) collective-permute-start(bf16[288,512]{1,0:T(8,128)(2,1)S(1)} %get-tuple-element.57), channel_id=1, source_target_pairs={{0,8},{8,0},{16,24},{24,16},{1,9},{9,1},{17,25},{25,17},{2,10},{10... | collective-permute-start | bytes 884744 | tf_op jit(solution)/shard_map/ppermute | solution.py:20
  65.3 5.8 %collective-permute-start.17 = (f32[4,264,512]{2,1,0:T(8,128)S(1)}, f32[4,264,512]{2,1,0:T(8,128)S(1)}, u32[]{:S(2)}, u32[]{:S(2)}) collective-permute-start(f32[4,264,512]{2,1,0:T(8,128)S(1)} %get-tuple-element.58), channel_id=1, source_target_pairs={{0,1},{1,0},{2,3},{3,2},{4,5},{5,4},{6,7},{7,6},{8,9},{9,8},{10,11... | collective-permute-start | bytes 6488072 | tf_op jit(solution)/shard_map/ppermute | solution.py:20
  65.4 15.0 %collective-permute-start.21 = (bf16[288,512]{1,0:T(8,128)(2,1)S(1)}, bf16[288,512]{1,0:T(8,128)(2,1)S(1)}, u32[]{:S(2)}, u32[]{:S(2)}) collective-permute-start(bf16[288,512]{1,0:T(8,128)(2,1)S(1)} %get-tuple-element.64), channel_id=1, source_target_pairs={{0,8},{8,0},{16,24},{24,16},{1,9},{9,1},{17,25},{25,17},{2,10},{10... | collective-permute-start | bytes 884744 | tf_op jit(solution)/shard_map/ppermute | solution.py:20
  68.1 16.4 %collective-permute-start.22 = (bf16[288,512]{1,0:T(8,128)(2,1)S(1)}, bf16[288,512]{1,0:T(8,128)(2,1)S(1)}, u32[]{:S(2)}, u32[]{:S(2)}) collective-permute-start(bf16[288,512]{1,0:T(8,128)(2,1)S(1)} %pack_text.1.refs_8_), channel_id=1, source_target_pairs={{0,16},{8,24},{16,0},{24,8},{1,17},{9,25},{17,1},{25,9},{2,18},{10... | collective-permute-start | bytes 884744 | tf_op jit(solution)/shard_map/ppermute | solution.py:20
  72.3 14.1 %collective-permute-start.18 = (bf16[288,512]{1,0:T(8,128)(2,1)S(1)}, bf16[288,512]{1,0:T(8,128)(2,1)S(1)}, u32[]{:S(2)}, u32[]{:S(2)}) collective-permute-start(bf16[288,512]{1,0:T(8,128)(2,1)S(1)} %get-tuple-element.60), channel_id=1, source_target_pairs={{0,2},{1,3},{2,0},{3,1},{4,6},{5,7},{6,4},{7,5},{8,10},{9,11},{10,... | collective-permute-start | bytes 884744 | tf_op jit(solution)/shard_map/ppermute | solution.py:20
  73.7 15.1 %collective-permute-start.19 = (bf16[288,512]{1,0:T(8,128)(2,1)S(1)}, bf16[288,512]{1,0:T(8,128)(2,1)S(1)}, u32[]{:S(2)}, u32[]{:S(2)}) collective-permute-start(bf16[288,512]{1,0:T(8,128)(2,1)S(1)} %get-tuple-element.61), channel_id=1, source_target_pairs={{0,4},{1,5},{2,6},{3,7},{4,0},{5,1},{6,2},{7,3},{8,12},{9,13},{10,... | collective-permute-start | bytes 884744 | tf_op jit(solution)/shard_map/ppermute | solution.py:20
  75.4 13.5 %collective-permute-start.20 = (bf16[288,512]{1,0:T(8,128)(2,1)S(1)}, bf16[288,512]{1,0:T(8,128)(2,1)S(1)}, u32[]{:S(2)}, u32[]{:S(2)}) collective-permute-start(bf16[288,512]{1,0:T(8,128)(2,1)S(1)} %get-tuple-element.62), channel_id=1, source_target_pairs={{0,6},{1,7},{2,4},{3,5},{4,2},{5,3},{6,0},{7,1},{8,14},{9,15},{10,... | collective-permute-start | bytes 884744 | tf_op jit(solution)/shard_map/ppermute | solution.py:20

commit v7 on v6

--- a/solution.py
+++ b/solution.py
@@ -21,99 +21,114 @@
 
 
 def gather_both(image, text, n_col, n_row):
+    line = n_row == 4
     images = [swap(image, "col", n_col, q) for q in range(2, n_col, 2)]
-    texts = [swap(text, "row", n_row, q) for q in range(1, n_row)]
-    odd = [swap(image, "col", n_col, 1)]
-    texts, images = lax.optimization_barrier((texts, images))
-    odd += [swap(i, "col", n_col, 1) for i in images]
-    return [image, *images], odd, [text, *texts]
+    texts = [swap(text, "row", n_row, q) for q in range(1, 3 if line else n_row)]
+    images, texts, text = lax.optimization_barrier((images, texts, text))
+    odd = [swap(i, "col", n_col, 1) for i in (image, *images)]
+    if line:
+        middle = lax.ppermute(text, "row", [(1, 2), (2, 1)])
+        return [image, *images], odd, [text, *texts], [middle, lax.ppermute(texts[1], "row", [(1, 0), (2, 3)])]
+    return [image, *images], odd, [text, *texts[:-1]], texts[-1:]
 
 
 def nt_dot(a, b):
     return lax.dot_general(a, b, (((1,), (1,)), ((), ())), preferred_element_type=jnp.float32)
 
 
-def stats_kernel(n_text, n_image, odd, block, coef_ref, place_ref, *refs):
-    pieces, refs = refs[:n_image], refs[n_image:]
-    texts = refs[:n_text]
-    before = refs[n_text:-9]
-    row_ref, col_ref, images, tile, row_max, col_max, col_sum, col_dot, row_diag = refs[-9:]
+def stats_kernel(first, n_text, block, coef_ref, place_ref, *refs):
+    texts, refs = refs[:n_text], refs[n_text:]
     coef = coef_ref[0, 0]
     r_place, c_place = place_ref[0, 0], place_ref[0, 1]
+    *refs, row_max, col_max, col_sum, col_dot, row_diag = refs
+    if first:
+        *refs, even, odd, row_ref, col_ref, tile = refs
+        halves = (even, odd)
+        each = len(refs) // 2
+        for i, piece in enumerate(refs):
+            at = (i % each) * block
+            halves[i // each][at : at + block, :] = piece[...]
+        before = None
+    else:
+        even, odd, *before, last, row_ref, col_ref, tile = refs
+        halves = (even, odd)
+        last[...] = functools.reduce(jnp.add, [text[...] for text in texts])
+        texts, n_text = [last], 1
     cols, rows = tile.shape
+    half = rows // 2
+    lead = 0 if first else col_ref.shape[1] - n_text
     col_max[...] = jnp.full(col_max.shape, -jnp.inf, jnp.float32)
     row_diag[...] = jnp.zeros(row_diag.shape, jnp.float32)
     n_col, n_row = row_ref.shape[1], col_ref.shape[1]
-    for j, piece in enumerate(pieces):
-        images[j * block : (j + 1) * block, :] = piece[...]
-
-    def products(j, carry):
-        at = pl.multiple_of(j * block, block)
-        image = images[pl.ds(at, block), :]
-        image_id = r_place * n_col + (c_place ^ (2 * j + odd))
-        top = None
-        for t in range(n_text):
-            part = pl.ds(t * block, block)
-            x = nt_dot(texts[t][...], image) * coef
-            tile[part, pl.ds(at, block)] = x
-            top_t = jnp.max(x, axis=0, keepdims=True)
-            top = top_t if top is None else jnp.maximum(top, top_t)
-            held = col_max[part, :]
-            for lane in range(0, block, LANES):
-                held = jnp.maximum(held, x[:, lane : lane + LANES])
-            col_max[part, :] = held
-        row_max[0:1, pl.ds(at, block)] = top
-        for t in range(n_text):
-
-            @pl.when(image_id == c_place * n_row + (r_place ^ t))
-            def _():
-                x = tile[pl.ds(t * block, block), pl.ds(at, block)]
-                down = lax.broadcasted_iota(jnp.int32, x.shape, 0)
-                across = lax.broadcasted_iota(jnp.int32, x.shape, 1)
-                row_diag[0:1, pl.ds(at, block)] = jnp.sum(
-                    jnp.where(down == across, x, 0.0), axis=0, keepdims=True
-                )
-
-        return carry
-
-    lax.fori_loop(0, rows // block, products, 0, unroll=4)
+
+    for which, images in enumerate(halves):
+
+        def products(j, carry):
+            image = images[pl.ds(pl.multiple_of(j * block, block), block), :]
+            at = pl.multiple_of(j * block + which * half, block)
+            image_id = r_place * n_col + (c_place ^ (2 * j + which))
+            top = None
+            for t in range(n_text):
+                part = pl.ds(t * block, block)
+                x = nt_dot(texts[t][...], image) * coef
+                tile[part, pl.ds(at, block)] = x
+                top_t = jnp.max(x, axis=0, keepdims=True)
+                top = top_t if top is None else jnp.maximum(top, top_t)
+                held = col_max[part, :]
+                for lane in range(0, block, LANES):
+                    held = jnp.maximum(held, x[:, lane : lane + LANES])
+                col_max[part, :] = held
+            row_max[0:1, pl.ds(at, block)] = top
+            for t in range(n_text):
+
+                @pl.when(image_id == c_place * n_row + (r_place ^ (lead + t)))
+                def _():
+                    x = tile[pl.ds(t * block, block), pl.ds(at, block)]
+                    down = lax.broadcasted_iota(jnp.int32, x.shape, 0)
+                    across = lax.broadcasted_iota(jnp.int32, x.shape, 1)
+                    row_diag[0:1, pl.ds(at, block)] = jnp.sum(
+                        jnp.where(down == across, x, 0.0), axis=0, keepdims=True
+                    )
+
+            return carry
+
+        lax.fori_loop(0, half // block, products, 0, unroll=4)
 
     col_max[...] = jnp.broadcast_to(
         jnp.max(col_max[...], axis=1, keepdims=True), col_max.shape
     )
-
-    lanes = range(0, rows, LANES)
-
-    def exponentials(i, acc):
-        part = pl.ds(pl.multiple_of(i * 8, 8), 8)
-        top = col_max[part, :]
-        total = dot = None
-        sums, dots = [], []
-        for n, lane in enumerate(lanes):
-            x = tile[part, lane : lane + LANES]
-            e = jnp.exp2(x - row_max[0:1, lane : lane + LANES])
-            sums.append(acc[0][n] + e)
-            dots.append(acc[1][n] + e * x)
-            e = jnp.exp2(x - top)
-            total = e if total is None else total + e
-            dot = e * x if dot is None else dot + e * x
-        col_sum[part, :] = total
-        col_dot[part, :] = dot
-        return tuple(sums), tuple(dots)
-
-    zeros = tuple(jnp.zeros((8, LANES), jnp.float32) for _ in lanes)
-    acc = lax.fori_loop(0, cols // 8, exponentials, (zeros, zeros), unroll=4)
+    sums = []
+    for which in range(2):
+        lanes = range(which * half, (which + 1) * half, LANES)
+
+        def exponentials(i, acc):
+            part = pl.ds(pl.multiple_of(i * 8, 8), 8)
+            top = col_max[part, :]
+            total = col_sum[part, :] if which else None
+            dot = col_dot[part, :] if which else None
+            new = [], []
+            for n, lane in enumerate(lanes):
+                x = tile[part, lane : lane + LANES]
+                e = jnp.exp2(x - row_max[0:1, lane : lane + LANES])
+                new[0].append(acc[0][n] + e)
+                new[1].append(acc[1][n] + e * x)
+                e = jnp.exp2(x - top)
+                total = e if total is None else total + e
+                dot = e * x if dot is None else dot + e * x
+            col_sum[part, :] = total
+            col_dot[part, :] = dot
+            return tuple(new[0]), tuple(new[1])
+
+        zeros = tuple(jnp.zeros((8, LANES), jnp.float32) for _ in lanes)
+        sums.append(lax.fori_loop(0, cols // 8, exponentials, (zeros, zeros), unroll=4))
 
     row_ids = lax.broadcasted_iota(jnp.int32, (n_col, block), 0)
-    if before:
-        placed = [before[0][i] for i in range(4)]
-    else:
-        placed = [jnp.zeros((n_col, block), jnp.float32)] * 4
-    for j in range(rows // block):
-        at = j * block
-        here = row_ids == (c_place ^ (2 * j + odd))
-        new = [row_max[0:1, at : at + block]]
-        for which in acc:
+    placed = [jnp.zeros((n_col, block), jnp.float32)] * 4
+    for q in range(n_col):
+        at = (q // 2) * block
+        here = row_ids == (c_place ^ q)
+        new = [row_max[0:1, at + (q % 2) * half : at + (q % 2) * half + block]]
+        for which in sums[q % 2]:
             new.append(
                 jnp.concatenate(
                     [
@@ -123,23 +138,62 @@
                     axis=1,
                 )
             )
-        new.append(row_diag[0:1, at : at + block])
+        new.append(row_diag[0:1, at + (q % 2) * half : at + (q % 2) * half + block])
         placed = [jnp.where(here, n, p) for n, p in zip(new, placed)]
+    if before:
+        placed = merged(placed, [before[0][i] for i in range(4)])
     for i in range(4):
         row_ref[i] = placed[i]
     row_ids = lax.broadcasted_iota(jnp.int32, (n_row, block), 0)
-    placed = [jnp.zeros((n_row, block), jnp.float32)] * 3
+    placed = [before[1][i] if before else jnp.zeros((n_row, block), jnp.float32) for i in range(3)]
     for t in range(n_text):
         part = pl.ds(t * block, block)
-        here = row_ids == (r_place ^ t)
+        here = row_ids == (r_place ^ (lead + t))
         new = [col_max[part, :].T[0:1, :]]
         for which in (col_sum, col_dot):
             new.append(jnp.sum(which[part, :].T, axis=0, keepdims=True))
         placed = [jnp.where(here, n, p) for n, p in zip(new, placed)]
-    if before:
-        placed = merged(placed, [before[1][i] for i in range(3)])
     for i in range(3):
         col_ref[i] = placed[i]
+
+
+def stats(coef, place, texts, images, before, n_col, n_row, keep):
+    block, width = texts[0].shape
+    first = not before
+    rows, cols = block * n_col, block * (len(texts) if first else 1)
+    vmem = pl.BlockSpec(memory_space=VMEM)
+    smem = pl.BlockSpec(memory_space=SMEM)
+    half = jax.ShapeDtypeStruct((rows // 2, width), jnp.bfloat16)
+    out_shape = [half, half] if first else [jax.ShapeDtypeStruct((block, width), jnp.bfloat16)]
+    out_shape += [
+        jax.ShapeDtypeStruct((4, n_col, block), jnp.float32),
+        jax.ShapeDtypeStruct((3, n_row, block), jnp.float32),
+    ]
+    scratch = [
+        VMEM((8, rows), jnp.float32),
+        VMEM((cols, LANES), jnp.float32),
+        VMEM((cols, LANES), jnp.float32),
+        VMEM((cols, LANES), jnp.float32),
+        VMEM((8, rows), jnp.float32),
+    ]
+    if keep:
+        out_shape.append(jax.ShapeDtypeStruct((cols, rows), jnp.float32))
+    else:
+        scratch.insert(0, VMEM((cols, rows), jnp.float32))
+    return pl.pallas_call(
+        functools.partial(stats_kernel, first, len(texts), block),
+        out_shape=tuple(out_shape),
+        in_specs=[smem, smem] + [vmem] * (len(texts) + len(images) + len(before)),
+        out_specs=(vmem,) * len(out_shape),
+        scratch_shapes=scratch,
+        compiler_params=pltpu.CompilerParams(
+            vmem_limit_bytes=(0 if keep else 4 * rows * cols) + 8 * 2**20
+        ),
+        cost_estimate=pl.CostEstimate(
+            flops=FLOPS * 2 * rows * cols * width, bytes_accessed=0, transcendentals=0
+        ),
+        name="stats" if first else "stats_last",
+    )(coef, place, *texts, *images, *before)
 
 
 def merged(a, b):
@@ -147,36 +201,6 @@
     wa, wb = jnp.exp2(a[0] - top), jnp.exp2(b[0] - top)
     out = [top] + [a[i] * wa + b[i] * wb for i in (1, 2)]
     return out + [a[i] + b[i] for i in range(3, len(a))]
-
-
-def stats(coef, place, images, texts, before, n_col):
-    block, width = texts[0].shape
-    rows, cols = block * len(images), block * len(texts)
-    vmem = pl.BlockSpec(memory_space=VMEM)
-    smem = pl.BlockSpec(memory_space=SMEM)
-    return pl.pallas_call(
-        functools.partial(stats_kernel, len(texts), len(images), 1 if before else 0, block),
-        out_shape=(
-            jax.ShapeDtypeStruct((4, n_col, block), jnp.float32),
-            jax.ShapeDtypeStruct((3, len(texts), block), jnp.float32),
-            jax.ShapeDtypeStruct((rows, width), jnp.bfloat16),
-        ),
-        in_specs=[smem, smem] + [vmem] * (len(images) + len(texts) + len(before)),
-        out_specs=(vmem,) * 3,
-        scratch_shapes=[
-            VMEM((cols, rows), jnp.float32),
-            VMEM((8, rows), jnp.float32),
-            VMEM((cols, LANES), jnp.float32),
-            VMEM((cols, LANES), jnp.float32),
-            VMEM((cols, LANES), jnp.float32),
-            VMEM((8, rows), jnp.float32),
-        ],
-        compiler_params=pltpu.CompilerParams(vmem_limit_bytes=4 * rows * cols + 8 * 2**20),
-        cost_estimate=pl.CostEstimate(
-            flops=FLOPS * 2 * rows * cols * width, bytes_accessed=0, transcendentals=0
-        ),
-        name="stats_odd" if before else "stats_even",
-    )(coef, place, *images, *texts, *before)
 
 
 def by_pairs(blocks, add):
@@ -381,7 +405,7 @@
     )(coef, base, *codes, *before)
 
 
-def text_block(text, t, halves, row_lse, col_lse, place_ref, scale_ref, coef_ref, extra, grad_ref, out_ref, total, powers):
+def text_block(text, tile, t, halves, row_lse, col_lse, place_ref, scale_ref, coef_ref, extra, grad_ref, out_ref, total, powers):
     coef = coef_ref[0, 0]
     r_place, c_place = place_ref[0, 0], place_ref[0, 1]
     half, width = halves[0].shape
@@ -397,14 +421,19 @@
     for which, images in enumerate(halves):
 
         def one(j, carry):
-            inner = nt_dot(text[...], images[pl.ds(pl.multiple_of(j * block, block), block), :])
             at = pl.multiple_of(j * block + which * half, block)
+            if tile is None:
+                image = images[pl.ds(pl.multiple_of(j * block, block), block), :]
+                xs = nt_dot(text[...], image) * coef
             column = c_place ^ (2 * j + which)
             same = jnp.where(r_place * n_col + column == text_id, 1.0, 0.0)
             lse = row_lse[pl.ds(column, 1), :]
             for r in range(0, size, step):
                 for lane in range(0, block, LANES):
-                    x = inner[r : r + step, lane : lane + LANES] * coef
+                    if tile is None:
+                        x = xs[r : r + step, lane : lane + LANES]
+                    else:
+                        x = tile[r : r + step, pl.ds(at + lane, LANES)]
                     e = jnp.exp2(x - lse[:, lane : lane + LANES]) + jnp.exp2(
                         x - col_lse_down[r : r + step, :]
                     )
@@ -439,15 +468,19 @@
     return scale * total
 
 
-def text_kernel(order, n_done, block, scale_ref, coef_ref, place_ref, *refs):
+def text_kernel(order, n_done, kept, block, scale_ref, coef_ref, place_ref, *refs):
     even, odd, row_lse, col_lse, row_extra, col_extra = refs[:6]
     n = len(order)
     texts, rest = refs[6 : 6 + n], refs[6 + n :]
+    if kept:
+        tile, rest = rest[0], rest[1:]
     done_grads, done_texts, rest = rest[:n_done], rest[n_done : 2 * n_done], rest[2 * n_done :]
     grads, outs = rest[:n], rest[n : 2 * n]
     for i, t in enumerate(order):
         text_block(
-            texts[i], t, (even, odd), row_lse, col_lse, place_ref, scale_ref, coef_ref, row_extra, grads[i], outs[i], *rest[-2:]
+            texts[i],
+            tile.at[pl.ds((t - min(order)) * block, block)] if kept else None,
+            t, (even, odd), row_lse, col_lse, place_ref, scale_ref, coef_ref, row_extra, grads[i], outs[i], *rest[-2:]
         )
     if n_done:
         far_ref = rest[2 * n]
@@ -467,7 +500,7 @@
         lax.fori_loop(0, half // block, one, 0)
 
 
-def text_grads(scale, coef, place, even, odd, row_lse, col_lse, row_extra, col_extra, texts, order, done):
+def text_grads(scale, coef, place, even, odd, row_lse, col_lse, row_extra, col_extra, texts, tile, order, done):
     half, width = even.shape
     block = texts[0].shape[0]
     n = len(order)
@@ -485,9 +518,10 @@
     if done:
         out_shape.append(jax.ShapeDtypeStruct((half // block, block + EXTRA, width), jnp.float32))
     operands = [even, odd, row_lse, col_lse, row_extra, col_extra, *[texts[t] for t in order]]
+    operands += tile
     operands += [done[t] for t in done] + [texts[t] for t in done]
     outs = pl.pallas_call(
-        functools.partial(text_kernel, tuple(order), len(done), block),
+        functools.partial(text_kernel, tuple(order), len(done), len(tile), block),
         out_shape=tuple(out_shape),
         in_specs=[smem] * 3 + [vmem] * len(operands),
         out_specs=(vmem,) * len(out_shape),
@@ -547,16 +581,23 @@
     scale = logit_scale.reshape(1, 1)
     coef = scale * LOG2E
     image_half, text_half = image_embeds.astype(jnp.bfloat16), text_embeds.astype(jnp.bfloat16)
-    even, odd, texts = gather_both(image_half, text_half, n_col, n_row)
-    row_parts, col_parts, even = stats(coef, place, even, texts, (), n_col)
-    row_parts, col_parts, odd = stats(coef, place, odd, texts, (row_parts, col_parts), n_col)
+    even, odd, texts, text_last = gather_both(image_half, text_half, n_col, n_row)
+    keep = 4 * n_row * n_col * block * block <= 16 * 2**20
+    even, odd, *before = stats(
+        coef, place, texts, (*even, *odd), (), n_col, n_row, keep
+    )
+    text_last, row_parts, col_parts, *tile_last = stats(
+        coef, place, text_last, (even, odd), before[:2], n_col, n_row, keep
+    )
+    texts = [*texts, text_last]
+    tile = before[2:]
     row_lse, row_extra, col_lse, col_extra = exchanged(row_parts, col_parts, n_col, n_row)
 
     held = (scale, coef, place, even, odd, row_lse, col_lse, row_extra, col_extra, texts)
     last = n_row - 1
-    grads, parts, _ = text_grads(*held, [last], {})
+    grads, parts, _ = text_grads(*held, tile_last, [last], {})
     received = swap(parts[last], "row", n_row, 1)
-    more, more_parts, far = text_grads(*held, list(range(last))[::-1], grads)
+    more, more_parts, far = text_grads(*held, tile, list(range(last))[::-1], grads)
     grads |= more
     parts |= more_parts
     codes = {q: [] for q in range(0, n_row, 2)}

time: 91.5 us -> 85.9 us (0.939)
  waiting for transfers between devices: 37.2 us -> 28.7 us
  starting transfers between devices: 22.6 us -> 25.4 us
    ppermute x23 -> x22, waiting for transfers between devices: 37.2 us -> 27.2 us  [swap(): return lax.ppermute(x, axis, [(i, i ^ q) for i in range(n)])]
    ppermute x0 -> x2, starting transfers between devices: none -> 1.96 us  [the longest x1 1.29 us: gather_both(): lax.ppermute(texts[1], 'row', [(1, 0), (2, 3)])]
    ppermute x0 -> x2, waiting for transfers between devices: none -> 1.51 us  [the longest x1 1.51 us: gather_both(): lax.ppermute(texts[1], 'row', [(1, 0), (2, 3)])]
    ppermute x23 -> x22, starting transfers between devices: 22.6 us -> 23.5 us  [swap(): return lax.ppermute(x, axis, [(i, i ^ q) for i in range(n)])]
  transfers between devices with their start and end apart: 23 -> 24, of which waited for: 10 -> 11; matrix products, arithmetic and copies ran while one was open for 1% -> 1% of each run, Pallas kernels for 19% -> 22%
where the time goes in v7:
time: 85.9 us; the launch traced here: 85.7 us
  waiting for transfers between devices  28.7 us (33%)
  Pallas kernels  27.5 us (32%)
  starting transfers between devices  25.4 us (30%)
  other arithmetic  2.43 us (3%)
  between operations  1.65 us (2%)
    ppermute x22, waiting for transfers between devices, swap(): return lax.ppermute(x, axis, [(i, i ^ q) for i in range(n)])  27.2 us
    ppermute x22, starting transfers between devices, swap(): return lax.ppermute(x, axis, [(i, i ^ q) for i in range(n)])  23.5 us
    pallas_call x2, Pallas kernels, stats(): pl.pallas_call(functools.partial(stats_kernel, first, len(texts), block),...  12.3 us
    pallas_call x2, Pallas kernels, text_grads(): pl.pallas_call(functools.partial(text_kernel, tuple(order), len(done), le...  7.33 us
    pallas_call x2, Pallas kernels, total_of(): pl.pallas_call(functools.partial(total_kernel, len(codes), in_order), out...  4.1 us
    pallas_call x1, Pallas kernels, image_grads(): pl.pallas_call(functools.partial(image_kernel, n_text, block), out_shape=...  1.94 us
  transfers between devices with their start and end apart: 24, of which 11 were waited for; matrix products, arithmetic and copies ran while one was open for 1% of the time, Pallas kernels for 22%

profile of v7, /device:TPU:0, one launch (start us, length us, event | category | flops | bytes accessed | tf_op | source)
XLA Modules:
  0.0 85.7 jit_solution(11311939798974409634)
XLA Ops:
  0.6 1.1 %convert_element_type.7.refs_0_.refs_8_.refs_4_ = bf16[256,512]{1,0:T(8,128)(2,1)S(1)} convert(f32[256,512]{1,0:T(8,128)} %param.4) | non-fusion elementwise | flops 131072 | bytes 786432 | tf_op jit(solution)/shard_map/convert_element_type | solution.py:583
  1.7 4.1 %collective-permute-start.4 = (bf16[256,512]{1,0:T(8,128)(2,1)S(1)}, bf16[256,512]{1,0:T(8,128)(2,1)S(1)}, u32[]{:S(2)}, u32[]{:S(2)}) collective-permute-start(bf16[256,512]{1,0:T(8,128)(2,1)S(1)} %convert_element_type.7.refs_0_.refs_8_.refs_4_), channel_id=1, source_target_pairs={{0,16},{8,24},{16,0},{24,8},{1,17},{9,25},{17,1},{25,9},{2,18},{10... | collective-permute-start | bytes 786440 | tf_op jit(solution)/shard_map/ppermute | solution.py:20
  5.8 1.6 %collective-permute-start.3 = (bf16[256,512]{1,0:T(8,128)(2,1)S(1)}, bf16[256,512]{1,0:T(8,128)(2,1)S(1)}, u32[]{:S(2)}, u32[]{:S(2)}) collective-permute-start(bf16[256,512]{1,0:T(8,128)(2,1)S(1)} %convert_element_type.7.refs_0_.refs_8_.refs_4_), channel_id=1, source_target_pairs={{0,8},{8,0},{16,24},{24,16},{1,9},{9,1},{17,25},{25,17},{2,10},{10... | collective-permute-start | bytes 786440 | tf_op jit(solution)/shard_map/ppermute | solution.py:20
  7.4 1.1 %convert_element_type.6.refs_3_ = bf16[256,512]{1,0:T(8,128)(2,1)S(1)} convert(f32[256,512]{1,0:T(8,128)} %param.3) | non-fusion elementwise | flops 131072 | bytes 786432 | tf_op jit(solution)/shard_map/convert_element_type | solution.py:583
  8.5 2.5 %collective-permute-start.2 = (bf16[256,512]{1,0:T(8,128)(2,1)S(1)}, bf16[256,512]{1,0:T(8,128)(2,1)S(1)}, u32[]{:S(2)}, u32[]{:S(2)}) collective-permute-start(bf16[256,512]{1,0:T(8,128)(2,1)S(1)} %convert_element_type.6.refs_3_), channel_id=1, source_target_pairs={{0,6},{1,7},{2,4},{3,5},{4,2},{5,3},{6,0},{7,1},{8,14},{9,15},{10,... | collective-permute-start | bytes 786440 | tf_op jit(solution)/shard_map/ppermute | solution.py:20
  12.0 5.8 %collective-permute-done.4.refs_2_.refs_6_ = bf16[256,512]{1,0:T(8,128)(2,1)S(1)} collective-permute-done((bf16[256,512]{1,0:T(8,128)(2,1)S(1)}, bf16[256,512]{1,0:T(8,128)(2,1)S(1)}, u32[]{:S(2)}, u32[]{:S(2)}) %collective-permute-start.4) | collective-permute-done | bytes 262176 | tf_op jit(solution)/shard_map/ppermute | solution.py:20
  18.7 3.8 %collective-permute-done.1.refs_5_ = bf16[256,512]{1,0:T(8,128)(2,1)S(1)} collective-permute-done((bf16[256,512]{1,0:T(8,128)(2,1)S(1)}, bf16[256,512]{1,0:T(8,128)(2,1)S(1)}, u32[]{:S(2)}, u32[]{:S(2)}) %collective-permute-start.1) | collective-permute-done | bytes 262176 | tf_op jit(solution)/shard_map/ppermute | solution.py:20
  24.6 1.3 %collective-permute-start.6 = (bf16[256,512]{1,0:T(8,128)(2,1)S(1)}, bf16[256,512]{1,0:T(8,128)(2,1)S(1)}, u32[]{:S(2)}, u32[]{:S(2)}) collective-permute-start(bf16[256,512]{1,0:T(8,128)(2,1)S(1)} %collective-permute-done.4.refs_2_.refs_6_), channel_id=1, source_target_pairs={{8,0},{16,24},{9,1},{17,25},{10,2},{18,26},{11,3},{19,27},{12,4},{... | collective-permute-start | bytes 786440 | tf_op jit(solution)/shard_map/ppermute | solution.py:31
  25.9 7.8 %stats.1 = (bf16[1024,512]{1,0:T(8,128)(2,1)S(1)}, bf16[1024,512]{1,0:T(8,128)(2,1)S(1)}, f32[4,8,256]{2,1,0:T(8,128)S(1)}, f32[3,4,256]{2,1,0:T(4,128)S(1)}, f32[768,2048]{1,0:T(8,128)S(1)}) custom-call(f32[1,1]{1,0:T(1,128)S(6)} %mul.147.coef_ref, s32[1,2]{1,0:T(1,128)S(1)} %add_bitcast_fusion.place_ref, ...), custom_call_target="tpu_custom_call" | custom-call | flops 32212254720 | tf_op jit(solution)/shard_map/stats/pallas_call | solution.py:183
  33.7 1.5 %collective-permute-done.6.refs_1_ = bf16[256,512]{1,0:T(8,128)(2,1)S(1)} collective-permute-done((bf16[256,512]{1,0:T(8,128)(2,1)S(1)}, bf16[256,512]{1,0:T(8,128)(2,1)S(1)}, u32[]{:S(2)}, u32[]{:S(2)}) %collective-permute-start.6) | collective-permute-done | bytes 262176 | tf_op jit(solution)/shard_map/ppermute | solution.py:31
  35.2 4.5 %stats_last.1 = (bf16[256,512]{1,0:T(8,128)(2,1)S(1)}, f32[4,8,256]{2,1,0:T(8,128)S(1)}, f32[3,4,256]{2,1,0:T(4,128)S(1)}, f32[256,2048]{1,0:T(8,128)S(1)}) custom-call(f32[1,1]{1,0:T(1,128)S(6)} %mul.147.coef_ref, s32[1,2]{1,0:T(1,128)S(1)} %add_bitcast_fusion.place_ref, bf16[256,512]{1,0:T(8,128)(2,1)S(1)} %collective-permute-done.5.refs_0_, ...), custom_call_target="tpu_custom_call" | custom-call | flops 10737418240 | tf_op jit(solution)/shard_map/stats_last/pallas_call | solution.py:183
  39.7 1.7 %collective-permute-start.13 = (f32[4,8,256]{2,1,0:T(8,128)S(1)}, f32[4,8,256]{2,1,0:T(8,128)S(1)}, u32[]{:S(2)}, u32[]{:S(2)}) collective-permute-start(f32[4,8,256]{2,1,0:T(8,128)S(1)} %get-tuple-element.50), channel_id=1, source_target_pairs={{0,6},{1,7},{2,4},{3,5},{4,2},{5,3},{6,0},{7,1},{8,14},{9,15},{10,... | collective-permute-start | bytes 98312 | tf_op jit(solution)/shard_map/ppermute | solution.py:20
  41.4 1.3 %collective-permute-start.12 = (f32[4,8,256]{2,1,0:T(8,128)S(1)}, f32[4,8,256]{2,1,0:T(8,128)S(1)}, u32[]{:S(2)}, u32[]{:S(2)}) collective-permute-start(f32[4,8,256]{2,1,0:T(8,128)S(1)} %get-tuple-element.50), channel_id=1, source_target_pairs={{0,4},{1,5},{2,6},{3,7},{4,0},{5,1},{6,2},{7,3},{8,12},{9,13},{10,... | collective-permute-start | bytes 98312 | tf_op jit(solution)/shard_map/ppermute | solution.py:20
  43.2 1.1 %collective-permute-start.14 = (f32[3,4,256]{2,1,0:T(4,128)S(1)}, f32[3,4,256]{2,1,0:T(4,128)S(1)}, u32[]{:S(2)}, u32[]{:S(2)}) collective-permute-start(f32[3,4,256]{2,1,0:T(4,128)S(1)} %get-tuple-element.49), channel_id=1, source_target_pairs={{0,8},{8,0},{16,24},{24,16},{1,9},{9,1},{17,25},{25,17},{2,10},{10... | collective-permute-start | bytes 36872 | tf_op jit(solution)/shard_map/ppermute | solution.py:20
  44.3 2.6 %collective-permute-done.14 = f32[3,4,256]{2,1,0:T(4,128)S(1)} collective-permute-done((f32[3,4,256]{2,1,0:T(4,128)S(1)}, f32[3,4,256]{2,1,0:T(4,128)S(1)}, u32[]{:S(2)}, u32[]{:S(2)}) %collective-permute-start.14) | collective-permute-done | bytes 12320 | tf_op jit(solution)/shard_map/ppermute | solution.py:20
  47.1 1.7 %collective-permute-start.15 = (f32[3,4,256]{2,1,0:T(4,128)S(1)}, f32[3,4,256]{2,1,0:T(4,128)S(1)}, u32[]{:S(2)}, u32[]{:S(2)}) collective-permute-start(f32[3,4,256]{2,1,0:T(4,128)S(1)} %pad_maximum_fusion.1), channel_id=1, source_target_pairs={{0,16},{8,24},{16,0},{24,8},{1,17},{9,25},{17,1},{25,9},{2,18},{10... | collective-permute-start | bytes 36872 | tf_op jit(solution)/shard_map/ppermute | solution.py:20
  48.7 3.0 %collective-permute-done.15 = f32[3,4,256]{2,1,0:T(4,128)S(1)} collective-permute-done((f32[3,4,256]{2,1,0:T(4,128)S(1)}, f32[3,4,256]{2,1,0:T(4,128)S(1)}, u32[]{:S(2)}, u32[]{:S(2)}) %collective-permute-start.15) | collective-permute-done | bytes 12320 | tf_op jit(solution)/shard_map/ppermute | solution.py:20
  51.9 1.8 %text_grads_1.1 = (bf16[256,2048]{1,0:T(8,128)(2,1)S(1)}, bf16[288,512]{1,0:T(8,128)(2,1)S(1)}) custom-call(f32[1,1]{1,0:T(1,128)} %bitcast.277.scale_ref, f32[1,1]{1,0:T(1,128)S(6)} %mul.147.coef_ref, s32[1,2]{1,0:T(1,128)S(1)} %add_bitcast_fusion.place_ref, bf16[1024,512]{1,0:T(8,128)(2,1)S(1)} %get-tuple-element.45.refs_2_.refs_0_, ...), custom_call_target="tpu_custom_call" | custom-call | flops 21474836480 | tf_op jit(solution)/shard_map/text_grads_1/pallas_call | solution.py:523
  53.7 1.1 %collective-permute-start.17 = (bf16[288,512]{1,0:T(8,128)(2,1)S(1)}, bf16[288,512]{1,0:T(8,128)(2,1)S(1)}, u32[]{:S(2)}, u32[]{:S(2)}) collective-permute-start(bf16[288,512]{1,0:T(8,128)(2,1)S(1)} %get-tuple-element.63), channel_id=1, source_target_pairs={{0,8},{8,0},{16,24},{24,16},{1,9},{9,1},{17,25},{25,17},{2,10},{10... | collective-permute-start | bytes 884744 | tf_op jit(solution)/shard_map/ppermute | solution.py:20
  54.8 5.5 %text_grads_3.1 = (bf16[256,2048]{1,0:T(8,128)(2,1)S(1)}, bf16[256,2048]{1,0:T(8,128)(2,1)S(1)}, bf16[256,2048]{1,0:T(8,128)(2,1)S(1)}, f32[264,512]{1,0:T(8,128...) custom-call(f32[1,1]{1,0:T(1,128)} %bitcast.278.scale_ref, ...), custom_call_target="tpu_custom_call" | custom-call | flops 64424509440 | tf_op jit(solution)/shard_map/text_grads_3/pallas_call | solution.py:523
  60.4 1.0 %collective-permute-start.22 = (bf16[288,512]{1,0:T(8,128)(2,1)S(1)}, bf16[288,512]{1,0:T(8,128)(2,1)S(1)}, u32[]{:S(2)}, u32[]{:S(2)}) collective-permute-start(bf16[288,512]{1,0:T(8,128)(2,1)S(1)} %get-tuple-element.70), channel_id=1, source_target_pairs={{0,8},{8,0},{16,24},{24,16},{1,9},{9,1},{17,25},{25,17},{2,10},{10... | collective-permute-start | bytes 884744 | tf_op jit(solution)/shard_map/ppermute | solution.py:20
  62.1 1.7 %collective-permute-start.23 = (bf16[288,512]{1,0:T(8,128)(2,1)S(1)}, bf16[288,512]{1,0:T(8,128)(2,1)S(1)}, u32[]{:S(2)}, u32[]{:S(2)}) collective-permute-start(bf16[288,512]{1,0:T(8,128)(2,1)S(1)} %pack_text.1.refs_8_), channel_id=1, source_target_pairs={{0,16},{8,24},{16,0},{24,8},{1,17},{9,25},{17,1},{25,9},{2,18},{10... | collective-permute-start | bytes 884744 | tf_op jit(solution)/shard_map/ppermute | solution.py:20
  63.8 1.9 %image_grads.1.near = f32[4,264,512]{2,1,0:T(8,128)S(1)} custom-call(f32[1,1]{1,0:T(1,128)} %bitcast.279.scale_ref, f32[4,256]{1,0:T(4,128)S(1)} %fusion.34.refs_5_.extra, bf16[256,2048]{1,0:T(8,128)(2,1)S(1)} %get-tuple-element.59.refs_0_, bf16[256,2048]{1,0:T(8,128)(2,1)S(1)} %get-tuple-element.60.refs_1_, ...), custom_call_target="tpu_custom_call" | custom-call | flops 21474836480 | tf_op jit(solution)/shard_map/image_grads/pallas_call | solution.py:562
  65.7 1.1 %pack_images.1 = (f32[264,512]{1,0:T(8,128)S(1)}, bf16[288,512]{1,0:T(8,128)(2,1)S(1)}, bf16[288,512]{1,0:T(8,128)(2,1)S(1)}, bf16[288,512]{1,0:T(8,128)(2,1)S(1)}) custom-call(f32[4,264,512]{2,1,0:T(8,128)S(1)} %image_grads.1.near, f32[4,264,512]{2,1,0:T(8,128)S(1)} %collective-permute-done.18.far), custom_call_target="tpu_custom_call" | custom-call | tf_op jit(solution)/shard_map/pack_images/pallas_call | solution.py:344
  66.9 1.6 %collective-permute-start.19 = (bf16[288,512]{1,0:T(8,128)(2,1)S(1)}, bf16[288,512]{1,0:T(8,128)(2,1)S(1)}, u32[]{:S(2)}, u32[]{:S(2)}) collective-permute-start(bf16[288,512]{1,0:T(8,128)(2,1)S(1)} %get-tuple-element.66), channel_id=1, source_target_pairs={{0,2},{1,3},{2,0},{3,1},{4,6},{5,7},{6,4},{7,5},{8,10},{9,11},{10,... | collective-permute-start | bytes 884744 | tf_op jit(solution)/shard_map/ppermute | solution.py:20
  68.4 0.7 collective-permute-start.20
  69.2 1.3 %collective-permute-start.21 = (bf16[288,512]{1,0:T(8,128)(2,1)S(1)}, bf16[288,512]{1,0:T(8,128)(2,1)S(1)}, u32[]{:S(2)}, u32[]{:S(2)}) collective-permute-start(bf16[288,512]{1,0:T(8,128)(2,1)S(1)} %get-tuple-element.68), channel_id=1, source_target_pairs={{0,6},{1,7},{2,4},{3,5},{4,2},{5,3},{6,0},{7,1},{8,14},{9,15},{10,... | collective-permute-start | bytes 884744 | tf_op jit(solution)/shard_map/ppermute | solution.py:20
  70.4 4.3 %collective-permute-done.22.refs_0_ = bf16[288,512]{1,0:T(8,128)(2,1)S(1)} collective-permute-done((bf16[288,512]{1,0:T(8,128)(2,1)S(1)}, bf16[288,512]{1,0:T(8,128)(2,1)S(1)}, u32[]{:S(2)}, u32[]{:S(2)}) %collective-permute-start.22) | collective-permute-done | bytes 294944 | tf_op jit(solution)/shard_map/ppermute | solution.py:20
  74.8 3.8 %collective-permute-done.23.refs_1_ = bf16[288,512]{1,0:T(8,128)(2,1)S(1)} collective-permute-done((bf16[288,512]{1,0:T(8,128)(2,1)S(1)}, bf16[288,512]{1,0:T(8,128)(2,1)S(1)}, u32[]{:S(2)}, u32[]{:S(2)}) %collective-permute-start.23) | collective-permute-done | bytes 294944 | tf_op jit(solution)/shard_map/ppermute | solution.py:20
  78.5 1.8 %grad_text.1 = (f32[256,512]{1,0:T(8,128)}, f32[8,256]{1,0:T(8,128)S(1)}, f32[1,1]{1,0:T(1,128)}) custom-call(f32[1,1]{1,0:T(1,128)S(6)} %mul.147.coef_ref, f32[264,512]{1,0:T(8,128)S(1)} %get-tuple-element.69.base, bf16[288,512]{1,0:T(8,128)(2,1)S(1)} %collective-permute-done.22.refs_0_, bf16[288,512]{1,0:T(8,128)(2,1)S(1)} %collective-permute-done.23.refs_1_), custom_call_target="tpu_custom_call" | custom-call | tf_op jit(solution)/shard_map/grad_text/pallas_call | solution.py:389
  80.4 2.9 %collective-permute-done.20.refs_1_ = bf16[288,512]{1,0:T(8,128)(2,1)S(1)} collective-permute-done((bf16[288,512]{1,0:T(8,128)(2,1)S(1)}, bf16[288,512]{1,0:T(8,128)(2,1)S(1)}, u32[]{:S(2)}, u32[]{:S(2)}) %collective-permute-start.20) | collective-permute-done | bytes 294944 | tf_op jit(solution)/shard_map/ppermute | solution.py:20
  83.3 2.3 %grad_image.1 = (f32[256,512]{1,0:T(8,128)}, f32[8,256]{1,0:T(8,128)}, f32[1,1]{1,0:T(1,128)}) custom-call(f32[1,1]{1,0:T(1,128)S(6)} %mul.147.coef_ref, f32[264,512]{1,0:T(8,128)S(1)} %get-tuple-element.65.base, bf16[288,512]{1,0:T(8,128)(2,1)S(1)} %collective-permute-done.19.refs_0_, bf16[288,512]{1,0:T(8,128)(2,1)S(1)} %collective-permute-done.20.refs_1_, ...), custom_call_target="tpu_custom_call" | custom-call | tf_op jit(solution)/shard_map/grad_image/pallas_call | solution.py:389
  (38 shorter events, 4.8 us)
Async XLA Ops:
  1.7 16.1 %collective-permute-start.4 = (bf16[256,512]{1,0:T(8,128)(2,1)S(1)}, bf16[256,512]{1,0:T(8,128)(2,1)S(1)}, u32[]{:S(2)}, u32[]{:S(2)}) collective-permute-start(bf16[256,512]{1,0:T(8,128)(2,1)S(1)} %convert_element_type.7.refs_0_.refs_8_.refs_4_), channel_id=1, source_target_pairs={{0,16},{8,24},{16,0},{24,8},{1,17},{9,25},{17,1},{25,9},{2,18},{10... | collective-permute-start | bytes 786440 | tf_op jit(solution)/shard_map/ppermute | solution.py:20
  5.8 12.2 %collective-permute-start.3 = (bf16[256,512]{1,0:T(8,128)(2,1)S(1)}, bf16[256,512]{1,0:T(8,128)(2,1)S(1)}, u32[]{:S(2)}, u32[]{:S(2)}) collective-permute-start(bf16[256,512]{1,0:T(8,128)(2,1)S(1)} %convert_element_type.7.refs_0_.refs_8_.refs_4_), channel_id=1, source_target_pairs={{0,8},{8,0},{16,24},{24,16},{1,9},{9,1},{17,25},{25,17},{2,10},{10... | collective-permute-start | bytes 786440 | tf_op jit(solution)/shard_map/ppermute | solution.py:20
  8.5 10.3 %collective-permute-start.2 = (bf16[256,512]{1,0:T(8,128)(2,1)S(1)}, bf16[256,512]{1,0:T(8,128)(2,1)S(1)}, u32[]{:S(2)}, u32[]{:S(2)}) collective-permute-start(bf16[256,512]{1,0:T(8,128)(2,1)S(1)} %convert_element_type.6.refs_3_), channel_id=1, source_target_pairs={{0,6},{1,7},{2,4},{3,5},{4,2},{5,3},{6,0},{7,1},{8,14},{9,15},{10,... | collective-permute-start | bytes 786440 | tf_op jit(solution)/shard_map/ppermute | solution.py:20
  11.0 11.6 %collective-permute-start.1 = (bf16[256,512]{1,0:T(8,128)(2,1)S(1)}, bf16[256,512]{1,0:T(8,128)(2,1)S(1)}, u32[]{:S(2)}, u32[]{:S(2)}) collective-permute-start(bf16[256,512]{1,0:T(8,128)(2,1)S(1)} %convert_element_type.6.refs_3_), channel_id=1, source_target_pairs={{0,4},{1,5},{2,6},{3,7},{4,0},{5,1},{6,2},{7,3},{8,12},{9,13},{10,... | collective-permute-start | bytes 786440 | tf_op jit(solution)/shard_map/ppermute | solution.py:20
  11.5 11.1 %collective-permute-start = (bf16[256,512]{1,0:T(8,128)(2,1)S(1)}, bf16[256,512]{1,0:T(8,128)(2,1)S(1)}, u32[]{:S(2)}, u32[]{:S(2)}) collective-permute-start(bf16[256,512]{1,0:T(8,128)(2,1)S(1)} %convert_element_type.6.refs_3_), channel_id=1, source_target_pairs={{0,2},{1,3},{2,0},{3,1},{4,6},{5,7},{6,4},{7,5},{8,10},{9,11},{10,... | collective-permute-start | bytes 786440 | tf_op jit(solution)/shard_map/ppermute | solution.py:20
  17.8 6.7 %collective-permute-start.7 = (bf16[256,512]{1,0:T(8,128)(2,1)S(1)}, bf16[256,512]{1,0:T(8,128)(2,1)S(1)}, u32[]{:S(2)}, u32[]{:S(2)}) collective-permute-start(bf16[256,512]{1,0:T(8,128)(2,1)S(1)} %convert_element_type.6.refs_3_), channel_id=1, source_target_pairs={{0,1},{1,0},{2,3},{3,2},{4,5},{5,4},{6,7},{7,6},{8,9},{9,8},{10,11... | collective-permute-start | bytes 786440 | tf_op jit(solution)/shard_map/ppermute | solution.py:20
  22.6 3.2 %collective-permute-start.8 = (bf16[256,512]{1,0:T(8,128)(2,1)S(1)}, bf16[256,512]{1,0:T(8,128)(2,1)S(1)}, u32[]{:S(2)}, u32[]{:S(2)}) collective-permute-start(bf16[256,512]{1,0:T(8,128)(2,1)S(1)} %collective-permute-done.refs_4_), channel_id=1, source_target_pairs={{0,1},{1,0},{2,3},{3,2},{4,5},{5,4},{6,7},{7,6},{8,9},{9,8},{10,11... | collective-permute-start | bytes 786440 | tf_op jit(solution)/shard_map/ppermute | solution.py:20
  22.6 3.2 %collective-permute-start.9 = (bf16[256,512]{1,0:T(8,128)(2,1)S(1)}, bf16[256,512]{1,0:T(8,128)(2,1)S(1)}, u32[]{:S(2)}, u32[]{:S(2)}) collective-permute-start(bf16[256,512]{1,0:T(8,128)(2,1)S(1)} %collective-permute-done.1.refs_5_), channel_id=1, source_target_pairs={{0,1},{1,0},{2,3},{3,2},{4,5},{5,4},{6,7},{7,6},{8,9},{9,8},{10,11... | collective-permute-start | bytes 786440 | tf_op jit(solution)/shard_map/ppermute | solution.py:20
  23.1 2.7 %collective-permute-start.10 = (bf16[256,512]{1,0:T(8,128)(2,1)S(1)}, bf16[256,512]{1,0:T(8,128)(2,1)S(1)}, u32[]{:S(2)}, u32[]{:S(2)}) collective-permute-start(bf16[256,512]{1,0:T(8,128)(2,1)S(1)} %collective-permute-done.2.refs_6_), channel_id=1, source_target_pairs={{0,1},{1,0},{2,3},{3,2},{4,5},{5,4},{6,7},{7,6},{8,9},{9,8},{10,11... | collective-permute-start | bytes 786440 | tf_op jit(solution)/shard_map/ppermute | solution.py:20
  23.9 9.8 %collective-permute-start.5 = (bf16[256,512]{1,0:T(8,128)(2,1)S(1)}, bf16[256,512]{1,0:T(8,128)(2,1)S(1)}, u32[]{:S(2)}, u32[]{:S(2)}) collective-permute-start(bf16[256,512]{1,0:T(8,128)(2,1)S(1)} %convert_element_type.7.refs_0_.refs_8_.refs_4_), channel_id=1, source_target_pairs={{8,16},{16,8},{9,17},{17,9},{10,18},{18,10},{11,19},{19,11},{12,20... | collective-permute-start | bytes 786440 | tf_op jit(solution)/shard_map/ppermute | solution.py:30
  24.6 10.6 %collective-permute-start.6 = (bf16[256,512]{1,0:T(8,128)(2,1)S(1)}, bf16[256,512]{1,0:T(8,128)(2,1)S(1)}, u32[]{:S(2)}, u32[]{:S(2)}) collective-permute-start(bf16[256,512]{1,0:T(8,128)(2,1)S(1)} %collective-permute-done.4.refs_2_.refs_6_), channel_id=1, source_target_pairs={{8,0},{16,24},{9,1},{17,25},{10,2},{18,26},{11,3},{19,27},{12,4},{... | collective-permute-start | bytes 786440 | tf_op jit(solution)/shard_map/ppermute | solution.py:31
  39.7 7.3 %collective-permute-start.13 = (f32[4,8,256]{2,1,0:T(8,128)S(1)}, f32[4,8,256]{2,1,0:T(8,128)S(1)}, u32[]{:S(2)}, u32[]{:S(2)}) collective-permute-start(f32[4,8,256]{2,1,0:T(8,128)S(1)} %get-tuple-element.50), channel_id=1, source_target_pairs={{0,6},{1,7},{2,4},{3,5},{4,2},{5,3},{6,0},{7,1},{8,14},{9,15},{10,... | collective-permute-start | bytes 98312 | tf_op jit(solution)/shard_map/ppermute | solution.py:20
  41.4 5.6 %collective-permute-start.12 = (f32[4,8,256]{2,1,0:T(8,128)S(1)}, f32[4,8,256]{2,1,0:T(8,128)S(1)}, u32[]{:S(2)}, u32[]{:S(2)}) collective-permute-start(f32[4,8,256]{2,1,0:T(8,128)S(1)} %get-tuple-element.50), channel_id=1, source_target_pairs={{0,4},{1,5},{2,6},{3,7},{4,0},{5,1},{6,2},{7,3},{8,12},{9,13},{10,... | collective-permute-start | bytes 98312 | tf_op jit(solution)/shard_map/ppermute | solution.py:20
  42.7 4.3 %collective-permute-start.11 = (f32[4,8,256]{2,1,0:T(8,128)S(1)}, f32[4,8,256]{2,1,0:T(8,128)S(1)}, u32[]{:S(2)}, u32[]{:S(2)}) collective-permute-start(f32[4,8,256]{2,1,0:T(8,128)S(1)} %get-tuple-element.50), channel_id=1, source_target_pairs={{0,2},{1,3},{2,0},{3,1},{4,6},{5,7},{6,4},{7,5},{8,10},{9,11},{10,... | collective-permute-start | bytes 98312 | tf_op jit(solution)/shard_map/ppermute | solution.py:20
  43.2 3.7 %collective-permute-start.14 = (f32[3,4,256]{2,1,0:T(4,128)S(1)}, f32[3,4,256]{2,1,0:T(4,128)S(1)}, u32[]{:S(2)}, u32[]{:S(2)}) collective-permute-start(f32[3,4,256]{2,1,0:T(4,128)S(1)} %get-tuple-element.49), channel_id=1, source_target_pairs={{0,8},{8,0},{16,24},{24,16},{1,9},{9,1},{17,25},{25,17},{2,10},{10... | collective-permute-start | bytes 36872 | tf_op jit(solution)/shard_map/ppermute | solution.py:20
  47.1 4.7 %collective-permute-start.15 = (f32[3,4,256]{2,1,0:T(4,128)S(1)}, f32[3,4,256]{2,1,0:T(4,128)S(1)}, u32[]{:S(2)}, u32[]{:S(2)}) collective-permute-start(f32[3,4,256]{2,1,0:T(4,128)S(1)} %pad_maximum_fusion.1), channel_id=1, source_target_pairs={{0,16},{8,24},{16,0},{24,8},{1,17},{9,25},{17,1},{25,9},{2,18},{10... | collective-permute-start | bytes 36872 | tf_op jit(solution)/shard_map/ppermute | solution.py:20
  48.7 3.1 %collective-permute-start.16 = (f32[4,8,256]{2,1,0:T(8,128)S(1)}, f32[4,8,256]{2,1,0:T(8,128)S(1)}, u32[]{:S(2)}, u32[]{:S(2)}) collective-permute-start(f32[4,8,256]{2,1,0:T(8,128)S(1)} %pad_maximum_fusion), channel_id=1, source_target_pairs={{0,1},{1,0},{2,3},{3,2},{4,5},{5,4},{6,7},{7,6},{8,9},{9,8},{10,11... | collective-permute-start | bytes 98312 | tf_op jit(solution)/shard_map/ppermute | solution.py:20
  53.7 7.8 %collective-permute-start.17 = (bf16[288,512]{1,0:T(8,128)(2,1)S(1)}, bf16[288,512]{1,0:T(8,128)(2,1)S(1)}, u32[]{:S(2)}, u32[]{:S(2)}) collective-permute-start(bf16[288,512]{1,0:T(8,128)(2,1)S(1)} %get-tuple-element.63), channel_id=1, source_target_pairs={{0,8},{8,0},{16,24},{24,16},{1,9},{9,1},{17,25},{25,17},{2,10},{10... | collective-permute-start | bytes 884744 | tf_op jit(solution)/shard_map/ppermute | solution.py:20
  60.3 5.4 %collective-permute-start.18 = (f32[4,264,512]{2,1,0:T(8,128)S(1)}, f32[4,264,512]{2,1,0:T(8,128)S(1)}, u32[]{:S(2)}, u32[]{:S(2)}) collective-permute-start(f32[4,264,512]{2,1,0:T(8,128)S(1)} %get-tuple-element.64), channel_id=1, source_target_pairs={{0,1},{1,0},{2,3},{3,2},{4,5},{5,4},{6,7},{7,6},{8,9},{9,8},{10,11... | collective-permute-start | bytes 6488072 | tf_op jit(solution)/shard_map/ppermute | solution.py:20
  60.4 14.3 %collective-permute-start.22 = (bf16[288,512]{1,0:T(8,128)(2,1)S(1)}, bf16[288,512]{1,0:T(8,128)(2,1)S(1)}, u32[]{:S(2)}, u32[]{:S(2)}) collective-permute-start(bf16[288,512]{1,0:T(8,128)(2,1)S(1)} %get-tuple-element.70), channel_id=1, source_target_pairs={{0,8},{8,0},{16,24},{24,16},{1,9},{9,1},{17,25},{25,17},{2,10},{10... | collective-permute-start | bytes 884744 | tf_op jit(solution)/shard_map/ppermute | solution.py:20
  62.1 16.4 %collective-permute-start.23 = (bf16[288,512]{1,0:T(8,128)(2,1)S(1)}, bf16[288,512]{1,0:T(8,128)(2,1)S(1)}, u32[]{:S(2)}, u32[]{:S(2)}) collective-permute-start(bf16[288,512]{1,0:T(8,128)(2,1)S(1)} %pack_text.1.refs_8_), channel_id=1, source_target_pairs={{0,16},{8,24},{16,0},{24,8},{1,17},{9,25},{17,1},{25,9},{2,18},{10... | collective-permute-start | bytes 884744 | tf_op jit(solution)/shard_map/ppermute | solution.py:20
  66.9 13.5 %collective-permute-start.19 = (bf16[288,512]{1,0:T(8,128)(2,1)S(1)}, bf16[288,512]{1,0:T(8,128)(2,1)S(1)}, u32[]{:S(2)}, u32[]{:S(2)}) collective-permute-start(bf16[288,512]{1,0:T(8,128)(2,1)S(1)} %get-tuple-element.66), channel_id=1, source_target_pairs={{0,2},{1,3},{2,0},{3,1},{4,6},{5,7},{6,4},{7,5},{8,10},{9,11},{10,... | collective-permute-start | bytes 884744 | tf_op jit(solution)/shard_map/ppermute | solution.py:20
  68.4 14.8 %collective-permute-start.20 = (bf16[288,512]{1,0:T(8,128)(2,1)S(1)}, bf16[288,512]{1,0:T(8,128)(2,1)S(1)}, u32[]{:S(2)}, u32[]{:S(2)}) collective-permute-start(bf16[288,512]{1,0:T(8,128)(2,1)S(1)} %get-tuple-element.67), channel_id=1, source_target_pairs={{0,4},{1,5},{2,6},{3,7},{4,0},{5,1},{6,2},{7,3},{8,12},{9,13},{10,... | collective-permute-start | bytes 884744 | tf_op jit(solution)/shard_map/ppermute | solution.py:20
  69.2 14.1 %collective-permute-start.21 = (bf16[288,512]{1,0:T(8,128)(2,1)S(1)}, bf16[288,512]{1,0:T(8,128)(2,1)S(1)}, u32[]{:S(2)}, u32[]{:S(2)}) collective-permute-start(bf16[288,512]{1,0:T(8,128)(2,1)S(1)} %get-tuple-element.68), channel_id=1, source_target_pairs={{0,6},{1,7},{2,4},{3,5},{4,2},{5,3},{6,0},{7,1},{8,14},{9,15},{10,... | collective-permute-start | bytes 884744 | tf_op jit(solution)/shard_map/ppermute | solution.py:20

commit v8 on v7

--- a/solution.py
+++ b/solution.py
@@ -66,7 +66,6 @@
         def products(j, carry):
             image = images[pl.ds(pl.multiple_of(j * block, block), block), :]
             at = pl.multiple_of(j * block + which * half, block)
-            image_id = r_place * n_col + (c_place ^ (2 * j + which))
             top = None
             for t in range(n_text):
                 part = pl.ds(t * block, block)
@@ -79,20 +78,23 @@
                     held = jnp.maximum(held, x[:, lane : lane + LANES])
                 col_max[part, :] = held
             row_max[0:1, pl.ds(at, block)] = top
-            for t in range(n_text):
-
-                @pl.when(image_id == c_place * n_row + (r_place ^ (lead + t)))
-                def _():
-                    x = tile[pl.ds(t * block, block), pl.ds(at, block)]
-                    down = lax.broadcasted_iota(jnp.int32, x.shape, 0)
-                    across = lax.broadcasted_iota(jnp.int32, x.shape, 1)
-                    row_diag[0:1, pl.ds(at, block)] = jnp.sum(
-                        jnp.where(down == across, x, 0.0), axis=0, keepdims=True
-                    )
-
             return carry
 
         lax.fori_loop(0, half // block, products, 0, unroll=4)
+
+    for t in range(n_text):
+        among = c_place * n_row + (r_place ^ (lead + t)) - r_place * n_col
+
+        @pl.when((among >= 0) & (among < n_col))
+        def _():
+            q = c_place ^ among
+            at = pl.multiple_of((q // 2) * block + (q % 2) * half, block)
+            x = tile[t * block : (t + 1) * block, pl.ds(at, block)]
+            down = lax.broadcasted_iota(jnp.int32, x.shape, 0)
+            across = lax.broadcasted_iota(jnp.int32, x.shape, 1)
+            row_diag[0:1, pl.ds(at, block)] = jnp.sum(
+                jnp.where(down == across, x, 0.0), axis=0, keepdims=True
+            )
 
     col_max[...] = jnp.broadcast_to(
         jnp.max(col_max[...], axis=1, keepdims=True), col_max.shape

time: 85.9 us -> 83.3 us (0.970)
  waiting for transfers between devices: 28.7 us -> 33 us
  Pallas kernels: 27.5 us -> 23.5 us
  starting transfers between devices: 25.4 us -> 22.5 us
    pallas_call x2, Pallas kernels: 12.3 us -> 8.27 us  [stats(): pl.pallas_call(functools.partial(stats_kernel, first, len(texts), block),...]
    ppermute x22, starting transfers between devices: 23.5 us -> 20.5 us  [swap(): return lax.ppermute(x, axis, [(i, i ^ q) for i in range(n)])]
    ppermute x1, waiting for transfers between devices: 1.51 us -> 3.64 us  [gather_both(): lax.ppermute(texts[1], 'row', [(1, 0), (2, 3)])]
    ppermute x22, waiting for transfers between devices: 27.2 us -> 29.3 us  [swap(): return lax.ppermute(x, axis, [(i, i ^ q) for i in range(n)])]
  transfers between devices with their start and end apart: 24 -> 24, of which waited for: 11 -> 11; matrix products, arithmetic and copies ran while one was open for 1% -> 1% of each run, Pallas kernels for 22% -> 20%
where the time goes in v8:
time: 83.3 us; the launch traced here: 83 us
  waiting for transfers between devices  33 us (40%)
  Pallas kernels  23.5 us (28%)
  starting transfers between devices  22.5 us (27%)
  other arithmetic  2.43 us (3%)
  between operations  1.65 us (2%)
    ppermute x22, waiting for transfers between devices, swap(): return lax.ppermute(x, axis, [(i, i ^ q) for i in range(n)])  29.3 us
    ppermute x22, starting transfers between devices, swap(): return lax.ppermute(x, axis, [(i, i ^ q) for i in range(n)])  20.5 us
    pallas_call x2, Pallas kernels, stats(): pl.pallas_call(functools.partial(stats_kernel, first, len(texts), block),...  8.27 us
    pallas_call x2, Pallas kernels, text_grads(): pl.pallas_call(functools.partial(text_kernel, tuple(order), len(done), le...  7.35 us
    pallas_call x2, Pallas kernels, total_of(): pl.pallas_call(functools.partial(total_kernel, len(codes), in_order), out...  4.1 us
    ppermute x1, waiting for transfers between devices, gather_both(): lax.ppermute(texts[1], 'row', [(1, 0), (2, 3)])  3.64 us
    pallas_call x1, Pallas kernels, image_grads(): pl.pallas_call(functools.partial(image_kernel, n_text, block), out_shape=...  1.95 us
  transfers between devices with their start and end apart: 24, of which 11 were waited for; matrix products, arithmetic and copies ran while one was open for 1% of the time, Pallas kernels for 20%

profile of v8, /device:TPU:0, one launch (start us, length us, event | category | flops | bytes accessed | tf_op | source)
XLA Modules:
  0.0 83.0 jit_solution(6534601678224694634)
XLA Ops:
  0.6 1.1 %convert_element_type.7.refs_0_.refs_8_.refs_4_ = bf16[256,512]{1,0:T(8,128)(2,1)S(1)} convert(f32[256,512]{1,0:T(8,128)} %param.4) | non-fusion elementwise | flops 131072 | bytes 786432 | tf_op jit(solution)/shard_map/convert_element_type | solution.py:585
  1.7 4.1 %collective-permute-start.4 = (bf16[256,512]{1,0:T(8,128)(2,1)S(1)}, bf16[256,512]{1,0:T(8,128)(2,1)S(1)}, u32[]{:S(2)}, u32[]{:S(2)}) collective-permute-start(bf16[256,512]{1,0:T(8,128)(2,1)S(1)} %convert_element_type.7.refs_0_.refs_8_.refs_4_), channel_id=1, source_target_pairs={{0,16},{8,24},{16,0},{24,8},{1,17},{9,25},{17,1},{25,9},{2,18},{10... | collective-permute-start | bytes 786440 | tf_op jit(solution)/shard_map/ppermute | solution.py:20
  5.8 1.6 %collective-permute-start.3 = (bf16[256,512]{1,0:T(8,128)(2,1)S(1)}, bf16[256,512]{1,0:T(8,128)(2,1)S(1)}, u32[]{:S(2)}, u32[]{:S(2)}) collective-permute-start(bf16[256,512]{1,0:T(8,128)(2,1)S(1)} %convert_element_type.7.refs_0_.refs_8_.refs_4_), channel_id=1, source_target_pairs={{0,8},{8,0},{16,24},{24,16},{1,9},{9,1},{17,25},{25,17},{2,10},{10... | collective-permute-start | bytes 786440 | tf_op jit(solution)/shard_map/ppermute | solution.py:20
  7.4 1.1 %convert_element_type.6.refs_3_ = bf16[256,512]{1,0:T(8,128)(2,1)S(1)} convert(f32[256,512]{1,0:T(8,128)} %param.3) | non-fusion elementwise | flops 131072 | bytes 786432 | tf_op jit(solution)/shard_map/convert_element_type | solution.py:585
  8.5 2.5 %collective-permute-start.2 = (bf16[256,512]{1,0:T(8,128)(2,1)S(1)}, bf16[256,512]{1,0:T(8,128)(2,1)S(1)}, u32[]{:S(2)}, u32[]{:S(2)}) collective-permute-start(bf16[256,512]{1,0:T(8,128)(2,1)S(1)} %convert_element_type.6.refs_3_), channel_id=1, source_target_pairs={{0,6},{1,7},{2,4},{3,5},{4,2},{5,3},{6,0},{7,1},{8,14},{9,15},{10,... | collective-permute-start | bytes 786440 | tf_op jit(solution)/shard_map/ppermute | solution.py:20
  12.0 5.8 %collective-permute-done.4.refs_2_.refs_6_ = bf16[256,512]{1,0:T(8,128)(2,1)S(1)} collective-permute-done((bf16[256,512]{1,0:T(8,128)(2,1)S(1)}, bf16[256,512]{1,0:T(8,128)(2,1)S(1)}, u32[]{:S(2)}, u32[]{:S(2)}) %collective-permute-start.4) | collective-permute-done | bytes 262176 | tf_op jit(solution)/shard_map/ppermute | solution.py:20
  18.0 0.7 collective-permute-done.2.refs_6_
  18.7 3.8 %collective-permute-done.1.refs_5_ = bf16[256,512]{1,0:T(8,128)(2,1)S(1)} collective-permute-done((bf16[256,512]{1,0:T(8,128)(2,1)S(1)}, bf16[256,512]{1,0:T(8,128)(2,1)S(1)}, u32[]{:S(2)}, u32[]{:S(2)}) %collective-permute-start.1) | collective-permute-done | bytes 262176 | tf_op jit(solution)/shard_map/ppermute | solution.py:20
  23.9 0.7 collective-permute-start.5
  24.6 1.3 %collective-permute-start.6 = (bf16[256,512]{1,0:T(8,128)(2,1)S(1)}, bf16[256,512]{1,0:T(8,128)(2,1)S(1)}, u32[]{:S(2)}, u32[]{:S(2)}) collective-permute-start(bf16[256,512]{1,0:T(8,128)(2,1)S(1)} %collective-permute-done.4.refs_2_.refs_6_), channel_id=1, source_target_pairs={{8,0},{16,24},{9,1},{17,25},{10,2},{18,26},{11,3},{19,27},{12,4},{... | collective-permute-start | bytes 786440 | tf_op jit(solution)/shard_map/ppermute | solution.py:31
  25.9 5.6 %stats.1 = (bf16[1024,512]{1,0:T(8,128)(2,1)S(1)}, bf16[1024,512]{1,0:T(8,128)(2,1)S(1)}, f32[4,8,256]{2,1,0:T(8,128)S(1)}, f32[3,4,256]{2,1,0:T(4,128)S(1)}, f32[768,2048]{1,0:T(8,128)S(1)}) custom-call(f32[1,1]{1,0:T(1,128)S(6)} %mul.147.coef_ref, s32[1,2]{1,0:T(1,128)S(1)} %add_bitcast_fusion.place_ref, ...), custom_call_target="tpu_custom_call" | custom-call | flops 32212254720 | tf_op jit(solution)/shard_map/stats/pallas_call | solution.py:185
  31.5 3.6 %collective-permute-done.6.refs_1_ = bf16[256,512]{1,0:T(8,128)(2,1)S(1)} collective-permute-done((bf16[256,512]{1,0:T(8,128)(2,1)S(1)}, bf16[256,512]{1,0:T(8,128)(2,1)S(1)}, u32[]{:S(2)}, u32[]{:S(2)}) %collective-permute-start.6) | collective-permute-done | bytes 262176 | tf_op jit(solution)/shard_map/ppermute | solution.py:31
  35.2 2.6 %stats_last.1 = (bf16[256,512]{1,0:T(8,128)(2,1)S(1)}, f32[4,8,256]{2,1,0:T(8,128)S(1)}, f32[3,4,256]{2,1,0:T(4,128)S(1)}, f32[256,2048]{1,0:T(8,128)S(1)}) custom-call(f32[1,1]{1,0:T(1,128)S(6)} %mul.147.coef_ref, s32[1,2]{1,0:T(1,128)S(1)} %add_bitcast_fusion.place_ref, bf16[256,512]{1,0:T(8,128)(2,1)S(1)} %collective-permute-done.5.refs_0_, ...), custom_call_target="tpu_custom_call" | custom-call | flops 10737418240 | tf_op jit(solution)/shard_map/stats_last/pallas_call | solution.py:185
  37.8 1.7 %collective-permute-start.13 = (f32[4,8,256]{2,1,0:T(8,128)S(1)}, f32[4,8,256]{2,1,0:T(8,128)S(1)}, u32[]{:S(2)}, u32[]{:S(2)}) collective-permute-start(f32[4,8,256]{2,1,0:T(8,128)S(1)} %get-tuple-element.50), channel_id=1, source_target_pairs={{0,6},{1,7},{2,4},{3,5},{4,2},{5,3},{6,0},{7,1},{8,14},{9,15},{10,... | collective-permute-start | bytes 98312 | tf_op jit(solution)/shard_map/ppermute | solution.py:20
  39.5 1.3 %collective-permute-start.12 = (f32[4,8,256]{2,1,0:T(8,128)S(1)}, f32[4,8,256]{2,1,0:T(8,128)S(1)}, u32[]{:S(2)}, u32[]{:S(2)}) collective-permute-start(f32[4,8,256]{2,1,0:T(8,128)S(1)} %get-tuple-element.50), channel_id=1, source_target_pairs={{0,4},{1,5},{2,6},{3,7},{4,0},{5,1},{6,2},{7,3},{8,12},{9,13},{10,... | collective-permute-start | bytes 98312 | tf_op jit(solution)/shard_map/ppermute | solution.py:20
  41.4 3.7 %collective-permute-done.14 = f32[3,4,256]{2,1,0:T(4,128)S(1)} collective-permute-done((f32[3,4,256]{2,1,0:T(4,128)S(1)}, f32[3,4,256]{2,1,0:T(4,128)S(1)}, u32[]{:S(2)}, u32[]{:S(2)}) %collective-permute-start.14) | collective-permute-done | bytes 12320 | tf_op jit(solution)/shard_map/ppermute | solution.py:20
  45.8 4.1 %collective-permute-done.15 = f32[3,4,256]{2,1,0:T(4,128)S(1)} collective-permute-done((f32[3,4,256]{2,1,0:T(4,128)S(1)}, f32[3,4,256]{2,1,0:T(4,128)S(1)}, u32[]{:S(2)}, u32[]{:S(2)}) %collective-permute-start.15) | collective-permute-done | bytes 12320 | tf_op jit(solution)/shard_map/ppermute | solution.py:20
  50.0 1.8 %text_grads_1.1 = (bf16[256,2048]{1,0:T(8,128)(2,1)S(1)}, bf16[288,512]{1,0:T(8,128)(2,1)S(1)}) custom-call(f32[1,1]{1,0:T(1,128)} %bitcast.277.scale_ref, f32[1,1]{1,0:T(1,128)S(6)} %mul.147.coef_ref, s32[1,2]{1,0:T(1,128)S(1)} %add_bitcast_fusion.place_ref, bf16[1024,512]{1,0:T(8,128)(2,1)S(1)} %get-tuple-element.45.refs_2_.refs_0_, ...), custom_call_target="tpu_custom_call" | custom-call | flops 21474836480 | tf_op jit(solution)/shard_map/text_grads_1/pallas_call | solution.py:525
  51.9 5.5 %text_grads_3.1 = (bf16[256,2048]{1,0:T(8,128)(2,1)S(1)}, bf16[256,2048]{1,0:T(8,128)(2,1)S(1)}, bf16[256,2048]{1,0:T(8,128)(2,1)S(1)}, f32[264,512]{1,0:T(8,128...) custom-call(f32[1,1]{1,0:T(1,128)} %bitcast.278.scale_ref, ...), custom_call_target="tpu_custom_call" | custom-call | flops 64424509440 | tf_op jit(solution)/shard_map/text_grads_3/pallas_call | solution.py:525
  57.5 2.1 %collective-permute-start.22 = (bf16[288,512]{1,0:T(8,128)(2,1)S(1)}, bf16[288,512]{1,0:T(8,128)(2,1)S(1)}, u32[]{:S(2)}, u32[]{:S(2)}) collective-permute-start(bf16[288,512]{1,0:T(8,128)(2,1)S(1)} %get-tuple-element.70), channel_id=1, source_target_pairs={{0,8},{8,0},{16,24},{24,16},{1,9},{9,1},{17,25},{25,17},{2,10},{10... | collective-permute-start | bytes 884744 | tf_op jit(solution)/shard_map/ppermute | solution.py:20
  59.6 0.7 pack_text.1.refs_8_
  60.3 0.9 %collective-permute-start.23 = (bf16[288,512]{1,0:T(8,128)(2,1)S(1)}, bf16[288,512]{1,0:T(8,128)(2,1)S(1)}, u32[]{:S(2)}, u32[]{:S(2)}) collective-permute-start(bf16[288,512]{1,0:T(8,128)(2,1)S(1)} %pack_text.1.refs_8_), channel_id=1, source_target_pairs={{0,16},{8,24},{16,0},{24,8},{1,17},{9,25},{17,1},{25,9},{2,18},{10... | collective-permute-start | bytes 884744 | tf_op jit(solution)/shard_map/ppermute | solution.py:20
  61.2 1.9 %image_grads.1.near = f32[4,264,512]{2,1,0:T(8,128)S(1)} custom-call(f32[1,1]{1,0:T(1,128)} %bitcast.279.scale_ref, f32[4,256]{1,0:T(4,128)S(1)} %fusion.34.refs_5_.extra, bf16[256,2048]{1,0:T(8,128)(2,1)S(1)} %get-tuple-element.59.refs_0_, bf16[256,2048]{1,0:T(8,128)(2,1)S(1)} %get-tuple-element.60.refs_1_, ...), custom_call_target="tpu_custom_call" | custom-call | flops 21474836480 | tf_op jit(solution)/shard_map/image_grads/pallas_call | solution.py:564
  63.1 1.1 %pack_images.1 = (f32[264,512]{1,0:T(8,128)S(1)}, bf16[288,512]{1,0:T(8,128)(2,1)S(1)}, bf16[288,512]{1,0:T(8,128)(2,1)S(1)}, bf16[288,512]{1,0:T(8,128)(2,1)S(1)}) custom-call(f32[4,264,512]{2,1,0:T(8,128)S(1)} %image_grads.1.near, f32[4,264,512]{2,1,0:T(8,128)S(1)} %collective-permute-done.18.far), custom_call_target="tpu_custom_call" | custom-call | tf_op jit(solution)/shard_map/pack_images/pallas_call | solution.py:346
  64.3 1.5 %collective-permute-start.19 = (bf16[288,512]{1,0:T(8,128)(2,1)S(1)}, bf16[288,512]{1,0:T(8,128)(2,1)S(1)}, u32[]{:S(2)}, u32[]{:S(2)}) collective-permute-start(bf16[288,512]{1,0:T(8,128)(2,1)S(1)} %get-tuple-element.66), channel_id=1, source_target_pairs={{0,2},{1,3},{2,0},{3,1},{4,6},{5,7},{6,4},{7,5},{8,10},{9,11},{10,... | collective-permute-start | bytes 884744 | tf_op jit(solution)/shard_map/ppermute | solution.py:20
  65.8 0.7 collective-permute-start.20
  66.5 1.3 %collective-permute-start.21 = (bf16[288,512]{1,0:T(8,128)(2,1)S(1)}, bf16[288,512]{1,0:T(8,128)(2,1)S(1)}, u32[]{:S(2)}, u32[]{:S(2)}) collective-permute-start(bf16[288,512]{1,0:T(8,128)(2,1)S(1)} %get-tuple-element.68), channel_id=1, source_target_pairs={{0,6},{1,7},{2,4},{3,5},{4,2},{5,3},{6,0},{7,1},{8,14},{9,15},{10,... | collective-permute-start | bytes 884744 | tf_op jit(solution)/shard_map/ppermute | solution.py:20
  67.8 4.2 %collective-permute-done.22.refs_0_ = bf16[288,512]{1,0:T(8,128)(2,1)S(1)} collective-permute-done((bf16[288,512]{1,0:T(8,128)(2,1)S(1)}, bf16[288,512]{1,0:T(8,128)(2,1)S(1)}, u32[]{:S(2)}, u32[]{:S(2)}) %collective-permute-start.22) | collective-permute-done | bytes 294944 | tf_op jit(solution)/shard_map/ppermute | solution.py:20
  72.1 4.6 %collective-permute-done.23.refs_1_ = bf16[288,512]{1,0:T(8,128)(2,1)S(1)} collective-permute-done((bf16[288,512]{1,0:T(8,128)(2,1)S(1)}, bf16[288,512]{1,0:T(8,128)(2,1)S(1)}, u32[]{:S(2)}, u32[]{:S(2)}) %collective-permute-start.23) | collective-permute-done | bytes 294944 | tf_op jit(solution)/shard_map/ppermute | solution.py:20
  76.7 1.8 %grad_text.1 = (f32[256,512]{1,0:T(8,128)}, f32[8,256]{1,0:T(8,128)S(1)}, f32[1,1]{1,0:T(1,128)}) custom-call(f32[1,1]{1,0:T(1,128)S(6)} %mul.147.coef_ref, f32[264,512]{1,0:T(8,128)S(1)} %get-tuple-element.69.base, bf16[288,512]{1,0:T(8,128)(2,1)S(1)} %collective-permute-done.22.refs_0_, bf16[288,512]{1,0:T(8,128)(2,1)S(1)} %collective-permute-done.23.refs_1_), custom_call_target="tpu_custom_call" | custom-call | tf_op jit(solution)/shard_map/grad_text/pallas_call | solution.py:391
  78.5 2.0 %collective-permute-done.20.refs_1_ = bf16[288,512]{1,0:T(8,128)(2,1)S(1)} collective-permute-done((bf16[288,512]{1,0:T(8,128)(2,1)S(1)}, bf16[288,512]{1,0:T(8,128)(2,1)S(1)}, u32[]{:S(2)}, u32[]{:S(2)}) %collective-permute-start.20) | collective-permute-done | bytes 294944 | tf_op jit(solution)/shard_map/ppermute | solution.py:20
  80.6 2.3 %grad_image.1 = (f32[256,512]{1,0:T(8,128)}, f32[8,256]{1,0:T(8,128)}, f32[1,1]{1,0:T(1,128)}) custom-call(f32[1,1]{1,0:T(1,128)S(6)} %mul.147.coef_ref, f32[264,512]{1,0:T(8,128)S(1)} %get-tuple-element.65.base, bf16[288,512]{1,0:T(8,128)(2,1)S(1)} %collective-permute-done.19.refs_0_, bf16[288,512]{1,0:T(8,128)(2,1)S(1)} %collective-permute-done.20.refs_1_, ...), custom_call_target="tpu_custom_call" | custom-call | tf_op jit(solution)/shard_map/grad_image/pallas_call | solution.py:391
  (38 shorter events, 3.4 us)
Async XLA Ops:
  1.7 16.1 %collective-permute-start.4 = (bf16[256,512]{1,0:T(8,128)(2,1)S(1)}, bf16[256,512]{1,0:T(8,128)(2,1)S(1)}, u32[]{:S(2)}, u32[]{:S(2)}) collective-permute-start(bf16[256,512]{1,0:T(8,128)(2,1)S(1)} %convert_element_type.7.refs_0_.refs_8_.refs_4_), channel_id=1, source_target_pairs={{0,16},{8,24},{16,0},{24,8},{1,17},{9,25},{17,1},{25,9},{2,18},{10... | collective-permute-start | bytes 786440 | tf_op jit(solution)/shard_map/ppermute | solution.py:20
  5.8 12.2 %collective-permute-start.3 = (bf16[256,512]{1,0:T(8,128)(2,1)S(1)}, bf16[256,512]{1,0:T(8,128)(2,1)S(1)}, u32[]{:S(2)}, u32[]{:S(2)}) collective-permute-start(bf16[256,512]{1,0:T(8,128)(2,1)S(1)} %convert_element_type.7.refs_0_.refs_8_.refs_4_), channel_id=1, source_target_pairs={{0,8},{8,0},{16,24},{24,16},{1,9},{9,1},{17,25},{25,17},{2,10},{10... | collective-permute-start | bytes 786440 | tf_op jit(solution)/shard_map/ppermute | solution.py:20
  8.5 10.3 %collective-permute-start.2 = (bf16[256,512]{1,0:T(8,128)(2,1)S(1)}, bf16[256,512]{1,0:T(8,128)(2,1)S(1)}, u32[]{:S(2)}, u32[]{:S(2)}) collective-permute-start(bf16[256,512]{1,0:T(8,128)(2,1)S(1)} %convert_element_type.6.refs_3_), channel_id=1, source_target_pairs={{0,6},{1,7},{2,4},{3,5},{4,2},{5,3},{6,0},{7,1},{8,14},{9,15},{10,... | collective-permute-start | bytes 786440 | tf_op jit(solution)/shard_map/ppermute | solution.py:20
  11.0 11.6 %collective-permute-start.1 = (bf16[256,512]{1,0:T(8,128)(2,1)S(1)}, bf16[256,512]{1,0:T(8,128)(2,1)S(1)}, u32[]{:S(2)}, u32[]{:S(2)}) collective-permute-start(bf16[256,512]{1,0:T(8,128)(2,1)S(1)} %convert_element_type.6.refs_3_), channel_id=1, source_target_pairs={{0,4},{1,5},{2,6},{3,7},{4,0},{5,1},{6,2},{7,3},{8,12},{9,13},{10,... | collective-permute-start | bytes 786440 | tf_op jit(solution)/shard_map/ppermute | solution.py:20
  11.5 11.1 %collective-permute-start = (bf16[256,512]{1,0:T(8,128)(2,1)S(1)}, bf16[256,512]{1,0:T(8,128)(2,1)S(1)}, u32[]{:S(2)}, u32[]{:S(2)}) collective-permute-start(bf16[256,512]{1,0:T(8,128)(2,1)S(1)} %convert_element_type.6.refs_3_), channel_id=1, source_target_pairs={{0,2},{1,3},{2,0},{3,1},{4,6},{5,7},{6,4},{7,5},{8,10},{9,11},{10,... | collective-permute-start | bytes 786440 | tf_op jit(solution)/shard_map/ppermute | solution.py:20
  17.8 6.7 %collective-permute-start.7 = (bf16[256,512]{1,0:T(8,128)(2,1)S(1)}, bf16[256,512]{1,0:T(8,128)(2,1)S(1)}, u32[]{:S(2)}, u32[]{:S(2)}) collective-permute-start(bf16[256,512]{1,0:T(8,128)(2,1)S(1)} %convert_element_type.6.refs_3_), channel_id=1, source_target_pairs={{0,1},{1,0},{2,3},{3,2},{4,5},{5,4},{6,7},{7,6},{8,9},{9,8},{10,11... | collective-permute-start | bytes 786440 | tf_op jit(solution)/shard_map/ppermute | solution.py:20
  22.6 3.2 %collective-permute-start.8 = (bf16[256,512]{1,0:T(8,128)(2,1)S(1)}, bf16[256,512]{1,0:T(8,128)(2,1)S(1)}, u32[]{:S(2)}, u32[]{:S(2)}) collective-permute-start(bf16[256,512]{1,0:T(8,128)(2,1)S(1)} %collective-permute-done.refs_4_), channel_id=1, source_target_pairs={{0,1},{1,0},{2,3},{3,2},{4,5},{5,4},{6,7},{7,6},{8,9},{9,8},{10,11... | collective-permute-start | bytes 786440 | tf_op jit(solution)/shard_map/ppermute | solution.py:20
  22.6 3.2 %collective-permute-start.9 = (bf16[256,512]{1,0:T(8,128)(2,1)S(1)}, bf16[256,512]{1,0:T(8,128)(2,1)S(1)}, u32[]{:S(2)}, u32[]{:S(2)}) collective-permute-start(bf16[256,512]{1,0:T(8,128)(2,1)S(1)} %collective-permute-done.1.refs_5_), channel_id=1, source_target_pairs={{0,1},{1,0},{2,3},{3,2},{4,5},{5,4},{6,7},{7,6},{8,9},{9,8},{10,11... | collective-permute-start | bytes 786440 | tf_op jit(solution)/shard_map/ppermute | solution.py:20
  23.1 2.7 %collective-permute-start.10 = (bf16[256,512]{1,0:T(8,128)(2,1)S(1)}, bf16[256,512]{1,0:T(8,128)(2,1)S(1)}, u32[]{:S(2)}, u32[]{:S(2)}) collective-permute-start(bf16[256,512]{1,0:T(8,128)(2,1)S(1)} %collective-permute-done.2.refs_6_), channel_id=1, source_target_pairs={{0,1},{1,0},{2,3},{3,2},{4,5},{5,4},{6,7},{7,6},{8,9},{9,8},{10,11... | collective-permute-start | bytes 786440 | tf_op jit(solution)/shard_map/ppermute | solution.py:20
  23.9 7.6 %collective-permute-start.5 = (bf16[256,512]{1,0:T(8,128)(2,1)S(1)}, bf16[256,512]{1,0:T(8,128)(2,1)S(1)}, u32[]{:S(2)}, u32[]{:S(2)}) collective-permute-start(bf16[256,512]{1,0:T(8,128)(2,1)S(1)} %convert_element_type.7.refs_0_.refs_8_.refs_4_), channel_id=1, source_target_pairs={{8,16},{16,8},{9,17},{17,9},{10,18},{18,10},{11,19},{19,11},{12,20... | collective-permute-start | bytes 786440 | tf_op jit(solution)/shard_map/ppermute | solution.py:30
  24.6 10.6 %collective-permute-start.6 = (bf16[256,512]{1,0:T(8,128)(2,1)S(1)}, bf16[256,512]{1,0:T(8,128)(2,1)S(1)}, u32[]{:S(2)}, u32[]{:S(2)}) collective-permute-start(bf16[256,512]{1,0:T(8,128)(2,1)S(1)} %collective-permute-done.4.refs_2_.refs_6_), channel_id=1, source_target_pairs={{8,0},{16,24},{9,1},{17,25},{10,2},{18,26},{11,3},{19,27},{12,4},{... | collective-permute-start | bytes 786440 | tf_op jit(solution)/shard_map/ppermute | solution.py:31
  37.8 7.3 %collective-permute-start.13 = (f32[4,8,256]{2,1,0:T(8,128)S(1)}, f32[4,8,256]{2,1,0:T(8,128)S(1)}, u32[]{:S(2)}, u32[]{:S(2)}) collective-permute-start(f32[4,8,256]{2,1,0:T(8,128)S(1)} %get-tuple-element.50), channel_id=1, source_target_pairs={{0,6},{1,7},{2,4},{3,5},{4,2},{5,3},{6,0},{7,1},{8,14},{9,15},{10,... | collective-permute-start | bytes 98312 | tf_op jit(solution)/shard_map/ppermute | solution.py:20
  39.5 5.6 %collective-permute-start.12 = (f32[4,8,256]{2,1,0:T(8,128)S(1)}, f32[4,8,256]{2,1,0:T(8,128)S(1)}, u32[]{:S(2)}, u32[]{:S(2)}) collective-permute-start(f32[4,8,256]{2,1,0:T(8,128)S(1)} %get-tuple-element.50), channel_id=1, source_target_pairs={{0,4},{1,5},{2,6},{3,7},{4,0},{5,1},{6,2},{7,3},{8,12},{9,13},{10,... | collective-permute-start | bytes 98312 | tf_op jit(solution)/shard_map/ppermute | solution.py:20
  40.8 4.3 %collective-permute-start.11 = (f32[4,8,256]{2,1,0:T(8,128)S(1)}, f32[4,8,256]{2,1,0:T(8,128)S(1)}, u32[]{:S(2)}, u32[]{:S(2)}) collective-permute-start(f32[4,8,256]{2,1,0:T(8,128)S(1)} %get-tuple-element.50), channel_id=1, source_target_pairs={{0,2},{1,3},{2,0},{3,1},{4,6},{5,7},{6,4},{7,5},{8,10},{9,11},{10,... | collective-permute-start | bytes 98312 | tf_op jit(solution)/shard_map/ppermute | solution.py:20
  41.4 3.7 %collective-permute-start.14 = (f32[3,4,256]{2,1,0:T(4,128)S(1)}, f32[3,4,256]{2,1,0:T(4,128)S(1)}, u32[]{:S(2)}, u32[]{:S(2)}) collective-permute-start(f32[3,4,256]{2,1,0:T(4,128)S(1)} %get-tuple-element.49), channel_id=1, source_target_pairs={{0,8},{8,0},{16,24},{24,16},{1,9},{9,1},{17,25},{25,17},{2,10},{10... | collective-permute-start | bytes 36872 | tf_op jit(solution)/shard_map/ppermute | solution.py:20
  45.2 4.7 %collective-permute-start.15 = (f32[3,4,256]{2,1,0:T(4,128)S(1)}, f32[3,4,256]{2,1,0:T(4,128)S(1)}, u32[]{:S(2)}, u32[]{:S(2)}) collective-permute-start(f32[3,4,256]{2,1,0:T(4,128)S(1)} %pad_maximum_fusion.1), channel_id=1, source_target_pairs={{0,16},{8,24},{16,0},{24,8},{1,17},{9,25},{17,1},{25,9},{2,18},{10... | collective-permute-start | bytes 36872 | tf_op jit(solution)/shard_map/ppermute | solution.py:20
  45.8 4.2 %collective-permute-start.16 = (f32[4,8,256]{2,1,0:T(8,128)S(1)}, f32[4,8,256]{2,1,0:T(8,128)S(1)}, u32[]{:S(2)}, u32[]{:S(2)}) collective-permute-start(f32[4,8,256]{2,1,0:T(8,128)S(1)} %pad_maximum_fusion), channel_id=1, source_target_pairs={{0,1},{1,0},{2,3},{3,2},{4,5},{5,4},{6,7},{7,6},{8,9},{9,8},{10,11... | collective-permute-start | bytes 98312 | tf_op jit(solution)/shard_map/ppermute | solution.py:20
  51.8 7.8 %collective-permute-start.17 = (bf16[288,512]{1,0:T(8,128)(2,1)S(1)}, bf16[288,512]{1,0:T(8,128)(2,1)S(1)}, u32[]{:S(2)}, u32[]{:S(2)}) collective-permute-start(bf16[288,512]{1,0:T(8,128)(2,1)S(1)} %get-tuple-element.63), channel_id=1, source_target_pairs={{0,8},{8,0},{16,24},{24,16},{1,9},{9,1},{17,25},{25,17},{2,10},{10... | collective-permute-start | bytes 884744 | tf_op jit(solution)/shard_map/ppermute | solution.py:20
  57.4 5.7 %collective-permute-start.18 = (f32[4,264,512]{2,1,0:T(8,128)S(1)}, f32[4,264,512]{2,1,0:T(8,128)S(1)}, u32[]{:S(2)}, u32[]{:S(2)}) collective-permute-start(f32[4,264,512]{2,1,0:T(8,128)S(1)} %get-tuple-element.64), channel_id=1, source_target_pairs={{0,1},{1,0},{2,3},{3,2},{4,5},{5,4},{6,7},{7,6},{8,9},{9,8},{10,11... | collective-permute-start | bytes 6488072 | tf_op jit(solution)/shard_map/ppermute | solution.py:20
  57.5 14.6 %collective-permute-start.22 = (bf16[288,512]{1,0:T(8,128)(2,1)S(1)}, bf16[288,512]{1,0:T(8,128)(2,1)S(1)}, u32[]{:S(2)}, u32[]{:S(2)}) collective-permute-start(bf16[288,512]{1,0:T(8,128)(2,1)S(1)} %get-tuple-element.70), channel_id=1, source_target_pairs={{0,8},{8,0},{16,24},{24,16},{1,9},{9,1},{17,25},{25,17},{2,10},{10... | collective-permute-start | bytes 884744 | tf_op jit(solution)/shard_map/ppermute | solution.py:20
  60.3 16.4 %collective-permute-start.23 = (bf16[288,512]{1,0:T(8,128)(2,1)S(1)}, bf16[288,512]{1,0:T(8,128)(2,1)S(1)}, u32[]{:S(2)}, u32[]{:S(2)}) collective-permute-start(bf16[288,512]{1,0:T(8,128)(2,1)S(1)} %pack_text.1.refs_8_), channel_id=1, source_target_pairs={{0,16},{8,24},{16,0},{24,8},{1,17},{9,25},{17,1},{25,9},{2,18},{10... | collective-permute-start | bytes 884744 | tf_op jit(solution)/shard_map/ppermute | solution.py:20
  64.3 14.3 %collective-permute-start.19 = (bf16[288,512]{1,0:T(8,128)(2,1)S(1)}, bf16[288,512]{1,0:T(8,128)(2,1)S(1)}, u32[]{:S(2)}, u32[]{:S(2)}) collective-permute-start(bf16[288,512]{1,0:T(8,128)(2,1)S(1)} %get-tuple-element.66), channel_id=1, source_target_pairs={{0,2},{1,3},{2,0},{3,1},{4,6},{5,7},{6,4},{7,5},{8,10},{9,11},{10,... | collective-permute-start | bytes 884744 | tf_op jit(solution)/shard_map/ppermute | solution.py:20
  65.8 14.8 %collective-permute-start.20 = (bf16[288,512]{1,0:T(8,128)(2,1)S(1)}, bf16[288,512]{1,0:T(8,128)(2,1)S(1)}, u32[]{:S(2)}, u32[]{:S(2)}) collective-permute-start(bf16[288,512]{1,0:T(8,128)(2,1)S(1)} %get-tuple-element.67), channel_id=1, source_target_pairs={{0,4},{1,5},{2,6},{3,7},{4,0},{5,1},{6,2},{7,3},{8,12},{9,13},{10,... | collective-permute-start | bytes 884744 | tf_op jit(solution)/shard_map/ppermute | solution.py:20
  66.5 14.1 %collective-permute-start.21 = (bf16[288,512]{1,0:T(8,128)(2,1)S(1)}, bf16[288,512]{1,0:T(8,128)(2,1)S(1)}, u32[]{:S(2)}, u32[]{:S(2)}) collective-permute-start(bf16[288,512]{1,0:T(8,128)(2,1)S(1)} %get-tuple-element.68), channel_id=1, source_target_pairs={{0,6},{1,7},{2,4},{3,5},{4,2},{5,3},{6,0},{7,1},{8,14},{9,15},{10,... | collective-permute-start | bytes 884744 | tf_op jit(solution)/shard_map/ppermute | solution.py:20

commit v9 on v8

--- a/solution.py
+++ b/solution.py
@@ -21,15 +21,19 @@
 
 
 def gather_both(image, text, n_col, n_row):
-    line = n_row == 4
     images = [swap(image, "col", n_col, q) for q in range(2, n_col, 2)]
-    texts = [swap(text, "row", n_row, q) for q in range(1, 3 if line else n_row)]
-    images, texts, text = lax.optimization_barrier((images, texts, text))
+    if n_row == 4:
+        ends = lax.ppermute(text, "row", [(0, 3), (3, 0)])
+        texts = [swap(text, "row", n_row, q) for q in (1, 2)]
+        images, texts, ends, text = lax.optimization_barrier((images, texts, ends, text))
+        last = [ends, lax.ppermute(text, "row", [(1, 2), (2, 1)])]
+    else:
+        texts = [swap(text, "row", n_row, q) for q in range(1, n_row)]
+        images, texts = lax.optimization_barrier((images, texts))
+        *texts, last = texts
+        last = [last]
     odd = [swap(i, "col", n_col, 1) for i in (image, *images)]
-    if line:
-        middle = lax.ppermute(text, "row", [(1, 2), (2, 1)])
-        return [image, *images], odd, [text, *texts], [middle, lax.ppermute(texts[1], "row", [(1, 0), (2, 3)])]
-    return [image, *images], odd, [text, *texts[:-1]], texts[-1:]
+    return [image, *images], odd, [text, *texts], last
 
 
 def nt_dot(a, b):
@@ -217,14 +221,16 @@
 
 
 def exchanged(row_parts, col_parts, n_col, n_row):
-    rows = [swap(row_parts, "col", n_col, q) for q in range(2, n_col, 2)]
-    cols = swap(col_parts, "row", n_row, 1)
-    rows, cols = lax.optimization_barrier((rows, cols))
-    rows = by_pairs([list(x) for x in (row_parts, *rows)], merged)
-    cols = merged(list(col_parts), list(cols))
-    for b in range(1, n_row.bit_length() - 1):
-        cols = merged(cols, list(swap(jnp.stack(cols), "row", n_row, 1 << b)))
-    rows = merged(rows, list(swap(jnp.stack(rows), "col", n_col, 1)))
+    rows, cols = list(row_parts), list(col_parts)
+    row_bits = [1 << b for b in range(1, n_col.bit_length() - 1)] + [1]
+    col_bits = [1 << b for b in range(n_row.bit_length() - 1)]
+    for n, bit in enumerate(row_bits):
+        received = swap(jnp.stack(rows), "col", n_col, bit)
+        if n < len(col_bits):
+            other = swap(jnp.stack(cols), "row", n_row, col_bits[n])
+            received, other = lax.optimization_barrier((received, other))
+            cols = merged(cols, list(other))
+        rows = merged(rows, list(received))
     return *lse_and_mean(rows), *lse_and_mean(cols)
 
 
@@ -349,7 +355,7 @@
         in_specs=[vmem] * 2,
         out_specs=(vmem,) * n,
         scratch_shapes=[VMEM((n - 1, size, LANES), jnp.float32)],
-        compiler_params=pltpu.CompilerParams(vmem_limit_bytes=6 * 2**20),
+        compiler_params=pltpu.CompilerParams(vmem_limit_bytes=(4 + 2 * n) * 2**20),
         name="pack_images",
     )(near, far)
     return own, codes
@@ -407,18 +413,16 @@
     )(coef, base, *codes, *before)
 
 
-def text_block(text, tile, t, halves, row_lse, col_lse, place_ref, scale_ref, coef_ref, extra, grad_ref, out_ref, total, powers):
+def logit_block(text, tile, t, halves, row_lse, col_lse, place_ref, coef_ref, grad_ref):
     coef = coef_ref[0, 0]
     r_place, c_place = place_ref[0, 0], place_ref[0, 1]
-    half, width = halves[0].shape
+    half = halves[0].shape[0]
     n_col, n_row = row_lse.shape[0], col_lse.shape[0]
-    size = text.shape[0]
-    block = size
+    size = block = text.shape[0]
     col_lse_down = jnp.broadcast_to(col_lse[pl.ds(r_place ^ t, 1), :], (LANES, size)).T
     text_id = c_place * n_row + (r_place ^ t)
-    step = 32
-    lane_ids = lax.broadcasted_iota(jnp.int32, (step, LANES), 1)
-    row_ids = lax.broadcasted_iota(jnp.int32, (step, LANES), 0)
+    lane_ids = lax.broadcasted_iota(jnp.int32, (STEP, LANES), 1)
+    row_ids = lax.broadcasted_iota(jnp.int32, (STEP, LANES), 0)
 
     for which, images in enumerate(halves):
 
@@ -430,150 +434,151 @@
             column = c_place ^ (2 * j + which)
             same = jnp.where(r_place * n_col + column == text_id, 1.0, 0.0)
             lse = row_lse[pl.ds(column, 1), :]
-            for r in range(0, size, step):
+            for r in range(0, size, STEP):
                 for lane in range(0, block, LANES):
                     if tile is None:
-                        x = xs[r : r + step, lane : lane + LANES]
+                        x = xs[r : r + STEP, lane : lane + LANES]
                     else:
-                        x = tile[r : r + step, pl.ds(at + lane, LANES)]
+                        x = tile[r : r + STEP, pl.ds(at + lane, LANES)]
                     e = jnp.exp2(x - lse[:, lane : lane + LANES]) + jnp.exp2(
-                        x - col_lse_down[r : r + step, :]
+                        x - col_lse_down[r : r + STEP, :]
                     )
                     g = 0.5 * e
                     if lane <= r < lane + LANES:
                         g = g - jnp.where(row_ids + (r - lane) == lane_ids, same, 0.0)
-                    grad_ref[r : r + step, pl.ds(at + lane, LANES)] = g.astype(jnp.bfloat16)
+                    grad_ref[r : r + STEP, pl.ds(at + lane, LANES)] = g.astype(jnp.bfloat16)
             return carry
 
         lax.fori_loop(0, half // block, one, 0, unroll=4)
-    total[:size, :] = scale_ref[0, 0] * (
-        jnp.dot(grad_ref[:, :half], halves[0][...], preferred_element_type=jnp.float32)
-        + jnp.dot(grad_ref[:, half:], halves[1][...], preferred_element_type=jnp.float32)
+
+
+def text_block(t, grad, halves, scale, extra, out, total, powers):
+    half, size = halves[0].shape[0], grad.shape[0]
+    total[:size, :] = scale * (
+        jnp.dot(grad[:, :half], halves[0][...], preferred_element_type=jnp.float32)
+        + jnp.dot(grad[:, half:], halves[1][...], preferred_element_type=jnp.float32)
     )
     put_extra(total.at[size:, :], extra)
     if t & 1:
-        encode(out_ref, powers, size, lambda r: total[r : r + STEP, :], total[size:, :])
+        encode(out, powers, size, lambda r: total[r : r + STEP, :], total[size:, :])
     else:
-        out_ref[...] = total[...]
-
-
-def image_block(grads, texts, at, block, scale):
-    total = None
-    for grad, text in zip(grads, texts):
-        part = lax.dot_general(
-            grad[:, pl.ds(at, block)],
-            text[...],
-            (((0,), (0,)), ((), ())),
-            preferred_element_type=jnp.float32,
-        )
-        total = part if total is None else total + part
-    return scale * total
-
-
-def text_kernel(order, n_done, kept, block, scale_ref, coef_ref, place_ref, *refs):
-    even, odd, row_lse, col_lse, row_extra, col_extra = refs[:6]
-    n = len(order)
-    texts, rest = refs[6 : 6 + n], refs[6 + n :]
-    if kept:
-        tile, rest = rest[0], rest[1:]
-    done_grads, done_texts, rest = rest[:n_done], rest[n_done : 2 * n_done], rest[2 * n_done :]
-    grads, outs = rest[:n], rest[n : 2 * n]
-    for i, t in enumerate(order):
-        text_block(
-            texts[i],
-            tile.at[pl.ds((t - min(order)) * block, block)] if kept else None,
-            t, (even, odd), row_lse, col_lse, place_ref, scale_ref, coef_ref, row_extra, grads[i], outs[i], *rest[-2:]
-        )
-    if n_done:
-        far_ref = rest[2 * n]
-        half = even.shape[0]
-
-        def one(j, carry):
-            far_ref[j, :block, :] = image_block(
-                [*done_grads, *grads],
-                [*done_texts, *texts],
-                pl.multiple_of(j * block + half, block),
-                block,
-                scale_ref[0, 0],
+        out[...] = total[...]
+
+
+def image_blocks(out, first, grads, texts, scale, extra, block):
+    def one(j, carry):
+        total = None
+        for grad, text in zip(grads, texts):
+            part = lax.dot_general(
+                grad[:, pl.ds(pl.multiple_of(j * block + first, block), block)],
+                text[...],
+                (((0,), (0,)), ((), ())),
+                preferred_element_type=jnp.float32,
             )
-            put_extra(far_ref.at[j, block:, :], col_extra)
-            return carry
-
-        lax.fori_loop(0, half // block, one, 0)
-
-
-def text_grads(scale, coef, place, even, odd, row_lse, col_lse, row_extra, col_extra, texts, tile, order, done):
+            total = part if total is None else total + part
+        out[j, :block, :] = scale * total
+        put_extra(out.at[j, block:, :], extra)
+        return carry
+
+    lax.fori_loop(0, out.shape[0], one, 0)
+
+
+def first_kernel(t, kept, scale_ref, coef_ref, place_ref, even, odd, row_lse, col_lse, row_extra, text, *refs):
+    tile = refs[0] if kept else None
+    grad, out, total, powers = refs[kept:]
+    logit_block(text, tile, t, (even, odd), row_lse, col_lse, place_ref, coef_ref, grad)
+    text_block(t, grad, (even, odd), scale_ref[0, 0], row_extra, out, total, powers)
+
+
+def logits_kernel(n, kept, scale_ref, coef_ref, place_ref, even, odd, row_lse, col_lse, col_extra, *refs):
+    texts, last, refs = refs[:n], refs[n], refs[n + 1 :]
+    tile, last_grad, refs = refs[0] if kept else None, refs[kept], refs[kept + 1 :]
+    grads, far = refs[:n], refs[n]
+    block = last.shape[0]
+    for t in range(n):
+        part = tile.at[pl.ds(t * block, block)] if kept else None
+        logit_block(texts[t], part, t, (even, odd), row_lse, col_lse, place_ref, coef_ref, grads[t])
+    image_blocks(
+        far, even.shape[0], (*grads, last_grad), (*texts, last), scale_ref[0, 0], col_extra, block
+    )
+
+
+def rest_kernel(n, scale_ref, even, odd, row_extra, col_extra, *refs):
+    texts, grads, refs = refs[: n + 1], refs[n + 1 : 2 * n + 2], refs[2 * n + 2 :]
+    outs, near, total, powers = refs[:n], refs[n], *refs[n + 1 :]
+    for t in range(n)[::-1]:
+        text_block(t, grads[t], (even, odd), scale_ref[0, 0], row_extra, outs[t], total, powers)
+    image_blocks(near, 0, grads, texts, scale_ref[0, 0], col_extra, texts[0].shape[0])
+
+
+def gradients(scale, coef, place, even, odd, texts, lses, extras, tile, tile_last):
     half, width = even.shape
     block = texts[0].shape[0]
-    n = len(order)
+    n = len(texts) - 1
+    kept = len(tile)
     vmem = pl.BlockSpec(memory_space=VMEM)
     smem = pl.BlockSpec(memory_space=SMEM)
-    out_shape = (
-        [jax.ShapeDtypeStruct((block, 2 * half), jnp.bfloat16)] * n
-        + [
-            jax.ShapeDtypeStruct((block + MORE, width), jnp.bfloat16)
-            if t & 1
-            else jax.ShapeDtypeStruct((block + EXTRA, width), jnp.float32)
-            for t in order
-        ]
-    )
-    if done:
-        out_shape.append(jax.ShapeDtypeStruct((half // block, block + EXTRA, width), jnp.float32))
-    operands = [even, odd, row_lse, col_lse, row_extra, col_extra, *[texts[t] for t in order]]
-    operands += tile
-    operands += [done[t] for t in done] + [texts[t] for t in done]
-    outs = pl.pallas_call(
-        functools.partial(text_kernel, tuple(order), len(done), len(tile), block),
-        out_shape=tuple(out_shape),
-        in_specs=[smem] * 3 + [vmem] * len(operands),
-        out_specs=(vmem,) * len(out_shape),
-        scratch_shapes=[
-            VMEM((block + EXTRA, width), jnp.float32),
-            VMEM((block, LANES), jnp.float32),
-        ],
-        compiler_params=pltpu.CompilerParams(vmem_limit_bytes=12 * 2**20),
-        cost_estimate=pl.CostEstimate(
-            flops=FLOPS * 4 * n * block * 2 * half * width, bytes_accessed=0, transcendentals=0
-        ),
-        name=f"text_grads_{n}",
-    )(scale, coef, place, *operands)
-    grads = {t: outs[i] for i, t in enumerate(order)}
-    parts = {t: outs[n + i] for i, t in enumerate(order)}
-    return grads, parts, outs[-1]
-
-
-def image_kernel(n_text, block, scale_ref, extra, *refs):
-    grads, texts, out_ref = refs[:n_text], refs[n_text : 2 * n_text], refs[-1]
-
-    def one(j, carry):
-        put_extra(out_ref.at[j, block:, :], extra)
-        out_ref[j, :block, :] = image_block(
-            grads, texts, pl.multiple_of(j * block, block), block, scale_ref[0, 0]
+    grad = jax.ShapeDtypeStruct((block, 2 * half), jnp.bfloat16)
+    images = jax.ShapeDtypeStruct((half // block, block + EXTRA, width), jnp.float32)
+    row_extra, col_extra = extras
+
+    def of_texts(t):
+        if t & 1:
+            return jax.ShapeDtypeStruct((block + MORE, width), jnp.bfloat16)
+        return jax.ShapeDtypeStruct((block + EXTRA, width), jnp.float32)
+
+    def call(kernel, name, out_shape, scalars, operands, blocks, scratch=True):
+        return pl.pallas_call(
+            kernel,
+            out_shape=tuple(out_shape),
+            in_specs=[smem] * len(scalars) + [vmem] * len(operands),
+            out_specs=(vmem,) * len(out_shape),
+            scratch_shapes=[
+                VMEM((block + EXTRA, width), jnp.float32),
+                VMEM((block, LANES), jnp.float32),
+            ]
+            if scratch
+            else [],
+            compiler_params=pltpu.CompilerParams(vmem_limit_bytes=(12 if kept else 20) * 2**20),
+            cost_estimate=pl.CostEstimate(
+                flops=FLOPS * 4 * blocks * block * 2 * half * width, bytes_accessed=0, transcendentals=0
+            ),
+            name=name,
+        )(*scalars, *operands)
+
+    grad_last, part_last = call(
+        functools.partial(first_kernel, n, kept),
+        "text_grads_last",
+        [grad, of_texts(n)],
+        (scale, coef, place),
+        (even, odd, *lses, row_extra, texts[n], *tile_last),
+        1,
+    )
+
+    def logits():
+        *grads, far = call(
+            functools.partial(logits_kernel, n, kept),
+            "logit_and_image_grads",
+            [grad] * n + [images],
+            (scale, coef, place),
+            (even, odd, *lses, col_extra, *texts, *tile, grad_last),
+            n,
+            False,
         )
-        return carry
-
-    lax.fori_loop(0, out_ref.shape[0], one, 0)
-
-
-def image_grads(scale, extra, grads, texts, after):
-    n_text = len(grads)
-    rows = grads[0].shape[1]
-    block, width = texts[0].shape
-    n = rows // block // 2
-    vmem = pl.BlockSpec(memory_space=VMEM)
-    return pl.pallas_call(
-        functools.partial(image_kernel, n_text, block),
-        out_shape=jax.ShapeDtypeStruct((n, block + EXTRA, width), jnp.float32),
-        in_specs=[pl.BlockSpec(memory_space=SMEM)]
-        + [vmem] * (2 * n_text + 1)
-        + [pl.BlockSpec(memory_space=pl.ANY)] * len(after),
-        out_specs=vmem,
-        compiler_params=pltpu.CompilerParams(vmem_limit_bytes=12 * 2**20),
-        cost_estimate=pl.CostEstimate(
-            flops=FLOPS * 2 * n * block * n_text * block * width, bytes_accessed=0, transcendentals=0
-        ),
-        name="image_grads",
-    )(scale, extra, *grads, *texts, *after)
+        return grads, far
+
+    def rest(grads):
+        *parts, near = call(
+            functools.partial(rest_kernel, n),
+            "text_and_image_grads",
+            [of_texts(t) for t in range(n)] + [images],
+            (scale,),
+            (even, odd, row_extra, col_extra, *texts, *grads, grad_last),
+            n,
+        )
+        return parts, near
+
+    return part_last, logits, rest
 
 
 def on_device(n_row, n_col, image_embeds, text_embeds, logit_scale):
@@ -595,27 +600,31 @@
     tile = before[2:]
     row_lse, row_extra, col_lse, col_extra = exchanged(row_parts, col_parts, n_col, n_row)
 
-    held = (scale, coef, place, even, odd, row_lse, col_lse, row_extra, col_extra, texts)
     last = n_row - 1
-    grads, parts, _ = text_grads(*held, tile_last, [last], {})
-    received = swap(parts[last], "row", n_row, 1)
-    more, more_parts, far = text_grads(*held, tile, list(range(last))[::-1], grads)
-    grads |= more
-    parts |= more_parts
+    part_last, logits, rest = gradients(
+        scale, coef, place, even, odd, texts, (row_lse, col_lse), (row_extra, col_extra), tile, tile_last
+    )
+    received = swap(part_last, "row", n_row, 1)
+    grads, far = logits()
+    far = swap(far, "col", n_col, 1)
+    parts, near = rest(grads)
+
     codes = {q: [] for q in range(0, n_row, 2)}
     codes[last ^ 1].append(received)
-    after = [pack_text(parts[last ^ 1], codes[last ^ 1])] if n_row > 2 else [received]
-    near = image_grads(scale, col_extra, [grads[t] for t in range(n_row)], texts, after)
+    if n_row > 2:
+        leaving = pack_text(parts[last ^ 1], codes[last ^ 1])
+        *odd_parts, far = lax.optimization_barrier((*parts[1:last:2], far))
+        parts[1:last:2] = odd_parts
     for q in range(1, last, 2):
         codes[q ^ 1].append(swap(parts[q], "row", n_row, 1))
     for b in range(1, n_row.bit_length() - 1):
         for q in [q for q in codes if q & (1 << b)]:
-            code = after[0] if (b, q) == (1, last ^ 1) else pack_text(parts[q], codes[q])
+            code = leaving if (b, q) == (1, last ^ 1) else pack_text(parts[q], codes[q])
             codes[q ^ (1 << b)].append(swap(code, "row", n_row, 1 << b))
             del codes[q]
     grad_text, text_extra, _ = total_of(coef, parts[0], codes[0], True, [], "grad_text")
 
-    own, others = pack_images(near, swap(far, "col", n_col, 1))
+    own, others = pack_images(near, far)
     others = [swap(code, "col", n_col, 2 * j) for j, code in enumerate(others, 1)]
     grad_image, _, grad_scale = total_of(coef, own, others, False, [text_extra], "grad_image")
     return grad_image, grad_text, grad_scale.reshape(())

time: 83.3 us -> 87.5 us (1.050)
  starting transfers between devices: 22.5 us -> 32.2 us
  waiting for transfers between devices: 33 us -> 26.8 us
    ppermute x2, starting transfers between devices: 1.96 us -> 7.62 us  [the longest x1 6.96 us: gather_both(): ends = lax.ppermute(text, 'row', [(0, 3), (3, 0)])]
    ppermute x22 -> x21, waiting for transfers between devices: 29.3 us -> 24.5 us  [swap(): return lax.ppermute(x, axis, [(i, i ^ q) for i in range(n)])]
    ppermute x22 -> x21, starting transfers between devices: 20.5 us -> 24.5 us  [swap(): return lax.ppermute(x, axis, [(i, i ^ q) for i in range(n)])]
    ppermute x2, waiting for transfers between devices: 3.64 us -> 2.32 us  [the longest x1 2.31 us: gather_both(): ends = lax.ppermute(text, 'row', [(0, 3), (3, 0)])]
  transfers between devices with their start and end apart: 24 -> 23, of which waited for: 11 -> 8; matrix products, arithmetic and copies ran while one was open for 1% -> 1% of each run, Pallas kernels for 20% -> 20%
where the time goes in v9:
time: 87.5 us; the launch traced here: 87.3 us
  starting transfers between devices  32.2 us (37%)
  waiting for transfers between devices  26.8 us (31%)
  Pallas kernels  24.2 us (28%)
  other arithmetic  2.42 us (3%)
  between operations  1.66 us (2%)
    ppermute x21, starting transfers between devices, swap(): return lax.ppermute(x, axis, [(i, i ^ q) for i in range(n)])  24.5 us
    ppermute x21, waiting for transfers between devices, swap(): return lax.ppermute(x, axis, [(i, i ^ q) for i in range(n)])  24.5 us
    pallas_call x3, Pallas kernels, call(): pl.pallas_call(kernel, out_shape=tuple(out_shape), in_specs=[smem] * len(...  10 us
    pallas_call x2, Pallas kernels, stats(): pl.pallas_call(functools.partial(stats_kernel, first, len(texts), block),...  8.26 us
    ppermute x1, starting transfers between devices, gather_both(): ends = lax.ppermute(text, 'row', [(0, 3), (3, 0)])  6.96 us
    pallas_call x2, Pallas kernels, total_of(): pl.pallas_call(functools.partial(total_kernel, len(codes), in_order), out...  4.11 us
    ppermute x1, waiting for transfers between devices, gather_both(): ends = lax.ppermute(text, 'row', [(0, 3), (3, 0)])  2.31 us
  transfers between devices with their start and end apart: 23, of which 8 were waited for; matrix products, arithmetic and copies ran while one was open for 1% of the time, Pallas kernels for 20%

profile of v9, /device:TPU:0, one launch (start us, length us, event | category | flops | bytes accessed | tf_op | source)
XLA Modules:
  0.0 87.3 jit_solution(13113212480280836168)
XLA Ops:
  0.6 1.1 %convert_element_type.7.refs_0_ = bf16[256,512]{1,0:T(8,128)(2,1)S(1)} convert(f32[256,512]{1,0:T(8,128)} %param.4) | non-fusion elementwise | flops 131072 | bytes 786432 | tf_op jit(solution)/shard_map/convert_element_type | solution.py:590
  1.7 7.0 %collective-permute-start.5 = (bf16[256,512]{1,0:T(8,128)(2,1)S(1)}, bf16[256,512]{1,0:T(8,128)(2,1)S(1)}, u32[]{:S(2)}, u32[]{:S(2)}) collective-permute-start(bf16[256,512]{1,0:T(8,128)(2,1)S(1)} %convert_element_type.7.refs_0_), channel_id=1, source_target_pairs={{0,24},{24,0},{1,25},{25,1},{2,26},{26,2},{3,27},{27,3},{4,28},{28... | collective-permute-start | bytes 786440 | tf_op jit(solution)/shard_map/ppermute | solution.py:26
  8.8 0.6 collective-permute-start.3
  9.3 1.1 %convert_element_type.6.refs_3_ = bf16[256,512]{1,0:T(8,128)(2,1)S(1)} convert(f32[256,512]{1,0:T(8,128)} %param.3) | non-fusion elementwise | flops 131072 | bytes 786432 | tf_op jit(solution)/shard_map/convert_element_type | solution.py:590
  10.4 2.7 %collective-permute-start.2 = (bf16[256,512]{1,0:T(8,128)(2,1)S(1)}, bf16[256,512]{1,0:T(8,128)(2,1)S(1)}, u32[]{:S(2)}, u32[]{:S(2)}) collective-permute-start(bf16[256,512]{1,0:T(8,128)(2,1)S(1)} %convert_element_type.6.refs_3_), channel_id=1, source_target_pairs={{0,6},{1,7},{2,4},{3,5},{4,2},{5,3},{6,0},{7,1},{8,14},{9,15},{10,... | collective-permute-start | bytes 786440 | tf_op jit(solution)/shard_map/ppermute | solution.py:20
  13.6 2.3 %collective-permute-done.5.refs_0_ = bf16[256,512]{1,0:T(8,128)(2,1)S(1)} collective-permute-done((bf16[256,512]{1,0:T(8,128)(2,1)S(1)}, bf16[256,512]{1,0:T(8,128)(2,1)S(1)}, u32[]{:S(2)}, u32[]{:S(2)}) %collective-permute-start.5) | collective-permute-done | bytes 262176 | tf_op jit(solution)/shard_map/ppermute | solution.py:26
  15.9 1.7 %collective-permute-start = (bf16[256,512]{1,0:T(8,128)(2,1)S(1)}, bf16[256,512]{1,0:T(8,128)(2,1)S(1)}, u32[]{:S(2)}, u32[]{:S(2)}) collective-permute-start(bf16[256,512]{1,0:T(8,128)(2,1)S(1)} %convert_element_type.6.refs_3_), channel_id=1, source_target_pairs={{0,2},{1,3},{2,0},{3,1},{4,6},{5,7},{6,4},{7,5},{8,10},{9,11},{10,... | collective-permute-start | bytes 786440 | tf_op jit(solution)/shard_map/ppermute | solution.py:20
  17.7 8.6 %collective-permute-done.4.refs_2_ = bf16[256,512]{1,0:T(8,128)(2,1)S(1)} collective-permute-done((bf16[256,512]{1,0:T(8,128)(2,1)S(1)}, bf16[256,512]{1,0:T(8,128)(2,1)S(1)}, u32[]{:S(2)}, u32[]{:S(2)}) %collective-permute-start.4) | collective-permute-done | bytes 262176 | tf_op jit(solution)/shard_map/ppermute | solution.py:20
  26.3 0.6 collective-permute-start.7
  28.1 0.7 collective-permute-start.10
  28.9 5.6 %stats.1 = (bf16[1024,512]{1,0:T(8,128)(2,1)S(1)}, bf16[1024,512]{1,0:T(8,128)(2,1)S(1)}, f32[4,8,256]{2,1,0:T(8,128)S(1)}, f32[3,4,256]{2,1,0:T(4,128)S(1)}, f32[768,2048]{1,0:T(8,128)S(1)}) custom-call(f32[1,1]{1,0:T(1,128)S(6)} %mul.127.coef_ref, s32[1,2]{1,0:T(1,128)S(1)} %add_bitcast_fusion.place_ref, bf16[256,512]{1,0:T(8,128)(2,1)S(1)} %convert_element_type.7.refs_0_, ...), custom_call_target="tpu_custom_call" | custom-call | flops 32212254720 | tf_op jit(solution)/shard_map/stats/pallas_call | solution.py:189
  34.5 2.6 %stats_last.1 = (bf16[256,512]{1,0:T(8,128)(2,1)S(1)}, f32[4,8,256]{2,1,0:T(8,128)S(1)}, f32[3,4,256]{2,1,0:T(4,128)S(1)}, f32[256,2048]{1,0:T(8,128)S(1)}) custom-call(f32[1,1]{1,0:T(1,128)S(6)} %mul.127.coef_ref, s32[1,2]{1,0:T(1,128)S(1)} %add_bitcast_fusion.place_ref, bf16[256,512]{1,0:T(8,128)(2,1)S(1)} %collective-permute-done.5.refs_0_, ...), custom_call_target="tpu_custom_call" | custom-call | flops 10737418240 | tf_op jit(solution)/shard_map/stats_last/pallas_call | solution.py:189
  37.2 1.4 %collective-permute-start.11 = (f32[4,8,256]{2,1,0:T(8,128)S(1)}, f32[4,8,256]{2,1,0:T(8,128)S(1)}, u32[]{:S(2)}, u32[]{:S(2)}) collective-permute-start(f32[4,8,256]{2,1,0:T(8,128)S(1)} %get-tuple-element.54), channel_id=1, source_target_pairs={{0,2},{1,3},{2,0},{3,1},{4,6},{5,7},{6,4},{7,5},{8,10},{9,11},{10,... | collective-permute-start | bytes 98312 | tf_op jit(solution)/shard_map/ppermute | solution.py:20
  38.6 5.5 %collective-permute-start.12 = (f32[3,4,256]{2,1,0:T(4,128)S(1)}, f32[3,4,256]{2,1,0:T(4,128)S(1)}, u32[]{:S(2)}, u32[]{:S(2)}) collective-permute-start(f32[3,4,256]{2,1,0:T(4,128)S(1)} %get-tuple-element.55), channel_id=1, source_target_pairs={{0,8},{8,0},{16,24},{24,16},{1,9},{9,1},{17,25},{25,17},{2,10},{10... | collective-permute-start | bytes 36872 | tf_op jit(solution)/shard_map/ppermute | solution.py:20
  44.2 1.7 %collective-permute-done.12 = f32[3,4,256]{2,1,0:T(4,128)S(1)} collective-permute-done((f32[3,4,256]{2,1,0:T(4,128)S(1)}, f32[3,4,256]{2,1,0:T(4,128)S(1)}, u32[]{:S(2)}, u32[]{:S(2)}) %collective-permute-start.12) | collective-permute-done | bytes 12320 | tf_op jit(solution)/shard_map/ppermute | solution.py:20
  45.9 1.6 %collective-permute-start.13 = (f32[4,8,256]{2,1,0:T(8,128)S(1)}, f32[4,8,256]{2,1,0:T(8,128)S(1)}, u32[]{:S(2)}, u32[]{:S(2)}) collective-permute-start(f32[4,8,256]{2,1,0:T(8,128)S(1)} %pad_maximum_fusion), channel_id=1, source_target_pairs={{0,4},{1,5},{2,6},{3,7},{4,0},{5,1},{6,2},{7,3},{8,12},{9,13},{10,... | collective-permute-start | bytes 98312 | tf_op jit(solution)/shard_map/ppermute | solution.py:20
  47.5 1.7 %collective-permute-start.14 = (f32[3,4,256]{2,1,0:T(4,128)S(1)}, f32[3,4,256]{2,1,0:T(4,128)S(1)}, u32[]{:S(2)}, u32[]{:S(2)}) collective-permute-start(f32[3,4,256]{2,1,0:T(4,128)S(1)} %pad_maximum_fusion.2), channel_id=1, source_target_pairs={{0,16},{8,24},{16,0},{24,8},{1,17},{9,25},{17,1},{25,9},{2,18},{10... | collective-permute-start | bytes 36872 | tf_op jit(solution)/shard_map/ppermute | solution.py:20
  49.2 2.9 %collective-permute-done.14 = f32[3,4,256]{2,1,0:T(4,128)S(1)} collective-permute-done((f32[3,4,256]{2,1,0:T(4,128)S(1)}, f32[3,4,256]{2,1,0:T(4,128)S(1)}, u32[]{:S(2)}, u32[]{:S(2)}) %collective-permute-start.14) | collective-permute-done | bytes 12320 | tf_op jit(solution)/shard_map/ppermute | solution.py:20
  52.3 1.2 %collective-permute-done.15 = f32[4,8,256]{2,1,0:T(8,128)S(1)} collective-permute-done((f32[4,8,256]{2,1,0:T(8,128)S(1)}, f32[4,8,256]{2,1,0:T(8,128)S(1)}, u32[]{:S(2)}, u32[]{:S(2)}) %collective-permute-start.15) | collective-permute-done | bytes 32800 | tf_op jit(solution)/shard_map/ppermute | solution.py:20
  53.5 1.8 %text_grads_last.1 = (bf16[256,2048]{1,0:T(8,128)(2,1)S(1)}, bf16[288,512]{1,0:T(8,128)(2,1)S(1)}) custom-call(f32[1,1]{1,0:T(1,128)} %bitcast.237.scale_ref, f32[1,1]{1,0:T(1,128)S(6)} %mul.127.coef_ref, s32[1,2]{1,0:T(1,128)S(1)} %add_bitcast_fusion.place_ref, bf16[1024,512]{1,0:T(8,128)(2,1)S(1)} %get-tuple-element.49.refs_2_.even, ...), custom_call_target="tpu_custom_call" | custom-call | flops 21474836480 | tf_op jit(solution)/shard_map/text_grads_last/pallas_call | solution.py:531
  55.3 2.1 %collective-permute-start.21 = (bf16[288,512]{1,0:T(8,128)(2,1)S(1)}, bf16[288,512]{1,0:T(8,128)(2,1)S(1)}, u32[]{:S(2)}, u32[]{:S(2)}) collective-permute-start(bf16[288,512]{1,0:T(8,128)(2,1)S(1)} %get-tuple-element.78), channel_id=1, source_target_pairs={{0,8},{8,0},{16,24},{24,16},{1,9},{9,1},{17,25},{25,17},{2,10},{10... | collective-permute-start | bytes 884744 | tf_op jit(solution)/shard_map/ppermute | solution.py:20
  57.4 4.2 %logit_and_image_grads.1 = (bf16[256,2048]{1,0:T(8,128)(2,1)S(1)}, bf16[256,2048]{1,0:T(8,128)(2,1)S(1)}, bf16[256,2048]{1,0:T(8,128)(2,1)S(1)}, f32[4,264,512]{2,1,0:T(8,128)S(1)}) custom-call(f32[1,1]{1,0:T(1,128)} %bitcast.238.scale_ref, f32[1,1]{1,0:T(1,128)S(6)} %mul.127.coef_ref, s32[1,2]{1,0:T(1,128)S(1)} %add_bitcast_fusion.place_ref, ...), custom_call_target="tpu_custom_call" | custom-call | flops 64424509440 | tf_op jit(solution)/shard_map/logit_and_image_grads/pallas_call | solution.py:531
  61.7 4.0 %text_and_image_grads.1 = (f32[264,512]{1,0:T(8,128)S(1)}, bf16[288,512]{1,0:T(8,128)(2,1)S(1)}, f32[264,512]{1,0:T(8,128)S(1)}, f32[4,264,512]{2,1,0:T(8,128)S(1)}) custom-call(f32[1,1]{1,0:T(1,128)} %bitcast.239.scale_ref, bf16[1024,512]{1,0:T(8,128)(2,1)S(1)} %get-tuple-element.49.refs_2_.even, bf16[1024,512]{1,0:T(8,128)(2,1)S(1)} %get-tuple-element.50.refs_3_.odd, ...), custom_call_target="tpu_custom_call" | custom-call | flops 64424509440 | tf_op jit(solution)/shard_map/text_and_image_grads/pallas_call | solution.py:531
  65.7 0.7 pack_text.1
  66.4 0.5 collective-permute-start.22
  66.9 1.3 %collective-permute-start.20 = (bf16[288,512]{1,0:T(8,128)(2,1)S(1)}, bf16[288,512]{1,0:T(8,128)(2,1)S(1)}, u32[]{:S(2)}, u32[]{:S(2)}) collective-permute-start(bf16[288,512]{1,0:T(8,128)(2,1)S(1)} %get-tuple-element.76), channel_id=1, source_target_pairs={{0,8},{8,0},{16,24},{24,16},{1,9},{9,1},{17,25},{25,17},{2,10},{10... | collective-permute-start | bytes 884744 | tf_op jit(solution)/shard_map/ppermute | solution.py:20
  68.2 1.1 %pack_images.1 = (f32[264,512]{1,0:T(8,128)S(1)}, bf16[288,512]{1,0:T(8,128)(2,1)S(1)}, bf16[288,512]{1,0:T(8,128)(2,1)S(1)}, bf16[288,512]{1,0:T(8,128)(2,1)S(1)}) custom-call(f32[4,264,512]{2,1,0:T(8,128)S(1)} %get-tuple-element.67.near, f32[4,264,512]{2,1,0:T(8,128)S(1)} %collective-permute-done.16.far), custom_call_target="tpu_custom_call" | custom-call | tf_op jit(solution)/shard_map/pack_images/pallas_call | solution.py:352
  69.3 0.6 collective-permute-start.17
  70.4 2.5 %collective-permute-start.19 = (bf16[288,512]{1,0:T(8,128)(2,1)S(1)}, bf16[288,512]{1,0:T(8,128)(2,1)S(1)}, u32[]{:S(2)}, u32[]{:S(2)}) collective-permute-start(bf16[288,512]{1,0:T(8,128)(2,1)S(1)} %get-tuple-element.74), channel_id=1, source_target_pairs={{0,6},{1,7},{2,4},{3,5},{4,2},{5,3},{6,0},{7,1},{8,14},{9,15},{10,... | collective-permute-start | bytes 884744 | tf_op jit(solution)/shard_map/ppermute | solution.py:20
  72.9 9.6 %collective-permute-done.22.refs_1_ = bf16[288,512]{1,0:T(8,128)(2,1)S(1)} collective-permute-done((bf16[288,512]{1,0:T(8,128)(2,1)S(1)}, bf16[288,512]{1,0:T(8,128)(2,1)S(1)}, u32[]{:S(2)}, u32[]{:S(2)}) %collective-permute-start.22) | collective-permute-done | bytes 294944 | tf_op jit(solution)/shard_map/ppermute | solution.py:20
  82.5 1.8 %grad_text.1 = (f32[256,512]{1,0:T(8,128)}, f32[8,256]{1,0:T(8,128)S(1)}, f32[1,1]{1,0:T(1,128)}) custom-call(f32[1,1]{1,0:T(1,128)S(6)} %mul.127.coef_ref, f32[264,512]{1,0:T(8,128)S(1)} %get-tuple-element.75.base, bf16[288,512]{1,0:T(8,128)(2,1)S(1)} %collective-permute-done.20.refs_0_, bf16[288,512]{1,0:T(8,128)(2,1)S(1)} %collective-permute-done.22.refs_1_), custom_call_target="tpu_custom_call" | custom-call | tf_op jit(solution)/shard_map/grad_text/pallas_call | solution.py:397
  84.9 2.3 %grad_image.1 = (f32[256,512]{1,0:T(8,128)}, f32[8,256]{1,0:T(8,128)}, f32[1,1]{1,0:T(1,128)}) custom-call(f32[1,1]{1,0:T(1,128)S(6)} %mul.127.coef_ref, f32[264,512]{1,0:T(8,128)S(1)} %get-tuple-element.71.base, bf16[288,512]{1,0:T(8,128)(2,1)S(1)} %collective-permute-done.17.refs_0_, bf16[288,512]{1,0:T(8,128)(2,1)S(1)} %collective-permute-done.18.refs_1_, ...), custom_call_target="tpu_custom_call" | custom-call | tf_op jit(solution)/shard_map/grad_image/pallas_call | solution.py:397
  (38 shorter events, 2.6 us)
Async XLA Ops:
  1.7 14.2 %collective-permute-start.5 = (bf16[256,512]{1,0:T(8,128)(2,1)S(1)}, bf16[256,512]{1,0:T(8,128)(2,1)S(1)}, u32[]{:S(2)}, u32[]{:S(2)}) collective-permute-start(bf16[256,512]{1,0:T(8,128)(2,1)S(1)} %convert_element_type.7.refs_0_), channel_id=1, source_target_pairs={{0,24},{24,0},{1,25},{25,1},{2,26},{26,2},{3,27},{27,3},{4,28},{28... | collective-permute-start | bytes 786440 | tf_op jit(solution)/shard_map/ppermute | solution.py:26
  8.7 17.6 %collective-permute-start.4 = (bf16[256,512]{1,0:T(8,128)(2,1)S(1)}, bf16[256,512]{1,0:T(8,128)(2,1)S(1)}, u32[]{:S(2)}, u32[]{:S(2)}) collective-permute-start(bf16[256,512]{1,0:T(8,128)(2,1)S(1)} %convert_element_type.7.refs_0_), channel_id=1, source_target_pairs={{0,16},{8,24},{16,0},{24,8},{1,17},{9,25},{17,1},{25,9},{2,18},{10... | collective-permute-start | bytes 786440 | tf_op jit(solution)/shard_map/ppermute | solution.py:20
  8.8 17.5 %collective-permute-start.3 = (bf16[256,512]{1,0:T(8,128)(2,1)S(1)}, bf16[256,512]{1,0:T(8,128)(2,1)S(1)}, u32[]{:S(2)}, u32[]{:S(2)}) collective-permute-start(bf16[256,512]{1,0:T(8,128)(2,1)S(1)} %convert_element_type.7.refs_0_), channel_id=1, source_target_pairs={{0,8},{8,0},{16,24},{24,16},{1,9},{9,1},{17,25},{25,17},{2,10},{10... | collective-permute-start | bytes 786440 | tf_op jit(solution)/shard_map/ppermute | solution.py:20
  10.4 15.9 %collective-permute-start.2 = (bf16[256,512]{1,0:T(8,128)(2,1)S(1)}, bf16[256,512]{1,0:T(8,128)(2,1)S(1)}, u32[]{:S(2)}, u32[]{:S(2)}) collective-permute-start(bf16[256,512]{1,0:T(8,128)(2,1)S(1)} %convert_element_type.6.refs_3_), channel_id=1, source_target_pairs={{0,6},{1,7},{2,4},{3,5},{4,2},{5,3},{6,0},{7,1},{8,14},{9,15},{10,... | collective-permute-start | bytes 786440 | tf_op jit(solution)/shard_map/ppermute | solution.py:20
  13.1 13.2 %collective-permute-start.1 = (bf16[256,512]{1,0:T(8,128)(2,1)S(1)}, bf16[256,512]{1,0:T(8,128)(2,1)S(1)}, u32[]{:S(2)}, u32[]{:S(2)}) collective-permute-start(bf16[256,512]{1,0:T(8,128)(2,1)S(1)} %convert_element_type.6.refs_3_), channel_id=1, source_target_pairs={{0,4},{1,5},{2,6},{3,7},{4,0},{5,1},{6,2},{7,3},{8,12},{9,13},{10,... | collective-permute-start | bytes 786440 | tf_op jit(solution)/shard_map/ppermute | solution.py:20
  15.9 10.3 %collective-permute-start = (bf16[256,512]{1,0:T(8,128)(2,1)S(1)}, bf16[256,512]{1,0:T(8,128)(2,1)S(1)}, u32[]{:S(2)}, u32[]{:S(2)}) collective-permute-start(bf16[256,512]{1,0:T(8,128)(2,1)S(1)} %convert_element_type.6.refs_3_), channel_id=1, source_target_pairs={{0,2},{1,3},{2,0},{3,1},{4,6},{5,7},{6,4},{7,5},{8,10},{9,11},{10,... | collective-permute-start | bytes 786440 | tf_op jit(solution)/shard_map/ppermute | solution.py:20
  26.2 2.5 %collective-permute-start.6 = (bf16[256,512]{1,0:T(8,128)(2,1)S(1)}, bf16[256,512]{1,0:T(8,128)(2,1)S(1)}, u32[]{:S(2)}, u32[]{:S(2)}) collective-permute-start(bf16[256,512]{1,0:T(8,128)(2,1)S(1)} %convert_element_type.6.refs_3_), channel_id=1, source_target_pairs={{0,1},{1,0},{2,3},{3,2},{4,5},{5,4},{6,7},{7,6},{8,9},{9,8},{10,11... | collective-permute-start | bytes 786440 | tf_op jit(solution)/shard_map/ppermute | solution.py:20
  26.3 2.5 %collective-permute-start.7 = (bf16[256,512]{1,0:T(8,128)(2,1)S(1)}, bf16[256,512]{1,0:T(8,128)(2,1)S(1)}, u32[]{:S(2)}, u32[]{:S(2)}) collective-permute-start(bf16[256,512]{1,0:T(8,128)(2,1)S(1)} %collective-permute-done.refs_4_), channel_id=1, source_target_pairs={{0,1},{1,0},{2,3},{3,2},{4,5},{5,4},{6,7},{7,6},{8,9},{9,8},{10,11... | collective-permute-start | bytes 786440 | tf_op jit(solution)/shard_map/ppermute | solution.py:20
  26.8 1.9 %collective-permute-start.8 = (bf16[256,512]{1,0:T(8,128)(2,1)S(1)}, bf16[256,512]{1,0:T(8,128)(2,1)S(1)}, u32[]{:S(2)}, u32[]{:S(2)}) collective-permute-start(bf16[256,512]{1,0:T(8,128)(2,1)S(1)} %collective-permute-done.1.refs_5_), channel_id=1, source_target_pairs={{0,1},{1,0},{2,3},{3,2},{4,5},{5,4},{6,7},{7,6},{8,9},{9,8},{10,11... | collective-permute-start | bytes 786440 | tf_op jit(solution)/shard_map/ppermute | solution.py:20
  26.9 2.0 %collective-permute-start.9 = (bf16[256,512]{1,0:T(8,128)(2,1)S(1)}, bf16[256,512]{1,0:T(8,128)(2,1)S(1)}, u32[]{:S(2)}, u32[]{:S(2)}) collective-permute-start(bf16[256,512]{1,0:T(8,128)(2,1)S(1)} %collective-permute-done.2.refs_6_), channel_id=1, source_target_pairs={{0,1},{1,0},{2,3},{3,2},{4,5},{5,4},{6,7},{7,6},{8,9},{9,8},{10,11... | collective-permute-start | bytes 786440 | tf_op jit(solution)/shard_map/ppermute | solution.py:20
  28.1 6.4 %collective-permute-start.10 = (bf16[256,512]{1,0:T(8,128)(2,1)S(1)}, bf16[256,512]{1,0:T(8,128)(2,1)S(1)}, u32[]{:S(2)}, u32[]{:S(2)}) collective-permute-start(bf16[256,512]{1,0:T(8,128)(2,1)S(1)} %convert_element_type.7.refs_0_), channel_id=1, source_target_pairs={{8,16},{16,8},{9,17},{17,9},{10,18},{18,10},{11,19},{19,11},{12,20... | collective-permute-start | bytes 786440 | tf_op jit(solution)/shard_map/ppermute | solution.py:29
  37.2 8.7 %collective-permute-start.11 = (f32[4,8,256]{2,1,0:T(8,128)S(1)}, f32[4,8,256]{2,1,0:T(8,128)S(1)}, u32[]{:S(2)}, u32[]{:S(2)}) collective-permute-start(f32[4,8,256]{2,1,0:T(8,128)S(1)} %get-tuple-element.54), channel_id=1, source_target_pairs={{0,2},{1,3},{2,0},{3,1},{4,6},{5,7},{6,4},{7,5},{8,10},{9,11},{10,... | collective-permute-start | bytes 98312 | tf_op jit(solution)/shard_map/ppermute | solution.py:20
  38.6 7.2 %collective-permute-start.12 = (f32[3,4,256]{2,1,0:T(4,128)S(1)}, f32[3,4,256]{2,1,0:T(4,128)S(1)}, u32[]{:S(2)}, u32[]{:S(2)}) collective-permute-start(f32[3,4,256]{2,1,0:T(4,128)S(1)} %get-tuple-element.55), channel_id=1, source_target_pairs={{0,8},{8,0},{16,24},{24,16},{1,9},{9,1},{17,25},{25,17},{2,10},{10... | collective-permute-start | bytes 36872 | tf_op jit(solution)/shard_map/ppermute | solution.py:20
  45.9 6.2 %collective-permute-start.13 = (f32[4,8,256]{2,1,0:T(8,128)S(1)}, f32[4,8,256]{2,1,0:T(8,128)S(1)}, u32[]{:S(2)}, u32[]{:S(2)}) collective-permute-start(f32[4,8,256]{2,1,0:T(8,128)S(1)} %pad_maximum_fusion), channel_id=1, source_target_pairs={{0,4},{1,5},{2,6},{3,7},{4,0},{5,1},{6,2},{7,3},{8,12},{9,13},{10,... | collective-permute-start | bytes 98312 | tf_op jit(solution)/shard_map/ppermute | solution.py:20
  47.5 4.6 %collective-permute-start.14 = (f32[3,4,256]{2,1,0:T(4,128)S(1)}, f32[3,4,256]{2,1,0:T(4,128)S(1)}, u32[]{:S(2)}, u32[]{:S(2)}) collective-permute-start(f32[3,4,256]{2,1,0:T(4,128)S(1)} %pad_maximum_fusion.2), channel_id=1, source_target_pairs={{0,16},{8,24},{16,0},{24,8},{1,17},{9,25},{17,1},{25,9},{2,18},{10... | collective-permute-start | bytes 36872 | tf_op jit(solution)/shard_map/ppermute | solution.py:20
  52.2 1.3 %collective-permute-start.15 = (f32[4,8,256]{2,1,0:T(8,128)S(1)}, f32[4,8,256]{2,1,0:T(8,128)S(1)}, u32[]{:S(2)}, u32[]{:S(2)}) collective-permute-start(f32[4,8,256]{2,1,0:T(8,128)S(1)} %pad_maximum_fusion.1), channel_id=1, source_target_pairs={{0,1},{1,0},{2,3},{3,2},{4,5},{5,4},{6,7},{7,6},{8,9},{9,8},{10,11... | collective-permute-start | bytes 98312 | tf_op jit(solution)/shard_map/ppermute | solution.py:20
  55.3 10.4 %collective-permute-start.21 = (bf16[288,512]{1,0:T(8,128)(2,1)S(1)}, bf16[288,512]{1,0:T(8,128)(2,1)S(1)}, u32[]{:S(2)}, u32[]{:S(2)}) collective-permute-start(bf16[288,512]{1,0:T(8,128)(2,1)S(1)} %get-tuple-element.78), channel_id=1, source_target_pairs={{0,8},{8,0},{16,24},{24,16},{1,9},{9,1},{17,25},{25,17},{2,10},{10... | collective-permute-start | bytes 884744 | tf_op jit(solution)/shard_map/ppermute | solution.py:20
  61.6 5.4 %collective-permute-start.16 = (f32[4,264,512]{2,1,0:T(8,128)S(1)}, f32[4,264,512]{2,1,0:T(8,128)S(1)}, u32[]{:S(2)}, u32[]{:S(2)}) collective-permute-start(f32[4,264,512]{2,1,0:T(8,128)S(1)} %get-tuple-element.69), channel_id=1, source_target_pairs={{0,1},{1,0},{2,3},{3,2},{4,5},{5,4},{6,7},{7,6},{8,9},{9,8},{10,11... | collective-permute-start | bytes 6488072 | tf_op jit(solution)/shard_map/ppermute | solution.py:20
  66.4 16.1 %collective-permute-start.22 = (bf16[288,512]{1,0:T(8,128)(2,1)S(1)}, bf16[288,512]{1,0:T(8,128)(2,1)S(1)}, u32[]{:S(2)}, u32[]{:S(2)}) collective-permute-start(bf16[288,512]{1,0:T(8,128)(2,1)S(1)} %pack_text.1), channel_id=1, source_target_pairs={{0,16},{8,24},{16,0},{24,8},{1,17},{9,25},{17,1},{25,9},{2,18},{10... | collective-permute-start | bytes 884744 | tf_op jit(solution)/shard_map/ppermute | solution.py:20
  66.9 15.6 %collective-permute-start.20 = (bf16[288,512]{1,0:T(8,128)(2,1)S(1)}, bf16[288,512]{1,0:T(8,128)(2,1)S(1)}, u32[]{:S(2)}, u32[]{:S(2)}) collective-permute-start(bf16[288,512]{1,0:T(8,128)(2,1)S(1)} %get-tuple-element.76), channel_id=1, source_target_pairs={{0,8},{8,0},{16,24},{24,16},{1,9},{9,1},{17,25},{25,17},{2,10},{10... | collective-permute-start | bytes 884744 | tf_op jit(solution)/shard_map/ppermute | solution.py:20
  69.3 15.1 %collective-permute-start.17 = (bf16[288,512]{1,0:T(8,128)(2,1)S(1)}, bf16[288,512]{1,0:T(8,128)(2,1)S(1)}, u32[]{:S(2)}, u32[]{:S(2)}) collective-permute-start(bf16[288,512]{1,0:T(8,128)(2,1)S(1)} %get-tuple-element.72), channel_id=1, source_target_pairs={{0,2},{1,3},{2,0},{3,1},{4,6},{5,7},{6,4},{7,5},{8,10},{9,11},{10,... | collective-permute-start | bytes 884744 | tf_op jit(solution)/shard_map/ppermute | solution.py:20
  70.0 14.9 %collective-permute-start.18 = (bf16[288,512]{1,0:T(8,128)(2,1)S(1)}, bf16[288,512]{1,0:T(8,128)(2,1)S(1)}, u32[]{:S(2)}, u32[]{:S(2)}) collective-permute-start(bf16[288,512]{1,0:T(8,128)(2,1)S(1)} %get-tuple-element.73), channel_id=1, source_target_pairs={{0,4},{1,5},{2,6},{3,7},{4,0},{5,1},{6,2},{7,3},{8,12},{9,13},{10,... | collective-permute-start | bytes 884744 | tf_op jit(solution)/shard_map/ppermute | solution.py:20
  70.4 14.4 %collective-permute-start.19 = (bf16[288,512]{1,0:T(8,128)(2,1)S(1)}, bf16[288,512]{1,0:T(8,128)(2,1)S(1)}, u32[]{:S(2)}, u32[]{:S(2)}) collective-permute-start(bf16[288,512]{1,0:T(8,128)(2,1)S(1)} %get-tuple-element.74), channel_id=1, source_target_pairs={{0,6},{1,7},{2,4},{3,5},{4,2},{5,3},{6,0},{7,1},{8,14},{9,15},{10,... | collective-permute-start | bytes 884744 | tf_op jit(solution)/shard_map/ppermute | solution.py:20

commit v10 on v8

--- a/solution.py
+++ b/solution.py
@@ -21,15 +21,11 @@
 
 
 def gather_both(image, text, n_col, n_row):
-    line = n_row == 4
     images = [swap(image, "col", n_col, q) for q in range(2, n_col, 2)]
-    texts = [swap(text, "row", n_row, q) for q in range(1, 3 if line else n_row)]
-    images, texts, text = lax.optimization_barrier((images, texts, text))
+    texts = [swap(text, "row", n_row, q) for q in range(1, n_row - 1)]
+    images, texts = lax.optimization_barrier((images, texts))
     odd = [swap(i, "col", n_col, 1) for i in (image, *images)]
-    if line:
-        middle = lax.ppermute(text, "row", [(1, 2), (2, 1)])
-        return [image, *images], odd, [text, *texts], [middle, lax.ppermute(texts[1], "row", [(1, 0), (2, 3)])]
-    return [image, *images], odd, [text, *texts[:-1]], texts[-1:]
+    return [image, *images], odd, [text, *texts], [swap(texts[-1], "row", n_row, 1)]
 
 
 def nt_dot(a, b):
@@ -349,7 +345,7 @@
         in_specs=[vmem] * 2,
         out_specs=(vmem,) * n,
         scratch_shapes=[VMEM((n - 1, size, LANES), jnp.float32)],
-        compiler_params=pltpu.CompilerParams(vmem_limit_bytes=6 * 2**20),
+        compiler_params=pltpu.CompilerParams(vmem_limit_bytes=(4 + 2 * n) * 2**20),
         name="pack_images",
     )(near, far)
     return own, codes
@@ -606,8 +602,10 @@
     codes[last ^ 1].append(received)
     after = [pack_text(parts[last ^ 1], codes[last ^ 1])] if n_row > 2 else [received]
     near = image_grads(scale, col_extra, [grads[t] for t in range(n_row)], texts, after)
-    for q in range(1, last, 2):
-        codes[q ^ 1].append(swap(parts[q], "row", n_row, 1))
+    far = swap(far, "col", n_col, 1)
+    odd_parts, far = lax.optimization_barrier(([parts[q] for q in range(1, last, 2)], far))
+    for q, part in zip(range(1, last, 2), odd_parts):
+        codes[q ^ 1].append(swap(part, "row", n_row, 1))
     for b in range(1, n_row.bit_length() - 1):
         for q in [q for q in codes if q & (1 << b)]:
             code = after[0] if (b, q) == (1, last ^ 1) else pack_text(parts[q], codes[q])
@@ -615,7 +613,7 @@
             del codes[q]
     grad_text, text_extra, _ = total_of(coef, parts[0], codes[0], True, [], "grad_text")
 
-    own, others = pack_images(near, swap(far, "col", n_col, 1))
+    own, others = pack_images(near, far)
     others = [swap(code, "col", n_col, 2 * j) for j, code in enumerate(others, 1)]
     grad_image, _, grad_scale = total_of(coef, own, others, False, [text_extra], "grad_image")
     return grad_image, grad_text, grad_scale.reshape(())

time: 83.3 us -> 81.4 us (0.977)
  starting transfers between devices: 22.5 us -> 21.2 us
    ppermute x2 -> x0, waiting for transfers between devices: 3.64 us -> none  [the longest x1 3.64 us: gather_both(): lax.ppermute(texts[1], 'row', [(1, 0), (2, 3)])]
    ppermute x22 -> x23, waiting for transfers between devices: 29.3 us -> 32.4 us  [swap(): return lax.ppermute(x, axis, [(i, i ^ q) for i in range(n)])]
    ppermute x2 -> x0, starting transfers between devices: 1.96 us -> none  [the longest x1 1.29 us: gather_both(): lax.ppermute(texts[1], 'row', [(1, 0), (2, 3)])]
    ppermute x22 -> x23, starting transfers between devices: 20.5 us -> 21.2 us  [swap(): return lax.ppermute(x, axis, [(i, i ^ q) for i in range(n)])]
  transfers between devices with their start and end apart: 24 -> 23, of which waited for: 11 -> 14; matrix products, arithmetic and copies ran while one was open for 1% -> 1% of each run, Pallas kernels for 20% -> 21%
where the time goes in v10:
time: 81.4 us; the launch traced here: 81.2 us
  waiting for transfers between devices  32.4 us (40%)
  Pallas kernels  23.5 us (29%)
  starting transfers between devices  21.2 us (26%)
  other arithmetic  2.43 us (3%)
  between operations  1.59 us (2%)
    ppermute x23, waiting for transfers between devices, swap(): return lax.ppermute(x, axis, [(i, i ^ q) for i in range(n)])  32.4 us
    ppermute x23, starting transfers between devices, swap(): return lax.ppermute(x, axis, [(i, i ^ q) for i in range(n)])  21.2 us
    pallas_call x2, Pallas kernels, stats(): pl.pallas_call(functools.partial(stats_kernel, first, len(texts), block),...  8.25 us
    pallas_call x2, Pallas kernels, text_grads(): pl.pallas_call(functools.partial(text_kernel, tuple(order), len(done), le...  7.38 us
    pallas_call x2, Pallas kernels, total_of(): pl.pallas_call(functools.partial(total_kernel, len(codes), in_order), out...  4.1 us
    pallas_call x1, Pallas kernels, image_grads(): pl.pallas_call(functools.partial(image_kernel, n_text, block), out_shape=...  1.95 us
  transfers between devices with their start and end apart: 23, of which 14 were waited for; matrix products, arithmetic and copies ran while one was open for 1% of the time, Pallas kernels for 21%

profile of v10, /device:TPU:0, one launch (start us, length us, event | category | flops | bytes accessed | tf_op | source)
XLA Modules:
  0.0 81.2 jit_solution(12097916560560223645)
XLA Ops:
  0.6 1.1 %convert_element_type.7.refs_0_.refs_8_.refs_4_ = bf16[256,512]{1,0:T(8,128)(2,1)S(1)} convert(f32[256,512]{1,0:T(8,128)} %param.4) | non-fusion elementwise | flops 131072 | bytes 786432 | tf_op jit(solution)/shard_map/convert_element_type | solution.py:581
  1.7 4.1 %collective-permute-start.4 = (bf16[256,512]{1,0:T(8,128)(2,1)S(1)}, bf16[256,512]{1,0:T(8,128)(2,1)S(1)}, u32[]{:S(2)}, u32[]{:S(2)}) collective-permute-start(bf16[256,512]{1,0:T(8,128)(2,1)S(1)} %convert_element_type.7.refs_0_.refs_8_.refs_4_), channel_id=1, source_target_pairs={{0,16},{8,24},{16,0},{24,8},{1,17},{9,25},{17,1},{25,9},{2,18},{10... | collective-permute-start | bytes 786440 | tf_op jit(solution)/shard_map/ppermute | solution.py:20
  5.8 1.6 %collective-permute-start.3 = (bf16[256,512]{1,0:T(8,128)(2,1)S(1)}, bf16[256,512]{1,0:T(8,128)(2,1)S(1)}, u32[]{:S(2)}, u32[]{:S(2)}) collective-permute-start(bf16[256,512]{1,0:T(8,128)(2,1)S(1)} %convert_element_type.7.refs_0_.refs_8_.refs_4_), channel_id=1, source_target_pairs={{0,8},{8,0},{16,24},{24,16},{1,9},{9,1},{17,25},{25,17},{2,10},{10... | collective-permute-start | bytes 786440 | tf_op jit(solution)/shard_map/ppermute | solution.py:20
  7.4 1.1 %convert_element_type.6.refs_3_ = bf16[256,512]{1,0:T(8,128)(2,1)S(1)} convert(f32[256,512]{1,0:T(8,128)} %param.3) | non-fusion elementwise | flops 131072 | bytes 786432 | tf_op jit(solution)/shard_map/convert_element_type | solution.py:581
  8.5 2.5 %collective-permute-start.2 = (bf16[256,512]{1,0:T(8,128)(2,1)S(1)}, bf16[256,512]{1,0:T(8,128)(2,1)S(1)}, u32[]{:S(2)}, u32[]{:S(2)}) collective-permute-start(bf16[256,512]{1,0:T(8,128)(2,1)S(1)} %convert_element_type.6.refs_3_), channel_id=1, source_target_pairs={{0,6},{1,7},{2,4},{3,5},{4,2},{5,3},{6,0},{7,1},{8,14},{9,15},{10,... | collective-permute-start | bytes 786440 | tf_op jit(solution)/shard_map/ppermute | solution.py:20
  12.0 5.8 %collective-permute-done.4.refs_2_.refs_6_ = bf16[256,512]{1,0:T(8,128)(2,1)S(1)} collective-permute-done((bf16[256,512]{1,0:T(8,128)(2,1)S(1)}, bf16[256,512]{1,0:T(8,128)(2,1)S(1)}, u32[]{:S(2)}, u32[]{:S(2)}) %collective-permute-start.4) | collective-permute-done | bytes 262176 | tf_op jit(solution)/shard_map/ppermute | solution.py:20
  18.0 0.7 collective-permute-done.2.refs_6_
  18.7 3.8 %collective-permute-done.1.refs_5_ = bf16[256,512]{1,0:T(8,128)(2,1)S(1)} collective-permute-done((bf16[256,512]{1,0:T(8,128)(2,1)S(1)}, bf16[256,512]{1,0:T(8,128)(2,1)S(1)}, u32[]{:S(2)}, u32[]{:S(2)}) %collective-permute-start.1) | collective-permute-done | bytes 262176 | tf_op jit(solution)/shard_map/ppermute | solution.py:20
  24.9 5.6 %stats.1 = (bf16[1024,512]{1,0:T(8,128)(2,1)S(1)}, bf16[1024,512]{1,0:T(8,128)(2,1)S(1)}, f32[4,8,256]{2,1,0:T(8,128)S(1)}, f32[3,4,256]{2,1,0:T(4,128)S(1)}, f32[768,2048]{1,0:T(8,128)S(1)}) custom-call(f32[1,1]{1,0:T(1,128)S(6)} %mul.147.coef_ref, s32[1,2]{1,0:T(1,128)S(1)} %add_bitcast_fusion.place_ref, ...), custom_call_target="tpu_custom_call" | custom-call | flops 32212254720 | tf_op jit(solution)/shard_map/stats/pallas_call | solution.py:181
  30.5 2.1 %collective-permute-done.5.refs_0_ = bf16[256,512]{1,0:T(8,128)(2,1)S(1)} collective-permute-done((bf16[256,512]{1,0:T(8,128)(2,1)S(1)}, bf16[256,512]{1,0:T(8,128)(2,1)S(1)}, u32[]{:S(2)}, u32[]{:S(2)}) %collective-permute-start.5) | collective-permute-done | bytes 262176 | tf_op jit(solution)/shard_map/ppermute | solution.py:20
  32.6 2.6 %stats_last.1 = (bf16[256,512]{1,0:T(8,128)(2,1)S(1)}, f32[4,8,256]{2,1,0:T(8,128)S(1)}, f32[3,4,256]{2,1,0:T(4,128)S(1)}, f32[256,2048]{1,0:T(8,128)S(1)}) custom-call(f32[1,1]{1,0:T(1,128)S(6)} %mul.147.coef_ref, s32[1,2]{1,0:T(1,128)S(1)} %add_bitcast_fusion.place_ref, bf16[256,512]{1,0:T(8,128)(2,1)S(1)} %collective-permute-done.5.refs_0_, ...), custom_call_target="tpu_custom_call" | custom-call | flops 10737418240 | tf_op jit(solution)/shard_map/stats_last/pallas_call | solution.py:181
  35.2 1.7 %collective-permute-start.12 = (f32[4,8,256]{2,1,0:T(8,128)S(1)}, f32[4,8,256]{2,1,0:T(8,128)S(1)}, u32[]{:S(2)}, u32[]{:S(2)}) collective-permute-start(f32[4,8,256]{2,1,0:T(8,128)S(1)} %get-tuple-element.50), channel_id=1, source_target_pairs={{0,6},{1,7},{2,4},{3,5},{4,2},{5,3},{6,0},{7,1},{8,14},{9,15},{10,... | collective-permute-start | bytes 98312 | tf_op jit(solution)/shard_map/ppermute | solution.py:20
  36.9 1.3 %collective-permute-start.11 = (f32[4,8,256]{2,1,0:T(8,128)S(1)}, f32[4,8,256]{2,1,0:T(8,128)S(1)}, u32[]{:S(2)}, u32[]{:S(2)}) collective-permute-start(f32[4,8,256]{2,1,0:T(8,128)S(1)} %get-tuple-element.50), channel_id=1, source_target_pairs={{0,4},{1,5},{2,6},{3,7},{4,0},{5,1},{6,2},{7,3},{8,12},{9,13},{10,... | collective-permute-start | bytes 98312 | tf_op jit(solution)/shard_map/ppermute | solution.py:20
  38.2 0.6 collective-permute-start.10
  39.2 3.3 %collective-permute-done.13 = f32[3,4,256]{2,1,0:T(4,128)S(1)} collective-permute-done((f32[3,4,256]{2,1,0:T(4,128)S(1)}, f32[3,4,256]{2,1,0:T(4,128)S(1)}, u32[]{:S(2)}, u32[]{:S(2)}) %collective-permute-start.13) | collective-permute-done | bytes 12320 | tf_op jit(solution)/shard_map/ppermute | solution.py:20
  43.0 4.3 %collective-permute-done.14 = f32[3,4,256]{2,1,0:T(4,128)S(1)} collective-permute-done((f32[3,4,256]{2,1,0:T(4,128)S(1)}, f32[3,4,256]{2,1,0:T(4,128)S(1)}, u32[]{:S(2)}, u32[]{:S(2)}) %collective-permute-start.14) | collective-permute-done | bytes 12320 | tf_op jit(solution)/shard_map/ppermute | solution.py:20
  47.4 1.8 %text_grads_1.1 = (bf16[256,2048]{1,0:T(8,128)(2,1)S(1)}, bf16[288,512]{1,0:T(8,128)(2,1)S(1)}) custom-call(f32[1,1]{1,0:T(1,128)} %bitcast.277.scale_ref, f32[1,1]{1,0:T(1,128)S(6)} %mul.147.coef_ref, s32[1,2]{1,0:T(1,128)S(1)} %add_bitcast_fusion.place_ref, bf16[1024,512]{1,0:T(8,128)(2,1)S(1)} %get-tuple-element.45.refs_1_.refs_0_, ...), custom_call_target="tpu_custom_call" | custom-call | flops 21474836480 | tf_op jit(solution)/shard_map/text_grads_1/pallas_call | solution.py:521
  49.7 5.5 %text_grads_3.1 = (bf16[256,2048]{1,0:T(8,128)(2,1)S(1)}, bf16[256,2048]{1,0:T(8,128)(2,1)S(1)}, bf16[256,2048]{1,0:T(8,128)(2,1)S(1)}, f32[264,512]{1,0:T(8,128...) custom-call(f32[1,1]{1,0:T(1,128)} %bitcast.278.scale_ref, ...), custom_call_target="tpu_custom_call" | custom-call | flops 64424509440 | tf_op jit(solution)/shard_map/text_grads_3/pallas_call | solution.py:521
  55.4 0.7 collective-permute-done.16.refs_0_
  56.0 0.7 pack_text.1.refs_8_
  56.8 1.9 %collective-permute-start.22 = (bf16[288,512]{1,0:T(8,128)(2,1)S(1)}, bf16[288,512]{1,0:T(8,128)(2,1)S(1)}, u32[]{:S(2)}, u32[]{:S(2)}) collective-permute-start(bf16[288,512]{1,0:T(8,128)(2,1)S(1)} %pack_text.1.refs_8_), channel_id=1, source_target_pairs={{0,16},{8,24},{16,0},{24,8},{1,17},{9,25},{17,1},{25,9},{2,18},{10... | collective-permute-start | bytes 884744 | tf_op jit(solution)/shard_map/ppermute | solution.py:20
  58.6 1.9 %image_grads.1.near = f32[4,264,512]{2,1,0:T(8,128)S(1)} custom-call(f32[1,1]{1,0:T(1,128)} %bitcast.279.scale_ref, f32[4,256]{1,0:T(4,128)S(1)} %fusion.34.refs_5_.extra, bf16[256,2048]{1,0:T(8,128)(2,1)S(1)} %get-tuple-element.59.refs_0_, bf16[256,2048]{1,0:T(8,128)(2,1)S(1)} %get-tuple-element.60.refs_1_, ...), custom_call_target="tpu_custom_call" | custom-call | flops 21474836480 | tf_op jit(solution)/shard_map/image_grads/pallas_call | solution.py:560
  60.6 0.6 collective-permute-start.21
  61.2 1.1 %pack_images.1 = (f32[264,512]{1,0:T(8,128)S(1)}, bf16[288,512]{1,0:T(8,128)(2,1)S(1)}, bf16[288,512]{1,0:T(8,128)(2,1)S(1)}, bf16[288,512]{1,0:T(8,128)(2,1)S(1)}) custom-call(f32[4,264,512]{2,1,0:T(8,128)S(1)} %image_grads.1.near, f32[4,264,512]{2,1,0:T(8,128)S(1)} %collective-permute-done.17.far), custom_call_target="tpu_custom_call" | custom-call | tf_op jit(solution)/shard_map/pack_images/pallas_call | solution.py:342
  62.3 1.6 %collective-permute-start.18 = (bf16[288,512]{1,0:T(8,128)(2,1)S(1)}, bf16[288,512]{1,0:T(8,128)(2,1)S(1)}, u32[]{:S(2)}, u32[]{:S(2)}) collective-permute-start(bf16[288,512]{1,0:T(8,128)(2,1)S(1)} %get-tuple-element.68), channel_id=1, source_target_pairs={{0,2},{1,3},{2,0},{3,1},{4,6},{5,7},{6,4},{7,5},{8,10},{9,11},{10,... | collective-permute-start | bytes 884744 | tf_op jit(solution)/shard_map/ppermute | solution.py:20
  63.9 0.7 collective-permute-start.19
  64.6 1.3 %collective-permute-start.20 = (bf16[288,512]{1,0:T(8,128)(2,1)S(1)}, bf16[288,512]{1,0:T(8,128)(2,1)S(1)}, u32[]{:S(2)}, u32[]{:S(2)}) collective-permute-start(bf16[288,512]{1,0:T(8,128)(2,1)S(1)} %get-tuple-element.70), channel_id=1, source_target_pairs={{0,6},{1,7},{2,4},{3,5},{4,2},{5,3},{6,0},{7,1},{8,14},{9,15},{10,... | collective-permute-start | bytes 884744 | tf_op jit(solution)/shard_map/ppermute | solution.py:20
  65.9 7.0 %collective-permute-done.22.refs_1_ = bf16[288,512]{1,0:T(8,128)(2,1)S(1)} collective-permute-done((bf16[288,512]{1,0:T(8,128)(2,1)S(1)}, bf16[288,512]{1,0:T(8,128)(2,1)S(1)}, u32[]{:S(2)}, u32[]{:S(2)}) %collective-permute-start.22) | collective-permute-done | bytes 294944 | tf_op jit(solution)/shard_map/ppermute | solution.py:20
  72.9 1.0 %collective-permute-done.21.refs_0_ = bf16[288,512]{1,0:T(8,128)(2,1)S(1)} collective-permute-done((bf16[288,512]{1,0:T(8,128)(2,1)S(1)}, bf16[288,512]{1,0:T(8,128)(2,1)S(1)}, u32[]{:S(2)}, u32[]{:S(2)}) %collective-permute-start.21) | collective-permute-done | bytes 294944 | tf_op jit(solution)/shard_map/ppermute | solution.py:20
  73.8 1.8 %grad_text.1 = (f32[256,512]{1,0:T(8,128)}, f32[8,256]{1,0:T(8,128)S(1)}, f32[1,1]{1,0:T(1,128)}) custom-call(f32[1,1]{1,0:T(1,128)S(6)} %mul.147.coef_ref, f32[264,512]{1,0:T(8,128)S(1)} %get-tuple-element.71.base, bf16[288,512]{1,0:T(8,128)(2,1)S(1)} %collective-permute-done.21.refs_0_, bf16[288,512]{1,0:T(8,128)(2,1)S(1)} %collective-permute-done.22.refs_1_), custom_call_target="tpu_custom_call" | custom-call | tf_op jit(solution)/shard_map/grad_text/pallas_call | solution.py:387
  75.7 3.0 %collective-permute-done.19.refs_1_ = bf16[288,512]{1,0:T(8,128)(2,1)S(1)} collective-permute-done((bf16[288,512]{1,0:T(8,128)(2,1)S(1)}, bf16[288,512]{1,0:T(8,128)(2,1)S(1)}, u32[]{:S(2)}, u32[]{:S(2)}) %collective-permute-start.19) | collective-permute-done | bytes 294944 | tf_op jit(solution)/shard_map/ppermute | solution.py:20
  78.7 2.3 %grad_image.1 = (f32[256,512]{1,0:T(8,128)}, f32[8,256]{1,0:T(8,128)}, f32[1,1]{1,0:T(1,128)}) custom-call(f32[1,1]{1,0:T(1,128)S(6)} %mul.147.coef_ref, f32[264,512]{1,0:T(8,128)S(1)} %get-tuple-element.67.base, bf16[288,512]{1,0:T(8,128)(2,1)S(1)} %collective-permute-done.18.refs_0_, bf16[288,512]{1,0:T(8,128)(2,1)S(1)} %collective-permute-done.19.refs_1_, ...), custom_call_target="tpu_custom_call" | custom-call | tf_op jit(solution)/shard_map/grad_image/pallas_call | solution.py:387
  (36 shorter events, 4.6 us)
Async XLA Ops:
  1.7 16.1 %collective-permute-start.4 = (bf16[256,512]{1,0:T(8,128)(2,1)S(1)}, bf16[256,512]{1,0:T(8,128)(2,1)S(1)}, u32[]{:S(2)}, u32[]{:S(2)}) collective-permute-start(bf16[256,512]{1,0:T(8,128)(2,1)S(1)} %convert_element_type.7.refs_0_.refs_8_.refs_4_), channel_id=1, source_target_pairs={{0,16},{8,24},{16,0},{24,8},{1,17},{9,25},{17,1},{25,9},{2,18},{10... | collective-permute-start | bytes 786440 | tf_op jit(solution)/shard_map/ppermute | solution.py:20
  5.8 12.2 %collective-permute-start.3 = (bf16[256,512]{1,0:T(8,128)(2,1)S(1)}, bf16[256,512]{1,0:T(8,128)(2,1)S(1)}, u32[]{:S(2)}, u32[]{:S(2)}) collective-permute-start(bf16[256,512]{1,0:T(8,128)(2,1)S(1)} %convert_element_type.7.refs_0_.refs_8_.refs_4_), channel_id=1, source_target_pairs={{0,8},{8,0},{16,24},{24,16},{1,9},{9,1},{17,25},{25,17},{2,10},{10... | collective-permute-start | bytes 786440 | tf_op jit(solution)/shard_map/ppermute | solution.py:20
  8.5 10.3 %collective-permute-start.2 = (bf16[256,512]{1,0:T(8,128)(2,1)S(1)}, bf16[256,512]{1,0:T(8,128)(2,1)S(1)}, u32[]{:S(2)}, u32[]{:S(2)}) collective-permute-start(bf16[256,512]{1,0:T(8,128)(2,1)S(1)} %convert_element_type.6.refs_3_), channel_id=1, source_target_pairs={{0,6},{1,7},{2,4},{3,5},{4,2},{5,3},{6,0},{7,1},{8,14},{9,15},{10,... | collective-permute-start | bytes 786440 | tf_op jit(solution)/shard_map/ppermute | solution.py:20
  11.0 11.6 %collective-permute-start.1 = (bf16[256,512]{1,0:T(8,128)(2,1)S(1)}, bf16[256,512]{1,0:T(8,128)(2,1)S(1)}, u32[]{:S(2)}, u32[]{:S(2)}) collective-permute-start(bf16[256,512]{1,0:T(8,128)(2,1)S(1)} %convert_element_type.6.refs_3_), channel_id=1, source_target_pairs={{0,4},{1,5},{2,6},{3,7},{4,0},{5,1},{6,2},{7,3},{8,12},{9,13},{10,... | collective-permute-start | bytes 786440 | tf_op jit(solution)/shard_map/ppermute | solution.py:20
  11.5 11.1 %collective-permute-start = (bf16[256,512]{1,0:T(8,128)(2,1)S(1)}, bf16[256,512]{1,0:T(8,128)(2,1)S(1)}, u32[]{:S(2)}, u32[]{:S(2)}) collective-permute-start(bf16[256,512]{1,0:T(8,128)(2,1)S(1)} %convert_element_type.6.refs_3_), channel_id=1, source_target_pairs={{0,2},{1,3},{2,0},{3,1},{4,6},{5,7},{6,4},{7,5},{8,10},{9,11},{10,... | collective-permute-start | bytes 786440 | tf_op jit(solution)/shard_map/ppermute | solution.py:20
  17.8 6.5 %collective-permute-start.6 = (bf16[256,512]{1,0:T(8,128)(2,1)S(1)}, bf16[256,512]{1,0:T(8,128)(2,1)S(1)}, u32[]{:S(2)}, u32[]{:S(2)}) collective-permute-start(bf16[256,512]{1,0:T(8,128)(2,1)S(1)} %convert_element_type.6.refs_3_), channel_id=1, source_target_pairs={{0,1},{1,0},{2,3},{3,2},{4,5},{5,4},{6,7},{7,6},{8,9},{9,8},{10,11... | collective-permute-start | bytes 786440 | tf_op jit(solution)/shard_map/ppermute | solution.py:20
  22.6 1.7 %collective-permute-start.7 = (bf16[256,512]{1,0:T(8,128)(2,1)S(1)}, bf16[256,512]{1,0:T(8,128)(2,1)S(1)}, u32[]{:S(2)}, u32[]{:S(2)}) collective-permute-start(bf16[256,512]{1,0:T(8,128)(2,1)S(1)} %collective-permute-done.refs_4_), channel_id=1, source_target_pairs={{0,1},{1,0},{2,3},{3,2},{4,5},{5,4},{6,7},{7,6},{8,9},{9,8},{10,11... | collective-permute-start | bytes 786440 | tf_op jit(solution)/shard_map/ppermute | solution.py:20
  22.6 1.9 %collective-permute-start.8 = (bf16[256,512]{1,0:T(8,128)(2,1)S(1)}, bf16[256,512]{1,0:T(8,128)(2,1)S(1)}, u32[]{:S(2)}, u32[]{:S(2)}) collective-permute-start(bf16[256,512]{1,0:T(8,128)(2,1)S(1)} %collective-permute-done.1.refs_5_), channel_id=1, source_target_pairs={{0,1},{1,0},{2,3},{3,2},{4,5},{5,4},{6,7},{7,6},{8,9},{9,8},{10,11... | collective-permute-start | bytes 786440 | tf_op jit(solution)/shard_map/ppermute | solution.py:20
  23.1 1.8 %collective-permute-start.9 = (bf16[256,512]{1,0:T(8,128)(2,1)S(1)}, bf16[256,512]{1,0:T(8,128)(2,1)S(1)}, u32[]{:S(2)}, u32[]{:S(2)}) collective-permute-start(bf16[256,512]{1,0:T(8,128)(2,1)S(1)} %collective-permute-done.2.refs_6_), channel_id=1, source_target_pairs={{0,1},{1,0},{2,3},{3,2},{4,5},{5,4},{6,7},{7,6},{8,9},{9,8},{10,11... | collective-permute-start | bytes 786440 | tf_op jit(solution)/shard_map/ppermute | solution.py:20
  23.9 8.7 %collective-permute-start.5 = (bf16[256,512]{1,0:T(8,128)(2,1)S(1)}, bf16[256,512]{1,0:T(8,128)(2,1)S(1)}, u32[]{:S(2)}, u32[]{:S(2)}) collective-permute-start(bf16[256,512]{1,0:T(8,128)(2,1)S(1)} %collective-permute-done.4.refs_2_.refs_6_), channel_id=1, source_target_pairs={{0,8},{8,0},{16,24},{24,16},{1,9},{9,1},{17,25},{25,17},{2,10},{10... | collective-permute-start | bytes 786440 | tf_op jit(solution)/shard_map/ppermute | solution.py:20
  35.2 7.3 %collective-permute-start.12 = (f32[4,8,256]{2,1,0:T(8,128)S(1)}, f32[4,8,256]{2,1,0:T(8,128)S(1)}, u32[]{:S(2)}, u32[]{:S(2)}) collective-permute-start(f32[4,8,256]{2,1,0:T(8,128)S(1)} %get-tuple-element.50), channel_id=1, source_target_pairs={{0,6},{1,7},{2,4},{3,5},{4,2},{5,3},{6,0},{7,1},{8,14},{9,15},{10,... | collective-permute-start | bytes 98312 | tf_op jit(solution)/shard_map/ppermute | solution.py:20
  36.9 5.6 %collective-permute-start.11 = (f32[4,8,256]{2,1,0:T(8,128)S(1)}, f32[4,8,256]{2,1,0:T(8,128)S(1)}, u32[]{:S(2)}, u32[]{:S(2)}) collective-permute-start(f32[4,8,256]{2,1,0:T(8,128)S(1)} %get-tuple-element.50), channel_id=1, source_target_pairs={{0,4},{1,5},{2,6},{3,7},{4,0},{5,1},{6,2},{7,3},{8,12},{9,13},{10,... | collective-permute-start | bytes 98312 | tf_op jit(solution)/shard_map/ppermute | solution.py:20
  38.2 4.3 %collective-permute-start.10 = (f32[4,8,256]{2,1,0:T(8,128)S(1)}, f32[4,8,256]{2,1,0:T(8,128)S(1)}, u32[]{:S(2)}, u32[]{:S(2)}) collective-permute-start(f32[4,8,256]{2,1,0:T(8,128)S(1)} %get-tuple-element.50), channel_id=1, source_target_pairs={{0,2},{1,3},{2,0},{3,1},{4,6},{5,7},{6,4},{7,5},{8,10},{9,11},{10,... | collective-permute-start | bytes 98312 | tf_op jit(solution)/shard_map/ppermute | solution.py:20
  38.8 3.7 %collective-permute-start.13 = (f32[3,4,256]{2,1,0:T(4,128)S(1)}, f32[3,4,256]{2,1,0:T(4,128)S(1)}, u32[]{:S(2)}, u32[]{:S(2)}) collective-permute-start(f32[3,4,256]{2,1,0:T(4,128)S(1)} %get-tuple-element.49), channel_id=1, source_target_pairs={{0,8},{8,0},{16,24},{24,16},{1,9},{9,1},{17,25},{25,17},{2,10},{10... | collective-permute-start | bytes 36872 | tf_op jit(solution)/shard_map/ppermute | solution.py:20
  42.6 4.7 %collective-permute-start.14 = (f32[3,4,256]{2,1,0:T(4,128)S(1)}, f32[3,4,256]{2,1,0:T(4,128)S(1)}, u32[]{:S(2)}, u32[]{:S(2)}) collective-permute-start(f32[3,4,256]{2,1,0:T(4,128)S(1)} %pad_maximum_fusion.1), channel_id=1, source_target_pairs={{0,16},{8,24},{16,0},{24,8},{1,17},{9,25},{17,1},{25,9},{2,18},{10... | collective-permute-start | bytes 36872 | tf_op jit(solution)/shard_map/ppermute | solution.py:20
  43.0 4.3 %collective-permute-start.15 = (f32[4,8,256]{2,1,0:T(8,128)S(1)}, f32[4,8,256]{2,1,0:T(8,128)S(1)}, u32[]{:S(2)}, u32[]{:S(2)}) collective-permute-start(f32[4,8,256]{2,1,0:T(8,128)S(1)} %pad_maximum_fusion), channel_id=1, source_target_pairs={{0,1},{1,0},{2,3},{3,2},{4,5},{5,4},{6,7},{7,6},{8,9},{9,8},{10,11... | collective-permute-start | bytes 98312 | tf_op jit(solution)/shard_map/ppermute | solution.py:20
  49.3 6.8 %collective-permute-start.16 = (bf16[288,512]{1,0:T(8,128)(2,1)S(1)}, bf16[288,512]{1,0:T(8,128)(2,1)S(1)}, u32[]{:S(2)}, u32[]{:S(2)}) collective-permute-start(bf16[288,512]{1,0:T(8,128)(2,1)S(1)} %get-tuple-element.63), channel_id=1, source_target_pairs={{0,8},{8,0},{16,24},{24,16},{1,9},{9,1},{17,25},{25,17},{2,10},{10... | collective-permute-start | bytes 884744 | tf_op jit(solution)/shard_map/ppermute | solution.py:20
  55.3 5.3 %collective-permute-start.17 = (f32[4,264,512]{2,1,0:T(8,128)S(1)}, f32[4,264,512]{2,1,0:T(8,128)S(1)}, u32[]{:S(2)}, u32[]{:S(2)}) collective-permute-start(f32[4,264,512]{2,1,0:T(8,128)S(1)} %get-tuple-element.65), channel_id=1, source_target_pairs={{0,1},{1,0},{2,3},{3,2},{4,5},{5,4},{6,7},{7,6},{8,9},{9,8},{10,11... | collective-permute-start | bytes 6488072 | tf_op jit(solution)/shard_map/ppermute | solution.py:20
  56.8 16.1 %collective-permute-start.22 = (bf16[288,512]{1,0:T(8,128)(2,1)S(1)}, bf16[288,512]{1,0:T(8,128)(2,1)S(1)}, u32[]{:S(2)}, u32[]{:S(2)}) collective-permute-start(bf16[288,512]{1,0:T(8,128)(2,1)S(1)} %pack_text.1.refs_8_), channel_id=1, source_target_pairs={{0,16},{8,24},{16,0},{24,8},{1,17},{9,25},{17,1},{25,9},{2,18},{10... | collective-permute-start | bytes 884744 | tf_op jit(solution)/shard_map/ppermute | solution.py:20
  60.6 13.2 %collective-permute-start.21 = (bf16[288,512]{1,0:T(8,128)(2,1)S(1)}, bf16[288,512]{1,0:T(8,128)(2,1)S(1)}, u32[]{:S(2)}, u32[]{:S(2)}) collective-permute-start(bf16[288,512]{1,0:T(8,128)(2,1)S(1)} %get-tuple-element.72), channel_id=1, source_target_pairs={{0,8},{8,0},{16,24},{24,16},{1,9},{9,1},{17,25},{25,17},{2,10},{10... | collective-permute-start | bytes 884744 | tf_op jit(solution)/shard_map/ppermute | solution.py:20
  62.3 13.3 %collective-permute-start.18 = (bf16[288,512]{1,0:T(8,128)(2,1)S(1)}, bf16[288,512]{1,0:T(8,128)(2,1)S(1)}, u32[]{:S(2)}, u32[]{:S(2)}) collective-permute-start(bf16[288,512]{1,0:T(8,128)(2,1)S(1)} %get-tuple-element.68), channel_id=1, source_target_pairs={{0,2},{1,3},{2,0},{3,1},{4,6},{5,7},{6,4},{7,5},{8,10},{9,11},{10,... | collective-permute-start | bytes 884744 | tf_op jit(solution)/shard_map/ppermute | solution.py:20
  63.9 14.8 %collective-permute-start.19 = (bf16[288,512]{1,0:T(8,128)(2,1)S(1)}, bf16[288,512]{1,0:T(8,128)(2,1)S(1)}, u32[]{:S(2)}, u32[]{:S(2)}) collective-permute-start(bf16[288,512]{1,0:T(8,128)(2,1)S(1)} %get-tuple-element.69), channel_id=1, source_target_pairs={{0,4},{1,5},{2,6},{3,7},{4,0},{5,1},{6,2},{7,3},{8,12},{9,13},{10,... | collective-permute-start | bytes 884744 | tf_op jit(solution)/shard_map/ppermute | solution.py:20
  64.6 14.1 %collective-permute-start.20 = (bf16[288,512]{1,0:T(8,128)(2,1)S(1)}, bf16[288,512]{1,0:T(8,128)(2,1)S(1)}, u32[]{:S(2)}, u32[]{:S(2)}) collective-permute-start(bf16[288,512]{1,0:T(8,128)(2,1)S(1)} %get-tuple-element.70), channel_id=1, source_target_pairs={{0,6},{1,7},{2,4},{3,5},{4,2},{5,3},{6,0},{7,1},{8,14},{9,15},{10,... | collective-permute-start | bytes 884744 | tf_op jit(solution)/shard_map/ppermute | solution.py:20

commit v11 on v10

--- a/solution.py
+++ b/solution.py
@@ -118,7 +118,7 @@
             return tuple(new[0]), tuple(new[1])
 
         zeros = tuple(jnp.zeros((8, LANES), jnp.float32) for _ in lanes)
-        sums.append(lax.fori_loop(0, cols // 8, exponentials, (zeros, zeros), unroll=4))
+        sums.append(lax.fori_loop(0, cols // 8, exponentials, (zeros, zeros), unroll=8))
 
     row_ids = lax.broadcasted_iota(jnp.int32, (n_col, block), 0)
     placed = [jnp.zeros((n_col, block), jnp.float32)] * 4
@@ -228,7 +228,7 @@
 LOW = 128
 BIAS = 125
 EXTRA = 8
-MORE = 32
+MORE = 2 * EXTRA
 STEP = 32
 
 
@@ -259,16 +259,17 @@
     rest = extra[:, :half] - first.astype(jnp.float32)
     second = rest.astype(jnp.bfloat16)
     third = (rest - second.astype(jnp.float32)).astype(jnp.bfloat16)
-    zeros = jnp.zeros((EXTRA, half), jnp.bfloat16)
-    out[size : size + 2 * EXTRA, :half] = jnp.concatenate([first, second], axis=0)
-    out[size : size + 2 * EXTRA, half:] = jnp.concatenate([third, zeros], axis=0)
-    out[size + 2 * EXTRA :, :] = jnp.zeros((MORE - 2 * EXTRA, width), jnp.bfloat16)
-    out[size + 2 * EXTRA :, :size] = powers[...].T[: MORE - 2 * EXTRA, :].astype(jnp.bfloat16)
+    fourth = powers[...].T[:EXTRA, :].astype(jnp.bfloat16)
+    if size < half:
+        fourth = jnp.concatenate([fourth, jnp.zeros((EXTRA, half - size), jnp.bfloat16)], axis=1)
+    out[size:, :half] = jnp.concatenate([first, second], axis=0)
+    out[size:, half:] = jnp.concatenate([third, fourth], axis=0)
 
 
 def decode_powers(code, size):
-    powers = code[size + 2 * EXTRA :, :size].astype(jnp.float32)
-    return jnp.broadcast_to(powers[0:1, :], (LANES, size)).T * (LOW / (LEVELS - 1))
+    half = code.shape[1] // 2
+    powers = code[size:, half : half + size].astype(jnp.float32)
+    return jnp.broadcast_to(powers[EXTRA : EXTRA + 1, :], (LANES, size)).T * (LOW / (LEVELS - 1))
 
 
 def decode(code, powers, r):
@@ -284,8 +285,8 @@
 
 def decode_extra(code, size):
     half = code.shape[1] // 2
-    left = code[size : size + 2 * EXTRA, :half].astype(jnp.float32)
-    right = code[size : size + 2 * EXTRA, half:].astype(jnp.float32)
+    left = code[size:, :half].astype(jnp.float32)
+    right = code[size:, half:].astype(jnp.float32)
     return left[:EXTRA] + left[EXTRA:] + right[:EXTRA]
 
 
@@ -355,7 +356,7 @@
     codes, before = refs[:n], refs[n:-6]
     out, extra, scalar, value, powers, sems = refs[-6:]
     size, width = base.shape[0] - EXTRA, base.shape[1]
-    combine = functools.partial(functools.reduce, jnp.add) if in_order else by_pairs_added
+    combine = functools.partial(functools.reduce, jnp.add) if in_order else first_and_pairs
     for c, code in enumerate(codes):
         powers[c] = decode_powers(code, size)
     copies = []
@@ -376,8 +377,33 @@
         copy.wait()
 
 
-def by_pairs_added(blocks):
-    return by_pairs(blocks, jnp.add)
+def add_kernel(base, code, out, powers):
+    size, half = base.shape[0] - EXTRA, base.shape[1] // 2
+    powers[...] = decode_powers(code, size)
+    for r in range(0, size, STEP):
+        out[r : r + STEP, :] = base[r : r + STEP, :] + decode(code, powers, r)
+    out[size:, :half] = base[size:, :half] + decode_extra(code, size)
+    out[size:, half:] = jnp.zeros((EXTRA, half), jnp.float32)
+
+
+def added(base, code):
+    vmem = pl.BlockSpec(memory_space=VMEM)
+    return pl.pallas_call(
+        add_kernel,
+        out_shape=jax.ShapeDtypeStruct(base.shape, jnp.float32),
+        in_specs=[vmem] * 2,
+        out_specs=vmem,
+        scratch_shapes=[VMEM((base.shape[0] - EXTRA, LANES), jnp.float32)],
+        compiler_params=pltpu.CompilerParams(vmem_limit_bytes=6 * 2**20),
+        name="added",
+    )(base, code)
+
+
+def first_and_pairs(blocks):
+    if len(blocks) == 1:
+        return blocks[0]
+    pairs = [blocks[0]] + [blocks[i] + blocks[i + 1] for i in range(1, len(blocks), 2)]
+    return by_pairs(pairs, jnp.add)
 
 
 def total_of(coef, base, codes, in_order, before, name):
@@ -495,7 +521,7 @@
             put_extra(far_ref.at[j, block:, :], col_extra)
             return carry
 
-        lax.fori_loop(0, half // block, one, 0)
+        lax.fori_loop(0, half // block, one, 0, unroll=4)
 
 
 def text_grads(scale, coef, place, even, odd, row_lse, col_lse, row_extra, col_extra, texts, tile, order, done):
@@ -548,7 +574,7 @@
         )
         return carry
 
-    lax.fori_loop(0, out_ref.shape[0], one, 0)
+    lax.fori_loop(0, out_ref.shape[0], one, 0, unroll=4)
 
 
 def image_grads(scale, extra, grads, texts, after):
@@ -615,7 +641,10 @@
 
     own, others = pack_images(near, far)
     others = [swap(code, "col", n_col, 2 * j) for j, code in enumerate(others, 1)]
-    grad_image, _, grad_scale = total_of(coef, own, others, False, [text_extra], "grad_image")
+    first, text_extra = lax.optimization_barrier((others[0], text_extra))
+    grad_image, _, grad_scale = total_of(
+        coef, added(own, first), others[1:], False, [text_extra], "grad_image"
+    )
     return grad_image, grad_text, grad_scale.reshape(())
 
 

time: 81.4 us -> 79.7 us (0.979)
  Pallas kernels: 23.5 us -> 22 us
  transfers between devices with their start and end apart: 23 -> 23, of which waited for: 14 -> 14; matrix products, arithmetic and copies ran while one was open for 1% -> 2% of each run, Pallas kernels for 21% -> 20%
where the time goes in v11:
time: 79.7 us; the launch traced here: 79.5 us
  waiting for transfers between devices  32.1 us (40%)
  Pallas kernels  22 us (28%)
  starting transfers between devices  21.4 us (27%)
  other arithmetic  2.43 us (3%)
  between operations  1.59 us (2%)
    ppermute x23, waiting for transfers between devices, swap(): return lax.ppermute(x, axis, [(i, i ^ q) for i in range(n)])  32.1 us
    ppermute x23, starting transfers between devices, swap(): return lax.ppermute(x, axis, [(i, i ^ q) for i in range(n)])  21.4 us
    pallas_call x2, Pallas kernels, stats(): pl.pallas_call(functools.partial(stats_kernel, first, len(texts), block),...  7.98 us
    pallas_call x2, Pallas kernels, text_grads(): pl.pallas_call(functools.partial(text_kernel, tuple(order), len(done), le...  6.79 us
    pallas_call x2, Pallas kernels, total_of(): pl.pallas_call(functools.partial(total_kernel, len(codes), in_order), out...  3.78 us
  transfers between devices with their start and end apart: 23, of which 14 were waited for; matrix products, arithmetic and copies ran while one was open for 2% of the time, Pallas kernels for 20%

profile of v11, /device:TPU:0, one launch (start us, length us, event | category | flops | bytes accessed | tf_op | source)
XLA Modules:
  0.0 79.5 jit_solution(3322673724264315795)
XLA Ops:
  0.6 1.1 %convert_element_type.7.refs_0_.refs_8_.refs_4_ = bf16[256,512]{1,0:T(8,128)(2,1)S(1)} convert(f32[256,512]{1,0:T(8,128)} %param.4) | non-fusion elementwise | flops 131072 | bytes 786432 | tf_op jit(solution)/shard_map/convert_element_type | solution.py:607
  1.7 4.1 %collective-permute-start.4 = (bf16[256,512]{1,0:T(8,128)(2,1)S(1)}, bf16[256,512]{1,0:T(8,128)(2,1)S(1)}, u32[]{:S(2)}, u32[]{:S(2)}) collective-permute-start(bf16[256,512]{1,0:T(8,128)(2,1)S(1)} %convert_element_type.7.refs_0_.refs_8_.refs_4_), channel_id=1, source_target_pairs={{0,16},{8,24},{16,0},{24,8},{1,17},{9,25},{17,1},{25,9},{2,18},{10... | collective-permute-start | bytes 786440 | tf_op jit(solution)/shard_map/ppermute | solution.py:20
  5.8 1.6 %collective-permute-start.3 = (bf16[256,512]{1,0:T(8,128)(2,1)S(1)}, bf16[256,512]{1,0:T(8,128)(2,1)S(1)}, u32[]{:S(2)}, u32[]{:S(2)}) collective-permute-start(bf16[256,512]{1,0:T(8,128)(2,1)S(1)} %convert_element_type.7.refs_0_.refs_8_.refs_4_), channel_id=1, source_target_pairs={{0,8},{8,0},{16,24},{24,16},{1,9},{9,1},{17,25},{25,17},{2,10},{10... | collective-permute-start | bytes 786440 | tf_op jit(solution)/shard_map/ppermute | solution.py:20
  7.4 1.1 %convert_element_type.6.refs_3_ = bf16[256,512]{1,0:T(8,128)(2,1)S(1)} convert(f32[256,512]{1,0:T(8,128)} %param.3) | non-fusion elementwise | flops 131072 | bytes 786432 | tf_op jit(solution)/shard_map/convert_element_type | solution.py:607
  8.5 2.5 %collective-permute-start.2 = (bf16[256,512]{1,0:T(8,128)(2,1)S(1)}, bf16[256,512]{1,0:T(8,128)(2,1)S(1)}, u32[]{:S(2)}, u32[]{:S(2)}) collective-permute-start(bf16[256,512]{1,0:T(8,128)(2,1)S(1)} %convert_element_type.6.refs_3_), channel_id=1, source_target_pairs={{0,6},{1,7},{2,4},{3,5},{4,2},{5,3},{6,0},{7,1},{8,14},{9,15},{10,... | collective-permute-start | bytes 786440 | tf_op jit(solution)/shard_map/ppermute | solution.py:20
  12.0 5.8 %collective-permute-done.4.refs_2_.refs_6_ = bf16[256,512]{1,0:T(8,128)(2,1)S(1)} collective-permute-done((bf16[256,512]{1,0:T(8,128)(2,1)S(1)}, bf16[256,512]{1,0:T(8,128)(2,1)S(1)}, u32[]{:S(2)}, u32[]{:S(2)}) %collective-permute-start.4) | collective-permute-done | bytes 262176 | tf_op jit(solution)/shard_map/ppermute | solution.py:20
  18.0 0.7 collective-permute-done.2.refs_6_
  18.7 3.8 %collective-permute-done.1.refs_5_ = bf16[256,512]{1,0:T(8,128)(2,1)S(1)} collective-permute-done((bf16[256,512]{1,0:T(8,128)(2,1)S(1)}, bf16[256,512]{1,0:T(8,128)(2,1)S(1)}, u32[]{:S(2)}, u32[]{:S(2)}) %collective-permute-start.1) | collective-permute-done | bytes 262176 | tf_op jit(solution)/shard_map/ppermute | solution.py:20
  24.9 5.4 %stats.1 = (bf16[1024,512]{1,0:T(8,128)(2,1)S(1)}, bf16[1024,512]{1,0:T(8,128)(2,1)S(1)}, f32[4,8,256]{2,1,0:T(8,128)S(1)}, f32[3,4,256]{2,1,0:T(4,128)S(1)}, f32[768,2048]{1,0:T(8,128)S(1)}) custom-call(f32[1,1]{1,0:T(1,128)S(6)} %mul.147.coef_ref, s32[1,2]{1,0:T(1,128)S(1)} %add_bitcast_fusion.place_ref, ...), custom_call_target="tpu_custom_call" | custom-call | flops 32212254720 | tf_op jit(solution)/shard_map/stats/pallas_call | solution.py:181
  30.3 2.3 %collective-permute-done.5.refs_0_ = bf16[256,512]{1,0:T(8,128)(2,1)S(1)} collective-permute-done((bf16[256,512]{1,0:T(8,128)(2,1)S(1)}, bf16[256,512]{1,0:T(8,128)(2,1)S(1)}, u32[]{:S(2)}, u32[]{:S(2)}) %collective-permute-start.5) | collective-permute-done | bytes 262176 | tf_op jit(solution)/shard_map/ppermute | solution.py:20
  32.6 2.6 %stats_last.1 = (bf16[256,512]{1,0:T(8,128)(2,1)S(1)}, f32[4,8,256]{2,1,0:T(8,128)S(1)}, f32[3,4,256]{2,1,0:T(4,128)S(1)}, f32[256,2048]{1,0:T(8,128)S(1)}) custom-call(f32[1,1]{1,0:T(1,128)S(6)} %mul.147.coef_ref, s32[1,2]{1,0:T(1,128)S(1)} %add_bitcast_fusion.place_ref, bf16[256,512]{1,0:T(8,128)(2,1)S(1)} %collective-permute-done.5.refs_0_, ...), custom_call_target="tpu_custom_call" | custom-call | flops 10737418240 | tf_op jit(solution)/shard_map/stats_last/pallas_call | solution.py:181
  35.2 1.7 %collective-permute-start.12 = (f32[4,8,256]{2,1,0:T(8,128)S(1)}, f32[4,8,256]{2,1,0:T(8,128)S(1)}, u32[]{:S(2)}, u32[]{:S(2)}) collective-permute-start(f32[4,8,256]{2,1,0:T(8,128)S(1)} %get-tuple-element.52), channel_id=1, source_target_pairs={{0,6},{1,7},{2,4},{3,5},{4,2},{5,3},{6,0},{7,1},{8,14},{9,15},{10,... | collective-permute-start | bytes 98312 | tf_op jit(solution)/shard_map/ppermute | solution.py:20
  36.9 1.3 %collective-permute-start.11 = (f32[4,8,256]{2,1,0:T(8,128)S(1)}, f32[4,8,256]{2,1,0:T(8,128)S(1)}, u32[]{:S(2)}, u32[]{:S(2)}) collective-permute-start(f32[4,8,256]{2,1,0:T(8,128)S(1)} %get-tuple-element.52), channel_id=1, source_target_pairs={{0,4},{1,5},{2,6},{3,7},{4,0},{5,1},{6,2},{7,3},{8,12},{9,13},{10,... | collective-permute-start | bytes 98312 | tf_op jit(solution)/shard_map/ppermute | solution.py:20
  38.2 0.6 collective-permute-start.10
  39.2 3.3 %collective-permute-done.13 = f32[3,4,256]{2,1,0:T(4,128)S(1)} collective-permute-done((f32[3,4,256]{2,1,0:T(4,128)S(1)}, f32[3,4,256]{2,1,0:T(4,128)S(1)}, u32[]{:S(2)}, u32[]{:S(2)}) %collective-permute-start.13) | collective-permute-done | bytes 12320 | tf_op jit(solution)/shard_map/ppermute | solution.py:20
  43.0 4.3 %collective-permute-done.14 = f32[3,4,256]{2,1,0:T(4,128)S(1)} collective-permute-done((f32[3,4,256]{2,1,0:T(4,128)S(1)}, f32[3,4,256]{2,1,0:T(4,128)S(1)}, u32[]{:S(2)}, u32[]{:S(2)}) %collective-permute-start.14) | collective-permute-done | bytes 12320 | tf_op jit(solution)/shard_map/ppermute | solution.py:20
  47.4 1.8 %text_grads_1.1 = (bf16[256,2048]{1,0:T(8,128)(2,1)S(1)}, bf16[272,512]{1,0:T(8,128)(2,1)S(1)}) custom-call(f32[1,1]{1,0:T(1,128)} %bitcast.277.scale_ref, f32[1,1]{1,0:T(1,128)S(6)} %mul.147.coef_ref, s32[1,2]{1,0:T(1,128)S(1)} %add_bitcast_fusion.place_ref, bf16[1024,512]{1,0:T(8,128)(2,1)S(1)} %get-tuple-element.47.refs_1_.refs_0_, ...), custom_call_target="tpu_custom_call" | custom-call | flops 21474836480 | tf_op jit(solution)/shard_map/text_grads_1/pallas_call | solution.py:547
  49.7 5.0 %text_grads_3.1 = (bf16[256,2048]{1,0:T(8,128)(2,1)S(1)}, bf16[256,2048]{1,0:T(8,128)(2,1)S(1)}, bf16[256,2048]{1,0:T(8,128)(2,1)S(1)}, f32[264,512]{1,0:T(8,128...) custom-call(f32[1,1]{1,0:T(1,128)} %bitcast.278.scale_ref, ...), custom_call_target="tpu_custom_call" | custom-call | flops 64424509440 | tf_op jit(solution)/shard_map/text_grads_3/pallas_call | solution.py:547
  54.7 1.1 %collective-permute-done.16.refs_0_ = bf16[272,512]{1,0:T(8,128)(2,1)S(1)} collective-permute-done((bf16[272,512]{1,0:T(8,128)(2,1)S(1)}, bf16[272,512]{1,0:T(8,128)(2,1)S(1)}, u32[]{:S(2)}, u32[]{:S(2)}) %collective-permute-start.16) | collective-permute-done | bytes 278560 | tf_op jit(solution)/shard_map/ppermute | solution.py:20
  55.8 0.7 pack_text.1.refs_8_
  56.5 1.7 %collective-permute-start.20 = (bf16[272,512]{1,0:T(8,128)(2,1)S(1)}, bf16[272,512]{1,0:T(8,128)(2,1)S(1)}, u32[]{:S(2)}, u32[]{:S(2)}) collective-permute-start(bf16[272,512]{1,0:T(8,128)(2,1)S(1)} %pack_text.1.refs_8_), channel_id=1, source_target_pairs={{0,16},{8,24},{16,0},{24,8},{1,17},{9,25},{17,1},{25,9},{2,18},{10... | collective-permute-start | bytes 835592 | tf_op jit(solution)/shard_map/ppermute | solution.py:20
  58.2 1.3 %image_grads.1.near = f32[4,264,512]{2,1,0:T(8,128)S(1)} custom-call(f32[1,1]{1,0:T(1,128)} %bitcast.279.scale_ref, f32[4,256]{1,0:T(4,128)S(1)} %fusion.34.refs_5_.extra, bf16[256,2048]{1,0:T(8,128)(2,1)S(1)} %get-tuple-element.61.refs_0_, bf16[256,2048]{1,0:T(8,128)(2,1)S(1)} %get-tuple-element.62.refs_1_, ...), custom_call_target="tpu_custom_call" | custom-call | flops 21474836480 | tf_op jit(solution)/shard_map/image_grads/pallas_call | solution.py:586
  59.5 1.0 %collective-permute-start.19 = (bf16[272,512]{1,0:T(8,128)(2,1)S(1)}, bf16[272,512]{1,0:T(8,128)(2,1)S(1)}, u32[]{:S(2)}, u32[]{:S(2)}) collective-permute-start(bf16[272,512]{1,0:T(8,128)(2,1)S(1)} %get-tuple-element.72), channel_id=1, source_target_pairs={{0,8},{8,0},{16,24},{24,16},{1,9},{9,1},{17,25},{25,17},{2,10},{10... | collective-permute-start | bytes 835592 | tf_op jit(solution)/shard_map/ppermute | solution.py:20
  60.6 1.1 %pack_images.1 = (f32[264,512]{1,0:T(8,128)S(1)}, bf16[272,512]{1,0:T(8,128)(2,1)S(1)}, bf16[272,512]{1,0:T(8,128)(2,1)S(1)}, bf16[272,512]{1,0:T(8,128)(2,1)S(1)}) custom-call(f32[4,264,512]{2,1,0:T(8,128)S(1)} %image_grads.1.near, f32[4,264,512]{2,1,0:T(8,128)S(1)} %collective-permute-done.17.far), custom_call_target="tpu_custom_call" | custom-call | tf_op jit(solution)/shard_map/pack_images/pallas_call | solution.py:343
  61.7 1.6 %collective-permute-start.18 = (bf16[272,512]{1,0:T(8,128)(2,1)S(1)}, bf16[272,512]{1,0:T(8,128)(2,1)S(1)}, u32[]{:S(2)}, u32[]{:S(2)}) collective-permute-start(bf16[272,512]{1,0:T(8,128)(2,1)S(1)} %get-tuple-element.70), channel_id=1, source_target_pairs={{0,2},{1,3},{2,0},{3,1},{4,6},{5,7},{6,4},{7,5},{8,10},{9,11},{10,... | collective-permute-start | bytes 835592 | tf_op jit(solution)/shard_map/ppermute | solution.py:20
  63.3 0.7 collective-permute-start.21
  64.0 1.3 %collective-permute-start.22 = (bf16[272,512]{1,0:T(8,128)(2,1)S(1)}, bf16[272,512]{1,0:T(8,128)(2,1)S(1)}, u32[]{:S(2)}, u32[]{:S(2)}) collective-permute-start(bf16[272,512]{1,0:T(8,128)(2,1)S(1)} %get-tuple-element.76), channel_id=1, source_target_pairs={{0,6},{1,7},{2,4},{3,5},{4,2},{5,3},{6,0},{7,1},{8,14},{9,15},{10,... | collective-permute-start | bytes 835592 | tf_op jit(solution)/shard_map/ppermute | solution.py:20
  65.3 6.3 %collective-permute-done.20.refs_1_ = bf16[272,512]{1,0:T(8,128)(2,1)S(1)} collective-permute-done((bf16[272,512]{1,0:T(8,128)(2,1)S(1)}, bf16[272,512]{1,0:T(8,128)(2,1)S(1)}, u32[]{:S(2)}, u32[]{:S(2)}) %collective-permute-start.20) | collective-permute-done | bytes 278560 | tf_op jit(solution)/shard_map/ppermute | solution.py:20
  71.5 1.0 %collective-permute-done.19.refs_0_ = bf16[272,512]{1,0:T(8,128)(2,1)S(1)} collective-permute-done((bf16[272,512]{1,0:T(8,128)(2,1)S(1)}, bf16[272,512]{1,0:T(8,128)(2,1)S(1)}, u32[]{:S(2)}, u32[]{:S(2)}) %collective-permute-start.19) | collective-permute-done | bytes 278560 | tf_op jit(solution)/shard_map/ppermute | solution.py:20
  72.5 1.8 %grad_text.1 = (f32[256,512]{1,0:T(8,128)}, f32[8,256]{1,0:T(8,128)S(1)}, f32[1,1]{1,0:T(1,128)}) custom-call(f32[1,1]{1,0:T(1,128)S(6)} %mul.147.coef_ref, f32[264,512]{1,0:T(8,128)S(1)} %get-tuple-element.71.base, bf16[272,512]{1,0:T(8,128)(2,1)S(1)} %collective-permute-done.19.refs_0_, bf16[272,512]{1,0:T(8,128)(2,1)S(1)} %collective-permute-done.20.refs_1_), custom_call_target="tpu_custom_call" | custom-call | tf_op jit(solution)/shard_map/grad_text/pallas_call | solution.py:413
  74.7 2.7 %collective-permute-done.21.refs_0_ = bf16[272,512]{1,0:T(8,128)(2,1)S(1)} collective-permute-done((bf16[272,512]{1,0:T(8,128)(2,1)S(1)}, bf16[272,512]{1,0:T(8,128)(2,1)S(1)}, u32[]{:S(2)}, u32[]{:S(2)}) %collective-permute-start.21) | collective-permute-done | bytes 278560 | tf_op jit(solution)/shard_map/ppermute | solution.py:20
  77.4 1.9 %grad_image.1 = (f32[256,512]{1,0:T(8,128)}, f32[8,256]{1,0:T(8,128)}, f32[1,1]{1,0:T(1,128)}) custom-call(f32[1,1]{1,0:T(1,128)S(6)} %mul.147.coef_ref, f32[264,512]{1,0:T(8,128)S(1)} %added.1.base, bf16[272,512]{1,0:T(8,128)(2,1)S(1)} %collective-permute-done.21.refs_0_, bf16[272,512]{1,0:T(8,128)(2,1)S(1)} %collective-permute-done.22.refs_1_, ...), custom_call_target="tpu_custom_call" | custom-call | tf_op jit(solution)/shard_map/grad_image/pallas_call | solution.py:413
  (37 shorter events, 4.9 us)
Async XLA Ops:
  1.7 16.1 %collective-permute-start.4 = (bf16[256,512]{1,0:T(8,128)(2,1)S(1)}, bf16[256,512]{1,0:T(8,128)(2,1)S(1)}, u32[]{:S(2)}, u32[]{:S(2)}) collective-permute-start(bf16[256,512]{1,0:T(8,128)(2,1)S(1)} %convert_element_type.7.refs_0_.refs_8_.refs_4_), channel_id=1, source_target_pairs={{0,16},{8,24},{16,0},{24,8},{1,17},{9,25},{17,1},{25,9},{2,18},{10... | collective-permute-start | bytes 786440 | tf_op jit(solution)/shard_map/ppermute | solution.py:20
  5.8 12.2 %collective-permute-start.3 = (bf16[256,512]{1,0:T(8,128)(2,1)S(1)}, bf16[256,512]{1,0:T(8,128)(2,1)S(1)}, u32[]{:S(2)}, u32[]{:S(2)}) collective-permute-start(bf16[256,512]{1,0:T(8,128)(2,1)S(1)} %convert_element_type.7.refs_0_.refs_8_.refs_4_), channel_id=1, source_target_pairs={{0,8},{8,0},{16,24},{24,16},{1,9},{9,1},{17,25},{25,17},{2,10},{10... | collective-permute-start | bytes 786440 | tf_op jit(solution)/shard_map/ppermute | solution.py:20
  8.5 10.3 %collective-permute-start.2 = (bf16[256,512]{1,0:T(8,128)(2,1)S(1)}, bf16[256,512]{1,0:T(8,128)(2,1)S(1)}, u32[]{:S(2)}, u32[]{:S(2)}) collective-permute-start(bf16[256,512]{1,0:T(8,128)(2,1)S(1)} %convert_element_type.6.refs_3_), channel_id=1, source_target_pairs={{0,6},{1,7},{2,4},{3,5},{4,2},{5,3},{6,0},{7,1},{8,14},{9,15},{10,... | collective-permute-start | bytes 786440 | tf_op jit(solution)/shard_map/ppermute | solution.py:20
  11.0 11.6 %collective-permute-start.1 = (bf16[256,512]{1,0:T(8,128)(2,1)S(1)}, bf16[256,512]{1,0:T(8,128)(2,1)S(1)}, u32[]{:S(2)}, u32[]{:S(2)}) collective-permute-start(bf16[256,512]{1,0:T(8,128)(2,1)S(1)} %convert_element_type.6.refs_3_), channel_id=1, source_target_pairs={{0,4},{1,5},{2,6},{3,7},{4,0},{5,1},{6,2},{7,3},{8,12},{9,13},{10,... | collective-permute-start | bytes 786440 | tf_op jit(solution)/shard_map/ppermute | solution.py:20
  11.5 11.1 %collective-permute-start = (bf16[256,512]{1,0:T(8,128)(2,1)S(1)}, bf16[256,512]{1,0:T(8,128)(2,1)S(1)}, u32[]{:S(2)}, u32[]{:S(2)}) collective-permute-start(bf16[256,512]{1,0:T(8,128)(2,1)S(1)} %convert_element_type.6.refs_3_), channel_id=1, source_target_pairs={{0,2},{1,3},{2,0},{3,1},{4,6},{5,7},{6,4},{7,5},{8,10},{9,11},{10,... | collective-permute-start | bytes 786440 | tf_op jit(solution)/shard_map/ppermute | solution.py:20
  17.8 6.5 %collective-permute-start.6 = (bf16[256,512]{1,0:T(8,128)(2,1)S(1)}, bf16[256,512]{1,0:T(8,128)(2,1)S(1)}, u32[]{:S(2)}, u32[]{:S(2)}) collective-permute-start(bf16[256,512]{1,0:T(8,128)(2,1)S(1)} %convert_element_type.6.refs_3_), channel_id=1, source_target_pairs={{0,1},{1,0},{2,3},{3,2},{4,5},{5,4},{6,7},{7,6},{8,9},{9,8},{10,11... | collective-permute-start | bytes 786440 | tf_op jit(solution)/shard_map/ppermute | solution.py:20
  22.6 1.7 %collective-permute-start.7 = (bf16[256,512]{1,0:T(8,128)(2,1)S(1)}, bf16[256,512]{1,0:T(8,128)(2,1)S(1)}, u32[]{:S(2)}, u32[]{:S(2)}) collective-permute-start(bf16[256,512]{1,0:T(8,128)(2,1)S(1)} %collective-permute-done.refs_4_), channel_id=1, source_target_pairs={{0,1},{1,0},{2,3},{3,2},{4,5},{5,4},{6,7},{7,6},{8,9},{9,8},{10,11... | collective-permute-start | bytes 786440 | tf_op jit(solution)/shard_map/ppermute | solution.py:20
  22.6 1.9 %collective-permute-start.8 = (bf16[256,512]{1,0:T(8,128)(2,1)S(1)}, bf16[256,512]{1,0:T(8,128)(2,1)S(1)}, u32[]{:S(2)}, u32[]{:S(2)}) collective-permute-start(bf16[256,512]{1,0:T(8,128)(2,1)S(1)} %collective-permute-done.1.refs_5_), channel_id=1, source_target_pairs={{0,1},{1,0},{2,3},{3,2},{4,5},{5,4},{6,7},{7,6},{8,9},{9,8},{10,11... | collective-permute-start | bytes 786440 | tf_op jit(solution)/shard_map/ppermute | solution.py:20
  23.1 1.8 %collective-permute-start.9 = (bf16[256,512]{1,0:T(8,128)(2,1)S(1)}, bf16[256,512]{1,0:T(8,128)(2,1)S(1)}, u32[]{:S(2)}, u32[]{:S(2)}) collective-permute-start(bf16[256,512]{1,0:T(8,128)(2,1)S(1)} %collective-permute-done.2.refs_6_), channel_id=1, source_target_pairs={{0,1},{1,0},{2,3},{3,2},{4,5},{5,4},{6,7},{7,6},{8,9},{9,8},{10,11... | collective-permute-start | bytes 786440 | tf_op jit(solution)/shard_map/ppermute | solution.py:20
  23.9 8.7 %collective-permute-start.5 = (bf16[256,512]{1,0:T(8,128)(2,1)S(1)}, bf16[256,512]{1,0:T(8,128)(2,1)S(1)}, u32[]{:S(2)}, u32[]{:S(2)}) collective-permute-start(bf16[256,512]{1,0:T(8,128)(2,1)S(1)} %collective-permute-done.4.refs_2_.refs_6_), channel_id=1, source_target_pairs={{0,8},{8,0},{16,24},{24,16},{1,9},{9,1},{17,25},{25,17},{2,10},{10... | collective-permute-start | bytes 786440 | tf_op jit(solution)/shard_map/ppermute | solution.py:20
  35.2 7.3 %collective-permute-start.12 = (f32[4,8,256]{2,1,0:T(8,128)S(1)}, f32[4,8,256]{2,1,0:T(8,128)S(1)}, u32[]{:S(2)}, u32[]{:S(2)}) collective-permute-start(f32[4,8,256]{2,1,0:T(8,128)S(1)} %get-tuple-element.52), channel_id=1, source_target_pairs={{0,6},{1,7},{2,4},{3,5},{4,2},{5,3},{6,0},{7,1},{8,14},{9,15},{10,... | collective-permute-start | bytes 98312 | tf_op jit(solution)/shard_map/ppermute | solution.py:20
  36.9 5.6 %collective-permute-start.11 = (f32[4,8,256]{2,1,0:T(8,128)S(1)}, f32[4,8,256]{2,1,0:T(8,128)S(1)}, u32[]{:S(2)}, u32[]{:S(2)}) collective-permute-start(f32[4,8,256]{2,1,0:T(8,128)S(1)} %get-tuple-element.52), channel_id=1, source_target_pairs={{0,4},{1,5},{2,6},{3,7},{4,0},{5,1},{6,2},{7,3},{8,12},{9,13},{10,... | collective-permute-start | bytes 98312 | tf_op jit(solution)/shard_map/ppermute | solution.py:20
  38.2 4.3 %collective-permute-start.10 = (f32[4,8,256]{2,1,0:T(8,128)S(1)}, f32[4,8,256]{2,1,0:T(8,128)S(1)}, u32[]{:S(2)}, u32[]{:S(2)}) collective-permute-start(f32[4,8,256]{2,1,0:T(8,128)S(1)} %get-tuple-element.52), channel_id=1, source_target_pairs={{0,2},{1,3},{2,0},{3,1},{4,6},{5,7},{6,4},{7,5},{8,10},{9,11},{10,... | collective-permute-start | bytes 98312 | tf_op jit(solution)/shard_map/ppermute | solution.py:20
  38.7 3.7 %collective-permute-start.13 = (f32[3,4,256]{2,1,0:T(4,128)S(1)}, f32[3,4,256]{2,1,0:T(4,128)S(1)}, u32[]{:S(2)}, u32[]{:S(2)}) collective-permute-start(f32[3,4,256]{2,1,0:T(4,128)S(1)} %get-tuple-element.51), channel_id=1, source_target_pairs={{0,8},{8,0},{16,24},{24,16},{1,9},{9,1},{17,25},{25,17},{2,10},{10... | collective-permute-start | bytes 36872 | tf_op jit(solution)/shard_map/ppermute | solution.py:20
  42.6 4.7 %collective-permute-start.14 = (f32[3,4,256]{2,1,0:T(4,128)S(1)}, f32[3,4,256]{2,1,0:T(4,128)S(1)}, u32[]{:S(2)}, u32[]{:S(2)}) collective-permute-start(f32[3,4,256]{2,1,0:T(4,128)S(1)} %pad_maximum_fusion.1), channel_id=1, source_target_pairs={{0,16},{8,24},{16,0},{24,8},{1,17},{9,25},{17,1},{25,9},{2,18},{10... | collective-permute-start | bytes 36872 | tf_op jit(solution)/shard_map/ppermute | solution.py:20
  43.0 4.3 %collective-permute-start.15 = (f32[4,8,256]{2,1,0:T(8,128)S(1)}, f32[4,8,256]{2,1,0:T(8,128)S(1)}, u32[]{:S(2)}, u32[]{:S(2)}) collective-permute-start(f32[4,8,256]{2,1,0:T(8,128)S(1)} %pad_maximum_fusion), channel_id=1, source_target_pairs={{0,1},{1,0},{2,3},{3,2},{4,5},{5,4},{6,7},{7,6},{8,9},{9,8},{10,11... | collective-permute-start | bytes 98312 | tf_op jit(solution)/shard_map/ppermute | solution.py:20
  49.2 6.6 %collective-permute-start.16 = (bf16[272,512]{1,0:T(8,128)(2,1)S(1)}, bf16[272,512]{1,0:T(8,128)(2,1)S(1)}, u32[]{:S(2)}, u32[]{:S(2)}) collective-permute-start(bf16[272,512]{1,0:T(8,128)(2,1)S(1)} %get-tuple-element.65), channel_id=1, source_target_pairs={{0,8},{8,0},{16,24},{24,16},{1,9},{9,1},{17,25},{25,17},{2,10},{10... | collective-permute-start | bytes 835592 | tf_op jit(solution)/shard_map/ppermute | solution.py:20
  54.6 4.9 %collective-permute-start.17 = (f32[4,264,512]{2,1,0:T(8,128)S(1)}, f32[4,264,512]{2,1,0:T(8,128)S(1)}, u32[]{:S(2)}, u32[]{:S(2)}) collective-permute-start(f32[4,264,512]{2,1,0:T(8,128)S(1)} %get-tuple-element.67), channel_id=1, source_target_pairs={{0,1},{1,0},{2,3},{3,2},{4,5},{5,4},{6,7},{7,6},{8,9},{9,8},{10,11... | collective-permute-start | bytes 6488072 | tf_op jit(solution)/shard_map/ppermute | solution.py:20
  56.5 15.0 %collective-permute-start.20 = (bf16[272,512]{1,0:T(8,128)(2,1)S(1)}, bf16[272,512]{1,0:T(8,128)(2,1)S(1)}, u32[]{:S(2)}, u32[]{:S(2)}) collective-permute-start(bf16[272,512]{1,0:T(8,128)(2,1)S(1)} %pack_text.1.refs_8_), channel_id=1, source_target_pairs={{0,16},{8,24},{16,0},{24,8},{1,17},{9,25},{17,1},{25,9},{2,18},{10... | collective-permute-start | bytes 835592 | tf_op jit(solution)/shard_map/ppermute | solution.py:20
  59.5 13.0 %collective-permute-start.19 = (bf16[272,512]{1,0:T(8,128)(2,1)S(1)}, bf16[272,512]{1,0:T(8,128)(2,1)S(1)}, u32[]{:S(2)}, u32[]{:S(2)}) collective-permute-start(bf16[272,512]{1,0:T(8,128)(2,1)S(1)} %get-tuple-element.72), channel_id=1, source_target_pairs={{0,8},{8,0},{16,24},{24,16},{1,9},{9,1},{17,25},{25,17},{2,10},{10... | collective-permute-start | bytes 835592 | tf_op jit(solution)/shard_map/ppermute | solution.py:20
  61.7 12.6 %collective-permute-start.18 = (bf16[272,512]{1,0:T(8,128)(2,1)S(1)}, bf16[272,512]{1,0:T(8,128)(2,1)S(1)}, u32[]{:S(2)}, u32[]{:S(2)}) collective-permute-start(bf16[272,512]{1,0:T(8,128)(2,1)S(1)} %get-tuple-element.70), channel_id=1, source_target_pairs={{0,2},{1,3},{2,0},{3,1},{4,6},{5,7},{6,4},{7,5},{8,10},{9,11},{10,... | collective-permute-start | bytes 835592 | tf_op jit(solution)/shard_map/ppermute | solution.py:20
  63.3 14.1 %collective-permute-start.21 = (bf16[272,512]{1,0:T(8,128)(2,1)S(1)}, bf16[272,512]{1,0:T(8,128)(2,1)S(1)}, u32[]{:S(2)}, u32[]{:S(2)}) collective-permute-start(bf16[272,512]{1,0:T(8,128)(2,1)S(1)} %get-tuple-element.75), channel_id=1, source_target_pairs={{0,4},{1,5},{2,6},{3,7},{4,0},{5,1},{6,2},{7,3},{8,12},{9,13},{10,... | collective-permute-start | bytes 835592 | tf_op jit(solution)/shard_map/ppermute | solution.py:20
  64.0 13.4 %collective-permute-start.22 = (bf16[272,512]{1,0:T(8,128)(2,1)S(1)}, bf16[272,512]{1,0:T(8,128)(2,1)S(1)}, u32[]{:S(2)}, u32[]{:S(2)}) collective-permute-start(bf16[272,512]{1,0:T(8,128)(2,1)S(1)} %get-tuple-element.76), channel_id=1, source_target_pairs={{0,6},{1,7},{2,4},{3,5},{4,2},{5,3},{6,0},{7,1},{8,14},{9,15},{10,... | collective-permute-start | bytes 835592 | tf_op jit(solution)/shard_map/ppermute | solution.py:20

commit v12 on v11

--- a/solution.py
+++ b/solution.py
@@ -32,13 +32,17 @@
     return lax.dot_general(a, b, (((1,), (1,)), ((), ())), preferred_element_type=jnp.float32)
 
 
-def stats_kernel(first, n_text, block, coef_ref, place_ref, *refs):
-    texts, refs = refs[:n_text], refs[n_text:]
+def stats_kernel(first, keep, n_text, block, coef_ref, place_ref, *refs):
     coef = coef_ref[0, 0]
     r_place, c_place = place_ref[0, 0], place_ref[0, 1]
-    *refs, row_max, col_max, col_sum, col_dot, row_diag = refs
+    texts, refs = refs[:n_text], refs[n_text:]
+    *refs, col_sum, col_dot, row_diag = refs
+    if keep:
+        *refs, tile, other, row_max, col_max = refs
+    else:
+        *refs, tile, row_max, col_max = refs
     if first:
-        *refs, even, odd, row_ref, col_ref, tile = refs
+        *refs, even, odd, row_ref, col_ref = refs
         halves = (even, odd)
         each = len(refs) // 2
         for i, piece in enumerate(refs):
@@ -46,7 +50,7 @@
             halves[i // each][at : at + block, :] = piece[...]
         before = None
     else:
-        even, odd, *before, last, row_ref, col_ref, tile = refs
+        even, odd, *before, last, row_ref, col_ref = refs
         halves = (even, odd)
         last[...] = functools.reduce(jnp.add, [text[...] for text in texts])
         texts, n_text = [last], 1
@@ -110,7 +114,11 @@
                 e = jnp.exp2(x - row_max[0:1, lane : lane + LANES])
                 new[0].append(acc[0][n] + e)
                 new[1].append(acc[1][n] + e * x)
+                if keep:
+                    tile[part, lane : lane + LANES] = e
                 e = jnp.exp2(x - top)
+                if keep:
+                    other[part, lane : lane + LANES] = e
                 total = e if total is None else total + e
                 dot = e * x if dot is None else dot + e * x
             col_sum[part, :] = total
@@ -167,19 +175,14 @@
         jax.ShapeDtypeStruct((4, n_col, block), jnp.float32),
         jax.ShapeDtypeStruct((3, n_row, block), jnp.float32),
     ]
-    scratch = [
-        VMEM((8, rows), jnp.float32),
-        VMEM((cols, LANES), jnp.float32),
-        VMEM((cols, LANES), jnp.float32),
-        VMEM((cols, LANES), jnp.float32),
-        VMEM((8, rows), jnp.float32),
-    ]
+    held = [(cols, rows), (cols, rows), (8, rows), (cols, LANES)]
+    scratch = [VMEM((cols, LANES), jnp.float32)] * 2 + [VMEM((8, rows), jnp.float32)]
     if keep:
-        out_shape.append(jax.ShapeDtypeStruct((cols, rows), jnp.float32))
+        out_shape += [jax.ShapeDtypeStruct(shape, jnp.float32) for shape in held]
     else:
-        scratch.insert(0, VMEM((cols, rows), jnp.float32))
+        scratch = [VMEM(shape, jnp.float32) for shape in held[1:]] + scratch
     return pl.pallas_call(
-        functools.partial(stats_kernel, first, len(texts), block),
+        functools.partial(stats_kernel, first, keep, len(texts) if first else 1, block),
         out_shape=tuple(out_shape),
         in_specs=[smem, smem] + [vmem] * (len(texts) + len(images) + len(before)),
         out_specs=(vmem,) * len(out_shape),
@@ -214,7 +217,9 @@
 
 def exchanged(row_parts, col_parts, n_col, n_row):
     rows = [swap(row_parts, "col", n_col, q) for q in range(2, n_col, 2)]
-    cols = swap(col_parts, "row", n_row, 1)
+    count = col_parts.shape[0]
+    fill = row_parts.size // col_parts.size + 1
+    cols = swap(jnp.concatenate([col_parts] * fill), "row", n_row, 1)[:count]
     rows, cols = lax.optimization_barrier((rows, cols))
     rows = by_pairs([list(x) for x in (row_parts, *rows)], merged)
     cols = merged(list(col_parts), list(cols))
@@ -357,6 +362,10 @@
     out, extra, scalar, value, powers, sems = refs[-6:]
     size, width = base.shape[0] - EXTRA, base.shape[1]
     combine = functools.partial(functools.reduce, jnp.add) if in_order else first_and_pairs
+    more = combine([base[size:, : width // 2]] + [decode_extra(code, size) for code in codes])
+    more = sum([b[...] for b in before], more)
+    extra[...] = more
+    scalar[0, 0] = jnp.sum(more) / coef_ref[0, 0]
     for c, code in enumerate(codes):
         powers[c] = decode_powers(code, size)
     copies = []
@@ -369,10 +378,6 @@
             )
         copies.append(pltpu.make_async_copy(value.at[part], out.at[part], sems.at[i]))
         copies[-1].start()
-    more = combine([base[size:, : width // 2]] + [decode_extra(code, size) for code in codes])
-    more = sum([b[...] for b in before], more)
-    extra[...] = more
-    scalar[0, 0] = jnp.sum(more) / coef_ref[0, 0]
     for copy in copies:
         copy.wait()
 
@@ -422,7 +427,7 @@
         scratch_shapes=[
             VMEM((size, width), jnp.float32),
             VMEM((len(codes), size, LANES), jnp.float32),
-            pltpu.SemaphoreType.DMA((4,)),
+            pltpu.SemaphoreType.DMA((8,)),
         ],
         compiler_params=pltpu.CompilerParams(vmem_limit_bytes=8 * 2**20),
         name=name,
@@ -437,6 +442,8 @@
     size = text.shape[0]
     block = size
     col_lse_down = jnp.broadcast_to(col_lse[pl.ds(r_place ^ t, 1), :], (LANES, size)).T
+    if tile:
+        col_scale = 0.5 * jnp.exp2(tile[3][...] - col_lse_down)
     text_id = c_place * n_row + (r_place ^ t)
     step = 32
     lane_ids = lax.broadcasted_iota(jnp.int32, (step, LANES), 1)
@@ -446,22 +453,29 @@
 
         def one(j, carry):
             at = pl.multiple_of(j * block + which * half, block)
-            if tile is None:
+            column = c_place ^ (2 * j + which)
+            lse = row_lse[pl.ds(column, 1), :]
+            if tile:
+                row_scale = 0.5 * jnp.exp2(tile[2][0:1, pl.ds(at, block)] - lse)
+            else:
                 image = images[pl.ds(pl.multiple_of(j * block, block), block), :]
                 xs = nt_dot(text[...], image) * coef
-            column = c_place ^ (2 * j + which)
             same = jnp.where(r_place * n_col + column == text_id, 1.0, 0.0)
-            lse = row_lse[pl.ds(column, 1), :]
             for r in range(0, size, step):
                 for lane in range(0, block, LANES):
-                    if tile is None:
+                    if tile:
+                        g = (
+                            tile[0][r : r + step, pl.ds(at + lane, LANES)]
+                            * row_scale[:, lane : lane + LANES]
+                            + tile[1][r : r + step, pl.ds(at + lane, LANES)]
+                            * col_scale[r : r + step, :]
+                        )
+                    else:
                         x = xs[r : r + step, lane : lane + LANES]
-                    else:
-                        x = tile[r : r + step, pl.ds(at + lane, LANES)]
-                    e = jnp.exp2(x - lse[:, lane : lane + LANES]) + jnp.exp2(
-                        x - col_lse_down[r : r + step, :]
-                    )
-                    g = 0.5 * e
+                        g = 0.5 * (
+                            jnp.exp2(x - lse[:, lane : lane + LANES])
+                            + jnp.exp2(x - col_lse_down[r : r + step, :])
+                        )
                     if lane <= r < lane + LANES:
                         g = g - jnp.where(row_ids + (r - lane) == lane_ids, same, 0.0)
                     grad_ref[r : r + step, pl.ds(at + lane, LANES)] = g.astype(jnp.bfloat16)
@@ -496,14 +510,16 @@
     even, odd, row_lse, col_lse, row_extra, col_extra = refs[:6]
     n = len(order)
     texts, rest = refs[6 : 6 + n], refs[6 + n :]
-    if kept:
-        tile, rest = rest[0], rest[1:]
+    tile, rest = rest[:kept], rest[kept:]
     done_grads, done_texts, rest = rest[:n_done], rest[n_done : 2 * n_done], rest[2 * n_done :]
     grads, outs = rest[:n], rest[n : 2 * n]
     for i, t in enumerate(order):
         text_block(
             texts[i],
-            tile.at[pl.ds((t - min(order)) * block, block)] if kept else None,
+            [
+                held if i == 2 else held.at[pl.ds((t - min(order)) * block, block)]
+                for i, held in enumerate(tile)
+            ],
             t, (even, odd), row_lse, col_lse, place_ref, scale_ref, coef_ref, row_extra, grads[i], outs[i], *rest[-2:]
         )
     if n_done:

time: 79.7 us -> 79.9 us (level)
  waiting for transfers between devices: 32.1 us -> 29.4 us
  Pallas kernels: 22 us -> 23.9 us
  starting transfers between devices: 21.4 us -> 22.3 us
    ppermute x23, waiting for transfers between devices: 32.1 us -> 29.4 us  [swap(): return lax.ppermute(x, axis, [(i, i ^ q) for i in range(n)])]
    pallas_call x2, Pallas kernels: 7.98 us -> 9.63 us  [stats(): pl.pallas_call(functools.partial(stats_kernel, first, keep, len(texts) if...]
    ppermute x23, starting transfers between devices: 21.4 us -> 22.3 us  [swap(): return lax.ppermute(x, axis, [(i, i ^ q) for i in range(n)])]
  transfers between devices with their start and end apart: 23 -> 23, of which waited for: 14 -> 15; matrix products, arithmetic and copies ran while one was open for 2% -> 2% of each run, Pallas kernels for 20% -> 21%
where the time goes in v12:
time: 79.9 us; the launch traced here: 79.7 us
  waiting for transfers between devices  29.4 us (37%)
  Pallas kernels  23.9 us (30%)
  starting transfers between devices  22.3 us (28%)
  other arithmetic  2.44 us (3%)
  between operations  1.6 us (2%)
    ppermute x23, waiting for transfers between devices, swap(): return lax.ppermute(x, axis, [(i, i ^ q) for i in range(n)])  29.4 us
    ppermute x23, starting transfers between devices, swap(): return lax.ppermute(x, axis, [(i, i ^ q) for i in range(n)])  22.3 us
    pallas_call x2, Pallas kernels, stats(): pl.pallas_call(functools.partial(stats_kernel, first, keep, len(texts) if...  9.63 us
    pallas_call x2, Pallas kernels, text_grads(): pl.pallas_call(functools.partial(text_kernel, tuple(order), len(done), le...  6.99 us
    pallas_call x2, Pallas kernels, total_of(): pl.pallas_call(functools.partial(total_kernel, len(codes), in_order), out...  3.79 us
  transfers between devices with their start and end apart: 23, of which 15 were waited for; matrix products, arithmetic and copies ran while one was open for 2% of the time, Pallas kernels for 21%

profile of v12, /device:TPU:0, one launch (start us, length us, event | category | flops | bytes accessed | tf_op | source)
XLA Modules:
  0.0 79.7 jit_solution(14753255276143832841)
XLA Ops:
  0.6 1.1 %convert_element_type.7.refs_0_.refs_8_.refs_4_ = bf16[256,512]{1,0:T(8,128)(2,1)S(1)} convert(f32[256,512]{1,0:T(8,128)} %param.4) | non-fusion elementwise | flops 131072 | bytes 786432 | tf_op jit(solution)/shard_map/convert_element_type | solution.py:623
  1.7 4.1 %collective-permute-start.4 = (bf16[256,512]{1,0:T(8,128)(2,1)S(1)}, bf16[256,512]{1,0:T(8,128)(2,1)S(1)}, u32[]{:S(2)}, u32[]{:S(2)}) collective-permute-start(bf16[256,512]{1,0:T(8,128)(2,1)S(1)} %convert_element_type.7.refs_0_.refs_8_.refs_4_), channel_id=1, source_target_pairs={{0,16},{8,24},{16,0},{24,8},{1,17},{9,25},{17,1},{25,9},{2,18},{10... | collective-permute-start | bytes 786440 | tf_op jit(solution)/shard_map/ppermute | solution.py:20
  5.8 1.6 %collective-permute-start.3 = (bf16[256,512]{1,0:T(8,128)(2,1)S(1)}, bf16[256,512]{1,0:T(8,128)(2,1)S(1)}, u32[]{:S(2)}, u32[]{:S(2)}) collective-permute-start(bf16[256,512]{1,0:T(8,128)(2,1)S(1)} %convert_element_type.7.refs_0_.refs_8_.refs_4_), channel_id=1, source_target_pairs={{0,8},{8,0},{16,24},{24,16},{1,9},{9,1},{17,25},{25,17},{2,10},{10... | collective-permute-start | bytes 786440 | tf_op jit(solution)/shard_map/ppermute | solution.py:20
  7.4 1.1 %convert_element_type.6.refs_3_ = bf16[256,512]{1,0:T(8,128)(2,1)S(1)} convert(f32[256,512]{1,0:T(8,128)} %param.3) | non-fusion elementwise | flops 131072 | bytes 786432 | tf_op jit(solution)/shard_map/convert_element_type | solution.py:623
  8.5 2.5 %collective-permute-start.2 = (bf16[256,512]{1,0:T(8,128)(2,1)S(1)}, bf16[256,512]{1,0:T(8,128)(2,1)S(1)}, u32[]{:S(2)}, u32[]{:S(2)}) collective-permute-start(bf16[256,512]{1,0:T(8,128)(2,1)S(1)} %convert_element_type.6.refs_3_), channel_id=1, source_target_pairs={{0,6},{1,7},{2,4},{3,5},{4,2},{5,3},{6,0},{7,1},{8,14},{9,15},{10,... | collective-permute-start | bytes 786440 | tf_op jit(solution)/shard_map/ppermute | solution.py:20
  12.0 5.8 %collective-permute-done.4.refs_2_.refs_6_ = bf16[256,512]{1,0:T(8,128)(2,1)S(1)} collective-permute-done((bf16[256,512]{1,0:T(8,128)(2,1)S(1)}, bf16[256,512]{1,0:T(8,128)(2,1)S(1)}, u32[]{:S(2)}, u32[]{:S(2)}) %collective-permute-start.4) | collective-permute-done | bytes 262176 | tf_op jit(solution)/shard_map/ppermute | solution.py:20
  18.0 0.7 collective-permute-done.2.refs_6_
  18.7 3.8 %collective-permute-done.1.refs_5_ = bf16[256,512]{1,0:T(8,128)(2,1)S(1)} collective-permute-done((bf16[256,512]{1,0:T(8,128)(2,1)S(1)}, bf16[256,512]{1,0:T(8,128)(2,1)S(1)}, u32[]{:S(2)}, u32[]{:S(2)}) %collective-permute-start.1) | collective-permute-done | bytes 262176 | tf_op jit(solution)/shard_map/ppermute | solution.py:20
  24.9 6.7 %stats.1 = (bf16[1024,512]{1,0:T(8,128)(2,1)S(1)}, bf16[1024,512]{1,0:T(8,128)(2,1)S(1)}, f32[4,8,256]{2,1,0:T(8,128)S(1)}, f32[3,4,256]{2,1,0:T(4,128)S(1)}, f3...) custom-call(f32[1,1]{1,0:T(1,128)S(6)} %mul.147.coef_ref, ...), custom_call_target="tpu_custom_call" | custom-call | flops 32212254720 | tf_op jit(solution)/shard_map/stats/pallas_call | solution.py:184
  31.6 1.0 %collective-permute-done.5.refs_0_ = bf16[256,512]{1,0:T(8,128)(2,1)S(1)} collective-permute-done((bf16[256,512]{1,0:T(8,128)(2,1)S(1)}, bf16[256,512]{1,0:T(8,128)(2,1)S(1)}, u32[]{:S(2)}, u32[]{:S(2)}) %collective-permute-start.5) | collective-permute-done | bytes 262176 | tf_op jit(solution)/shard_map/ppermute | solution.py:20
  32.6 3.0 %stats_last.1 = (bf16[256,512]{1,0:T(8,128)(2,1)S(1)}, f32[4,8,256]{2,1,0:T(8,128)S(1)}, f32[3,4,256]{2,1,0:T(4,128)S(1)}, f32[256,2048]{1,0:T(8,128)S(1)}, f32[...) custom-call(f32[1,1]{1,0:T(1,128)S(6)} %mul.147.coef_ref, ...), custom_call_target="tpu_custom_call" | custom-call | flops 10737418240 | tf_op jit(solution)/shard_map/stats_last/pallas_call | solution.py:184
  36.1 1.7 %collective-permute-start.12 = (f32[4,8,256]{2,1,0:T(8,128)S(1)}, f32[4,8,256]{2,1,0:T(8,128)S(1)}, u32[]{:S(2)}, u32[]{:S(2)}) collective-permute-start(f32[4,8,256]{2,1,0:T(8,128)S(1)} %get-tuple-element.58), channel_id=1, source_target_pairs={{0,6},{1,7},{2,4},{3,5},{4,2},{5,3},{6,0},{7,1},{8,14},{9,15},{10,... | collective-permute-start | bytes 98312 | tf_op jit(solution)/shard_map/ppermute | solution.py:20
  37.7 1.3 %collective-permute-start.11 = (f32[4,8,256]{2,1,0:T(8,128)S(1)}, f32[4,8,256]{2,1,0:T(8,128)S(1)}, u32[]{:S(2)}, u32[]{:S(2)}) collective-permute-start(f32[4,8,256]{2,1,0:T(8,128)S(1)} %get-tuple-element.58), channel_id=1, source_target_pairs={{0,4},{1,5},{2,6},{3,7},{4,0},{5,1},{6,2},{7,3},{8,12},{9,13},{10,... | collective-permute-start | bytes 98312 | tf_op jit(solution)/shard_map/ppermute | solution.py:20
  39.6 1.5 %collective-permute-done.12 = f32[4,8,256]{2,1,0:T(8,128)S(1)} collective-permute-done((f32[4,8,256]{2,1,0:T(8,128)S(1)}, f32[4,8,256]{2,1,0:T(8,128)S(1)}, u32[]{:S(2)}, u32[]{:S(2)}) %collective-permute-start.12) | collective-permute-done | bytes 32800 | tf_op jit(solution)/shard_map/ppermute | solution.py:20
  41.6 1.3 %collective-permute-done.10 = f32[4,8,256]{2,1,0:T(8,128)S(1)} collective-permute-done((f32[4,8,256]{2,1,0:T(8,128)S(1)}, f32[4,8,256]{2,1,0:T(8,128)S(1)}, u32[]{:S(2)}, u32[]{:S(2)}) %collective-permute-start.10) | collective-permute-done | bytes 32800 | tf_op jit(solution)/shard_map/ppermute | solution.py:20
  43.5 4.3 %collective-permute-done.14 = f32[3,4,256]{2,1,0:T(4,128)S(1)} collective-permute-done((f32[3,4,256]{2,1,0:T(4,128)S(1)}, f32[3,4,256]{2,1,0:T(4,128)S(1)}, u32[]{:S(2)}, u32[]{:S(2)}) %collective-permute-start.14) | collective-permute-done | bytes 12320 | tf_op jit(solution)/shard_map/ppermute | solution.py:20
  47.9 1.9 %text_grads_1.1 = (bf16[256,2048]{1,0:T(8,128)(2,1)S(1)}, bf16[272,512]{1,0:T(8,128)(2,1)S(1)}) custom-call(f32[1,1]{1,0:T(1,128)} %bitcast.277.scale_ref, f32[1,1]{1,0:T(1,128)S(6)} %mul.147.coef_ref, s32[1,2]{1,0:T(1,128)S(1)} %add_bitcast_fusion.place_ref, bf16[1024,512]{1,0:T(8,128)(2,1)S(1)} %get-tuple-element.53.refs_1_.refs_0_, ...), custom_call_target="tpu_custom_call" | custom-call | flops 21474836480 | tf_op jit(solution)/shard_map/text_grads_1/pallas_call | solution.py:563
  49.8 1.6 %collective-permute-start.16 = (bf16[272,512]{1,0:T(8,128)(2,1)S(1)}, bf16[272,512]{1,0:T(8,128)(2,1)S(1)}, u32[]{:S(2)}, u32[]{:S(2)}) collective-permute-start(bf16[272,512]{1,0:T(8,128)(2,1)S(1)} %get-tuple-element.77), channel_id=1, source_target_pairs={{0,8},{8,0},{16,24},{24,16},{1,9},{9,1},{17,25},{25,17},{2,10},{10... | collective-permute-start | bytes 835592 | tf_op jit(solution)/shard_map/ppermute | solution.py:20
  51.4 5.1 %text_grads_3.1 = (bf16[256,2048]{1,0:T(8,128)(2,1)S(1)}, bf16[256,2048]{1,0:T(8,128)(2,1)S(1)}, bf16[256,2048]{1,0:T(8,128)(2,1)S(1)}, f32[264,512]{1,0:T(8,128...) custom-call(f32[1,1]{1,0:T(1,128)} %bitcast.278.scale_ref, ...), custom_call_target="tpu_custom_call" | custom-call | flops 64424509440 | tf_op jit(solution)/shard_map/text_grads_3/pallas_call | solution.py:563
  56.6 0.7 pack_text.1.refs_8_
  57.3 1.5 %collective-permute-start.20 = (bf16[272,512]{1,0:T(8,128)(2,1)S(1)}, bf16[272,512]{1,0:T(8,128)(2,1)S(1)}, u32[]{:S(2)}, u32[]{:S(2)}) collective-permute-start(bf16[272,512]{1,0:T(8,128)(2,1)S(1)} %pack_text.1.refs_8_), channel_id=1, source_target_pairs={{0,16},{8,24},{16,0},{24,8},{1,17},{9,25},{17,1},{25,9},{2,18},{10... | collective-permute-start | bytes 835592 | tf_op jit(solution)/shard_map/ppermute | solution.py:20
  58.8 1.3 %image_grads.1.near = f32[4,264,512]{2,1,0:T(8,128)S(1)} custom-call(f32[1,1]{1,0:T(1,128)} %bitcast.279.scale_ref, f32[4,256]{1,0:T(4,128)S(1)} %fusion.34.refs_5_.extra, bf16[256,2048]{1,0:T(8,128)(2,1)S(1)} %get-tuple-element.73.refs_0_, bf16[256,2048]{1,0:T(8,128)(2,1)S(1)} %get-tuple-element.74.refs_1_, ...), custom_call_target="tpu_custom_call" | custom-call | flops 21474836480 | tf_op jit(solution)/shard_map/image_grads/pallas_call | solution.py:602
  60.2 0.6 collective-permute-done.17.far
  60.8 1.0 %collective-permute-start.19 = (bf16[272,512]{1,0:T(8,128)(2,1)S(1)}, bf16[272,512]{1,0:T(8,128)(2,1)S(1)}, u32[]{:S(2)}, u32[]{:S(2)}) collective-permute-start(bf16[272,512]{1,0:T(8,128)(2,1)S(1)} %get-tuple-element.84), channel_id=1, source_target_pairs={{0,8},{8,0},{16,24},{24,16},{1,9},{9,1},{17,25},{25,17},{2,10},{10... | collective-permute-start | bytes 835592 | tf_op jit(solution)/shard_map/ppermute | solution.py:20
  61.8 1.1 %pack_images.1 = (f32[264,512]{1,0:T(8,128)S(1)}, bf16[272,512]{1,0:T(8,128)(2,1)S(1)}, bf16[272,512]{1,0:T(8,128)(2,1)S(1)}, bf16[272,512]{1,0:T(8,128)(2,1)S(1)}) custom-call(f32[4,264,512]{2,1,0:T(8,128)S(1)} %image_grads.1.near, f32[4,264,512]{2,1,0:T(8,128)S(1)} %collective-permute-done.17.far), custom_call_target="tpu_custom_call" | custom-call | tf_op jit(solution)/shard_map/pack_images/pallas_call | solution.py:348
  62.9 0.6 collective-permute-start.18
  63.5 1.4 %collective-permute-start.21 = (bf16[272,512]{1,0:T(8,128)(2,1)S(1)}, bf16[272,512]{1,0:T(8,128)(2,1)S(1)}, u32[]{:S(2)}, u32[]{:S(2)}) collective-permute-start(bf16[272,512]{1,0:T(8,128)(2,1)S(1)} %get-tuple-element.87), channel_id=1, source_target_pairs={{0,4},{1,5},{2,6},{3,7},{4,0},{5,1},{6,2},{7,3},{8,12},{9,13},{10,... | collective-permute-start | bytes 835592 | tf_op jit(solution)/shard_map/ppermute | solution.py:20
  64.9 1.5 %collective-permute-start.22 = (bf16[272,512]{1,0:T(8,128)(2,1)S(1)}, bf16[272,512]{1,0:T(8,128)(2,1)S(1)}, u32[]{:S(2)}, u32[]{:S(2)}) collective-permute-start(bf16[272,512]{1,0:T(8,128)(2,1)S(1)} %get-tuple-element.88), channel_id=1, source_target_pairs={{0,6},{1,7},{2,4},{3,5},{4,2},{5,3},{6,0},{7,1},{8,14},{9,15},{10,... | collective-permute-start | bytes 835592 | tf_op jit(solution)/shard_map/ppermute | solution.py:20
  66.5 6.8 %collective-permute-done.20.refs_1_ = bf16[272,512]{1,0:T(8,128)(2,1)S(1)} collective-permute-done((bf16[272,512]{1,0:T(8,128)(2,1)S(1)}, bf16[272,512]{1,0:T(8,128)(2,1)S(1)}, u32[]{:S(2)}, u32[]{:S(2)}) %collective-permute-start.20) | collective-permute-done | bytes 278560 | tf_op jit(solution)/shard_map/ppermute | solution.py:20
  73.3 2.1 %collective-permute-done.19.refs_0_ = bf16[272,512]{1,0:T(8,128)(2,1)S(1)} collective-permute-done((bf16[272,512]{1,0:T(8,128)(2,1)S(1)}, bf16[272,512]{1,0:T(8,128)(2,1)S(1)}, u32[]{:S(2)}, u32[]{:S(2)}) %collective-permute-start.19) | collective-permute-done | bytes 278560 | tf_op jit(solution)/shard_map/ppermute | solution.py:20
  75.4 1.9 %grad_text.1 = (f32[256,512]{1,0:T(8,128)}, f32[8,256]{1,0:T(8,128)S(1)}, f32[1,1]{1,0:T(1,128)}) custom-call(f32[1,1]{1,0:T(1,128)S(6)} %mul.147.coef_ref, f32[264,512]{1,0:T(8,128)S(1)} %get-tuple-element.83.base, bf16[272,512]{1,0:T(8,128)(2,1)S(1)} %collective-permute-done.19.refs_0_, bf16[272,512]{1,0:T(8,128)(2,1)S(1)} %collective-permute-done.20.refs_1_), custom_call_target="tpu_custom_call" | custom-call | tf_op jit(solution)/shard_map/grad_text/pallas_call | solution.py:418
  77.6 1.9 %grad_image.1 = (f32[256,512]{1,0:T(8,128)}, f32[8,256]{1,0:T(8,128)}, f32[1,1]{1,0:T(1,128)}) custom-call(f32[1,1]{1,0:T(1,128)S(6)} %mul.147.coef_ref, f32[264,512]{1,0:T(8,128)S(1)} %added.1.base, bf16[272,512]{1,0:T(8,128)(2,1)S(1)} %collective-permute-done.21.refs_0_, bf16[272,512]{1,0:T(8,128)(2,1)S(1)} %collective-permute-done.22.refs_1_, ...), custom_call_target="tpu_custom_call" | custom-call | tf_op jit(solution)/shard_map/grad_image/pallas_call | solution.py:418
  (39 shorter events, 5.6 us)
Async XLA Ops:
  1.7 16.1 %collective-permute-start.4 = (bf16[256,512]{1,0:T(8,128)(2,1)S(1)}, bf16[256,512]{1,0:T(8,128)(2,1)S(1)}, u32[]{:S(2)}, u32[]{:S(2)}) collective-permute-start(bf16[256,512]{1,0:T(8,128)(2,1)S(1)} %convert_element_type.7.refs_0_.refs_8_.refs_4_), channel_id=1, source_target_pairs={{0,16},{8,24},{16,0},{24,8},{1,17},{9,25},{17,1},{25,9},{2,18},{10... | collective-permute-start | bytes 786440 | tf_op jit(solution)/shard_map/ppermute | solution.py:20
  5.8 12.2 %collective-permute-start.3 = (bf16[256,512]{1,0:T(8,128)(2,1)S(1)}, bf16[256,512]{1,0:T(8,128)(2,1)S(1)}, u32[]{:S(2)}, u32[]{:S(2)}) collective-permute-start(bf16[256,512]{1,0:T(8,128)(2,1)S(1)} %convert_element_type.7.refs_0_.refs_8_.refs_4_), channel_id=1, source_target_pairs={{0,8},{8,0},{16,24},{24,16},{1,9},{9,1},{17,25},{25,17},{2,10},{10... | collective-permute-start | bytes 786440 | tf_op jit(solution)/shard_map/ppermute | solution.py:20
  8.5 10.3 %collective-permute-start.2 = (bf16[256,512]{1,0:T(8,128)(2,1)S(1)}, bf16[256,512]{1,0:T(8,128)(2,1)S(1)}, u32[]{:S(2)}, u32[]{:S(2)}) collective-permute-start(bf16[256,512]{1,0:T(8,128)(2,1)S(1)} %convert_element_type.6.refs_3_), channel_id=1, source_target_pairs={{0,6},{1,7},{2,4},{3,5},{4,2},{5,3},{6,0},{7,1},{8,14},{9,15},{10,... | collective-permute-start | bytes 786440 | tf_op jit(solution)/shard_map/ppermute | solution.py:20
  11.0 11.6 %collective-permute-start.1 = (bf16[256,512]{1,0:T(8,128)(2,1)S(1)}, bf16[256,512]{1,0:T(8,128)(2,1)S(1)}, u32[]{:S(2)}, u32[]{:S(2)}) collective-permute-start(bf16[256,512]{1,0:T(8,128)(2,1)S(1)} %convert_element_type.6.refs_3_), channel_id=1, source_target_pairs={{0,4},{1,5},{2,6},{3,7},{4,0},{5,1},{6,2},{7,3},{8,12},{9,13},{10,... | collective-permute-start | bytes 786440 | tf_op jit(solution)/shard_map/ppermute | solution.py:20
  11.5 11.1 %collective-permute-start = (bf16[256,512]{1,0:T(8,128)(2,1)S(1)}, bf16[256,512]{1,0:T(8,128)(2,1)S(1)}, u32[]{:S(2)}, u32[]{:S(2)}) collective-permute-start(bf16[256,512]{1,0:T(8,128)(2,1)S(1)} %convert_element_type.6.refs_3_), channel_id=1, source_target_pairs={{0,2},{1,3},{2,0},{3,1},{4,6},{5,7},{6,4},{7,5},{8,10},{9,11},{10,... | collective-permute-start | bytes 786440 | tf_op jit(solution)/shard_map/ppermute | solution.py:20
  17.8 6.5 %collective-permute-start.6 = (bf16[256,512]{1,0:T(8,128)(2,1)S(1)}, bf16[256,512]{1,0:T(8,128)(2,1)S(1)}, u32[]{:S(2)}, u32[]{:S(2)}) collective-permute-start(bf16[256,512]{1,0:T(8,128)(2,1)S(1)} %convert_element_type.6.refs_3_), channel_id=1, source_target_pairs={{0,1},{1,0},{2,3},{3,2},{4,5},{5,4},{6,7},{7,6},{8,9},{9,8},{10,11... | collective-permute-start | bytes 786440 | tf_op jit(solution)/shard_map/ppermute | solution.py:20
  22.6 1.7 %collective-permute-start.7 = (bf16[256,512]{1,0:T(8,128)(2,1)S(1)}, bf16[256,512]{1,0:T(8,128)(2,1)S(1)}, u32[]{:S(2)}, u32[]{:S(2)}) collective-permute-start(bf16[256,512]{1,0:T(8,128)(2,1)S(1)} %collective-permute-done.refs_4_), channel_id=1, source_target_pairs={{0,1},{1,0},{2,3},{3,2},{4,5},{5,4},{6,7},{7,6},{8,9},{9,8},{10,11... | collective-permute-start | bytes 786440 | tf_op jit(solution)/shard_map/ppermute | solution.py:20
  22.6 1.9 %collective-permute-start.8 = (bf16[256,512]{1,0:T(8,128)(2,1)S(1)}, bf16[256,512]{1,0:T(8,128)(2,1)S(1)}, u32[]{:S(2)}, u32[]{:S(2)}) collective-permute-start(bf16[256,512]{1,0:T(8,128)(2,1)S(1)} %collective-permute-done.1.refs_5_), channel_id=1, source_target_pairs={{0,1},{1,0},{2,3},{3,2},{4,5},{5,4},{6,7},{7,6},{8,9},{9,8},{10,11... | collective-permute-start | bytes 786440 | tf_op jit(solution)/shard_map/ppermute | solution.py:20
  23.1 1.8 %collective-permute-start.9 = (bf16[256,512]{1,0:T(8,128)(2,1)S(1)}, bf16[256,512]{1,0:T(8,128)(2,1)S(1)}, u32[]{:S(2)}, u32[]{:S(2)}) collective-permute-start(bf16[256,512]{1,0:T(8,128)(2,1)S(1)} %collective-permute-done.2.refs_6_), channel_id=1, source_target_pairs={{0,1},{1,0},{2,3},{3,2},{4,5},{5,4},{6,7},{7,6},{8,9},{9,8},{10,11... | collective-permute-start | bytes 786440 | tf_op jit(solution)/shard_map/ppermute | solution.py:20
  23.9 8.7 %collective-permute-start.5 = (bf16[256,512]{1,0:T(8,128)(2,1)S(1)}, bf16[256,512]{1,0:T(8,128)(2,1)S(1)}, u32[]{:S(2)}, u32[]{:S(2)}) collective-permute-start(bf16[256,512]{1,0:T(8,128)(2,1)S(1)} %collective-permute-done.4.refs_2_.refs_6_), channel_id=1, source_target_pairs={{0,8},{8,0},{16,24},{24,16},{1,9},{9,1},{17,25},{25,17},{2,10},{10... | collective-permute-start | bytes 786440 | tf_op jit(solution)/shard_map/ppermute | solution.py:20
  35.6 4.0 %collective-permute-start.13 = (f32[9,4,256]{2,1,0:T(4,128)S(1)}, f32[9,4,256]{2,1,0:T(4,128)S(1)}, u32[]{:S(2)}, u32[]{:S(2)}) collective-permute-start(f32[9,4,256]{2,1,0:T(4,128)S(1)} %pad_maximum_fusion), channel_id=1, source_target_pairs={{0,8},{8,0},{16,24},{24,16},{1,9},{9,1},{17,25},{25,17},{2,10},{10... | collective-permute-start | bytes 110600 | tf_op jit(solution)/shard_map/ppermute | solution.py:20
  36.1 5.0 %collective-permute-start.12 = (f32[4,8,256]{2,1,0:T(8,128)S(1)}, f32[4,8,256]{2,1,0:T(8,128)S(1)}, u32[]{:S(2)}, u32[]{:S(2)}) collective-permute-start(f32[4,8,256]{2,1,0:T(8,128)S(1)} %get-tuple-element.58), channel_id=1, source_target_pairs={{0,6},{1,7},{2,4},{3,5},{4,2},{5,3},{6,0},{7,1},{8,14},{9,15},{10,... | collective-permute-start | bytes 98312 | tf_op jit(solution)/shard_map/ppermute | solution.py:20
  37.7 3.9 %collective-permute-start.11 = (f32[4,8,256]{2,1,0:T(8,128)S(1)}, f32[4,8,256]{2,1,0:T(8,128)S(1)}, u32[]{:S(2)}, u32[]{:S(2)}) collective-permute-start(f32[4,8,256]{2,1,0:T(8,128)S(1)} %get-tuple-element.58), channel_id=1, source_target_pairs={{0,4},{1,5},{2,6},{3,7},{4,0},{5,1},{6,2},{7,3},{8,12},{9,13},{10,... | collective-permute-start | bytes 98312 | tf_op jit(solution)/shard_map/ppermute | solution.py:20
  39.0 3.9 %collective-permute-start.10 = (f32[4,8,256]{2,1,0:T(8,128)S(1)}, f32[4,8,256]{2,1,0:T(8,128)S(1)}, u32[]{:S(2)}, u32[]{:S(2)}) collective-permute-start(f32[4,8,256]{2,1,0:T(8,128)S(1)} %get-tuple-element.58), channel_id=1, source_target_pairs={{0,2},{1,3},{2,0},{3,1},{4,6},{5,7},{6,4},{7,5},{8,10},{9,11},{10,... | collective-permute-start | bytes 98312 | tf_op jit(solution)/shard_map/ppermute | solution.py:20
  43.1 4.7 %collective-permute-start.14 = (f32[3,4,256]{2,1,0:T(4,128)S(1)}, f32[3,4,256]{2,1,0:T(4,128)S(1)}, u32[]{:S(2)}, u32[]{:S(2)}) collective-permute-start(f32[3,4,256]{2,1,0:T(4,128)S(1)} %pad_maximum_fusion.2), channel_id=1, source_target_pairs={{0,16},{8,24},{16,0},{24,8},{1,17},{9,25},{17,1},{25,9},{2,18},{10... | collective-permute-start | bytes 36872 | tf_op jit(solution)/shard_map/ppermute | solution.py:20
  43.5 4.3 %collective-permute-start.15 = (f32[4,8,256]{2,1,0:T(8,128)S(1)}, f32[4,8,256]{2,1,0:T(8,128)S(1)}, u32[]{:S(2)}, u32[]{:S(2)}) collective-permute-start(f32[4,8,256]{2,1,0:T(8,128)S(1)} %pad_maximum_fusion.1), channel_id=1, source_target_pairs={{0,1},{1,0},{2,3},{3,2},{4,5},{5,4},{6,7},{7,6},{8,9},{9,8},{10,11... | collective-permute-start | bytes 98312 | tf_op jit(solution)/shard_map/ppermute | solution.py:20
  49.8 6.8 %collective-permute-start.16 = (bf16[272,512]{1,0:T(8,128)(2,1)S(1)}, bf16[272,512]{1,0:T(8,128)(2,1)S(1)}, u32[]{:S(2)}, u32[]{:S(2)}) collective-permute-start(bf16[272,512]{1,0:T(8,128)(2,1)S(1)} %get-tuple-element.77), channel_id=1, source_target_pairs={{0,8},{8,0},{16,24},{24,16},{1,9},{9,1},{17,25},{25,17},{2,10},{10... | collective-permute-start | bytes 835592 | tf_op jit(solution)/shard_map/ppermute | solution.py:20
  56.5 4.3 %collective-permute-start.17 = (f32[4,264,512]{2,1,0:T(8,128)S(1)}, f32[4,264,512]{2,1,0:T(8,128)S(1)}, u32[]{:S(2)}, u32[]{:S(2)}) collective-permute-start(f32[4,264,512]{2,1,0:T(8,128)S(1)} %get-tuple-element.79), channel_id=1, source_target_pairs={{0,1},{1,0},{2,3},{3,2},{4,5},{5,4},{6,7},{7,6},{8,9},{9,8},{10,11... | collective-permute-start | bytes 6488072 | tf_op jit(solution)/shard_map/ppermute | solution.py:20
  57.3 16.0 %collective-permute-start.20 = (bf16[272,512]{1,0:T(8,128)(2,1)S(1)}, bf16[272,512]{1,0:T(8,128)(2,1)S(1)}, u32[]{:S(2)}, u32[]{:S(2)}) collective-permute-start(bf16[272,512]{1,0:T(8,128)(2,1)S(1)} %pack_text.1.refs_8_), channel_id=1, source_target_pairs={{0,16},{8,24},{16,0},{24,8},{1,17},{9,25},{17,1},{25,9},{2,18},{10... | collective-permute-start | bytes 835592 | tf_op jit(solution)/shard_map/ppermute | solution.py:20
  60.8 14.6 %collective-permute-start.19 = (bf16[272,512]{1,0:T(8,128)(2,1)S(1)}, bf16[272,512]{1,0:T(8,128)(2,1)S(1)}, u32[]{:S(2)}, u32[]{:S(2)}) collective-permute-start(bf16[272,512]{1,0:T(8,128)(2,1)S(1)} %get-tuple-element.84), channel_id=1, source_target_pairs={{0,8},{8,0},{16,24},{24,16},{1,9},{9,1},{17,25},{25,17},{2,10},{10... | collective-permute-start | bytes 835592 | tf_op jit(solution)/shard_map/ppermute | solution.py:20
  62.9 14.3 %collective-permute-start.18 = (bf16[272,512]{1,0:T(8,128)(2,1)S(1)}, bf16[272,512]{1,0:T(8,128)(2,1)S(1)}, u32[]{:S(2)}, u32[]{:S(2)}) collective-permute-start(bf16[272,512]{1,0:T(8,128)(2,1)S(1)} %get-tuple-element.82), channel_id=1, source_target_pairs={{0,2},{1,3},{2,0},{3,1},{4,6},{5,7},{6,4},{7,5},{8,10},{9,11},{10,... | collective-permute-start | bytes 835592 | tf_op jit(solution)/shard_map/ppermute | solution.py:20
  63.5 14.0 %collective-permute-start.21 = (bf16[272,512]{1,0:T(8,128)(2,1)S(1)}, bf16[272,512]{1,0:T(8,128)(2,1)S(1)}, u32[]{:S(2)}, u32[]{:S(2)}) collective-permute-start(bf16[272,512]{1,0:T(8,128)(2,1)S(1)} %get-tuple-element.87), channel_id=1, source_target_pairs={{0,4},{1,5},{2,6},{3,7},{4,0},{5,1},{6,2},{7,3},{8,12},{9,13},{10,... | collective-permute-start | bytes 835592 | tf_op jit(solution)/shard_map/ppermute | solution.py:20
  64.9 12.6 %collective-permute-start.22 = (bf16[272,512]{1,0:T(8,128)(2,1)S(1)}, bf16[272,512]{1,0:T(8,128)(2,1)S(1)}, u32[]{:S(2)}, u32[]{:S(2)}) collective-permute-start(bf16[272,512]{1,0:T(8,128)(2,1)S(1)} %get-tuple-element.88), channel_id=1, source_target_pairs={{0,6},{1,7},{2,4},{3,5},{4,2},{5,3},{6,0},{7,1},{8,14},{9,15},{10,... | collective-permute-start | bytes 835592 | tf_op jit(solution)/shard_map/ppermute | solution.py:20

commit v13 on v11

--- a/solution.py
+++ b/solution.py
@@ -213,14 +213,18 @@
 
 
 def exchanged(row_parts, col_parts, n_col, n_row):
-    rows = [swap(row_parts, "col", n_col, q) for q in range(2, n_col, 2)]
-    cols = swap(col_parts, "row", n_row, 1)
-    rows, cols = lax.optimization_barrier((rows, cols))
-    rows = by_pairs([list(x) for x in (row_parts, *rows)], merged)
-    cols = merged(list(col_parts), list(cols))
-    for b in range(1, n_row.bit_length() - 1):
-        cols = merged(cols, list(swap(jnp.stack(cols), "row", n_row, 1 << b)))
-    rows = merged(rows, list(swap(jnp.stack(rows), "col", n_col, 1)))
+    rows, cols = list(row_parts), list(col_parts)
+    count = len(cols)
+    fill = row_parts.size // col_parts.size + 1
+    row_bits = [1 << b for b in range(1, n_col.bit_length() - 1)] + [1]
+    col_bits = [1 << b for b in range(n_row.bit_length() - 1)]
+    for n, bit in enumerate(row_bits):
+        received = swap(jnp.stack(rows), "col", n_col, bit)
+        if n < len(col_bits):
+            other = swap(jnp.stack(cols * fill), "row", n_row, col_bits[n])
+            received, other = lax.optimization_barrier((received, other))
+            cols = merged(cols, list(other[:count]))
+        rows = merged(rows, list(received))
     return *lse_and_mean(rows), *lse_and_mean(cols)
 
 
@@ -429,7 +433,7 @@
     )(coef, base, *codes, *before)
 
 
-def text_block(text, tile, t, halves, row_lse, col_lse, place_ref, scale_ref, coef_ref, extra, grad_ref, out_ref, total, powers):
+def text_block(text, tile, t, halves, row_lse, col_lse, place_ref, coef_ref, grad_ref):
     coef = coef_ref[0, 0]
     r_place, c_place = place_ref[0, 0], place_ref[0, 1]
     half, width = halves[0].shape
@@ -468,15 +472,6 @@
             return carry
 
         lax.fori_loop(0, half // block, one, 0, unroll=4)
-    total[:size, :] = scale_ref[0, 0] * (
-        jnp.dot(grad_ref[:, :half], halves[0][...], preferred_element_type=jnp.float32)
-        + jnp.dot(grad_ref[:, half:], halves[1][...], preferred_element_type=jnp.float32)
-    )
-    put_extra(total.at[size:, :], extra)
-    if t & 1:
-        encode(out_ref, powers, size, lambda r: total[r : r + STEP, :], total[size:, :])
-    else:
-        out_ref[...] = total[...]
 
 
 def image_block(grads, texts, at, block, scale):
@@ -499,24 +494,47 @@
     if kept:
         tile, rest = rest[0], rest[1:]
     done_grads, done_texts, rest = rest[:n_done], rest[n_done : 2 * n_done], rest[2 * n_done :]
-    grads, outs = rest[:n], rest[n : 2 * n]
+    grads, outs, rest = rest[0], rest[1 : 1 + n], rest[1 + n :]
+    total, powers = rest[-2:]
+    lowest = min(order)
     for i, t in enumerate(order):
         text_block(
             texts[i],
-            tile.at[pl.ds((t - min(order)) * block, block)] if kept else None,
-            t, (even, odd), row_lse, col_lse, place_ref, scale_ref, coef_ref, row_extra, grads[i], outs[i], *rest[-2:]
+            tile.at[pl.ds((t - lowest) * block, block)] if kept else None,
+            t,
+            (even, odd),
+            row_lse,
+            col_lse,
+            place_ref,
+            coef_ref,
+            grads.at[pl.ds((t - lowest) * block, block)],
         )
+    half = even.shape[0]
+    scale = scale_ref[0, 0]
+    total[...] = scale * (
+        jnp.dot(grads[:, :half], even[...], preferred_element_type=jnp.float32)
+        + jnp.dot(grads[:, half:], odd[...], preferred_element_type=jnp.float32)
+    )
+    for i, t in enumerate(order):
+        at = (t - lowest) * block
+        if t & 1:
+            extra_rows = rest[-3]
+            put_extra(extra_rows, row_extra)
+            encode(outs[i], powers, block, lambda r, at=at: total[at + r : at + r + STEP, :], extra_rows[...])
+        else:
+            outs[i][:block, :] = total[at : at + block, :]
+            put_extra(outs[i].at[block:, :], row_extra)
     if n_done:
-        far_ref = rest[2 * n]
-        half = even.shape[0]
+        far_ref = rest[0]
+        by_text = {t: (grads.at[pl.ds((t - lowest) * block, block)], texts[i]) for i, t in enumerate(order)}
 
         def one(j, carry):
             far_ref[j, :block, :] = image_block(
-                [*done_grads, *grads],
-                [*done_texts, *texts],
+                [*done_grads, *[by_text[t][0] for t in order]],
+                [*done_texts, *[by_text[t][1] for t in order]],
                 pl.multiple_of(j * block + half, block),
                 block,
-                scale_ref[0, 0],
+                scale,
             )
             put_extra(far_ref.at[j, block:, :], col_extra)
             return carry
@@ -531,7 +549,7 @@
     vmem = pl.BlockSpec(memory_space=VMEM)
     smem = pl.BlockSpec(memory_space=SMEM)
     out_shape = (
-        [jax.ShapeDtypeStruct((block, 2 * half), jnp.bfloat16)] * n
+        [jax.ShapeDtypeStruct((n * block, 2 * half), jnp.bfloat16)]
         + [
             jax.ShapeDtypeStruct((block + MORE, width), jnp.bfloat16)
             if t & 1
@@ -543,29 +561,30 @@
         out_shape.append(jax.ShapeDtypeStruct((half // block, block + EXTRA, width), jnp.float32))
     operands = [even, odd, row_lse, col_lse, row_extra, col_extra, *[texts[t] for t in order]]
     operands += tile
-    operands += [done[t] for t in done] + [texts[t] for t in done]
+    operands += [grad for _, grad in done] + [texts[t] for t, _ in done]
     outs = pl.pallas_call(
         functools.partial(text_kernel, tuple(order), len(done), len(tile), block),
         out_shape=tuple(out_shape),
         in_specs=[smem] * 3 + [vmem] * len(operands),
         out_specs=(vmem,) * len(out_shape),
         scratch_shapes=[
-            VMEM((block + EXTRA, width), jnp.float32),
+            VMEM((EXTRA, width), jnp.float32),
+            VMEM((n * block, width), jnp.float32),
             VMEM((block, LANES), jnp.float32),
         ],
-        compiler_params=pltpu.CompilerParams(vmem_limit_bytes=12 * 2**20),
+        compiler_params=pltpu.CompilerParams(vmem_limit_bytes=(10 + 2 * n) * 2**20),
         cost_estimate=pl.CostEstimate(
             flops=FLOPS * 4 * n * block * 2 * half * width, bytes_accessed=0, transcendentals=0
         ),
         name=f"text_grads_{n}",
     )(scale, coef, place, *operands)
-    grads = {t: outs[i] for i, t in enumerate(order)}
-    parts = {t: outs[n + i] for i, t in enumerate(order)}
-    return grads, parts, outs[-1]
-
-
-def image_kernel(n_text, block, scale_ref, extra, *refs):
-    grads, texts, out_ref = refs[:n_text], refs[n_text : 2 * n_text], refs[-1]
+    parts = {t: outs[1 + i] for i, t in enumerate(order)}
+    return outs[0], parts, outs[-1]
+
+
+def image_kernel(n_text, block, scale_ref, extra, near_grads, last_grad, *refs):
+    texts, out_ref = refs[:n_text], refs[-1]
+    grads = [near_grads.at[pl.ds(t * block, block)] for t in range(n_text - 1)] + [last_grad]
 
     def one(j, carry):
         put_extra(out_ref.at[j, block:, :], extra)
@@ -578,7 +597,7 @@
 
 
 def image_grads(scale, extra, grads, texts, after):
-    n_text = len(grads)
+    n_text = len(texts)
     rows = grads[0].shape[1]
     block, width = texts[0].shape
     n = rows // block // 2
@@ -587,7 +606,7 @@
         functools.partial(image_kernel, n_text, block),
         out_shape=jax.ShapeDtypeStruct((n, block + EXTRA, width), jnp.float32),
         in_specs=[pl.BlockSpec(memory_space=SMEM)]
-        + [vmem] * (2 * n_text + 1)
+        + [vmem] * (n_text + 3)
         + [pl.BlockSpec(memory_space=pl.ANY)] * len(after),
         out_specs=vmem,
         compiler_params=pltpu.CompilerParams(vmem_limit_bytes=12 * 2**20),
@@ -619,15 +638,14 @@
 
     held = (scale, coef, place, even, odd, row_lse, col_lse, row_extra, col_extra, texts)
     last = n_row - 1
-    grads, parts, _ = text_grads(*held, tile_last, [last], {})
+    last_grad, parts, _ = text_grads(*held, tile_last, [last], [])
     received = swap(parts[last], "row", n_row, 1)
-    more, more_parts, far = text_grads(*held, tile, list(range(last))[::-1], grads)
-    grads |= more
+    near_grads, more_parts, far = text_grads(*held, tile, list(range(last))[::-1], [(last, last_grad)])
     parts |= more_parts
     codes = {q: [] for q in range(0, n_row, 2)}
     codes[last ^ 1].append(received)
     after = [pack_text(parts[last ^ 1], codes[last ^ 1])] if n_row > 2 else [received]
-    near = image_grads(scale, col_extra, [grads[t] for t in range(n_row)], texts, after)
+    near = image_grads(scale, col_extra, [near_grads, last_grad], texts, after)
     far = swap(far, "col", n_col, 1)
     odd_parts, far = lax.optimization_barrier(([parts[q] for q in range(1, last, 2)], far))
     for q, part in zip(range(1, last, 2), odd_parts):

time: 79.7 us -> 80.4 us (level)
  starting transfers between devices: 21.4 us -> 23.1 us
    ppermute x23 -> x22, starting transfers between devices: 21.4 us -> 23.1 us  [swap(): return lax.ppermute(x, axis, [(i, i ^ q) for i in range(n)])]
    ppermute x23 -> x22, waiting for transfers between devices: 32.1 us -> 31.4 us  [swap(): return lax.ppermute(x, axis, [(i, i ^ q) for i in range(n)])]
  transfers between devices with their start and end apart: 23 -> 22, of which waited for: 14 -> 16; matrix products, arithmetic and copies ran while one was open for 2% -> 1% of each run, Pallas kernels for 20% -> 19%
where the time goes in v13:
time: 80.4 us; the launch traced here: 80.2 us
  waiting for transfers between devices  31.4 us (39%)
  starting transfers between devices  23.1 us (29%)
  Pallas kernels  21.5 us (27%)
  other arithmetic  2.44 us (3%)
  between operations  1.61 us (2%)
    ppermute x22, waiting for transfers between devices, swap(): return lax.ppermute(x, axis, [(i, i ^ q) for i in range(n)])  31.4 us
    ppermute x22, starting transfers between devices, swap(): return lax.ppermute(x, axis, [(i, i ^ q) for i in range(n)])  23.1 us
    pallas_call x2, Pallas kernels, stats(): pl.pallas_call(functools.partial(stats_kernel, first, len(texts), block),...  7.98 us
    pallas_call x2, Pallas kernels, text_grads(): pl.pallas_call(functools.partial(text_kernel, tuple(order), len(done), le...  6.3 us
    pallas_call x2, Pallas kernels, total_of(): pl.pallas_call(functools.partial(total_kernel, len(codes), in_order), out...  3.78 us
  transfers between devices with their start and end apart: 22, of which 16 were waited for; matrix products, arithmetic and copies ran while one was open for 1% of the time, Pallas kernels for 19%

profile of v13, /device:TPU:0, one launch (start us, length us, event | category | flops | bytes accessed | tf_op | source)
XLA Modules:
  0.0 80.2 jit_solution(4254578786039367383)
XLA Ops:
  0.6 1.1 %convert_element_type.7.refs_0_.refs_8_ = bf16[256,512]{1,0:T(8,128)(2,1)S(1)} convert(f32[256,512]{1,0:T(8,128)} %param.4) | non-fusion elementwise | flops 131072 | bytes 786432 | tf_op jit(solution)/shard_map/convert_element_type | solution.py:626
  1.7 4.1 %collective-permute-start.4 = (bf16[256,512]{1,0:T(8,128)(2,1)S(1)}, bf16[256,512]{1,0:T(8,128)(2,1)S(1)}, u32[]{:S(2)}, u32[]{:S(2)}) collective-permute-start(bf16[256,512]{1,0:T(8,128)(2,1)S(1)} %convert_element_type.7.refs_0_.refs_8_), channel_id=1, source_target_pairs={{0,16},{8,24},{16,0},{24,8},{1,17},{9,25},{17,1},{25,9},{2,18},{10... | collective-permute-start | bytes 786440 | tf_op jit(solution)/shard_map/ppermute | solution.py:20
  5.8 1.6 %collective-permute-start.3 = (bf16[256,512]{1,0:T(8,128)(2,1)S(1)}, bf16[256,512]{1,0:T(8,128)(2,1)S(1)}, u32[]{:S(2)}, u32[]{:S(2)}) collective-permute-start(bf16[256,512]{1,0:T(8,128)(2,1)S(1)} %convert_element_type.7.refs_0_.refs_8_), channel_id=1, source_target_pairs={{0,8},{8,0},{16,24},{24,16},{1,9},{9,1},{17,25},{25,17},{2,10},{10... | collective-permute-start | bytes 786440 | tf_op jit(solution)/shard_map/ppermute | solution.py:20
  7.4 1.1 %convert_element_type.6.refs_3_ = bf16[256,512]{1,0:T(8,128)(2,1)S(1)} convert(f32[256,512]{1,0:T(8,128)} %param.3) | non-fusion elementwise | flops 131072 | bytes 786432 | tf_op jit(solution)/shard_map/convert_element_type | solution.py:626
  8.5 2.5 %collective-permute-start.2 = (bf16[256,512]{1,0:T(8,128)(2,1)S(1)}, bf16[256,512]{1,0:T(8,128)(2,1)S(1)}, u32[]{:S(2)}, u32[]{:S(2)}) collective-permute-start(bf16[256,512]{1,0:T(8,128)(2,1)S(1)} %convert_element_type.6.refs_3_), channel_id=1, source_target_pairs={{0,6},{1,7},{2,4},{3,5},{4,2},{5,3},{6,0},{7,1},{8,14},{9,15},{10,... | collective-permute-start | bytes 786440 | tf_op jit(solution)/shard_map/ppermute | solution.py:20
  12.0 5.8 %collective-permute-done.4.refs_2_.refs_6_ = bf16[256,512]{1,0:T(8,128)(2,1)S(1)} collective-permute-done((bf16[256,512]{1,0:T(8,128)(2,1)S(1)}, bf16[256,512]{1,0:T(8,128)(2,1)S(1)}, u32[]{:S(2)}, u32[]{:S(2)}) %collective-permute-start.4) | collective-permute-done | bytes 262176 | tf_op jit(solution)/shard_map/ppermute | solution.py:20
  18.7 3.8 %collective-permute-done.1.refs_5_ = bf16[256,512]{1,0:T(8,128)(2,1)S(1)} collective-permute-done((bf16[256,512]{1,0:T(8,128)(2,1)S(1)}, bf16[256,512]{1,0:T(8,128)(2,1)S(1)}, u32[]{:S(2)}, u32[]{:S(2)}) %collective-permute-start.1) | collective-permute-done | bytes 262176 | tf_op jit(solution)/shard_map/ppermute | solution.py:20
  24.9 5.4 %stats.1 = (bf16[1024,512]{1,0:T(8,128)(2,1)S(1)}, bf16[1024,512]{1,0:T(8,128)(2,1)S(1)}, f32[4,8,256]{2,1,0:T(8,128)S(1)}, f32[3,4,256]{2,1,0:T(4,128)S(1)}, f32[768,2048]{1,0:T(8,128)S(1)}) custom-call(f32[1,1]{1,0:T(1,128)S(6)} %mul.127.coef_ref, s32[1,2]{1,0:T(1,128)S(1)} %add_bitcast_fusion.place_ref, ...), custom_call_target="tpu_custom_call" | custom-call | flops 32212254720 | tf_op jit(solution)/shard_map/stats/pallas_call | solution.py:181
  30.3 2.3 %collective-permute-done.5.refs_0_ = bf16[256,512]{1,0:T(8,128)(2,1)S(1)} collective-permute-done((bf16[256,512]{1,0:T(8,128)(2,1)S(1)}, bf16[256,512]{1,0:T(8,128)(2,1)S(1)}, u32[]{:S(2)}, u32[]{:S(2)}) %collective-permute-start.5) | collective-permute-done | bytes 262176 | tf_op jit(solution)/shard_map/ppermute | solution.py:20
  32.6 2.6 %stats_last.1 = (bf16[256,512]{1,0:T(8,128)(2,1)S(1)}, f32[4,8,256]{2,1,0:T(8,128)S(1)}, f32[3,4,256]{2,1,0:T(4,128)S(1)}, f32[256,2048]{1,0:T(8,128)S(1)}) custom-call(f32[1,1]{1,0:T(1,128)S(6)} %mul.127.coef_ref, s32[1,2]{1,0:T(1,128)S(1)} %add_bitcast_fusion.place_ref, bf16[256,512]{1,0:T(8,128)(2,1)S(1)} %collective-permute-done.5.refs_0_, ...), custom_call_target="tpu_custom_call" | custom-call | flops 10737418240 | tf_op jit(solution)/shard_map/stats_last/pallas_call | solution.py:181
  35.7 1.5 %collective-permute-start.10 = (f32[4,8,256]{2,1,0:T(8,128)S(1)}, f32[4,8,256]{2,1,0:T(8,128)S(1)}, u32[]{:S(2)}, u32[]{:S(2)}) collective-permute-start(f32[4,8,256]{2,1,0:T(8,128)S(1)} %get-tuple-element.50), channel_id=1, source_target_pairs={{0,2},{1,3},{2,0},{3,1},{4,6},{5,7},{6,4},{7,5},{8,10},{9,11},{10,... | collective-permute-start | bytes 98312 | tf_op jit(solution)/shard_map/ppermute | solution.py:20
  37.2 2.4 %collective-permute-done.10 = f32[4,8,256]{2,1,0:T(8,128)S(1)} collective-permute-done((f32[4,8,256]{2,1,0:T(8,128)S(1)}, f32[4,8,256]{2,1,0:T(8,128)S(1)}, u32[]{:S(2)}, u32[]{:S(2)}) %collective-permute-start.10) | collective-permute-done | bytes 32800 | tf_op jit(solution)/shard_map/ppermute | solution.py:20
  40.2 1.4 %collective-permute-start.12 = (f32[4,8,256]{2,1,0:T(8,128)S(1)}, f32[4,8,256]{2,1,0:T(8,128)S(1)}, u32[]{:S(2)}, u32[]{:S(2)}) collective-permute-start(f32[4,8,256]{2,1,0:T(8,128)S(1)} %pad_maximum_fusion.1), channel_id=1, source_target_pairs={{0,4},{1,5},{2,6},{3,7},{4,0},{5,1},{6,2},{7,3},{8,12},{9,13},{10,... | collective-permute-start | bytes 98312 | tf_op jit(solution)/shard_map/ppermute | solution.py:20
  41.6 2.5 %collective-permute-done.12 = f32[4,8,256]{2,1,0:T(8,128)S(1)} collective-permute-done((f32[4,8,256]{2,1,0:T(8,128)S(1)}, f32[4,8,256]{2,1,0:T(8,128)S(1)}, u32[]{:S(2)}, u32[]{:S(2)}) %collective-permute-start.12) | collective-permute-done | bytes 32800 | tf_op jit(solution)/shard_map/ppermute | solution.py:20
  44.8 1.2 %collective-permute-done.14 = f32[4,8,256]{2,1,0:T(8,128)S(1)} collective-permute-done((f32[4,8,256]{2,1,0:T(8,128)S(1)}, f32[4,8,256]{2,1,0:T(8,128)S(1)}, u32[]{:S(2)}, u32[]{:S(2)}) %collective-permute-start.14) | collective-permute-done | bytes 32800 | tf_op jit(solution)/shard_map/ppermute | solution.py:20
  46.1 1.8 %text_grads_1.1 = (bf16[256,2048]{1,0:T(8,128)(2,1)S(1)}, bf16[272,512]{1,0:T(8,128)(2,1)S(1)}) custom-call(f32[1,1]{1,0:T(1,128)} %bitcast.241.scale_ref, f32[1,1]{1,0:T(1,128)S(6)} %mul.127.coef_ref, s32[1,2]{1,0:T(1,128)S(1)} %add_bitcast_fusion.place_ref, bf16[1024,512]{1,0:T(8,128)(2,1)S(1)} %get-tuple-element.45.refs_1_.refs_0_, ...), custom_call_target="tpu_custom_call" | custom-call | flops 21474836480 | tf_op jit(solution)/shard_map/text_grads_1/pallas_call | solution.py:565
  47.9 1.7 %collective-permute-start.15 = (bf16[272,512]{1,0:T(8,128)(2,1)S(1)}, bf16[272,512]{1,0:T(8,128)(2,1)S(1)}, u32[]{:S(2)}, u32[]{:S(2)}) collective-permute-start(bf16[272,512]{1,0:T(8,128)(2,1)S(1)} %get-tuple-element.61), channel_id=1, source_target_pairs={{0,8},{8,0},{16,24},{24,16},{1,9},{9,1},{17,25},{25,17},{2,10},{10... | collective-permute-start | bytes 835592 | tf_op jit(solution)/shard_map/ppermute | solution.py:20
  49.5 4.5 %text_grads_3.1 = (bf16[768,2048]{1,0:T(8,128)(2,1)S(1)}, f32[264,512]{1,0:T(8,128)S(1)}, bf16[272,512]{1,0:T(8,128)(2,1)S(1)}, f32[264,512]{1,0:T(8,128)S(1)}, f32[4,264,512]{2,1,0:T(8,128)S(1)}) custom-call(f32[1,1]{1,0:T(1,128)} %bitcast.242.scale_ref, f32[1,1]{1,0:T(1,128)S(6)} %mul.127.coef_ref, s32[1,2]{1,0:T(1,128)S(1)} %add_bitcast_fusion.place_ref, ...), custom_call_target="tpu_custom_call" | custom-call | flops 64424509440 | tf_op jit(solution)/shard_map/text_grads_3/pallas_call | solution.py:565
  54.1 2.5 %collective-permute-done.15.refs_0_ = bf16[272,512]{1,0:T(8,128)(2,1)S(1)} collective-permute-done((bf16[272,512]{1,0:T(8,128)(2,1)S(1)}, bf16[272,512]{1,0:T(8,128)(2,1)S(1)}, u32[]{:S(2)}, u32[]{:S(2)}) %collective-permute-start.15) | collective-permute-done | bytes 278560 | tf_op jit(solution)/shard_map/ppermute | solution.py:20
  56.6 0.7 pack_text.1.refs_4_
  57.3 2.0 %collective-permute-start.19 = (bf16[272,512]{1,0:T(8,128)(2,1)S(1)}, bf16[272,512]{1,0:T(8,128)(2,1)S(1)}, u32[]{:S(2)}, u32[]{:S(2)}) collective-permute-start(bf16[272,512]{1,0:T(8,128)(2,1)S(1)} %pack_text.1.refs_4_), channel_id=1, source_target_pairs={{0,16},{8,24},{16,0},{24,8},{1,17},{9,25},{17,1},{25,9},{2,18},{10... | collective-permute-start | bytes 835592 | tf_op jit(solution)/shard_map/ppermute | solution.py:20
  59.4 1.3 %image_grads.1.near = f32[4,264,512]{2,1,0:T(8,128)S(1)} custom-call(f32[1,1]{1,0:T(1,128)} %bitcast.243.scale_ref, f32[4,256]{1,0:T(4,128)S(1)} %fusion.28.refs_5_.extra, bf16[768,2048]{1,0:T(8,128)(2,1)S(1)} %get-tuple-element.59.near_grads, bf16[256,2048]{1,0:T(8,128)(2,1)S(1)} %get-tuple-element.58.refs_10_.last_grad, ...), custom_call_target="tpu_custom_call" | custom-call | flops 21474836480 | tf_op jit(solution)/shard_map/image_grads/pallas_call | solution.py:605
  60.7 1.7 %collective-permute-start.18 = (bf16[272,512]{1,0:T(8,128)(2,1)S(1)}, bf16[272,512]{1,0:T(8,128)(2,1)S(1)}, u32[]{:S(2)}, u32[]{:S(2)}) collective-permute-start(bf16[272,512]{1,0:T(8,128)(2,1)S(1)} %get-tuple-element.68), channel_id=1, source_target_pairs={{0,8},{8,0},{16,24},{24,16},{1,9},{9,1},{17,25},{25,17},{2,10},{10... | collective-permute-start | bytes 835592 | tf_op jit(solution)/shard_map/ppermute | solution.py:20
  62.4 1.1 %pack_images.1 = (f32[264,512]{1,0:T(8,128)S(1)}, bf16[272,512]{1,0:T(8,128)(2,1)S(1)}, bf16[272,512]{1,0:T(8,128)(2,1)S(1)}, bf16[272,512]{1,0:T(8,128)(2,1)S(1)}) custom-call(f32[4,264,512]{2,1,0:T(8,128)S(1)} %image_grads.1.near, f32[4,264,512]{2,1,0:T(8,128)S(1)} %collective-permute-done.16.far), custom_call_target="tpu_custom_call" | custom-call | tf_op jit(solution)/shard_map/pack_images/pallas_call | solution.py:347
  63.5 1.5 %collective-permute-start.17 = (bf16[272,512]{1,0:T(8,128)(2,1)S(1)}, bf16[272,512]{1,0:T(8,128)(2,1)S(1)}, u32[]{:S(2)}, u32[]{:S(2)}) collective-permute-start(bf16[272,512]{1,0:T(8,128)(2,1)S(1)} %get-tuple-element.66), channel_id=1, source_target_pairs={{0,2},{1,3},{2,0},{3,1},{4,6},{5,7},{6,4},{7,5},{8,10},{9,11},{10,... | collective-permute-start | bytes 835592 | tf_op jit(solution)/shard_map/ppermute | solution.py:20
  65.0 0.7 collective-permute-start.20
  65.8 1.3 %collective-permute-start.21 = (bf16[272,512]{1,0:T(8,128)(2,1)S(1)}, bf16[272,512]{1,0:T(8,128)(2,1)S(1)}, u32[]{:S(2)}, u32[]{:S(2)}) collective-permute-start(bf16[272,512]{1,0:T(8,128)(2,1)S(1)} %get-tuple-element.72), channel_id=1, source_target_pairs={{0,6},{1,7},{2,4},{3,5},{4,2},{5,3},{6,0},{7,1},{8,14},{9,15},{10,... | collective-permute-start | bytes 835592 | tf_op jit(solution)/shard_map/ppermute | solution.py:20
  67.1 5.2 %collective-permute-done.19.refs_1_ = bf16[272,512]{1,0:T(8,128)(2,1)S(1)} collective-permute-done((bf16[272,512]{1,0:T(8,128)(2,1)S(1)}, bf16[272,512]{1,0:T(8,128)(2,1)S(1)}, u32[]{:S(2)}, u32[]{:S(2)}) %collective-permute-start.19) | collective-permute-done | bytes 278560 | tf_op jit(solution)/shard_map/ppermute | solution.py:20
  72.3 0.9 %collective-permute-done.18.refs_0_ = bf16[272,512]{1,0:T(8,128)(2,1)S(1)} collective-permute-done((bf16[272,512]{1,0:T(8,128)(2,1)S(1)}, bf16[272,512]{1,0:T(8,128)(2,1)S(1)}, u32[]{:S(2)}, u32[]{:S(2)}) %collective-permute-start.18) | collective-permute-done | bytes 278560 | tf_op jit(solution)/shard_map/ppermute | solution.py:20
  73.2 1.8 %grad_text.1 = (f32[256,512]{1,0:T(8,128)}, f32[8,256]{1,0:T(8,128)S(1)}, f32[1,1]{1,0:T(1,128)}) custom-call(f32[1,1]{1,0:T(1,128)S(6)} %mul.127.coef_ref, f32[264,512]{1,0:T(8,128)S(1)} %get-tuple-element.67.base, bf16[272,512]{1,0:T(8,128)(2,1)S(1)} %collective-permute-done.18.refs_0_, bf16[272,512]{1,0:T(8,128)(2,1)S(1)} %collective-permute-done.19.refs_1_), custom_call_target="tpu_custom_call" | custom-call | tf_op jit(solution)/shard_map/grad_text/pallas_call | solution.py:417
  75.4 2.7 %collective-permute-done.20.refs_0_ = bf16[272,512]{1,0:T(8,128)(2,1)S(1)} collective-permute-done((bf16[272,512]{1,0:T(8,128)(2,1)S(1)}, bf16[272,512]{1,0:T(8,128)(2,1)S(1)}, u32[]{:S(2)}, u32[]{:S(2)}) %collective-permute-start.20) | collective-permute-done | bytes 278560 | tf_op jit(solution)/shard_map/ppermute | solution.py:20
  78.1 1.9 %grad_image.1 = (f32[256,512]{1,0:T(8,128)}, f32[8,256]{1,0:T(8,128)}, f32[1,1]{1,0:T(1,128)}) custom-call(f32[1,1]{1,0:T(1,128)S(6)} %mul.127.coef_ref, f32[264,512]{1,0:T(8,128)S(1)} %added.1.base, bf16[272,512]{1,0:T(8,128)(2,1)S(1)} %collective-permute-done.20.refs_0_, bf16[272,512]{1,0:T(8,128)(2,1)S(1)} %collective-permute-done.21.refs_1_, ...), custom_call_target="tpu_custom_call" | custom-call | tf_op jit(solution)/shard_map/grad_image/pallas_call | solution.py:417
  (44 shorter events, 5.9 us)
Async XLA Ops:
  1.7 16.1 %collective-permute-start.4 = (bf16[256,512]{1,0:T(8,128)(2,1)S(1)}, bf16[256,512]{1,0:T(8,128)(2,1)S(1)}, u32[]{:S(2)}, u32[]{:S(2)}) collective-permute-start(bf16[256,512]{1,0:T(8,128)(2,1)S(1)} %convert_element_type.7.refs_0_.refs_8_), channel_id=1, source_target_pairs={{0,16},{8,24},{16,0},{24,8},{1,17},{9,25},{17,1},{25,9},{2,18},{10... | collective-permute-start | bytes 786440 | tf_op jit(solution)/shard_map/ppermute | solution.py:20
  5.8 12.2 %collective-permute-start.3 = (bf16[256,512]{1,0:T(8,128)(2,1)S(1)}, bf16[256,512]{1,0:T(8,128)(2,1)S(1)}, u32[]{:S(2)}, u32[]{:S(2)}) collective-permute-start(bf16[256,512]{1,0:T(8,128)(2,1)S(1)} %convert_element_type.7.refs_0_.refs_8_), channel_id=1, source_target_pairs={{0,8},{8,0},{16,24},{24,16},{1,9},{9,1},{17,25},{25,17},{2,10},{10... | collective-permute-start | bytes 786440 | tf_op jit(solution)/shard_map/ppermute | solution.py:20
  8.5 10.3 %collective-permute-start.2 = (bf16[256,512]{1,0:T(8,128)(2,1)S(1)}, bf16[256,512]{1,0:T(8,128)(2,1)S(1)}, u32[]{:S(2)}, u32[]{:S(2)}) collective-permute-start(bf16[256,512]{1,0:T(8,128)(2,1)S(1)} %convert_element_type.6.refs_3_), channel_id=1, source_target_pairs={{0,6},{1,7},{2,4},{3,5},{4,2},{5,3},{6,0},{7,1},{8,14},{9,15},{10,... | collective-permute-start | bytes 786440 | tf_op jit(solution)/shard_map/ppermute | solution.py:20
  11.0 11.6 %collective-permute-start.1 = (bf16[256,512]{1,0:T(8,128)(2,1)S(1)}, bf16[256,512]{1,0:T(8,128)(2,1)S(1)}, u32[]{:S(2)}, u32[]{:S(2)}) collective-permute-start(bf16[256,512]{1,0:T(8,128)(2,1)S(1)} %convert_element_type.6.refs_3_), channel_id=1, source_target_pairs={{0,4},{1,5},{2,6},{3,7},{4,0},{5,1},{6,2},{7,3},{8,12},{9,13},{10,... | collective-permute-start | bytes 786440 | tf_op jit(solution)/shard_map/ppermute | solution.py:20
  11.5 11.1 %collective-permute-start = (bf16[256,512]{1,0:T(8,128)(2,1)S(1)}, bf16[256,512]{1,0:T(8,128)(2,1)S(1)}, u32[]{:S(2)}, u32[]{:S(2)}) collective-permute-start(bf16[256,512]{1,0:T(8,128)(2,1)S(1)} %convert_element_type.6.refs_3_), channel_id=1, source_target_pairs={{0,2},{1,3},{2,0},{3,1},{4,6},{5,7},{6,4},{7,5},{8,10},{9,11},{10,... | collective-permute-start | bytes 786440 | tf_op jit(solution)/shard_map/ppermute | solution.py:20
  17.8 6.5 %collective-permute-start.6 = (bf16[256,512]{1,0:T(8,128)(2,1)S(1)}, bf16[256,512]{1,0:T(8,128)(2,1)S(1)}, u32[]{:S(2)}, u32[]{:S(2)}) collective-permute-start(bf16[256,512]{1,0:T(8,128)(2,1)S(1)} %convert_element_type.6.refs_3_), channel_id=1, source_target_pairs={{0,1},{1,0},{2,3},{3,2},{4,5},{5,4},{6,7},{7,6},{8,9},{9,8},{10,11... | collective-permute-start | bytes 786440 | tf_op jit(solution)/shard_map/ppermute | solution.py:20
  22.6 1.7 %collective-permute-start.7 = (bf16[256,512]{1,0:T(8,128)(2,1)S(1)}, bf16[256,512]{1,0:T(8,128)(2,1)S(1)}, u32[]{:S(2)}, u32[]{:S(2)}) collective-permute-start(bf16[256,512]{1,0:T(8,128)(2,1)S(1)} %collective-permute-done.refs_4_), channel_id=1, source_target_pairs={{0,1},{1,0},{2,3},{3,2},{4,5},{5,4},{6,7},{7,6},{8,9},{9,8},{10,11... | collective-permute-start | bytes 786440 | tf_op jit(solution)/shard_map/ppermute | solution.py:20
  22.6 1.9 %collective-permute-start.8 = (bf16[256,512]{1,0:T(8,128)(2,1)S(1)}, bf16[256,512]{1,0:T(8,128)(2,1)S(1)}, u32[]{:S(2)}, u32[]{:S(2)}) collective-permute-start(bf16[256,512]{1,0:T(8,128)(2,1)S(1)} %collective-permute-done.1.refs_5_), channel_id=1, source_target_pairs={{0,1},{1,0},{2,3},{3,2},{4,5},{5,4},{6,7},{7,6},{8,9},{9,8},{10,11... | collective-permute-start | bytes 786440 | tf_op jit(solution)/shard_map/ppermute | solution.py:20
  23.1 1.8 %collective-permute-start.9 = (bf16[256,512]{1,0:T(8,128)(2,1)S(1)}, bf16[256,512]{1,0:T(8,128)(2,1)S(1)}, u32[]{:S(2)}, u32[]{:S(2)}) collective-permute-start(bf16[256,512]{1,0:T(8,128)(2,1)S(1)} %collective-permute-done.2.refs_6_), channel_id=1, source_target_pairs={{0,1},{1,0},{2,3},{3,2},{4,5},{5,4},{6,7},{7,6},{8,9},{9,8},{10,11... | collective-permute-start | bytes 786440 | tf_op jit(solution)/shard_map/ppermute | solution.py:20
  23.9 8.7 %collective-permute-start.5 = (bf16[256,512]{1,0:T(8,128)(2,1)S(1)}, bf16[256,512]{1,0:T(8,128)(2,1)S(1)}, u32[]{:S(2)}, u32[]{:S(2)}) collective-permute-start(bf16[256,512]{1,0:T(8,128)(2,1)S(1)} %collective-permute-done.4.refs_2_.refs_6_), channel_id=1, source_target_pairs={{0,8},{8,0},{16,24},{24,16},{1,9},{9,1},{17,25},{25,17},{2,10},{10... | collective-permute-start | bytes 786440 | tf_op jit(solution)/shard_map/ppermute | solution.py:20
  35.2 4.4 %collective-permute-start.11 = (f32[9,4,256]{2,1,0:T(4,128)S(1)}, f32[9,4,256]{2,1,0:T(4,128)S(1)}, u32[]{:S(2)}, u32[]{:S(2)}) collective-permute-start(f32[9,4,256]{2,1,0:T(4,128)S(1)} %pad_maximum_fusion), channel_id=1, source_target_pairs={{0,8},{8,0},{16,24},{24,16},{1,9},{9,1},{17,25},{25,17},{2,10},{10... | collective-permute-start | bytes 110600 | tf_op jit(solution)/shard_map/ppermute | solution.py:20
  35.7 3.9 %collective-permute-start.10 = (f32[4,8,256]{2,1,0:T(8,128)S(1)}, f32[4,8,256]{2,1,0:T(8,128)S(1)}, u32[]{:S(2)}, u32[]{:S(2)}) collective-permute-start(f32[4,8,256]{2,1,0:T(8,128)S(1)} %get-tuple-element.50), channel_id=1, source_target_pairs={{0,2},{1,3},{2,0},{3,1},{4,6},{5,7},{6,4},{7,5},{8,10},{9,11},{10,... | collective-permute-start | bytes 98312 | tf_op jit(solution)/shard_map/ppermute | solution.py:20
  39.8 4.9 %collective-permute-start.13 = (f32[9,4,256]{2,1,0:T(4,128)S(1)}, f32[9,4,256]{2,1,0:T(4,128)S(1)}, u32[]{:S(2)}, u32[]{:S(2)}) collective-permute-start(f32[9,4,256]{2,1,0:T(4,128)S(1)} %constant_dynamic-update-slice_fusion), channel_id=1, source_target_pairs={{0,16},{8,24},{16,0},{24,8},{1,17},{9,25},{17,1},{25,9},{2,18},{10... | collective-permute-start | bytes 110600 | tf_op jit(solution)/shard_map/ppermute | solution.py:20
  40.2 3.9 %collective-permute-start.12 = (f32[4,8,256]{2,1,0:T(8,128)S(1)}, f32[4,8,256]{2,1,0:T(8,128)S(1)}, u32[]{:S(2)}, u32[]{:S(2)}) collective-permute-start(f32[4,8,256]{2,1,0:T(8,128)S(1)} %pad_maximum_fusion.1), channel_id=1, source_target_pairs={{0,4},{1,5},{2,6},{3,7},{4,0},{5,1},{6,2},{7,3},{8,12},{9,13},{10,... | collective-permute-start | bytes 98312 | tf_op jit(solution)/shard_map/ppermute | solution.py:20
  44.7 1.3 %collective-permute-start.14 = (f32[4,8,256]{2,1,0:T(8,128)S(1)}, f32[4,8,256]{2,1,0:T(8,128)S(1)}, u32[]{:S(2)}, u32[]{:S(2)}) collective-permute-start(f32[4,8,256]{2,1,0:T(8,128)S(1)} %pad_maximum_fusion.2), channel_id=1, source_target_pairs={{0,1},{1,0},{2,3},{3,2},{4,5},{5,4},{6,7},{7,6},{8,9},{9,8},{10,11... | collective-permute-start | bytes 98312 | tf_op jit(solution)/shard_map/ppermute | solution.py:20
  47.9 8.8 %collective-permute-start.15 = (bf16[272,512]{1,0:T(8,128)(2,1)S(1)}, bf16[272,512]{1,0:T(8,128)(2,1)S(1)}, u32[]{:S(2)}, u32[]{:S(2)}) collective-permute-start(bf16[272,512]{1,0:T(8,128)(2,1)S(1)} %get-tuple-element.61), channel_id=1, source_target_pairs={{0,8},{8,0},{16,24},{24,16},{1,9},{9,1},{17,25},{25,17},{2,10},{10... | collective-permute-start | bytes 835592 | tf_op jit(solution)/shard_map/ppermute | solution.py:20
  54.0 6.7 %collective-permute-start.16 = (f32[4,264,512]{2,1,0:T(8,128)S(1)}, f32[4,264,512]{2,1,0:T(8,128)S(1)}, u32[]{:S(2)}, u32[]{:S(2)}) collective-permute-start(f32[4,264,512]{2,1,0:T(8,128)S(1)} %get-tuple-element.63), channel_id=1, source_target_pairs={{0,1},{1,0},{2,3},{3,2},{4,5},{5,4},{6,7},{7,6},{8,9},{9,8},{10,11... | collective-permute-start | bytes 6488072 | tf_op jit(solution)/shard_map/ppermute | solution.py:20
  57.3 14.9 %collective-permute-start.19 = (bf16[272,512]{1,0:T(8,128)(2,1)S(1)}, bf16[272,512]{1,0:T(8,128)(2,1)S(1)}, u32[]{:S(2)}, u32[]{:S(2)}) collective-permute-start(bf16[272,512]{1,0:T(8,128)(2,1)S(1)} %pack_text.1.refs_4_), channel_id=1, source_target_pairs={{0,16},{8,24},{16,0},{24,8},{1,17},{9,25},{17,1},{25,9},{2,18},{10... | collective-permute-start | bytes 835592 | tf_op jit(solution)/shard_map/ppermute | solution.py:20
  60.7 12.5 %collective-permute-start.18 = (bf16[272,512]{1,0:T(8,128)(2,1)S(1)}, bf16[272,512]{1,0:T(8,128)(2,1)S(1)}, u32[]{:S(2)}, u32[]{:S(2)}) collective-permute-start(bf16[272,512]{1,0:T(8,128)(2,1)S(1)} %get-tuple-element.68), channel_id=1, source_target_pairs={{0,8},{8,0},{16,24},{24,16},{1,9},{9,1},{17,25},{25,17},{2,10},{10... | collective-permute-start | bytes 835592 | tf_op jit(solution)/shard_map/ppermute | solution.py:20
  63.5 11.6 %collective-permute-start.17 = (bf16[272,512]{1,0:T(8,128)(2,1)S(1)}, bf16[272,512]{1,0:T(8,128)(2,1)S(1)}, u32[]{:S(2)}, u32[]{:S(2)}) collective-permute-start(bf16[272,512]{1,0:T(8,128)(2,1)S(1)} %get-tuple-element.66), channel_id=1, source_target_pairs={{0,2},{1,3},{2,0},{3,1},{4,6},{5,7},{6,4},{7,5},{8,10},{9,11},{10,... | collective-permute-start | bytes 835592 | tf_op jit(solution)/shard_map/ppermute | solution.py:20
  65.0 13.0 %collective-permute-start.20 = (bf16[272,512]{1,0:T(8,128)(2,1)S(1)}, bf16[272,512]{1,0:T(8,128)(2,1)S(1)}, u32[]{:S(2)}, u32[]{:S(2)}) collective-permute-start(bf16[272,512]{1,0:T(8,128)(2,1)S(1)} %get-tuple-element.71), channel_id=1, source_target_pairs={{0,4},{1,5},{2,6},{3,7},{4,0},{5,1},{6,2},{7,3},{8,12},{9,13},{10,... | collective-permute-start | bytes 835592 | tf_op jit(solution)/shard_map/ppermute | solution.py:20
  65.8 12.3 %collective-permute-start.21 = (bf16[272,512]{1,0:T(8,128)(2,1)S(1)}, bf16[272,512]{1,0:T(8,128)(2,1)S(1)}, u32[]{:S(2)}, u32[]{:S(2)}) collective-permute-start(bf16[272,512]{1,0:T(8,128)(2,1)S(1)} %get-tuple-element.72), channel_id=1, source_target_pairs={{0,6},{1,7},{2,4},{3,5},{4,2},{5,3},{6,0},{7,1},{8,14},{9,15},{10,... | collective-permute-start | bytes 835592 | tf_op jit(solution)/shard_map/ppermute | solution.py:20

commit v14 on v13

--- a/solution.py
+++ b/solution.py
@@ -23,36 +23,32 @@
 def gather_both(image, text, n_col, n_row):
     images = [swap(image, "col", n_col, q) for q in range(2, n_col, 2)]
     texts = [swap(text, "row", n_row, q) for q in range(1, n_row - 1)]
-    images, texts = lax.optimization_barrier((images, texts))
+    texts.append(swap(texts[-1], "row", n_row, 1))
+    images, texts[:-1] = lax.optimization_barrier((images, texts[:-1]))
     odd = [swap(i, "col", n_col, 1) for i in (image, *images)]
-    return [image, *images], odd, [text, *texts], [swap(texts[-1], "row", n_row, 1)]
+    return [image, *images], odd, [text, *texts]
 
 
 def nt_dot(a, b):
     return lax.dot_general(a, b, (((1,), (1,)), ((), ())), preferred_element_type=jnp.float32)
 
 
-def stats_kernel(first, n_text, block, coef_ref, place_ref, *refs):
-    texts, refs = refs[:n_text], refs[n_text:]
+def stats_kernel(n_text, block, coef_ref, place_ref, *refs):
+    received, refs = refs[:n_text], refs[n_text:]
     coef = coef_ref[0, 0]
     r_place, c_place = place_ref[0, 0], place_ref[0, 1]
-    *refs, row_max, col_max, col_sum, col_dot, row_diag = refs
-    if first:
-        *refs, even, odd, row_ref, col_ref, tile = refs
-        halves = (even, odd)
-        each = len(refs) // 2
-        for i, piece in enumerate(refs):
-            at = (i % each) * block
-            halves[i // each][at : at + block, :] = piece[...]
-        before = None
-    else:
-        even, odd, *before, last, row_ref, col_ref, tile = refs
-        halves = (even, odd)
-        last[...] = functools.reduce(jnp.add, [text[...] for text in texts])
-        texts, n_text = [last], 1
+    *refs, row_ref, col_ref, tile, row_max, col_max, col_sum, col_dot, row_diag = refs
+    *refs, even, odd = refs
+    pieces, texts = refs[:-n_text], refs[-n_text:]
+    for text, whole in zip(texts, received):
+        text[...] = whole[:block, :]
+    halves = (even, odd)
+    each = len(pieces) // 2
+    for i, piece in enumerate(pieces):
+        at = (i % each) * block
+        halves[i // each][at : at + block, :] = piece[...]
     cols, rows = tile.shape
     half = rows // 2
-    lead = 0 if first else col_ref.shape[1] - n_text
     col_max[...] = jnp.full(col_max.shape, -jnp.inf, jnp.float32)
     row_diag[...] = jnp.zeros(row_diag.shape, jnp.float32)
     n_col, n_row = row_ref.shape[1], col_ref.shape[1]
@@ -79,7 +75,7 @@
         lax.fori_loop(0, half // block, products, 0, unroll=4)
 
     for t in range(n_text):
-        among = c_place * n_row + (r_place ^ (lead + t)) - r_place * n_col
+        among = c_place * n_row + (r_place ^ t) - r_place * n_col
 
         @pl.when((among >= 0) & (among < n_col))
         def _():
@@ -138,15 +134,13 @@
             )
         new.append(row_diag[0:1, at + (q % 2) * half : at + (q % 2) * half + block])
         placed = [jnp.where(here, n, p) for n, p in zip(new, placed)]
-    if before:
-        placed = merged(placed, [before[0][i] for i in range(4)])
     for i in range(4):
         row_ref[i] = placed[i]
     row_ids = lax.broadcasted_iota(jnp.int32, (n_row, block), 0)
-    placed = [before[1][i] if before else jnp.zeros((n_row, block), jnp.float32) for i in range(3)]
+    placed = [jnp.zeros((n_row, block), jnp.float32)] * 3
     for t in range(n_text):
         part = pl.ds(t * block, block)
-        here = row_ids == (r_place ^ (lead + t))
+        here = row_ids == (r_place ^ t)
         new = [col_max[part, :].T[0:1, :]]
         for which in (col_sum, col_dot):
             new.append(jnp.sum(which[part, :].T, axis=0, keepdims=True))
@@ -155,17 +149,16 @@
         col_ref[i] = placed[i]
 
 
-def stats(coef, place, texts, images, before, n_col, n_row, keep):
-    block, width = texts[0].shape
-    first = not before
-    rows, cols = block * n_col, block * (len(texts) if first else 1)
+def stats(coef, place, texts, images, keep):
+    block, width = images[0].shape
+    rows, cols = block * len(images), block * len(texts)
     vmem = pl.BlockSpec(memory_space=VMEM)
     smem = pl.BlockSpec(memory_space=SMEM)
-    half = jax.ShapeDtypeStruct((rows // 2, width), jnp.bfloat16)
-    out_shape = [half, half] if first else [jax.ShapeDtypeStruct((block, width), jnp.bfloat16)]
+    out_shape = [jax.ShapeDtypeStruct((block, width), jnp.bfloat16)] * len(texts)
+    out_shape += [jax.ShapeDtypeStruct((rows // 2, width), jnp.bfloat16)] * 2
     out_shape += [
-        jax.ShapeDtypeStruct((4, n_col, block), jnp.float32),
-        jax.ShapeDtypeStruct((3, n_row, block), jnp.float32),
+        jax.ShapeDtypeStruct((4, len(images), block), jnp.float32),
+        jax.ShapeDtypeStruct((3, len(texts), block), jnp.float32),
     ]
     scratch = [
         VMEM((8, rows), jnp.float32),
@@ -178,10 +171,10 @@
         out_shape.append(jax.ShapeDtypeStruct((cols, rows), jnp.float32))
     else:
         scratch.insert(0, VMEM((cols, rows), jnp.float32))
-    return pl.pallas_call(
-        functools.partial(stats_kernel, first, len(texts), block),
+    outs = pl.pallas_call(
+        functools.partial(stats_kernel, len(texts), block),
         out_shape=tuple(out_shape),
-        in_specs=[smem, smem] + [vmem] * (len(texts) + len(images) + len(before)),
+        in_specs=[smem, smem] + [vmem] * (len(texts) + len(images)),
         out_specs=(vmem,) * len(out_shape),
         scratch_shapes=scratch,
         compiler_params=pltpu.CompilerParams(
@@ -190,8 +183,9 @@
         cost_estimate=pl.CostEstimate(
             flops=FLOPS * 2 * rows * cols * width, bytes_accessed=0, transcendentals=0
         ),
-        name="stats" if first else "stats_last",
-    )(coef, place, *texts, *images, *before)
+        name="stats",
+    )(coef, place, *texts, *images)
+    return outs[: len(texts)], *outs[len(texts) : len(texts) + 4], outs[len(texts) + 4 :]
 
 
 def merged(a, b):
@@ -321,12 +315,15 @@
         out_specs=vmem,
         scratch_shapes=[VMEM((size, LANES), jnp.float32), VMEM((len(codes), size, LANES), jnp.float32)],
         compiler_params=pltpu.CompilerParams(vmem_limit_bytes=6 * 2**20),
+        cost_estimate=pl.CostEstimate(
+            flops=FLOPS * 32 * size * size * width, bytes_accessed=0, transcendentals=0
+        ),
         name="pack_text",
     )(base, *codes)
 
 
-def pack_images_kernel(near, far, own, *refs):
-    outs, powers = refs[:-1], refs[-1]
+def pack_images_kernel(n, near, far, *refs):
+    own, *outs, powers = refs[-n - 1 :]
     size = near.shape[1] - EXTRA
     own[...] = near[0] + far[0]
     for j, out in enumerate(outs, 1):
@@ -339,20 +336,23 @@
         )
 
 
-def pack_images(near, far):
+def pack_images(near, far, after):
     n, rows, width = near.shape
     size = rows - EXTRA
     vmem = pl.BlockSpec(memory_space=VMEM)
     code = jax.ShapeDtypeStruct((size + MORE, width), jnp.bfloat16)
     own, *codes = pl.pallas_call(
-        pack_images_kernel,
+        functools.partial(pack_images_kernel, n),
         out_shape=(jax.ShapeDtypeStruct((rows, width), jnp.float32),) + (code,) * (n - 1),
-        in_specs=[vmem] * 2,
+        in_specs=[vmem] * 2 + [pl.BlockSpec(memory_space=pl.ANY)] * len(after),
         out_specs=(vmem,) * n,
         scratch_shapes=[VMEM((n - 1, size, LANES), jnp.float32)],
         compiler_params=pltpu.CompilerParams(vmem_limit_bytes=(4 + 2 * n) * 2**20),
+        cost_estimate=pl.CostEstimate(
+            flops=FLOPS * 8 * n * size * size * width, bytes_accessed=0, transcendentals=0
+        ),
         name="pack_images",
-    )(near, far)
+    )(near, far, *after)
     return own, codes
 
 
@@ -500,7 +500,7 @@
     for i, t in enumerate(order):
         text_block(
             texts[i],
-            tile.at[pl.ds((t - lowest) * block, block)] if kept else None,
+            tile.at[pl.ds(t * block, block)] if kept else None,
             t,
             (even, odd),
             row_lse,
@@ -525,21 +525,23 @@
             outs[i][:block, :] = total[at : at + block, :]
             put_extra(outs[i].at[block:, :], row_extra)
     if n_done:
-        far_ref = rest[0]
+        far_ref, near_ref = rest[:2]
         by_text = {t: (grads.at[pl.ds((t - lowest) * block, block)], texts[i]) for i, t in enumerate(order)}
 
-        def one(j, carry):
-            far_ref[j, :block, :] = image_block(
-                [*done_grads, *[by_text[t][0] for t in order]],
-                [*done_texts, *[by_text[t][1] for t in order]],
-                pl.multiple_of(j * block + half, block),
-                block,
-                scale,
-            )
-            put_extra(far_ref.at[j, block:, :], col_extra)
-            return carry
-
-        lax.fori_loop(0, half // block, one, 0, unroll=4)
+        for images_ref, first in ((far_ref, half), (near_ref, 0)):
+
+            def one(j, carry):
+                images_ref[j, :block, :] = image_block(
+                    [*done_grads, *[by_text[t][0] for t in order]],
+                    [*done_texts, *[by_text[t][1] for t in order]],
+                    pl.multiple_of(j * block + first, block),
+                    block,
+                    scale,
+                )
+                put_extra(images_ref.at[j, block:, :], col_extra)
+                return carry
+
+            lax.fori_loop(0, half // block, one, 0, unroll=4)
 
 
 def text_grads(scale, coef, place, even, odd, row_lse, col_lse, row_extra, col_extra, texts, tile, order, done):
@@ -558,7 +560,7 @@
         ]
     )
     if done:
-        out_shape.append(jax.ShapeDtypeStruct((half // block, block + EXTRA, width), jnp.float32))
+        out_shape += [jax.ShapeDtypeStruct((half // block, block + EXTRA, width), jnp.float32)] * 2
     operands = [even, odd, row_lse, col_lse, row_extra, col_extra, *[texts[t] for t in order]]
     operands += tile
     operands += [grad for _, grad in done] + [texts[t] for t, _ in done]
@@ -579,42 +581,7 @@
         name=f"text_grads_{n}",
     )(scale, coef, place, *operands)
     parts = {t: outs[1 + i] for i, t in enumerate(order)}
-    return outs[0], parts, outs[-1]
-
-
-def image_kernel(n_text, block, scale_ref, extra, near_grads, last_grad, *refs):
-    texts, out_ref = refs[:n_text], refs[-1]
-    grads = [near_grads.at[pl.ds(t * block, block)] for t in range(n_text - 1)] + [last_grad]
-
-    def one(j, carry):
-        put_extra(out_ref.at[j, block:, :], extra)
-        out_ref[j, :block, :] = image_block(
-            grads, texts, pl.multiple_of(j * block, block), block, scale_ref[0, 0]
-        )
-        return carry
-
-    lax.fori_loop(0, out_ref.shape[0], one, 0, unroll=4)
-
-
-def image_grads(scale, extra, grads, texts, after):
-    n_text = len(texts)
-    rows = grads[0].shape[1]
-    block, width = texts[0].shape
-    n = rows // block // 2
-    vmem = pl.BlockSpec(memory_space=VMEM)
-    return pl.pallas_call(
-        functools.partial(image_kernel, n_text, block),
-        out_shape=jax.ShapeDtypeStruct((n, block + EXTRA, width), jnp.float32),
-        in_specs=[pl.BlockSpec(memory_space=SMEM)]
-        + [vmem] * (n_text + 3)
-        + [pl.BlockSpec(memory_space=pl.ANY)] * len(after),
-        out_specs=vmem,
-        compiler_params=pltpu.CompilerParams(vmem_limit_bytes=12 * 2**20),
-        cost_estimate=pl.CostEstimate(
-            flops=FLOPS * 2 * n * block * n_text * block * width, bytes_accessed=0, transcendentals=0
-        ),
-        name="image_grads",
-    )(scale, extra, *grads, *texts, *after)
+    return outs[0], parts, outs[1 + n :]
 
 
 def on_device(n_row, n_col, image_embeds, text_embeds, logit_scale):
@@ -623,29 +590,22 @@
     place = jnp.stack([r, c]).reshape(1, 2)
     scale = logit_scale.reshape(1, 1)
     coef = scale * LOG2E
-    image_half, text_half = image_embeds.astype(jnp.bfloat16), text_embeds.astype(jnp.bfloat16)
-    even, odd, texts, text_last = gather_both(image_half, text_half, n_col, n_row)
+    image_half = image_embeds.astype(jnp.bfloat16)
+    text_half = jnp.pad(text_embeds.astype(jnp.bfloat16), ((0, 16), (0, 0)))
+    even, odd, texts = gather_both(image_half, text_half, n_col, n_row)
     keep = 4 * n_row * n_col * block * block <= 16 * 2**20
-    even, odd, *before = stats(
-        coef, place, texts, (*even, *odd), (), n_col, n_row, keep
-    )
-    text_last, row_parts, col_parts, *tile_last = stats(
-        coef, place, text_last, (even, odd), before[:2], n_col, n_row, keep
-    )
-    texts = [*texts, text_last]
-    tile = before[2:]
+    texts, even, odd, row_parts, col_parts, tile = stats(coef, place, texts, (*even, *odd), keep)
     row_lse, row_extra, col_lse, col_extra = exchanged(row_parts, col_parts, n_col, n_row)
 
     held = (scale, coef, place, even, odd, row_lse, col_lse, row_extra, col_extra, texts)
     last = n_row - 1
-    last_grad, parts, _ = text_grads(*held, tile_last, [last], [])
+    last_grad, parts, _ = text_grads(*held, tile, [last], [])
     received = swap(parts[last], "row", n_row, 1)
-    near_grads, more_parts, far = text_grads(*held, tile, list(range(last))[::-1], [(last, last_grad)])
+    _, more_parts, (far, near) = text_grads(*held, tile, list(range(last))[::-1], [(last, last_grad)])
     parts |= more_parts
     codes = {q: [] for q in range(0, n_row, 2)}
     codes[last ^ 1].append(received)
     after = [pack_text(parts[last ^ 1], codes[last ^ 1])] if n_row > 2 else [received]
-    near = image_grads(scale, col_extra, [near_grads, last_grad], texts, after)
     far = swap(far, "col", n_col, 1)
     odd_parts, far = lax.optimization_barrier(([parts[q] for q in range(1, last, 2)], far))
     for q, part in zip(range(1, last, 2), odd_parts):
@@ -657,7 +617,7 @@
             del codes[q]
     grad_text, text_extra, _ = total_of(coef, parts[0], codes[0], True, [], "grad_text")
 
-    own, others = pack_images(near, far)
+    own, others = pack_images(near, far, after)
     others = [swap(code, "col", n_col, 2 * j) for j, code in enumerate(others, 1)]
     first, text_extra = lax.optimization_barrier((others[0], text_extra))
     grad_image, _, grad_scale = total_of(

time: 80.4 us -> 81.5 us (1.014)
  starting transfers between devices: 23.1 us -> 25.1 us
    pallas_call x4 -> x2, Pallas kernels: 10.4 us -> 8.27 us  [the longest x1 7.15 us: stats(): pl.pallas_call(functools.partial(stats_kernel, len(texts), block), out_sh...]
    ppermute x22, starting transfers between devices: 23.1 us -> 25.1 us  [swap(): return lax.ppermute(x, axis, [(i, i ^ q) for i in range(n)])]
    pallas_call x2, Pallas kernels: 6.3 us -> 8.23 us  [text_grads(): pl.pallas_call(functools.partial(text_kernel, tuple(order), len(done), le...]
  transfers between devices with their start and end apart: 22 -> 22, of which waited for: 16 -> 15; matrix products, arithmetic and copies ran while one was open for 1% -> 1% of each run, Pallas kernels for 19% -> 13%
where the time goes in v14:
time: 81.5 us; the launch traced here: 81.3 us
  waiting for transfers between devices  30.8 us (38%)
  starting transfers between devices  25.1 us (31%)
  Pallas kernels  21.3 us (26%)
  other arithmetic  2.42 us (3%)
  between operations  1.6 us (2%)
    ppermute x22, waiting for transfers between devices, swap(): return lax.ppermute(x, axis, [(i, i ^ q) for i in range(n)])  30.8 us
    ppermute x22, starting transfers between devices, swap(): return lax.ppermute(x, axis, [(i, i ^ q) for i in range(n)])  25.1 us
    pallas_call x2, Pallas kernels, text_grads(): pl.pallas_call(functools.partial(text_kernel, tuple(order), len(done), le...  8.23 us
    pallas_call x1, Pallas kernels, stats(): pl.pallas_call(functools.partial(stats_kernel, len(texts), block), out_sh...  7.15 us
    pallas_call x2, Pallas kernels, total_of(): pl.pallas_call(functools.partial(total_kernel, len(codes), in_order), out...  3.78 us
  transfers between devices with their start and end apart: 22, of which 15 were waited for; matrix products, arithmetic and copies ran while one was open for 1% of the time, Pallas kernels for 13%

profile of v14, /device:TPU:0, one launch (start us, length us, event | category | flops | bytes accessed | tf_op | source)
XLA Modules:
  0.0 81.3 jit_solution(14504834183345842373)
XLA Ops:
  0.6 1.1 %convert_element_type.8 = bf16[256,512]{1,0:T(8,128)(2,1)S(1)} convert(f32[256,512]{1,0:T(8,128)} %param.4) | non-fusion elementwise | flops 131072 | bytes 786432 | tf_op jit(solution)/shard_map/convert_element_type | solution.py:594
  1.7 4.1 %collective-permute-start.4 = (bf16[272,512]{1,0:T(8,128)(2,1)S(1)}, bf16[272,512]{1,0:T(8,128)(2,1)S(1)}, u32[]{:S(2)}, u32[]{:S(2)}) collective-permute-start(bf16[272,512]{1,0:T(8,128)(2,1)S(1)} %pad.4.refs_0_), channel_id=1, source_target_pairs={{0,16},{8,24},{16,0},{24,8},{1,17},{9,25},{17,1},{25,9},{2,18},{10... | collective-permute-start | bytes 835592 | tf_op jit(solution)/shard_map/ppermute | solution.py:20
  5.8 1.6 %collective-permute-start.3 = (bf16[272,512]{1,0:T(8,128)(2,1)S(1)}, bf16[272,512]{1,0:T(8,128)(2,1)S(1)}, u32[]{:S(2)}, u32[]{:S(2)}) collective-permute-start(bf16[272,512]{1,0:T(8,128)(2,1)S(1)} %pad.4.refs_0_), channel_id=1, source_target_pairs={{0,8},{8,0},{16,24},{24,16},{1,9},{9,1},{17,25},{25,17},{2,10},{10... | collective-permute-start | bytes 835592 | tf_op jit(solution)/shard_map/ppermute | solution.py:20
  7.4 1.1 %convert_element_type.9.refs_4_ = bf16[256,512]{1,0:T(8,128)(2,1)S(1)} convert(f32[256,512]{1,0:T(8,128)} %param.3) | non-fusion elementwise | flops 131072 | bytes 786432 | tf_op jit(solution)/shard_map/convert_element_type | solution.py:593
  8.5 2.5 %collective-permute-start.2 = (bf16[256,512]{1,0:T(8,128)(2,1)S(1)}, bf16[256,512]{1,0:T(8,128)(2,1)S(1)}, u32[]{:S(2)}, u32[]{:S(2)}) collective-permute-start(bf16[256,512]{1,0:T(8,128)(2,1)S(1)} %convert_element_type.9.refs_4_), channel_id=1, source_target_pairs={{0,6},{1,7},{2,4},{3,5},{4,2},{5,3},{6,0},{7,1},{8,14},{9,15},{10,... | collective-permute-start | bytes 786440 | tf_op jit(solution)/shard_map/ppermute | solution.py:20
  12.0 6.5 %collective-permute-done.4.refs_2_ = bf16[272,512]{1,0:T(8,128)(2,1)S(1)} collective-permute-done((bf16[272,512]{1,0:T(8,128)(2,1)S(1)}, bf16[272,512]{1,0:T(8,128)(2,1)S(1)}, u32[]{:S(2)}, u32[]{:S(2)}) %collective-permute-start.4) | collective-permute-done | bytes 278560 | tf_op jit(solution)/shard_map/ppermute | solution.py:20
  18.6 0.6 collective-permute-start.5
  19.2 3.4 %collective-permute-done.1.refs_6_ = bf16[256,512]{1,0:T(8,128)(2,1)S(1)} collective-permute-done((bf16[256,512]{1,0:T(8,128)(2,1)S(1)}, bf16[256,512]{1,0:T(8,128)(2,1)S(1)}, u32[]{:S(2)}, u32[]{:S(2)}) %collective-permute-start.1) | collective-permute-done | bytes 262176 | tf_op jit(solution)/shard_map/ppermute | solution.py:20
  25.0 1.4 %collective-permute-done.5.refs_3_ = bf16[272,512]{1,0:T(8,128)(2,1)S(1)} collective-permute-done((bf16[272,512]{1,0:T(8,128)(2,1)S(1)}, bf16[272,512]{1,0:T(8,128)(2,1)S(1)}, u32[]{:S(2)}, u32[]{:S(2)}) %collective-permute-start.5) | collective-permute-done | bytes 278560 | tf_op jit(solution)/shard_map/ppermute | solution.py:20
  26.4 7.2 %stats.1 = (bf16[256,512]{1,0:T(8,128)(2,1)S(1)}, bf16[256,512]{1,0:T(8,128)(2,1)S(1)}, bf16[256,512]{1,0:T(8,128)(2,1)S(1)}, bf16[256,512]{1,0:T(8,128)(2,1)S(1...) custom-call(f32[1,1]{1,0:T(1,128)S(6)} %mul.127.coef_ref, ...), custom_call_target="tpu_custom_call" | custom-call | flops 42949672960 | tf_op jit(solution)/shard_map/stats/pallas_call | solution.py:174
  33.5 1.4 %collective-permute-start.11 = (f32[9,4,256]{2,1,0:T(4,128)S(1)}, f32[9,4,256]{2,1,0:T(4,128)S(1)}, u32[]{:S(2)}, u32[]{:S(2)}) collective-permute-start(f32[9,4,256]{2,1,0:T(4,128)S(1)} %pad_maximum_fusion), channel_id=1, source_target_pairs={{0,8},{8,0},{16,24},{24,16},{1,9},{9,1},{17,25},{25,17},{2,10},{10... | collective-permute-start | bytes 110600 | tf_op jit(solution)/shard_map/ppermute | solution.py:20
  34.9 1.6 %collective-permute-start.10 = (f32[4,8,256]{2,1,0:T(8,128)S(1)}, f32[4,8,256]{2,1,0:T(8,128)S(1)}, u32[]{:S(2)}, u32[]{:S(2)}) collective-permute-start(f32[4,8,256]{2,1,0:T(8,128)S(1)} %get-tuple-element.47), channel_id=1, source_target_pairs={{0,2},{1,3},{2,0},{3,1},{4,6},{5,7},{6,4},{7,5},{8,10},{9,11},{10,... | collective-permute-start | bytes 98312 | tf_op jit(solution)/shard_map/ppermute | solution.py:20
  36.5 2.3 %collective-permute-done.10 = f32[4,8,256]{2,1,0:T(8,128)S(1)} collective-permute-done((f32[4,8,256]{2,1,0:T(8,128)S(1)}, f32[4,8,256]{2,1,0:T(8,128)S(1)}, u32[]{:S(2)}, u32[]{:S(2)}) %collective-permute-start.10) | collective-permute-done | bytes 32800 | tf_op jit(solution)/shard_map/ppermute | solution.py:20
  39.0 3.4 %collective-permute-start.13 = (f32[9,4,256]{2,1,0:T(4,128)S(1)}, f32[9,4,256]{2,1,0:T(4,128)S(1)}, u32[]{:S(2)}, u32[]{:S(2)}) collective-permute-start(f32[9,4,256]{2,1,0:T(4,128)S(1)} %constant_dynamic-update-slice_fusion), channel_id=1, source_target_pairs={{0,16},{8,24},{16,0},{24,8},{1,17},{9,25},{17,1},{25,9},{2,18},{10... | collective-permute-start | bytes 110600 | tf_op jit(solution)/shard_map/ppermute | solution.py:20
  42.4 1.5 %collective-permute-start.12 = (f32[4,8,256]{2,1,0:T(8,128)S(1)}, f32[4,8,256]{2,1,0:T(8,128)S(1)}, u32[]{:S(2)}, u32[]{:S(2)}) collective-permute-start(f32[4,8,256]{2,1,0:T(8,128)S(1)} %pad_maximum_fusion.1), channel_id=1, source_target_pairs={{0,4},{1,5},{2,6},{3,7},{4,0},{5,1},{6,2},{7,3},{8,12},{9,13},{10,... | collective-permute-start | bytes 98312 | tf_op jit(solution)/shard_map/ppermute | solution.py:20
  44.0 2.4 %collective-permute-done.12 = f32[4,8,256]{2,1,0:T(8,128)S(1)} collective-permute-done((f32[4,8,256]{2,1,0:T(8,128)S(1)}, f32[4,8,256]{2,1,0:T(8,128)S(1)}, u32[]{:S(2)}, u32[]{:S(2)}) %collective-permute-start.12) | collective-permute-done | bytes 32800 | tf_op jit(solution)/shard_map/ppermute | solution.py:20
  46.5 1.2 %collective-permute-done.14 = f32[4,8,256]{2,1,0:T(8,128)S(1)} collective-permute-done((f32[4,8,256]{2,1,0:T(8,128)S(1)}, f32[4,8,256]{2,1,0:T(8,128)S(1)}, u32[]{:S(2)}, u32[]{:S(2)}) %collective-permute-start.14) | collective-permute-done | bytes 32800 | tf_op jit(solution)/shard_map/ppermute | solution.py:20
  47.7 1.7 %text_grads_1.1 = (bf16[256,2048]{1,0:T(8,128)(2,1)S(1)}, bf16[272,512]{1,0:T(8,128)(2,1)S(1)}) custom-call(f32[1,1]{1,0:T(1,128)} %bitcast.241.scale_ref, f32[1,1]{1,0:T(1,128)S(6)} %mul.127.coef_ref, s32[1,2]{1,0:T(1,128)S(1)} %add_bitcast_fusion.place_ref, bf16[1024,512]{1,0:T(8,128)(2,1)S(1)} %get-tuple-element.45.refs_0_, ...), custom_call_target="tpu_custom_call" | custom-call | flops 21474836480 | tf_op jit(solution)/shard_map/text_grads_1/pallas_call | solution.py:567
  49.9 6.5 %text_grads_3.1 = (bf16[768,2048]{1,0:T(8,128)(2,1)}, f32[264,512]{1,0:T(8,128)S(1)}, bf16[272,512]{1,0:T(8,128)(2,1)S(1)}, f32[264,512]{1,0:T(8,128)S(1)}, f32[...) custom-call(f32[1,1]{1,0:T(1,128)} %bitcast.242.scale_ref, f32[1,1]{1,0:T(1,128)S(6)} %mul.127.coef_ref, ...), custom_call_target="tpu_custom_call" | custom-call | flops 64424509440 | tf_op jit(solution)/shard_map/text_grads_3/pallas_call | solution.py:567
  56.4 1.9 %collective-permute-done.16.refs_0_ = bf16[272,512]{1,0:T(8,128)(2,1)S(1)} collective-permute-done((bf16[272,512]{1,0:T(8,128)(2,1)S(1)}, bf16[272,512]{1,0:T(8,128)(2,1)S(1)}, u32[]{:S(2)}, u32[]{:S(2)}) %collective-permute-start.16) | collective-permute-done | bytes 278560 | tf_op jit(solution)/shard_map/ppermute | solution.py:20
  58.3 0.7 pack_text.1.refs_0_
  59.0 1.0 %collective-permute-start.19 = (bf16[272,512]{1,0:T(8,128)(2,1)S(1)}, bf16[272,512]{1,0:T(8,128)(2,1)S(1)}, u32[]{:S(2)}, u32[]{:S(2)}) collective-permute-start(bf16[272,512]{1,0:T(8,128)(2,1)S(1)} %pack_text.1.refs_0_), channel_id=1, source_target_pairs={{0,16},{8,24},{16,0},{24,8},{1,17},{9,25},{17,1},{25,9},{2,18},{10... | collective-permute-start | bytes 835592 | tf_op jit(solution)/shard_map/ppermute | solution.py:20
  60.0 0.7 collective-permute-done.15.far
  60.7 1.7 %collective-permute-start.18 = (bf16[272,512]{1,0:T(8,128)(2,1)S(1)}, bf16[272,512]{1,0:T(8,128)(2,1)S(1)}, u32[]{:S(2)}, u32[]{:S(2)}) collective-permute-start(bf16[272,512]{1,0:T(8,128)(2,1)S(1)} %get-tuple-element.68), channel_id=1, source_target_pairs={{0,8},{8,0},{16,24},{24,16},{1,9},{9,1},{17,25},{25,17},{2,10},{10... | collective-permute-start | bytes 835592 | tf_op jit(solution)/shard_map/ppermute | solution.py:20
  62.4 1.1 %pack_images.1 = (f32[264,512]{1,0:T(8,128)S(1)}, bf16[272,512]{1,0:T(8,128)(2,1)S(1)}, bf16[272,512]{1,0:T(8,128)(2,1)S(1)}, bf16[272,512]{1,0:T(8,128)(2,1)S(1)}) custom-call(f32[4,264,512]{2,1,0:T(8,128)S(1)} %get-tuple-element.59.near, f32[4,264,512]{2,1,0:T(8,128)S(1)} %collective-permute-done.15.far, bf16[272,512]{1,0:T(8,128)(2,1)S(1)} %pack_text.1.refs_0_), custom_call_target="tpu_custom_call" | custom-call | flops 21474836480 | tf_op jit(solution)/shard_map/pack_images/pallas_call | solution.py:344
  63.5 1.6 %collective-permute-start.17 = (bf16[272,512]{1,0:T(8,128)(2,1)S(1)}, bf16[272,512]{1,0:T(8,128)(2,1)S(1)}, u32[]{:S(2)}, u32[]{:S(2)}) collective-permute-start(bf16[272,512]{1,0:T(8,128)(2,1)S(1)} %get-tuple-element.66), channel_id=1, source_target_pairs={{0,2},{1,3},{2,0},{3,1},{4,6},{5,7},{6,4},{7,5},{8,10},{9,11},{10,... | collective-permute-start | bytes 835592 | tf_op jit(solution)/shard_map/ppermute | solution.py:20
  65.1 1.6 %collective-permute-start.20 = (bf16[272,512]{1,0:T(8,128)(2,1)S(1)}, bf16[272,512]{1,0:T(8,128)(2,1)S(1)}, u32[]{:S(2)}, u32[]{:S(2)}) collective-permute-start(bf16[272,512]{1,0:T(8,128)(2,1)S(1)} %get-tuple-element.71), channel_id=1, source_target_pairs={{0,4},{1,5},{2,6},{3,7},{4,0},{5,1},{6,2},{7,3},{8,12},{9,13},{10,... | collective-permute-start | bytes 835592 | tf_op jit(solution)/shard_map/ppermute | solution.py:20
  67.1 6.8 %collective-permute-done.19.refs_1_ = bf16[272,512]{1,0:T(8,128)(2,1)S(1)} collective-permute-done((bf16[272,512]{1,0:T(8,128)(2,1)S(1)}, bf16[272,512]{1,0:T(8,128)(2,1)S(1)}, u32[]{:S(2)}, u32[]{:S(2)}) %collective-permute-start.19) | collective-permute-done | bytes 278560 | tf_op jit(solution)/shard_map/ppermute | solution.py:20
  73.9 0.8 %collective-permute-done.18.refs_0_ = bf16[272,512]{1,0:T(8,128)(2,1)S(1)} collective-permute-done((bf16[272,512]{1,0:T(8,128)(2,1)S(1)}, bf16[272,512]{1,0:T(8,128)(2,1)S(1)}, u32[]{:S(2)}, u32[]{:S(2)}) %collective-permute-start.18) | collective-permute-done | bytes 278560 | tf_op jit(solution)/shard_map/ppermute | solution.py:20
  74.8 1.8 %grad_text.1 = (f32[256,512]{1,0:T(8,128)}, f32[8,256]{1,0:T(8,128)S(1)}, f32[1,1]{1,0:T(1,128)}) custom-call(f32[1,1]{1,0:T(1,128)S(6)} %mul.127.coef_ref, f32[264,512]{1,0:T(8,128)S(1)} %get-tuple-element.67.base, bf16[272,512]{1,0:T(8,128)(2,1)S(1)} %collective-permute-done.18.refs_0_, bf16[272,512]{1,0:T(8,128)(2,1)S(1)} %collective-permute-done.19.refs_1_), custom_call_target="tpu_custom_call" | custom-call | tf_op jit(solution)/shard_map/grad_text/pallas_call | solution.py:417
  76.9 2.3 %collective-permute-done.20.refs_0_ = bf16[272,512]{1,0:T(8,128)(2,1)S(1)} collective-permute-done((bf16[272,512]{1,0:T(8,128)(2,1)S(1)}, bf16[272,512]{1,0:T(8,128)(2,1)S(1)}, u32[]{:S(2)}, u32[]{:S(2)}) %collective-permute-start.20) | collective-permute-done | bytes 278560 | tf_op jit(solution)/shard_map/ppermute | solution.py:20
  79.2 1.9 %grad_image.1 = (f32[256,512]{1,0:T(8,128)}, f32[8,256]{1,0:T(8,128)}, f32[1,1]{1,0:T(1,128)}) custom-call(f32[1,1]{1,0:T(1,128)S(6)} %mul.127.coef_ref, f32[264,512]{1,0:T(8,128)S(1)} %added.1.base, bf16[272,512]{1,0:T(8,128)(2,1)S(1)} %collective-permute-done.20.refs_0_, bf16[272,512]{1,0:T(8,128)(2,1)S(1)} %collective-permute-done.21.refs_1_, ...), custom_call_target="tpu_custom_call" | custom-call | tf_op jit(solution)/shard_map/grad_image/pallas_call | solution.py:417
  (43 shorter events, 4.2 us)
Async XLA Ops:
  1.7 16.8 %collective-permute-start.4 = (bf16[272,512]{1,0:T(8,128)(2,1)S(1)}, bf16[272,512]{1,0:T(8,128)(2,1)S(1)}, u32[]{:S(2)}, u32[]{:S(2)}) collective-permute-start(bf16[272,512]{1,0:T(8,128)(2,1)S(1)} %pad.4.refs_0_), channel_id=1, source_target_pairs={{0,16},{8,24},{16,0},{24,8},{1,17},{9,25},{17,1},{25,9},{2,18},{10... | collective-permute-start | bytes 835592 | tf_op jit(solution)/shard_map/ppermute | solution.py:20
  5.8 16.8 %collective-permute-start.3 = (bf16[272,512]{1,0:T(8,128)(2,1)S(1)}, bf16[272,512]{1,0:T(8,128)(2,1)S(1)}, u32[]{:S(2)}, u32[]{:S(2)}) collective-permute-start(bf16[272,512]{1,0:T(8,128)(2,1)S(1)} %pad.4.refs_0_), channel_id=1, source_target_pairs={{0,8},{8,0},{16,24},{24,16},{1,9},{9,1},{17,25},{25,17},{2,10},{10... | collective-permute-start | bytes 835592 | tf_op jit(solution)/shard_map/ppermute | solution.py:20
  8.5 10.7 %collective-permute-start.2 = (bf16[256,512]{1,0:T(8,128)(2,1)S(1)}, bf16[256,512]{1,0:T(8,128)(2,1)S(1)}, u32[]{:S(2)}, u32[]{:S(2)}) collective-permute-start(bf16[256,512]{1,0:T(8,128)(2,1)S(1)} %convert_element_type.9.refs_4_), channel_id=1, source_target_pairs={{0,6},{1,7},{2,4},{3,5},{4,2},{5,3},{6,0},{7,1},{8,14},{9,15},{10,... | collective-permute-start | bytes 786440 | tf_op jit(solution)/shard_map/ppermute | solution.py:20
  11.0 11.6 %collective-permute-start.1 = (bf16[256,512]{1,0:T(8,128)(2,1)S(1)}, bf16[256,512]{1,0:T(8,128)(2,1)S(1)}, u32[]{:S(2)}, u32[]{:S(2)}) collective-permute-start(bf16[256,512]{1,0:T(8,128)(2,1)S(1)} %convert_element_type.9.refs_4_), channel_id=1, source_target_pairs={{0,4},{1,5},{2,6},{3,7},{4,0},{5,1},{6,2},{7,3},{8,12},{9,13},{10,... | collective-permute-start | bytes 786440 | tf_op jit(solution)/shard_map/ppermute | solution.py:20
  11.5 11.1 %collective-permute-start = (bf16[256,512]{1,0:T(8,128)(2,1)S(1)}, bf16[256,512]{1,0:T(8,128)(2,1)S(1)}, u32[]{:S(2)}, u32[]{:S(2)}) collective-permute-start(bf16[256,512]{1,0:T(8,128)(2,1)S(1)} %convert_element_type.9.refs_4_), channel_id=1, source_target_pairs={{0,2},{1,3},{2,0},{3,1},{4,6},{5,7},{6,4},{7,5},{8,10},{9,11},{10,... | collective-permute-start | bytes 786440 | tf_op jit(solution)/shard_map/ppermute | solution.py:20
  18.6 7.8 %collective-permute-start.5 = (bf16[272,512]{1,0:T(8,128)(2,1)S(1)}, bf16[272,512]{1,0:T(8,128)(2,1)S(1)}, u32[]{:S(2)}, u32[]{:S(2)}) collective-permute-start(bf16[272,512]{1,0:T(8,128)(2,1)S(1)} %collective-permute-done.4.refs_2_), channel_id=1, source_target_pairs={{0,8},{8,0},{16,24},{24,16},{1,9},{9,1},{17,25},{25,17},{2,10},{10... | collective-permute-start | bytes 835592 | tf_op jit(solution)/shard_map/ppermute | solution.py:20
  19.2 4.7 %collective-permute-start.6 = (bf16[256,512]{1,0:T(8,128)(2,1)S(1)}, bf16[256,512]{1,0:T(8,128)(2,1)S(1)}, u32[]{:S(2)}, u32[]{:S(2)}) collective-permute-start(bf16[256,512]{1,0:T(8,128)(2,1)S(1)} %convert_element_type.9.refs_4_), channel_id=1, source_target_pairs={{0,1},{1,0},{2,3},{3,2},{4,5},{5,4},{6,7},{7,6},{8,9},{9,8},{10,11... | collective-permute-start | bytes 786440 | tf_op jit(solution)/shard_map/ppermute | solution.py:20
  22.7 1.5 %collective-permute-start.7 = (bf16[256,512]{1,0:T(8,128)(2,1)S(1)}, bf16[256,512]{1,0:T(8,128)(2,1)S(1)}, u32[]{:S(2)}, u32[]{:S(2)}) collective-permute-start(bf16[256,512]{1,0:T(8,128)(2,1)S(1)} %collective-permute-done.refs_5_), channel_id=1, source_target_pairs={{0,1},{1,0},{2,3},{3,2},{4,5},{5,4},{6,7},{7,6},{8,9},{9,8},{10,11... | collective-permute-start | bytes 786440 | tf_op jit(solution)/shard_map/ppermute | solution.py:20
  22.7 1.9 %collective-permute-start.8 = (bf16[256,512]{1,0:T(8,128)(2,1)S(1)}, bf16[256,512]{1,0:T(8,128)(2,1)S(1)}, u32[]{:S(2)}, u32[]{:S(2)}) collective-permute-start(bf16[256,512]{1,0:T(8,128)(2,1)S(1)} %collective-permute-done.1.refs_6_), channel_id=1, source_target_pairs={{0,1},{1,0},{2,3},{3,2},{4,5},{5,4},{6,7},{7,6},{8,9},{9,8},{10,11... | collective-permute-start | bytes 786440 | tf_op jit(solution)/shard_map/ppermute | solution.py:20
  23.2 1.8 %collective-permute-start.9 = (bf16[256,512]{1,0:T(8,128)(2,1)S(1)}, bf16[256,512]{1,0:T(8,128)(2,1)S(1)}, u32[]{:S(2)}, u32[]{:S(2)}) collective-permute-start(bf16[256,512]{1,0:T(8,128)(2,1)S(1)} %collective-permute-done.2.refs_7_), channel_id=1, source_target_pairs={{0,1},{1,0},{2,3},{3,2},{4,5},{5,4},{6,7},{7,6},{8,9},{9,8},{10,11... | collective-permute-start | bytes 786440 | tf_op jit(solution)/shard_map/ppermute | solution.py:20
  33.5 5.3 %collective-permute-start.11 = (f32[9,4,256]{2,1,0:T(4,128)S(1)}, f32[9,4,256]{2,1,0:T(4,128)S(1)}, u32[]{:S(2)}, u32[]{:S(2)}) collective-permute-start(f32[9,4,256]{2,1,0:T(4,128)S(1)} %pad_maximum_fusion), channel_id=1, source_target_pairs={{0,8},{8,0},{16,24},{24,16},{1,9},{9,1},{17,25},{25,17},{2,10},{10... | collective-permute-start | bytes 110600 | tf_op jit(solution)/shard_map/ppermute | solution.py:20
  34.9 3.9 %collective-permute-start.10 = (f32[4,8,256]{2,1,0:T(8,128)S(1)}, f32[4,8,256]{2,1,0:T(8,128)S(1)}, u32[]{:S(2)}, u32[]{:S(2)}) collective-permute-start(f32[4,8,256]{2,1,0:T(8,128)S(1)} %get-tuple-element.47), channel_id=1, source_target_pairs={{0,2},{1,3},{2,0},{3,1},{4,6},{5,7},{6,4},{7,5},{8,10},{9,11},{10,... | collective-permute-start | bytes 98312 | tf_op jit(solution)/shard_map/ppermute | solution.py:20
  39.0 7.4 %collective-permute-start.13 = (f32[9,4,256]{2,1,0:T(4,128)S(1)}, f32[9,4,256]{2,1,0:T(4,128)S(1)}, u32[]{:S(2)}, u32[]{:S(2)}) collective-permute-start(f32[9,4,256]{2,1,0:T(4,128)S(1)} %constant_dynamic-update-slice_fusion), channel_id=1, source_target_pairs={{0,16},{8,24},{16,0},{24,8},{1,17},{9,25},{17,1},{25,9},{2,18},{10... | collective-permute-start | bytes 110600 | tf_op jit(solution)/shard_map/ppermute | solution.py:20
  42.4 3.9 %collective-permute-start.12 = (f32[4,8,256]{2,1,0:T(8,128)S(1)}, f32[4,8,256]{2,1,0:T(8,128)S(1)}, u32[]{:S(2)}, u32[]{:S(2)}) collective-permute-start(f32[4,8,256]{2,1,0:T(8,128)S(1)} %pad_maximum_fusion.1), channel_id=1, source_target_pairs={{0,4},{1,5},{2,6},{3,7},{4,0},{5,1},{6,2},{7,3},{8,12},{9,13},{10,... | collective-permute-start | bytes 98312 | tf_op jit(solution)/shard_map/ppermute | solution.py:20
  46.4 1.3 %collective-permute-start.14 = (f32[4,8,256]{2,1,0:T(8,128)S(1)}, f32[4,8,256]{2,1,0:T(8,128)S(1)}, u32[]{:S(2)}, u32[]{:S(2)}) collective-permute-start(f32[4,8,256]{2,1,0:T(8,128)S(1)} %pad_maximum_fusion.2), channel_id=1, source_target_pairs={{0,1},{1,0},{2,3},{3,2},{4,5},{5,4},{6,7},{7,6},{8,9},{9,8},{10,11... | collective-permute-start | bytes 98312 | tf_op jit(solution)/shard_map/ppermute | solution.py:20
  49.5 8.8 %collective-permute-start.16 = (bf16[272,512]{1,0:T(8,128)(2,1)S(1)}, bf16[272,512]{1,0:T(8,128)(2,1)S(1)}, u32[]{:S(2)}, u32[]{:S(2)}) collective-permute-start(bf16[272,512]{1,0:T(8,128)(2,1)S(1)} %get-tuple-element.64), channel_id=1, source_target_pairs={{0,8},{8,0},{16,24},{24,16},{1,9},{9,1},{17,25},{25,17},{2,10},{10... | collective-permute-start | bytes 835592 | tf_op jit(solution)/shard_map/ppermute | solution.py:20
  56.3 4.3 %collective-permute-start.15 = (f32[4,264,512]{2,1,0:T(8,128)S(1)}, f32[4,264,512]{2,1,0:T(8,128)S(1)}, u32[]{:S(2)}, u32[]{:S(2)}) collective-permute-start(f32[4,264,512]{2,1,0:T(8,128)S(1)} %get-tuple-element.61), channel_id=1, source_target_pairs={{0,1},{1,0},{2,3},{3,2},{4,5},{5,4},{6,7},{7,6},{8,9},{9,8},{10,11... | collective-permute-start | bytes 6488072 | tf_op jit(solution)/shard_map/ppermute | solution.py:20
  59.0 14.9 %collective-permute-start.19 = (bf16[272,512]{1,0:T(8,128)(2,1)S(1)}, bf16[272,512]{1,0:T(8,128)(2,1)S(1)}, u32[]{:S(2)}, u32[]{:S(2)}) collective-permute-start(bf16[272,512]{1,0:T(8,128)(2,1)S(1)} %pack_text.1.refs_0_), channel_id=1, source_target_pairs={{0,16},{8,24},{16,0},{24,8},{1,17},{9,25},{17,1},{25,9},{2,18},{10... | collective-permute-start | bytes 835592 | tf_op jit(solution)/shard_map/ppermute | solution.py:20
  60.7 14.1 %collective-permute-start.18 = (bf16[272,512]{1,0:T(8,128)(2,1)S(1)}, bf16[272,512]{1,0:T(8,128)(2,1)S(1)}, u32[]{:S(2)}, u32[]{:S(2)}) collective-permute-start(bf16[272,512]{1,0:T(8,128)(2,1)S(1)} %get-tuple-element.68), channel_id=1, source_target_pairs={{0,8},{8,0},{16,24},{24,16},{1,9},{9,1},{17,25},{25,17},{2,10},{10... | collective-permute-start | bytes 835592 | tf_op jit(solution)/shard_map/ppermute | solution.py:20
  63.5 13.1 %collective-permute-start.17 = (bf16[272,512]{1,0:T(8,128)(2,1)S(1)}, bf16[272,512]{1,0:T(8,128)(2,1)S(1)}, u32[]{:S(2)}, u32[]{:S(2)}) collective-permute-start(bf16[272,512]{1,0:T(8,128)(2,1)S(1)} %get-tuple-element.66), channel_id=1, source_target_pairs={{0,2},{1,3},{2,0},{3,1},{4,6},{5,7},{6,4},{7,5},{8,10},{9,11},{10,... | collective-permute-start | bytes 835592 | tf_op jit(solution)/shard_map/ppermute | solution.py:20
  65.1 14.1 %collective-permute-start.20 = (bf16[272,512]{1,0:T(8,128)(2,1)S(1)}, bf16[272,512]{1,0:T(8,128)(2,1)S(1)}, u32[]{:S(2)}, u32[]{:S(2)}) collective-permute-start(bf16[272,512]{1,0:T(8,128)(2,1)S(1)} %get-tuple-element.71), channel_id=1, source_target_pairs={{0,4},{1,5},{2,6},{3,7},{4,0},{5,1},{6,2},{7,3},{8,12},{9,13},{10,... | collective-permute-start | bytes 835592 | tf_op jit(solution)/shard_map/ppermute | solution.py:20
  66.7 12.5 %collective-permute-start.21 = (bf16[272,512]{1,0:T(8,128)(2,1)S(1)}, bf16[272,512]{1,0:T(8,128)(2,1)S(1)}, u32[]{:S(2)}, u32[]{:S(2)}) collective-permute-start(bf16[272,512]{1,0:T(8,128)(2,1)S(1)} %get-tuple-element.72), channel_id=1, source_target_pairs={{0,6},{1,7},{2,4},{3,5},{4,2},{5,3},{6,0},{7,1},{8,14},{9,15},{10,... | collective-permute-start | bytes 835592 | tf_op jit(solution)/shard_map/ppermute | solution.py:20

commit v15 on v14

--- a/solution.py
+++ b/solution.py
@@ -23,32 +23,35 @@
 def gather_both(image, text, n_col, n_row):
     images = [swap(image, "col", n_col, q) for q in range(2, n_col, 2)]
     texts = [swap(text, "row", n_row, q) for q in range(1, n_row - 1)]
-    texts.append(swap(texts[-1], "row", n_row, 1))
-    images, texts[:-1] = lax.optimization_barrier((images, texts[:-1]))
+    last = swap(texts[-1], "row", n_row, 1)
+    images, texts = lax.optimization_barrier((images, texts))
     odd = [swap(i, "col", n_col, 1) for i in (image, *images)]
-    return [image, *images], odd, [text, *texts]
+    return [image, *images], odd, [text, *texts], last
 
 
 def nt_dot(a, b):
     return lax.dot_general(a, b, (((1,), (1,)), ((), ())), preferred_element_type=jnp.float32)
 
 
-def stats_kernel(n_text, block, coef_ref, place_ref, *refs):
-    received, refs = refs[:n_text], refs[n_text:]
+def stats_kernel(first, n_text, block, coef_ref, place_ref, *refs):
+    texts, refs = refs[:n_text], refs[n_text:]
     coef = coef_ref[0, 0]
     r_place, c_place = place_ref[0, 0], place_ref[0, 1]
-    *refs, row_ref, col_ref, tile, row_max, col_max, col_sum, col_dot, row_diag = refs
-    *refs, even, odd = refs
-    pieces, texts = refs[:-n_text], refs[-n_text:]
-    for text, whole in zip(texts, received):
-        text[...] = whole[:block, :]
-    halves = (even, odd)
-    each = len(pieces) // 2
-    for i, piece in enumerate(pieces):
-        at = (i % each) * block
-        halves[i // each][at : at + block, :] = piece[...]
+    *refs, row_max, col_max, col_sum, col_dot, row_diag = refs
+    if first:
+        *refs, even, odd, row_ref, col_ref, tile = refs
+        halves = (even, odd)
+        each = len(refs) // 2
+        for i, piece in enumerate(refs):
+            at = (i % each) * block
+            halves[i // each][at : at + block, :] = piece[...]
+        before = None
+    else:
+        even, odd, *before, row_ref, col_ref, tile = refs
+        halves = (even, odd)
     cols, rows = tile.shape
     half = rows // 2
+    lead = 0 if first else col_ref.shape[1] - n_text
     col_max[...] = jnp.full(col_max.shape, -jnp.inf, jnp.float32)
     row_diag[...] = jnp.zeros(row_diag.shape, jnp.float32)
     n_col, n_row = row_ref.shape[1], col_ref.shape[1]
@@ -61,7 +64,7 @@
             top = None
             for t in range(n_text):
                 part = pl.ds(t * block, block)
-                x = nt_dot(texts[t][...], image) * coef
+                x = nt_dot(texts[t][:block, :], image) * coef
                 tile[part, pl.ds(at, block)] = x
                 top_t = jnp.max(x, axis=0, keepdims=True)
                 top = top_t if top is None else jnp.maximum(top, top_t)
@@ -75,7 +78,7 @@
         lax.fori_loop(0, half // block, products, 0, unroll=4)
 
     for t in range(n_text):
-        among = c_place * n_row + (r_place ^ t) - r_place * n_col
+        among = c_place * n_row + (r_place ^ (lead + t)) - r_place * n_col
 
         @pl.when((among >= 0) & (among < n_col))
         def _():
@@ -134,13 +137,15 @@
             )
         new.append(row_diag[0:1, at + (q % 2) * half : at + (q % 2) * half + block])
         placed = [jnp.where(here, n, p) for n, p in zip(new, placed)]
+    if before:
+        placed = merged(placed, [before[0][i] for i in range(4)])
     for i in range(4):
         row_ref[i] = placed[i]
     row_ids = lax.broadcasted_iota(jnp.int32, (n_row, block), 0)
-    placed = [jnp.zeros((n_row, block), jnp.float32)] * 3
+    placed = [before[1][i] if before else jnp.zeros((n_row, block), jnp.float32) for i in range(3)]
     for t in range(n_text):
         part = pl.ds(t * block, block)
-        here = row_ids == (r_place ^ t)
+        here = row_ids == (r_place ^ (lead + t))
         new = [col_max[part, :].T[0:1, :]]
         for which in (col_sum, col_dot):
             new.append(jnp.sum(which[part, :].T, axis=0, keepdims=True))
@@ -149,16 +154,17 @@
         col_ref[i] = placed[i]
 
 
-def stats(coef, place, texts, images, keep):
-    block, width = images[0].shape
-    rows, cols = block * len(images), block * len(texts)
+def stats(coef, place, texts, images, before, n_col, n_row, block, keep):
+    width = texts[0].shape[1]
+    first = not before
+    rows, cols = block * n_col, block * len(texts)
     vmem = pl.BlockSpec(memory_space=VMEM)
     smem = pl.BlockSpec(memory_space=SMEM)
-    out_shape = [jax.ShapeDtypeStruct((block, width), jnp.bfloat16)] * len(texts)
-    out_shape += [jax.ShapeDtypeStruct((rows // 2, width), jnp.bfloat16)] * 2
+    half = jax.ShapeDtypeStruct((rows // 2, width), jnp.bfloat16)
+    out_shape = [half, half] if first else []
     out_shape += [
-        jax.ShapeDtypeStruct((4, len(images), block), jnp.float32),
-        jax.ShapeDtypeStruct((3, len(texts), block), jnp.float32),
+        jax.ShapeDtypeStruct((4, n_col, block), jnp.float32),
+        jax.ShapeDtypeStruct((3, n_row, block), jnp.float32),
     ]
     scratch = [
         VMEM((8, rows), jnp.float32),
@@ -171,21 +177,20 @@
         out_shape.append(jax.ShapeDtypeStruct((cols, rows), jnp.float32))
     else:
         scratch.insert(0, VMEM((cols, rows), jnp.float32))
-    outs = pl.pallas_call(
-        functools.partial(stats_kernel, len(texts), block),
+    return pl.pallas_call(
+        functools.partial(stats_kernel, first, len(texts), block),
         out_shape=tuple(out_shape),
-        in_specs=[smem, smem] + [vmem] * (len(texts) + len(images)),
+        in_specs=[smem, smem] + [vmem] * (len(texts) + len(images) + len(before)),
         out_specs=(vmem,) * len(out_shape),
         scratch_shapes=scratch,
         compiler_params=pltpu.CompilerParams(
             vmem_limit_bytes=(0 if keep else 4 * rows * cols) + 8 * 2**20
         ),
         cost_estimate=pl.CostEstimate(
-            flops=FLOPS * 2 * rows * cols * width, bytes_accessed=0, transcendentals=0
+            flops=2 * rows * width, bytes_accessed=0, transcendentals=0
         ),
-        name="stats",
-    )(coef, place, *texts, *images)
-    return outs[: len(texts)], *outs[len(texts) : len(texts) + 4], outs[len(texts) + 4 :]
+        name="stats" if first else "stats_last",
+    )(coef, place, *texts, *images, *before)
 
 
 def merged(a, b):
@@ -433,13 +438,12 @@
     )(coef, base, *codes, *before)
 
 
-def text_block(text, tile, t, halves, row_lse, col_lse, place_ref, coef_ref, grad_ref):
+def text_block(block, text, tile, t, halves, row_lse, col_lse, place_ref, coef_ref, grad_ref):
     coef = coef_ref[0, 0]
     r_place, c_place = place_ref[0, 0], place_ref[0, 1]
     half, width = halves[0].shape
     n_col, n_row = row_lse.shape[0], col_lse.shape[0]
-    size = text.shape[0]
-    block = size
+    size = block
     col_lse_down = jnp.broadcast_to(col_lse[pl.ds(r_place ^ t, 1), :], (LANES, size)).T
     text_id = c_place * n_row + (r_place ^ t)
     step = 32
@@ -452,7 +456,7 @@
             at = pl.multiple_of(j * block + which * half, block)
             if tile is None:
                 image = images[pl.ds(pl.multiple_of(j * block, block), block), :]
-                xs = nt_dot(text[...], image) * coef
+                xs = nt_dot(text[:block, :], image) * coef
             column = c_place ^ (2 * j + which)
             same = jnp.where(r_place * n_col + column == text_id, 1.0, 0.0)
             lse = row_lse[pl.ds(column, 1), :]
@@ -479,7 +483,7 @@
     for grad, text in zip(grads, texts):
         part = lax.dot_general(
             grad[:, pl.ds(at, block)],
-            text[...],
+            text[:block, :],
             (((0,), (0,)), ((), ())),
             preferred_element_type=jnp.float32,
         )
@@ -499,8 +503,9 @@
     lowest = min(order)
     for i, t in enumerate(order):
         text_block(
+            block,
             texts[i],
-            tile.at[pl.ds(t * block, block)] if kept else None,
+            tile.at[pl.ds((t - lowest) * block, block)] if kept else None,
             t,
             (even, odd),
             row_lse,
@@ -546,7 +551,7 @@
 
 def text_grads(scale, coef, place, even, odd, row_lse, col_lse, row_extra, col_extra, texts, tile, order, done):
     half, width = even.shape
-    block = texts[0].shape[0]
+    block = row_lse.shape[1]
     n = len(order)
     vmem = pl.BlockSpec(memory_space=VMEM)
     smem = pl.BlockSpec(memory_space=SMEM)
@@ -592,14 +597,21 @@
     coef = scale * LOG2E
     image_half = image_embeds.astype(jnp.bfloat16)
     text_half = jnp.pad(text_embeds.astype(jnp.bfloat16), ((0, 16), (0, 0)))
-    even, odd, texts = gather_both(image_half, text_half, n_col, n_row)
+    even, odd, texts, text_last = gather_both(image_half, text_half, n_col, n_row)
     keep = 4 * n_row * n_col * block * block <= 16 * 2**20
-    texts, even, odd, row_parts, col_parts, tile = stats(coef, place, texts, (*even, *odd), keep)
+    even, odd, *before = stats(
+        coef, place, texts, (*even, *odd), (), n_col, n_row, block, keep
+    )
+    row_parts, col_parts, *tile_last = stats(
+        coef, place, [text_last], (even, odd), before[:2], n_col, n_row, block, keep
+    )
+    texts = [*texts, text_last]
+    tile = before[2:]
     row_lse, row_extra, col_lse, col_extra = exchanged(row_parts, col_parts, n_col, n_row)
 
     held = (scale, coef, place, even, odd, row_lse, col_lse, row_extra, col_extra, texts)
     last = n_row - 1
-    last_grad, parts, _ = text_grads(*held, tile, [last], [])
+    last_grad, parts, _ = text_grads(*held, tile_last, [last], [])
     received = swap(parts[last], "row", n_row, 1)
     _, more_parts, (far, near) = text_grads(*held, tile, list(range(last))[::-1], [(last, last_grad)])
     parts |= more_parts

time: 81.5 us -> 77.5 us (0.951)
  starting transfers between devices: 25.1 us -> 22.7 us
  waiting for transfers between devices: 30.8 us -> 28.5 us
    ppermute x22, waiting for transfers between devices: 30.8 us -> 28.5 us  [swap(): return lax.ppermute(x, axis, [(i, i ^ q) for i in range(n)])]
    ppermute x22, starting transfers between devices: 25.1 us -> 22.7 us  [swap(): return lax.ppermute(x, axis, [(i, i ^ q) for i in range(n)])]
    pallas_call x1 -> x2, Pallas kernels: 7.15 us -> 7.92 us  [stats(): pl.pallas_call(functools.partial(stats_kernel, first, len(texts), block),...]
  transfers between devices with their start and end apart: 22 -> 22, of which waited for: 15 -> 15; matrix products, arithmetic and copies ran while one was open for 1% -> 2% of each run, Pallas kernels for 13% -> 20%
where the time goes in v15:
time: 77.5 us; the launch traced here: 77.3 us
  waiting for transfers between devices  28.5 us (37%)
  starting transfers between devices  22.7 us (29%)
  Pallas kernels  22 us (28%)
  other arithmetic  2.42 us (3%)
  between operations  1.61 us (2%)
    ppermute x22, waiting for transfers between devices, swap(): return lax.ppermute(x, axis, [(i, i ^ q) for i in range(n)])  28.5 us
    ppermute x22, starting transfers between devices, swap(): return lax.ppermute(x, axis, [(i, i ^ q) for i in range(n)])  22.7 us
    pallas_call x2, Pallas kernels, text_grads(): pl.pallas_call(functools.partial(text_kernel, tuple(order), len(done), le...  8.16 us
    pallas_call x2, Pallas kernels, stats(): pl.pallas_call(functools.partial(stats_kernel, first, len(texts), block),...  7.92 us
    pallas_call x2, Pallas kernels, total_of(): pl.pallas_call(functools.partial(total_kernel, len(codes), in_order), out...  3.78 us
  transfers between devices with their start and end apart: 22, of which 15 were waited for; matrix products, arithmetic and copies ran while one was open for 2% of the time, Pallas kernels for 20%

profile of v15, /device:TPU:0, one launch (start us, length us, event | category | flops | bytes accessed | tf_op | source)
XLA Modules:
  0.0 77.3 jit_solution(12014200432824767094)
XLA Ops:
  0.6 1.1 %convert_element_type.8 = bf16[256,512]{1,0:T(8,128)(2,1)S(1)} convert(f32[256,512]{1,0:T(8,128)} %param.4) | non-fusion elementwise | flops 131072 | bytes 786432 | tf_op jit(solution)/shard_map/convert_element_type | solution.py:599
  1.7 4.1 %collective-permute-start.4 = (bf16[272,512]{1,0:T(8,128)(2,1)S(1)}, bf16[272,512]{1,0:T(8,128)(2,1)S(1)}, u32[]{:S(2)}, u32[]{:S(2)}) collective-permute-start(bf16[272,512]{1,0:T(8,128)(2,1)S(1)} %pad.4.refs_0_.refs_8_), channel_id=1, source_target_pairs={{0,16},{8,24},{16,0},{24,8},{1,17},{9,25},{17,1},{25,9},{2,18},{10... | collective-permute-start | bytes 835592 | tf_op jit(solution)/shard_map/ppermute | solution.py:20
  5.8 1.6 %collective-permute-start.3 = (bf16[272,512]{1,0:T(8,128)(2,1)S(1)}, bf16[272,512]{1,0:T(8,128)(2,1)S(1)}, u32[]{:S(2)}, u32[]{:S(2)}) collective-permute-start(bf16[272,512]{1,0:T(8,128)(2,1)S(1)} %pad.4.refs_0_.refs_8_), channel_id=1, source_target_pairs={{0,8},{8,0},{16,24},{24,16},{1,9},{9,1},{17,25},{25,17},{2,10},{10... | collective-permute-start | bytes 835592 | tf_op jit(solution)/shard_map/ppermute | solution.py:20
  7.4 1.1 %convert_element_type.9.refs_3_ = bf16[256,512]{1,0:T(8,128)(2,1)S(1)} convert(f32[256,512]{1,0:T(8,128)} %param.3) | non-fusion elementwise | flops 131072 | bytes 786432 | tf_op jit(solution)/shard_map/convert_element_type | solution.py:598
  8.5 2.5 %collective-permute-start.2 = (bf16[256,512]{1,0:T(8,128)(2,1)S(1)}, bf16[256,512]{1,0:T(8,128)(2,1)S(1)}, u32[]{:S(2)}, u32[]{:S(2)}) collective-permute-start(bf16[256,512]{1,0:T(8,128)(2,1)S(1)} %convert_element_type.9.refs_3_), channel_id=1, source_target_pairs={{0,6},{1,7},{2,4},{3,5},{4,2},{5,3},{6,0},{7,1},{8,14},{9,15},{10,... | collective-permute-start | bytes 786440 | tf_op jit(solution)/shard_map/ppermute | solution.py:20
  12.0 6.5 %collective-permute-done.4.refs_2_.refs_6_ = bf16[272,512]{1,0:T(8,128)(2,1)S(1)} collective-permute-done((bf16[272,512]{1,0:T(8,128)(2,1)S(1)}, bf16[272,512]{1,0:T(8,128)(2,1)S(1)}, u32[]{:S(2)}, u32[]{:S(2)}) %collective-permute-start.4) | collective-permute-done | bytes 278560 | tf_op jit(solution)/shard_map/ppermute | solution.py:20
  18.6 0.6 collective-permute-start.9
  19.2 3.4 %collective-permute-done.1.refs_5_ = bf16[256,512]{1,0:T(8,128)(2,1)S(1)} collective-permute-done((bf16[256,512]{1,0:T(8,128)(2,1)S(1)}, bf16[256,512]{1,0:T(8,128)(2,1)S(1)}, u32[]{:S(2)}, u32[]{:S(2)}) %collective-permute-start.1) | collective-permute-done | bytes 262176 | tf_op jit(solution)/shard_map/ppermute | solution.py:20
  25.0 5.3 %stats.1 = (bf16[1024,512]{1,0:T(8,128)(2,1)S(1)}, bf16[1024,512]{1,0:T(8,128)(2,1)S(1)}, f32[4,8,256]{2,1,0:T(8,128)S(1)}, f32[3,4,256]{2,1,0:T(4,128)S(1)}, f32[768,2048]{1,0:T(8,128)S(1)}) custom-call(f32[1,1]{1,0:T(1,128)S(6)} %mul.127.coef_ref, s32[1,2]{1,0:T(1,128)S(1)} %add_bitcast_fusion.place_ref, bf16[272,512]{1,0:T(8,128)(2,1)S(1)} %pad.4.refs_0_.refs_8_, ...), custom_call_target="tpu_custom_call" | custom-call | flops 2097152 | tf_op jit(solution)/shard_map/stats/pallas_call | solution.py:180
  30.3 2.6 %stats_last.1 = (f32[4,8,256]{2,1,0:T(8,128)S(1)}, f32[3,4,256]{2,1,0:T(4,128)S(1)}, f32[256,2048]{1,0:T(8,128)S(1)}) custom-call(f32[1,1]{1,0:T(1,128)S(6)} %mul.127.coef_ref, s32[1,2]{1,0:T(1,128)S(1)} %add_bitcast_fusion.place_ref, bf16[272,512]{1,0:T(8,128)(2,1)S(1)} %collective-permute-done.9.refs_0_.refs_6_.refs_11_, ...), custom_call_target="tpu_custom_call" | custom-call | flops 2097152 | tf_op jit(solution)/shard_map/stats_last/pallas_call | solution.py:180
  33.3 1.6 %collective-permute-start.10 = (f32[4,8,256]{2,1,0:T(8,128)S(1)}, f32[4,8,256]{2,1,0:T(8,128)S(1)}, u32[]{:S(2)}, u32[]{:S(2)}) collective-permute-start(f32[4,8,256]{2,1,0:T(8,128)S(1)} %get-tuple-element.48), channel_id=1, source_target_pairs={{0,2},{1,3},{2,0},{3,1},{4,6},{5,7},{6,4},{7,5},{8,10},{9,11},{10,... | collective-permute-start | bytes 98312 | tf_op jit(solution)/shard_map/ppermute | solution.py:20
  34.9 2.3 %collective-permute-done.10 = f32[4,8,256]{2,1,0:T(8,128)S(1)} collective-permute-done((f32[4,8,256]{2,1,0:T(8,128)S(1)}, f32[4,8,256]{2,1,0:T(8,128)S(1)}, u32[]{:S(2)}, u32[]{:S(2)}) %collective-permute-start.10) | collective-permute-done | bytes 32800 | tf_op jit(solution)/shard_map/ppermute | solution.py:20
  37.9 1.5 %collective-permute-start.12 = (f32[4,8,256]{2,1,0:T(8,128)S(1)}, f32[4,8,256]{2,1,0:T(8,128)S(1)}, u32[]{:S(2)}, u32[]{:S(2)}) collective-permute-start(f32[4,8,256]{2,1,0:T(8,128)S(1)} %pad_maximum_fusion.1), channel_id=1, source_target_pairs={{0,4},{1,5},{2,6},{3,7},{4,0},{5,1},{6,2},{7,3},{8,12},{9,13},{10,... | collective-permute-start | bytes 98312 | tf_op jit(solution)/shard_map/ppermute | solution.py:20
  39.4 2.4 %collective-permute-done.12 = f32[4,8,256]{2,1,0:T(8,128)S(1)} collective-permute-done((f32[4,8,256]{2,1,0:T(8,128)S(1)}, f32[4,8,256]{2,1,0:T(8,128)S(1)}, u32[]{:S(2)}, u32[]{:S(2)}) %collective-permute-start.12) | collective-permute-done | bytes 32800 | tf_op jit(solution)/shard_map/ppermute | solution.py:20
  42.5 1.2 %collective-permute-done.14 = f32[4,8,256]{2,1,0:T(8,128)S(1)} collective-permute-done((f32[4,8,256]{2,1,0:T(8,128)S(1)}, f32[4,8,256]{2,1,0:T(8,128)S(1)}, u32[]{:S(2)}, u32[]{:S(2)}) %collective-permute-start.14) | collective-permute-done | bytes 32800 | tf_op jit(solution)/shard_map/ppermute | solution.py:20
  43.7 1.8 %text_grads_1.1 = (bf16[256,2048]{1,0:T(8,128)(2,1)S(1)}, bf16[272,512]{1,0:T(8,128)(2,1)S(1)}) custom-call(f32[1,1]{1,0:T(1,128)} %bitcast.241.scale_ref, f32[1,1]{1,0:T(1,128)S(6)} %mul.127.coef_ref, s32[1,2]{1,0:T(1,128)S(1)} %add_bitcast_fusion.place_ref, bf16[1024,512]{1,0:T(8,128)(2,1)S(1)} %get-tuple-element.44.refs_1_.refs_0_, ...), custom_call_target="tpu_custom_call" | custom-call | flops 21474836480 | tf_op jit(solution)/shard_map/text_grads_1/pallas_call | solution.py:572
  45.5 1.8 %collective-permute-start.16 = (bf16[272,512]{1,0:T(8,128)(2,1)S(1)}, bf16[272,512]{1,0:T(8,128)(2,1)S(1)}, u32[]{:S(2)}, u32[]{:S(2)}) collective-permute-start(bf16[272,512]{1,0:T(8,128)(2,1)S(1)} %get-tuple-element.62), channel_id=1, source_target_pairs={{0,8},{8,0},{16,24},{24,16},{1,9},{9,1},{17,25},{25,17},{2,10},{10... | collective-permute-start | bytes 835592 | tf_op jit(solution)/shard_map/ppermute | solution.py:20
  47.3 6.4 %text_grads_3.1 = (bf16[768,2048]{1,0:T(8,128)(2,1)}, f32[264,512]{1,0:T(8,128)S(1)}, bf16[272,512]{1,0:T(8,128)(2,1)S(1)}, f32[264,512]{1,0:T(8,128)S(1)}, f32[...) custom-call(f32[1,1]{1,0:T(1,128)} %bitcast.242.scale_ref, f32[1,1]{1,0:T(1,128)S(6)} %mul.127.coef_ref, ...), custom_call_target="tpu_custom_call" | custom-call | flops 64424509440 | tf_op jit(solution)/shard_map/text_grads_3/pallas_call | solution.py:572
  53.7 0.6 collective-permute-done.16.refs_0_
  54.3 0.7 pack_text.1.refs_0_
  55.0 2.0 %collective-permute-start.19 = (bf16[272,512]{1,0:T(8,128)(2,1)S(1)}, bf16[272,512]{1,0:T(8,128)(2,1)S(1)}, u32[]{:S(2)}, u32[]{:S(2)}) collective-permute-start(bf16[272,512]{1,0:T(8,128)(2,1)S(1)} %pack_text.1.refs_0_), channel_id=1, source_target_pairs={{0,16},{8,24},{16,0},{24,8},{1,17},{9,25},{17,1},{25,9},{2,18},{10... | collective-permute-start | bytes 835592 | tf_op jit(solution)/shard_map/ppermute | solution.py:20
  57.0 0.9 %collective-permute-done.15.far = f32[4,264,512]{2,1,0:T(8,128)S(1)} collective-permute-done((f32[4,264,512]{2,1,0:T(8,128)S(1)}, f32[4,264,512]{2,1,0:T(8,128)S(1)}, u32[]{:S(2)}, u32[]{:S(2)}) %collective-permute-start.15) | collective-permute-done | bytes 2162720 | tf_op jit(solution)/shard_map/ppermute | solution.py:20
  57.9 0.8 %collective-permute-start.18 = (bf16[272,512]{1,0:T(8,128)(2,1)S(1)}, bf16[272,512]{1,0:T(8,128)(2,1)S(1)}, u32[]{:S(2)}, u32[]{:S(2)}) collective-permute-start(bf16[272,512]{1,0:T(8,128)(2,1)S(1)} %get-tuple-element.66), channel_id=1, source_target_pairs={{0,8},{8,0},{16,24},{24,16},{1,9},{9,1},{17,25},{25,17},{2,10},{10... | collective-permute-start | bytes 835592 | tf_op jit(solution)/shard_map/ppermute | solution.py:20
  58.7 1.1 %pack_images.1 = (f32[264,512]{1,0:T(8,128)S(1)}, bf16[272,512]{1,0:T(8,128)(2,1)S(1)}, bf16[272,512]{1,0:T(8,128)(2,1)S(1)}, bf16[272,512]{1,0:T(8,128)(2,1)S(1)}) custom-call(f32[4,264,512]{2,1,0:T(8,128)S(1)} %get-tuple-element.57.near, f32[4,264,512]{2,1,0:T(8,128)S(1)} %collective-permute-done.15.far, bf16[272,512]{1,0:T(8,128)(2,1)S(1)} %pack_text.1.refs_0_), custom_call_target="tpu_custom_call" | custom-call | flops 21474836480 | tf_op jit(solution)/shard_map/pack_images/pallas_call | solution.py:349
  59.9 1.4 %collective-permute-start.17 = (bf16[272,512]{1,0:T(8,128)(2,1)S(1)}, bf16[272,512]{1,0:T(8,128)(2,1)S(1)}, u32[]{:S(2)}, u32[]{:S(2)}) collective-permute-start(bf16[272,512]{1,0:T(8,128)(2,1)S(1)} %get-tuple-element.64), channel_id=1, source_target_pairs={{0,2},{1,3},{2,0},{3,1},{4,6},{5,7},{6,4},{7,5},{8,10},{9,11},{10,... | collective-permute-start | bytes 835592 | tf_op jit(solution)/shard_map/ppermute | solution.py:20
  61.3 0.7 collective-permute-start.20
  62.0 1.4 %collective-permute-start.21 = (bf16[272,512]{1,0:T(8,128)(2,1)S(1)}, bf16[272,512]{1,0:T(8,128)(2,1)S(1)}, u32[]{:S(2)}, u32[]{:S(2)}) collective-permute-start(bf16[272,512]{1,0:T(8,128)(2,1)S(1)} %get-tuple-element.70), channel_id=1, source_target_pairs={{0,6},{1,7},{2,4},{3,5},{4,2},{5,3},{6,0},{7,1},{8,14},{9,15},{10,... | collective-permute-start | bytes 835592 | tf_op jit(solution)/shard_map/ppermute | solution.py:20
  63.4 7.1 %collective-permute-done.19.refs_1_ = bf16[272,512]{1,0:T(8,128)(2,1)S(1)} collective-permute-done((bf16[272,512]{1,0:T(8,128)(2,1)S(1)}, bf16[272,512]{1,0:T(8,128)(2,1)S(1)}, u32[]{:S(2)}, u32[]{:S(2)}) %collective-permute-start.19) | collective-permute-done | bytes 278560 | tf_op jit(solution)/shard_map/ppermute | solution.py:20
  70.5 1.5 %collective-permute-done.18.refs_0_ = bf16[272,512]{1,0:T(8,128)(2,1)S(1)} collective-permute-done((bf16[272,512]{1,0:T(8,128)(2,1)S(1)}, bf16[272,512]{1,0:T(8,128)(2,1)S(1)}, u32[]{:S(2)}, u32[]{:S(2)}) %collective-permute-start.18) | collective-permute-done | bytes 278560 | tf_op jit(solution)/shard_map/ppermute | solution.py:20
  72.0 1.8 %grad_text.1 = (f32[256,512]{1,0:T(8,128)}, f32[8,256]{1,0:T(8,128)S(1)}, f32[1,1]{1,0:T(1,128)}) custom-call(f32[1,1]{1,0:T(1,128)S(6)} %mul.127.coef_ref, f32[264,512]{1,0:T(8,128)S(1)} %get-tuple-element.65.base, bf16[272,512]{1,0:T(8,128)(2,1)S(1)} %collective-permute-done.18.refs_0_, bf16[272,512]{1,0:T(8,128)(2,1)S(1)} %collective-permute-done.19.refs_1_), custom_call_target="tpu_custom_call" | custom-call | tf_op jit(solution)/shard_map/grad_text/pallas_call | solution.py:422
  74.1 1.0 %collective-permute-done.20.refs_0_ = bf16[272,512]{1,0:T(8,128)(2,1)S(1)} collective-permute-done((bf16[272,512]{1,0:T(8,128)(2,1)S(1)}, bf16[272,512]{1,0:T(8,128)(2,1)S(1)}, u32[]{:S(2)}, u32[]{:S(2)}) %collective-permute-start.20) | collective-permute-done | bytes 278560 | tf_op jit(solution)/shard_map/ppermute | solution.py:20
  75.2 1.9 %grad_image.1 = (f32[256,512]{1,0:T(8,128)}, f32[8,256]{1,0:T(8,128)}, f32[1,1]{1,0:T(1,128)}) custom-call(f32[1,1]{1,0:T(1,128)S(6)} %mul.127.coef_ref, f32[264,512]{1,0:T(8,128)S(1)} %added.1.base, bf16[272,512]{1,0:T(8,128)(2,1)S(1)} %collective-permute-done.20.refs_0_, bf16[272,512]{1,0:T(8,128)(2,1)S(1)} %collective-permute-done.21.refs_1_, ...), custom_call_target="tpu_custom_call" | custom-call | tf_op jit(solution)/shard_map/grad_image/pallas_call | solution.py:422
  (44 shorter events, 4.9 us)
Async XLA Ops:
  1.7 16.8 %collective-permute-start.4 = (bf16[272,512]{1,0:T(8,128)(2,1)S(1)}, bf16[272,512]{1,0:T(8,128)(2,1)S(1)}, u32[]{:S(2)}, u32[]{:S(2)}) collective-permute-start(bf16[272,512]{1,0:T(8,128)(2,1)S(1)} %pad.4.refs_0_.refs_8_), channel_id=1, source_target_pairs={{0,16},{8,24},{16,0},{24,8},{1,17},{9,25},{17,1},{25,9},{2,18},{10... | collective-permute-start | bytes 835592 | tf_op jit(solution)/shard_map/ppermute | solution.py:20
  5.8 16.8 %collective-permute-start.3 = (bf16[272,512]{1,0:T(8,128)(2,1)S(1)}, bf16[272,512]{1,0:T(8,128)(2,1)S(1)}, u32[]{:S(2)}, u32[]{:S(2)}) collective-permute-start(bf16[272,512]{1,0:T(8,128)(2,1)S(1)} %pad.4.refs_0_.refs_8_), channel_id=1, source_target_pairs={{0,8},{8,0},{16,24},{24,16},{1,9},{9,1},{17,25},{25,17},{2,10},{10... | collective-permute-start | bytes 835592 | tf_op jit(solution)/shard_map/ppermute | solution.py:20
  8.5 10.7 %collective-permute-start.2 = (bf16[256,512]{1,0:T(8,128)(2,1)S(1)}, bf16[256,512]{1,0:T(8,128)(2,1)S(1)}, u32[]{:S(2)}, u32[]{:S(2)}) collective-permute-start(bf16[256,512]{1,0:T(8,128)(2,1)S(1)} %convert_element_type.9.refs_3_), channel_id=1, source_target_pairs={{0,6},{1,7},{2,4},{3,5},{4,2},{5,3},{6,0},{7,1},{8,14},{9,15},{10,... | collective-permute-start | bytes 786440 | tf_op jit(solution)/shard_map/ppermute | solution.py:20
  11.0 11.6 %collective-permute-start.1 = (bf16[256,512]{1,0:T(8,128)(2,1)S(1)}, bf16[256,512]{1,0:T(8,128)(2,1)S(1)}, u32[]{:S(2)}, u32[]{:S(2)}) collective-permute-start(bf16[256,512]{1,0:T(8,128)(2,1)S(1)} %convert_element_type.9.refs_3_), channel_id=1, source_target_pairs={{0,4},{1,5},{2,6},{3,7},{4,0},{5,1},{6,2},{7,3},{8,12},{9,13},{10,... | collective-permute-start | bytes 786440 | tf_op jit(solution)/shard_map/ppermute | solution.py:20
  11.5 11.1 %collective-permute-start = (bf16[256,512]{1,0:T(8,128)(2,1)S(1)}, bf16[256,512]{1,0:T(8,128)(2,1)S(1)}, u32[]{:S(2)}, u32[]{:S(2)}) collective-permute-start(bf16[256,512]{1,0:T(8,128)(2,1)S(1)} %convert_element_type.9.refs_3_), channel_id=1, source_target_pairs={{0,2},{1,3},{2,0},{3,1},{4,6},{5,7},{6,4},{7,5},{8,10},{9,11},{10,... | collective-permute-start | bytes 786440 | tf_op jit(solution)/shard_map/ppermute | solution.py:20
  18.6 11.7 %collective-permute-start.9 = (bf16[272,512]{1,0:T(8,128)(2,1)S(1)}, bf16[272,512]{1,0:T(8,128)(2,1)S(1)}, u32[]{:S(2)}, u32[]{:S(2)}) collective-permute-start(bf16[272,512]{1,0:T(8,128)(2,1)S(1)} %collective-permute-done.4.refs_2_.refs_6_), channel_id=1, source_target_pairs={{0,8},{8,0},{16,24},{24,16},{1,9},{9,1},{17,25},{25,17},{2,10},{10... | collective-permute-start | bytes 835592 | tf_op jit(solution)/shard_map/ppermute | solution.py:20
  19.2 4.7 %collective-permute-start.5 = (bf16[256,512]{1,0:T(8,128)(2,1)S(1)}, bf16[256,512]{1,0:T(8,128)(2,1)S(1)}, u32[]{:S(2)}, u32[]{:S(2)}) collective-permute-start(bf16[256,512]{1,0:T(8,128)(2,1)S(1)} %convert_element_type.9.refs_3_), channel_id=1, source_target_pairs={{0,1},{1,0},{2,3},{3,2},{4,5},{5,4},{6,7},{7,6},{8,9},{9,8},{10,11... | collective-permute-start | bytes 786440 | tf_op jit(solution)/shard_map/ppermute | solution.py:20
  22.7 1.5 %collective-permute-start.6 = (bf16[256,512]{1,0:T(8,128)(2,1)S(1)}, bf16[256,512]{1,0:T(8,128)(2,1)S(1)}, u32[]{:S(2)}, u32[]{:S(2)}) collective-permute-start(bf16[256,512]{1,0:T(8,128)(2,1)S(1)} %collective-permute-done.refs_4_), channel_id=1, source_target_pairs={{0,1},{1,0},{2,3},{3,2},{4,5},{5,4},{6,7},{7,6},{8,9},{9,8},{10,11... | collective-permute-start | bytes 786440 | tf_op jit(solution)/shard_map/ppermute | solution.py:20
  22.7 1.9 %collective-permute-start.7 = (bf16[256,512]{1,0:T(8,128)(2,1)S(1)}, bf16[256,512]{1,0:T(8,128)(2,1)S(1)}, u32[]{:S(2)}, u32[]{:S(2)}) collective-permute-start(bf16[256,512]{1,0:T(8,128)(2,1)S(1)} %collective-permute-done.1.refs_5_), channel_id=1, source_target_pairs={{0,1},{1,0},{2,3},{3,2},{4,5},{5,4},{6,7},{7,6},{8,9},{9,8},{10,11... | collective-permute-start | bytes 786440 | tf_op jit(solution)/shard_map/ppermute | solution.py:20
  23.2 1.8 %collective-permute-start.8 = (bf16[256,512]{1,0:T(8,128)(2,1)S(1)}, bf16[256,512]{1,0:T(8,128)(2,1)S(1)}, u32[]{:S(2)}, u32[]{:S(2)}) collective-permute-start(bf16[256,512]{1,0:T(8,128)(2,1)S(1)} %collective-permute-done.2.refs_6_), channel_id=1, source_target_pairs={{0,1},{1,0},{2,3},{3,2},{4,5},{5,4},{6,7},{7,6},{8,9},{9,8},{10,11... | collective-permute-start | bytes 786440 | tf_op jit(solution)/shard_map/ppermute | solution.py:20
  32.9 4.3 %collective-permute-start.11 = (f32[9,4,256]{2,1,0:T(4,128)S(1)}, f32[9,4,256]{2,1,0:T(4,128)S(1)}, u32[]{:S(2)}, u32[]{:S(2)}) collective-permute-start(f32[9,4,256]{2,1,0:T(4,128)S(1)} %pad_maximum_fusion), channel_id=1, source_target_pairs={{0,8},{8,0},{16,24},{24,16},{1,9},{9,1},{17,25},{25,17},{2,10},{10... | collective-permute-start | bytes 110600 | tf_op jit(solution)/shard_map/ppermute | solution.py:20
  33.3 3.9 %collective-permute-start.10 = (f32[4,8,256]{2,1,0:T(8,128)S(1)}, f32[4,8,256]{2,1,0:T(8,128)S(1)}, u32[]{:S(2)}, u32[]{:S(2)}) collective-permute-start(f32[4,8,256]{2,1,0:T(8,128)S(1)} %get-tuple-element.48), channel_id=1, source_target_pairs={{0,2},{1,3},{2,0},{3,1},{4,6},{5,7},{6,4},{7,5},{8,10},{9,11},{10,... | collective-permute-start | bytes 98312 | tf_op jit(solution)/shard_map/ppermute | solution.py:20
  37.4 4.9 %collective-permute-start.13 = (f32[9,4,256]{2,1,0:T(4,128)S(1)}, f32[9,4,256]{2,1,0:T(4,128)S(1)}, u32[]{:S(2)}, u32[]{:S(2)}) collective-permute-start(f32[9,4,256]{2,1,0:T(4,128)S(1)} %constant_dynamic-update-slice_fusion), channel_id=1, source_target_pairs={{0,16},{8,24},{16,0},{24,8},{1,17},{9,25},{17,1},{25,9},{2,18},{10... | collective-permute-start | bytes 110600 | tf_op jit(solution)/shard_map/ppermute | solution.py:20
  37.9 3.9 %collective-permute-start.12 = (f32[4,8,256]{2,1,0:T(8,128)S(1)}, f32[4,8,256]{2,1,0:T(8,128)S(1)}, u32[]{:S(2)}, u32[]{:S(2)}) collective-permute-start(f32[4,8,256]{2,1,0:T(8,128)S(1)} %pad_maximum_fusion.1), channel_id=1, source_target_pairs={{0,4},{1,5},{2,6},{3,7},{4,0},{5,1},{6,2},{7,3},{8,12},{9,13},{10,... | collective-permute-start | bytes 98312 | tf_op jit(solution)/shard_map/ppermute | solution.py:20
  42.4 1.3 %collective-permute-start.14 = (f32[4,8,256]{2,1,0:T(8,128)S(1)}, f32[4,8,256]{2,1,0:T(8,128)S(1)}, u32[]{:S(2)}, u32[]{:S(2)}) collective-permute-start(f32[4,8,256]{2,1,0:T(8,128)S(1)} %pad_maximum_fusion.2), channel_id=1, source_target_pairs={{0,1},{1,0},{2,3},{3,2},{4,5},{5,4},{6,7},{7,6},{8,9},{9,8},{10,11... | collective-permute-start | bytes 98312 | tf_op jit(solution)/shard_map/ppermute | solution.py:20
  45.5 8.8 %collective-permute-start.16 = (bf16[272,512]{1,0:T(8,128)(2,1)S(1)}, bf16[272,512]{1,0:T(8,128)(2,1)S(1)}, u32[]{:S(2)}, u32[]{:S(2)}) collective-permute-start(bf16[272,512]{1,0:T(8,128)(2,1)S(1)} %get-tuple-element.62), channel_id=1, source_target_pairs={{0,8},{8,0},{16,24},{24,16},{1,9},{9,1},{17,25},{25,17},{2,10},{10... | collective-permute-start | bytes 835592 | tf_op jit(solution)/shard_map/ppermute | solution.py:20
  53.6 4.3 %collective-permute-start.15 = (f32[4,264,512]{2,1,0:T(8,128)S(1)}, f32[4,264,512]{2,1,0:T(8,128)S(1)}, u32[]{:S(2)}, u32[]{:S(2)}) collective-permute-start(f32[4,264,512]{2,1,0:T(8,128)S(1)} %get-tuple-element.59), channel_id=1, source_target_pairs={{0,1},{1,0},{2,3},{3,2},{4,5},{5,4},{6,7},{7,6},{8,9},{9,8},{10,11... | collective-permute-start | bytes 6488072 | tf_op jit(solution)/shard_map/ppermute | solution.py:20
  55.0 15.5 %collective-permute-start.19 = (bf16[272,512]{1,0:T(8,128)(2,1)S(1)}, bf16[272,512]{1,0:T(8,128)(2,1)S(1)}, u32[]{:S(2)}, u32[]{:S(2)}) collective-permute-start(bf16[272,512]{1,0:T(8,128)(2,1)S(1)} %pack_text.1.refs_0_), channel_id=1, source_target_pairs={{0,16},{8,24},{16,0},{24,8},{1,17},{9,25},{17,1},{25,9},{2,18},{10... | collective-permute-start | bytes 835592 | tf_op jit(solution)/shard_map/ppermute | solution.py:20
  57.9 14.0 %collective-permute-start.18 = (bf16[272,512]{1,0:T(8,128)(2,1)S(1)}, bf16[272,512]{1,0:T(8,128)(2,1)S(1)}, u32[]{:S(2)}, u32[]{:S(2)}) collective-permute-start(bf16[272,512]{1,0:T(8,128)(2,1)S(1)} %get-tuple-element.66), channel_id=1, source_target_pairs={{0,8},{8,0},{16,24},{24,16},{1,9},{9,1},{17,25},{25,17},{2,10},{10... | collective-permute-start | bytes 835592 | tf_op jit(solution)/shard_map/ppermute | solution.py:20
  59.9 14.0 %collective-permute-start.17 = (bf16[272,512]{1,0:T(8,128)(2,1)S(1)}, bf16[272,512]{1,0:T(8,128)(2,1)S(1)}, u32[]{:S(2)}, u32[]{:S(2)}) collective-permute-start(bf16[272,512]{1,0:T(8,128)(2,1)S(1)} %get-tuple-element.64), channel_id=1, source_target_pairs={{0,2},{1,3},{2,0},{3,1},{4,6},{5,7},{6,4},{7,5},{8,10},{9,11},{10,... | collective-permute-start | bytes 835592 | tf_op jit(solution)/shard_map/ppermute | solution.py:20
  61.3 13.9 %collective-permute-start.20 = (bf16[272,512]{1,0:T(8,128)(2,1)S(1)}, bf16[272,512]{1,0:T(8,128)(2,1)S(1)}, u32[]{:S(2)}, u32[]{:S(2)}) collective-permute-start(bf16[272,512]{1,0:T(8,128)(2,1)S(1)} %get-tuple-element.69), channel_id=1, source_target_pairs={{0,4},{1,5},{2,6},{3,7},{4,0},{5,1},{6,2},{7,3},{8,12},{9,13},{10,... | collective-permute-start | bytes 835592 | tf_op jit(solution)/shard_map/ppermute | solution.py:20
  62.0 13.1 %collective-permute-start.21 = (bf16[272,512]{1,0:T(8,128)(2,1)S(1)}, bf16[272,512]{1,0:T(8,128)(2,1)S(1)}, u32[]{:S(2)}, u32[]{:S(2)}) collective-permute-start(bf16[272,512]{1,0:T(8,128)(2,1)S(1)} %get-tuple-element.70), channel_id=1, source_target_pairs={{0,6},{1,7},{2,4},{3,5},{4,2},{5,3},{6,0},{7,1},{8,14},{9,15},{10,... | collective-permute-start | bytes 835592 | tf_op jit(solution)/shard_map/ppermute | solution.py:20

commit v16 on v15

--- a/solution.py
+++ b/solution.py
@@ -478,17 +478,8 @@
         lax.fori_loop(0, half // block, one, 0, unroll=4)
 
 
-def image_block(grads, texts, at, block, scale):
-    total = None
-    for grad, text in zip(grads, texts):
-        part = lax.dot_general(
-            grad[:, pl.ds(at, block)],
-            text[:block, :],
-            (((0,), (0,)), ((), ())),
-            preferred_element_type=jnp.float32,
-        )
-        total = part if total is None else total + part
-    return scale * total
+def over_texts(grad, text):
+    return lax.dot_general(grad, text, (((0,), (0,)), ((), ())), preferred_element_type=jnp.float32)
 
 
 def text_kernel(order, n_done, kept, block, scale_ref, coef_ref, place_ref, *refs):
@@ -531,18 +522,18 @@
             put_extra(outs[i].at[block:, :], row_extra)
     if n_done:
         far_ref, near_ref = rest[:2]
-        by_text = {t: (grads.at[pl.ds((t - lowest) * block, block)], texts[i]) for i, t in enumerate(order)}
+        stacked = rest[-4]
+        for i, t in enumerate(order):
+            stacked[(t - lowest) * block : (t - lowest + 1) * block, :] = texts[i][:block, :]
 
         for images_ref, first in ((far_ref, half), (near_ref, 0)):
 
             def one(j, carry):
-                images_ref[j, :block, :] = image_block(
-                    [*done_grads, *[by_text[t][0] for t in order]],
-                    [*done_texts, *[by_text[t][1] for t in order]],
-                    pl.multiple_of(j * block + first, block),
-                    block,
-                    scale,
-                )
+                part = pl.ds(pl.multiple_of(j * block + first, block), block)
+                total = over_texts(grads[:, part], stacked[...])
+                for grad, text in zip(done_grads, done_texts):
+                    total = total + over_texts(grad[:, part], text[:block, :])
+                images_ref[j, :block, :] = scale * total
                 put_extra(images_ref.at[j, block:, :], col_extra)
                 return carry
 
@@ -575,6 +566,7 @@
         in_specs=[smem] * 3 + [vmem] * len(operands),
         out_specs=(vmem,) * len(out_shape),
         scratch_shapes=[
+            VMEM((n * block, width), jnp.bfloat16),
             VMEM((EXTRA, width), jnp.float32),
             VMEM((n * block, width), jnp.float32),
             VMEM((block, LANES), jnp.float32),

time: 77.5 us -> 78.8 us (1.017)
  Pallas kernels: 22 us -> 23.4 us
    pallas_call x2, Pallas kernels: 8.16 us -> 9.57 us  [text_grads(): pl.pallas_call(functools.partial(text_kernel, tuple(order), len(done), le...]
  transfers between devices with their start and end apart: 22 -> 22, of which waited for: 15 -> 14; matrix products, arithmetic and copies ran while one was open for 2% -> 1% of each run, Pallas kernels for 20% -> 22%
where the time goes in v16:
time: 78.8 us; the launch traced here: 78.6 us
  waiting for transfers between devices  28.9 us (37%)
  Pallas kernels  23.4 us (30%)
  starting transfers between devices  22.2 us (28%)
  other arithmetic  2.42 us (3%)
  between operations  1.6 us (2%)
    ppermute x22, waiting for transfers between devices, swap(): return lax.ppermute(x, axis, [(i, i ^ q) for i in range(n)])  28.9 us
    ppermute x22, starting transfers between devices, swap(): return lax.ppermute(x, axis, [(i, i ^ q) for i in range(n)])  22.2 us
    pallas_call x2, Pallas kernels, text_grads(): pl.pallas_call(functools.partial(text_kernel, tuple(order), len(done), le...  9.57 us
    pallas_call x2, Pallas kernels, stats(): pl.pallas_call(functools.partial(stats_kernel, first, len(texts), block),...  7.92 us
    pallas_call x2, Pallas kernels, total_of(): pl.pallas_call(functools.partial(total_kernel, len(codes), in_order), out...  3.78 us
  transfers between devices with their start and end apart: 22, of which 14 were waited for; matrix products, arithmetic and copies ran while one was open for 1% of the time, Pallas kernels for 22%

profile of v16, /device:TPU:0, one launch (start us, length us, event | category | flops | bytes accessed | tf_op | source)
XLA Modules:
  0.0 78.6 jit_solution(5944890291836840571)
XLA Ops:
  0.6 1.1 %convert_element_type.8 = bf16[256,512]{1,0:T(8,128)(2,1)S(1)} convert(f32[256,512]{1,0:T(8,128)} %param.4) | non-fusion elementwise | flops 131072 | bytes 786432 | tf_op jit(solution)/shard_map/convert_element_type | solution.py:591
  1.7 4.1 %collective-permute-start.4 = (bf16[272,512]{1,0:T(8,128)(2,1)S(1)}, bf16[272,512]{1,0:T(8,128)(2,1)S(1)}, u32[]{:S(2)}, u32[]{:S(2)}) collective-permute-start(bf16[272,512]{1,0:T(8,128)(2,1)S(1)} %pad.4.refs_0_.refs_8_), channel_id=1, source_target_pairs={{0,16},{8,24},{16,0},{24,8},{1,17},{9,25},{17,1},{25,9},{2,18},{10... | collective-permute-start | bytes 835592 | tf_op jit(solution)/shard_map/ppermute | solution.py:20
  5.8 1.6 %collective-permute-start.3 = (bf16[272,512]{1,0:T(8,128)(2,1)S(1)}, bf16[272,512]{1,0:T(8,128)(2,1)S(1)}, u32[]{:S(2)}, u32[]{:S(2)}) collective-permute-start(bf16[272,512]{1,0:T(8,128)(2,1)S(1)} %pad.4.refs_0_.refs_8_), channel_id=1, source_target_pairs={{0,8},{8,0},{16,24},{24,16},{1,9},{9,1},{17,25},{25,17},{2,10},{10... | collective-permute-start | bytes 835592 | tf_op jit(solution)/shard_map/ppermute | solution.py:20
  7.4 1.1 %convert_element_type.9.refs_3_ = bf16[256,512]{1,0:T(8,128)(2,1)S(1)} convert(f32[256,512]{1,0:T(8,128)} %param.3) | non-fusion elementwise | flops 131072 | bytes 786432 | tf_op jit(solution)/shard_map/convert_element_type | solution.py:590
  8.5 2.5 %collective-permute-start.2 = (bf16[256,512]{1,0:T(8,128)(2,1)S(1)}, bf16[256,512]{1,0:T(8,128)(2,1)S(1)}, u32[]{:S(2)}, u32[]{:S(2)}) collective-permute-start(bf16[256,512]{1,0:T(8,128)(2,1)S(1)} %convert_element_type.9.refs_3_), channel_id=1, source_target_pairs={{0,6},{1,7},{2,4},{3,5},{4,2},{5,3},{6,0},{7,1},{8,14},{9,15},{10,... | collective-permute-start | bytes 786440 | tf_op jit(solution)/shard_map/ppermute | solution.py:20
  11.5 0.5 collective-permute-start
  12.0 6.5 %collective-permute-done.4.refs_2_.refs_6_ = bf16[272,512]{1,0:T(8,128)(2,1)S(1)} collective-permute-done((bf16[272,512]{1,0:T(8,128)(2,1)S(1)}, bf16[272,512]{1,0:T(8,128)(2,1)S(1)}, u32[]{:S(2)}, u32[]{:S(2)}) %collective-permute-start.4) | collective-permute-done | bytes 278560 | tf_op jit(solution)/shard_map/ppermute | solution.py:20
  18.6 0.6 collective-permute-start.9
  19.2 3.4 %collective-permute-done.1.refs_5_ = bf16[256,512]{1,0:T(8,128)(2,1)S(1)} collective-permute-done((bf16[256,512]{1,0:T(8,128)(2,1)S(1)}, bf16[256,512]{1,0:T(8,128)(2,1)S(1)}, u32[]{:S(2)}, u32[]{:S(2)}) %collective-permute-start.1) | collective-permute-done | bytes 262176 | tf_op jit(solution)/shard_map/ppermute | solution.py:20
  22.7 0.5 collective-permute-start.7
  25.0 5.3 %stats.1 = (bf16[1024,512]{1,0:T(8,128)(2,1)S(1)}, bf16[1024,512]{1,0:T(8,128)(2,1)S(1)}, f32[4,8,256]{2,1,0:T(8,128)S(1)}, f32[3,4,256]{2,1,0:T(4,128)S(1)}, f32[768,2048]{1,0:T(8,128)S(1)}) custom-call(f32[1,1]{1,0:T(1,128)S(6)} %mul.127.coef_ref, s32[1,2]{1,0:T(1,128)S(1)} %add_bitcast_fusion.place_ref, bf16[272,512]{1,0:T(8,128)(2,1)S(1)} %pad.4.refs_0_.refs_8_, ...), custom_call_target="tpu_custom_call" | custom-call | flops 2097152 | tf_op jit(solution)/shard_map/stats/pallas_call | solution.py:180
  30.3 2.6 %stats_last.1 = (f32[4,8,256]{2,1,0:T(8,128)S(1)}, f32[3,4,256]{2,1,0:T(4,128)S(1)}, f32[256,2048]{1,0:T(8,128)S(1)}) custom-call(f32[1,1]{1,0:T(1,128)S(6)} %mul.127.coef_ref, s32[1,2]{1,0:T(1,128)S(1)} %add_bitcast_fusion.place_ref, bf16[272,512]{1,0:T(8,128)(2,1)S(1)} %collective-permute-done.9.refs_0_.refs_6_.refs_11_, ...), custom_call_target="tpu_custom_call" | custom-call | flops 2097152 | tf_op jit(solution)/shard_map/stats_last/pallas_call | solution.py:180
  33.3 1.6 %collective-permute-start.10 = (f32[4,8,256]{2,1,0:T(8,128)S(1)}, f32[4,8,256]{2,1,0:T(8,128)S(1)}, u32[]{:S(2)}, u32[]{:S(2)}) collective-permute-start(f32[4,8,256]{2,1,0:T(8,128)S(1)} %get-tuple-element.48), channel_id=1, source_target_pairs={{0,2},{1,3},{2,0},{3,1},{4,6},{5,7},{6,4},{7,5},{8,10},{9,11},{10,... | collective-permute-start | bytes 98312 | tf_op jit(solution)/shard_map/ppermute | solution.py:20
  34.9 2.3 %collective-permute-done.10 = f32[4,8,256]{2,1,0:T(8,128)S(1)} collective-permute-done((f32[4,8,256]{2,1,0:T(8,128)S(1)}, f32[4,8,256]{2,1,0:T(8,128)S(1)}, u32[]{:S(2)}, u32[]{:S(2)}) %collective-permute-start.10) | collective-permute-done | bytes 32800 | tf_op jit(solution)/shard_map/ppermute | solution.py:20
  37.4 0.5 collective-permute-start.13
  37.9 1.5 %collective-permute-start.12 = (f32[4,8,256]{2,1,0:T(8,128)S(1)}, f32[4,8,256]{2,1,0:T(8,128)S(1)}, u32[]{:S(2)}, u32[]{:S(2)}) collective-permute-start(f32[4,8,256]{2,1,0:T(8,128)S(1)} %pad_maximum_fusion.1), channel_id=1, source_target_pairs={{0,4},{1,5},{2,6},{3,7},{4,0},{5,1},{6,2},{7,3},{8,12},{9,13},{10,... | collective-permute-start | bytes 98312 | tf_op jit(solution)/shard_map/ppermute | solution.py:20
  39.4 2.4 %collective-permute-done.12 = f32[4,8,256]{2,1,0:T(8,128)S(1)} collective-permute-done((f32[4,8,256]{2,1,0:T(8,128)S(1)}, f32[4,8,256]{2,1,0:T(8,128)S(1)}, u32[]{:S(2)}, u32[]{:S(2)}) %collective-permute-start.12) | collective-permute-done | bytes 32800 | tf_op jit(solution)/shard_map/ppermute | solution.py:20
  42.5 1.2 %collective-permute-done.14 = f32[4,8,256]{2,1,0:T(8,128)S(1)} collective-permute-done((f32[4,8,256]{2,1,0:T(8,128)S(1)}, f32[4,8,256]{2,1,0:T(8,128)S(1)}, u32[]{:S(2)}, u32[]{:S(2)}) %collective-permute-start.14) | collective-permute-done | bytes 32800 | tf_op jit(solution)/shard_map/ppermute | solution.py:20
  43.7 1.8 %text_grads_1.1 = (bf16[256,2048]{1,0:T(8,128)(2,1)S(1)}, bf16[272,512]{1,0:T(8,128)(2,1)S(1)}) custom-call(f32[1,1]{1,0:T(1,128)} %bitcast.241.scale_ref, f32[1,1]{1,0:T(1,128)S(6)} %mul.127.coef_ref, s32[1,2]{1,0:T(1,128)S(1)} %add_bitcast_fusion.place_ref, bf16[1024,512]{1,0:T(8,128)(2,1)S(1)} %get-tuple-element.44.refs_1_.refs_0_, ...), custom_call_target="tpu_custom_call" | custom-call | flops 21474836480 | tf_op jit(solution)/shard_map/text_grads_1/pallas_call | solution.py:563
  45.5 1.8 %collective-permute-start.16 = (bf16[272,512]{1,0:T(8,128)(2,1)S(1)}, bf16[272,512]{1,0:T(8,128)(2,1)S(1)}, u32[]{:S(2)}, u32[]{:S(2)}) collective-permute-start(bf16[272,512]{1,0:T(8,128)(2,1)S(1)} %get-tuple-element.62), channel_id=1, source_target_pairs={{0,8},{8,0},{16,24},{24,16},{1,9},{9,1},{17,25},{25,17},{2,10},{10... | collective-permute-start | bytes 835592 | tf_op jit(solution)/shard_map/ppermute | solution.py:20
  47.3 7.8 %text_grads_3.1 = (bf16[768,2048]{1,0:T(8,128)(2,1)}, f32[264,512]{1,0:T(8,128)S(1)}, bf16[272,512]{1,0:T(8,128)(2,1)S(1)}, f32[264,512]{1,0:T(8,128)S(1)}, f32[...) custom-call(f32[1,1]{1,0:T(1,128)} %bitcast.242.scale_ref, f32[1,1]{1,0:T(1,128)S(6)} %mul.127.coef_ref, ...), custom_call_target="tpu_custom_call" | custom-call | flops 64424509440 | tf_op jit(solution)/shard_map/text_grads_3/pallas_call | solution.py:563
  55.0 0.7 pack_text.1.refs_0_
  55.7 2.0 %collective-permute-start.19 = (bf16[272,512]{1,0:T(8,128)(2,1)S(1)}, bf16[272,512]{1,0:T(8,128)(2,1)S(1)}, u32[]{:S(2)}, u32[]{:S(2)}) collective-permute-start(bf16[272,512]{1,0:T(8,128)(2,1)S(1)} %pack_text.1.refs_0_), channel_id=1, source_target_pairs={{0,16},{8,24},{16,0},{24,8},{1,17},{9,25},{17,1},{25,9},{2,18},{10... | collective-permute-start | bytes 835592 | tf_op jit(solution)/shard_map/ppermute | solution.py:20
  57.8 1.5 %collective-permute-done.15.far = f32[4,264,512]{2,1,0:T(8,128)S(1)} collective-permute-done((f32[4,264,512]{2,1,0:T(8,128)S(1)}, f32[4,264,512]{2,1,0:T(8,128)S(1)}, u32[]{:S(2)}, u32[]{:S(2)}) %collective-permute-start.15) | collective-permute-done | bytes 2162720 | tf_op jit(solution)/shard_map/ppermute | solution.py:20
  59.6 1.1 %pack_images.1 = (f32[264,512]{1,0:T(8,128)S(1)}, bf16[272,512]{1,0:T(8,128)(2,1)S(1)}, bf16[272,512]{1,0:T(8,128)(2,1)S(1)}, bf16[272,512]{1,0:T(8,128)(2,1)S(1)}) custom-call(f32[4,264,512]{2,1,0:T(8,128)S(1)} %get-tuple-element.57.near, f32[4,264,512]{2,1,0:T(8,128)S(1)} %collective-permute-done.15.far, bf16[272,512]{1,0:T(8,128)(2,1)S(1)} %pack_text.1.refs_0_), custom_call_target="tpu_custom_call" | custom-call | flops 21474836480 | tf_op jit(solution)/shard_map/pack_images/pallas_call | solution.py:349
  60.7 1.7 %collective-permute-start.17 = (bf16[272,512]{1,0:T(8,128)(2,1)S(1)}, bf16[272,512]{1,0:T(8,128)(2,1)S(1)}, u32[]{:S(2)}, u32[]{:S(2)}) collective-permute-start(bf16[272,512]{1,0:T(8,128)(2,1)S(1)} %get-tuple-element.64), channel_id=1, source_target_pairs={{0,2},{1,3},{2,0},{3,1},{4,6},{5,7},{6,4},{7,5},{8,10},{9,11},{10,... | collective-permute-start | bytes 835592 | tf_op jit(solution)/shard_map/ppermute | solution.py:20
  62.4 1.0 %collective-permute-start.20 = (bf16[272,512]{1,0:T(8,128)(2,1)S(1)}, bf16[272,512]{1,0:T(8,128)(2,1)S(1)}, u32[]{:S(2)}, u32[]{:S(2)}) collective-permute-start(bf16[272,512]{1,0:T(8,128)(2,1)S(1)} %get-tuple-element.69), channel_id=1, source_target_pairs={{0,4},{1,5},{2,6},{3,7},{4,0},{5,1},{6,2},{7,3},{8,12},{9,13},{10,... | collective-permute-start | bytes 835592 | tf_op jit(solution)/shard_map/ppermute | solution.py:20
  63.4 0.9 %collective-permute-start.21 = (bf16[272,512]{1,0:T(8,128)(2,1)S(1)}, bf16[272,512]{1,0:T(8,128)(2,1)S(1)}, u32[]{:S(2)}, u32[]{:S(2)}) collective-permute-start(bf16[272,512]{1,0:T(8,128)(2,1)S(1)} %get-tuple-element.70), channel_id=1, source_target_pairs={{0,6},{1,7},{2,4},{3,5},{4,2},{5,3},{6,0},{7,1},{8,14},{9,15},{10,... | collective-permute-start | bytes 835592 | tf_op jit(solution)/shard_map/ppermute | solution.py:20
  64.3 7.3 %collective-permute-done.19.refs_1_ = bf16[272,512]{1,0:T(8,128)(2,1)S(1)} collective-permute-done((bf16[272,512]{1,0:T(8,128)(2,1)S(1)}, bf16[272,512]{1,0:T(8,128)(2,1)S(1)}, u32[]{:S(2)}, u32[]{:S(2)}) %collective-permute-start.19) | collective-permute-done | bytes 278560 | tf_op jit(solution)/shard_map/ppermute | solution.py:20
  71.6 2.2 %collective-permute-done.18.refs_0_ = bf16[272,512]{1,0:T(8,128)(2,1)S(1)} collective-permute-done((bf16[272,512]{1,0:T(8,128)(2,1)S(1)}, bf16[272,512]{1,0:T(8,128)(2,1)S(1)}, u32[]{:S(2)}, u32[]{:S(2)}) %collective-permute-start.18) | collective-permute-done | bytes 278560 | tf_op jit(solution)/shard_map/ppermute | solution.py:20
  73.9 1.8 %grad_text.1 = (f32[256,512]{1,0:T(8,128)}, f32[8,256]{1,0:T(8,128)S(1)}, f32[1,1]{1,0:T(1,128)}) custom-call(f32[1,1]{1,0:T(1,128)S(6)} %mul.127.coef_ref, f32[264,512]{1,0:T(8,128)S(1)} %get-tuple-element.65.base, bf16[272,512]{1,0:T(8,128)(2,1)S(1)} %collective-permute-done.18.refs_0_, bf16[272,512]{1,0:T(8,128)(2,1)S(1)} %collective-permute-done.19.refs_1_), custom_call_target="tpu_custom_call" | custom-call | tf_op jit(solution)/shard_map/grad_text/pallas_call | solution.py:422
  76.5 1.9 %grad_image.1 = (f32[256,512]{1,0:T(8,128)}, f32[8,256]{1,0:T(8,128)}, f32[1,1]{1,0:T(1,128)}) custom-call(f32[1,1]{1,0:T(1,128)S(6)} %mul.127.coef_ref, f32[264,512]{1,0:T(8,128)S(1)} %added.1.base, bf16[272,512]{1,0:T(8,128)(2,1)S(1)} %collective-permute-done.20.refs_0_, bf16[272,512]{1,0:T(8,128)(2,1)S(1)} %collective-permute-done.21.refs_1_, ...), custom_call_target="tpu_custom_call" | custom-call | tf_op jit(solution)/shard_map/grad_image/pallas_call | solution.py:422
  (44 shorter events, 4.1 us)
Async XLA Ops:
  1.7 16.8 %collective-permute-start.4 = (bf16[272,512]{1,0:T(8,128)(2,1)S(1)}, bf16[272,512]{1,0:T(8,128)(2,1)S(1)}, u32[]{:S(2)}, u32[]{:S(2)}) collective-permute-start(bf16[272,512]{1,0:T(8,128)(2,1)S(1)} %pad.4.refs_0_.refs_8_), channel_id=1, source_target_pairs={{0,16},{8,24},{16,0},{24,8},{1,17},{9,25},{17,1},{25,9},{2,18},{10... | collective-permute-start | bytes 835592 | tf_op jit(solution)/shard_map/ppermute | solution.py:20
  5.8 16.8 %collective-permute-start.3 = (bf16[272,512]{1,0:T(8,128)(2,1)S(1)}, bf16[272,512]{1,0:T(8,128)(2,1)S(1)}, u32[]{:S(2)}, u32[]{:S(2)}) collective-permute-start(bf16[272,512]{1,0:T(8,128)(2,1)S(1)} %pad.4.refs_0_.refs_8_), channel_id=1, source_target_pairs={{0,8},{8,0},{16,24},{24,16},{1,9},{9,1},{17,25},{25,17},{2,10},{10... | collective-permute-start | bytes 835592 | tf_op jit(solution)/shard_map/ppermute | solution.py:20
  8.5 10.7 %collective-permute-start.2 = (bf16[256,512]{1,0:T(8,128)(2,1)S(1)}, bf16[256,512]{1,0:T(8,128)(2,1)S(1)}, u32[]{:S(2)}, u32[]{:S(2)}) collective-permute-start(bf16[256,512]{1,0:T(8,128)(2,1)S(1)} %convert_element_type.9.refs_3_), channel_id=1, source_target_pairs={{0,6},{1,7},{2,4},{3,5},{4,2},{5,3},{6,0},{7,1},{8,14},{9,15},{10,... | collective-permute-start | bytes 786440 | tf_op jit(solution)/shard_map/ppermute | solution.py:20
  11.0 11.6 %collective-permute-start.1 = (bf16[256,512]{1,0:T(8,128)(2,1)S(1)}, bf16[256,512]{1,0:T(8,128)(2,1)S(1)}, u32[]{:S(2)}, u32[]{:S(2)}) collective-permute-start(bf16[256,512]{1,0:T(8,128)(2,1)S(1)} %convert_element_type.9.refs_3_), channel_id=1, source_target_pairs={{0,4},{1,5},{2,6},{3,7},{4,0},{5,1},{6,2},{7,3},{8,12},{9,13},{10,... | collective-permute-start | bytes 786440 | tf_op jit(solution)/shard_map/ppermute | solution.py:20
  11.5 11.1 %collective-permute-start = (bf16[256,512]{1,0:T(8,128)(2,1)S(1)}, bf16[256,512]{1,0:T(8,128)(2,1)S(1)}, u32[]{:S(2)}, u32[]{:S(2)}) collective-permute-start(bf16[256,512]{1,0:T(8,128)(2,1)S(1)} %convert_element_type.9.refs_3_), channel_id=1, source_target_pairs={{0,2},{1,3},{2,0},{3,1},{4,6},{5,7},{6,4},{7,5},{8,10},{9,11},{10,... | collective-permute-start | bytes 786440 | tf_op jit(solution)/shard_map/ppermute | solution.py:20
  18.6 11.7 %collective-permute-start.9 = (bf16[272,512]{1,0:T(8,128)(2,1)S(1)}, bf16[272,512]{1,0:T(8,128)(2,1)S(1)}, u32[]{:S(2)}, u32[]{:S(2)}) collective-permute-start(bf16[272,512]{1,0:T(8,128)(2,1)S(1)} %collective-permute-done.4.refs_2_.refs_6_), channel_id=1, source_target_pairs={{0,8},{8,0},{16,24},{24,16},{1,9},{9,1},{17,25},{25,17},{2,10},{10... | collective-permute-start | bytes 835592 | tf_op jit(solution)/shard_map/ppermute | solution.py:20
  19.2 4.7 %collective-permute-start.5 = (bf16[256,512]{1,0:T(8,128)(2,1)S(1)}, bf16[256,512]{1,0:T(8,128)(2,1)S(1)}, u32[]{:S(2)}, u32[]{:S(2)}) collective-permute-start(bf16[256,512]{1,0:T(8,128)(2,1)S(1)} %convert_element_type.9.refs_3_), channel_id=1, source_target_pairs={{0,1},{1,0},{2,3},{3,2},{4,5},{5,4},{6,7},{7,6},{8,9},{9,8},{10,11... | collective-permute-start | bytes 786440 | tf_op jit(solution)/shard_map/ppermute | solution.py:20
  22.7 1.5 %collective-permute-start.6 = (bf16[256,512]{1,0:T(8,128)(2,1)S(1)}, bf16[256,512]{1,0:T(8,128)(2,1)S(1)}, u32[]{:S(2)}, u32[]{:S(2)}) collective-permute-start(bf16[256,512]{1,0:T(8,128)(2,1)S(1)} %collective-permute-done.refs_4_), channel_id=1, source_target_pairs={{0,1},{1,0},{2,3},{3,2},{4,5},{5,4},{6,7},{7,6},{8,9},{9,8},{10,11... | collective-permute-start | bytes 786440 | tf_op jit(solution)/shard_map/ppermute | solution.py:20
  22.7 1.9 %collective-permute-start.7 = (bf16[256,512]{1,0:T(8,128)(2,1)S(1)}, bf16[256,512]{1,0:T(8,128)(2,1)S(1)}, u32[]{:S(2)}, u32[]{:S(2)}) collective-permute-start(bf16[256,512]{1,0:T(8,128)(2,1)S(1)} %collective-permute-done.1.refs_5_), channel_id=1, source_target_pairs={{0,1},{1,0},{2,3},{3,2},{4,5},{5,4},{6,7},{7,6},{8,9},{9,8},{10,11... | collective-permute-start | bytes 786440 | tf_op jit(solution)/shard_map/ppermute | solution.py:20
  23.2 1.8 %collective-permute-start.8 = (bf16[256,512]{1,0:T(8,128)(2,1)S(1)}, bf16[256,512]{1,0:T(8,128)(2,1)S(1)}, u32[]{:S(2)}, u32[]{:S(2)}) collective-permute-start(bf16[256,512]{1,0:T(8,128)(2,1)S(1)} %collective-permute-done.2.refs_6_), channel_id=1, source_target_pairs={{0,1},{1,0},{2,3},{3,2},{4,5},{5,4},{6,7},{7,6},{8,9},{9,8},{10,11... | collective-permute-start | bytes 786440 | tf_op jit(solution)/shard_map/ppermute | solution.py:20
  32.9 4.3 %collective-permute-start.11 = (f32[9,4,256]{2,1,0:T(4,128)S(1)}, f32[9,4,256]{2,1,0:T(4,128)S(1)}, u32[]{:S(2)}, u32[]{:S(2)}) collective-permute-start(f32[9,4,256]{2,1,0:T(4,128)S(1)} %pad_maximum_fusion), channel_id=1, source_target_pairs={{0,8},{8,0},{16,24},{24,16},{1,9},{9,1},{17,25},{25,17},{2,10},{10... | collective-permute-start | bytes 110600 | tf_op jit(solution)/shard_map/ppermute | solution.py:20
  33.3 3.9 %collective-permute-start.10 = (f32[4,8,256]{2,1,0:T(8,128)S(1)}, f32[4,8,256]{2,1,0:T(8,128)S(1)}, u32[]{:S(2)}, u32[]{:S(2)}) collective-permute-start(f32[4,8,256]{2,1,0:T(8,128)S(1)} %get-tuple-element.48), channel_id=1, source_target_pairs={{0,2},{1,3},{2,0},{3,1},{4,6},{5,7},{6,4},{7,5},{8,10},{9,11},{10,... | collective-permute-start | bytes 98312 | tf_op jit(solution)/shard_map/ppermute | solution.py:20
  37.4 4.9 %collective-permute-start.13 = (f32[9,4,256]{2,1,0:T(4,128)S(1)}, f32[9,4,256]{2,1,0:T(4,128)S(1)}, u32[]{:S(2)}, u32[]{:S(2)}) collective-permute-start(f32[9,4,256]{2,1,0:T(4,128)S(1)} %constant_dynamic-update-slice_fusion), channel_id=1, source_target_pairs={{0,16},{8,24},{16,0},{24,8},{1,17},{9,25},{17,1},{25,9},{2,18},{10... | collective-permute-start | bytes 110600 | tf_op jit(solution)/shard_map/ppermute | solution.py:20
  37.9 3.9 %collective-permute-start.12 = (f32[4,8,256]{2,1,0:T(8,128)S(1)}, f32[4,8,256]{2,1,0:T(8,128)S(1)}, u32[]{:S(2)}, u32[]{:S(2)}) collective-permute-start(f32[4,8,256]{2,1,0:T(8,128)S(1)} %pad_maximum_fusion.1), channel_id=1, source_target_pairs={{0,4},{1,5},{2,6},{3,7},{4,0},{5,1},{6,2},{7,3},{8,12},{9,13},{10,... | collective-permute-start | bytes 98312 | tf_op jit(solution)/shard_map/ppermute | solution.py:20
  42.4 1.3 %collective-permute-start.14 = (f32[4,8,256]{2,1,0:T(8,128)S(1)}, f32[4,8,256]{2,1,0:T(8,128)S(1)}, u32[]{:S(2)}, u32[]{:S(2)}) collective-permute-start(f32[4,8,256]{2,1,0:T(8,128)S(1)} %pad_maximum_fusion.2), channel_id=1, source_target_pairs={{0,1},{1,0},{2,3},{3,2},{4,5},{5,4},{6,7},{7,6},{8,9},{9,8},{10,11... | collective-permute-start | bytes 98312 | tf_op jit(solution)/shard_map/ppermute | solution.py:20
  45.5 9.5 %collective-permute-start.16 = (bf16[272,512]{1,0:T(8,128)(2,1)S(1)}, bf16[272,512]{1,0:T(8,128)(2,1)S(1)}, u32[]{:S(2)}, u32[]{:S(2)}) collective-permute-start(bf16[272,512]{1,0:T(8,128)(2,1)S(1)} %get-tuple-element.62), channel_id=1, source_target_pairs={{0,8},{8,0},{16,24},{24,16},{1,9},{9,1},{17,25},{25,17},{2,10},{10... | collective-permute-start | bytes 835592 | tf_op jit(solution)/shard_map/ppermute | solution.py:20
  55.0 4.3 %collective-permute-start.15 = (f32[4,264,512]{2,1,0:T(8,128)S(1)}, f32[4,264,512]{2,1,0:T(8,128)S(1)}, u32[]{:S(2)}, u32[]{:S(2)}) collective-permute-start(f32[4,264,512]{2,1,0:T(8,128)S(1)} %get-tuple-element.59), channel_id=1, source_target_pairs={{0,1},{1,0},{2,3},{3,2},{4,5},{5,4},{6,7},{7,6},{8,9},{9,8},{10,11... | collective-permute-start | bytes 6488072 | tf_op jit(solution)/shard_map/ppermute | solution.py:20
  55.7 15.9 %collective-permute-start.19 = (bf16[272,512]{1,0:T(8,128)(2,1)S(1)}, bf16[272,512]{1,0:T(8,128)(2,1)S(1)}, u32[]{:S(2)}, u32[]{:S(2)}) collective-permute-start(bf16[272,512]{1,0:T(8,128)(2,1)S(1)} %pack_text.1.refs_0_), channel_id=1, source_target_pairs={{0,16},{8,24},{16,0},{24,8},{1,17},{9,25},{17,1},{25,9},{2,18},{10... | collective-permute-start | bytes 835592 | tf_op jit(solution)/shard_map/ppermute | solution.py:20
  59.3 14.6 %collective-permute-start.18 = (bf16[272,512]{1,0:T(8,128)(2,1)S(1)}, bf16[272,512]{1,0:T(8,128)(2,1)S(1)}, u32[]{:S(2)}, u32[]{:S(2)}) collective-permute-start(bf16[272,512]{1,0:T(8,128)(2,1)S(1)} %get-tuple-element.66), channel_id=1, source_target_pairs={{0,8},{8,0},{16,24},{24,16},{1,9},{9,1},{17,25},{25,17},{2,10},{10... | collective-permute-start | bytes 835592 | tf_op jit(solution)/shard_map/ppermute | solution.py:20
  60.7 15.0 %collective-permute-start.17 = (bf16[272,512]{1,0:T(8,128)(2,1)S(1)}, bf16[272,512]{1,0:T(8,128)(2,1)S(1)}, u32[]{:S(2)}, u32[]{:S(2)}) collective-permute-start(bf16[272,512]{1,0:T(8,128)(2,1)S(1)} %get-tuple-element.64), channel_id=1, source_target_pairs={{0,2},{1,3},{2,0},{3,1},{4,6},{5,7},{6,4},{7,5},{8,10},{9,11},{10,... | collective-permute-start | bytes 835592 | tf_op jit(solution)/shard_map/ppermute | solution.py:20
  62.4 14.1 %collective-permute-start.20 = (bf16[272,512]{1,0:T(8,128)(2,1)S(1)}, bf16[272,512]{1,0:T(8,128)(2,1)S(1)}, u32[]{:S(2)}, u32[]{:S(2)}) collective-permute-start(bf16[272,512]{1,0:T(8,128)(2,1)S(1)} %get-tuple-element.69), channel_id=1, source_target_pairs={{0,4},{1,5},{2,6},{3,7},{4,0},{5,1},{6,2},{7,3},{8,12},{9,13},{10,... | collective-permute-start | bytes 835592 | tf_op jit(solution)/shard_map/ppermute | solution.py:20
  63.4 13.1 %collective-permute-start.21 = (bf16[272,512]{1,0:T(8,128)(2,1)S(1)}, bf16[272,512]{1,0:T(8,128)(2,1)S(1)}, u32[]{:S(2)}, u32[]{:S(2)}) collective-permute-start(bf16[272,512]{1,0:T(8,128)(2,1)S(1)} %get-tuple-element.70), channel_id=1, source_target_pairs={{0,6},{1,7},{2,4},{3,5},{4,2},{5,3},{6,0},{7,1},{8,14},{9,15},{10,... | collective-permute-start | bytes 835592 | tf_op jit(solution)/shard_map/ppermute | solution.py:20

commit v17 on v15

--- a/solution.py
+++ b/solution.py
@@ -27,6 +27,42 @@
     images, texts = lax.optimization_barrier((images, texts))
     odd = [swap(i, "col", n_col, 1) for i in (image, *images)]
     return [image, *images], odd, [text, *texts], last
+
+
+def cast_kernel(image_ref, text_ref, image_out, text_out, image, text, sems):
+    copies = [
+        pltpu.make_async_copy(text_ref, text, sems.at[0]),
+        pltpu.make_async_copy(image_ref, image, sems.at[1]),
+    ]
+    for copy in copies:
+        copy.start()
+    block, width = text.shape
+    text_out[block:, :] = jnp.zeros((text_out.shape[0] - block, width), jnp.bfloat16)
+    copies[0].wait()
+    text_out[:block, :] = text[...].astype(jnp.bfloat16)
+    copies[1].wait()
+    image_out[...] = image[...].astype(jnp.bfloat16)
+
+
+def cast(image, text, more):
+    block, width = text.shape
+    vmem = pl.BlockSpec(memory_space=VMEM)
+    return pl.pallas_call(
+        cast_kernel,
+        out_shape=(
+            jax.ShapeDtypeStruct(image.shape, jnp.bfloat16),
+            jax.ShapeDtypeStruct((block + more, width), jnp.bfloat16),
+        ),
+        in_specs=[pl.BlockSpec(memory_space=pl.ANY)] * 2,
+        out_specs=(vmem, vmem),
+        scratch_shapes=[
+            VMEM(image.shape, jnp.float32),
+            VMEM(text.shape, jnp.float32),
+            pltpu.SemaphoreType.DMA((2,)),
+        ],
+        compiler_params=pltpu.CompilerParams(vmem_limit_bytes=4 * 2**20),
+        name="cast",
+    )(image, text)
 
 
 def nt_dot(a, b):
@@ -595,8 +631,7 @@
     place = jnp.stack([r, c]).reshape(1, 2)
     scale = logit_scale.reshape(1, 1)
     coef = scale * LOG2E
-    image_half = image_embeds.astype(jnp.bfloat16)
-    text_half = jnp.pad(text_embeds.astype(jnp.bfloat16), ((0, 16), (0, 0)))
+    image_half, text_half = cast(image_embeds, text_embeds, 16)
     even, odd, texts, text_last = gather_both(image_half, text_half, n_col, n_row)
     keep = 4 * n_row * n_col * block * block <= 16 * 2**20
     even, odd, *before = stats(

time: 77.5 us -> 78 us (level)
  other arithmetic: 2.42 us -> 0.27 us
  local copies, waits for them, and re-layouts: 0.07 us -> 2.13 us
    convert_element_type x2 -> x0, other arithmetic: 2.15 us -> none  [the longest x1 1.07 us: on_device(): text_half = jnp.pad(text_embeds.astype(jnp.bfloat16), ((0, 16), (0, 0)))]
    unnamed x5 -> x9, local copies, waits for them, and re-layouts: 0.04 us -> 2.12 us
  transfers between devices with their start and end apart: 22 -> 22, of which waited for: 15 -> 14; matrix products, arithmetic and copies ran while one was open for 2% -> 0% of each run, Pallas kernels for 20% -> 20%
where the time goes in v17:
time: 78 us; the launch traced here: 77.8 us
  waiting for transfers between devices  29 us (37%)
  starting transfers between devices  22.7 us (29%)
  Pallas kernels  22.1 us (28%)
  local copies, waits for them, and re-layouts  2.13 us (3%)
  between operations  1.62 us (2%)
    ppermute x22, waiting for transfers between devices, swap(): return lax.ppermute(x, axis, [(i, i ^ q) for i in range(n)])  29 us
    ppermute x22, starting transfers between devices, swap(): return lax.ppermute(x, axis, [(i, i ^ q) for i in range(n)])  22.7 us
    pallas_call x2, Pallas kernels, text_grads(): pl.pallas_call(functools.partial(text_kernel, tuple(order), len(done), le...  8.15 us
    pallas_call x2, Pallas kernels, stats(): pl.pallas_call(functools.partial(stats_kernel, first, len(texts), block),...  7.91 us
    pallas_call x2, Pallas kernels, total_of(): pl.pallas_call(functools.partial(total_kernel, len(codes), in_order), out...  3.78 us
    unnamed x9, local copies, waits for them, and re-layouts  2.12 us
  transfers between devices with their start and end apart: 22, of which 14 were waited for; matrix products, arithmetic and copies ran while one was open for 0% of the time, Pallas kernels for 20%

profile of v17, /device:TPU:0, one launch (start us, length us, event | category | flops | bytes accessed | tf_op | source)
XLA Modules:
  0.0 77.8 jit_solution(9432196072820789466)
XLA Ops:
  0.6 1.0 %copy-done = f32[256,512]{1,0:T(8,128)S(1)} copy-done((f32[256,512]{1,0:T(8,128)S(1)}, f32[256,512]{1,0:T(8,128)}, u32[]{:S(2)}) %copy-start) | copy-done | bytes 524312
  1.7 1.0 %copy-done.1 = f32[256,512]{1,0:T(8,128)S(1)} copy-done((f32[256,512]{1,0:T(8,128)S(1)}, f32[256,512]{1,0:T(8,128)}, u32[]{:S(2)}) %copy-start.1) | copy-done | bytes 524312
  2.9 4.1 %collective-permute-start.4 = (bf16[272,512]{1,0:T(8,128)(2,1)S(1)}, bf16[272,512]{1,0:T(8,128)(2,1)S(1)}, u32[]{:S(2)}, u32[]{:S(2)}) collective-permute-start(bf16[272,512]{1,0:T(8,128)(2,1)S(1)} %get-tuple-element.41.refs_0_.refs_8_), channel_id=1, source_target_pairs={{0,16},{8,24},{16,0},{24,8},{1,17},{9,25},{17,1},{25,9},{2,18},{10... | collective-permute-start | bytes 835592 | tf_op jit(solution)/shard_map/ppermute | solution.py:20
  7.0 1.6 %collective-permute-start.3 = (bf16[272,512]{1,0:T(8,128)(2,1)S(1)}, bf16[272,512]{1,0:T(8,128)(2,1)S(1)}, u32[]{:S(2)}, u32[]{:S(2)}) collective-permute-start(bf16[272,512]{1,0:T(8,128)(2,1)S(1)} %get-tuple-element.41.refs_0_.refs_8_), channel_id=1, source_target_pairs={{0,8},{8,0},{16,24},{24,16},{1,9},{9,1},{17,25},{25,17},{2,10},{10... | collective-permute-start | bytes 835592 | tf_op jit(solution)/shard_map/ppermute | solution.py:20
  8.5 2.4 %collective-permute-start.2 = (bf16[256,512]{1,0:T(8,128)(2,1)S(1)}, bf16[256,512]{1,0:T(8,128)(2,1)S(1)}, u32[]{:S(2)}, u32[]{:S(2)}) collective-permute-start(bf16[256,512]{1,0:T(8,128)(2,1)S(1)} %get-tuple-element.42.refs_3_), channel_id=1, source_target_pairs={{0,6},{1,7},{2,4},{3,5},{4,2},{5,3},{6,0},{7,1},{8,14},{9,15},{10,... | collective-permute-start | bytes 786440 | tf_op jit(solution)/shard_map/ppermute | solution.py:20
  12.0 7.7 %collective-permute-done.4.refs_2_.refs_6_ = bf16[272,512]{1,0:T(8,128)(2,1)S(1)} collective-permute-done((bf16[272,512]{1,0:T(8,128)(2,1)S(1)}, bf16[272,512]{1,0:T(8,128)(2,1)S(1)}, u32[]{:S(2)}, u32[]{:S(2)}) %collective-permute-start.4) | collective-permute-done | bytes 278560 | tf_op jit(solution)/shard_map/ppermute | solution.py:20
  19.7 0.6 collective-permute-start.9
  20.3 2.2 %collective-permute-done.1.refs_5_ = bf16[256,512]{1,0:T(8,128)(2,1)S(1)} collective-permute-done((bf16[256,512]{1,0:T(8,128)(2,1)S(1)}, bf16[256,512]{1,0:T(8,128)(2,1)S(1)}, u32[]{:S(2)}, u32[]{:S(2)}) %collective-permute-start.1) | collective-permute-done | bytes 262176 | tf_op jit(solution)/shard_map/ppermute | solution.py:20
  24.9 5.4 %stats.1 = (bf16[1024,512]{1,0:T(8,128)(2,1)S(1)}, bf16[1024,512]{1,0:T(8,128)(2,1)S(1)}, f32[4,8,256]{2,1,0:T(8,128)S(1)}, f32[3,4,256]{2,1,0:T(4,128)S(1)}, f32[768,2048]{1,0:T(8,128)S(1)}) custom-call(f32[1,1]{1,0:T(1,128)S(6)} %mul.127.coef_ref, s32[1,2]{1,0:T(1,128)S(1)} %add_bitcast_fusion.place_ref, ...), custom_call_target="tpu_custom_call" | custom-call | flops 2097152 | tf_op jit(solution)/shard_map/stats/pallas_call | solution.py:216
  30.3 2.6 %stats_last.1 = (f32[4,8,256]{2,1,0:T(8,128)S(1)}, f32[3,4,256]{2,1,0:T(4,128)S(1)}, f32[256,2048]{1,0:T(8,128)S(1)}) custom-call(f32[1,1]{1,0:T(1,128)S(6)} %mul.127.coef_ref, s32[1,2]{1,0:T(1,128)S(1)} %add_bitcast_fusion.place_ref, bf16[272,512]{1,0:T(8,128)(2,1)S(1)} %collective-permute-done.9.refs_0_.refs_6_.refs_11_, ...), custom_call_target="tpu_custom_call" | custom-call | flops 2097152 | tf_op jit(solution)/shard_map/stats_last/pallas_call | solution.py:216
  33.3 1.6 %collective-permute-start.10 = (f32[4,8,256]{2,1,0:T(8,128)S(1)}, f32[4,8,256]{2,1,0:T(8,128)S(1)}, u32[]{:S(2)}, u32[]{:S(2)}) collective-permute-start(f32[4,8,256]{2,1,0:T(8,128)S(1)} %get-tuple-element.52), channel_id=1, source_target_pairs={{0,2},{1,3},{2,0},{3,1},{4,6},{5,7},{6,4},{7,5},{8,10},{9,11},{10,... | collective-permute-start | bytes 98312 | tf_op jit(solution)/shard_map/ppermute | solution.py:20
  34.9 2.3 %collective-permute-done.10 = f32[4,8,256]{2,1,0:T(8,128)S(1)} collective-permute-done((f32[4,8,256]{2,1,0:T(8,128)S(1)}, f32[4,8,256]{2,1,0:T(8,128)S(1)}, u32[]{:S(2)}, u32[]{:S(2)}) %collective-permute-start.10) | collective-permute-done | bytes 32800 | tf_op jit(solution)/shard_map/ppermute | solution.py:20
  37.4 1.7 %collective-permute-start.13 = (f32[9,4,256]{2,1,0:T(4,128)S(1)}, f32[9,4,256]{2,1,0:T(4,128)S(1)}, u32[]{:S(2)}, u32[]{:S(2)}) collective-permute-start(f32[9,4,256]{2,1,0:T(4,128)S(1)} %constant_dynamic-update-slice_fusion), channel_id=1, source_target_pairs={{0,16},{8,24},{16,0},{24,8},{1,17},{9,25},{17,1},{25,9},{2,18},{10... | collective-permute-start | bytes 110600 | tf_op jit(solution)/shard_map/ppermute | solution.py:20
  39.0 1.5 %collective-permute-start.12 = (f32[4,8,256]{2,1,0:T(8,128)S(1)}, f32[4,8,256]{2,1,0:T(8,128)S(1)}, u32[]{:S(2)}, u32[]{:S(2)}) collective-permute-start(f32[4,8,256]{2,1,0:T(8,128)S(1)} %pad_maximum_fusion.1), channel_id=1, source_target_pairs={{0,4},{1,5},{2,6},{3,7},{4,0},{5,1},{6,2},{7,3},{8,12},{9,13},{10,... | collective-permute-start | bytes 98312 | tf_op jit(solution)/shard_map/ppermute | solution.py:20
  40.6 2.4 %collective-permute-done.12 = f32[4,8,256]{2,1,0:T(8,128)S(1)} collective-permute-done((f32[4,8,256]{2,1,0:T(8,128)S(1)}, f32[4,8,256]{2,1,0:T(8,128)S(1)}, u32[]{:S(2)}, u32[]{:S(2)}) %collective-permute-start.12) | collective-permute-done | bytes 32800 | tf_op jit(solution)/shard_map/ppermute | solution.py:20
  43.1 1.2 %collective-permute-done.14 = f32[4,8,256]{2,1,0:T(8,128)S(1)} collective-permute-done((f32[4,8,256]{2,1,0:T(8,128)S(1)}, f32[4,8,256]{2,1,0:T(8,128)S(1)}, u32[]{:S(2)}, u32[]{:S(2)}) %collective-permute-start.14) | collective-permute-done | bytes 32800 | tf_op jit(solution)/shard_map/ppermute | solution.py:20
  44.4 1.8 %text_grads_1.1 = (bf16[256,2048]{1,0:T(8,128)(2,1)S(1)}, bf16[272,512]{1,0:T(8,128)(2,1)S(1)}) custom-call(f32[1,1]{1,0:T(1,128)} %bitcast.241.scale_ref, f32[1,1]{1,0:T(1,128)S(6)} %mul.127.coef_ref, s32[1,2]{1,0:T(1,128)S(1)} %add_bitcast_fusion.place_ref, bf16[1024,512]{1,0:T(8,128)(2,1)S(1)} %get-tuple-element.48.refs_1_.refs_0_, ...), custom_call_target="tpu_custom_call" | custom-call | flops 21474836480 | tf_op jit(solution)/shard_map/text_grads_1/pallas_call | solution.py:608
  46.2 1.5 %collective-permute-start.16 = (bf16[272,512]{1,0:T(8,128)(2,1)S(1)}, bf16[272,512]{1,0:T(8,128)(2,1)S(1)}, u32[]{:S(2)}, u32[]{:S(2)}) collective-permute-start(bf16[272,512]{1,0:T(8,128)(2,1)S(1)} %get-tuple-element.66), channel_id=1, source_target_pairs={{0,8},{8,0},{16,24},{24,16},{1,9},{9,1},{17,25},{25,17},{2,10},{10... | collective-permute-start | bytes 835592 | tf_op jit(solution)/shard_map/ppermute | solution.py:20
  47.6 6.4 %text_grads_3.1 = (bf16[768,2048]{1,0:T(8,128)(2,1)}, f32[264,512]{1,0:T(8,128)S(1)}, bf16[272,512]{1,0:T(8,128)(2,1)S(1)}, f32[264,512]{1,0:T(8,128)S(1)}, f32[...) custom-call(f32[1,1]{1,0:T(1,128)} %bitcast.242.scale_ref, f32[1,1]{1,0:T(1,128)S(6)} %mul.127.coef_ref, ...), custom_call_target="tpu_custom_call" | custom-call | flops 64424509440 | tf_op jit(solution)/shard_map/text_grads_3/pallas_call | solution.py:608
  54.0 0.9 %collective-permute-done.16.refs_0_ = bf16[272,512]{1,0:T(8,128)(2,1)S(1)} collective-permute-done((bf16[272,512]{1,0:T(8,128)(2,1)S(1)}, bf16[272,512]{1,0:T(8,128)(2,1)S(1)}, u32[]{:S(2)}, u32[]{:S(2)}) %collective-permute-start.16) | collective-permute-done | bytes 278560 | tf_op jit(solution)/shard_map/ppermute | solution.py:20
  54.9 0.7 pack_text.1.refs_0_
  55.6 1.4 %collective-permute-start.19 = (bf16[272,512]{1,0:T(8,128)(2,1)S(1)}, bf16[272,512]{1,0:T(8,128)(2,1)S(1)}, u32[]{:S(2)}, u32[]{:S(2)}) collective-permute-start(bf16[272,512]{1,0:T(8,128)(2,1)S(1)} %pack_text.1.refs_0_), channel_id=1, source_target_pairs={{0,16},{8,24},{16,0},{24,8},{1,17},{9,25},{17,1},{25,9},{2,18},{10... | collective-permute-start | bytes 835592 | tf_op jit(solution)/shard_map/ppermute | solution.py:20
  57.0 1.3 %collective-permute-done.15.far = f32[4,264,512]{2,1,0:T(8,128)S(1)} collective-permute-done((f32[4,264,512]{2,1,0:T(8,128)S(1)}, f32[4,264,512]{2,1,0:T(8,128)S(1)}, u32[]{:S(2)}, u32[]{:S(2)}) %collective-permute-start.15) | collective-permute-done | bytes 2162720 | tf_op jit(solution)/shard_map/ppermute | solution.py:20
  58.3 0.6 collective-permute-start.18
  58.9 1.1 %pack_images.1 = (f32[264,512]{1,0:T(8,128)S(1)}, bf16[272,512]{1,0:T(8,128)(2,1)S(1)}, bf16[272,512]{1,0:T(8,128)(2,1)S(1)}, bf16[272,512]{1,0:T(8,128)(2,1)S(1)}) custom-call(f32[4,264,512]{2,1,0:T(8,128)S(1)} %get-tuple-element.61.near, f32[4,264,512]{2,1,0:T(8,128)S(1)} %collective-permute-done.15.far, bf16[272,512]{1,0:T(8,128)(2,1)S(1)} %pack_text.1.refs_0_), custom_call_target="tpu_custom_call" | custom-call | flops 21474836480 | tf_op jit(solution)/shard_map/pack_images/pallas_call | solution.py:385
  60.0 1.5 %collective-permute-start.17 = (bf16[272,512]{1,0:T(8,128)(2,1)S(1)}, bf16[272,512]{1,0:T(8,128)(2,1)S(1)}, u32[]{:S(2)}, u32[]{:S(2)}) collective-permute-start(bf16[272,512]{1,0:T(8,128)(2,1)S(1)} %get-tuple-element.68), channel_id=1, source_target_pairs={{0,2},{1,3},{2,0},{3,1},{4,6},{5,7},{6,4},{7,5},{8,10},{9,11},{10,... | collective-permute-start | bytes 835592 | tf_op jit(solution)/shard_map/ppermute | solution.py:20
  61.6 1.6 %collective-permute-start.20 = (bf16[272,512]{1,0:T(8,128)(2,1)S(1)}, bf16[272,512]{1,0:T(8,128)(2,1)S(1)}, u32[]{:S(2)}, u32[]{:S(2)}) collective-permute-start(bf16[272,512]{1,0:T(8,128)(2,1)S(1)} %get-tuple-element.73), channel_id=1, source_target_pairs={{0,4},{1,5},{2,6},{3,7},{4,0},{5,1},{6,2},{7,3},{8,12},{9,13},{10,... | collective-permute-start | bytes 835592 | tf_op jit(solution)/shard_map/ppermute | solution.py:20
  63.6 7.2 %collective-permute-done.19.refs_1_ = bf16[272,512]{1,0:T(8,128)(2,1)S(1)} collective-permute-done((bf16[272,512]{1,0:T(8,128)(2,1)S(1)}, bf16[272,512]{1,0:T(8,128)(2,1)S(1)}, u32[]{:S(2)}, u32[]{:S(2)}) %collective-permute-start.19) | collective-permute-done | bytes 278560 | tf_op jit(solution)/shard_map/ppermute | solution.py:20
  70.8 1.5 %collective-permute-done.18.refs_0_ = bf16[272,512]{1,0:T(8,128)(2,1)S(1)} collective-permute-done((bf16[272,512]{1,0:T(8,128)(2,1)S(1)}, bf16[272,512]{1,0:T(8,128)(2,1)S(1)}, u32[]{:S(2)}, u32[]{:S(2)}) %collective-permute-start.18) | collective-permute-done | bytes 278560 | tf_op jit(solution)/shard_map/ppermute | solution.py:20
  72.3 1.8 %grad_text.1 = (f32[256,512]{1,0:T(8,128)}, f32[8,256]{1,0:T(8,128)S(1)}, f32[1,1]{1,0:T(1,128)}) custom-call(f32[1,1]{1,0:T(1,128)S(6)} %mul.127.coef_ref, f32[264,512]{1,0:T(8,128)S(1)} %get-tuple-element.69.base, bf16[272,512]{1,0:T(8,128)(2,1)S(1)} %collective-permute-done.18.refs_0_, bf16[272,512]{1,0:T(8,128)(2,1)S(1)} %collective-permute-done.19.refs_1_), custom_call_target="tpu_custom_call" | custom-call | tf_op jit(solution)/shard_map/grad_text/pallas_call | solution.py:458
  74.5 1.2 %collective-permute-done.20.refs_0_ = bf16[272,512]{1,0:T(8,128)(2,1)S(1)} collective-permute-done((bf16[272,512]{1,0:T(8,128)(2,1)S(1)}, bf16[272,512]{1,0:T(8,128)(2,1)S(1)}, u32[]{:S(2)}, u32[]{:S(2)}) %collective-permute-start.20) | collective-permute-done | bytes 278560 | tf_op jit(solution)/shard_map/ppermute | solution.py:20
  75.7 1.9 %grad_image.1 = (f32[256,512]{1,0:T(8,128)}, f32[8,256]{1,0:T(8,128)}, f32[1,1]{1,0:T(1,128)}) custom-call(f32[1,1]{1,0:T(1,128)S(6)} %mul.127.coef_ref, f32[264,512]{1,0:T(8,128)S(1)} %added.1.base, bf16[272,512]{1,0:T(8,128)(2,1)S(1)} %collective-permute-done.20.refs_0_, bf16[272,512]{1,0:T(8,128)(2,1)S(1)} %collective-permute-done.21.refs_1_, ...), custom_call_target="tpu_custom_call" | custom-call | tf_op jit(solution)/shard_map/grad_image/pallas_call | solution.py:458
  (46 shorter events, 4.5 us)
Async XLA Ops:
  0.6 1.0 %copy-start = (f32[256,512]{1,0:T(8,128)S(1)}, f32[256,512]{1,0:T(8,128)}, u32[]{:S(2)}) copy-start(f32[256,512]{1,0:T(8,128)} %image_ref.1) | copy-start | bytes 1572868
  1.7 1.0 %copy-start.1 = (f32[256,512]{1,0:T(8,128)S(1)}, f32[256,512]{1,0:T(8,128)}, u32[]{:S(2)}) copy-start(f32[256,512]{1,0:T(8,128)} %text_ref.1) | copy-start | bytes 1572868
  2.9 16.8 %collective-permute-start.4 = (bf16[272,512]{1,0:T(8,128)(2,1)S(1)}, bf16[272,512]{1,0:T(8,128)(2,1)S(1)}, u32[]{:S(2)}, u32[]{:S(2)}) collective-permute-start(bf16[272,512]{1,0:T(8,128)(2,1)S(1)} %get-tuple-element.41.refs_0_.refs_8_), channel_id=1, source_target_pairs={{0,16},{8,24},{16,0},{24,8},{1,17},{9,25},{17,1},{25,9},{2,18},{10... | collective-permute-start | bytes 835592 | tf_op jit(solution)/shard_map/ppermute | solution.py:20
  7.0 15.7 %collective-permute-start.3 = (bf16[272,512]{1,0:T(8,128)(2,1)S(1)}, bf16[272,512]{1,0:T(8,128)(2,1)S(1)}, u32[]{:S(2)}, u32[]{:S(2)}) collective-permute-start(bf16[272,512]{1,0:T(8,128)(2,1)S(1)} %get-tuple-element.41.refs_0_.refs_8_), channel_id=1, source_target_pairs={{0,8},{8,0},{16,24},{24,16},{1,9},{9,1},{17,25},{25,17},{2,10},{10... | collective-permute-start | bytes 835592 | tf_op jit(solution)/shard_map/ppermute | solution.py:20
  8.5 11.8 %collective-permute-start.2 = (bf16[256,512]{1,0:T(8,128)(2,1)S(1)}, bf16[256,512]{1,0:T(8,128)(2,1)S(1)}, u32[]{:S(2)}, u32[]{:S(2)}) collective-permute-start(bf16[256,512]{1,0:T(8,128)(2,1)S(1)} %get-tuple-element.42.refs_3_), channel_id=1, source_target_pairs={{0,6},{1,7},{2,4},{3,5},{4,2},{5,3},{6,0},{7,1},{8,14},{9,15},{10,... | collective-permute-start | bytes 786440 | tf_op jit(solution)/shard_map/ppermute | solution.py:20
  11.0 11.6 %collective-permute-start.1 = (bf16[256,512]{1,0:T(8,128)(2,1)S(1)}, bf16[256,512]{1,0:T(8,128)(2,1)S(1)}, u32[]{:S(2)}, u32[]{:S(2)}) collective-permute-start(bf16[256,512]{1,0:T(8,128)(2,1)S(1)} %get-tuple-element.42.refs_3_), channel_id=1, source_target_pairs={{0,4},{1,5},{2,6},{3,7},{4,0},{5,1},{6,2},{7,3},{8,12},{9,13},{10,... | collective-permute-start | bytes 786440 | tf_op jit(solution)/shard_map/ppermute | solution.py:20
  11.5 11.1 %collective-permute-start = (bf16[256,512]{1,0:T(8,128)(2,1)S(1)}, bf16[256,512]{1,0:T(8,128)(2,1)S(1)}, u32[]{:S(2)}, u32[]{:S(2)}) collective-permute-start(bf16[256,512]{1,0:T(8,128)(2,1)S(1)} %get-tuple-element.42.refs_3_), channel_id=1, source_target_pairs={{0,2},{1,3},{2,0},{3,1},{4,6},{5,7},{6,4},{7,5},{8,10},{9,11},{10,... | collective-permute-start | bytes 786440 | tf_op jit(solution)/shard_map/ppermute | solution.py:20
  19.7 10.6 %collective-permute-start.9 = (bf16[272,512]{1,0:T(8,128)(2,1)S(1)}, bf16[272,512]{1,0:T(8,128)(2,1)S(1)}, u32[]{:S(2)}, u32[]{:S(2)}) collective-permute-start(bf16[272,512]{1,0:T(8,128)(2,1)S(1)} %collective-permute-done.4.refs_2_.refs_6_), channel_id=1, source_target_pairs={{0,8},{8,0},{16,24},{24,16},{1,9},{9,1},{17,25},{25,17},{2,10},{10... | collective-permute-start | bytes 835592 | tf_op jit(solution)/shard_map/ppermute | solution.py:20
  20.3 3.6 %collective-permute-start.5 = (bf16[256,512]{1,0:T(8,128)(2,1)S(1)}, bf16[256,512]{1,0:T(8,128)(2,1)S(1)}, u32[]{:S(2)}, u32[]{:S(2)}) collective-permute-start(bf16[256,512]{1,0:T(8,128)(2,1)S(1)} %get-tuple-element.42.refs_3_), channel_id=1, source_target_pairs={{0,1},{1,0},{2,3},{3,2},{4,5},{5,4},{6,7},{7,6},{8,9},{9,8},{10,11... | collective-permute-start | bytes 786440 | tf_op jit(solution)/shard_map/ppermute | solution.py:20
  22.7 1.5 %collective-permute-start.6 = (bf16[256,512]{1,0:T(8,128)(2,1)S(1)}, bf16[256,512]{1,0:T(8,128)(2,1)S(1)}, u32[]{:S(2)}, u32[]{:S(2)}) collective-permute-start(bf16[256,512]{1,0:T(8,128)(2,1)S(1)} %collective-permute-done.refs_4_), channel_id=1, source_target_pairs={{0,1},{1,0},{2,3},{3,2},{4,5},{5,4},{6,7},{7,6},{8,9},{9,8},{10,11... | collective-permute-start | bytes 786440 | tf_op jit(solution)/shard_map/ppermute | solution.py:20
  22.7 1.9 %collective-permute-start.7 = (bf16[256,512]{1,0:T(8,128)(2,1)S(1)}, bf16[256,512]{1,0:T(8,128)(2,1)S(1)}, u32[]{:S(2)}, u32[]{:S(2)}) collective-permute-start(bf16[256,512]{1,0:T(8,128)(2,1)S(1)} %collective-permute-done.1.refs_5_), channel_id=1, source_target_pairs={{0,1},{1,0},{2,3},{3,2},{4,5},{5,4},{6,7},{7,6},{8,9},{9,8},{10,11... | collective-permute-start | bytes 786440 | tf_op jit(solution)/shard_map/ppermute | solution.py:20
  23.2 1.8 %collective-permute-start.8 = (bf16[256,512]{1,0:T(8,128)(2,1)S(1)}, bf16[256,512]{1,0:T(8,128)(2,1)S(1)}, u32[]{:S(2)}, u32[]{:S(2)}) collective-permute-start(bf16[256,512]{1,0:T(8,128)(2,1)S(1)} %collective-permute-done.2.refs_6_), channel_id=1, source_target_pairs={{0,1},{1,0},{2,3},{3,2},{4,5},{5,4},{6,7},{7,6},{8,9},{9,8},{10,11... | collective-permute-start | bytes 786440 | tf_op jit(solution)/shard_map/ppermute | solution.py:20
  32.9 4.3 %collective-permute-start.11 = (f32[9,4,256]{2,1,0:T(4,128)S(1)}, f32[9,4,256]{2,1,0:T(4,128)S(1)}, u32[]{:S(2)}, u32[]{:S(2)}) collective-permute-start(f32[9,4,256]{2,1,0:T(4,128)S(1)} %pad_maximum_fusion), channel_id=1, source_target_pairs={{0,8},{8,0},{16,24},{24,16},{1,9},{9,1},{17,25},{25,17},{2,10},{10... | collective-permute-start | bytes 110600 | tf_op jit(solution)/shard_map/ppermute | solution.py:20
  33.3 3.9 %collective-permute-start.10 = (f32[4,8,256]{2,1,0:T(8,128)S(1)}, f32[4,8,256]{2,1,0:T(8,128)S(1)}, u32[]{:S(2)}, u32[]{:S(2)}) collective-permute-start(f32[4,8,256]{2,1,0:T(8,128)S(1)} %get-tuple-element.52), channel_id=1, source_target_pairs={{0,2},{1,3},{2,0},{3,1},{4,6},{5,7},{6,4},{7,5},{8,10},{9,11},{10,... | collective-permute-start | bytes 98312 | tf_op jit(solution)/shard_map/ppermute | solution.py:20
  37.4 5.6 %collective-permute-start.13 = (f32[9,4,256]{2,1,0:T(4,128)S(1)}, f32[9,4,256]{2,1,0:T(4,128)S(1)}, u32[]{:S(2)}, u32[]{:S(2)}) collective-permute-start(f32[9,4,256]{2,1,0:T(4,128)S(1)} %constant_dynamic-update-slice_fusion), channel_id=1, source_target_pairs={{0,16},{8,24},{16,0},{24,8},{1,17},{9,25},{17,1},{25,9},{2,18},{10... | collective-permute-start | bytes 110600 | tf_op jit(solution)/shard_map/ppermute | solution.py:20
  39.0 3.9 %collective-permute-start.12 = (f32[4,8,256]{2,1,0:T(8,128)S(1)}, f32[4,8,256]{2,1,0:T(8,128)S(1)}, u32[]{:S(2)}, u32[]{:S(2)}) collective-permute-start(f32[4,8,256]{2,1,0:T(8,128)S(1)} %pad_maximum_fusion.1), channel_id=1, source_target_pairs={{0,4},{1,5},{2,6},{3,7},{4,0},{5,1},{6,2},{7,3},{8,12},{9,13},{10,... | collective-permute-start | bytes 98312 | tf_op jit(solution)/shard_map/ppermute | solution.py:20
  43.0 1.3 %collective-permute-start.14 = (f32[4,8,256]{2,1,0:T(8,128)S(1)}, f32[4,8,256]{2,1,0:T(8,128)S(1)}, u32[]{:S(2)}, u32[]{:S(2)}) collective-permute-start(f32[4,8,256]{2,1,0:T(8,128)S(1)} %pad_maximum_fusion.2), channel_id=1, source_target_pairs={{0,1},{1,0},{2,3},{3,2},{4,5},{5,4},{6,7},{7,6},{8,9},{9,8},{10,11... | collective-permute-start | bytes 98312 | tf_op jit(solution)/shard_map/ppermute | solution.py:20
  46.2 8.8 %collective-permute-start.16 = (bf16[272,512]{1,0:T(8,128)(2,1)S(1)}, bf16[272,512]{1,0:T(8,128)(2,1)S(1)}, u32[]{:S(2)}, u32[]{:S(2)}) collective-permute-start(bf16[272,512]{1,0:T(8,128)(2,1)S(1)} %get-tuple-element.66), channel_id=1, source_target_pairs={{0,8},{8,0},{16,24},{24,16},{1,9},{9,1},{17,25},{25,17},{2,10},{10... | collective-permute-start | bytes 835592 | tf_op jit(solution)/shard_map/ppermute | solution.py:20
  54.0 4.3 %collective-permute-start.15 = (f32[4,264,512]{2,1,0:T(8,128)S(1)}, f32[4,264,512]{2,1,0:T(8,128)S(1)}, u32[]{:S(2)}, u32[]{:S(2)}) collective-permute-start(f32[4,264,512]{2,1,0:T(8,128)S(1)} %get-tuple-element.63), channel_id=1, source_target_pairs={{0,1},{1,0},{2,3},{3,2},{4,5},{5,4},{6,7},{7,6},{8,9},{9,8},{10,11... | collective-permute-start | bytes 6488072 | tf_op jit(solution)/shard_map/ppermute | solution.py:20
  55.6 15.2 %collective-permute-start.19 = (bf16[272,512]{1,0:T(8,128)(2,1)S(1)}, bf16[272,512]{1,0:T(8,128)(2,1)S(1)}, u32[]{:S(2)}, u32[]{:S(2)}) collective-permute-start(bf16[272,512]{1,0:T(8,128)(2,1)S(1)} %pack_text.1.refs_0_), channel_id=1, source_target_pairs={{0,16},{8,24},{16,0},{24,8},{1,17},{9,25},{17,1},{25,9},{2,18},{10... | collective-permute-start | bytes 835592 | tf_op jit(solution)/shard_map/ppermute | solution.py:20
  58.3 14.0 %collective-permute-start.18 = (bf16[272,512]{1,0:T(8,128)(2,1)S(1)}, bf16[272,512]{1,0:T(8,128)(2,1)S(1)}, u32[]{:S(2)}, u32[]{:S(2)}) collective-permute-start(bf16[272,512]{1,0:T(8,128)(2,1)S(1)} %get-tuple-element.70), channel_id=1, source_target_pairs={{0,8},{8,0},{16,24},{24,16},{1,9},{9,1},{17,25},{25,17},{2,10},{10... | collective-permute-start | bytes 835592 | tf_op jit(solution)/shard_map/ppermute | solution.py:20
  60.0 14.1 %collective-permute-start.17 = (bf16[272,512]{1,0:T(8,128)(2,1)S(1)}, bf16[272,512]{1,0:T(8,128)(2,1)S(1)}, u32[]{:S(2)}, u32[]{:S(2)}) collective-permute-start(bf16[272,512]{1,0:T(8,128)(2,1)S(1)} %get-tuple-element.68), channel_id=1, source_target_pairs={{0,2},{1,3},{2,0},{3,1},{4,6},{5,7},{6,4},{7,5},{8,10},{9,11},{10,... | collective-permute-start | bytes 835592 | tf_op jit(solution)/shard_map/ppermute | solution.py:20
  61.6 14.1 %collective-permute-start.20 = (bf16[272,512]{1,0:T(8,128)(2,1)S(1)}, bf16[272,512]{1,0:T(8,128)(2,1)S(1)}, u32[]{:S(2)}, u32[]{:S(2)}) collective-permute-start(bf16[272,512]{1,0:T(8,128)(2,1)S(1)} %get-tuple-element.73), channel_id=1, source_target_pairs={{0,4},{1,5},{2,6},{3,7},{4,0},{5,1},{6,2},{7,3},{8,12},{9,13},{10,... | collective-permute-start | bytes 835592 | tf_op jit(solution)/shard_map/ppermute | solution.py:20
  63.1 12.6 %collective-permute-start.21 = (bf16[272,512]{1,0:T(8,128)(2,1)S(1)}, bf16[272,512]{1,0:T(8,128)(2,1)S(1)}, u32[]{:S(2)}, u32[]{:S(2)}) collective-permute-start(bf16[272,512]{1,0:T(8,128)(2,1)S(1)} %get-tuple-element.74), channel_id=1, source_target_pairs={{0,6},{1,7},{2,4},{3,5},{4,2},{5,3},{6,0},{7,1},{8,14},{9,15},{10,... | collective-permute-start | bytes 835592 | tf_op jit(solution)/shard_map/ppermute | solution.py:20

commit v18 on v15

--- a/solution.py
+++ b/solution.py
@@ -366,6 +366,13 @@
     out, extra, scalar, value, powers, sems = refs[-6:]
     size, width = base.shape[0] - EXTRA, base.shape[1]
     combine = functools.partial(functools.reduce, jnp.add) if in_order else first_and_pairs
+    more = combine([base[size:, : width // 2]] + [decode_extra(code, size) for code in codes])
+    more = sum([b[...] for b in before], more)
+    extra[...] = more
+    if before:
+        scalar[0, 0] = jnp.sum(more) / coef_ref[0, 0]
+    else:
+        scalar[0, 0] = 0.0
     for c, code in enumerate(codes):
         powers[c] = decode_powers(code, size)
     copies = []
@@ -378,10 +385,6 @@
             )
         copies.append(pltpu.make_async_copy(value.at[part], out.at[part], sems.at[i]))
         copies[-1].start()
-    more = combine([base[size:, : width // 2]] + [decode_extra(code, size) for code in codes])
-    more = sum([b[...] for b in before], more)
-    extra[...] = more
-    scalar[0, 0] = jnp.sum(more) / coef_ref[0, 0]
     for copy in copies:
         copy.wait()
 
@@ -478,11 +481,11 @@
         lax.fori_loop(0, half // block, one, 0, unroll=4)
 
 
-def image_block(grads, texts, at, block, scale):
+def image_block(grads, texts, at, count, scale, block):
     total = None
     for grad, text in zip(grads, texts):
         part = lax.dot_general(
-            grad[:, pl.ds(at, block)],
+            grad[:, pl.ds(at, count)],
             text[:block, :],
             (((0,), (0,)), ((), ())),
             preferred_element_type=jnp.float32,
@@ -536,17 +539,20 @@
         for images_ref, first in ((far_ref, half), (near_ref, 0)):
 
             def one(j, carry):
-                images_ref[j, :block, :] = image_block(
+                pair = image_block(
                     [*done_grads, *[by_text[t][0] for t in order]],
                     [*done_texts, *[by_text[t][1] for t in order]],
-                    pl.multiple_of(j * block + first, block),
+                    pl.multiple_of(2 * j * block + first, block),
+                    2 * block,
+                    scale,
                     block,
-                    scale,
                 )
-                put_extra(images_ref.at[j, block:, :], col_extra)
+                for n in range(2):
+                    images_ref[2 * j + n, :block, :] = pair[n * block : (n + 1) * block]
+                    put_extra(images_ref.at[2 * j + n, block:, :], col_extra)
                 return carry
 
-            lax.fori_loop(0, half // block, one, 0, unroll=4)
+            lax.fori_loop(0, half // block // 2, one, 0, unroll=2)
 
 
 def text_grads(scale, coef, place, even, odd, row_lse, col_lse, row_extra, col_extra, texts, tile, order, done):

time: 77.5 us -> 78.4 us (1.012)
  Pallas kernels: 22 us -> 23.1 us
    pallas_call x2, Pallas kernels: 8.16 us -> 9.19 us  [text_grads(): pl.pallas_call(functools.partial(text_kernel, tuple(order), len(done), le...]
  transfers between devices with their start and end apart: 22 -> 22, of which waited for: 15 -> 14; matrix products, arithmetic and copies ran while one was open for 2% -> 1% of each run, Pallas kernels for 20% -> 22%
where the time goes in v18:
time: 78.4 us; the launch traced here: 78.2 us
  waiting for transfers between devices  28.8 us (37%)
  Pallas kernels  23.1 us (29%)
  starting transfers between devices  22.2 us (28%)
  other arithmetic  2.42 us (3%)
  between operations  1.6 us (2%)
    ppermute x22, waiting for transfers between devices, swap(): return lax.ppermute(x, axis, [(i, i ^ q) for i in range(n)])  28.8 us
    ppermute x22, starting transfers between devices, swap(): return lax.ppermute(x, axis, [(i, i ^ q) for i in range(n)])  22.2 us
    pallas_call x2, Pallas kernels, text_grads(): pl.pallas_call(functools.partial(text_kernel, tuple(order), len(done), le...  9.19 us
    pallas_call x2, Pallas kernels, stats(): pl.pallas_call(functools.partial(stats_kernel, first, len(texts), block),...  7.92 us
    pallas_call x2, Pallas kernels, total_of(): pl.pallas_call(functools.partial(total_kernel, len(codes), in_order), out...  3.86 us
  transfers between devices with their start and end apart: 22, of which 14 were waited for; matrix products, arithmetic and copies ran while one was open for 1% of the time, Pallas kernels for 22%

profile of v18, /device:TPU:0, one launch (start us, length us, event | category | flops | bytes accessed | tf_op | source)
XLA Modules:
  0.0 78.2 jit_solution(10392457047637331861)
XLA Ops:
  0.6 1.1 %convert_element_type.8 = bf16[256,512]{1,0:T(8,128)(2,1)S(1)} convert(f32[256,512]{1,0:T(8,128)} %param.4) | non-fusion elementwise | flops 131072 | bytes 786432 | tf_op jit(solution)/shard_map/convert_element_type | solution.py:605
  1.7 4.1 %collective-permute-start.4 = (bf16[272,512]{1,0:T(8,128)(2,1)S(1)}, bf16[272,512]{1,0:T(8,128)(2,1)S(1)}, u32[]{:S(2)}, u32[]{:S(2)}) collective-permute-start(bf16[272,512]{1,0:T(8,128)(2,1)S(1)} %pad.4.refs_0_.refs_8_), channel_id=1, source_target_pairs={{0,16},{8,24},{16,0},{24,8},{1,17},{9,25},{17,1},{25,9},{2,18},{10... | collective-permute-start | bytes 835592 | tf_op jit(solution)/shard_map/ppermute | solution.py:20
  5.8 1.6 %collective-permute-start.3 = (bf16[272,512]{1,0:T(8,128)(2,1)S(1)}, bf16[272,512]{1,0:T(8,128)(2,1)S(1)}, u32[]{:S(2)}, u32[]{:S(2)}) collective-permute-start(bf16[272,512]{1,0:T(8,128)(2,1)S(1)} %pad.4.refs_0_.refs_8_), channel_id=1, source_target_pairs={{0,8},{8,0},{16,24},{24,16},{1,9},{9,1},{17,25},{25,17},{2,10},{10... | collective-permute-start | bytes 835592 | tf_op jit(solution)/shard_map/ppermute | solution.py:20
  7.4 1.1 %convert_element_type.9.refs_3_ = bf16[256,512]{1,0:T(8,128)(2,1)S(1)} convert(f32[256,512]{1,0:T(8,128)} %param.3) | non-fusion elementwise | flops 131072 | bytes 786432 | tf_op jit(solution)/shard_map/convert_element_type | solution.py:604
  8.5 2.5 %collective-permute-start.2 = (bf16[256,512]{1,0:T(8,128)(2,1)S(1)}, bf16[256,512]{1,0:T(8,128)(2,1)S(1)}, u32[]{:S(2)}, u32[]{:S(2)}) collective-permute-start(bf16[256,512]{1,0:T(8,128)(2,1)S(1)} %convert_element_type.9.refs_3_), channel_id=1, source_target_pairs={{0,6},{1,7},{2,4},{3,5},{4,2},{5,3},{6,0},{7,1},{8,14},{9,15},{10,... | collective-permute-start | bytes 786440 | tf_op jit(solution)/shard_map/ppermute | solution.py:20
  11.5 0.5 collective-permute-start
  12.0 6.5 %collective-permute-done.4.refs_2_.refs_6_ = bf16[272,512]{1,0:T(8,128)(2,1)S(1)} collective-permute-done((bf16[272,512]{1,0:T(8,128)(2,1)S(1)}, bf16[272,512]{1,0:T(8,128)(2,1)S(1)}, u32[]{:S(2)}, u32[]{:S(2)}) %collective-permute-start.4) | collective-permute-done | bytes 278560 | tf_op jit(solution)/shard_map/ppermute | solution.py:20
  18.6 0.6 collective-permute-start.9
  19.2 3.4 %collective-permute-done.1.refs_5_ = bf16[256,512]{1,0:T(8,128)(2,1)S(1)} collective-permute-done((bf16[256,512]{1,0:T(8,128)(2,1)S(1)}, bf16[256,512]{1,0:T(8,128)(2,1)S(1)}, u32[]{:S(2)}, u32[]{:S(2)}) %collective-permute-start.1) | collective-permute-done | bytes 262176 | tf_op jit(solution)/shard_map/ppermute | solution.py:20
  22.7 0.5 collective-permute-start.7
  25.0 5.3 %stats.1 = (bf16[1024,512]{1,0:T(8,128)(2,1)S(1)}, bf16[1024,512]{1,0:T(8,128)(2,1)S(1)}, f32[4,8,256]{2,1,0:T(8,128)S(1)}, f32[3,4,256]{2,1,0:T(4,128)S(1)}, f32[768,2048]{1,0:T(8,128)S(1)}) custom-call(f32[1,1]{1,0:T(1,128)S(6)} %mul.127.coef_ref, s32[1,2]{1,0:T(1,128)S(1)} %add_bitcast_fusion.place_ref, bf16[272,512]{1,0:T(8,128)(2,1)S(1)} %pad.4.refs_0_.refs_8_, ...), custom_call_target="tpu_custom_call" | custom-call | flops 2097152 | tf_op jit(solution)/shard_map/stats/pallas_call | solution.py:180
  30.3 2.6 %stats_last.1 = (f32[4,8,256]{2,1,0:T(8,128)S(1)}, f32[3,4,256]{2,1,0:T(4,128)S(1)}, f32[256,2048]{1,0:T(8,128)S(1)}) custom-call(f32[1,1]{1,0:T(1,128)S(6)} %mul.127.coef_ref, s32[1,2]{1,0:T(1,128)S(1)} %add_bitcast_fusion.place_ref, bf16[272,512]{1,0:T(8,128)(2,1)S(1)} %collective-permute-done.9.refs_0_.refs_6_.refs_11_, ...), custom_call_target="tpu_custom_call" | custom-call | flops 2097152 | tf_op jit(solution)/shard_map/stats_last/pallas_call | solution.py:180
  33.3 1.6 %collective-permute-start.10 = (f32[4,8,256]{2,1,0:T(8,128)S(1)}, f32[4,8,256]{2,1,0:T(8,128)S(1)}, u32[]{:S(2)}, u32[]{:S(2)}) collective-permute-start(f32[4,8,256]{2,1,0:T(8,128)S(1)} %get-tuple-element.48), channel_id=1, source_target_pairs={{0,2},{1,3},{2,0},{3,1},{4,6},{5,7},{6,4},{7,5},{8,10},{9,11},{10,... | collective-permute-start | bytes 98312 | tf_op jit(solution)/shard_map/ppermute | solution.py:20
  34.9 2.3 %collective-permute-done.10 = f32[4,8,256]{2,1,0:T(8,128)S(1)} collective-permute-done((f32[4,8,256]{2,1,0:T(8,128)S(1)}, f32[4,8,256]{2,1,0:T(8,128)S(1)}, u32[]{:S(2)}, u32[]{:S(2)}) %collective-permute-start.10) | collective-permute-done | bytes 32800 | tf_op jit(solution)/shard_map/ppermute | solution.py:20
  37.4 0.5 collective-permute-start.13
  37.9 1.5 %collective-permute-start.12 = (f32[4,8,256]{2,1,0:T(8,128)S(1)}, f32[4,8,256]{2,1,0:T(8,128)S(1)}, u32[]{:S(2)}, u32[]{:S(2)}) collective-permute-start(f32[4,8,256]{2,1,0:T(8,128)S(1)} %pad_maximum_fusion.1), channel_id=1, source_target_pairs={{0,4},{1,5},{2,6},{3,7},{4,0},{5,1},{6,2},{7,3},{8,12},{9,13},{10,... | collective-permute-start | bytes 98312 | tf_op jit(solution)/shard_map/ppermute | solution.py:20
  39.4 2.4 %collective-permute-done.12 = f32[4,8,256]{2,1,0:T(8,128)S(1)} collective-permute-done((f32[4,8,256]{2,1,0:T(8,128)S(1)}, f32[4,8,256]{2,1,0:T(8,128)S(1)}, u32[]{:S(2)}, u32[]{:S(2)}) %collective-permute-start.12) | collective-permute-done | bytes 32800 | tf_op jit(solution)/shard_map/ppermute | solution.py:20
  42.5 1.2 %collective-permute-done.14 = f32[4,8,256]{2,1,0:T(8,128)S(1)} collective-permute-done((f32[4,8,256]{2,1,0:T(8,128)S(1)}, f32[4,8,256]{2,1,0:T(8,128)S(1)}, u32[]{:S(2)}, u32[]{:S(2)}) %collective-permute-start.14) | collective-permute-done | bytes 32800 | tf_op jit(solution)/shard_map/ppermute | solution.py:20
  43.7 1.8 %text_grads_1.1 = (bf16[256,2048]{1,0:T(8,128)(2,1)S(1)}, bf16[272,512]{1,0:T(8,128)(2,1)S(1)}) custom-call(f32[1,1]{1,0:T(1,128)} %bitcast.241.scale_ref, f32[1,1]{1,0:T(1,128)S(6)} %mul.127.coef_ref, s32[1,2]{1,0:T(1,128)S(1)} %add_bitcast_fusion.place_ref, bf16[1024,512]{1,0:T(8,128)(2,1)S(1)} %get-tuple-element.44.refs_1_.refs_0_, ...), custom_call_target="tpu_custom_call" | custom-call | flops 21474836480 | tf_op jit(solution)/shard_map/text_grads_1/pallas_call | solution.py:578
  45.5 1.8 %collective-permute-start.16 = (bf16[272,512]{1,0:T(8,128)(2,1)S(1)}, bf16[272,512]{1,0:T(8,128)(2,1)S(1)}, u32[]{:S(2)}, u32[]{:S(2)}) collective-permute-start(bf16[272,512]{1,0:T(8,128)(2,1)S(1)} %get-tuple-element.62), channel_id=1, source_target_pairs={{0,8},{8,0},{16,24},{24,16},{1,9},{9,1},{17,25},{25,17},{2,10},{10... | collective-permute-start | bytes 835592 | tf_op jit(solution)/shard_map/ppermute | solution.py:20
  47.3 7.4 %text_grads_3.1 = (bf16[768,2048]{1,0:T(8,128)(2,1)}, f32[264,512]{1,0:T(8,128)S(1)}, bf16[272,512]{1,0:T(8,128)(2,1)S(1)}, f32[264,512]{1,0:T(8,128)S(1)}, f32[...) custom-call(f32[1,1]{1,0:T(1,128)} %bitcast.242.scale_ref, f32[1,1]{1,0:T(1,128)S(6)} %mul.127.coef_ref, ...), custom_call_target="tpu_custom_call" | custom-call | flops 64424509440 | tf_op jit(solution)/shard_map/text_grads_3/pallas_call | solution.py:578
  54.7 0.7 pack_text.1.refs_0_
  55.4 2.0 %collective-permute-start.19 = (bf16[272,512]{1,0:T(8,128)(2,1)S(1)}, bf16[272,512]{1,0:T(8,128)(2,1)S(1)}, u32[]{:S(2)}, u32[]{:S(2)}) collective-permute-start(bf16[272,512]{1,0:T(8,128)(2,1)S(1)} %pack_text.1.refs_0_), channel_id=1, source_target_pairs={{0,16},{8,24},{16,0},{24,8},{1,17},{9,25},{17,1},{25,9},{2,18},{10... | collective-permute-start | bytes 835592 | tf_op jit(solution)/shard_map/ppermute | solution.py:20
  57.4 1.5 %collective-permute-done.15.far = f32[4,264,512]{2,1,0:T(8,128)S(1)} collective-permute-done((f32[4,264,512]{2,1,0:T(8,128)S(1)}, f32[4,264,512]{2,1,0:T(8,128)S(1)}, u32[]{:S(2)}, u32[]{:S(2)}) %collective-permute-start.15) | collective-permute-done | bytes 2162720 | tf_op jit(solution)/shard_map/ppermute | solution.py:20
  59.2 1.1 %pack_images.1 = (f32[264,512]{1,0:T(8,128)S(1)}, bf16[272,512]{1,0:T(8,128)(2,1)S(1)}, bf16[272,512]{1,0:T(8,128)(2,1)S(1)}, bf16[272,512]{1,0:T(8,128)(2,1)S(1)}) custom-call(f32[4,264,512]{2,1,0:T(8,128)S(1)} %get-tuple-element.57.near, f32[4,264,512]{2,1,0:T(8,128)S(1)} %collective-permute-done.15.far, bf16[272,512]{1,0:T(8,128)(2,1)S(1)} %pack_text.1.refs_0_), custom_call_target="tpu_custom_call" | custom-call | flops 21474836480 | tf_op jit(solution)/shard_map/pack_images/pallas_call | solution.py:349
  60.4 1.7 %collective-permute-start.17 = (bf16[272,512]{1,0:T(8,128)(2,1)S(1)}, bf16[272,512]{1,0:T(8,128)(2,1)S(1)}, u32[]{:S(2)}, u32[]{:S(2)}) collective-permute-start(bf16[272,512]{1,0:T(8,128)(2,1)S(1)} %get-tuple-element.64), channel_id=1, source_target_pairs={{0,2},{1,3},{2,0},{3,1},{4,6},{5,7},{6,4},{7,5},{8,10},{9,11},{10,... | collective-permute-start | bytes 835592 | tf_op jit(solution)/shard_map/ppermute | solution.py:20
  62.0 1.0 %collective-permute-start.20 = (bf16[272,512]{1,0:T(8,128)(2,1)S(1)}, bf16[272,512]{1,0:T(8,128)(2,1)S(1)}, u32[]{:S(2)}, u32[]{:S(2)}) collective-permute-start(bf16[272,512]{1,0:T(8,128)(2,1)S(1)} %get-tuple-element.69), channel_id=1, source_target_pairs={{0,4},{1,5},{2,6},{3,7},{4,0},{5,1},{6,2},{7,3},{8,12},{9,13},{10,... | collective-permute-start | bytes 835592 | tf_op jit(solution)/shard_map/ppermute | solution.py:20
  63.0 0.9 %collective-permute-start.21 = (bf16[272,512]{1,0:T(8,128)(2,1)S(1)}, bf16[272,512]{1,0:T(8,128)(2,1)S(1)}, u32[]{:S(2)}, u32[]{:S(2)}) collective-permute-start(bf16[272,512]{1,0:T(8,128)(2,1)S(1)} %get-tuple-element.70), channel_id=1, source_target_pairs={{0,6},{1,7},{2,4},{3,5},{4,2},{5,3},{6,0},{7,1},{8,14},{9,15},{10,... | collective-permute-start | bytes 835592 | tf_op jit(solution)/shard_map/ppermute | solution.py:20
  63.9 7.3 %collective-permute-done.19.refs_1_ = bf16[272,512]{1,0:T(8,128)(2,1)S(1)} collective-permute-done((bf16[272,512]{1,0:T(8,128)(2,1)S(1)}, bf16[272,512]{1,0:T(8,128)(2,1)S(1)}, u32[]{:S(2)}, u32[]{:S(2)}) %collective-permute-start.19) | collective-permute-done | bytes 278560 | tf_op jit(solution)/shard_map/ppermute | solution.py:20
  71.2 2.2 %collective-permute-done.18.refs_0_ = bf16[272,512]{1,0:T(8,128)(2,1)S(1)} collective-permute-done((bf16[272,512]{1,0:T(8,128)(2,1)S(1)}, bf16[272,512]{1,0:T(8,128)(2,1)S(1)}, u32[]{:S(2)}, u32[]{:S(2)}) %collective-permute-start.18) | collective-permute-done | bytes 278560 | tf_op jit(solution)/shard_map/ppermute | solution.py:20
  73.5 1.9 %grad_text.1 = (f32[256,512]{1,0:T(8,128)}, f32[8,256]{1,0:T(8,128)S(1)}, f32[1,1]{1,0:T(1,128)}) custom-call(f32[1,1]{1,0:T(1,128)S(6)} %mul.127.coef_ref, f32[264,512]{1,0:T(8,128)S(1)} %get-tuple-element.65.base, bf16[272,512]{1,0:T(8,128)(2,1)S(1)} %collective-permute-done.18.refs_0_, bf16[272,512]{1,0:T(8,128)(2,1)S(1)} %collective-permute-done.19.refs_1_), custom_call_target="tpu_custom_call" | custom-call | tf_op jit(solution)/shard_map/grad_text/pallas_call | solution.py:425
  76.1 1.9 %grad_image.1 = (f32[256,512]{1,0:T(8,128)}, f32[8,256]{1,0:T(8,128)}, f32[1,1]{1,0:T(1,128)}) custom-call(f32[1,1]{1,0:T(1,128)S(6)} %mul.127.coef_ref, f32[264,512]{1,0:T(8,128)S(1)} %added.1.base, bf16[272,512]{1,0:T(8,128)(2,1)S(1)} %collective-permute-done.20.refs_0_, bf16[272,512]{1,0:T(8,128)(2,1)S(1)} %collective-permute-done.21.refs_1_, ...), custom_call_target="tpu_custom_call" | custom-call | tf_op jit(solution)/shard_map/grad_image/pallas_call | solution.py:425
  (44 shorter events, 4.0 us)
Async XLA Ops:
  1.7 16.8 %collective-permute-start.4 = (bf16[272,512]{1,0:T(8,128)(2,1)S(1)}, bf16[272,512]{1,0:T(8,128)(2,1)S(1)}, u32[]{:S(2)}, u32[]{:S(2)}) collective-permute-start(bf16[272,512]{1,0:T(8,128)(2,1)S(1)} %pad.4.refs_0_.refs_8_), channel_id=1, source_target_pairs={{0,16},{8,24},{16,0},{24,8},{1,17},{9,25},{17,1},{25,9},{2,18},{10... | collective-permute-start | bytes 835592 | tf_op jit(solution)/shard_map/ppermute | solution.py:20
  5.8 16.8 %collective-permute-start.3 = (bf16[272,512]{1,0:T(8,128)(2,1)S(1)}, bf16[272,512]{1,0:T(8,128)(2,1)S(1)}, u32[]{:S(2)}, u32[]{:S(2)}) collective-permute-start(bf16[272,512]{1,0:T(8,128)(2,1)S(1)} %pad.4.refs_0_.refs_8_), channel_id=1, source_target_pairs={{0,8},{8,0},{16,24},{24,16},{1,9},{9,1},{17,25},{25,17},{2,10},{10... | collective-permute-start | bytes 835592 | tf_op jit(solution)/shard_map/ppermute | solution.py:20
  8.5 10.7 %collective-permute-start.2 = (bf16[256,512]{1,0:T(8,128)(2,1)S(1)}, bf16[256,512]{1,0:T(8,128)(2,1)S(1)}, u32[]{:S(2)}, u32[]{:S(2)}) collective-permute-start(bf16[256,512]{1,0:T(8,128)(2,1)S(1)} %convert_element_type.9.refs_3_), channel_id=1, source_target_pairs={{0,6},{1,7},{2,4},{3,5},{4,2},{5,3},{6,0},{7,1},{8,14},{9,15},{10,... | collective-permute-start | bytes 786440 | tf_op jit(solution)/shard_map/ppermute | solution.py:20
  11.0 11.6 %collective-permute-start.1 = (bf16[256,512]{1,0:T(8,128)(2,1)S(1)}, bf16[256,512]{1,0:T(8,128)(2,1)S(1)}, u32[]{:S(2)}, u32[]{:S(2)}) collective-permute-start(bf16[256,512]{1,0:T(8,128)(2,1)S(1)} %convert_element_type.9.refs_3_), channel_id=1, source_target_pairs={{0,4},{1,5},{2,6},{3,7},{4,0},{5,1},{6,2},{7,3},{8,12},{9,13},{10,... | collective-permute-start | bytes 786440 | tf_op jit(solution)/shard_map/ppermute | solution.py:20
  11.5 11.1 %collective-permute-start = (bf16[256,512]{1,0:T(8,128)(2,1)S(1)}, bf16[256,512]{1,0:T(8,128)(2,1)S(1)}, u32[]{:S(2)}, u32[]{:S(2)}) collective-permute-start(bf16[256,512]{1,0:T(8,128)(2,1)S(1)} %convert_element_type.9.refs_3_), channel_id=1, source_target_pairs={{0,2},{1,3},{2,0},{3,1},{4,6},{5,7},{6,4},{7,5},{8,10},{9,11},{10,... | collective-permute-start | bytes 786440 | tf_op jit(solution)/shard_map/ppermute | solution.py:20
  18.6 11.7 %collective-permute-start.9 = (bf16[272,512]{1,0:T(8,128)(2,1)S(1)}, bf16[272,512]{1,0:T(8,128)(2,1)S(1)}, u32[]{:S(2)}, u32[]{:S(2)}) collective-permute-start(bf16[272,512]{1,0:T(8,128)(2,1)S(1)} %collective-permute-done.4.refs_2_.refs_6_), channel_id=1, source_target_pairs={{0,8},{8,0},{16,24},{24,16},{1,9},{9,1},{17,25},{25,17},{2,10},{10... | collective-permute-start | bytes 835592 | tf_op jit(solution)/shard_map/ppermute | solution.py:20
  19.2 4.7 %collective-permute-start.5 = (bf16[256,512]{1,0:T(8,128)(2,1)S(1)}, bf16[256,512]{1,0:T(8,128)(2,1)S(1)}, u32[]{:S(2)}, u32[]{:S(2)}) collective-permute-start(bf16[256,512]{1,0:T(8,128)(2,1)S(1)} %convert_element_type.9.refs_3_), channel_id=1, source_target_pairs={{0,1},{1,0},{2,3},{3,2},{4,5},{5,4},{6,7},{7,6},{8,9},{9,8},{10,11... | collective-permute-start | bytes 786440 | tf_op jit(solution)/shard_map/ppermute | solution.py:20
  22.7 1.5 %collective-permute-start.6 = (bf16[256,512]{1,0:T(8,128)(2,1)S(1)}, bf16[256,512]{1,0:T(8,128)(2,1)S(1)}, u32[]{:S(2)}, u32[]{:S(2)}) collective-permute-start(bf16[256,512]{1,0:T(8,128)(2,1)S(1)} %collective-permute-done.refs_4_), channel_id=1, source_target_pairs={{0,1},{1,0},{2,3},{3,2},{4,5},{5,4},{6,7},{7,6},{8,9},{9,8},{10,11... | collective-permute-start | bytes 786440 | tf_op jit(solution)/shard_map/ppermute | solution.py:20
  22.7 1.9 %collective-permute-start.7 = (bf16[256,512]{1,0:T(8,128)(2,1)S(1)}, bf16[256,512]{1,0:T(8,128)(2,1)S(1)}, u32[]{:S(2)}, u32[]{:S(2)}) collective-permute-start(bf16[256,512]{1,0:T(8,128)(2,1)S(1)} %collective-permute-done.1.refs_5_), channel_id=1, source_target_pairs={{0,1},{1,0},{2,3},{3,2},{4,5},{5,4},{6,7},{7,6},{8,9},{9,8},{10,11... | collective-permute-start | bytes 786440 | tf_op jit(solution)/shard_map/ppermute | solution.py:20
  23.2 1.8 %collective-permute-start.8 = (bf16[256,512]{1,0:T(8,128)(2,1)S(1)}, bf16[256,512]{1,0:T(8,128)(2,1)S(1)}, u32[]{:S(2)}, u32[]{:S(2)}) collective-permute-start(bf16[256,512]{1,0:T(8,128)(2,1)S(1)} %collective-permute-done.2.refs_6_), channel_id=1, source_target_pairs={{0,1},{1,0},{2,3},{3,2},{4,5},{5,4},{6,7},{7,6},{8,9},{9,8},{10,11... | collective-permute-start | bytes 786440 | tf_op jit(solution)/shard_map/ppermute | solution.py:20
  32.9 4.3 %collective-permute-start.11 = (f32[9,4,256]{2,1,0:T(4,128)S(1)}, f32[9,4,256]{2,1,0:T(4,128)S(1)}, u32[]{:S(2)}, u32[]{:S(2)}) collective-permute-start(f32[9,4,256]{2,1,0:T(4,128)S(1)} %pad_maximum_fusion), channel_id=1, source_target_pairs={{0,8},{8,0},{16,24},{24,16},{1,9},{9,1},{17,25},{25,17},{2,10},{10... | collective-permute-start | bytes 110600 | tf_op jit(solution)/shard_map/ppermute | solution.py:20
  33.3 3.9 %collective-permute-start.10 = (f32[4,8,256]{2,1,0:T(8,128)S(1)}, f32[4,8,256]{2,1,0:T(8,128)S(1)}, u32[]{:S(2)}, u32[]{:S(2)}) collective-permute-start(f32[4,8,256]{2,1,0:T(8,128)S(1)} %get-tuple-element.48), channel_id=1, source_target_pairs={{0,2},{1,3},{2,0},{3,1},{4,6},{5,7},{6,4},{7,5},{8,10},{9,11},{10,... | collective-permute-start | bytes 98312 | tf_op jit(solution)/shard_map/ppermute | solution.py:20
  37.4 4.9 %collective-permute-start.13 = (f32[9,4,256]{2,1,0:T(4,128)S(1)}, f32[9,4,256]{2,1,0:T(4,128)S(1)}, u32[]{:S(2)}, u32[]{:S(2)}) collective-permute-start(f32[9,4,256]{2,1,0:T(4,128)S(1)} %constant_dynamic-update-slice_fusion), channel_id=1, source_target_pairs={{0,16},{8,24},{16,0},{24,8},{1,17},{9,25},{17,1},{25,9},{2,18},{10... | collective-permute-start | bytes 110600 | tf_op jit(solution)/shard_map/ppermute | solution.py:20
  37.9 3.9 %collective-permute-start.12 = (f32[4,8,256]{2,1,0:T(8,128)S(1)}, f32[4,8,256]{2,1,0:T(8,128)S(1)}, u32[]{:S(2)}, u32[]{:S(2)}) collective-permute-start(f32[4,8,256]{2,1,0:T(8,128)S(1)} %pad_maximum_fusion.1), channel_id=1, source_target_pairs={{0,4},{1,5},{2,6},{3,7},{4,0},{5,1},{6,2},{7,3},{8,12},{9,13},{10,... | collective-permute-start | bytes 98312 | tf_op jit(solution)/shard_map/ppermute | solution.py:20
  42.4 1.3 %collective-permute-start.14 = (f32[4,8,256]{2,1,0:T(8,128)S(1)}, f32[4,8,256]{2,1,0:T(8,128)S(1)}, u32[]{:S(2)}, u32[]{:S(2)}) collective-permute-start(f32[4,8,256]{2,1,0:T(8,128)S(1)} %pad_maximum_fusion.2), channel_id=1, source_target_pairs={{0,1},{1,0},{2,3},{3,2},{4,5},{5,4},{6,7},{7,6},{8,9},{9,8},{10,11... | collective-permute-start | bytes 98312 | tf_op jit(solution)/shard_map/ppermute | solution.py:20
  45.5 9.2 %collective-permute-start.16 = (bf16[272,512]{1,0:T(8,128)(2,1)S(1)}, bf16[272,512]{1,0:T(8,128)(2,1)S(1)}, u32[]{:S(2)}, u32[]{:S(2)}) collective-permute-start(bf16[272,512]{1,0:T(8,128)(2,1)S(1)} %get-tuple-element.62), channel_id=1, source_target_pairs={{0,8},{8,0},{16,24},{24,16},{1,9},{9,1},{17,25},{25,17},{2,10},{10... | collective-permute-start | bytes 835592 | tf_op jit(solution)/shard_map/ppermute | solution.py:20
  54.7 4.3 %collective-permute-start.15 = (f32[4,264,512]{2,1,0:T(8,128)S(1)}, f32[4,264,512]{2,1,0:T(8,128)S(1)}, u32[]{:S(2)}, u32[]{:S(2)}) collective-permute-start(f32[4,264,512]{2,1,0:T(8,128)S(1)} %get-tuple-element.59), channel_id=1, source_target_pairs={{0,1},{1,0},{2,3},{3,2},{4,5},{5,4},{6,7},{7,6},{8,9},{9,8},{10,11... | collective-permute-start | bytes 6488072 | tf_op jit(solution)/shard_map/ppermute | solution.py:20
  55.4 15.9 %collective-permute-start.19 = (bf16[272,512]{1,0:T(8,128)(2,1)S(1)}, bf16[272,512]{1,0:T(8,128)(2,1)S(1)}, u32[]{:S(2)}, u32[]{:S(2)}) collective-permute-start(bf16[272,512]{1,0:T(8,128)(2,1)S(1)} %pack_text.1.refs_0_), channel_id=1, source_target_pairs={{0,16},{8,24},{16,0},{24,8},{1,17},{9,25},{17,1},{25,9},{2,18},{10... | collective-permute-start | bytes 835592 | tf_op jit(solution)/shard_map/ppermute | solution.py:20
  58.9 14.6 %collective-permute-start.18 = (bf16[272,512]{1,0:T(8,128)(2,1)S(1)}, bf16[272,512]{1,0:T(8,128)(2,1)S(1)}, u32[]{:S(2)}, u32[]{:S(2)}) collective-permute-start(bf16[272,512]{1,0:T(8,128)(2,1)S(1)} %get-tuple-element.66), channel_id=1, source_target_pairs={{0,8},{8,0},{16,24},{24,16},{1,9},{9,1},{17,25},{25,17},{2,10},{10... | collective-permute-start | bytes 835592 | tf_op jit(solution)/shard_map/ppermute | solution.py:20
  60.4 15.1 %collective-permute-start.17 = (bf16[272,512]{1,0:T(8,128)(2,1)S(1)}, bf16[272,512]{1,0:T(8,128)(2,1)S(1)}, u32[]{:S(2)}, u32[]{:S(2)}) collective-permute-start(bf16[272,512]{1,0:T(8,128)(2,1)S(1)} %get-tuple-element.64), channel_id=1, source_target_pairs={{0,2},{1,3},{2,0},{3,1},{4,6},{5,7},{6,4},{7,5},{8,10},{9,11},{10,... | collective-permute-start | bytes 835592 | tf_op jit(solution)/shard_map/ppermute | solution.py:20
  62.0 14.1 %collective-permute-start.20 = (bf16[272,512]{1,0:T(8,128)(2,1)S(1)}, bf16[272,512]{1,0:T(8,128)(2,1)S(1)}, u32[]{:S(2)}, u32[]{:S(2)}) collective-permute-start(bf16[272,512]{1,0:T(8,128)(2,1)S(1)} %get-tuple-element.69), channel_id=1, source_target_pairs={{0,4},{1,5},{2,6},{3,7},{4,0},{5,1},{6,2},{7,3},{8,12},{9,13},{10,... | collective-permute-start | bytes 835592 | tf_op jit(solution)/shard_map/ppermute | solution.py:20
  63.0 13.1 %collective-permute-start.21 = (bf16[272,512]{1,0:T(8,128)(2,1)S(1)}, bf16[272,512]{1,0:T(8,128)(2,1)S(1)}, u32[]{:S(2)}, u32[]{:S(2)}) collective-permute-start(bf16[272,512]{1,0:T(8,128)(2,1)S(1)} %get-tuple-element.70), channel_id=1, source_target_pairs={{0,6},{1,7},{2,4},{3,5},{4,2},{5,3},{6,0},{7,1},{8,14},{9,15},{10,... | collective-permute-start | bytes 835592 | tf_op jit(solution)/shard_map/ppermute | solution.py:20

commit v19 on v15

--- a/solution.py
+++ b/solution.py
@@ -478,11 +478,11 @@
         lax.fori_loop(0, half // block, one, 0, unroll=4)
 
 
-def image_block(grads, texts, at, block, scale):
+def image_block(grads, texts, at, count, scale, block):
     total = None
     for grad, text in zip(grads, texts):
         part = lax.dot_general(
-            grad[:, pl.ds(at, block)],
+            grad[:, pl.ds(at, count)],
             text[:block, :],
             (((0,), (0,)), ((), ())),
             preferred_element_type=jnp.float32,
@@ -536,13 +536,15 @@
         for images_ref, first in ((far_ref, half), (near_ref, 0)):
 
             def one(j, carry):
-                images_ref[j, :block, :] = image_block(
-                    [*done_grads, *[by_text[t][0] for t in order]],
-                    [*done_texts, *[by_text[t][1] for t in order]],
-                    pl.multiple_of(j * block + first, block),
-                    block,
-                    scale,
-                )
+                for n in range(0, block, LANES):
+                    images_ref[j, n : n + LANES, :] = image_block(
+                        [*done_grads, *[by_text[t][0] for t in order]],
+                        [*done_texts, *[by_text[t][1] for t in order]],
+                        pl.multiple_of(j * block + first + n, LANES),
+                        LANES,
+                        scale,
+                        block,
+                    )
                 put_extra(images_ref.at[j, block:, :], col_extra)
                 return carry
 

time: 77.5 us -> 79.3 us (1.023)
  Pallas kernels: 22 us -> 23.8 us
    pallas_call x2, Pallas kernels: 8.16 us -> 10 us  [text_grads(): pl.pallas_call(functools.partial(text_kernel, tuple(order), len(done), le...]
  transfers between devices with their start and end apart: 22 -> 22, of which waited for: 15 -> 14; matrix products, arithmetic and copies ran while one was open for 2% -> 1% of each run, Pallas kernels for 20% -> 22%
where the time goes in v19:
time: 79.3 us; the launch traced here: 79.1 us
  waiting for transfers between devices  28.9 us (36%)
  Pallas kernels  23.8 us (30%)
  starting transfers between devices  22.2 us (28%)
  other arithmetic  2.42 us (3%)
  between operations  1.6 us (2%)
    ppermute x22, waiting for transfers between devices, swap(): return lax.ppermute(x, axis, [(i, i ^ q) for i in range(n)])  28.9 us
    ppermute x22, starting transfers between devices, swap(): return lax.ppermute(x, axis, [(i, i ^ q) for i in range(n)])  22.2 us
    pallas_call x2, Pallas kernels, text_grads(): pl.pallas_call(functools.partial(text_kernel, tuple(order), len(done), le...  10 us
    pallas_call x2, Pallas kernels, stats(): pl.pallas_call(functools.partial(stats_kernel, first, len(texts), block),...  7.92 us
    pallas_call x2, Pallas kernels, total_of(): pl.pallas_call(functools.partial(total_kernel, len(codes), in_order), out...  3.78 us
  transfers between devices with their start and end apart: 22, of which 14 were waited for; matrix products, arithmetic and copies ran while one was open for 1% of the time, Pallas kernels for 22%

profile of v19, /device:TPU:0, one launch (start us, length us, event | category | flops | bytes accessed | tf_op | source)
XLA Modules:
  0.0 79.1 jit_solution(3301930498992071103)
XLA Ops:
  0.6 1.1 %convert_element_type.8 = bf16[256,512]{1,0:T(8,128)(2,1)S(1)} convert(f32[256,512]{1,0:T(8,128)} %param.4) | non-fusion elementwise | flops 131072 | bytes 786432 | tf_op jit(solution)/shard_map/convert_element_type | solution.py:601
  1.7 4.1 %collective-permute-start.4 = (bf16[272,512]{1,0:T(8,128)(2,1)S(1)}, bf16[272,512]{1,0:T(8,128)(2,1)S(1)}, u32[]{:S(2)}, u32[]{:S(2)}) collective-permute-start(bf16[272,512]{1,0:T(8,128)(2,1)S(1)} %pad.4.refs_0_.refs_8_), channel_id=1, source_target_pairs={{0,16},{8,24},{16,0},{24,8},{1,17},{9,25},{17,1},{25,9},{2,18},{10... | collective-permute-start | bytes 835592 | tf_op jit(solution)/shard_map/ppermute | solution.py:20
  5.8 1.6 %collective-permute-start.3 = (bf16[272,512]{1,0:T(8,128)(2,1)S(1)}, bf16[272,512]{1,0:T(8,128)(2,1)S(1)}, u32[]{:S(2)}, u32[]{:S(2)}) collective-permute-start(bf16[272,512]{1,0:T(8,128)(2,1)S(1)} %pad.4.refs_0_.refs_8_), channel_id=1, source_target_pairs={{0,8},{8,0},{16,24},{24,16},{1,9},{9,1},{17,25},{25,17},{2,10},{10... | collective-permute-start | bytes 835592 | tf_op jit(solution)/shard_map/ppermute | solution.py:20
  7.4 1.1 %convert_element_type.9.refs_3_ = bf16[256,512]{1,0:T(8,128)(2,1)S(1)} convert(f32[256,512]{1,0:T(8,128)} %param.3) | non-fusion elementwise | flops 131072 | bytes 786432 | tf_op jit(solution)/shard_map/convert_element_type | solution.py:600
  8.5 2.5 %collective-permute-start.2 = (bf16[256,512]{1,0:T(8,128)(2,1)S(1)}, bf16[256,512]{1,0:T(8,128)(2,1)S(1)}, u32[]{:S(2)}, u32[]{:S(2)}) collective-permute-start(bf16[256,512]{1,0:T(8,128)(2,1)S(1)} %convert_element_type.9.refs_3_), channel_id=1, source_target_pairs={{0,6},{1,7},{2,4},{3,5},{4,2},{5,3},{6,0},{7,1},{8,14},{9,15},{10,... | collective-permute-start | bytes 786440 | tf_op jit(solution)/shard_map/ppermute | solution.py:20
  11.5 0.5 collective-permute-start
  12.0 6.5 %collective-permute-done.4.refs_2_.refs_6_ = bf16[272,512]{1,0:T(8,128)(2,1)S(1)} collective-permute-done((bf16[272,512]{1,0:T(8,128)(2,1)S(1)}, bf16[272,512]{1,0:T(8,128)(2,1)S(1)}, u32[]{:S(2)}, u32[]{:S(2)}) %collective-permute-start.4) | collective-permute-done | bytes 278560 | tf_op jit(solution)/shard_map/ppermute | solution.py:20
  18.6 0.6 collective-permute-start.9
  19.2 3.4 %collective-permute-done.1.refs_5_ = bf16[256,512]{1,0:T(8,128)(2,1)S(1)} collective-permute-done((bf16[256,512]{1,0:T(8,128)(2,1)S(1)}, bf16[256,512]{1,0:T(8,128)(2,1)S(1)}, u32[]{:S(2)}, u32[]{:S(2)}) %collective-permute-start.1) | collective-permute-done | bytes 262176 | tf_op jit(solution)/shard_map/ppermute | solution.py:20
  22.7 0.5 collective-permute-start.7
  25.0 5.3 %stats.1 = (bf16[1024,512]{1,0:T(8,128)(2,1)S(1)}, bf16[1024,512]{1,0:T(8,128)(2,1)S(1)}, f32[4,8,256]{2,1,0:T(8,128)S(1)}, f32[3,4,256]{2,1,0:T(4,128)S(1)}, f32[768,2048]{1,0:T(8,128)S(1)}) custom-call(f32[1,1]{1,0:T(1,128)S(6)} %mul.127.coef_ref, s32[1,2]{1,0:T(1,128)S(1)} %add_bitcast_fusion.place_ref, bf16[272,512]{1,0:T(8,128)(2,1)S(1)} %pad.4.refs_0_.refs_8_, ...), custom_call_target="tpu_custom_call" | custom-call | flops 2097152 | tf_op jit(solution)/shard_map/stats/pallas_call | solution.py:180
  30.3 2.6 %stats_last.1 = (f32[4,8,256]{2,1,0:T(8,128)S(1)}, f32[3,4,256]{2,1,0:T(4,128)S(1)}, f32[256,2048]{1,0:T(8,128)S(1)}) custom-call(f32[1,1]{1,0:T(1,128)S(6)} %mul.127.coef_ref, s32[1,2]{1,0:T(1,128)S(1)} %add_bitcast_fusion.place_ref, bf16[272,512]{1,0:T(8,128)(2,1)S(1)} %collective-permute-done.9.refs_0_.refs_6_.refs_11_, ...), custom_call_target="tpu_custom_call" | custom-call | flops 2097152 | tf_op jit(solution)/shard_map/stats_last/pallas_call | solution.py:180
  33.3 1.6 %collective-permute-start.10 = (f32[4,8,256]{2,1,0:T(8,128)S(1)}, f32[4,8,256]{2,1,0:T(8,128)S(1)}, u32[]{:S(2)}, u32[]{:S(2)}) collective-permute-start(f32[4,8,256]{2,1,0:T(8,128)S(1)} %get-tuple-element.48), channel_id=1, source_target_pairs={{0,2},{1,3},{2,0},{3,1},{4,6},{5,7},{6,4},{7,5},{8,10},{9,11},{10,... | collective-permute-start | bytes 98312 | tf_op jit(solution)/shard_map/ppermute | solution.py:20
  34.9 2.3 %collective-permute-done.10 = f32[4,8,256]{2,1,0:T(8,128)S(1)} collective-permute-done((f32[4,8,256]{2,1,0:T(8,128)S(1)}, f32[4,8,256]{2,1,0:T(8,128)S(1)}, u32[]{:S(2)}, u32[]{:S(2)}) %collective-permute-start.10) | collective-permute-done | bytes 32800 | tf_op jit(solution)/shard_map/ppermute | solution.py:20
  37.4 0.5 collective-permute-start.13
  37.9 1.5 %collective-permute-start.12 = (f32[4,8,256]{2,1,0:T(8,128)S(1)}, f32[4,8,256]{2,1,0:T(8,128)S(1)}, u32[]{:S(2)}, u32[]{:S(2)}) collective-permute-start(f32[4,8,256]{2,1,0:T(8,128)S(1)} %pad_maximum_fusion.1), channel_id=1, source_target_pairs={{0,4},{1,5},{2,6},{3,7},{4,0},{5,1},{6,2},{7,3},{8,12},{9,13},{10,... | collective-permute-start | bytes 98312 | tf_op jit(solution)/shard_map/ppermute | solution.py:20
  39.4 2.4 %collective-permute-done.12 = f32[4,8,256]{2,1,0:T(8,128)S(1)} collective-permute-done((f32[4,8,256]{2,1,0:T(8,128)S(1)}, f32[4,8,256]{2,1,0:T(8,128)S(1)}, u32[]{:S(2)}, u32[]{:S(2)}) %collective-permute-start.12) | collective-permute-done | bytes 32800 | tf_op jit(solution)/shard_map/ppermute | solution.py:20
  42.5 1.2 %collective-permute-done.14 = f32[4,8,256]{2,1,0:T(8,128)S(1)} collective-permute-done((f32[4,8,256]{2,1,0:T(8,128)S(1)}, f32[4,8,256]{2,1,0:T(8,128)S(1)}, u32[]{:S(2)}, u32[]{:S(2)}) %collective-permute-start.14) | collective-permute-done | bytes 32800 | tf_op jit(solution)/shard_map/ppermute | solution.py:20
  43.7 1.8 %text_grads_1.1 = (bf16[256,2048]{1,0:T(8,128)(2,1)S(1)}, bf16[272,512]{1,0:T(8,128)(2,1)S(1)}) custom-call(f32[1,1]{1,0:T(1,128)} %bitcast.241.scale_ref, f32[1,1]{1,0:T(1,128)S(6)} %mul.127.coef_ref, s32[1,2]{1,0:T(1,128)S(1)} %add_bitcast_fusion.place_ref, bf16[1024,512]{1,0:T(8,128)(2,1)S(1)} %get-tuple-element.44.refs_1_.refs_0_, ...), custom_call_target="tpu_custom_call" | custom-call | flops 21474836480 | tf_op jit(solution)/shard_map/text_grads_1/pallas_call | solution.py:574
  45.5 1.8 %collective-permute-start.16 = (bf16[272,512]{1,0:T(8,128)(2,1)S(1)}, bf16[272,512]{1,0:T(8,128)(2,1)S(1)}, u32[]{:S(2)}, u32[]{:S(2)}) collective-permute-start(bf16[272,512]{1,0:T(8,128)(2,1)S(1)} %get-tuple-element.62), channel_id=1, source_target_pairs={{0,8},{8,0},{16,24},{24,16},{1,9},{9,1},{17,25},{25,17},{2,10},{10... | collective-permute-start | bytes 835592 | tf_op jit(solution)/shard_map/ppermute | solution.py:20
  47.3 8.2 %text_grads_3.1 = (bf16[768,2048]{1,0:T(8,128)(2,1)}, f32[264,512]{1,0:T(8,128)S(1)}, bf16[272,512]{1,0:T(8,128)(2,1)S(1)}, f32[264,512]{1,0:T(8,128)S(1)}, f32[...) custom-call(f32[1,1]{1,0:T(1,128)} %bitcast.242.scale_ref, f32[1,1]{1,0:T(1,128)S(6)} %mul.127.coef_ref, ...), custom_call_target="tpu_custom_call" | custom-call | flops 64424509440 | tf_op jit(solution)/shard_map/text_grads_3/pallas_call | solution.py:574
  55.5 0.7 pack_text.1.refs_0_
  56.2 2.0 %collective-permute-start.19 = (bf16[272,512]{1,0:T(8,128)(2,1)S(1)}, bf16[272,512]{1,0:T(8,128)(2,1)S(1)}, u32[]{:S(2)}, u32[]{:S(2)}) collective-permute-start(bf16[272,512]{1,0:T(8,128)(2,1)S(1)} %pack_text.1.refs_0_), channel_id=1, source_target_pairs={{0,16},{8,24},{16,0},{24,8},{1,17},{9,25},{17,1},{25,9},{2,18},{10... | collective-permute-start | bytes 835592 | tf_op jit(solution)/shard_map/ppermute | solution.py:20
  58.2 1.5 %collective-permute-done.15.far = f32[4,264,512]{2,1,0:T(8,128)S(1)} collective-permute-done((f32[4,264,512]{2,1,0:T(8,128)S(1)}, f32[4,264,512]{2,1,0:T(8,128)S(1)}, u32[]{:S(2)}, u32[]{:S(2)}) %collective-permute-start.15) | collective-permute-done | bytes 2162720 | tf_op jit(solution)/shard_map/ppermute | solution.py:20
  60.0 1.1 %pack_images.1 = (f32[264,512]{1,0:T(8,128)S(1)}, bf16[272,512]{1,0:T(8,128)(2,1)S(1)}, bf16[272,512]{1,0:T(8,128)(2,1)S(1)}, bf16[272,512]{1,0:T(8,128)(2,1)S(1)}) custom-call(f32[4,264,512]{2,1,0:T(8,128)S(1)} %get-tuple-element.57.near, f32[4,264,512]{2,1,0:T(8,128)S(1)} %collective-permute-done.15.far, bf16[272,512]{1,0:T(8,128)(2,1)S(1)} %pack_text.1.refs_0_), custom_call_target="tpu_custom_call" | custom-call | flops 21474836480 | tf_op jit(solution)/shard_map/pack_images/pallas_call | solution.py:349
  61.2 1.7 %collective-permute-start.17 = (bf16[272,512]{1,0:T(8,128)(2,1)S(1)}, bf16[272,512]{1,0:T(8,128)(2,1)S(1)}, u32[]{:S(2)}, u32[]{:S(2)}) collective-permute-start(bf16[272,512]{1,0:T(8,128)(2,1)S(1)} %get-tuple-element.64), channel_id=1, source_target_pairs={{0,2},{1,3},{2,0},{3,1},{4,6},{5,7},{6,4},{7,5},{8,10},{9,11},{10,... | collective-permute-start | bytes 835592 | tf_op jit(solution)/shard_map/ppermute | solution.py:20
  62.8 1.0 %collective-permute-start.20 = (bf16[272,512]{1,0:T(8,128)(2,1)S(1)}, bf16[272,512]{1,0:T(8,128)(2,1)S(1)}, u32[]{:S(2)}, u32[]{:S(2)}) collective-permute-start(bf16[272,512]{1,0:T(8,128)(2,1)S(1)} %get-tuple-element.69), channel_id=1, source_target_pairs={{0,4},{1,5},{2,6},{3,7},{4,0},{5,1},{6,2},{7,3},{8,12},{9,13},{10,... | collective-permute-start | bytes 835592 | tf_op jit(solution)/shard_map/ppermute | solution.py:20
  63.8 0.9 %collective-permute-start.21 = (bf16[272,512]{1,0:T(8,128)(2,1)S(1)}, bf16[272,512]{1,0:T(8,128)(2,1)S(1)}, u32[]{:S(2)}, u32[]{:S(2)}) collective-permute-start(bf16[272,512]{1,0:T(8,128)(2,1)S(1)} %get-tuple-element.70), channel_id=1, source_target_pairs={{0,6},{1,7},{2,4},{3,5},{4,2},{5,3},{6,0},{7,1},{8,14},{9,15},{10,... | collective-permute-start | bytes 835592 | tf_op jit(solution)/shard_map/ppermute | solution.py:20
  64.7 7.3 %collective-permute-done.19.refs_1_ = bf16[272,512]{1,0:T(8,128)(2,1)S(1)} collective-permute-done((bf16[272,512]{1,0:T(8,128)(2,1)S(1)}, bf16[272,512]{1,0:T(8,128)(2,1)S(1)}, u32[]{:S(2)}, u32[]{:S(2)}) %collective-permute-start.19) | collective-permute-done | bytes 278560 | tf_op jit(solution)/shard_map/ppermute | solution.py:20
  72.0 2.2 %collective-permute-done.18.refs_0_ = bf16[272,512]{1,0:T(8,128)(2,1)S(1)} collective-permute-done((bf16[272,512]{1,0:T(8,128)(2,1)S(1)}, bf16[272,512]{1,0:T(8,128)(2,1)S(1)}, u32[]{:S(2)}, u32[]{:S(2)}) %collective-permute-start.18) | collective-permute-done | bytes 278560 | tf_op jit(solution)/shard_map/ppermute | solution.py:20
  74.3 1.8 %grad_text.1 = (f32[256,512]{1,0:T(8,128)}, f32[8,256]{1,0:T(8,128)S(1)}, f32[1,1]{1,0:T(1,128)}) custom-call(f32[1,1]{1,0:T(1,128)S(6)} %mul.127.coef_ref, f32[264,512]{1,0:T(8,128)S(1)} %get-tuple-element.65.base, bf16[272,512]{1,0:T(8,128)(2,1)S(1)} %collective-permute-done.18.refs_0_, bf16[272,512]{1,0:T(8,128)(2,1)S(1)} %collective-permute-done.19.refs_1_), custom_call_target="tpu_custom_call" | custom-call | tf_op jit(solution)/shard_map/grad_text/pallas_call | solution.py:422
  77.0 1.9 %grad_image.1 = (f32[256,512]{1,0:T(8,128)}, f32[8,256]{1,0:T(8,128)}, f32[1,1]{1,0:T(1,128)}) custom-call(f32[1,1]{1,0:T(1,128)S(6)} %mul.127.coef_ref, f32[264,512]{1,0:T(8,128)S(1)} %added.1.base, bf16[272,512]{1,0:T(8,128)(2,1)S(1)} %collective-permute-done.20.refs_0_, bf16[272,512]{1,0:T(8,128)(2,1)S(1)} %collective-permute-done.21.refs_1_, ...), custom_call_target="tpu_custom_call" | custom-call | tf_op jit(solution)/shard_map/grad_image/pallas_call | solution.py:422
  (44 shorter events, 4.1 us)
Async XLA Ops:
  1.7 16.8 %collective-permute-start.4 = (bf16[272,512]{1,0:T(8,128)(2,1)S(1)}, bf16[272,512]{1,0:T(8,128)(2,1)S(1)}, u32[]{:S(2)}, u32[]{:S(2)}) collective-permute-start(bf16[272,512]{1,0:T(8,128)(2,1)S(1)} %pad.4.refs_0_.refs_8_), channel_id=1, source_target_pairs={{0,16},{8,24},{16,0},{24,8},{1,17},{9,25},{17,1},{25,9},{2,18},{10... | collective-permute-start | bytes 835592 | tf_op jit(solution)/shard_map/ppermute | solution.py:20
  5.8 16.8 %collective-permute-start.3 = (bf16[272,512]{1,0:T(8,128)(2,1)S(1)}, bf16[272,512]{1,0:T(8,128)(2,1)S(1)}, u32[]{:S(2)}, u32[]{:S(2)}) collective-permute-start(bf16[272,512]{1,0:T(8,128)(2,1)S(1)} %pad.4.refs_0_.refs_8_), channel_id=1, source_target_pairs={{0,8},{8,0},{16,24},{24,16},{1,9},{9,1},{17,25},{25,17},{2,10},{10... | collective-permute-start | bytes 835592 | tf_op jit(solution)/shard_map/ppermute | solution.py:20
  8.5 10.7 %collective-permute-start.2 = (bf16[256,512]{1,0:T(8,128)(2,1)S(1)}, bf16[256,512]{1,0:T(8,128)(2,1)S(1)}, u32[]{:S(2)}, u32[]{:S(2)}) collective-permute-start(bf16[256,512]{1,0:T(8,128)(2,1)S(1)} %convert_element_type.9.refs_3_), channel_id=1, source_target_pairs={{0,6},{1,7},{2,4},{3,5},{4,2},{5,3},{6,0},{7,1},{8,14},{9,15},{10,... | collective-permute-start | bytes 786440 | tf_op jit(solution)/shard_map/ppermute | solution.py:20
  11.0 11.6 %collective-permute-start.1 = (bf16[256,512]{1,0:T(8,128)(2,1)S(1)}, bf16[256,512]{1,0:T(8,128)(2,1)S(1)}, u32[]{:S(2)}, u32[]{:S(2)}) collective-permute-start(bf16[256,512]{1,0:T(8,128)(2,1)S(1)} %convert_element_type.9.refs_3_), channel_id=1, source_target_pairs={{0,4},{1,5},{2,6},{3,7},{4,0},{5,1},{6,2},{7,3},{8,12},{9,13},{10,... | collective-permute-start | bytes 786440 | tf_op jit(solution)/shard_map/ppermute | solution.py:20
  11.5 11.1 %collective-permute-start = (bf16[256,512]{1,0:T(8,128)(2,1)S(1)}, bf16[256,512]{1,0:T(8,128)(2,1)S(1)}, u32[]{:S(2)}, u32[]{:S(2)}) collective-permute-start(bf16[256,512]{1,0:T(8,128)(2,1)S(1)} %convert_element_type.9.refs_3_), channel_id=1, source_target_pairs={{0,2},{1,3},{2,0},{3,1},{4,6},{5,7},{6,4},{7,5},{8,10},{9,11},{10,... | collective-permute-start | bytes 786440 | tf_op jit(solution)/shard_map/ppermute | solution.py:20
  18.6 11.7 %collective-permute-start.9 = (bf16[272,512]{1,0:T(8,128)(2,1)S(1)}, bf16[272,512]{1,0:T(8,128)(2,1)S(1)}, u32[]{:S(2)}, u32[]{:S(2)}) collective-permute-start(bf16[272,512]{1,0:T(8,128)(2,1)S(1)} %collective-permute-done.4.refs_2_.refs_6_), channel_id=1, source_target_pairs={{0,8},{8,0},{16,24},{24,16},{1,9},{9,1},{17,25},{25,17},{2,10},{10... | collective-permute-start | bytes 835592 | tf_op jit(solution)/shard_map/ppermute | solution.py:20
  19.2 4.7 %collective-permute-start.5 = (bf16[256,512]{1,0:T(8,128)(2,1)S(1)}, bf16[256,512]{1,0:T(8,128)(2,1)S(1)}, u32[]{:S(2)}, u32[]{:S(2)}) collective-permute-start(bf16[256,512]{1,0:T(8,128)(2,1)S(1)} %convert_element_type.9.refs_3_), channel_id=1, source_target_pairs={{0,1},{1,0},{2,3},{3,2},{4,5},{5,4},{6,7},{7,6},{8,9},{9,8},{10,11... | collective-permute-start | bytes 786440 | tf_op jit(solution)/shard_map/ppermute | solution.py:20
  22.7 1.5 %collective-permute-start.6 = (bf16[256,512]{1,0:T(8,128)(2,1)S(1)}, bf16[256,512]{1,0:T(8,128)(2,1)S(1)}, u32[]{:S(2)}, u32[]{:S(2)}) collective-permute-start(bf16[256,512]{1,0:T(8,128)(2,1)S(1)} %collective-permute-done.refs_4_), channel_id=1, source_target_pairs={{0,1},{1,0},{2,3},{3,2},{4,5},{5,4},{6,7},{7,6},{8,9},{9,8},{10,11... | collective-permute-start | bytes 786440 | tf_op jit(solution)/shard_map/ppermute | solution.py:20
  22.7 1.9 %collective-permute-start.7 = (bf16[256,512]{1,0:T(8,128)(2,1)S(1)}, bf16[256,512]{1,0:T(8,128)(2,1)S(1)}, u32[]{:S(2)}, u32[]{:S(2)}) collective-permute-start(bf16[256,512]{1,0:T(8,128)(2,1)S(1)} %collective-permute-done.1.refs_5_), channel_id=1, source_target_pairs={{0,1},{1,0},{2,3},{3,2},{4,5},{5,4},{6,7},{7,6},{8,9},{9,8},{10,11... | collective-permute-start | bytes 786440 | tf_op jit(solution)/shard_map/ppermute | solution.py:20
  23.2 1.8 %collective-permute-start.8 = (bf16[256,512]{1,0:T(8,128)(2,1)S(1)}, bf16[256,512]{1,0:T(8,128)(2,1)S(1)}, u32[]{:S(2)}, u32[]{:S(2)}) collective-permute-start(bf16[256,512]{1,0:T(8,128)(2,1)S(1)} %collective-permute-done.2.refs_6_), channel_id=1, source_target_pairs={{0,1},{1,0},{2,3},{3,2},{4,5},{5,4},{6,7},{7,6},{8,9},{9,8},{10,11... | collective-permute-start | bytes 786440 | tf_op jit(solution)/shard_map/ppermute | solution.py:20
  32.9 4.3 %collective-permute-start.11 = (f32[9,4,256]{2,1,0:T(4,128)S(1)}, f32[9,4,256]{2,1,0:T(4,128)S(1)}, u32[]{:S(2)}, u32[]{:S(2)}) collective-permute-start(f32[9,4,256]{2,1,0:T(4,128)S(1)} %pad_maximum_fusion), channel_id=1, source_target_pairs={{0,8},{8,0},{16,24},{24,16},{1,9},{9,1},{17,25},{25,17},{2,10},{10... | collective-permute-start | bytes 110600 | tf_op jit(solution)/shard_map/ppermute | solution.py:20
  33.3 3.9 %collective-permute-start.10 = (f32[4,8,256]{2,1,0:T(8,128)S(1)}, f32[4,8,256]{2,1,0:T(8,128)S(1)}, u32[]{:S(2)}, u32[]{:S(2)}) collective-permute-start(f32[4,8,256]{2,1,0:T(8,128)S(1)} %get-tuple-element.48), channel_id=1, source_target_pairs={{0,2},{1,3},{2,0},{3,1},{4,6},{5,7},{6,4},{7,5},{8,10},{9,11},{10,... | collective-permute-start | bytes 98312 | tf_op jit(solution)/shard_map/ppermute | solution.py:20
  37.4 4.9 %collective-permute-start.13 = (f32[9,4,256]{2,1,0:T(4,128)S(1)}, f32[9,4,256]{2,1,0:T(4,128)S(1)}, u32[]{:S(2)}, u32[]{:S(2)}) collective-permute-start(f32[9,4,256]{2,1,0:T(4,128)S(1)} %constant_dynamic-update-slice_fusion), channel_id=1, source_target_pairs={{0,16},{8,24},{16,0},{24,8},{1,17},{9,25},{17,1},{25,9},{2,18},{10... | collective-permute-start | bytes 110600 | tf_op jit(solution)/shard_map/ppermute | solution.py:20
  37.9 3.9 %collective-permute-start.12 = (f32[4,8,256]{2,1,0:T(8,128)S(1)}, f32[4,8,256]{2,1,0:T(8,128)S(1)}, u32[]{:S(2)}, u32[]{:S(2)}) collective-permute-start(f32[4,8,256]{2,1,0:T(8,128)S(1)} %pad_maximum_fusion.1), channel_id=1, source_target_pairs={{0,4},{1,5},{2,6},{3,7},{4,0},{5,1},{6,2},{7,3},{8,12},{9,13},{10,... | collective-permute-start | bytes 98312 | tf_op jit(solution)/shard_map/ppermute | solution.py:20
  42.4 1.3 %collective-permute-start.14 = (f32[4,8,256]{2,1,0:T(8,128)S(1)}, f32[4,8,256]{2,1,0:T(8,128)S(1)}, u32[]{:S(2)}, u32[]{:S(2)}) collective-permute-start(f32[4,8,256]{2,1,0:T(8,128)S(1)} %pad_maximum_fusion.2), channel_id=1, source_target_pairs={{0,1},{1,0},{2,3},{3,2},{4,5},{5,4},{6,7},{7,6},{8,9},{9,8},{10,11... | collective-permute-start | bytes 98312 | tf_op jit(solution)/shard_map/ppermute | solution.py:20
  45.5 10.0 %collective-permute-start.16 = (bf16[272,512]{1,0:T(8,128)(2,1)S(1)}, bf16[272,512]{1,0:T(8,128)(2,1)S(1)}, u32[]{:S(2)}, u32[]{:S(2)}) collective-permute-start(bf16[272,512]{1,0:T(8,128)(2,1)S(1)} %get-tuple-element.62), channel_id=1, source_target_pairs={{0,8},{8,0},{16,24},{24,16},{1,9},{9,1},{17,25},{25,17},{2,10},{10... | collective-permute-start | bytes 835592 | tf_op jit(solution)/shard_map/ppermute | solution.py:20
  55.5 4.3 %collective-permute-start.15 = (f32[4,264,512]{2,1,0:T(8,128)S(1)}, f32[4,264,512]{2,1,0:T(8,128)S(1)}, u32[]{:S(2)}, u32[]{:S(2)}) collective-permute-start(f32[4,264,512]{2,1,0:T(8,128)S(1)} %get-tuple-element.59), channel_id=1, source_target_pairs={{0,1},{1,0},{2,3},{3,2},{4,5},{5,4},{6,7},{7,6},{8,9},{9,8},{10,11... | collective-permute-start | bytes 6488072 | tf_op jit(solution)/shard_map/ppermute | solution.py:20
  56.2 15.9 %collective-permute-start.19 = (bf16[272,512]{1,0:T(8,128)(2,1)S(1)}, bf16[272,512]{1,0:T(8,128)(2,1)S(1)}, u32[]{:S(2)}, u32[]{:S(2)}) collective-permute-start(bf16[272,512]{1,0:T(8,128)(2,1)S(1)} %pack_text.1.refs_0_), channel_id=1, source_target_pairs={{0,16},{8,24},{16,0},{24,8},{1,17},{9,25},{17,1},{25,9},{2,18},{10... | collective-permute-start | bytes 835592 | tf_op jit(solution)/shard_map/ppermute | solution.py:20
  59.7 14.6 %collective-permute-start.18 = (bf16[272,512]{1,0:T(8,128)(2,1)S(1)}, bf16[272,512]{1,0:T(8,128)(2,1)S(1)}, u32[]{:S(2)}, u32[]{:S(2)}) collective-permute-start(bf16[272,512]{1,0:T(8,128)(2,1)S(1)} %get-tuple-element.66), channel_id=1, source_target_pairs={{0,8},{8,0},{16,24},{24,16},{1,9},{9,1},{17,25},{25,17},{2,10},{10... | collective-permute-start | bytes 835592 | tf_op jit(solution)/shard_map/ppermute | solution.py:20
  61.2 15.0 %collective-permute-start.17 = (bf16[272,512]{1,0:T(8,128)(2,1)S(1)}, bf16[272,512]{1,0:T(8,128)(2,1)S(1)}, u32[]{:S(2)}, u32[]{:S(2)}) collective-permute-start(bf16[272,512]{1,0:T(8,128)(2,1)S(1)} %get-tuple-element.64), channel_id=1, source_target_pairs={{0,2},{1,3},{2,0},{3,1},{4,6},{5,7},{6,4},{7,5},{8,10},{9,11},{10,... | collective-permute-start | bytes 835592 | tf_op jit(solution)/shard_map/ppermute | solution.py:20
  62.8 14.1 %collective-permute-start.20 = (bf16[272,512]{1,0:T(8,128)(2,1)S(1)}, bf16[272,512]{1,0:T(8,128)(2,1)S(1)}, u32[]{:S(2)}, u32[]{:S(2)}) collective-permute-start(bf16[272,512]{1,0:T(8,128)(2,1)S(1)} %get-tuple-element.69), channel_id=1, source_target_pairs={{0,4},{1,5},{2,6},{3,7},{4,0},{5,1},{6,2},{7,3},{8,12},{9,13},{10,... | collective-permute-start | bytes 835592 | tf_op jit(solution)/shard_map/ppermute | solution.py:20
  63.8 13.1 %collective-permute-start.21 = (bf16[272,512]{1,0:T(8,128)(2,1)S(1)}, bf16[272,512]{1,0:T(8,128)(2,1)S(1)}, u32[]{:S(2)}, u32[]{:S(2)}) collective-permute-start(bf16[272,512]{1,0:T(8,128)(2,1)S(1)} %get-tuple-element.70), channel_id=1, source_target_pairs={{0,6},{1,7},{2,4},{3,5},{4,2},{5,3},{6,0},{7,1},{8,14},{9,15},{10,... | collective-permute-start | bytes 835592 | tf_op jit(solution)/shard_map/ppermute | solution.py:20
